TPU v7x, 32 devices: a whole 2x2x4 slice. The times are simulated.
32 devices in a mesh: groups: 2 (over x), rows: 16 (over z, y, core).
Axes of the slice: x: 2, y: 2, z: 4, core: 2. Of those that a mesh axis runs over, the one named last changes fastest.
Arguments:
- train_feats: bfloat16 [65536, 2048], P(('groups', 'rows')), parts along dimension 0, may hold values from -6 to 6
- queries: bfloat16 [2, 512, 2048], P(None, ('groups', 'rows')), parts along dimension 1, may hold values from -6 to 6
- inverse_fisher: bfloat16 [1, 2048, 2048], P(None, None, 'rows'), may hold values from -0.125 to 0.125
Outputs:
- scores: float32 [65536, 512], P(('groups', 'rows')), parts along dimension 0
There are 2 independent parts, one for each index of `groups`. A program takes and returns all parts, laid end to end along the dimension named above; an argument that names none is the same for every part. Nothing has to cross between parts.
All inputs are finite; a program needn't handle non-finite values.
Results may differ from a plain program's by a relative error of at most 0.0029.
Values may be sent and summed in bfloat16 or wider, within the bound.
No kernel may reach another device: no remote copies, remote signals or barrier semaphores. Data moves between devices by JAX's collectives and lax.ppermute only.
A program may use at most 64 MiB of HBM per device.

v0:
```python
import jax
import jax.numpy as jnp
from jax import lax
from jax.sharding import PartitionSpec as P


def condition_block(query_block, inverse_fisher):
    group_count, group_width, column_count = inverse_fisher.shape
    gathered = lax.all_gather(query_block, "rows", axis=1, tiled=True)
    block_count, query_count, feature_count = gathered.shape
    flattened = gathered.reshape(block_count * query_count, group_count, group_width)
    partial_value = jnp.einsum(
        "qgk,gkc->qgc", flattened, inverse_fisher, preferred_element_type=jnp.float32
    ).astype(jnp.bfloat16)
    complete = lax.all_gather(partial_value, "rows", axis=2, tiled=True)
    return complete.reshape(block_count * query_count, feature_count)


def score_tile(train_feats, conditioned):
    score_scale = 1.0 / train_feats.shape[1] ** 0.5
    products = lax.dot_general(
        train_feats, conditioned, (((1,), (1,)), ((), ())), preferred_element_type=jnp.float32
    )
    return products * score_scale


def per_device(train_feats, queries, inverse_fisher):
    conditioned = condition_block(queries, inverse_fisher)
    return score_tile(train_feats, conditioned)


def solution(mesh):
    placed = (P(("groups", "rows"), None), P(None, ("groups", "rows"), None), P(None, None, "rows"))
    return jax.shard_map(
        per_device,
        mesh=mesh,
        in_specs=placed,
        out_specs=P(("groups", "rows"), None),
        check_vma=False,
    )
```

profile of v0, /device:TPU:0, one launch (start us, length us, event | category | flops | bytes accessed | tf_op | source)
XLA Modules:
  0.0 119.8 jit_solution(4222742148399841609)
XLA Ops:
  6.5 0.0 copy-start
  6.5 0.0 all-gather.3.cloned.1.call-start
  6.5 0.7 all-gather.3.cloned.1.call-update
  7.3 0.0 all-gather.5.cloned.1.call-start
  7.3 46.4 %all-gather.3.cloned.1.call-done = bf16[2,256,2048]{2,1,0:T(8,128)(2,1)} async-done(((bf16[2,16,2048]{2,1,0:T(8,128)(2,1)}), bf16[2,256,2048]{2,1,0:T(8,128)(2,1)}) %all-gather.3.cloned.1.call-update) | async-done | bytes 2097168 | tf_op jit(solution)/shard_map/all_gather | solution.py:9
  53.7 0.0 copy-done
  53.7 3.1 %fusion.1 = bf16[512,1,128]{0,2,1:T(8,128)(2,1)} fusion(bf16[512,2048]{1,0:T(8,128)(2,1)} %bitcast.15, bf16[1,2048,128]{2,1,0:T(8,128)(2,1)S(1)} %copy-done), kind=kOutput, calls=%fused_computation.3 | convolution fusion | flops 268500992 | bytes 2752512 | tf_op jit(solution)/shard_map/qgk,gkc->qgc/dot_general | solution.py:12
  56.8 0.0 all-gather.5.cloned.1.call-update
  56.8 40.3 %all-gather.5.cloned.1.call-done = bf16[512,1,2048]{0,2,1:T(8,128)(2,1)} async-done(((bf16[512,1,128]{0,2,1:T(8,128)(2,1)}), bf16[512,1,2048]{0,2,1:T(8,128)(2,1)}) %all-gather.5.cloned.1.call-update) | async-done | bytes 2097168 | tf_op jit(solution)/shard_map/all_gather | solution.py:15
  97.1 10.5 %multiply_bitcast_fusion = f32[2048,512]{0,1:T(8,128)} fusion(bf16[2048,2048]{1,0:T(8,128)(2,1)} %param.3, bf16[512,1,2048]{0,2,1:T(8,128)(2,1)} %all-gather.5.cloned.1.call-done), kind=kOutput, calls=%fused_computation | convolution fusion | flops 4296015872 | bytes 14680064 | tf_op jit(solution)/shard_map/dot_general | solution.py:21
  107.7 5.3 %copy.4 = f32[2048,512]{1,0:T(8,128)} copy(f32[2048,512]{0,1:T(8,128)} %multiply_bitcast_fusion) | data formatting | bytes 8388608 | tf_op jit(solution)/shard_map/mul | solution.py:24
Async XLA Ops:
  6.5 47.2 %copy-start = (bf16[1,2048,128]{2,1,0:T(8,128)(2,1)S(1)}, bf16[1,2048,128]{2,1,0:T(8,128)(2,1)}, u32[]{:S(2)}) copy-start(bf16[1,2048,128]{2,1,0:T(8,128)(2,1)} %param.5) | copy-start | bytes 1572868
  6.5 47.2 %all-gather.3.cloned.1.call-start = ((), (), s32[]{:S(2)}) async-start(), calls=%async_computation | async-start | bytes 2228224 | tf_op jit(solution)/shard_map/all_gather | solution.py:9
  7.3 89.9 %all-gather.5.cloned.1.call-start = ((), (), s32[]{:S(2)}) async-start(), calls=%async_computation.1 | async-start | bytes 2228224 | tf_op jit(solution)/shard_map/all_gather | solution.py:15
Sparse Core Ops, SparseCore 0:
  9.5 44.1 all-gather.2
  56.9 40.1 all-gather.4
where the time goes:
time: 120 us
  waiting for transfers between devices  87.5 us (73%)
  matrix products  13.6 us (11%)
  between operations  13.4 us (11%)
  local copies, waits for them, and re-layouts  5.34 us (4%)
    all_gather x1, waiting for transfers between devices, condition_block(): gathered = lax.all_gather(query_block, 'rows', axis=1, tiled=True)  46.4 us
    all_gather x1, waiting for transfers between devices, condition_block(): complete = lax.all_gather(partial_value, 'rows', axis=2, tiled=True)  40.3 us
    dot_general x1, matrix products, score_tile(): lax.dot_general(train_feats, conditioned, (((1,), (1,)), ((), ())), prefe...  10.5 us
    mul x1, local copies, waits for them, and re-layouts, score_tile(): return products * score_scale  5.34 us
    dot_general x1, matrix products, condition_block(): jnp.einsum('qgk,gkc->qgc', flattened, inverse_fisher, preferred_element_t...  3.07 us
  transfers between devices with their start and end apart: 2, of which 2 were waited for; matrix products, arithmetic and copies ran while one was open for 0% of the time, Pallas kernels for 0%

commit v1 on v0

v1 whole, which is shorter than its diff:
```python
import functools

import jax
import jax.numpy as jnp
from jax import lax
from jax.experimental import pallas as pl
from jax.experimental.pallas import tpu as pltpu
from jax.sharding import PartitionSpec as P

VMEM = pl.BlockSpec(memory_space=pltpu.VMEM)


class Grid:
    def __init__(self, row_count):
        chips = row_count // 2
        self.near = 1
        while self.near * self.near * 4 <= chips:
            self.near *= 2
        self.far = chips // self.near
        self.chips = chips

    def rank(self, far, near, core):
        return ((far % self.far) * self.near + near % self.near) * 2 + core

    def fetch(self, block, far, near, core):
        pairs = [
            (self.rank(f + far, n + near, c ^ core), self.rank(f, n, c))
            for f in range(self.far)
            for n in range(self.near)
            for c in range(2)
        ]
        return lax.ppermute(block, "rows", pairs)

    def slots(self):
        return [(far, near) for near in range(self.near) for far in range(self.far)]

    def gather(self, block):
        found = {(0, 0): block}
        for near in range(1, self.near):
            found[0, near] = self.fetch(block, 0, near, 0)
        for far in range(1, self.far):
            found[far, 0] = self.fetch(block, far, 0, 0)
        for far in range(1, self.far):
            for near in range(1, self.near):
                found[far, near] = self.fetch(found[far, 0], 0, near, 0)
        return [found[slot] for slot in self.slots()]

    def place(self):
        row = lax.axis_index("rows")
        core, chip = lax.rem(row, 2), lax.div(row, 2)
        far, near = lax.div(chip, self.near), lax.rem(chip, self.near)
        chips = [
            lax.rem(far + f, self.far) * self.near + lax.rem(near + n, self.near) for f, n in self.slots()
        ]
        return core, chips


def condition_kernel(grid, *refs):
    query_refs = refs[: grid.chips]
    own_ref, peer_ref, out_ref, sorted_ref, columns_ref = refs[grid.chips :]
    core, chips = grid.place()
    width = own_ref.shape[-1]
    columns_ref[:, pl.ds(pl.multiple_of(core * width, width), width)] = own_ref[0]
    columns_ref[:, pl.ds(pl.multiple_of((1 - core) * width, width), width)] = peer_ref[0]
    for chip, query_ref in zip(chips, query_refs):
        sorted_ref[:, pl.ds(chip, 1)] = query_ref[...][:, None]
    rows = sorted_ref[...].reshape(-1, sorted_ref.shape[-1])
    out_ref[...] = jnp.dot(rows, columns_ref[...], preferred_element_type=jnp.float32).astype(out_ref.dtype)


def condition(grid, queries, own, peer):
    blocks, count, features = queries[0].shape
    width = own.shape[-1]
    return pl.pallas_call(
        functools.partial(condition_kernel, grid),
        out_shape=jax.ShapeDtypeStruct((blocks * grid.chips * count, 2 * width), jnp.bfloat16),
        in_specs=[VMEM] * (grid.chips + 2),
        out_specs=VMEM,
        scratch_shapes=[
            pltpu.VMEM((blocks, grid.chips, count, features), jnp.bfloat16),
            pltpu.VMEM((features, 2 * width), jnp.bfloat16),
        ],
        compiler_params=pltpu.CompilerParams(vmem_limit_bytes=12 << 20),
        cost_estimate=pl.CostEstimate(flops=1 << 28, bytes_accessed=3 << 20, transcendentals=0),
        name="condition",
    )(*queries, own, peer)


def score_kernel(grid, tile, shape, *refs):
    blocks, count, width = shape
    train_ref, own_refs, peer_refs = refs[0], refs[1 : 1 + grid.chips], refs[1 + grid.chips : 1 + 2 * grid.chips]
    out_ref, sorted_ref, tile_ref, sem = refs[1 + 2 * grid.chips :]
    core, chips = grid.place()
    features = train_ref.shape[1]
    for which, parts in ((core, own_refs), (1 - core, peer_refs)):
        for chip, part_ref in zip(chips, parts):
            columns = pl.ds(pl.multiple_of(chip * width, width), width)
            sorted_ref[:, :, pl.ds(which, 1), :, columns] = part_ref[...].reshape(
                blocks, grid.chips, 1, count, width
            )
    scale = 1.0 / features**0.5
    steps = train_ref.shape[0] // tile

    def copy(step, slot):
        return pltpu.make_async_copy(
            tile_ref.at[slot], out_ref.at[pl.ds(pl.multiple_of(step * tile, tile), tile)], sem.at[slot]
        )

    @pl.loop(0, steps)
    def _(step):
        slot = lax.rem(step, 2)

        @pl.when(step >= 2)
        def _():
            copy(step - 2, slot).wait()

        products = lax.dot_general(
            train_ref[pl.ds(pl.multiple_of(step * tile, tile), tile)],
            sorted_ref[...].reshape(-1, features),
            (((1,), (1,)), ((), ())),
            preferred_element_type=jnp.float32,
        )
        tile_ref[slot] = products * scale
        copy(step, slot).start()

    for step in range(max(steps - 2, 0), steps):
        copy(step, step % 2).wait()


def score(grid, train_feats, own, peer, blocks):
    rows, features = train_feats.shape
    queries, width = own[0].shape
    count = queries // (blocks * grid.chips)
    tile = 256
    return pl.pallas_call(
        functools.partial(score_kernel, grid, tile, (blocks, count, width)),
        out_shape=jax.ShapeDtypeStruct((rows, 2 * queries), jnp.float32),
        in_specs=[VMEM] * (1 + 2 * grid.chips),
        out_specs=pl.BlockSpec(memory_space=pl.ANY),
        scratch_shapes=[
            pltpu.VMEM((blocks, grid.chips, 2, count, features), jnp.bfloat16),
            pltpu.VMEM((2, tile, 2 * queries), jnp.float32),
            pltpu.SemaphoreType.DMA((2,)),
        ],
        compiler_params=pltpu.CompilerParams(vmem_limit_bytes=24 << 20),
        cost_estimate=pl.CostEstimate(
            flops=4 * rows * features * queries, bytes_accessed=16 << 20, transcendentals=0
        ),
        name="score",
    )(pltpu.with_memory_space_constraint(train_feats, pltpu.VMEM), *own, *peer)


def two_level(grid, train_feats, queries, inverse_fisher):
    peer_fisher = grid.fetch(inverse_fisher, 0, 0, 1)
    gathered = grid.gather(queries)
    block = condition(grid, gathered, inverse_fisher, peer_fisher)
    own = grid.gather(block)
    peer = [grid.fetch(part, 0, 0, 1) for part in own]
    return score(grid, train_feats, own, peer, queries.shape[0])


def one_level(train_feats, queries, inverse_fisher):
    group_count, group_width, _ = inverse_fisher.shape
    gathered = lax.all_gather(queries, "rows", axis=1, tiled=True)
    flattened = gathered.reshape(-1, group_count, group_width)
    part = jnp.einsum("qgk,gkc->qgc", flattened, inverse_fisher, preferred_element_type=jnp.float32)
    complete = lax.all_gather(part.astype(jnp.bfloat16), "rows", axis=2, tiled=True)
    conditioned = complete.reshape(flattened.shape[0], -1)
    products = lax.dot_general(
        train_feats, conditioned, (((1,), (1,)), ((), ())), preferred_element_type=jnp.float32
    )
    return products * (1.0 / train_feats.shape[1] ** 0.5)


def per_device(row_count, train_feats, queries, inverse_fisher):
    group_count, _, width = inverse_fisher.shape
    whole_tiles = group_count == 1 and width % 128 == 0 and queries.shape[1] % 16 == 0
    if row_count % 2 == 0 and whole_tiles and train_feats.shape[0] % 512 == 0:
        return two_level(Grid(row_count), train_feats, queries, inverse_fisher)
    return one_level(train_feats, queries, inverse_fisher)


def solution(mesh):
    placed = (P(("groups", "rows"), None), P(None, ("groups", "rows"), None), P(None, None, "rows"))
    return jax.shard_map(
        functools.partial(per_device, mesh.shape["rows"]),
        mesh=mesh,
        in_specs=placed,
        out_specs=P(("groups", "rows"), None),
        check_vma=False,
    )
```

time: 120 us -> 60.8 us (0.51)
  waiting for transfers between devices: 87.5 us -> 25.5 us
  starting transfers between devices: 0.04 us -> 21.7 us
  matrix products: 13.6 us -> 0 us
  between operations: 13.4 us -> 0.06 us
  Pallas kernels: 0 us -> 7.97 us
    all_gather x2 -> x0, waiting for transfers between devices: 86.7 us -> none  [the longest x1 46.4 us: condition_block(): gathered = lax.all_gather(query_block, 'rows', axis=1, tiled=True)]
    ppermute x0 -> x23, waiting for transfers between devices: none -> 25.5 us  [fetch(): return lax.ppermute(block, 'rows', pairs)]
    ppermute x0 -> x23, starting transfers between devices: none -> 21.7 us  [fetch(): return lax.ppermute(block, 'rows', pairs)]
    dot_general x2 -> x0, matrix products: 13.6 us -> none  [the longest x1 10.5 us: score_tile(): lax.dot_general(train_feats, conditioned, (((1,), (1,)), ((), ())), prefe...]
    pallas_call x0 -> x2, Pallas kernels: none -> 7.97 us  [the longest x1 7.16 us: score(): pl.pallas_call(functools.partial(score_kernel, grid, tile, (blocks, count...]
    mul x1 -> x0, local copies, waits for them, and re-layouts: 5.34 us -> none  [score_tile(): return products * score_scale]
    unnamed x2 -> x6, local copies, waits for them, and re-layouts: 0.01 us -> 5.33 us
  transfers between devices with their start and end apart: 2 -> 23, of which waited for: 2 -> 10; matrix products, arithmetic and copies ran while one was open for 0% -> 0% of each run, Pallas kernels for 0% -> 0%
where the time goes in v1:
time: 60.8 us; the launch traced here: 60.6 us
  waiting for transfers between devices  25.5 us (42%)
  starting transfers between devices  21.7 us (36%)
  Pallas kernels  7.97 us (13%)
  local copies, waits for them, and re-layouts  5.33 us (9%)
    ppermute x23, waiting for transfers between devices, fetch(): return lax.ppermute(block, 'rows', pairs)  25.5 us
    ppermute x23, starting transfers between devices, fetch(): return lax.ppermute(block, 'rows', pairs)  21.7 us
    pallas_call x1, Pallas kernels, score(): pl.pallas_call(functools.partial(score_kernel, grid, tile, (blocks, count...  7.16 us
    unnamed x6, local copies, waits for them, and re-layouts  5.33 us
  transfers between devices with their start and end apart: 23, of which 10 were waited for; matrix products, arithmetic and copies ran while one was open for 0% of the time, Pallas kernels for 0%

profile of v1, /device:TPU:0, one launch (start us, length us, event | category | flops | bytes accessed | tf_op | source)
XLA Modules:
  0.0 60.6 jit_solution(7217198880091497666)
XLA Ops:
  0.0 0.5 collective-permute-start.7
  0.5 2.6 %collective-permute-start.2 = (bf16[2,16,2048]{2,1,0:T(8,128)(2,1)}, bf16[2,16,2048]{2,1,0:T(8,128)(2,1)S(1)}, u32[]{:S(2)}, u32[]{:S(2)}) collective-permute-start(bf16[2,16,2048]{2,1,0:T(8,128)(2,1)} %refs_0_.2), channel_id=1, source_target_pairs={{12,0},{13,1},{14,2},{15,3},{0,4},{1,5},{2,6},{3,7},{4,8},{5,9},{6... | collective-permute-start | bytes 393224 | tf_op jit(solution)/shard_map/ppermute | solution.py:32
  3.0 2.6 %collective-permute-start.1 = (bf16[2,16,2048]{2,1,0:T(8,128)(2,1)}, bf16[2,16,2048]{2,1,0:T(8,128)(2,1)S(1)}, u32[]{:S(2)}, u32[]{:S(2)}) collective-permute-start(bf16[2,16,2048]{2,1,0:T(8,128)(2,1)} %refs_0_.2), channel_id=1, source_target_pairs={{8,0},{9,1},{10,2},{11,3},{12,4},{13,5},{14,6},{15,7},{0,8},{1,9},... | collective-permute-start | bytes 393224 | tf_op jit(solution)/shard_map/ppermute | solution.py:32
  5.6 1.3 %collective-permute-start = (bf16[2,16,2048]{2,1,0:T(8,128)(2,1)}, bf16[2,16,2048]{2,1,0:T(8,128)(2,1)S(1)}, u32[]{:S(2)}, u32[]{:S(2)}) collective-permute-start(bf16[2,16,2048]{2,1,0:T(8,128)(2,1)} %refs_0_.2), channel_id=1, source_target_pairs={{4,0},{5,1},{6,2},{7,3},{8,4},{9,5},{10,6},{11,7},{12,8},{13,9},{1... | collective-permute-start | bytes 393224 | tf_op jit(solution)/shard_map/ppermute | solution.py:32
  7.0 1.5 %collective-permute-start.3 = (bf16[2,16,2048]{2,1,0:T(8,128)(2,1)}, bf16[2,16,2048]{2,1,0:T(8,128)(2,1)S(1)}, u32[]{:S(2)}, u32[]{:S(2)}) collective-permute-start(bf16[2,16,2048]{2,1,0:T(8,128)(2,1)} %refs_0_.2), channel_id=1, source_target_pairs={{2,0},{3,1},{0,2},{1,3},{6,4},{7,5},{4,6},{5,7},{10,8},{11,9},{8,1... | collective-permute-start | bytes 393224 | tf_op jit(solution)/shard_map/ppermute | solution.py:32
  8.5 1.2 %collective-permute-done.2.refs_3_ = bf16[2,16,2048]{2,1,0:T(8,128)(2,1)S(1)} collective-permute-done((bf16[2,16,2048]{2,1,0:T(8,128)(2,1)}, bf16[2,16,2048]{2,1,0:T(8,128)(2,1)S(1)}, u32[]{:S(2)}, u32[]{:S(2)}) %collective-permute-start.2) | collective-permute-done | bytes 131104 | tf_op jit(solution)/shard_map/ppermute | solution.py:32
  9.7 1.7 %collective-permute-start.6 = (bf16[2,16,2048]{2,1,0:T(8,128)(2,1)S(1)}, bf16[2,16,2048]{2,1,0:T(8,128)(2,1)S(1)}, u32[]{:S(2)}, u32[]{:S(2)}) collective-permute-start(bf16[2,16,2048]{2,1,0:T(8,128)(2,1)S(1)} %collective-permute-done.2.refs_3_), channel_id=1, source_target_pairs={{2,0},{3,1},{0,2},{1,3},{6,4},{7,5},{4,6},{5,7},{10,8},{11,9},{8,1... | collective-permute-start | bytes 393224 | tf_op jit(solution)/shard_map/ppermute | solution.py:32
  11.4 3.8 %collective-permute-done.1.refs_2_ = bf16[2,16,2048]{2,1,0:T(8,128)(2,1)S(1)} collective-permute-done((bf16[2,16,2048]{2,1,0:T(8,128)(2,1)}, bf16[2,16,2048]{2,1,0:T(8,128)(2,1)S(1)}, u32[]{:S(2)}, u32[]{:S(2)}) %collective-permute-start.1) | collective-permute-done | bytes 131104 | tf_op jit(solution)/shard_map/ppermute | solution.py:32
  15.1 1.5 %collective-permute-start.5 = (bf16[2,16,2048]{2,1,0:T(8,128)(2,1)S(1)}, bf16[2,16,2048]{2,1,0:T(8,128)(2,1)S(1)}, u32[]{:S(2)}, u32[]{:S(2)}) collective-permute-start(bf16[2,16,2048]{2,1,0:T(8,128)(2,1)S(1)} %collective-permute-done.1.refs_2_), channel_id=1, source_target_pairs={{2,0},{3,1},{0,2},{1,3},{6,4},{7,5},{4,6},{5,7},{10,8},{11,9},{8,1... | collective-permute-start | bytes 393224 | tf_op jit(solution)/shard_map/ppermute | solution.py:32
  16.6 0.5 collective-permute-start.4
  17.2 4.3 %collective-permute-done.5.refs_6_ = bf16[2,16,2048]{2,1,0:T(8,128)(2,1)S(1)} collective-permute-done((bf16[2,16,2048]{2,1,0:T(8,128)(2,1)S(1)}, bf16[2,16,2048]{2,1,0:T(8,128)(2,1)S(1)}, u32[]{:S(2)}, u32[]{:S(2)}) %collective-permute-start.5) | collective-permute-done | bytes 131104 | tf_op jit(solution)/shard_map/ppermute | solution.py:32
  21.5 1.8 %collective-permute-done.4.refs_5_ = bf16[2,16,2048]{2,1,0:T(8,128)(2,1)S(1)} collective-permute-done((bf16[2,16,2048]{2,1,0:T(8,128)(2,1)S(1)}, bf16[2,16,2048]{2,1,0:T(8,128)(2,1)S(1)}, u32[]{:S(2)}, u32[]{:S(2)}) %collective-permute-start.4) | collective-permute-done | bytes 131104 | tf_op jit(solution)/shard_map/ppermute | solution.py:32
  23.3 1.0 %copy-done = bf16[1,2048,128]{2,1,0:T(8,128)(2,1)S(1)} copy-done((bf16[1,2048,128]{2,1,0:T(8,128)(2,1)S(1)}, bf16[1,2048,128]{2,1,0:T(8,128)(2,1)}, u32[]{:S(2)}) %copy-start) | copy-done | bytes 524312
  24.4 0.9 %copy-done.1 = bf16[2,16,2048]{2,1,0:T(8,128)(2,1)S(1)} copy-done((bf16[2,16,2048]{2,1,0:T(8,128)(2,1)S(1)}, bf16[2,16,2048]{2,1,0:T(8,128)(2,1)}, u32[]{:S(2)}) %copy-start.1) | copy-done | bytes 131096
  25.3 0.8 %condition.1.refs_1_ = bf16[256,256]{1,0:T(8,128)(2,1)S(1)} custom-call(bf16[2,16,2048]{2,1,0:T(8,128)(2,1)S(1)} %copy-done.1, bf16[2,16,2048]{2,1,0:T(8,128)(2,1)S(1)} %collective-permute-done.refs_1_, bf16[2,16,2048]{2,1,0:T(8,128)(2,1)S(1)} %collective-permute-done.1.refs_2_, bf16[2,16,2048]{2,1,0:T(8,128)(2,1)S(1)} %collective-permute-done.2.refs_3_, ...), custom_call_target="tpu_custom_call" | custom-call | flops 268435456 | bytes 3145728 | tf_op jit(solution)/shard_map/condition/pallas_call | solution.py:74
  26.1 1.6 %collective-permute-start.11 = (bf16[256,256]{1,0:T(8,128)(2,1)S(1)}, bf16[256,256]{1,0:T(8,128)(2,1)S(1)}, u32[]{:S(2)}, u32[]{:S(2)}) collective-permute-start(bf16[256,256]{1,0:T(8,128)(2,1)S(1)} %condition.1.refs_1_), channel_id=1, source_target_pairs={{2,0},{3,1},{0,2},{1,3},{6,4},{7,5},{4,6},{5,7},{10,8},{11,9},{8,1... | collective-permute-start | bytes 393224 | tf_op jit(solution)/shard_map/ppermute | solution.py:32
  27.6 1.5 %collective-permute-start.10 = (bf16[256,256]{1,0:T(8,128)(2,1)S(1)}, bf16[256,256]{1,0:T(8,128)(2,1)S(1)}, u32[]{:S(2)}, u32[]{:S(2)}) collective-permute-start(bf16[256,256]{1,0:T(8,128)(2,1)S(1)} %condition.1.refs_1_), channel_id=1, source_target_pairs={{12,0},{13,1},{14,2},{15,3},{0,4},{1,5},{2,6},{3,7},{4,8},{5,9},{6... | collective-permute-start | bytes 393224 | tf_op jit(solution)/shard_map/ppermute | solution.py:32
  29.1 3.2 %collective-permute-start.9 = (bf16[256,256]{1,0:T(8,128)(2,1)S(1)}, bf16[256,256]{1,0:T(8,128)(2,1)S(1)}, u32[]{:S(2)}, u32[]{:S(2)}) collective-permute-start(bf16[256,256]{1,0:T(8,128)(2,1)S(1)} %condition.1.refs_1_), channel_id=1, source_target_pairs={{8,0},{9,1},{10,2},{11,3},{12,4},{13,5},{14,6},{15,7},{0,8},{1,9},... | collective-permute-start | bytes 393224 | tf_op jit(solution)/shard_map/ppermute | solution.py:32
  32.3 0.3 collective-permute-start.8
  32.6 3.3 %collective-permute-done.10.refs_4_ = bf16[256,256]{1,0:T(8,128)(2,1)S(1)} collective-permute-done((bf16[256,256]{1,0:T(8,128)(2,1)S(1)}, bf16[256,256]{1,0:T(8,128)(2,1)S(1)}, u32[]{:S(2)}, u32[]{:S(2)}) %collective-permute-start.10) | collective-permute-done | bytes 131104 | tf_op jit(solution)/shard_map/ppermute | solution.py:32
  35.9 0.5 collective-permute-start.14
  36.4 4.0 %collective-permute-done.9.refs_3_ = bf16[256,256]{1,0:T(8,128)(2,1)S(1)} collective-permute-done((bf16[256,256]{1,0:T(8,128)(2,1)S(1)}, bf16[256,256]{1,0:T(8,128)(2,1)S(1)}, u32[]{:S(2)}, u32[]{:S(2)}) %collective-permute-start.9) | collective-permute-done | bytes 131104 | tf_op jit(solution)/shard_map/ppermute | solution.py:32
  40.4 0.5 collective-permute-start.13
  41.0 0.1 collective-permute-done.8.refs_2_
  41.1 1.4 %collective-permute-start.12 = (bf16[256,256]{1,0:T(8,128)(2,1)S(1)}, bf16[256,256]{1,0:T(8,128)(2,1)S(1)}, u32[]{:S(2)}, u32[]{:S(2)}) collective-permute-start(bf16[256,256]{1,0:T(8,128)(2,1)S(1)} %collective-permute-done.8.refs_2_), channel_id=1, source_target_pairs={{2,0},{3,1},{0,2},{1,3},{6,4},{7,5},{4,6},{5,7},{10,8},{11,9},{8,1... | collective-permute-start | bytes 393224 | tf_op jit(solution)/shard_map/ppermute | solution.py:32
  42.5 0.5 collective-permute-start.16
  43.0 0.1 collective-permute-start.22
  43.1 3.7 %collective-permute-done.13.refs_7_ = bf16[256,256]{1,0:T(8,128)(2,1)S(1)} collective-permute-done((bf16[256,256]{1,0:T(8,128)(2,1)S(1)}, bf16[256,256]{1,0:T(8,128)(2,1)S(1)}, u32[]{:S(2)}, u32[]{:S(2)}) %collective-permute-start.13) | collective-permute-done | bytes 131104 | tf_op jit(solution)/shard_map/ppermute | solution.py:32
  46.8 1.9 %collective-permute-done.12.refs_6_ = bf16[256,256]{1,0:T(8,128)(2,1)S(1)} collective-permute-done((bf16[256,256]{1,0:T(8,128)(2,1)S(1)}, bf16[256,256]{1,0:T(8,128)(2,1)S(1)}, u32[]{:S(2)}, u32[]{:S(2)}) %collective-permute-start.12) | collective-permute-done | bytes 131104 | tf_op jit(solution)/shard_map/ppermute | solution.py:32
  48.7 1.3 %collective-permute-done.20.refs_14_ = bf16[256,256]{1,0:T(8,128)(2,1)S(1)} collective-permute-done((bf16[256,256]{1,0:T(8,128)(2,1)S(1)}, bf16[256,256]{1,0:T(8,128)(2,1)S(1)}, u32[]{:S(2)}, u32[]{:S(2)}) %collective-permute-start.20) | collective-permute-done | bytes 131104 | tf_op jit(solution)/shard_map/ppermute | solution.py:32
  50.0 3.4 %copy-done.2 = bf16[2048,2048]{1,0:T(8,128)(2,1)S(1)} copy-done((bf16[2048,2048]{1,0:T(8,128)(2,1)S(1)}, bf16[2048,2048]{1,0:T(8,128)(2,1)}, u32[]{:S(2)}) %copy-start.2) | copy-done | bytes 8388632
  53.4 7.2 %score.1 = f32[2048,512]{1,0:T(8,128)} custom-call(bf16[2048,2048]{1,0:T(8,128)(2,1)S(1)} %copy-done.2, bf16[256,256]{1,0:T(8,128)(2,1)S(1)} %condition.1.refs_1_, bf16[256,256]{1,0:T(8,128)(2,1)S(1)} %collective-permute-done.8.refs_2_, bf16[256,256]{1,0:T(8,128)(2,1)S(1)} %collective-permute-done.9.refs_3_, ...), custom_call_target="tpu_custom_call" | custom-call | flops 4294967296 | bytes 16777216 | tf_op jit(solution)/shard_map/score/pallas_call | solution.py:135
  (22 shorter events, 0.1 us)
Async XLA Ops:
  0.0 23.3 %collective-permute-start.7 = (bf16[1,2048,128]{2,1,0:T(8,128)(2,1)}, bf16[1,2048,128]{2,1,0:T(8,128)(2,1)S(1)}, u32[]{:S(2)}, u32[]{:S(2)}) collective-permute-start(bf16[1,2048,128]{2,1,0:T(8,128)(2,1)} %refs_8_.1), channel_id=1, source_target_pairs={{1,0},{0,1},{3,2},{2,3},{5,4},{4,5},{7,6},{6,7},{9,8},{8,9},{11,10... | collective-permute-start | bytes 1572872 | tf_op jit(solution)/shard_map/ppermute | solution.py:32
  0.5 9.3 %collective-permute-start.2 = (bf16[2,16,2048]{2,1,0:T(8,128)(2,1)}, bf16[2,16,2048]{2,1,0:T(8,128)(2,1)S(1)}, u32[]{:S(2)}, u32[]{:S(2)}) collective-permute-start(bf16[2,16,2048]{2,1,0:T(8,128)(2,1)} %refs_0_.2), channel_id=1, source_target_pairs={{12,0},{13,1},{14,2},{15,3},{0,4},{1,5},{2,6},{3,7},{4,8},{5,9},{6... | collective-permute-start | bytes 393224 | tf_op jit(solution)/shard_map/ppermute | solution.py:32
  3.0 12.1 %collective-permute-start.1 = (bf16[2,16,2048]{2,1,0:T(8,128)(2,1)}, bf16[2,16,2048]{2,1,0:T(8,128)(2,1)S(1)}, u32[]{:S(2)}, u32[]{:S(2)}) collective-permute-start(bf16[2,16,2048]{2,1,0:T(8,128)(2,1)} %refs_0_.2), channel_id=1, source_target_pairs={{8,0},{9,1},{10,2},{11,3},{12,4},{13,5},{14,6},{15,7},{0,8},{1,9},... | collective-permute-start | bytes 393224 | tf_op jit(solution)/shard_map/ppermute | solution.py:32
  5.6 11.0 %collective-permute-start = (bf16[2,16,2048]{2,1,0:T(8,128)(2,1)}, bf16[2,16,2048]{2,1,0:T(8,128)(2,1)S(1)}, u32[]{:S(2)}, u32[]{:S(2)}) collective-permute-start(bf16[2,16,2048]{2,1,0:T(8,128)(2,1)} %refs_0_.2), channel_id=1, source_target_pairs={{4,0},{5,1},{6,2},{7,3},{8,4},{9,5},{10,6},{11,7},{12,8},{13,9},{1... | collective-permute-start | bytes 393224 | tf_op jit(solution)/shard_map/ppermute | solution.py:32
  7.0 10.2 %collective-permute-start.3 = (bf16[2,16,2048]{2,1,0:T(8,128)(2,1)}, bf16[2,16,2048]{2,1,0:T(8,128)(2,1)S(1)}, u32[]{:S(2)}, u32[]{:S(2)}) collective-permute-start(bf16[2,16,2048]{2,1,0:T(8,128)(2,1)} %refs_0_.2), channel_id=1, source_target_pairs={{2,0},{3,1},{0,2},{1,3},{6,4},{7,5},{4,6},{5,7},{10,8},{11,9},{8,1... | collective-permute-start | bytes 393224 | tf_op jit(solution)/shard_map/ppermute | solution.py:32
  9.7 7.4 %collective-permute-start.6 = (bf16[2,16,2048]{2,1,0:T(8,128)(2,1)S(1)}, bf16[2,16,2048]{2,1,0:T(8,128)(2,1)S(1)}, u32[]{:S(2)}, u32[]{:S(2)}) collective-permute-start(bf16[2,16,2048]{2,1,0:T(8,128)(2,1)S(1)} %collective-permute-done.2.refs_3_), channel_id=1, source_target_pairs={{2,0},{3,1},{0,2},{1,3},{6,4},{7,5},{4,6},{5,7},{10,8},{11,9},{8,1... | collective-permute-start | bytes 393224 | tf_op jit(solution)/shard_map/ppermute | solution.py:32
  15.1 6.4 %collective-permute-start.5 = (bf16[2,16,2048]{2,1,0:T(8,128)(2,1)S(1)}, bf16[2,16,2048]{2,1,0:T(8,128)(2,1)S(1)}, u32[]{:S(2)}, u32[]{:S(2)}) collective-permute-start(bf16[2,16,2048]{2,1,0:T(8,128)(2,1)S(1)} %collective-permute-done.1.refs_2_), channel_id=1, source_target_pairs={{2,0},{3,1},{0,2},{1,3},{6,4},{7,5},{4,6},{5,7},{10,8},{11,9},{8,1... | collective-permute-start | bytes 393224 | tf_op jit(solution)/shard_map/ppermute | solution.py:32
  16.6 6.7 %collective-permute-start.4 = (bf16[2,16,2048]{2,1,0:T(8,128)(2,1)S(1)}, bf16[2,16,2048]{2,1,0:T(8,128)(2,1)S(1)}, u32[]{:S(2)}, u32[]{:S(2)}) collective-permute-start(bf16[2,16,2048]{2,1,0:T(8,128)(2,1)S(1)} %collective-permute-done.refs_1_), channel_id=1, source_target_pairs={{2,0},{3,1},{0,2},{1,3},{6,4},{7,5},{4,6},{5,7},{10,8},{11,9},{8,1... | collective-permute-start | bytes 393224 | tf_op jit(solution)/shard_map/ppermute | solution.py:32
  23.3 1.0 %copy-start = (bf16[1,2048,128]{2,1,0:T(8,128)(2,1)S(1)}, bf16[1,2048,128]{2,1,0:T(8,128)(2,1)}, u32[]{:S(2)}) copy-start(bf16[1,2048,128]{2,1,0:T(8,128)(2,1)} %refs_8_.1) | copy-start | bytes 1572868
  24.4 0.9 %copy-start.1 = (bf16[2,16,2048]{2,1,0:T(8,128)(2,1)S(1)}, bf16[2,16,2048]{2,1,0:T(8,128)(2,1)}, u32[]{:S(2)}) copy-start(bf16[2,16,2048]{2,1,0:T(8,128)(2,1)} %refs_0_.2) | copy-start | bytes 393220
  26.1 6.6 %collective-permute-start.11 = (bf16[256,256]{1,0:T(8,128)(2,1)S(1)}, bf16[256,256]{1,0:T(8,128)(2,1)S(1)}, u32[]{:S(2)}, u32[]{:S(2)}) collective-permute-start(bf16[256,256]{1,0:T(8,128)(2,1)S(1)} %condition.1.refs_1_), channel_id=1, source_target_pairs={{2,0},{3,1},{0,2},{1,3},{6,4},{7,5},{4,6},{5,7},{10,8},{11,9},{8,1... | collective-permute-start | bytes 393224 | tf_op jit(solution)/shard_map/ppermute | solution.py:32
  27.6 8.3 %collective-permute-start.10 = (bf16[256,256]{1,0:T(8,128)(2,1)S(1)}, bf16[256,256]{1,0:T(8,128)(2,1)S(1)}, u32[]{:S(2)}, u32[]{:S(2)}) collective-permute-start(bf16[256,256]{1,0:T(8,128)(2,1)S(1)} %condition.1.refs_1_), channel_id=1, source_target_pairs={{12,0},{13,1},{14,2},{15,3},{0,4},{1,5},{2,6},{3,7},{4,8},{5,9},{6... | collective-permute-start | bytes 393224 | tf_op jit(solution)/shard_map/ppermute | solution.py:32
  29.1 6.8 %collective-permute-start.15 = (bf16[256,256]{1,0:T(8,128)(2,1)S(1)}, bf16[256,256]{1,0:T(8,128)(2,1)S(1)}, u32[]{:S(2)}, u32[]{:S(2)}) collective-permute-start(bf16[256,256]{1,0:T(8,128)(2,1)S(1)} %condition.1.refs_1_), channel_id=1, source_target_pairs={{1,0},{0,1},{3,2},{2,3},{5,4},{4,5},{7,6},{6,7},{9,8},{8,9},{11,10... | collective-permute-start | bytes 393224 | tf_op jit(solution)/shard_map/ppermute | solution.py:32
  29.1 11.3 %collective-permute-start.9 = (bf16[256,256]{1,0:T(8,128)(2,1)S(1)}, bf16[256,256]{1,0:T(8,128)(2,1)S(1)}, u32[]{:S(2)}, u32[]{:S(2)}) collective-permute-start(bf16[256,256]{1,0:T(8,128)(2,1)S(1)} %condition.1.refs_1_), channel_id=1, source_target_pairs={{8,0},{9,1},{10,2},{11,3},{12,4},{13,5},{14,6},{15,7},{0,8},{1,9},... | collective-permute-start | bytes 393224 | tf_op jit(solution)/shard_map/ppermute | solution.py:32
  32.3 8.7 %collective-permute-start.8 = (bf16[256,256]{1,0:T(8,128)(2,1)S(1)}, bf16[256,256]{1,0:T(8,128)(2,1)S(1)}, u32[]{:S(2)}, u32[]{:S(2)}) collective-permute-start(bf16[256,256]{1,0:T(8,128)(2,1)S(1)} %condition.1.refs_1_), channel_id=1, source_target_pairs={{4,0},{5,1},{6,2},{7,3},{8,4},{9,5},{10,6},{11,7},{12,8},{13,9},{1... | collective-permute-start | bytes 393224 | tf_op jit(solution)/shard_map/ppermute | solution.py:32
  32.6 9.8 %collective-permute-start.19 = (bf16[256,256]{1,0:T(8,128)(2,1)S(1)}, bf16[256,256]{1,0:T(8,128)(2,1)S(1)}, u32[]{:S(2)}, u32[]{:S(2)}) collective-permute-start(bf16[256,256]{1,0:T(8,128)(2,1)S(1)} %collective-permute-done.11.refs_5_), channel_id=1, source_target_pairs={{1,0},{0,1},{3,2},{2,3},{5,4},{4,5},{7,6},{6,7},{9,8},{8,9},{11,10... | collective-permute-start | bytes 393224 | tf_op jit(solution)/shard_map/ppermute | solution.py:32
  35.9 6.6 %collective-permute-start.18 = (bf16[256,256]{1,0:T(8,128)(2,1)S(1)}, bf16[256,256]{1,0:T(8,128)(2,1)S(1)}, u32[]{:S(2)}, u32[]{:S(2)}) collective-permute-start(bf16[256,256]{1,0:T(8,128)(2,1)S(1)} %collective-permute-done.10.refs_4_), channel_id=1, source_target_pairs={{1,0},{0,1},{3,2},{2,3},{5,4},{4,5},{7,6},{6,7},{9,8},{8,9},{11,10... | collective-permute-start | bytes 393224 | tf_op jit(solution)/shard_map/ppermute | solution.py:32
  35.9 7.1 %collective-permute-start.14 = (bf16[256,256]{1,0:T(8,128)(2,1)S(1)}, bf16[256,256]{1,0:T(8,128)(2,1)S(1)}, u32[]{:S(2)}, u32[]{:S(2)}) collective-permute-start(bf16[256,256]{1,0:T(8,128)(2,1)S(1)} %collective-permute-done.10.refs_4_), channel_id=1, source_target_pairs={{2,0},{3,1},{0,2},{1,3},{6,4},{7,5},{4,6},{5,7},{10,8},{11,9},{8,1... | collective-permute-start | bytes 393224 | tf_op jit(solution)/shard_map/ppermute | solution.py:32
  40.4 6.4 %collective-permute-start.13 = (bf16[256,256]{1,0:T(8,128)(2,1)S(1)}, bf16[256,256]{1,0:T(8,128)(2,1)S(1)}, u32[]{:S(2)}, u32[]{:S(2)}) collective-permute-start(bf16[256,256]{1,0:T(8,128)(2,1)S(1)} %collective-permute-done.9.refs_3_), channel_id=1, source_target_pairs={{2,0},{3,1},{0,2},{1,3},{6,4},{7,5},{4,6},{5,7},{10,8},{11,9},{8,1... | collective-permute-start | bytes 393224 | tf_op jit(solution)/shard_map/ppermute | solution.py:32
  41.1 7.6 %collective-permute-start.12 = (bf16[256,256]{1,0:T(8,128)(2,1)S(1)}, bf16[256,256]{1,0:T(8,128)(2,1)S(1)}, u32[]{:S(2)}, u32[]{:S(2)}) collective-permute-start(bf16[256,256]{1,0:T(8,128)(2,1)S(1)} %collective-permute-done.8.refs_2_), channel_id=1, source_target_pairs={{2,0},{3,1},{0,2},{1,3},{6,4},{7,5},{4,6},{5,7},{10,8},{11,9},{8,1... | collective-permute-start | bytes 393224 | tf_op jit(solution)/shard_map/ppermute | solution.py:32
  42.5 6.2 %collective-permute-start.17 = (bf16[256,256]{1,0:T(8,128)(2,1)S(1)}, bf16[256,256]{1,0:T(8,128)(2,1)S(1)}, u32[]{:S(2)}, u32[]{:S(2)}) collective-permute-start(bf16[256,256]{1,0:T(8,128)(2,1)S(1)} %collective-permute-done.9.refs_3_), channel_id=1, source_target_pairs={{1,0},{0,1},{3,2},{2,3},{5,4},{4,5},{7,6},{6,7},{9,8},{8,9},{11,10... | collective-permute-start | bytes 393224 | tf_op jit(solution)/shard_map/ppermute | solution.py:32
  42.5 6.2 %collective-permute-start.16 = (bf16[256,256]{1,0:T(8,128)(2,1)S(1)}, bf16[256,256]{1,0:T(8,128)(2,1)S(1)}, u32[]{:S(2)}, u32[]{:S(2)}) collective-permute-start(bf16[256,256]{1,0:T(8,128)(2,1)S(1)} %collective-permute-done.8.refs_2_), channel_id=1, source_target_pairs={{1,0},{0,1},{3,2},{2,3},{5,4},{4,5},{7,6},{6,7},{9,8},{8,9},{11,10... | collective-permute-start | bytes 393224 | tf_op jit(solution)/shard_map/ppermute | solution.py:32
  43.0 5.7 %collective-permute-start.22 = (bf16[256,256]{1,0:T(8,128)(2,1)S(1)}, bf16[256,256]{1,0:T(8,128)(2,1)S(1)}, u32[]{:S(2)}, u32[]{:S(2)}) collective-permute-start(bf16[256,256]{1,0:T(8,128)(2,1)S(1)} %collective-permute-done.14.refs_8_), channel_id=1, source_target_pairs={{1,0},{0,1},{3,2},{2,3},{5,4},{4,5},{7,6},{6,7},{9,8},{8,9},{11,10... | collective-permute-start | bytes 393224 | tf_op jit(solution)/shard_map/ppermute | solution.py:32
  46.8 1.9 %collective-permute-start.21 = (bf16[256,256]{1,0:T(8,128)(2,1)S(1)}, bf16[256,256]{1,0:T(8,128)(2,1)S(1)}, u32[]{:S(2)}, u32[]{:S(2)}) collective-permute-start(bf16[256,256]{1,0:T(8,128)(2,1)S(1)} %collective-permute-done.13.refs_7_), channel_id=1, source_target_pairs={{1,0},{0,1},{3,2},{2,3},{5,4},{4,5},{7,6},{6,7},{9,8},{8,9},{11,10... | collective-permute-start | bytes 393224 | tf_op jit(solution)/shard_map/ppermute | solution.py:32
  48.7 1.3 %collective-permute-start.20 = (bf16[256,256]{1,0:T(8,128)(2,1)S(1)}, bf16[256,256]{1,0:T(8,128)(2,1)S(1)}, u32[]{:S(2)}, u32[]{:S(2)}) collective-permute-start(bf16[256,256]{1,0:T(8,128)(2,1)S(1)} %collective-permute-done.12.refs_6_), channel_id=1, source_target_pairs={{1,0},{0,1},{3,2},{2,3},{5,4},{4,5},{7,6},{6,7},{9,8},{8,9},{11,10... | collective-permute-start | bytes 393224 | tf_op jit(solution)/shard_map/ppermute | solution.py:32
  50.0 3.4 %copy-start.2 = (bf16[2048,2048]{1,0:T(8,128)(2,1)S(1)}, bf16[2048,2048]{1,0:T(8,128)(2,1)}, u32[]{:S(2)}) copy-start(bf16[2048,2048]{1,0:T(8,128)(2,1)} %refs_0_.3) | copy-start | bytes 25165828

commit v2 on v1

v2 whole, which is shorter than its diff:
```python
import functools

import jax
import jax.numpy as jnp
from jax import lax
from jax.experimental import pallas as pl
from jax.experimental.pallas import tpu as pltpu
from jax.sharding import PartitionSpec as P

VMEM = pl.BlockSpec(memory_space=pltpu.VMEM)
ANY = pl.BlockSpec(memory_space=pl.ANY)


class Grid:
    def __init__(self, row_count):
        chips = row_count // 2
        self.near = 2
        self.far = chips // 2
        self.fars = [0] + sorted(range(1, self.far), key=lambda m: (m & 1, m))

    def swap(self, block, far, near, core):
        step = (far * self.near + near) * 2 + core
        pairs = [(row ^ step, row) for row in range(self.far * self.near * 2)]
        return lax.ppermute(block, "rows", pairs)

    def place(self):
        row = lax.axis_index("rows")
        chip = lax.div(row, 2)
        return lax.div(chip, self.near), lax.rem(chip, self.near), lax.rem(row, 2)


def flip(part, mask):
    return lax.bitwise_xor(part, jnp.int32(mask))


def columns(index, width):
    return pl.ds(pl.multiple_of(index * width, width), width)


def stage_kernel(count, *refs):
    sources, targets, sems = refs[:count], refs[count : 2 * count], refs[2 * count]
    copies = [
        pltpu.make_async_copy(source, target, sems.at[i]) for i, (source, target) in enumerate(zip(sources, targets))
    ]
    for copy in copies:
        copy.start()
    for copy in copies:
        copy.wait()


def stage(*arrays):
    size = sum(a.size * a.dtype.itemsize for a in arrays)
    return pl.pallas_call(
        functools.partial(stage_kernel, len(arrays)),
        out_shape=[pltpu.VMEM(a.shape, a.dtype) for a in arrays],
        in_specs=[ANY] * len(arrays),
        out_specs=[VMEM] * len(arrays),
        scratch_shapes=[pltpu.SemaphoreType.DMA((len(arrays),))],
        compiler_params=pltpu.CompilerParams(vmem_limit_bytes=4 << 20),
        cost_estimate=pl.CostEstimate(flops=0, bytes_accessed=2 * size, transcendentals=0),
        name="stage",
    )(*(pltpu.with_memory_space_constraint(a, pltpu.HBM) for a in arrays))


def condition_kernel(grid, *refs):
    query_refs = refs[: grid.far]
    fisher_refs = refs[grid.far : grid.far + 4]
    out_ref, sorted_ref, columns_ref = refs[grid.far + 4 :]
    far, near, core = grid.place()
    width = fisher_refs[0].shape[-1]
    for index, fisher_ref in enumerate(fisher_refs):
        place = flip(near, index // 2) * 2 + flip(core, index % 2)
        columns_ref[:, columns(place, width)] = fisher_ref[0]
    for mask, query_ref in zip(grid.fars, query_refs):
        sorted_ref[:, pl.ds(flip(far, mask), 1)] = query_ref[...][:, None]
    rows = sorted_ref[...].reshape(-1, sorted_ref.shape[-1])
    out_ref[...] = jnp.dot(rows, columns_ref[...], preferred_element_type=jnp.float32).astype(out_ref.dtype)


def condition(grid, queries, fishers):
    blocks, count, features = queries[0].shape
    width = fishers[0].shape[-1]
    return pl.pallas_call(
        functools.partial(condition_kernel, grid),
        out_shape=jax.ShapeDtypeStruct((blocks * grid.far * count, 4 * width), jnp.bfloat16),
        in_specs=[VMEM] * (grid.far + 4),
        out_specs=VMEM,
        scratch_shapes=[
            pltpu.VMEM((blocks, grid.far, count, features), jnp.bfloat16),
            pltpu.VMEM((features, 4 * width), jnp.bfloat16),
        ],
        compiler_params=pltpu.CompilerParams(vmem_limit_bytes=12 << 20),
        cost_estimate=pl.CostEstimate(flops=1 << 28, bytes_accessed=3 << 20, transcendentals=0),
        name="condition",
    )(*queries, *fishers)


def score_kernel(grid, tile, shape, masks, *refs):
    blocks, count, width = shape
    train_ref, part_refs = refs[0], refs[1 : 1 + len(masks)]
    out_ref, sorted_ref, tile_ref, sem = refs[1 + len(masks) :]
    far, near, core = grid.place()
    features = train_ref.shape[1]
    for (far_mask, near_mask, core_mask), part_ref in zip(masks, part_refs):
        group = flip(near, near_mask) * 2 + flip(core, core_mask)
        sorted_ref[:, :, pl.ds(group, 1), :, columns(flip(far, far_mask), width)] = part_ref[...].reshape(
            blocks, grid.far, 1, count, width
        )
    scale = 1.0 / features**0.5
    steps = train_ref.shape[0] // tile

    def copy(step, slot):
        return pltpu.make_async_copy(
            tile_ref.at[slot], out_ref.at[pl.ds(pl.multiple_of(step * tile, tile), tile)], sem.at[slot]
        )

    @pl.loop(0, steps)
    def _(step):
        slot = lax.rem(step, 2)

        @pl.when(step >= 2)
        def _():
            copy(step - 2, slot).wait()

        products = lax.dot_general(
            train_ref[pl.ds(pl.multiple_of(step * tile, tile), tile)],
            sorted_ref[...].reshape(-1, features),
            (((1,), (1,)), ((), ())),
            preferred_element_type=jnp.float32,
        )
        tile_ref[slot] = products * scale
        copy(step, slot).start()

    for step in range(max(steps - 2, 0), steps):
        copy(step, step % 2).wait()


def score(grid, train_feats, parts, blocks):
    rows, features = train_feats.shape
    queries, width = parts[0, 0, 0].shape
    count = queries // (blocks * grid.far)
    tile = 256
    return pl.pallas_call(
        functools.partial(score_kernel, grid, tile, (blocks, count, width), list(parts)),
        out_shape=jax.ShapeDtypeStruct((rows, 4 * queries), jnp.float32),
        in_specs=[VMEM] * (1 + len(parts)),
        out_specs=ANY,
        scratch_shapes=[
            pltpu.VMEM((blocks, grid.far, 4, count, features), jnp.bfloat16),
            pltpu.VMEM((2, tile, 4 * queries), jnp.float32),
            pltpu.SemaphoreType.DMA((2,)),
        ],
        compiler_params=pltpu.CompilerParams(vmem_limit_bytes=24 << 20),
        cost_estimate=pl.CostEstimate(
            flops=8 * rows * features * queries, bytes_accessed=16 << 20, transcendentals=0
        ),
        name="score",
    )(pltpu.with_memory_space_constraint(train_feats, pltpu.VMEM), *parts.values())


def two_level(grid, train_feats, queries, inverse_fisher):
    near_fisher = grid.swap(inverse_fisher, 0, 1, 0)
    core_fisher = grid.swap(inverse_fisher, 0, 0, 1)
    gathered = [grid.swap(queries, mask, 0, 0) for mask in grid.fars[1:]]
    staged = stage(train_feats, queries, inverse_fisher)
    near_fisher, gathered, staged = lax.optimization_barrier((near_fisher, gathered, staged))
    train_here, queries_here, fisher_here = staged
    both_fisher = grid.swap(near_fisher, 0, 0, 1)
    block = condition(grid, [queries_here, *gathered], [fisher_here, core_fisher, near_fisher, both_fisher])
    parts = {(0, 0, 0): block}
    for mask in grid.fars[1:]:
        parts[mask, 0, 0] = grid.swap(block, mask, 0, 0)
    for mask in grid.fars:
        parts[mask, 1, 0] = grid.swap(parts[mask, 0, 0], 0, 1, 0)
    for near in range(2):
        for mask in grid.fars:
            parts[mask, near, 1] = grid.swap(parts[mask, near, 0], 0, 0, 1)
    return score(grid, train_here, parts, queries.shape[0])


def one_level(train_feats, queries, inverse_fisher):
    group_count, group_width, _ = inverse_fisher.shape
    gathered = lax.all_gather(queries, "rows", axis=1, tiled=True)
    flattened = gathered.reshape(-1, group_count, group_width)
    part = jnp.einsum("qgk,gkc->qgc", flattened, inverse_fisher, preferred_element_type=jnp.float32)
    complete = lax.all_gather(part.astype(jnp.bfloat16), "rows", axis=2, tiled=True)
    conditioned = complete.reshape(flattened.shape[0], -1)
    products = lax.dot_general(
        train_feats, conditioned, (((1,), (1,)), ((), ())), preferred_element_type=jnp.float32
    )
    return products * (1.0 / train_feats.shape[1] ** 0.5)


def per_device(row_count, train_feats, queries, inverse_fisher):
    group_count, _, width = inverse_fisher.shape
    whole_tiles = group_count == 1 and width % 128 == 0 and queries.shape[1] % 16 == 0
    if row_count >= 8 and row_count & (row_count - 1) == 0 and whole_tiles and train_feats.shape[0] % 512 == 0:
        return two_level(Grid(row_count), train_feats, queries, inverse_fisher)
    return one_level(train_feats, queries, inverse_fisher)


def solution(mesh):
    placed = (P(("groups", "rows"), None), P(None, ("groups", "rows"), None), P(None, None, "rows"))
    return jax.shard_map(
        functools.partial(per_device, mesh.shape["rows"]),
        mesh=mesh,
        in_specs=placed,
        out_specs=P(("groups", "rows"), None),
        check_vma=False,
    )
```

time: 60.8 us -> 49.9 us (0.82)
  waiting for transfers between devices: 25.5 us -> 19.9 us
  local copies, waits for them, and re-layouts: 5.33 us -> 0 us
  starting transfers between devices: 21.7 us -> 17.9 us
  Pallas kernels: 7.97 us -> 11.5 us
    ppermute x23 -> x21, waiting for transfers between devices: 25.5 us -> 19.9 us  [swap(): return lax.ppermute(block, 'rows', pairs)]
    unnamed x6 -> x0, local copies, waits for them, and re-layouts: 5.33 us -> none
    ppermute x23 -> x21, starting transfers between devices: 21.7 us -> 17.9 us  [swap(): return lax.ppermute(block, 'rows', pairs)]
    pallas_call x0 -> x1, Pallas kernels: none -> 3.49 us  [stage(): pl.pallas_call(functools.partial(stage_kernel, len(arrays)), out_shape=[p...]
  transfers between devices with their start and end apart: 23 -> 21, of which waited for: 10 -> 8; matrix products, arithmetic and copies ran while one was open for 0% -> 0% of each run, Pallas kernels for 0% -> 7%
where the time goes in v2:
time: 49.9 us; the launch traced here: 49.4 us
  waiting for transfers between devices  19.9 us (40%)
  starting transfers between devices  17.9 us (36%)
  Pallas kernels  11.5 us (23%)
    ppermute x21, waiting for transfers between devices, swap(): return lax.ppermute(block, 'rows', pairs)  19.9 us
    ppermute x21, starting transfers between devices, swap(): return lax.ppermute(block, 'rows', pairs)  17.9 us
    pallas_call x1, Pallas kernels, score(): pl.pallas_call(functools.partial(score_kernel, grid, tile, (blocks, count...  7.04 us
    pallas_call x1, Pallas kernels, stage(): pl.pallas_call(functools.partial(stage_kernel, len(arrays)), out_shape=[p...  3.49 us
  transfers between devices with their start and end apart: 21, of which 8 were waited for; matrix products, arithmetic and copies ran while one was open for 0% of the time, Pallas kernels for 7%

profile of v2, /device:TPU:0, one launch (start us, length us, event | category | flops | bytes accessed | tf_op | source)
XLA Modules:
  0.0 49.4 jit_solution(10573118397005466646)
XLA Ops:
  0.0 3.0 %collective-permute-start = (bf16[1,2048,128]{2,1,0:T(8,128)(2,1)}, bf16[1,2048,128]{2,1,0:T(8,128)(2,1)S(1)}, u32[]{:S(2)}, u32[]{:S(2)}) collective-permute-start(bf16[1,2048,128]{2,1,0:T(8,128)(2,1)} %refs_2_.1), channel_id=1, source_target_pairs={{2,0},{3,1},{0,2},{1,3},{6,4},{7,5},{4,6},{5,7},{10,8},{11,9},{8,1... | collective-permute-start | bytes 1572872 | tf_op jit(solution)/shard_map/ppermute | solution.py:24
  3.0 1.6 %collective-permute-start.2 = (bf16[2,16,2048]{2,1,0:T(8,128)(2,1)}, bf16[2,16,2048]{2,1,0:T(8,128)(2,1)S(1)}, u32[]{:S(2)}, u32[]{:S(2)}) collective-permute-start(bf16[2,16,2048]{2,1,0:T(8,128)(2,1)} %refs_1_.1), channel_id=1, source_target_pairs={{4,0},{5,1},{6,2},{7,3},{0,4},{1,5},{2,6},{3,7},{12,8},{13,9},{14,... | collective-permute-start | bytes 393224 | tf_op jit(solution)/shard_map/ppermute | solution.py:24
  4.5 2.6 %collective-permute-start.1 = (bf16[2,16,2048]{2,1,0:T(8,128)(2,1)}, bf16[2,16,2048]{2,1,0:T(8,128)(2,1)S(1)}, u32[]{:S(2)}, u32[]{:S(2)}) collective-permute-start(bf16[2,16,2048]{2,1,0:T(8,128)(2,1)} %refs_1_.1), channel_id=1, source_target_pairs={{8,0},{9,1},{10,2},{11,3},{12,4},{13,5},{14,6},{15,7},{0,8},{1,9},... | collective-permute-start | bytes 393224 | tf_op jit(solution)/shard_map/ppermute | solution.py:24
  7.1 0.2 collective-permute-start.3
  7.4 3.5 %stage.1 = (bf16[2048,2048]{1,0:T(8,128)(2,1)S(1)}, bf16[2,16,2048]{2,1,0:T(8,128)(2,1)S(1)}, bf16[1,2048,128]{2,1,0:T(8,128)(2,1)S(1)}) custom-call(bf16[2048,2048]{1,0:T(8,128)(2,1)} %refs_0_.1, bf16[2,16,2048]{2,1,0:T(8,128)(2,1)} %refs_1_.1, bf16[1,2048,128]{2,1,0:T(8,128)(2,1)} %refs_2_.1), custom_call_target="tpu_custom_call" | custom-call | bytes 18087936 | tf_op jit(solution)/shard_map/stage/pallas_call | solution.py:53
  10.9 6.5 %collective-permute-done.1.refs_1_ = bf16[2,16,2048]{2,1,0:T(8,128)(2,1)S(1)} collective-permute-done((bf16[2,16,2048]{2,1,0:T(8,128)(2,1)}, bf16[2,16,2048]{2,1,0:T(8,128)(2,1)S(1)}, u32[]{:S(2)}, u32[]{:S(2)}) %collective-permute-start.1) | collective-permute-done | bytes 131104 | tf_op jit(solution)/shard_map/ppermute | solution.py:24
  17.4 0.0 collective-permute-done.refs_6_
  17.4 0.0 collective-permute-start.5
  17.4 0.0 collective-permute-done.4.refs_5_
  17.4 1.9 %collective-permute-done.5.refs_7_ = bf16[1,2048,128]{2,1,0:T(8,128)(2,1)S(1)} collective-permute-done((bf16[1,2048,128]{2,1,0:T(8,128)(2,1)S(1)}, bf16[1,2048,128]{2,1,0:T(8,128)(2,1)S(1)}, u32[]{:S(2)}, u32[]{:S(2)}) %collective-permute-start.5) | collective-permute-done | bytes 524320 | tf_op jit(solution)/shard_map/ppermute | solution.py:24
  19.3 1.0 %condition.1.refs_1_ = bf16[128,512]{1,0:T(8,128)(2,1)S(1)} custom-call(bf16[2,16,2048]{2,1,0:T(8,128)(2,1)S(1)} %get-tuple-element.19.refs_0_, bf16[2,16,2048]{2,1,0:T(8,128)(2,1)S(1)} %collective-permute-done.1.refs_1_, bf16[2,16,2048]{2,1,0:T(8,128)(2,1)S(1)} %collective-permute-done.2.refs_2_, bf16[2,16,2048]{2,1,0:T(8,128)(2,1)S(1)} %collective-permute-done.3.refs_3_, ...), custom_call_target="tpu_custom_call" | custom-call | flops 268435456 | bytes 3145728 | tf_op jit(solution)/shard_map/condition/pallas_call | solution.py:83
  20.3 0.6 %collective-permute-start.9 = (bf16[128,512]{1,0:T(8,128)(2,1)S(1)}, bf16[128,512]{1,0:T(8,128)(2,1)S(1)}, u32[]{:S(2)}, u32[]{:S(2)}) collective-permute-start(bf16[128,512]{1,0:T(8,128)(2,1)S(1)} %condition.1.refs_1_), channel_id=1, source_target_pairs={{2,0},{3,1},{0,2},{1,3},{6,4},{7,5},{4,6},{5,7},{10,8},{11,9},{8,1... | collective-permute-start | bytes 393224 | tf_op jit(solution)/shard_map/ppermute | solution.py:24
  20.9 2.5 %collective-permute-start.8 = (bf16[128,512]{1,0:T(8,128)(2,1)S(1)}, bf16[128,512]{1,0:T(8,128)(2,1)S(1)}, u32[]{:S(2)}, u32[]{:S(2)}) collective-permute-start(bf16[128,512]{1,0:T(8,128)(2,1)S(1)} %condition.1.refs_1_), channel_id=1, source_target_pairs={{12,0},{13,1},{14,2},{15,3},{8,4},{9,5},{10,6},{11,7},{4,8},{5,9},... | collective-permute-start | bytes 393224 | tf_op jit(solution)/shard_map/ppermute | solution.py:24
  23.4 1.0 %collective-permute-start.7 = (bf16[128,512]{1,0:T(8,128)(2,1)S(1)}, bf16[128,512]{1,0:T(8,128)(2,1)S(1)}, u32[]{:S(2)}, u32[]{:S(2)}) collective-permute-start(bf16[128,512]{1,0:T(8,128)(2,1)S(1)} %condition.1.refs_1_), channel_id=1, source_target_pairs={{4,0},{5,1},{6,2},{7,3},{0,4},{1,5},{2,6},{3,7},{12,8},{13,9},{14,... | collective-permute-start | bytes 393224 | tf_op jit(solution)/shard_map/ppermute | solution.py:24
  24.4 0.9 %collective-permute-start.6 = (bf16[128,512]{1,0:T(8,128)(2,1)S(1)}, bf16[128,512]{1,0:T(8,128)(2,1)S(1)}, u32[]{:S(2)}, u32[]{:S(2)}) collective-permute-start(bf16[128,512]{1,0:T(8,128)(2,1)S(1)} %condition.1.refs_1_), channel_id=1, source_target_pairs={{8,0},{9,1},{10,2},{11,3},{12,4},{13,5},{14,6},{15,7},{0,8},{1,9},... | collective-permute-start | bytes 393224 | tf_op jit(solution)/shard_map/ppermute | solution.py:24
  25.3 0.6 %collective-permute-done.9.refs_5_ = bf16[128,512]{1,0:T(8,128)(2,1)S(1)} collective-permute-done((bf16[128,512]{1,0:T(8,128)(2,1)S(1)}, bf16[128,512]{1,0:T(8,128)(2,1)S(1)}, u32[]{:S(2)}, u32[]{:S(2)}) %collective-permute-start.9) | collective-permute-done | bytes 131104 | tf_op jit(solution)/shard_map/ppermute | solution.py:24
  25.9 0.0 collective-permute-start.17
  25.9 3.1 %collective-permute-done.8.refs_4_ = bf16[128,512]{1,0:T(8,128)(2,1)S(1)} collective-permute-done((bf16[128,512]{1,0:T(8,128)(2,1)S(1)}, bf16[128,512]{1,0:T(8,128)(2,1)S(1)}, u32[]{:S(2)}, u32[]{:S(2)}) %collective-permute-start.8) | collective-permute-done | bytes 131104 | tf_op jit(solution)/shard_map/ppermute | solution.py:24
  29.1 0.0 collective-permute-start.16
  29.1 0.0 collective-permute-done.13.refs_9_
  29.1 1.5 %collective-permute-start.12 = (bf16[128,512]{1,0:T(8,128)(2,1)S(1)}, bf16[128,512]{1,0:T(8,128)(2,1)S(1)}, u32[]{:S(2)}, u32[]{:S(2)}) collective-permute-start(bf16[128,512]{1,0:T(8,128)(2,1)S(1)} %collective-permute-done.8.refs_4_), channel_id=1, source_target_pairs={{2,0},{3,1},{0,2},{1,3},{6,4},{7,5},{4,6},{5,7},{10,8},{11,9},{8,1... | collective-permute-start | bytes 393224 | tf_op jit(solution)/shard_map/ppermute | solution.py:24
  30.6 0.5 %collective-permute-done.7.refs_3_ = bf16[128,512]{1,0:T(8,128)(2,1)S(1)} collective-permute-done((bf16[128,512]{1,0:T(8,128)(2,1)S(1)}, bf16[128,512]{1,0:T(8,128)(2,1)S(1)}, u32[]{:S(2)}, u32[]{:S(2)}) %collective-permute-start.7) | collective-permute-done | bytes 131104 | tf_op jit(solution)/shard_map/ppermute | solution.py:24
  31.1 1.5 %collective-permute-start.11 = (bf16[128,512]{1,0:T(8,128)(2,1)S(1)}, bf16[128,512]{1,0:T(8,128)(2,1)S(1)}, u32[]{:S(2)}, u32[]{:S(2)}) collective-permute-start(bf16[128,512]{1,0:T(8,128)(2,1)S(1)} %collective-permute-done.7.refs_3_), channel_id=1, source_target_pairs={{2,0},{3,1},{0,2},{1,3},{6,4},{7,5},{4,6},{5,7},{10,8},{11,9},{8,1... | collective-permute-start | bytes 393224 | tf_op jit(solution)/shard_map/ppermute | solution.py:24
  32.7 3.3 %collective-permute-done.6.refs_2_ = bf16[128,512]{1,0:T(8,128)(2,1)S(1)} collective-permute-done((bf16[128,512]{1,0:T(8,128)(2,1)S(1)}, bf16[128,512]{1,0:T(8,128)(2,1)S(1)}, u32[]{:S(2)}, u32[]{:S(2)}) %collective-permute-start.6) | collective-permute-done | bytes 131104 | tf_op jit(solution)/shard_map/ppermute | solution.py:24
  36.0 1.5 %collective-permute-start.10 = (bf16[128,512]{1,0:T(8,128)(2,1)S(1)}, bf16[128,512]{1,0:T(8,128)(2,1)S(1)}, u32[]{:S(2)}, u32[]{:S(2)}) collective-permute-start(bf16[128,512]{1,0:T(8,128)(2,1)S(1)} %collective-permute-done.6.refs_2_), channel_id=1, source_target_pairs={{2,0},{3,1},{0,2},{1,3},{6,4},{7,5},{4,6},{5,7},{10,8},{11,9},{8,1... | collective-permute-start | bytes 393224 | tf_op jit(solution)/shard_map/ppermute | solution.py:24
  37.5 0.0 collective-permute-done.17.refs_13_
  37.5 0.5 %collective-permute-start.14 = (bf16[128,512]{1,0:T(8,128)(2,1)S(1)}, bf16[128,512]{1,0:T(8,128)(2,1)S(1)}, u32[]{:S(2)}, u32[]{:S(2)}) collective-permute-start(bf16[128,512]{1,0:T(8,128)(2,1)S(1)} %collective-permute-done.6.refs_2_), channel_id=1, source_target_pairs={{1,0},{0,1},{3,2},{2,3},{5,4},{4,5},{7,6},{6,7},{9,8},{8,9},{11,10... | collective-permute-start | bytes 393224 | tf_op jit(solution)/shard_map/ppermute | solution.py:24
  38.0 0.1 collective-permute-start.20
  38.1 0.4 collective-permute-start.19
  38.5 2.4 %collective-permute-done.10.refs_6_ = bf16[128,512]{1,0:T(8,128)(2,1)S(1)} collective-permute-done((bf16[128,512]{1,0:T(8,128)(2,1)S(1)}, bf16[128,512]{1,0:T(8,128)(2,1)S(1)}, u32[]{:S(2)}, u32[]{:S(2)}) %collective-permute-start.10) | collective-permute-done | bytes 131104 | tf_op jit(solution)/shard_map/ppermute | solution.py:24
  41.0 1.3 %collective-permute-done.18.refs_14_ = bf16[128,512]{1,0:T(8,128)(2,1)S(1)} collective-permute-done((bf16[128,512]{1,0:T(8,128)(2,1)S(1)}, bf16[128,512]{1,0:T(8,128)(2,1)S(1)}, u32[]{:S(2)}, u32[]{:S(2)}) %collective-permute-start.18) | collective-permute-done | bytes 131104 | tf_op jit(solution)/shard_map/ppermute | solution.py:24
  42.3 7.0 %score.1 = f32[2048,512]{1,0:T(8,128)} custom-call(bf16[2048,2048]{1,0:T(8,128)(2,1)S(1)} %get-tuple-element.18.refs_0_, bf16[128,512]{1,0:T(8,128)(2,1)S(1)} %condition.1.refs_1_, bf16[128,512]{1,0:T(8,128)(2,1)S(1)} %collective-permute-done.6.refs_2_, bf16[128,512]{1,0:T(8,128)(2,1)S(1)} %collective-permute-done.7.refs_3_, ...), custom_call_target="tpu_custom_call" | custom-call | flops 4294967296 | bytes 16777216 | tf_op jit(solution)/shard_map/score/pallas_call | solution.py:143
  (13 shorter events, 0.0 us)
Async XLA Ops:
  0.0 17.4 %collective-permute-start = (bf16[1,2048,128]{2,1,0:T(8,128)(2,1)}, bf16[1,2048,128]{2,1,0:T(8,128)(2,1)S(1)}, u32[]{:S(2)}, u32[]{:S(2)}) collective-permute-start(bf16[1,2048,128]{2,1,0:T(8,128)(2,1)} %refs_2_.1), channel_id=1, source_target_pairs={{2,0},{3,1},{0,2},{1,3},{6,4},{7,5},{4,6},{5,7},{10,8},{11,9},{8,1... | collective-permute-start | bytes 1572872 | tf_op jit(solution)/shard_map/ppermute | solution.py:24
  3.0 7.9 %collective-permute-start.2 = (bf16[2,16,2048]{2,1,0:T(8,128)(2,1)}, bf16[2,16,2048]{2,1,0:T(8,128)(2,1)S(1)}, u32[]{:S(2)}, u32[]{:S(2)}) collective-permute-start(bf16[2,16,2048]{2,1,0:T(8,128)(2,1)} %refs_1_.1), channel_id=1, source_target_pairs={{4,0},{5,1},{6,2},{7,3},{0,4},{1,5},{2,6},{3,7},{12,8},{13,9},{14,... | collective-permute-start | bytes 393224 | tf_op jit(solution)/shard_map/ppermute | solution.py:24
  4.5 12.9 %collective-permute-start.1 = (bf16[2,16,2048]{2,1,0:T(8,128)(2,1)}, bf16[2,16,2048]{2,1,0:T(8,128)(2,1)S(1)}, u32[]{:S(2)}, u32[]{:S(2)}) collective-permute-start(bf16[2,16,2048]{2,1,0:T(8,128)(2,1)} %refs_1_.1), channel_id=1, source_target_pairs={{8,0},{9,1},{10,2},{11,3},{12,4},{13,5},{14,6},{15,7},{0,8},{1,9},... | collective-permute-start | bytes 393224 | tf_op jit(solution)/shard_map/ppermute | solution.py:24
  7.1 10.3 %collective-permute-start.3 = (bf16[2,16,2048]{2,1,0:T(8,128)(2,1)}, bf16[2,16,2048]{2,1,0:T(8,128)(2,1)S(1)}, u32[]{:S(2)}, u32[]{:S(2)}) collective-permute-start(bf16[2,16,2048]{2,1,0:T(8,128)(2,1)} %refs_1_.1), channel_id=1, source_target_pairs={{12,0},{13,1},{14,2},{15,3},{8,4},{9,5},{10,6},{11,7},{4,8},{5,9},... | collective-permute-start | bytes 393224 | tf_op jit(solution)/shard_map/ppermute | solution.py:24
  7.4 10.1 %collective-permute-start.4 = (bf16[1,2048,128]{2,1,0:T(8,128)(2,1)}, bf16[1,2048,128]{2,1,0:T(8,128)(2,1)S(1)}, u32[]{:S(2)}, u32[]{:S(2)}) collective-permute-start(bf16[1,2048,128]{2,1,0:T(8,128)(2,1)} %refs_2_.1), channel_id=1, source_target_pairs={{1,0},{0,1},{3,2},{2,3},{5,4},{4,5},{7,6},{6,7},{9,8},{8,9},{11,10... | collective-permute-start | bytes 1572872 | tf_op jit(solution)/shard_map/ppermute | solution.py:24
  17.4 1.9 %collective-permute-start.5 = (bf16[1,2048,128]{2,1,0:T(8,128)(2,1)S(1)}, bf16[1,2048,128]{2,1,0:T(8,128)(2,1)S(1)}, u32[]{:S(2)}, u32[]{:S(2)}) collective-permute-start(bf16[1,2048,128]{2,1,0:T(8,128)(2,1)S(1)} %collective-permute-done.refs_6_), channel_id=1, source_target_pairs={{1,0},{0,1},{3,2},{2,3},{5,4},{4,5},{7,6},{6,7},{9,8},{8,9},{11,10... | collective-permute-start | bytes 1572872 | tf_op jit(solution)/shard_map/ppermute | solution.py:24
  20.3 5.6 %collective-permute-start.9 = (bf16[128,512]{1,0:T(8,128)(2,1)S(1)}, bf16[128,512]{1,0:T(8,128)(2,1)S(1)}, u32[]{:S(2)}, u32[]{:S(2)}) collective-permute-start(bf16[128,512]{1,0:T(8,128)(2,1)S(1)} %condition.1.refs_1_), channel_id=1, source_target_pairs={{2,0},{3,1},{0,2},{1,3},{6,4},{7,5},{4,6},{5,7},{10,8},{11,9},{8,1... | collective-permute-start | bytes 393224 | tf_op jit(solution)/shard_map/ppermute | solution.py:24
  20.9 8.2 %collective-permute-start.8 = (bf16[128,512]{1,0:T(8,128)(2,1)S(1)}, bf16[128,512]{1,0:T(8,128)(2,1)S(1)}, u32[]{:S(2)}, u32[]{:S(2)}) collective-permute-start(bf16[128,512]{1,0:T(8,128)(2,1)S(1)} %condition.1.refs_1_), channel_id=1, source_target_pairs={{12,0},{13,1},{14,2},{15,3},{8,4},{9,5},{10,6},{11,7},{4,8},{5,9},... | collective-permute-start | bytes 393224 | tf_op jit(solution)/shard_map/ppermute | solution.py:24
  23.4 5.7 %collective-permute-start.13 = (bf16[128,512]{1,0:T(8,128)(2,1)S(1)}, bf16[128,512]{1,0:T(8,128)(2,1)S(1)}, u32[]{:S(2)}, u32[]{:S(2)}) collective-permute-start(bf16[128,512]{1,0:T(8,128)(2,1)S(1)} %condition.1.refs_1_), channel_id=1, source_target_pairs={{1,0},{0,1},{3,2},{2,3},{5,4},{4,5},{7,6},{6,7},{9,8},{8,9},{11,10... | collective-permute-start | bytes 393224 | tf_op jit(solution)/shard_map/ppermute | solution.py:24
  23.4 7.7 %collective-permute-start.7 = (bf16[128,512]{1,0:T(8,128)(2,1)S(1)}, bf16[128,512]{1,0:T(8,128)(2,1)S(1)}, u32[]{:S(2)}, u32[]{:S(2)}) collective-permute-start(bf16[128,512]{1,0:T(8,128)(2,1)S(1)} %condition.1.refs_1_), channel_id=1, source_target_pairs={{4,0},{5,1},{6,2},{7,3},{0,4},{1,5},{2,6},{3,7},{12,8},{13,9},{14,... | collective-permute-start | bytes 393224 | tf_op jit(solution)/shard_map/ppermute | solution.py:24
  24.4 11.6 %collective-permute-start.6 = (bf16[128,512]{1,0:T(8,128)(2,1)S(1)}, bf16[128,512]{1,0:T(8,128)(2,1)S(1)}, u32[]{:S(2)}, u32[]{:S(2)}) collective-permute-start(bf16[128,512]{1,0:T(8,128)(2,1)S(1)} %condition.1.refs_1_), channel_id=1, source_target_pairs={{8,0},{9,1},{10,2},{11,3},{12,4},{13,5},{14,6},{15,7},{0,8},{1,9},... | collective-permute-start | bytes 393224 | tf_op jit(solution)/shard_map/ppermute | solution.py:24
  25.9 11.6 %collective-permute-start.17 = (bf16[128,512]{1,0:T(8,128)(2,1)S(1)}, bf16[128,512]{1,0:T(8,128)(2,1)S(1)}, u32[]{:S(2)}, u32[]{:S(2)}) collective-permute-start(bf16[128,512]{1,0:T(8,128)(2,1)S(1)} %collective-permute-done.9.refs_5_), channel_id=1, source_target_pairs={{1,0},{0,1},{3,2},{2,3},{5,4},{4,5},{7,6},{6,7},{9,8},{8,9},{11,10... | collective-permute-start | bytes 393224 | tf_op jit(solution)/shard_map/ppermute | solution.py:24
  29.1 8.4 %collective-permute-start.16 = (bf16[128,512]{1,0:T(8,128)(2,1)S(1)}, bf16[128,512]{1,0:T(8,128)(2,1)S(1)}, u32[]{:S(2)}, u32[]{:S(2)}) collective-permute-start(bf16[128,512]{1,0:T(8,128)(2,1)S(1)} %collective-permute-done.8.refs_4_), channel_id=1, source_target_pairs={{1,0},{0,1},{3,2},{2,3},{5,4},{4,5},{7,6},{6,7},{9,8},{8,9},{11,10... | collective-permute-start | bytes 393224 | tf_op jit(solution)/shard_map/ppermute | solution.py:24
  29.1 8.9 %collective-permute-start.12 = (bf16[128,512]{1,0:T(8,128)(2,1)S(1)}, bf16[128,512]{1,0:T(8,128)(2,1)S(1)}, u32[]{:S(2)}, u32[]{:S(2)}) collective-permute-start(bf16[128,512]{1,0:T(8,128)(2,1)S(1)} %collective-permute-done.8.refs_4_), channel_id=1, source_target_pairs={{2,0},{3,1},{0,2},{1,3},{6,4},{7,5},{4,6},{5,7},{10,8},{11,9},{8,1... | collective-permute-start | bytes 393224 | tf_op jit(solution)/shard_map/ppermute | solution.py:24
  31.1 6.9 %collective-permute-start.11 = (bf16[128,512]{1,0:T(8,128)(2,1)S(1)}, bf16[128,512]{1,0:T(8,128)(2,1)S(1)}, u32[]{:S(2)}, u32[]{:S(2)}) collective-permute-start(bf16[128,512]{1,0:T(8,128)(2,1)S(1)} %collective-permute-done.7.refs_3_), channel_id=1, source_target_pairs={{2,0},{3,1},{0,2},{1,3},{6,4},{7,5},{4,6},{5,7},{10,8},{11,9},{8,1... | collective-permute-start | bytes 393224 | tf_op jit(solution)/shard_map/ppermute | solution.py:24
  36.0 5.0 %collective-permute-start.10 = (bf16[128,512]{1,0:T(8,128)(2,1)S(1)}, bf16[128,512]{1,0:T(8,128)(2,1)S(1)}, u32[]{:S(2)}, u32[]{:S(2)}) collective-permute-start(bf16[128,512]{1,0:T(8,128)(2,1)S(1)} %collective-permute-done.6.refs_2_), channel_id=1, source_target_pairs={{2,0},{3,1},{0,2},{1,3},{6,4},{7,5},{4,6},{5,7},{10,8},{11,9},{8,1... | collective-permute-start | bytes 393224 | tf_op jit(solution)/shard_map/ppermute | solution.py:24
  37.5 3.5 %collective-permute-start.15 = (bf16[128,512]{1,0:T(8,128)(2,1)S(1)}, bf16[128,512]{1,0:T(8,128)(2,1)S(1)}, u32[]{:S(2)}, u32[]{:S(2)}) collective-permute-start(bf16[128,512]{1,0:T(8,128)(2,1)S(1)} %collective-permute-done.7.refs_3_), channel_id=1, source_target_pairs={{1,0},{0,1},{3,2},{2,3},{5,4},{4,5},{7,6},{6,7},{9,8},{8,9},{11,10... | collective-permute-start | bytes 393224 | tf_op jit(solution)/shard_map/ppermute | solution.py:24
  37.5 3.5 %collective-permute-start.14 = (bf16[128,512]{1,0:T(8,128)(2,1)S(1)}, bf16[128,512]{1,0:T(8,128)(2,1)S(1)}, u32[]{:S(2)}, u32[]{:S(2)}) collective-permute-start(bf16[128,512]{1,0:T(8,128)(2,1)S(1)} %collective-permute-done.6.refs_2_), channel_id=1, source_target_pairs={{1,0},{0,1},{3,2},{2,3},{5,4},{4,5},{7,6},{6,7},{9,8},{8,9},{11,10... | collective-permute-start | bytes 393224 | tf_op jit(solution)/shard_map/ppermute | solution.py:24
  38.0 3.0 %collective-permute-start.20 = (bf16[128,512]{1,0:T(8,128)(2,1)S(1)}, bf16[128,512]{1,0:T(8,128)(2,1)S(1)}, u32[]{:S(2)}, u32[]{:S(2)}) collective-permute-start(bf16[128,512]{1,0:T(8,128)(2,1)S(1)} %collective-permute-done.12.refs_8_), channel_id=1, source_target_pairs={{1,0},{0,1},{3,2},{2,3},{5,4},{4,5},{7,6},{6,7},{9,8},{8,9},{11,10... | collective-permute-start | bytes 393224 | tf_op jit(solution)/shard_map/ppermute | solution.py:24
  38.1 2.9 %collective-permute-start.19 = (bf16[128,512]{1,0:T(8,128)(2,1)S(1)}, bf16[128,512]{1,0:T(8,128)(2,1)S(1)}, u32[]{:S(2)}, u32[]{:S(2)}) collective-permute-start(bf16[128,512]{1,0:T(8,128)(2,1)S(1)} %collective-permute-done.11.refs_7_), channel_id=1, source_target_pairs={{1,0},{0,1},{3,2},{2,3},{5,4},{4,5},{7,6},{6,7},{9,8},{8,9},{11,10... | collective-permute-start | bytes 393224 | tf_op jit(solution)/shard_map/ppermute | solution.py:24
  41.0 1.3 %collective-permute-start.18 = (bf16[128,512]{1,0:T(8,128)(2,1)S(1)}, bf16[128,512]{1,0:T(8,128)(2,1)S(1)}, u32[]{:S(2)}, u32[]{:S(2)}) collective-permute-start(bf16[128,512]{1,0:T(8,128)(2,1)S(1)} %collective-permute-done.10.refs_6_), channel_id=1, source_target_pairs={{1,0},{0,1},{3,2},{2,3},{5,4},{4,5},{7,6},{6,7},{9,8},{8,9},{11,10... | collective-permute-start | bytes 393224 | tf_op jit(solution)/shard_map/ppermute | solution.py:24

commit v3 on v2

--- a/solution.py
+++ b/solution.py
@@ -16,7 +16,7 @@
         chips = row_count // 2
         self.near = 2
         self.far = chips // 2
-        self.fars = [0] + sorted(range(1, self.far), key=lambda m: (m & 1, m))
+        self.fars = range(self.far)
 
     def swap(self, block, far, near, core):
         step = (far * self.near + near) * 2 + core
@@ -159,22 +159,34 @@
 
 
 def two_level(grid, train_feats, queries, inverse_fisher):
+    mirror, beside = grid.far - 1, 1
+    core_fisher = grid.swap(inverse_fisher, 0, 0, 1)
+    gathered = {0: queries}
+    gathered[beside] = grid.swap(queries, beside, 0, 0)
+    gathered[mirror] = grid.swap(queries, mirror, 0, 0)
     near_fisher = grid.swap(inverse_fisher, 0, 1, 0)
-    core_fisher = grid.swap(inverse_fisher, 0, 0, 1)
-    gathered = [grid.swap(queries, mask, 0, 0) for mask in grid.fars[1:]]
     staged = stage(train_feats, queries, inverse_fisher)
-    near_fisher, gathered, staged = lax.optimization_barrier((near_fisher, gathered, staged))
-    train_here, queries_here, fisher_here = staged
+    gathered, staged = lax.optimization_barrier((gathered, staged))
+    train_here, gathered[0], fisher_here = staged
+    gathered[mirror ^ beside] = grid.swap(gathered[mirror], beside, 0, 0)
+    near_fisher, gathered = lax.optimization_barrier((near_fisher, gathered))
     both_fisher = grid.swap(near_fisher, 0, 0, 1)
-    block = condition(grid, [queries_here, *gathered], [fisher_here, core_fisher, near_fisher, both_fisher])
+    block = condition(
+        grid, [gathered[mask] for mask in grid.fars], [fisher_here, core_fisher, near_fisher, both_fisher]
+    )
+
     parts = {(0, 0, 0): block}
+    parts[0, 0, 1] = grid.swap(block, 0, 0, 1)
+    parts[0, 1, 0] = grid.swap(block, 0, 1, 0)
+    parts[beside, 0, 0] = grid.swap(block, beside, 0, 0)
+    parts[mirror, 0, 0] = grid.swap(block, mirror, 0, 0)
+    parts[mirror ^ beside, 0, 0] = grid.swap(parts[mirror, 0, 0], beside, 0, 0)
     for mask in grid.fars[1:]:
-        parts[mask, 0, 0] = grid.swap(block, mask, 0, 0)
+        parts[mask, 0, 1] = grid.swap(parts[mask, 0, 0], 0, 0, 1)
+    for mask in (mirror ^ beside, mirror, beside):
+        parts[mask, 1, 0] = grid.swap(parts[mask, 0, 0], 0, 1, 0)
     for mask in grid.fars:
-        parts[mask, 1, 0] = grid.swap(parts[mask, 0, 0], 0, 1, 0)
-    for near in range(2):
-        for mask in grid.fars:
-            parts[mask, near, 1] = grid.swap(parts[mask, near, 0], 0, 0, 1)
+        parts[mask, 1, 1] = grid.swap(parts[mask, 1, 0], 0, 0, 1)
     return score(grid, train_here, parts, queries.shape[0])
 
 
@@ -194,7 +206,7 @@
 def per_device(row_count, train_feats, queries, inverse_fisher):
     group_count, _, width = inverse_fisher.shape
     whole_tiles = group_count == 1 and width % 128 == 0 and queries.shape[1] % 16 == 0
-    if row_count >= 8 and row_count & (row_count - 1) == 0 and whole_tiles and train_feats.shape[0] % 512 == 0:
+    if row_count == 16 and whole_tiles and train_feats.shape[0] % 512 == 0:
         return two_level(Grid(row_count), train_feats, queries, inverse_fisher)
     return one_level(train_feats, queries, inverse_fisher)
 

time: 49.9 us -> 50 us (level)
  waiting for transfers between devices: 19.9 us -> 21.8 us
  starting transfers between devices: 17.9 us -> 16.5 us
    ppermute x21, waiting for transfers between devices: 19.9 us -> 21.8 us  [swap(): return lax.ppermute(block, 'rows', pairs)]
    ppermute x21, starting transfers between devices: 17.9 us -> 16.5 us  [swap(): return lax.ppermute(block, 'rows', pairs)]
  transfers between devices with their start and end apart: 21 -> 21, of which waited for: 8 -> 10; matrix products, arithmetic and copies ran while one was open for 0% -> 0% of each run, Pallas kernels for 7% -> 7%
where the time goes in v3:
time: 50 us; the launch traced here: 49.8 us
  waiting for transfers between devices  21.8 us (44%)
  starting transfers between devices  16.5 us (33%)
  Pallas kernels  11.5 us (23%)
    ppermute x21, waiting for transfers between devices, swap(): return lax.ppermute(block, 'rows', pairs)  21.8 us
    ppermute x21, starting transfers between devices, swap(): return lax.ppermute(block, 'rows', pairs)  16.5 us
    pallas_call x1, Pallas kernels, score(): pl.pallas_call(functools.partial(score_kernel, grid, tile, (blocks, count...  7.04 us
    pallas_call x1, Pallas kernels, stage(): pl.pallas_call(functools.partial(stage_kernel, len(arrays)), out_shape=[p...  3.49 us
  transfers between devices with their start and end apart: 21, of which 10 were waited for; matrix products, arithmetic and copies ran while one was open for 0% of the time, Pallas kernels for 7%

profile of v3, /device:TPU:0, one launch (start us, length us, event | category | flops | bytes accessed | tf_op | source)
XLA Modules:
  0.0 49.8 jit_solution(13467051373886717549)
XLA Ops:
  0.0 3.0 %collective-permute-start.2 = (bf16[1,2048,128]{2,1,0:T(8,128)(2,1)}, bf16[1,2048,128]{2,1,0:T(8,128)(2,1)S(1)}, u32[]{:S(2)}, u32[]{:S(2)}) collective-permute-start(bf16[1,2048,128]{2,1,0:T(8,128)(2,1)} %refs_2_.1), channel_id=1, source_target_pairs={{2,0},{3,1},{0,2},{1,3},{6,4},{7,5},{4,6},{5,7},{10,8},{11,9},{8,1... | collective-permute-start | bytes 1572872 | tf_op jit(solution)/shard_map/ppermute | solution.py:24
  3.0 3.6 %collective-permute-start.1 = (bf16[2,16,2048]{2,1,0:T(8,128)(2,1)}, bf16[2,16,2048]{2,1,0:T(8,128)(2,1)S(1)}, u32[]{:S(2)}, u32[]{:S(2)}) collective-permute-start(bf16[2,16,2048]{2,1,0:T(8,128)(2,1)} %refs_1_.1), channel_id=1, source_target_pairs={{12,0},{13,1},{14,2},{15,3},{8,4},{9,5},{10,6},{11,7},{4,8},{5,9},... | collective-permute-start | bytes 393224 | tf_op jit(solution)/shard_map/ppermute | solution.py:24
  6.6 0.0 collective-permute-start
  6.6 3.5 %stage.1 = (bf16[2048,2048]{1,0:T(8,128)(2,1)S(1)}, bf16[2,16,2048]{2,1,0:T(8,128)(2,1)S(1)}, bf16[1,2048,128]{2,1,0:T(8,128)(2,1)S(1)}) custom-call(bf16[2048,2048]{1,0:T(8,128)(2,1)} %refs_0_.1, bf16[2,16,2048]{2,1,0:T(8,128)(2,1)} %refs_1_.1, bf16[1,2048,128]{2,1,0:T(8,128)(2,1)} %refs_2_.1), custom_call_target="tpu_custom_call" | custom-call | bytes 18087936 | tf_op jit(solution)/shard_map/stage/pallas_call | solution.py:53
  10.1 1.3 %collective-permute-done.1.refs_3_ = bf16[2,16,2048]{2,1,0:T(8,128)(2,1)S(1)} collective-permute-done((bf16[2,16,2048]{2,1,0:T(8,128)(2,1)}, bf16[2,16,2048]{2,1,0:T(8,128)(2,1)S(1)}, u32[]{:S(2)}, u32[]{:S(2)}) %collective-permute-start.1) | collective-permute-done | bytes 131104 | tf_op jit(solution)/shard_map/ppermute | solution.py:24
  11.4 1.5 %collective-permute-done.refs_1_ = bf16[2,16,2048]{2,1,0:T(8,128)(2,1)S(1)} collective-permute-done((bf16[2,16,2048]{2,1,0:T(8,128)(2,1)}, bf16[2,16,2048]{2,1,0:T(8,128)(2,1)S(1)}, u32[]{:S(2)}, u32[]{:S(2)}) %collective-permute-start) | collective-permute-done | bytes 131104 | tf_op jit(solution)/shard_map/ppermute | solution.py:24
  12.9 1.7 %collective-permute-start.3 = (bf16[2,16,2048]{2,1,0:T(8,128)(2,1)S(1)}, bf16[2,16,2048]{2,1,0:T(8,128)(2,1)S(1)}, u32[]{:S(2)}, u32[]{:S(2)}) collective-permute-start(bf16[2,16,2048]{2,1,0:T(8,128)(2,1)S(1)} %collective-permute-done.1.refs_3_), channel_id=1, source_target_pairs={{4,0},{5,1},{6,2},{7,3},{0,4},{1,5},{2,6},{3,7},{12,8},{13,9},{14,... | collective-permute-start | bytes 393224 | tf_op jit(solution)/shard_map/ppermute | solution.py:24
  14.6 0.0 collective-permute-start.4
  14.6 3.3 %collective-permute-done.3.refs_2_ = bf16[2,16,2048]{2,1,0:T(8,128)(2,1)S(1)} collective-permute-done((bf16[2,16,2048]{2,1,0:T(8,128)(2,1)S(1)}, bf16[2,16,2048]{2,1,0:T(8,128)(2,1)S(1)}, u32[]{:S(2)}, u32[]{:S(2)}) %collective-permute-start.3) | collective-permute-done | bytes 131104 | tf_op jit(solution)/shard_map/ppermute | solution.py:24
  17.9 0.0 collective-permute-done.2.refs_6_
  17.9 0.0 collective-permute-start.5
  17.9 0.0 collective-permute-done.4.refs_5_
  17.9 1.9 %collective-permute-done.5.refs_7_ = bf16[1,2048,128]{2,1,0:T(8,128)(2,1)S(1)} collective-permute-done((bf16[1,2048,128]{2,1,0:T(8,128)(2,1)S(1)}, bf16[1,2048,128]{2,1,0:T(8,128)(2,1)S(1)}, u32[]{:S(2)}, u32[]{:S(2)}) %collective-permute-start.5) | collective-permute-done | bytes 524320 | tf_op jit(solution)/shard_map/ppermute | solution.py:24
  19.8 1.0 %condition.1.refs_1_ = bf16[128,512]{1,0:T(8,128)(2,1)S(1)} custom-call(bf16[2,16,2048]{2,1,0:T(8,128)(2,1)S(1)} %get-tuple-element.25.refs_0_, bf16[2,16,2048]{2,1,0:T(8,128)(2,1)S(1)} %collective-permute-done.refs_1_, bf16[2,16,2048]{2,1,0:T(8,128)(2,1)S(1)} %collective-permute-done.3.refs_2_, bf16[2,16,2048]{2,1,0:T(8,128)(2,1)S(1)} %collective-permute-done.1.refs_3_, ...), custom_call_target="tpu_custom_call" | custom-call | flops 268435456 | bytes 3145728 | tf_op jit(solution)/shard_map/condition/pallas_call | solution.py:83
  20.8 2.2 %collective-permute-start.9 = (bf16[128,512]{1,0:T(8,128)(2,1)S(1)}, bf16[128,512]{1,0:T(8,128)(2,1)S(1)}, u32[]{:S(2)}, u32[]{:S(2)}) collective-permute-start(bf16[128,512]{1,0:T(8,128)(2,1)S(1)} %condition.1.refs_1_), channel_id=1, source_target_pairs={{12,0},{13,1},{14,2},{15,3},{8,4},{9,5},{10,6},{11,7},{4,8},{5,9},... | collective-permute-start | bytes 393224 | tf_op jit(solution)/shard_map/ppermute | solution.py:24
  22.9 0.5 %collective-permute-start.7 = (bf16[128,512]{1,0:T(8,128)(2,1)S(1)}, bf16[128,512]{1,0:T(8,128)(2,1)S(1)}, u32[]{:S(2)}, u32[]{:S(2)}) collective-permute-start(bf16[128,512]{1,0:T(8,128)(2,1)S(1)} %condition.1.refs_1_), channel_id=1, source_target_pairs={{2,0},{3,1},{0,2},{1,3},{6,4},{7,5},{4,6},{5,7},{10,8},{11,9},{8,1... | collective-permute-start | bytes 393224 | tf_op jit(solution)/shard_map/ppermute | solution.py:24
  23.4 5.6 %collective-permute-done.9.refs_5_ = bf16[128,512]{1,0:T(8,128)(2,1)S(1)} collective-permute-done((bf16[128,512]{1,0:T(8,128)(2,1)S(1)}, bf16[128,512]{1,0:T(8,128)(2,1)S(1)}, u32[]{:S(2)}, u32[]{:S(2)}) %collective-permute-start.9) | collective-permute-done | bytes 131104 | tf_op jit(solution)/shard_map/ppermute | solution.py:24
  29.1 1.8 %collective-permute-start.10 = (bf16[128,512]{1,0:T(8,128)(2,1)S(1)}, bf16[128,512]{1,0:T(8,128)(2,1)S(1)}, u32[]{:S(2)}, u32[]{:S(2)}) collective-permute-start(bf16[128,512]{1,0:T(8,128)(2,1)S(1)} %collective-permute-done.9.refs_5_), channel_id=1, source_target_pairs={{4,0},{5,1},{6,2},{7,3},{0,4},{1,5},{2,6},{3,7},{12,8},{13,9},{14,... | collective-permute-start | bytes 393224 | tf_op jit(solution)/shard_map/ppermute | solution.py:24
  30.9 0.5 %collective-permute-start.15 = (bf16[128,512]{1,0:T(8,128)(2,1)S(1)}, bf16[128,512]{1,0:T(8,128)(2,1)S(1)}, u32[]{:S(2)}, u32[]{:S(2)}) collective-permute-start(bf16[128,512]{1,0:T(8,128)(2,1)S(1)} %collective-permute-done.9.refs_5_), channel_id=1, source_target_pairs={{2,0},{3,1},{0,2},{1,3},{6,4},{7,5},{4,6},{5,7},{10,8},{11,9},{8,1... | collective-permute-start | bytes 393224 | tf_op jit(solution)/shard_map/ppermute | solution.py:24
  31.4 1.6 %collective-permute-start.16 = (bf16[128,512]{1,0:T(8,128)(2,1)S(1)}, bf16[128,512]{1,0:T(8,128)(2,1)S(1)}, u32[]{:S(2)}, u32[]{:S(2)}) collective-permute-start(bf16[128,512]{1,0:T(8,128)(2,1)S(1)} %collective-permute-done.8.refs_4_), channel_id=1, source_target_pairs={{2,0},{3,1},{0,2},{1,3},{6,4},{7,5},{4,6},{5,7},{10,8},{11,9},{8,1... | collective-permute-start | bytes 393224 | tf_op jit(solution)/shard_map/ppermute | solution.py:24
  33.0 0.2 collective-permute-start.11
  33.1 0.9 %collective-permute-done.10.refs_6_ = bf16[128,512]{1,0:T(8,128)(2,1)S(1)} collective-permute-done((bf16[128,512]{1,0:T(8,128)(2,1)S(1)}, bf16[128,512]{1,0:T(8,128)(2,1)S(1)}, u32[]{:S(2)}, u32[]{:S(2)}) %collective-permute-start.10) | collective-permute-done | bytes 131104 | tf_op jit(solution)/shard_map/ppermute | solution.py:24
  34.0 0.5 %collective-permute-start.14 = (bf16[128,512]{1,0:T(8,128)(2,1)S(1)}, bf16[128,512]{1,0:T(8,128)(2,1)S(1)}, u32[]{:S(2)}, u32[]{:S(2)}) collective-permute-start(bf16[128,512]{1,0:T(8,128)(2,1)S(1)} %collective-permute-done.10.refs_6_), channel_id=1, source_target_pairs={{2,0},{3,1},{0,2},{1,3},{6,4},{7,5},{4,6},{5,7},{10,8},{11,9},{8,1... | collective-permute-start | bytes 393224 | tf_op jit(solution)/shard_map/ppermute | solution.py:24
  34.5 2.6 %collective-permute-done.15.refs_11_ = bf16[128,512]{1,0:T(8,128)(2,1)S(1)} collective-permute-done((bf16[128,512]{1,0:T(8,128)(2,1)S(1)}, bf16[128,512]{1,0:T(8,128)(2,1)S(1)}, u32[]{:S(2)}, u32[]{:S(2)}) %collective-permute-start.15) | collective-permute-done | bytes 131104 | tf_op jit(solution)/shard_map/ppermute | solution.py:24
  37.2 0.5 %collective-permute-start.12 = (bf16[128,512]{1,0:T(8,128)(2,1)S(1)}, bf16[128,512]{1,0:T(8,128)(2,1)S(1)}, u32[]{:S(2)}, u32[]{:S(2)}) collective-permute-start(bf16[128,512]{1,0:T(8,128)(2,1)S(1)} %collective-permute-done.10.refs_6_), channel_id=1, source_target_pairs={{1,0},{0,1},{3,2},{2,3},{5,4},{4,5},{7,6},{6,7},{9,8},{8,9},{11,10... | collective-permute-start | bytes 393224 | tf_op jit(solution)/shard_map/ppermute | solution.py:24
  37.7 2.3 %collective-permute-done.16.refs_12_ = bf16[128,512]{1,0:T(8,128)(2,1)S(1)} collective-permute-done((bf16[128,512]{1,0:T(8,128)(2,1)S(1)}, bf16[128,512]{1,0:T(8,128)(2,1)S(1)}, u32[]{:S(2)}, u32[]{:S(2)}) %collective-permute-start.16) | collective-permute-done | bytes 131104 | tf_op jit(solution)/shard_map/ppermute | solution.py:24
  40.0 0.5 %collective-permute-start.18 = (bf16[128,512]{1,0:T(8,128)(2,1)S(1)}, bf16[128,512]{1,0:T(8,128)(2,1)S(1)}, u32[]{:S(2)}, u32[]{:S(2)}) collective-permute-start(bf16[128,512]{1,0:T(8,128)(2,1)S(1)} %collective-permute-done.16.refs_12_), channel_id=1, source_target_pairs={{1,0},{0,1},{3,2},{2,3},{5,4},{4,5},{7,6},{6,7},{9,8},{8,9},{11,10... | collective-permute-start | bytes 393224 | tf_op jit(solution)/shard_map/ppermute | solution.py:24
  40.5 0.9 %collective-permute-done.14.refs_10_ = bf16[128,512]{1,0:T(8,128)(2,1)S(1)} collective-permute-done((bf16[128,512]{1,0:T(8,128)(2,1)S(1)}, bf16[128,512]{1,0:T(8,128)(2,1)S(1)}, u32[]{:S(2)}, u32[]{:S(2)}) %collective-permute-start.14) | collective-permute-done | bytes 131104 | tf_op jit(solution)/shard_map/ppermute | solution.py:24
  41.5 0.0 collective-permute-start.19
  41.5 0.0 collective-permute-done.18.refs_14_
  41.5 1.3 %collective-permute-done.19.refs_15_ = bf16[128,512]{1,0:T(8,128)(2,1)S(1)} collective-permute-done((bf16[128,512]{1,0:T(8,128)(2,1)S(1)}, bf16[128,512]{1,0:T(8,128)(2,1)S(1)}, u32[]{:S(2)}, u32[]{:S(2)}) %collective-permute-start.19) | collective-permute-done | bytes 131104 | tf_op jit(solution)/shard_map/ppermute | solution.py:24
  42.8 7.0 %score.1 = f32[2048,512]{1,0:T(8,128)} custom-call(bf16[2048,2048]{1,0:T(8,128)(2,1)S(1)} %get-tuple-element.21.refs_0_, bf16[128,512]{1,0:T(8,128)(2,1)S(1)} %condition.1.refs_1_, bf16[128,512]{1,0:T(8,128)(2,1)S(1)} %collective-permute-done.6.refs_2_, bf16[128,512]{1,0:T(8,128)(2,1)S(1)} %collective-permute-done.7.refs_3_, ...), custom_call_target="tpu_custom_call" | custom-call | flops 4294967296 | bytes 16777216 | tf_op jit(solution)/shard_map/score/pallas_call | solution.py:143
  (15 shorter events, 0.0 us)
Async XLA Ops:
  0.0 14.6 %copy-start = (bf16[1,2048,128]{2,1,0:T(8,128)(2,1)S(1)}, bf16[1,2048,128]{2,1,0:T(8,128)(2,1)}, u32[]{:S(2)}) copy-start(bf16[1,2048,128]{2,1,0:T(8,128)(2,1)} %refs_2_.1) | copy-start | bytes 1572868
  0.0 17.9 %collective-permute-start.2 = (bf16[1,2048,128]{2,1,0:T(8,128)(2,1)}, bf16[1,2048,128]{2,1,0:T(8,128)(2,1)S(1)}, u32[]{:S(2)}, u32[]{:S(2)}) collective-permute-start(bf16[1,2048,128]{2,1,0:T(8,128)(2,1)} %refs_2_.1), channel_id=1, source_target_pairs={{2,0},{3,1},{0,2},{1,3},{6,4},{7,5},{4,6},{5,7},{10,8},{11,9},{8,1... | collective-permute-start | bytes 1572872 | tf_op jit(solution)/shard_map/ppermute | solution.py:24
  3.0 8.4 %collective-permute-start.1 = (bf16[2,16,2048]{2,1,0:T(8,128)(2,1)}, bf16[2,16,2048]{2,1,0:T(8,128)(2,1)S(1)}, u32[]{:S(2)}, u32[]{:S(2)}) collective-permute-start(bf16[2,16,2048]{2,1,0:T(8,128)(2,1)} %refs_1_.1), channel_id=1, source_target_pairs={{12,0},{13,1},{14,2},{15,3},{8,4},{9,5},{10,6},{11,7},{4,8},{5,9},... | collective-permute-start | bytes 393224 | tf_op jit(solution)/shard_map/ppermute | solution.py:24
  6.6 6.3 %collective-permute-start = (bf16[2,16,2048]{2,1,0:T(8,128)(2,1)}, bf16[2,16,2048]{2,1,0:T(8,128)(2,1)S(1)}, u32[]{:S(2)}, u32[]{:S(2)}) collective-permute-start(bf16[2,16,2048]{2,1,0:T(8,128)(2,1)} %refs_1_.1), channel_id=1, source_target_pairs={{4,0},{5,1},{6,2},{7,3},{0,4},{1,5},{2,6},{3,7},{12,8},{13,9},{14,... | collective-permute-start | bytes 393224 | tf_op jit(solution)/shard_map/ppermute | solution.py:24
  12.9 5.0 %collective-permute-start.3 = (bf16[2,16,2048]{2,1,0:T(8,128)(2,1)S(1)}, bf16[2,16,2048]{2,1,0:T(8,128)(2,1)S(1)}, u32[]{:S(2)}, u32[]{:S(2)}) collective-permute-start(bf16[2,16,2048]{2,1,0:T(8,128)(2,1)S(1)} %collective-permute-done.1.refs_3_), channel_id=1, source_target_pairs={{4,0},{5,1},{6,2},{7,3},{0,4},{1,5},{2,6},{3,7},{12,8},{13,9},{14,... | collective-permute-start | bytes 393224 | tf_op jit(solution)/shard_map/ppermute | solution.py:24
  14.6 3.3 %collective-permute-start.4 = (bf16[1,2048,128]{2,1,0:T(8,128)(2,1)S(1)}, bf16[1,2048,128]{2,1,0:T(8,128)(2,1)S(1)}, u32[]{:S(2)}, u32[]{:S(2)}) collective-permute-start(bf16[1,2048,128]{2,1,0:T(8,128)(2,1)S(1)} %copy-done), channel_id=1, source_target_pairs={{1,0},{0,1},{3,2},{2,3},{5,4},{4,5},{7,6},{6,7},{9,8},{8,9},{11,10... | collective-permute-start | bytes 1572872 | tf_op jit(solution)/shard_map/ppermute | solution.py:24
  17.9 1.9 %collective-permute-start.5 = (bf16[1,2048,128]{2,1,0:T(8,128)(2,1)S(1)}, bf16[1,2048,128]{2,1,0:T(8,128)(2,1)S(1)}, u32[]{:S(2)}, u32[]{:S(2)}) collective-permute-start(bf16[1,2048,128]{2,1,0:T(8,128)(2,1)S(1)} %collective-permute-done.2.refs_6_), channel_id=1, source_target_pairs={{1,0},{0,1},{3,2},{2,3},{5,4},{4,5},{7,6},{6,7},{9,8},{8,9},{11,10... | collective-permute-start | bytes 1572872 | tf_op jit(solution)/shard_map/ppermute | solution.py:24
  20.8 8.3 %collective-permute-start.9 = (bf16[128,512]{1,0:T(8,128)(2,1)S(1)}, bf16[128,512]{1,0:T(8,128)(2,1)S(1)}, u32[]{:S(2)}, u32[]{:S(2)}) collective-permute-start(bf16[128,512]{1,0:T(8,128)(2,1)S(1)} %condition.1.refs_1_), channel_id=1, source_target_pairs={{12,0},{13,1},{14,2},{15,3},{8,4},{9,5},{10,6},{11,7},{4,8},{5,9},... | collective-permute-start | bytes 393224 | tf_op jit(solution)/shard_map/ppermute | solution.py:24
  22.9 8.5 %collective-permute-start.8 = (bf16[128,512]{1,0:T(8,128)(2,1)S(1)}, bf16[128,512]{1,0:T(8,128)(2,1)S(1)}, u32[]{:S(2)}, u32[]{:S(2)}) collective-permute-start(bf16[128,512]{1,0:T(8,128)(2,1)S(1)} %condition.1.refs_1_), channel_id=1, source_target_pairs={{4,0},{5,1},{6,2},{7,3},{0,4},{1,5},{2,6},{3,7},{12,8},{13,9},{14,... | collective-permute-start | bytes 393224 | tf_op jit(solution)/shard_map/ppermute | solution.py:24
  22.9 8.5 %collective-permute-start.7 = (bf16[128,512]{1,0:T(8,128)(2,1)S(1)}, bf16[128,512]{1,0:T(8,128)(2,1)S(1)}, u32[]{:S(2)}, u32[]{:S(2)}) collective-permute-start(bf16[128,512]{1,0:T(8,128)(2,1)S(1)} %condition.1.refs_1_), channel_id=1, source_target_pairs={{2,0},{3,1},{0,2},{1,3},{6,4},{7,5},{4,6},{5,7},{10,8},{11,9},{8,1... | collective-permute-start | bytes 393224 | tf_op jit(solution)/shard_map/ppermute | solution.py:24
  23.4 9.5 %collective-permute-start.6 = (bf16[128,512]{1,0:T(8,128)(2,1)S(1)}, bf16[128,512]{1,0:T(8,128)(2,1)S(1)}, u32[]{:S(2)}, u32[]{:S(2)}) collective-permute-start(bf16[128,512]{1,0:T(8,128)(2,1)S(1)} %condition.1.refs_1_), channel_id=1, source_target_pairs={{1,0},{0,1},{3,2},{2,3},{5,4},{4,5},{7,6},{6,7},{9,8},{8,9},{11,10... | collective-permute-start | bytes 393224 | tf_op jit(solution)/shard_map/ppermute | solution.py:24
  29.1 5.0 %collective-permute-start.10 = (bf16[128,512]{1,0:T(8,128)(2,1)S(1)}, bf16[128,512]{1,0:T(8,128)(2,1)S(1)}, u32[]{:S(2)}, u32[]{:S(2)}) collective-permute-start(bf16[128,512]{1,0:T(8,128)(2,1)S(1)} %collective-permute-done.9.refs_5_), channel_id=1, source_target_pairs={{4,0},{5,1},{6,2},{7,3},{0,4},{1,5},{2,6},{3,7},{12,8},{13,9},{14,... | collective-permute-start | bytes 393224 | tf_op jit(solution)/shard_map/ppermute | solution.py:24
  30.9 6.3 %collective-permute-start.15 = (bf16[128,512]{1,0:T(8,128)(2,1)S(1)}, bf16[128,512]{1,0:T(8,128)(2,1)S(1)}, u32[]{:S(2)}, u32[]{:S(2)}) collective-permute-start(bf16[128,512]{1,0:T(8,128)(2,1)S(1)} %collective-permute-done.9.refs_5_), channel_id=1, source_target_pairs={{2,0},{3,1},{0,2},{1,3},{6,4},{7,5},{4,6},{5,7},{10,8},{11,9},{8,1... | collective-permute-start | bytes 393224 | tf_op jit(solution)/shard_map/ppermute | solution.py:24
  31.4 5.8 %collective-permute-start.13 = (bf16[128,512]{1,0:T(8,128)(2,1)S(1)}, bf16[128,512]{1,0:T(8,128)(2,1)S(1)}, u32[]{:S(2)}, u32[]{:S(2)}) collective-permute-start(bf16[128,512]{1,0:T(8,128)(2,1)S(1)} %collective-permute-done.9.refs_5_), channel_id=1, source_target_pairs={{1,0},{0,1},{3,2},{2,3},{5,4},{4,5},{7,6},{6,7},{9,8},{8,9},{11,10... | collective-permute-start | bytes 393224 | tf_op jit(solution)/shard_map/ppermute | solution.py:24
  31.4 8.6 %collective-permute-start.16 = (bf16[128,512]{1,0:T(8,128)(2,1)S(1)}, bf16[128,512]{1,0:T(8,128)(2,1)S(1)}, u32[]{:S(2)}, u32[]{:S(2)}) collective-permute-start(bf16[128,512]{1,0:T(8,128)(2,1)S(1)} %collective-permute-done.8.refs_4_), channel_id=1, source_target_pairs={{2,0},{3,1},{0,2},{1,3},{6,4},{7,5},{4,6},{5,7},{10,8},{11,9},{8,1... | collective-permute-start | bytes 393224 | tf_op jit(solution)/shard_map/ppermute | solution.py:24
  33.0 7.0 %collective-permute-start.11 = (bf16[128,512]{1,0:T(8,128)(2,1)S(1)}, bf16[128,512]{1,0:T(8,128)(2,1)S(1)}, u32[]{:S(2)}, u32[]{:S(2)}) collective-permute-start(bf16[128,512]{1,0:T(8,128)(2,1)S(1)} %collective-permute-done.8.refs_4_), channel_id=1, source_target_pairs={{1,0},{0,1},{3,2},{2,3},{5,4},{4,5},{7,6},{6,7},{9,8},{8,9},{11,10... | collective-permute-start | bytes 393224 | tf_op jit(solution)/shard_map/ppermute | solution.py:24
  34.0 7.4 %collective-permute-start.14 = (bf16[128,512]{1,0:T(8,128)(2,1)S(1)}, bf16[128,512]{1,0:T(8,128)(2,1)S(1)}, u32[]{:S(2)}, u32[]{:S(2)}) collective-permute-start(bf16[128,512]{1,0:T(8,128)(2,1)S(1)} %collective-permute-done.10.refs_6_), channel_id=1, source_target_pairs={{2,0},{3,1},{0,2},{1,3},{6,4},{7,5},{4,6},{5,7},{10,8},{11,9},{8,1... | collective-permute-start | bytes 393224 | tf_op jit(solution)/shard_map/ppermute | solution.py:24
  37.2 4.3 %collective-permute-start.17 = (bf16[128,512]{1,0:T(8,128)(2,1)S(1)}, bf16[128,512]{1,0:T(8,128)(2,1)S(1)}, u32[]{:S(2)}, u32[]{:S(2)}) collective-permute-start(bf16[128,512]{1,0:T(8,128)(2,1)S(1)} %collective-permute-done.7.refs_3_), channel_id=1, source_target_pairs={{1,0},{0,1},{3,2},{2,3},{5,4},{4,5},{7,6},{6,7},{9,8},{8,9},{11,10... | collective-permute-start | bytes 393224 | tf_op jit(solution)/shard_map/ppermute | solution.py:24
  37.2 4.3 %collective-permute-start.12 = (bf16[128,512]{1,0:T(8,128)(2,1)S(1)}, bf16[128,512]{1,0:T(8,128)(2,1)S(1)}, u32[]{:S(2)}, u32[]{:S(2)}) collective-permute-start(bf16[128,512]{1,0:T(8,128)(2,1)S(1)} %collective-permute-done.10.refs_6_), channel_id=1, source_target_pairs={{1,0},{0,1},{3,2},{2,3},{5,4},{4,5},{7,6},{6,7},{9,8},{8,9},{11,10... | collective-permute-start | bytes 393224 | tf_op jit(solution)/shard_map/ppermute | solution.py:24
  40.0 1.5 %collective-permute-start.20 = (bf16[128,512]{1,0:T(8,128)(2,1)S(1)}, bf16[128,512]{1,0:T(8,128)(2,1)S(1)}, u32[]{:S(2)}, u32[]{:S(2)}) collective-permute-start(bf16[128,512]{1,0:T(8,128)(2,1)S(1)} %collective-permute-done.15.refs_11_), channel_id=1, source_target_pairs={{1,0},{0,1},{3,2},{2,3},{5,4},{4,5},{7,6},{6,7},{9,8},{8,9},{11,10... | collective-permute-start | bytes 393224 | tf_op jit(solution)/shard_map/ppermute | solution.py:24
  40.0 1.5 %collective-permute-start.18 = (bf16[128,512]{1,0:T(8,128)(2,1)S(1)}, bf16[128,512]{1,0:T(8,128)(2,1)S(1)}, u32[]{:S(2)}, u32[]{:S(2)}) collective-permute-start(bf16[128,512]{1,0:T(8,128)(2,1)S(1)} %collective-permute-done.16.refs_12_), channel_id=1, source_target_pairs={{1,0},{0,1},{3,2},{2,3},{5,4},{4,5},{7,6},{6,7},{9,8},{8,9},{11,10... | collective-permute-start | bytes 393224 | tf_op jit(solution)/shard_map/ppermute | solution.py:24
  41.5 1.3 %collective-permute-start.19 = (bf16[128,512]{1,0:T(8,128)(2,1)S(1)}, bf16[128,512]{1,0:T(8,128)(2,1)S(1)}, u32[]{:S(2)}, u32[]{:S(2)}) collective-permute-start(bf16[128,512]{1,0:T(8,128)(2,1)S(1)} %collective-permute-done.14.refs_10_), channel_id=1, source_target_pairs={{1,0},{0,1},{3,2},{2,3},{5,4},{4,5},{7,6},{6,7},{9,8},{8,9},{11,10... | collective-permute-start | bytes 393224 | tf_op jit(solution)/shard_map/ppermute | solution.py:24

commit v4 on v3

--- a/solution.py
+++ b/solution.py
@@ -95,24 +95,43 @@
     )(*queries, *fishers)
 
 
-def score_kernel(grid, tile, shape, masks, *refs):
+def score_kernel(grid, tile, shape, mask, first, last, *refs):
     blocks, count, width = shape
-    train_ref, part_refs = refs[0], refs[1 : 1 + len(masks)]
-    out_ref, sorted_ref, tile_ref, sem = refs[1 + len(masks) :]
+    train_ref, part_refs, refs = refs[0], refs[1:5], refs[5:]
+    total_ref, refs = (None, refs) if first else (refs[0], refs[1:])
+    out_ref, sorted_ref, refs = refs[0], refs[1], refs[2:]
     far, near, core = grid.place()
     features = train_ref.shape[1]
-    for (far_mask, near_mask, core_mask), part_ref in zip(masks, part_refs):
-        group = flip(near, near_mask) * 2 + flip(core, core_mask)
-        sorted_ref[:, :, pl.ds(group, 1), :, columns(flip(far, far_mask), width)] = part_ref[...].reshape(
-            blocks, grid.far, 1, count, width
-        )
+    for index, part_ref in enumerate(part_refs):
+        group = flip(near, index // 2) * 2 + flip(core, index % 2)
+        sorted_ref[:, :, pl.ds(group, 1)] = part_ref[...].reshape(blocks, grid.far, 1, count, width)
     scale = 1.0 / features**0.5
     steps = train_ref.shape[0] // tile
 
+    def rows(step):
+        return pl.ds(pl.multiple_of(step * tile, tile), tile)
+
+    def products(step):
+        value = lax.dot_general(
+            train_ref[rows(step), columns(flip(far, mask), width)],
+            sorted_ref[...].reshape(-1, width),
+            (((1,), (1,)), ((), ())),
+            preferred_element_type=jnp.float32,
+        )
+        return value if first else total_ref[rows(step)] + value
+
+    if not last:
+
+        @pl.loop(0, steps)
+        def _(step):
+            out_ref[rows(step)] = products(step)
+
+        return
+
+    tile_ref, sem = refs
+
     def copy(step, slot):
-        return pltpu.make_async_copy(
-            tile_ref.at[slot], out_ref.at[pl.ds(pl.multiple_of(step * tile, tile), tile)], sem.at[slot]
-        )
+        return pltpu.make_async_copy(tile_ref.at[slot], out_ref.at[rows(step)], sem.at[slot])
 
     @pl.loop(0, steps)
     def _(step):
@@ -122,72 +141,84 @@
         def _():
             copy(step - 2, slot).wait()
 
-        products = lax.dot_general(
-            train_ref[pl.ds(pl.multiple_of(step * tile, tile), tile)],
-            sorted_ref[...].reshape(-1, features),
-            (((1,), (1,)), ((), ())),
-            preferred_element_type=jnp.float32,
-        )
-        tile_ref[slot] = products * scale
+        tile_ref[slot] = products(step) * scale
         copy(step, slot).start()
 
     for step in range(max(steps - 2, 0), steps):
         copy(step, step % 2).wait()
 
 
-def score(grid, train_feats, parts, blocks):
+def score(grid, train_feats, parts, total, mask, blocks, last):
     rows, features = train_feats.shape
-    queries, width = parts[0, 0, 0].shape
+    queries, width = parts[0].shape
     count = queries // (blocks * grid.far)
     tile = 256
+    first = total is None
+    totals = [] if first else [total]
+    shape = (rows, 4 * queries)
+    scratch = [pltpu.VMEM((blocks, grid.far, 4, count, width), jnp.bfloat16)]
+    if last:
+        scratch += [pltpu.VMEM((2, tile, 4 * queries), jnp.float32), pltpu.SemaphoreType.DMA((2,))]
     return pl.pallas_call(
-        functools.partial(score_kernel, grid, tile, (blocks, count, width), list(parts)),
-        out_shape=jax.ShapeDtypeStruct((rows, 4 * queries), jnp.float32),
-        in_specs=[VMEM] * (1 + len(parts)),
-        out_specs=ANY,
-        scratch_shapes=[
-            pltpu.VMEM((blocks, grid.far, 4, count, features), jnp.bfloat16),
-            pltpu.VMEM((2, tile, 4 * queries), jnp.float32),
-            pltpu.SemaphoreType.DMA((2,)),
-        ],
-        compiler_params=pltpu.CompilerParams(vmem_limit_bytes=24 << 20),
+        functools.partial(score_kernel, grid, tile, (blocks, count, width), mask, first, last),
+        out_shape=jax.ShapeDtypeStruct(shape, jnp.float32) if last else pltpu.VMEM(shape, jnp.float32),
+        in_specs=[VMEM] * (5 + len(totals)),
+        out_specs=ANY if last else VMEM,
+        scratch_shapes=scratch,
+        input_output_aliases={} if first or last else {5: 0},
+        compiler_params=pltpu.CompilerParams(vmem_limit_bytes=12 << 20),
         cost_estimate=pl.CostEstimate(
-            flops=8 * rows * features * queries, bytes_accessed=16 << 20, transcendentals=0
+            flops=8 * rows * width * queries, bytes_accessed=4 << 20, transcendentals=0
         ),
         name="score",
-    )(pltpu.with_memory_space_constraint(train_feats, pltpu.VMEM), *parts.values())
+    )(*(pltpu.with_memory_space_constraint(a, pltpu.VMEM) for a in (train_feats, *parts, *totals)))
 
 
 def two_level(grid, train_feats, queries, inverse_fisher):
     mirror, beside = grid.far - 1, 1
+    relayed = mirror ^ beside
     core_fisher = grid.swap(inverse_fisher, 0, 0, 1)
     gathered = {0: queries}
     gathered[beside] = grid.swap(queries, beside, 0, 0)
     gathered[mirror] = grid.swap(queries, mirror, 0, 0)
     near_fisher = grid.swap(inverse_fisher, 0, 1, 0)
     staged = stage(train_feats, queries, inverse_fisher)
-    gathered, staged = lax.optimization_barrier((gathered, staged))
+    gathered[mirror], staged = lax.optimization_barrier((gathered[mirror], staged))
     train_here, gathered[0], fisher_here = staged
-    gathered[mirror ^ beside] = grid.swap(gathered[mirror], beside, 0, 0)
+    gathered[relayed] = grid.swap(gathered[mirror], beside, 0, 0)
     near_fisher, gathered = lax.optimization_barrier((near_fisher, gathered))
     both_fisher = grid.swap(near_fisher, 0, 0, 1)
     block = condition(
         grid, [gathered[mask] for mask in grid.fars], [fisher_here, core_fisher, near_fisher, both_fisher]
     )
 
+    blocks = queries.shape[0]
+
+    def add(total, mask):
+        four = [parts[mask, near, core] for near in range(2) for core in range(2)]
+        return score(grid, train_here, four, total, mask, blocks, mask == relayed)
+
     parts = {(0, 0, 0): block}
     parts[0, 0, 1] = grid.swap(block, 0, 0, 1)
     parts[0, 1, 0] = grid.swap(block, 0, 1, 0)
     parts[beside, 0, 0] = grid.swap(block, beside, 0, 0)
     parts[mirror, 0, 0] = grid.swap(block, mirror, 0, 0)
-    parts[mirror ^ beside, 0, 0] = grid.swap(parts[mirror, 0, 0], beside, 0, 0)
-    for mask in grid.fars[1:]:
-        parts[mask, 0, 1] = grid.swap(parts[mask, 0, 0], 0, 0, 1)
-    for mask in (mirror ^ beside, mirror, beside):
-        parts[mask, 1, 0] = grid.swap(parts[mask, 0, 0], 0, 1, 0)
-    for mask in grid.fars:
-        parts[mask, 1, 1] = grid.swap(parts[mask, 1, 0], 0, 0, 1)
-    return score(grid, train_here, parts, queries.shape[0])
+    parts[0, 1, 1] = grid.swap(parts[0, 1, 0], 0, 0, 1)
+    parts[beside, 0, 1] = grid.swap(parts[beside, 0, 0], 0, 0, 1)
+    parts[beside, 1, 0] = grid.swap(parts[0, 1, 0], beside, 0, 0)
+    parts[beside, 1, 1] = grid.swap(parts[beside, 1, 0], 0, 0, 1)
+    parts[mirror, 0, 1] = grid.swap(parts[mirror, 0, 0], 0, 0, 1)
+    parts[mirror, 1, 0] = grid.swap(parts[mirror, 0, 0], 0, 1, 0)
+    parts[relayed, 0, 0] = grid.swap(parts[mirror, 0, 0], beside, 0, 0)
+    parts[relayed, 0, 1] = grid.swap(parts[relayed, 0, 0], 0, 0, 1)
+    parts[relayed, 1, 0] = grid.swap(parts[relayed, 0, 0], 0, 1, 0)
+    total = add(None, 0)
+    parts[mirror, 1, 0], total = lax.optimization_barrier((parts[mirror, 1, 0], total))
+    parts[mirror, 1, 1] = grid.swap(parts[mirror, 1, 0], 0, 0, 1)
+    total = add(total, beside)
+    parts[relayed, 1, 0], total = lax.optimization_barrier((parts[relayed, 1, 0], total))
+    parts[relayed, 1, 1] = grid.swap(parts[relayed, 1, 0], 0, 0, 1)
+    return add(add(total, mirror), relayed)
 
 
 def one_level(train_feats, queries, inverse_fisher):

time: 50 us -> 51.3 us (1.026)
  waiting for transfers between devices: 21.8 us -> 15.1 us
  Pallas kernels: 11.5 us -> 17.6 us
  starting transfers between devices: 16.5 us -> 18.3 us
    ppermute x21, waiting for transfers between devices: 21.8 us -> 15.1 us  [swap(): return lax.ppermute(block, 'rows', pairs)]
    pallas_call x1 -> x4, Pallas kernels: 7.04 us -> 13.2 us  [score(): pl.pallas_call(functools.partial(score_kernel, grid, tile, (blocks, count...]
    ppermute x21, starting transfers between devices: 16.5 us -> 18.3 us  [swap(): return lax.ppermute(block, 'rows', pairs)]
  transfers between devices with their start and end apart: 21 -> 21, of which waited for: 10 -> 8; matrix products, arithmetic and copies ran while one was open for 0% -> 0% of each run, Pallas kernels for 7% -> 23%
where the time goes in v4:
time: 51.3 us; the launch traced here: 51.2 us
  starting transfers between devices  18.3 us (36%)
  Pallas kernels  17.6 us (34%)
  waiting for transfers between devices  15.1 us (29%)
    ppermute x21, starting transfers between devices, swap(): return lax.ppermute(block, 'rows', pairs)  18.3 us
    ppermute x21, waiting for transfers between devices, swap(): return lax.ppermute(block, 'rows', pairs)  15.1 us
    pallas_call x4, Pallas kernels, score(): pl.pallas_call(functools.partial(score_kernel, grid, tile, (blocks, count...  13.2 us
    pallas_call x1, Pallas kernels, stage(): pl.pallas_call(functools.partial(stage_kernel, len(arrays)), out_shape=[p...  3.49 us
  transfers between devices with their start and end apart: 21, of which 8 were waited for; matrix products, arithmetic and copies ran while one was open for 0% of the time, Pallas kernels for 23%

profile of v4, /device:TPU:0, one launch (start us, length us, event | category | flops | bytes accessed | tf_op | source)
XLA Modules:
  0.0 51.2 jit_solution(5695842516389985779)
XLA Ops:
  0.0 3.0 %collective-permute-start.1 = (bf16[1,2048,128]{2,1,0:T(8,128)(2,1)}, bf16[1,2048,128]{2,1,0:T(8,128)(2,1)S(1)}, u32[]{:S(2)}, u32[]{:S(2)}) collective-permute-start(bf16[1,2048,128]{2,1,0:T(8,128)(2,1)} %refs_2_.1), channel_id=1, source_target_pairs={{2,0},{3,1},{0,2},{1,3},{6,4},{7,5},{4,6},{5,7},{10,8},{11,9},{8,1... | collective-permute-start | bytes 1572872 | tf_op jit(solution)/shard_map/ppermute | solution.py:24
  3.0 3.6 %collective-permute-start = (bf16[2,16,2048]{2,1,0:T(8,128)(2,1)}, bf16[2,16,2048]{2,1,0:T(8,128)(2,1)S(1)}, u32[]{:S(2)}, u32[]{:S(2)}) collective-permute-start(bf16[2,16,2048]{2,1,0:T(8,128)(2,1)} %refs_1_.1), channel_id=1, source_target_pairs={{12,0},{13,1},{14,2},{15,3},{8,4},{9,5},{10,6},{11,7},{4,8},{5,9},... | collective-permute-start | bytes 393224 | tf_op jit(solution)/shard_map/ppermute | solution.py:24
  6.6 0.0 collective-permute-start.2
  6.6 3.5 %stage.1 = (bf16[2048,2048]{1,0:T(8,128)(2,1)S(1)}, bf16[2,16,2048]{2,1,0:T(8,128)(2,1)S(1)}, bf16[1,2048,128]{2,1,0:T(8,128)(2,1)S(1)}) custom-call(bf16[2048,2048]{1,0:T(8,128)(2,1)} %refs_0_.1, bf16[2,16,2048]{2,1,0:T(8,128)(2,1)} %refs_1_.1, bf16[1,2048,128]{2,1,0:T(8,128)(2,1)} %refs_2_.1), custom_call_target="tpu_custom_call" | custom-call | bytes 18087936 | tf_op jit(solution)/shard_map/stage/pallas_call | solution.py:53
  10.1 1.3 %collective-permute-done.refs_3_ = bf16[2,16,2048]{2,1,0:T(8,128)(2,1)S(1)} collective-permute-done((bf16[2,16,2048]{2,1,0:T(8,128)(2,1)}, bf16[2,16,2048]{2,1,0:T(8,128)(2,1)S(1)}, u32[]{:S(2)}, u32[]{:S(2)}) %collective-permute-start) | collective-permute-done | bytes 131104 | tf_op jit(solution)/shard_map/ppermute | solution.py:24
  11.4 1.1 %collective-permute-start.3 = (bf16[2,16,2048]{2,1,0:T(8,128)(2,1)S(1)}, bf16[2,16,2048]{2,1,0:T(8,128)(2,1)S(1)}, u32[]{:S(2)}, u32[]{:S(2)}) collective-permute-start(bf16[2,16,2048]{2,1,0:T(8,128)(2,1)S(1)} %collective-permute-done.refs_3_), channel_id=1, source_target_pairs={{4,0},{5,1},{6,2},{7,3},{0,4},{1,5},{2,6},{3,7},{12,8},{13,9},{14,... | collective-permute-start | bytes 393224 | tf_op jit(solution)/shard_map/ppermute | solution.py:24
  12.5 1.2 %collective-permute-done.2.refs_1_ = bf16[2,16,2048]{2,1,0:T(8,128)(2,1)S(1)} collective-permute-done((bf16[2,16,2048]{2,1,0:T(8,128)(2,1)}, bf16[2,16,2048]{2,1,0:T(8,128)(2,1)S(1)}, u32[]{:S(2)}, u32[]{:S(2)}) %collective-permute-start.2) | collective-permute-done | bytes 131104 | tf_op jit(solution)/shard_map/ppermute | solution.py:24
  13.7 2.6 %collective-permute-done.3.refs_2_ = bf16[2,16,2048]{2,1,0:T(8,128)(2,1)S(1)} collective-permute-done((bf16[2,16,2048]{2,1,0:T(8,128)(2,1)S(1)}, bf16[2,16,2048]{2,1,0:T(8,128)(2,1)S(1)}, u32[]{:S(2)}, u32[]{:S(2)}) %collective-permute-start.3) | collective-permute-done | bytes 131104 | tf_op jit(solution)/shard_map/ppermute | solution.py:24
  16.4 1.9 %collective-permute-done.5.refs_7_ = bf16[1,2048,128]{2,1,0:T(8,128)(2,1)S(1)} collective-permute-done((bf16[1,2048,128]{2,1,0:T(8,128)(2,1)S(1)}, bf16[1,2048,128]{2,1,0:T(8,128)(2,1)S(1)}, u32[]{:S(2)}, u32[]{:S(2)}) %collective-permute-start.5) | collective-permute-done | bytes 524320 | tf_op jit(solution)/shard_map/ppermute | solution.py:24
  18.3 1.0 %condition.1.refs_1_ = bf16[128,512]{1,0:T(8,128)(2,1)S(1)} custom-call(bf16[2,16,2048]{2,1,0:T(8,128)(2,1)S(1)} %get-tuple-element.27.refs_0_, bf16[2,16,2048]{2,1,0:T(8,128)(2,1)S(1)} %collective-permute-done.2.refs_1_, bf16[2,16,2048]{2,1,0:T(8,128)(2,1)S(1)} %collective-permute-done.3.refs_2_, bf16[2,16,2048]{2,1,0:T(8,128)(2,1)S(1)} %collective-permute-done.refs_3_, ...), custom_call_target="tpu_custom_call" | custom-call | flops 268435456 | bytes 3145728 | tf_op jit(solution)/shard_map/condition/pallas_call | solution.py:83
  19.3 0.5 %collective-permute-start.12 = (bf16[128,512]{1,0:T(8,128)(2,1)S(1)}, bf16[128,512]{1,0:T(8,128)(2,1)S(1)}, u32[]{:S(2)}, u32[]{:S(2)}) collective-permute-start(bf16[128,512]{1,0:T(8,128)(2,1)S(1)} %condition.1.refs_1_), channel_id=1, source_target_pairs={{2,0},{3,1},{0,2},{1,3},{6,4},{7,5},{4,6},{5,7},{10,8},{11,9},{8,1... | collective-permute-start | bytes 393224 | tf_op jit(solution)/shard_map/ppermute | solution.py:24
  19.8 3.6 %collective-permute-start.6 = (bf16[128,512]{1,0:T(8,128)(2,1)S(1)}, bf16[128,512]{1,0:T(8,128)(2,1)S(1)}, u32[]{:S(2)}, u32[]{:S(2)}) collective-permute-start(bf16[128,512]{1,0:T(8,128)(2,1)S(1)} %condition.1.refs_1_), channel_id=1, source_target_pairs={{12,0},{13,1},{14,2},{15,3},{8,4},{9,5},{10,6},{11,7},{4,8},{5,9},... | collective-permute-start | bytes 393224 | tf_op jit(solution)/shard_map/ppermute | solution.py:24
  23.4 0.0 collective-permute-start.16
  23.4 0.0 collective-permute-start.10
  23.4 1.4 %collective-permute-done.12.refs_3_ = bf16[128,512]{1,0:T(8,128)(2,1)S(1)} collective-permute-done((bf16[128,512]{1,0:T(8,128)(2,1)S(1)}, bf16[128,512]{1,0:T(8,128)(2,1)S(1)}, u32[]{:S(2)}, u32[]{:S(2)}) %collective-permute-start.12) | collective-permute-done | bytes 131104 | tf_op jit(solution)/shard_map/ppermute | solution.py:24
  24.9 1.1 %collective-permute-start.13 = (bf16[128,512]{1,0:T(8,128)(2,1)S(1)}, bf16[128,512]{1,0:T(8,128)(2,1)S(1)}, u32[]{:S(2)}, u32[]{:S(2)}) collective-permute-start(bf16[128,512]{1,0:T(8,128)(2,1)S(1)} %collective-permute-done.12.refs_3_), channel_id=1, source_target_pairs={{4,0},{5,1},{6,2},{7,3},{0,4},{1,5},{2,6},{3,7},{12,8},{13,9},{14,... | collective-permute-start | bytes 393224 | tf_op jit(solution)/shard_map/ppermute | solution.py:24
  26.0 0.0 collective-permute-start.17
  26.0 2.0 %collective-permute-done.6.refs_1_ = bf16[128,512]{1,0:T(8,128)(2,1)S(1)} collective-permute-done((bf16[128,512]{1,0:T(8,128)(2,1)S(1)}, bf16[128,512]{1,0:T(8,128)(2,1)S(1)}, u32[]{:S(2)}, u32[]{:S(2)}) %collective-permute-start.6) | collective-permute-done | bytes 131104 | tf_op jit(solution)/shard_map/ppermute | solution.py:24
  28.0 1.5 %collective-permute-start.7 = (bf16[128,512]{1,0:T(8,128)(2,1)S(1)}, bf16[128,512]{1,0:T(8,128)(2,1)S(1)}, u32[]{:S(2)}, u32[]{:S(2)}) collective-permute-start(bf16[128,512]{1,0:T(8,128)(2,1)S(1)} %collective-permute-done.6.refs_1_), channel_id=1, source_target_pairs={{4,0},{5,1},{6,2},{7,3},{0,4},{1,5},{2,6},{3,7},{12,8},{13,9},{14,... | collective-permute-start | bytes 393224 | tf_op jit(solution)/shard_map/ppermute | solution.py:24
  29.4 0.0 collective-permute-done.16.refs_2_
  29.4 1.1 %collective-permute-start.15 = (bf16[128,512]{1,0:T(8,128)(2,1)S(1)}, bf16[128,512]{1,0:T(8,128)(2,1)S(1)}, u32[]{:S(2)}, u32[]{:S(2)}) collective-permute-start(bf16[128,512]{1,0:T(8,128)(2,1)S(1)} %collective-permute-done.6.refs_1_), channel_id=1, source_target_pairs={{2,0},{3,1},{0,2},{1,3},{6,4},{7,5},{4,6},{5,7},{10,8},{11,9},{8,1... | collective-permute-start | bytes 393224 | tf_op jit(solution)/shard_map/ppermute | solution.py:24
  30.5 2.5 %collective-permute-done.13.refs_3_ = bf16[128,512]{1,0:T(8,128)(2,1)S(1)} collective-permute-done((bf16[128,512]{1,0:T(8,128)(2,1)S(1)}, bf16[128,512]{1,0:T(8,128)(2,1)S(1)}, u32[]{:S(2)}, u32[]{:S(2)}) %collective-permute-start.13) | collective-permute-done | bytes 131104 | tf_op jit(solution)/shard_map/ppermute | solution.py:24
  33.1 0.5 collective-permute-start.19
  33.6 2.1 %collective-permute-done.7.refs_1_ = bf16[128,512]{1,0:T(8,128)(2,1)S(1)} collective-permute-done((bf16[128,512]{1,0:T(8,128)(2,1)S(1)}, bf16[128,512]{1,0:T(8,128)(2,1)S(1)}, u32[]{:S(2)}, u32[]{:S(2)}) %collective-permute-start.7) | collective-permute-done | bytes 131104 | tf_op jit(solution)/shard_map/ppermute | solution.py:24
  35.7 1.5 %collective-permute-start.9 = (bf16[128,512]{1,0:T(8,128)(2,1)S(1)}, bf16[128,512]{1,0:T(8,128)(2,1)S(1)}, u32[]{:S(2)}, u32[]{:S(2)}) collective-permute-start(bf16[128,512]{1,0:T(8,128)(2,1)S(1)} %collective-permute-done.7.refs_1_), channel_id=1, source_target_pairs={{2,0},{3,1},{0,2},{1,3},{6,4},{7,5},{4,6},{5,7},{10,8},{11,9},{8,1... | collective-permute-start | bytes 393224 | tf_op jit(solution)/shard_map/ppermute | solution.py:24
  37.2 2.7 %score.4.refs_5_ = f32[2048,512]{1,0:T(8,128)S(1)} custom-call(bf16[2048,2048]{1,0:T(8,128)(2,1)S(1)} %get-tuple-element.24.refs_0_, bf16[128,512]{1,0:T(8,128)(2,1)S(1)} %condition.1.refs_1_, bf16[128,512]{1,0:T(8,128)(2,1)S(1)} %collective-permute-done.16.refs_2_, bf16[128,512]{1,0:T(8,128)(2,1)S(1)} %collective-permute-done.12.refs_3_, ...), custom_call_target="tpu_custom_call" | custom-call | flops 1073741824 | bytes 4194304 | tf_op jit(solution)/shard_map/score/pallas_call | solution.py:162
  39.9 0.1 collective-permute-start.20
  40.0 0.5 collective-permute-start.8
  40.5 2.8 %score.5.refs_5_ = f32[2048,512]{1,0:T(8,128)S(1)} custom-call(bf16[2048,2048]{1,0:T(8,128)(2,1)S(1)} %get-tuple-element.24.refs_0_, bf16[128,512]{1,0:T(8,128)(2,1)S(1)} %collective-permute-done.10.refs_1_, bf16[128,512]{1,0:T(8,128)(2,1)S(1)} %collective-permute-done.11.refs_2_, ...), custom_call_target="tpu_custom_call", output_to_operand_aliasing={{}: (5, {})} | custom-call | flops 1073741824 | bytes 4194304 | tf_op jit(solution)/shard_map/score/pallas_call | solution.py:162
  43.3 0.1 collective-permute-start.18
  43.5 2.8 %score.6.refs_5_ = f32[2048,512]{1,0:T(8,128)S(1)} custom-call(bf16[2048,2048]{1,0:T(8,128)(2,1)S(1)} %get-tuple-element.24.refs_0_, bf16[128,512]{1,0:T(8,128)(2,1)S(1)} %collective-permute-done.6.refs_1_, bf16[128,512]{1,0:T(8,128)(2,1)S(1)} %collective-permute-done.19.refs_2_, ...), custom_call_target="tpu_custom_call", output_to_operand_aliasing={{}: (5, {})} | custom-call | flops 1073741824 | bytes 4194304 | tf_op jit(solution)/shard_map/score/pallas_call | solution.py:162
  46.2 4.9 %score.7 = f32[2048,512]{1,0:T(8,128)} custom-call(bf16[2048,2048]{1,0:T(8,128)(2,1)S(1)} %get-tuple-element.24.refs_0_, bf16[128,512]{1,0:T(8,128)(2,1)S(1)} %collective-permute-done.7.refs_1_, bf16[128,512]{1,0:T(8,128)(2,1)S(1)} %collective-permute-done.8.refs_2_, bf16[128,512]{1,0:T(8,128)(2,1)S(1)} %collective-permute-done.9.refs_3_, ...), custom_call_target="tpu_custom_call" | custom-call | flops 1073741824 | bytes 4194304 | tf_op jit(solution)/shard_map/score/pallas_call | solution.py:162
  (18 shorter events, 0.0 us)
Async XLA Ops:
  0.0 12.5 %copy-start = (bf16[1,2048,128]{2,1,0:T(8,128)(2,1)S(1)}, bf16[1,2048,128]{2,1,0:T(8,128)(2,1)}, u32[]{:S(2)}) copy-start(bf16[1,2048,128]{2,1,0:T(8,128)(2,1)} %refs_2_.1) | copy-start | bytes 1572868
  0.0 16.4 %collective-permute-start.1 = (bf16[1,2048,128]{2,1,0:T(8,128)(2,1)}, bf16[1,2048,128]{2,1,0:T(8,128)(2,1)S(1)}, u32[]{:S(2)}, u32[]{:S(2)}) collective-permute-start(bf16[1,2048,128]{2,1,0:T(8,128)(2,1)} %refs_2_.1), channel_id=1, source_target_pairs={{2,0},{3,1},{0,2},{1,3},{6,4},{7,5},{4,6},{5,7},{10,8},{11,9},{8,1... | collective-permute-start | bytes 1572872 | tf_op jit(solution)/shard_map/ppermute | solution.py:24
  3.0 8.4 %collective-permute-start = (bf16[2,16,2048]{2,1,0:T(8,128)(2,1)}, bf16[2,16,2048]{2,1,0:T(8,128)(2,1)S(1)}, u32[]{:S(2)}, u32[]{:S(2)}) collective-permute-start(bf16[2,16,2048]{2,1,0:T(8,128)(2,1)} %refs_1_.1), channel_id=1, source_target_pairs={{12,0},{13,1},{14,2},{15,3},{8,4},{9,5},{10,6},{11,7},{4,8},{5,9},... | collective-permute-start | bytes 393224 | tf_op jit(solution)/shard_map/ppermute | solution.py:24
  6.6 7.2 %collective-permute-start.2 = (bf16[2,16,2048]{2,1,0:T(8,128)(2,1)}, bf16[2,16,2048]{2,1,0:T(8,128)(2,1)S(1)}, u32[]{:S(2)}, u32[]{:S(2)}) collective-permute-start(bf16[2,16,2048]{2,1,0:T(8,128)(2,1)} %refs_1_.1), channel_id=1, source_target_pairs={{4,0},{5,1},{6,2},{7,3},{0,4},{1,5},{2,6},{3,7},{12,8},{13,9},{14,... | collective-permute-start | bytes 393224 | tf_op jit(solution)/shard_map/ppermute | solution.py:24
  11.4 5.0 %collective-permute-start.3 = (bf16[2,16,2048]{2,1,0:T(8,128)(2,1)S(1)}, bf16[2,16,2048]{2,1,0:T(8,128)(2,1)S(1)}, u32[]{:S(2)}, u32[]{:S(2)}) collective-permute-start(bf16[2,16,2048]{2,1,0:T(8,128)(2,1)S(1)} %collective-permute-done.refs_3_), channel_id=1, source_target_pairs={{4,0},{5,1},{6,2},{7,3},{0,4},{1,5},{2,6},{3,7},{12,8},{13,9},{14,... | collective-permute-start | bytes 393224 | tf_op jit(solution)/shard_map/ppermute | solution.py:24
  12.5 3.9 %collective-permute-start.4 = (bf16[1,2048,128]{2,1,0:T(8,128)(2,1)S(1)}, bf16[1,2048,128]{2,1,0:T(8,128)(2,1)S(1)}, u32[]{:S(2)}, u32[]{:S(2)}) collective-permute-start(bf16[1,2048,128]{2,1,0:T(8,128)(2,1)S(1)} %copy-done), channel_id=1, source_target_pairs={{1,0},{0,1},{3,2},{2,3},{5,4},{4,5},{7,6},{6,7},{9,8},{8,9},{11,10... | collective-permute-start | bytes 1572872 | tf_op jit(solution)/shard_map/ppermute | solution.py:24
  16.4 1.9 %collective-permute-start.5 = (bf16[1,2048,128]{2,1,0:T(8,128)(2,1)S(1)}, bf16[1,2048,128]{2,1,0:T(8,128)(2,1)S(1)}, u32[]{:S(2)}, u32[]{:S(2)}) collective-permute-start(bf16[1,2048,128]{2,1,0:T(8,128)(2,1)S(1)} %collective-permute-done.1.refs_6_), channel_id=1, source_target_pairs={{1,0},{0,1},{3,2},{2,3},{5,4},{4,5},{7,6},{6,7},{9,8},{8,9},{11,10... | collective-permute-start | bytes 1572872 | tf_op jit(solution)/shard_map/ppermute | solution.py:24
  19.3 5.6 %collective-permute-start.12 = (bf16[128,512]{1,0:T(8,128)(2,1)S(1)}, bf16[128,512]{1,0:T(8,128)(2,1)S(1)}, u32[]{:S(2)}, u32[]{:S(2)}) collective-permute-start(bf16[128,512]{1,0:T(8,128)(2,1)S(1)} %condition.1.refs_1_), channel_id=1, source_target_pairs={{2,0},{3,1},{0,2},{1,3},{6,4},{7,5},{4,6},{5,7},{10,8},{11,9},{8,1... | collective-permute-start | bytes 393224 | tf_op jit(solution)/shard_map/ppermute | solution.py:24
  19.8 8.2 %collective-permute-start.6 = (bf16[128,512]{1,0:T(8,128)(2,1)S(1)}, bf16[128,512]{1,0:T(8,128)(2,1)S(1)}, u32[]{:S(2)}, u32[]{:S(2)}) collective-permute-start(bf16[128,512]{1,0:T(8,128)(2,1)S(1)} %condition.1.refs_1_), channel_id=1, source_target_pairs={{12,0},{13,1},{14,2},{15,3},{8,4},{9,5},{10,6},{11,7},{4,8},{5,9},... | collective-permute-start | bytes 393224 | tf_op jit(solution)/shard_map/ppermute | solution.py:24
  23.4 6.0 %collective-permute-start.16 = (bf16[128,512]{1,0:T(8,128)(2,1)S(1)}, bf16[128,512]{1,0:T(8,128)(2,1)S(1)}, u32[]{:S(2)}, u32[]{:S(2)}) collective-permute-start(bf16[128,512]{1,0:T(8,128)(2,1)S(1)} %condition.1.refs_1_), channel_id=1, source_target_pairs={{1,0},{0,1},{3,2},{2,3},{5,4},{4,5},{7,6},{6,7},{9,8},{8,9},{11,10... | collective-permute-start | bytes 393224 | tf_op jit(solution)/shard_map/ppermute | solution.py:24
  23.4 7.1 %collective-permute-start.10 = (bf16[128,512]{1,0:T(8,128)(2,1)S(1)}, bf16[128,512]{1,0:T(8,128)(2,1)S(1)}, u32[]{:S(2)}, u32[]{:S(2)}) collective-permute-start(bf16[128,512]{1,0:T(8,128)(2,1)S(1)} %condition.1.refs_1_), channel_id=1, source_target_pairs={{4,0},{5,1},{6,2},{7,3},{0,4},{1,5},{2,6},{3,7},{12,8},{13,9},{14,... | collective-permute-start | bytes 393224 | tf_op jit(solution)/shard_map/ppermute | solution.py:24
  24.9 8.2 %collective-permute-start.13 = (bf16[128,512]{1,0:T(8,128)(2,1)S(1)}, bf16[128,512]{1,0:T(8,128)(2,1)S(1)}, u32[]{:S(2)}, u32[]{:S(2)}) collective-permute-start(bf16[128,512]{1,0:T(8,128)(2,1)S(1)} %collective-permute-done.12.refs_3_), channel_id=1, source_target_pairs={{4,0},{5,1},{6,2},{7,3},{0,4},{1,5},{2,6},{3,7},{12,8},{13,9},{14,... | collective-permute-start | bytes 393224 | tf_op jit(solution)/shard_map/ppermute | solution.py:24
  26.0 7.1 %collective-permute-start.17 = (bf16[128,512]{1,0:T(8,128)(2,1)S(1)}, bf16[128,512]{1,0:T(8,128)(2,1)S(1)}, u32[]{:S(2)}, u32[]{:S(2)}) collective-permute-start(bf16[128,512]{1,0:T(8,128)(2,1)S(1)} %collective-permute-done.12.refs_3_), channel_id=1, source_target_pairs={{1,0},{0,1},{3,2},{2,3},{5,4},{4,5},{7,6},{6,7},{9,8},{8,9},{11,10... | collective-permute-start | bytes 393224 | tf_op jit(solution)/shard_map/ppermute | solution.py:24
  28.0 7.7 %collective-permute-start.7 = (bf16[128,512]{1,0:T(8,128)(2,1)S(1)}, bf16[128,512]{1,0:T(8,128)(2,1)S(1)}, u32[]{:S(2)}, u32[]{:S(2)}) collective-permute-start(bf16[128,512]{1,0:T(8,128)(2,1)S(1)} %collective-permute-done.6.refs_1_), channel_id=1, source_target_pairs={{4,0},{5,1},{6,2},{7,3},{0,4},{1,5},{2,6},{3,7},{12,8},{13,9},{14,... | collective-permute-start | bytes 393224 | tf_op jit(solution)/shard_map/ppermute | solution.py:24
  29.4 10.5 %collective-permute-start.15 = (bf16[128,512]{1,0:T(8,128)(2,1)S(1)}, bf16[128,512]{1,0:T(8,128)(2,1)S(1)}, u32[]{:S(2)}, u32[]{:S(2)}) collective-permute-start(bf16[128,512]{1,0:T(8,128)(2,1)S(1)} %collective-permute-done.6.refs_1_), channel_id=1, source_target_pairs={{2,0},{3,1},{0,2},{1,3},{6,4},{7,5},{4,6},{5,7},{10,8},{11,9},{8,1... | collective-permute-start | bytes 393224 | tf_op jit(solution)/shard_map/ppermute | solution.py:24
  30.5 9.5 %collective-permute-start.11 = (bf16[128,512]{1,0:T(8,128)(2,1)S(1)}, bf16[128,512]{1,0:T(8,128)(2,1)S(1)}, u32[]{:S(2)}, u32[]{:S(2)}) collective-permute-start(bf16[128,512]{1,0:T(8,128)(2,1)S(1)} %collective-permute-done.10.refs_1_), channel_id=1, source_target_pairs={{1,0},{0,1},{3,2},{2,3},{5,4},{4,5},{7,6},{6,7},{9,8},{8,9},{11,10... | collective-permute-start | bytes 393224 | tf_op jit(solution)/shard_map/ppermute | solution.py:24
  33.1 7.4 %collective-permute-start.14 = (bf16[128,512]{1,0:T(8,128)(2,1)S(1)}, bf16[128,512]{1,0:T(8,128)(2,1)S(1)}, u32[]{:S(2)}, u32[]{:S(2)}) collective-permute-start(bf16[128,512]{1,0:T(8,128)(2,1)S(1)} %collective-permute-done.13.refs_3_), channel_id=1, source_target_pairs={{1,0},{0,1},{3,2},{2,3},{5,4},{4,5},{7,6},{6,7},{9,8},{8,9},{11,10... | collective-permute-start | bytes 393224 | tf_op jit(solution)/shard_map/ppermute | solution.py:24
  33.1 10.4 %collective-permute-start.19 = (bf16[128,512]{1,0:T(8,128)(2,1)S(1)}, bf16[128,512]{1,0:T(8,128)(2,1)S(1)}, u32[]{:S(2)}, u32[]{:S(2)}) collective-permute-start(bf16[128,512]{1,0:T(8,128)(2,1)S(1)} %collective-permute-done.6.refs_1_), channel_id=1, source_target_pairs={{1,0},{0,1},{3,2},{2,3},{5,4},{4,5},{7,6},{6,7},{9,8},{8,9},{11,10... | collective-permute-start | bytes 393224 | tf_op jit(solution)/shard_map/ppermute | solution.py:24
  35.7 7.6 %collective-permute-start.9 = (bf16[128,512]{1,0:T(8,128)(2,1)S(1)}, bf16[128,512]{1,0:T(8,128)(2,1)S(1)}, u32[]{:S(2)}, u32[]{:S(2)}) collective-permute-start(bf16[128,512]{1,0:T(8,128)(2,1)S(1)} %collective-permute-done.7.refs_1_), channel_id=1, source_target_pairs={{2,0},{3,1},{0,2},{1,3},{6,4},{7,5},{4,6},{5,7},{10,8},{11,9},{8,1... | collective-permute-start | bytes 393224 | tf_op jit(solution)/shard_map/ppermute | solution.py:24
  39.9 3.5 %collective-permute-start.20 = (bf16[128,512]{1,0:T(8,128)(2,1)S(1)}, bf16[128,512]{1,0:T(8,128)(2,1)S(1)}, u32[]{:S(2)}, u32[]{:S(2)}) collective-permute-start(bf16[128,512]{1,0:T(8,128)(2,1)S(1)} %collective-permute-done.15.refs_3_), channel_id=1, source_target_pairs={{1,0},{0,1},{3,2},{2,3},{5,4},{4,5},{7,6},{6,7},{9,8},{8,9},{11,10... | collective-permute-start | bytes 393224 | tf_op jit(solution)/shard_map/ppermute | solution.py:24
  40.0 6.2 %collective-permute-start.8 = (bf16[128,512]{1,0:T(8,128)(2,1)S(1)}, bf16[128,512]{1,0:T(8,128)(2,1)S(1)}, u32[]{:S(2)}, u32[]{:S(2)}) collective-permute-start(bf16[128,512]{1,0:T(8,128)(2,1)S(1)} %collective-permute-done.7.refs_1_), channel_id=1, source_target_pairs={{1,0},{0,1},{3,2},{2,3},{5,4},{4,5},{7,6},{6,7},{9,8},{8,9},{11,10... | collective-permute-start | bytes 393224 | tf_op jit(solution)/shard_map/ppermute | solution.py:24
  43.3 2.9 %collective-permute-start.18 = (bf16[128,512]{1,0:T(8,128)(2,1)S(1)}, bf16[128,512]{1,0:T(8,128)(2,1)S(1)}, u32[]{:S(2)}, u32[]{:S(2)}) collective-permute-start(bf16[128,512]{1,0:T(8,128)(2,1)S(1)} %collective-permute-done.9.refs_3_), channel_id=1, source_target_pairs={{1,0},{0,1},{3,2},{2,3},{5,4},{4,5},{7,6},{6,7},{9,8},{8,9},{11,10... | collective-permute-start | bytes 393224 | tf_op jit(solution)/shard_map/ppermute | solution.py:24

commit v5 on v4

--- a/solution.py
+++ b/solution.py
@@ -99,12 +99,13 @@
     blocks, count, width = shape
     train_ref, part_refs, refs = refs[0], refs[1:5], refs[5:]
     total_ref, refs = (None, refs) if first else (refs[0], refs[1:])
-    out_ref, sorted_ref, refs = refs[0], refs[1], refs[2:]
+    out_ref, sorted_ref, turned_ref, refs = refs[0], refs[1], refs[2], refs[3:]
     far, near, core = grid.place()
     features = train_ref.shape[1]
     for index, part_ref in enumerate(part_refs):
         group = flip(near, index // 2) * 2 + flip(core, index % 2)
         sorted_ref[:, :, pl.ds(group, 1)] = part_ref[...].reshape(blocks, grid.far, 1, count, width)
+    turned_ref[...] = sorted_ref[...].reshape(-1, width).T
     scale = 1.0 / features**0.5
     steps = train_ref.shape[0] // tile
 
@@ -112,10 +113,9 @@
         return pl.ds(pl.multiple_of(step * tile, tile), tile)
 
     def products(step):
-        value = lax.dot_general(
+        value = jnp.dot(
             train_ref[rows(step), columns(flip(far, mask), width)],
-            sorted_ref[...].reshape(-1, width),
-            (((1,), (1,)), ((), ())),
+            turned_ref[...],
             preferred_element_type=jnp.float32,
         )
         return value if first else total_ref[rows(step)] + value
@@ -128,37 +128,35 @@
 
         return
 
-    tile_ref, sem = refs
-
-    def copy(step, slot):
-        return pltpu.make_async_copy(tile_ref.at[slot], out_ref.at[rows(step)], sem.at[slot])
+    here_ref, sem = refs
+
+    def copy(step):
+        return pltpu.make_async_copy(here_ref.at[rows(step)], out_ref.at[rows(step)], sem.at[step])
 
     @pl.loop(0, steps)
     def _(step):
-        slot = lax.rem(step, 2)
-
-        @pl.when(step >= 2)
-        def _():
-            copy(step - 2, slot).wait()
-
-        tile_ref[slot] = products(step) * scale
-        copy(step, slot).start()
-
-    for step in range(max(steps - 2, 0), steps):
-        copy(step, step % 2).wait()
+        here_ref[rows(step)] = products(step) * scale
+        copy(step).start()
+
+    @pl.loop(0, steps)
+    def _(step):
+        copy(step).wait()
 
 
 def score(grid, train_feats, parts, total, mask, blocks, last):
     rows, features = train_feats.shape
     queries, width = parts[0].shape
     count = queries // (blocks * grid.far)
-    tile = 256
+    tile = 512
     first = total is None
     totals = [] if first else [total]
     shape = (rows, 4 * queries)
-    scratch = [pltpu.VMEM((blocks, grid.far, 4, count, width), jnp.bfloat16)]
+    scratch = [
+        pltpu.VMEM((blocks, grid.far, 4, count, width), jnp.bfloat16),
+        pltpu.VMEM((width, 4 * queries), jnp.bfloat16),
+    ]
     if last:
-        scratch += [pltpu.VMEM((2, tile, 4 * queries), jnp.float32), pltpu.SemaphoreType.DMA((2,))]
+        scratch += [pltpu.VMEM(shape, jnp.float32), pltpu.SemaphoreType.DMA((rows // tile,))]
     return pl.pallas_call(
         functools.partial(score_kernel, grid, tile, (blocks, count, width), mask, first, last),
         out_shape=jax.ShapeDtypeStruct(shape, jnp.float32) if last else pltpu.VMEM(shape, jnp.float32),
@@ -166,7 +164,7 @@
         out_specs=ANY if last else VMEM,
         scratch_shapes=scratch,
         input_output_aliases={} if first or last else {5: 0},
-        compiler_params=pltpu.CompilerParams(vmem_limit_bytes=12 << 20),
+        compiler_params=pltpu.CompilerParams(vmem_limit_bytes=16 << 20),
         cost_estimate=pl.CostEstimate(
             flops=8 * rows * width * queries, bytes_accessed=4 << 20, transcendentals=0
         ),
@@ -196,29 +194,39 @@
 
     def add(total, mask):
         four = [parts[mask, near, core] for near in range(2) for core in range(2)]
-        return score(grid, train_here, four, total, mask, blocks, mask == relayed)
+        return score(grid, train_here, four, total, mask, blocks, mask == beside)
 
     parts = {(0, 0, 0): block}
-    parts[0, 0, 1] = grid.swap(block, 0, 0, 1)
-    parts[0, 1, 0] = grid.swap(block, 0, 1, 0)
-    parts[beside, 0, 0] = grid.swap(block, beside, 0, 0)
-    parts[mirror, 0, 0] = grid.swap(block, mirror, 0, 0)
-    parts[0, 1, 1] = grid.swap(parts[0, 1, 0], 0, 0, 1)
-    parts[beside, 0, 1] = grid.swap(parts[beside, 0, 0], 0, 0, 1)
-    parts[beside, 1, 0] = grid.swap(parts[0, 1, 0], beside, 0, 0)
-    parts[beside, 1, 1] = grid.swap(parts[beside, 1, 0], 0, 0, 1)
-    parts[mirror, 0, 1] = grid.swap(parts[mirror, 0, 0], 0, 0, 1)
-    parts[mirror, 1, 0] = grid.swap(parts[mirror, 0, 0], 0, 1, 0)
-    parts[relayed, 0, 0] = grid.swap(parts[mirror, 0, 0], beside, 0, 0)
-    parts[relayed, 0, 1] = grid.swap(parts[relayed, 0, 0], 0, 0, 1)
-    parts[relayed, 1, 0] = grid.swap(parts[relayed, 0, 0], 0, 1, 0)
+
+    def swap(source, *step):
+        place = tuple(a ^ b for a, b in zip(source, step))
+        parts[place] = grid.swap(parts[source], *step)
+
+    def meet(*places, total=None):
+        held, total = lax.optimization_barrier(([parts[place] for place in places], total))
+        parts.update(zip(places, held))
+        return total
+
+    own, far_one, far_three, near_one = (0, 0, 0), (beside, 0, 0), (mirror, 0, 0), (0, 1, 0)
+    swap(own, *far_three)
+    swap(own, *far_one)
+    swap(own, *near_one)
+    swap(own, 0, 0, 1)
+    meet(far_three, far_one, near_one)
+    swap(far_three, beside, 1, 0)
+    swap(far_three, beside, 0, 0)
+    swap(far_three, 0, 1, 0)
+    swap(far_one, 0, 1, 0)
+    swap(near_one, 0, 0, 1)
+    swap(far_three, 0, 0, 1)
+    swap(far_one, 0, 0, 1)
     total = add(None, 0)
-    parts[mirror, 1, 0], total = lax.optimization_barrier((parts[mirror, 1, 0], total))
-    parts[mirror, 1, 1] = grid.swap(parts[mirror, 1, 0], 0, 0, 1)
-    total = add(total, beside)
-    parts[relayed, 1, 0], total = lax.optimization_barrier((parts[relayed, 1, 0], total))
-    parts[relayed, 1, 1] = grid.swap(parts[relayed, 1, 0], 0, 0, 1)
-    return add(add(total, mirror), relayed)
+    total = meet((relayed, 1, 0), (relayed, 0, 0), (mirror, 1, 0), total=total)
+    swap((relayed, 1, 0), 0, 0, 1)
+    swap((relayed, 0, 0), 0, 0, 1)
+    swap((mirror, 1, 0), 0, 0, 1)
+    swap((beside, 1, 0), 0, 0, 1)
+    return add(add(add(total, relayed), mirror), beside)
 
 
 def one_level(train_feats, queries, inverse_fisher):

time: 51.3 us -> 50.1 us (0.977)
  Pallas kernels: 17.6 us -> 13.8 us
  waiting for transfers between devices: 15.1 us -> 18.7 us
  starting transfers between devices: 18.3 us -> 17.4 us
    pallas_call x4, Pallas kernels: 13.2 us -> 9.3 us  [score(): pl.pallas_call(functools.partial(score_kernel, grid, tile, (blocks, count...]
    ppermute x21, waiting for transfers between devices: 15.1 us -> 18.7 us  [swap(): return lax.ppermute(block, 'rows', pairs)]
    ppermute x21, starting transfers between devices: 18.3 us -> 17.4 us  [swap(): return lax.ppermute(block, 'rows', pairs)]
  transfers between devices with their start and end apart: 21 -> 21, of which waited for: 8 -> 10; matrix products, arithmetic and copies ran while one was open for 0% -> 0% of each run, Pallas kernels for 23% -> 20%
where the time goes in v5:
time: 50.1 us; the launch traced here: 49.9 us
  waiting for transfers between devices  18.7 us (37%)
  starting transfers between devices  17.4 us (35%)
  Pallas kernels  13.8 us (28%)
    ppermute x21, waiting for transfers between devices, swap(): return lax.ppermute(block, 'rows', pairs)  18.7 us
    ppermute x21, starting transfers between devices, swap(): return lax.ppermute(block, 'rows', pairs)  17.4 us
    pallas_call x4, Pallas kernels, score(): pl.pallas_call(functools.partial(score_kernel, grid, tile, (blocks, count...  9.3 us
    pallas_call x1, Pallas kernels, stage(): pl.pallas_call(functools.partial(stage_kernel, len(arrays)), out_shape=[p...  3.49 us
  transfers between devices with their start and end apart: 21, of which 10 were waited for; matrix products, arithmetic and copies ran while one was open for 0% of the time, Pallas kernels for 20%

profile of v5, /device:TPU:0, one launch (start us, length us, event | category | flops | bytes accessed | tf_op | source)
XLA Modules:
  0.0 49.9 jit_solution(3469157542837576688)
XLA Ops:
  0.0 3.0 %collective-permute-start.1 = (bf16[1,2048,128]{2,1,0:T(8,128)(2,1)}, bf16[1,2048,128]{2,1,0:T(8,128)(2,1)S(1)}, u32[]{:S(2)}, u32[]{:S(2)}) collective-permute-start(bf16[1,2048,128]{2,1,0:T(8,128)(2,1)} %refs_2_.1), channel_id=1, source_target_pairs={{2,0},{3,1},{0,2},{1,3},{6,4},{7,5},{4,6},{5,7},{10,8},{11,9},{8,1... | collective-permute-start | bytes 1572872 | tf_op jit(solution)/shard_map/ppermute | solution.py:24
  3.0 3.6 %collective-permute-start = (bf16[2,16,2048]{2,1,0:T(8,128)(2,1)}, bf16[2,16,2048]{2,1,0:T(8,128)(2,1)S(1)}, u32[]{:S(2)}, u32[]{:S(2)}) collective-permute-start(bf16[2,16,2048]{2,1,0:T(8,128)(2,1)} %refs_1_.1), channel_id=1, source_target_pairs={{12,0},{13,1},{14,2},{15,3},{8,4},{9,5},{10,6},{11,7},{4,8},{5,9},... | collective-permute-start | bytes 393224 | tf_op jit(solution)/shard_map/ppermute | solution.py:24
  6.6 3.5 %stage.1 = (bf16[2048,2048]{1,0:T(8,128)(2,1)S(1)}, bf16[2,16,2048]{2,1,0:T(8,128)(2,1)S(1)}, bf16[1,2048,128]{2,1,0:T(8,128)(2,1)S(1)}) custom-call(bf16[2048,2048]{1,0:T(8,128)(2,1)} %refs_0_.1, bf16[2,16,2048]{2,1,0:T(8,128)(2,1)} %refs_1_.1, bf16[1,2048,128]{2,1,0:T(8,128)(2,1)} %refs_2_.1), custom_call_target="tpu_custom_call" | custom-call | bytes 18087936 | tf_op jit(solution)/shard_map/stage/pallas_call | solution.py:53
  10.1 1.3 %collective-permute-done.refs_3_ = bf16[2,16,2048]{2,1,0:T(8,128)(2,1)S(1)} collective-permute-done((bf16[2,16,2048]{2,1,0:T(8,128)(2,1)}, bf16[2,16,2048]{2,1,0:T(8,128)(2,1)S(1)}, u32[]{:S(2)}, u32[]{:S(2)}) %collective-permute-start) | collective-permute-done | bytes 131104 | tf_op jit(solution)/shard_map/ppermute | solution.py:24
  11.4 1.1 %collective-permute-start.3 = (bf16[2,16,2048]{2,1,0:T(8,128)(2,1)S(1)}, bf16[2,16,2048]{2,1,0:T(8,128)(2,1)S(1)}, u32[]{:S(2)}, u32[]{:S(2)}) collective-permute-start(bf16[2,16,2048]{2,1,0:T(8,128)(2,1)S(1)} %collective-permute-done.refs_3_), channel_id=1, source_target_pairs={{4,0},{5,1},{6,2},{7,3},{0,4},{1,5},{2,6},{3,7},{12,8},{13,9},{14,... | collective-permute-start | bytes 393224 | tf_op jit(solution)/shard_map/ppermute | solution.py:24
  12.5 0.0 collective-permute-start.4
  12.5 1.2 %collective-permute-done.2.refs_1_ = bf16[2,16,2048]{2,1,0:T(8,128)(2,1)S(1)} collective-permute-done((bf16[2,16,2048]{2,1,0:T(8,128)(2,1)}, bf16[2,16,2048]{2,1,0:T(8,128)(2,1)S(1)}, u32[]{:S(2)}, u32[]{:S(2)}) %collective-permute-start.2) | collective-permute-done | bytes 131104 | tf_op jit(solution)/shard_map/ppermute | solution.py:24
  13.7 2.6 %collective-permute-done.3.refs_2_ = bf16[2,16,2048]{2,1,0:T(8,128)(2,1)S(1)} collective-permute-done((bf16[2,16,2048]{2,1,0:T(8,128)(2,1)S(1)}, bf16[2,16,2048]{2,1,0:T(8,128)(2,1)S(1)}, u32[]{:S(2)}, u32[]{:S(2)}) %collective-permute-start.3) | collective-permute-done | bytes 131104 | tf_op jit(solution)/shard_map/ppermute | solution.py:24
  16.4 0.0 collective-permute-done.4.refs_5_
  16.4 1.9 %collective-permute-done.5.refs_7_ = bf16[1,2048,128]{2,1,0:T(8,128)(2,1)S(1)} collective-permute-done((bf16[1,2048,128]{2,1,0:T(8,128)(2,1)S(1)}, bf16[1,2048,128]{2,1,0:T(8,128)(2,1)S(1)}, u32[]{:S(2)}, u32[]{:S(2)}) %collective-permute-start.5) | collective-permute-done | bytes 524320 | tf_op jit(solution)/shard_map/ppermute | solution.py:24
  18.3 1.0 %condition.1.refs_1_ = bf16[128,512]{1,0:T(8,128)(2,1)S(1)} custom-call(bf16[2,16,2048]{2,1,0:T(8,128)(2,1)S(1)} %get-tuple-element.30.refs_0_, bf16[2,16,2048]{2,1,0:T(8,128)(2,1)S(1)} %collective-permute-done.2.refs_1_, bf16[2,16,2048]{2,1,0:T(8,128)(2,1)S(1)} %collective-permute-done.3.refs_2_, bf16[2,16,2048]{2,1,0:T(8,128)(2,1)S(1)} %collective-permute-done.refs_3_, ...), custom_call_target="tpu_custom_call" | custom-call | flops 268435456 | bytes 3145728 | tf_op jit(solution)/shard_map/condition/pallas_call | solution.py:83
  19.3 3.7 %collective-permute-start.6 = (bf16[128,512]{1,0:T(8,128)(2,1)S(1)}, bf16[128,512]{1,0:T(8,128)(2,1)S(1)}, u32[]{:S(2)}, u32[]{:S(2)}) collective-permute-start(bf16[128,512]{1,0:T(8,128)(2,1)S(1)} %condition.1.refs_1_), channel_id=1, source_target_pairs={{12,0},{13,1},{14,2},{15,3},{8,4},{9,5},{10,6},{11,7},{4,8},{5,9},... | collective-permute-start | bytes 393224 | tf_op jit(solution)/shard_map/ppermute | solution.py:24
  22.9 0.5 %collective-permute-start.8 = (bf16[128,512]{1,0:T(8,128)(2,1)S(1)}, bf16[128,512]{1,0:T(8,128)(2,1)S(1)}, u32[]{:S(2)}, u32[]{:S(2)}) collective-permute-start(bf16[128,512]{1,0:T(8,128)(2,1)S(1)} %condition.1.refs_1_), channel_id=1, source_target_pairs={{2,0},{3,1},{0,2},{1,3},{6,4},{7,5},{4,6},{5,7},{10,8},{11,9},{8,1... | collective-permute-start | bytes 393224 | tf_op jit(solution)/shard_map/ppermute | solution.py:24
  23.4 4.1 %collective-permute-done.6.refs_1_ = bf16[128,512]{1,0:T(8,128)(2,1)S(1)} collective-permute-done((bf16[128,512]{1,0:T(8,128)(2,1)S(1)}, bf16[128,512]{1,0:T(8,128)(2,1)S(1)}, u32[]{:S(2)}, u32[]{:S(2)}) %collective-permute-start.6) | collective-permute-done | bytes 131104 | tf_op jit(solution)/shard_map/ppermute | solution.py:24
  27.5 2.1 %collective-permute-done.7.refs_1_ = bf16[128,512]{1,0:T(8,128)(2,1)S(1)} collective-permute-done((bf16[128,512]{1,0:T(8,128)(2,1)S(1)}, bf16[128,512]{1,0:T(8,128)(2,1)S(1)}, u32[]{:S(2)}, u32[]{:S(2)}) %collective-permute-start.7) | collective-permute-done | bytes 131104 | tf_op jit(solution)/shard_map/ppermute | solution.py:24
  29.6 1.6 %collective-permute-start.13 = (bf16[128,512]{1,0:T(8,128)(2,1)S(1)}, bf16[128,512]{1,0:T(8,128)(2,1)S(1)}, u32[]{:S(2)}, u32[]{:S(2)}) collective-permute-start(bf16[128,512]{1,0:T(8,128)(2,1)S(1)} %collective-permute-done.6.refs_1_), channel_id=1, source_target_pairs={{6,0},{7,1},{4,2},{5,3},{2,4},{3,5},{0,6},{1,7},{14,8},{15,9},{12,... | collective-permute-start | bytes 393224 | tf_op jit(solution)/shard_map/ppermute | solution.py:24
  31.3 0.3 collective-permute-start.14
  31.6 1.5 %collective-permute-start.15 = (bf16[128,512]{1,0:T(8,128)(2,1)S(1)}, bf16[128,512]{1,0:T(8,128)(2,1)S(1)}, u32[]{:S(2)}, u32[]{:S(2)}) collective-permute-start(bf16[128,512]{1,0:T(8,128)(2,1)S(1)} %collective-permute-done.6.refs_1_), channel_id=1, source_target_pairs={{2,0},{3,1},{0,2},{1,3},{6,4},{7,5},{4,6},{5,7},{10,8},{11,9},{8,1... | collective-permute-start | bytes 393224 | tf_op jit(solution)/shard_map/ppermute | solution.py:24
  33.1 0.5 %collective-permute-start.10 = (bf16[128,512]{1,0:T(8,128)(2,1)S(1)}, bf16[128,512]{1,0:T(8,128)(2,1)S(1)}, u32[]{:S(2)}, u32[]{:S(2)}) collective-permute-start(bf16[128,512]{1,0:T(8,128)(2,1)S(1)} %collective-permute-done.7.refs_1_), channel_id=1, source_target_pairs={{2,0},{3,1},{0,2},{1,3},{6,4},{7,5},{4,6},{5,7},{10,8},{11,9},{8,1... | collective-permute-start | bytes 393224 | tf_op jit(solution)/shard_map/ppermute | solution.py:24
  33.6 2.0 %score.4.refs_5_ = f32[2048,512]{1,0:T(8,128)S(1)} custom-call(bf16[2048,2048]{1,0:T(8,128)(2,1)S(1)} %get-tuple-element.27.refs_0_, bf16[128,512]{1,0:T(8,128)(2,1)S(1)} %condition.1.refs_1_, bf16[128,512]{1,0:T(8,128)(2,1)S(1)} %collective-permute-done.16.refs_2_, bf16[128,512]{1,0:T(8,128)(2,1)S(1)} %collective-permute-done.8.refs_3_, ...), custom_call_target="tpu_custom_call" | custom-call | flops 1073741824 | bytes 4194304 | tf_op jit(solution)/shard_map/score/pallas_call | solution.py:160
  35.6 1.2 %collective-permute-done.13.refs_3_ = bf16[128,512]{1,0:T(8,128)(2,1)S(1)} collective-permute-done((bf16[128,512]{1,0:T(8,128)(2,1)S(1)}, bf16[128,512]{1,0:T(8,128)(2,1)S(1)}, u32[]{:S(2)}, u32[]{:S(2)}) %collective-permute-start.13) | collective-permute-done | bytes 131104 | tf_op jit(solution)/shard_map/ppermute | solution.py:24
  36.9 1.4 %collective-permute-done.14.refs_1_ = bf16[128,512]{1,0:T(8,128)(2,1)S(1)} collective-permute-done((bf16[128,512]{1,0:T(8,128)(2,1)S(1)}, bf16[128,512]{1,0:T(8,128)(2,1)S(1)}, u32[]{:S(2)}, u32[]{:S(2)}) %collective-permute-start.14) | collective-permute-done | bytes 131104 | tf_op jit(solution)/shard_map/ppermute | solution.py:24
  38.3 1.0 %collective-permute-done.15.refs_3_ = bf16[128,512]{1,0:T(8,128)(2,1)S(1)} collective-permute-done((bf16[128,512]{1,0:T(8,128)(2,1)S(1)}, bf16[128,512]{1,0:T(8,128)(2,1)S(1)}, u32[]{:S(2)}, u32[]{:S(2)}) %collective-permute-start.15) | collective-permute-done | bytes 131104 | tf_op jit(solution)/shard_map/ppermute | solution.py:24
  39.3 0.5 %collective-permute-start.20 = (bf16[128,512]{1,0:T(8,128)(2,1)S(1)}, bf16[128,512]{1,0:T(8,128)(2,1)S(1)}, u32[]{:S(2)}, u32[]{:S(2)}) collective-permute-start(bf16[128,512]{1,0:T(8,128)(2,1)S(1)} %collective-permute-done.13.refs_3_), channel_id=1, source_target_pairs={{1,0},{0,1},{3,2},{2,3},{5,4},{4,5},{7,6},{6,7},{9,8},{8,9},{11,10... | collective-permute-start | bytes 393224 | tf_op jit(solution)/shard_map/ppermute | solution.py:24
  39.8 0.0 collective-permute-start.12
  39.8 0.5 %collective-permute-start.18 = (bf16[128,512]{1,0:T(8,128)(2,1)S(1)}, bf16[128,512]{1,0:T(8,128)(2,1)S(1)}, u32[]{:S(2)}, u32[]{:S(2)}) collective-permute-start(bf16[128,512]{1,0:T(8,128)(2,1)S(1)} %collective-permute-done.15.refs_3_), channel_id=1, source_target_pairs={{1,0},{0,1},{3,2},{2,3},{5,4},{4,5},{7,6},{6,7},{9,8},{8,9},{11,10... | collective-permute-start | bytes 393224 | tf_op jit(solution)/shard_map/ppermute | solution.py:24
  40.4 1.7 %collective-permute-done.10.refs_3_ = bf16[128,512]{1,0:T(8,128)(2,1)S(1)} collective-permute-done((bf16[128,512]{1,0:T(8,128)(2,1)S(1)}, bf16[128,512]{1,0:T(8,128)(2,1)S(1)}, u32[]{:S(2)}, u32[]{:S(2)}) %collective-permute-start.10) | collective-permute-done | bytes 131104 | tf_op jit(solution)/shard_map/ppermute | solution.py:24
  42.1 0.0 collective-permute-start.9
  42.1 0.5 collective-permute-start.11
  42.6 2.1 %score.5.refs_5_ = f32[2048,512]{1,0:T(8,128)S(1)} custom-call(bf16[2048,2048]{1,0:T(8,128)(2,1)S(1)} %get-tuple-element.27.refs_0_, bf16[128,512]{1,0:T(8,128)(2,1)S(1)} %collective-permute-done.14.refs_1_, bf16[128,512]{1,0:T(8,128)(2,1)S(1)} %collective-permute-done.19.refs_2_, ...), custom_call_target="tpu_custom_call", output_to_operand_aliasing={{}: (5, {})} | custom-call | flops 1073741824 | bytes 4194304 | tf_op jit(solution)/shard_map/score/pallas_call | solution.py:160
  44.7 2.2 %score.6.refs_5_ = f32[2048,512]{1,0:T(8,128)S(1)} custom-call(bf16[2048,2048]{1,0:T(8,128)(2,1)S(1)} %get-tuple-element.27.refs_0_, bf16[128,512]{1,0:T(8,128)(2,1)S(1)} %collective-permute-done.6.refs_1_, bf16[128,512]{1,0:T(8,128)(2,1)S(1)} %collective-permute-done.12.refs_2_, ...), custom_call_target="tpu_custom_call", output_to_operand_aliasing={{}: (5, {})} | custom-call | flops 1073741824 | bytes 4194304 | tf_op jit(solution)/shard_map/score/pallas_call | solution.py:160
  46.9 3.0 %score.7 = f32[2048,512]{1,0:T(8,128)} custom-call(bf16[2048,2048]{1,0:T(8,128)(2,1)S(1)} %get-tuple-element.27.refs_0_, bf16[128,512]{1,0:T(8,128)(2,1)S(1)} %collective-permute-done.7.refs_1_, bf16[128,512]{1,0:T(8,128)(2,1)S(1)} %collective-permute-done.9.refs_2_, bf16[128,512]{1,0:T(8,128)(2,1)S(1)} %collective-permute-done.10.refs_3_, ...), custom_call_target="tpu_custom_call" | custom-call | flops 1073741824 | bytes 4194304 | tf_op jit(solution)/shard_map/score/pallas_call | solution.py:160
  (18 shorter events, 0.0 us)
Async XLA Ops:
  0.0 12.5 %copy-start = (bf16[1,2048,128]{2,1,0:T(8,128)(2,1)S(1)}, bf16[1,2048,128]{2,1,0:T(8,128)(2,1)}, u32[]{:S(2)}) copy-start(bf16[1,2048,128]{2,1,0:T(8,128)(2,1)} %refs_2_.1) | copy-start | bytes 1572868
  0.0 16.4 %collective-permute-start.1 = (bf16[1,2048,128]{2,1,0:T(8,128)(2,1)}, bf16[1,2048,128]{2,1,0:T(8,128)(2,1)S(1)}, u32[]{:S(2)}, u32[]{:S(2)}) collective-permute-start(bf16[1,2048,128]{2,1,0:T(8,128)(2,1)} %refs_2_.1), channel_id=1, source_target_pairs={{2,0},{3,1},{0,2},{1,3},{6,4},{7,5},{4,6},{5,7},{10,8},{11,9},{8,1... | collective-permute-start | bytes 1572872 | tf_op jit(solution)/shard_map/ppermute | solution.py:24
  3.0 8.4 %collective-permute-start = (bf16[2,16,2048]{2,1,0:T(8,128)(2,1)}, bf16[2,16,2048]{2,1,0:T(8,128)(2,1)S(1)}, u32[]{:S(2)}, u32[]{:S(2)}) collective-permute-start(bf16[2,16,2048]{2,1,0:T(8,128)(2,1)} %refs_1_.1), channel_id=1, source_target_pairs={{12,0},{13,1},{14,2},{15,3},{8,4},{9,5},{10,6},{11,7},{4,8},{5,9},... | collective-permute-start | bytes 393224 | tf_op jit(solution)/shard_map/ppermute | solution.py:24
  6.6 7.2 %collective-permute-start.2 = (bf16[2,16,2048]{2,1,0:T(8,128)(2,1)}, bf16[2,16,2048]{2,1,0:T(8,128)(2,1)S(1)}, u32[]{:S(2)}, u32[]{:S(2)}) collective-permute-start(bf16[2,16,2048]{2,1,0:T(8,128)(2,1)} %refs_1_.1), channel_id=1, source_target_pairs={{4,0},{5,1},{6,2},{7,3},{0,4},{1,5},{2,6},{3,7},{12,8},{13,9},{14,... | collective-permute-start | bytes 393224 | tf_op jit(solution)/shard_map/ppermute | solution.py:24
  11.4 5.0 %collective-permute-start.3 = (bf16[2,16,2048]{2,1,0:T(8,128)(2,1)S(1)}, bf16[2,16,2048]{2,1,0:T(8,128)(2,1)S(1)}, u32[]{:S(2)}, u32[]{:S(2)}) collective-permute-start(bf16[2,16,2048]{2,1,0:T(8,128)(2,1)S(1)} %collective-permute-done.refs_3_), channel_id=1, source_target_pairs={{4,0},{5,1},{6,2},{7,3},{0,4},{1,5},{2,6},{3,7},{12,8},{13,9},{14,... | collective-permute-start | bytes 393224 | tf_op jit(solution)/shard_map/ppermute | solution.py:24
  12.5 3.9 %collective-permute-start.4 = (bf16[1,2048,128]{2,1,0:T(8,128)(2,1)S(1)}, bf16[1,2048,128]{2,1,0:T(8,128)(2,1)S(1)}, u32[]{:S(2)}, u32[]{:S(2)}) collective-permute-start(bf16[1,2048,128]{2,1,0:T(8,128)(2,1)S(1)} %copy-done), channel_id=1, source_target_pairs={{1,0},{0,1},{3,2},{2,3},{5,4},{4,5},{7,6},{6,7},{9,8},{8,9},{11,10... | collective-permute-start | bytes 1572872 | tf_op jit(solution)/shard_map/ppermute | solution.py:24
  16.4 1.9 %collective-permute-start.5 = (bf16[1,2048,128]{2,1,0:T(8,128)(2,1)S(1)}, bf16[1,2048,128]{2,1,0:T(8,128)(2,1)S(1)}, u32[]{:S(2)}, u32[]{:S(2)}) collective-permute-start(bf16[1,2048,128]{2,1,0:T(8,128)(2,1)S(1)} %collective-permute-done.1.refs_6_), channel_id=1, source_target_pairs={{1,0},{0,1},{3,2},{2,3},{5,4},{4,5},{7,6},{6,7},{9,8},{8,9},{11,10... | collective-permute-start | bytes 1572872 | tf_op jit(solution)/shard_map/ppermute | solution.py:24
  19.3 8.2 %collective-permute-start.6 = (bf16[128,512]{1,0:T(8,128)(2,1)S(1)}, bf16[128,512]{1,0:T(8,128)(2,1)S(1)}, u32[]{:S(2)}, u32[]{:S(2)}) collective-permute-start(bf16[128,512]{1,0:T(8,128)(2,1)S(1)} %condition.1.refs_1_), channel_id=1, source_target_pairs={{12,0},{13,1},{14,2},{15,3},{8,4},{9,5},{10,6},{11,7},{4,8},{5,9},... | collective-permute-start | bytes 393224 | tf_op jit(solution)/shard_map/ppermute | solution.py:24
  22.9 6.7 %collective-permute-start.7 = (bf16[128,512]{1,0:T(8,128)(2,1)S(1)}, bf16[128,512]{1,0:T(8,128)(2,1)S(1)}, u32[]{:S(2)}, u32[]{:S(2)}) collective-permute-start(bf16[128,512]{1,0:T(8,128)(2,1)S(1)} %condition.1.refs_1_), channel_id=1, source_target_pairs={{4,0},{5,1},{6,2},{7,3},{0,4},{1,5},{2,6},{3,7},{12,8},{13,9},{14,... | collective-permute-start | bytes 393224 | tf_op jit(solution)/shard_map/ppermute | solution.py:24
  22.9 6.7 %collective-permute-start.8 = (bf16[128,512]{1,0:T(8,128)(2,1)S(1)}, bf16[128,512]{1,0:T(8,128)(2,1)S(1)}, u32[]{:S(2)}, u32[]{:S(2)}) collective-permute-start(bf16[128,512]{1,0:T(8,128)(2,1)S(1)} %condition.1.refs_1_), channel_id=1, source_target_pairs={{2,0},{3,1},{0,2},{1,3},{6,4},{7,5},{4,6},{5,7},{10,8},{11,9},{8,1... | collective-permute-start | bytes 393224 | tf_op jit(solution)/shard_map/ppermute | solution.py:24
  23.4 9.7 %collective-permute-start.16 = (bf16[128,512]{1,0:T(8,128)(2,1)S(1)}, bf16[128,512]{1,0:T(8,128)(2,1)S(1)}, u32[]{:S(2)}, u32[]{:S(2)}) collective-permute-start(bf16[128,512]{1,0:T(8,128)(2,1)S(1)} %condition.1.refs_1_), channel_id=1, source_target_pairs={{1,0},{0,1},{3,2},{2,3},{5,4},{4,5},{7,6},{6,7},{9,8},{8,9},{11,10... | collective-permute-start | bytes 393224 | tf_op jit(solution)/shard_map/ppermute | solution.py:24
  29.6 4.0 %collective-permute-start.17 = (bf16[128,512]{1,0:T(8,128)(2,1)S(1)}, bf16[128,512]{1,0:T(8,128)(2,1)S(1)}, u32[]{:S(2)}, u32[]{:S(2)}) collective-permute-start(bf16[128,512]{1,0:T(8,128)(2,1)S(1)} %collective-permute-done.8.refs_3_), channel_id=1, source_target_pairs={{1,0},{0,1},{3,2},{2,3},{5,4},{4,5},{7,6},{6,7},{9,8},{8,9},{11,10... | collective-permute-start | bytes 393224 | tf_op jit(solution)/shard_map/ppermute | solution.py:24
  29.6 7.2 %collective-permute-start.13 = (bf16[128,512]{1,0:T(8,128)(2,1)S(1)}, bf16[128,512]{1,0:T(8,128)(2,1)S(1)}, u32[]{:S(2)}, u32[]{:S(2)}) collective-permute-start(bf16[128,512]{1,0:T(8,128)(2,1)S(1)} %collective-permute-done.6.refs_1_), channel_id=1, source_target_pairs={{6,0},{7,1},{4,2},{5,3},{2,4},{3,5},{0,6},{1,7},{14,8},{15,9},{12,... | collective-permute-start | bytes 393224 | tf_op jit(solution)/shard_map/ppermute | solution.py:24
  31.3 7.0 %collective-permute-start.14 = (bf16[128,512]{1,0:T(8,128)(2,1)S(1)}, bf16[128,512]{1,0:T(8,128)(2,1)S(1)}, u32[]{:S(2)}, u32[]{:S(2)}) collective-permute-start(bf16[128,512]{1,0:T(8,128)(2,1)S(1)} %collective-permute-done.6.refs_1_), channel_id=1, source_target_pairs={{4,0},{5,1},{6,2},{7,3},{0,4},{1,5},{2,6},{3,7},{12,8},{13,9},{14,... | collective-permute-start | bytes 393224 | tf_op jit(solution)/shard_map/ppermute | solution.py:24
  31.6 7.7 %collective-permute-start.15 = (bf16[128,512]{1,0:T(8,128)(2,1)S(1)}, bf16[128,512]{1,0:T(8,128)(2,1)S(1)}, u32[]{:S(2)}, u32[]{:S(2)}) collective-permute-start(bf16[128,512]{1,0:T(8,128)(2,1)S(1)} %collective-permute-done.6.refs_1_), channel_id=1, source_target_pairs={{2,0},{3,1},{0,2},{1,3},{6,4},{7,5},{4,6},{5,7},{10,8},{11,9},{8,1... | collective-permute-start | bytes 393224 | tf_op jit(solution)/shard_map/ppermute | solution.py:24
  33.1 8.9 %collective-permute-start.10 = (bf16[128,512]{1,0:T(8,128)(2,1)S(1)}, bf16[128,512]{1,0:T(8,128)(2,1)S(1)}, u32[]{:S(2)}, u32[]{:S(2)}) collective-permute-start(bf16[128,512]{1,0:T(8,128)(2,1)S(1)} %collective-permute-done.7.refs_1_), channel_id=1, source_target_pairs={{2,0},{3,1},{0,2},{1,3},{6,4},{7,5},{4,6},{5,7},{10,8},{11,9},{8,1... | collective-permute-start | bytes 393224 | tf_op jit(solution)/shard_map/ppermute | solution.py:24
  39.3 2.7 %collective-permute-start.19 = (bf16[128,512]{1,0:T(8,128)(2,1)S(1)}, bf16[128,512]{1,0:T(8,128)(2,1)S(1)}, u32[]{:S(2)}, u32[]{:S(2)}) collective-permute-start(bf16[128,512]{1,0:T(8,128)(2,1)S(1)} %collective-permute-done.14.refs_1_), channel_id=1, source_target_pairs={{1,0},{0,1},{3,2},{2,3},{5,4},{4,5},{7,6},{6,7},{9,8},{8,9},{11,10... | collective-permute-start | bytes 393224 | tf_op jit(solution)/shard_map/ppermute | solution.py:24
  39.3 3.2 %collective-permute-start.20 = (bf16[128,512]{1,0:T(8,128)(2,1)S(1)}, bf16[128,512]{1,0:T(8,128)(2,1)S(1)}, u32[]{:S(2)}, u32[]{:S(2)}) collective-permute-start(bf16[128,512]{1,0:T(8,128)(2,1)S(1)} %collective-permute-done.13.refs_3_), channel_id=1, source_target_pairs={{1,0},{0,1},{3,2},{2,3},{5,4},{4,5},{7,6},{6,7},{9,8},{8,9},{11,10... | collective-permute-start | bytes 393224 | tf_op jit(solution)/shard_map/ppermute | solution.py:24
  39.8 4.9 %collective-permute-start.12 = (bf16[128,512]{1,0:T(8,128)(2,1)S(1)}, bf16[128,512]{1,0:T(8,128)(2,1)S(1)}, u32[]{:S(2)}, u32[]{:S(2)}) collective-permute-start(bf16[128,512]{1,0:T(8,128)(2,1)S(1)} %collective-permute-done.6.refs_1_), channel_id=1, source_target_pairs={{1,0},{0,1},{3,2},{2,3},{5,4},{4,5},{7,6},{6,7},{9,8},{8,9},{11,10... | collective-permute-start | bytes 393224 | tf_op jit(solution)/shard_map/ppermute | solution.py:24
  39.8 4.9 %collective-permute-start.18 = (bf16[128,512]{1,0:T(8,128)(2,1)S(1)}, bf16[128,512]{1,0:T(8,128)(2,1)S(1)}, u32[]{:S(2)}, u32[]{:S(2)}) collective-permute-start(bf16[128,512]{1,0:T(8,128)(2,1)S(1)} %collective-permute-done.15.refs_3_), channel_id=1, source_target_pairs={{1,0},{0,1},{3,2},{2,3},{5,4},{4,5},{7,6},{6,7},{9,8},{8,9},{11,10... | collective-permute-start | bytes 393224 | tf_op jit(solution)/shard_map/ppermute | solution.py:24
  42.1 4.8 %collective-permute-start.9 = (bf16[128,512]{1,0:T(8,128)(2,1)S(1)}, bf16[128,512]{1,0:T(8,128)(2,1)S(1)}, u32[]{:S(2)}, u32[]{:S(2)}) collective-permute-start(bf16[128,512]{1,0:T(8,128)(2,1)S(1)} %collective-permute-done.7.refs_1_), channel_id=1, source_target_pairs={{1,0},{0,1},{3,2},{2,3},{5,4},{4,5},{7,6},{6,7},{9,8},{8,9},{11,10... | collective-permute-start | bytes 393224 | tf_op jit(solution)/shard_map/ppermute | solution.py:24
  42.1 4.8 %collective-permute-start.11 = (bf16[128,512]{1,0:T(8,128)(2,1)S(1)}, bf16[128,512]{1,0:T(8,128)(2,1)S(1)}, u32[]{:S(2)}, u32[]{:S(2)}) collective-permute-start(bf16[128,512]{1,0:T(8,128)(2,1)S(1)} %collective-permute-done.10.refs_3_), channel_id=1, source_target_pairs={{1,0},{0,1},{3,2},{2,3},{5,4},{4,5},{7,6},{6,7},{9,8},{8,9},{11,10... | collective-permute-start | bytes 393224 | tf_op jit(solution)/shard_map/ppermute | solution.py:24

commit v6 on v5

v6 whole, which is shorter than its diff:
```python
import functools

import jax
import jax.numpy as jnp
from jax import lax
from jax.experimental import pallas as pl
from jax.experimental.pallas import tpu as pltpu
from jax.sharding import PartitionSpec as P

VMEM = pl.BlockSpec(memory_space=pltpu.VMEM)
ANY = pl.BlockSpec(memory_space=pl.ANY)


class Grid:
    def __init__(self, row_count):
        self.far = row_count // 4

    def swap(self, block, far, near, core):
        step = (far * 2 + near) * 2 + core
        return lax.ppermute(block, "rows", [(row ^ step, row) for row in range(self.far * 4)])

    def place(self):
        row = lax.axis_index("rows")
        return lax.div(row, 4), lax.rem(lax.div(row, 2), 2), lax.rem(row, 2)


def flip(part, mask):
    return lax.bitwise_xor(part, jnp.int32(mask))


def columns(index, width):
    return pl.ds(pl.multiple_of(index * width, width), width)


def stage_kernel(count, *refs):
    sources, targets, sems = refs[:count], refs[count : 2 * count], refs[2 * count]
    copies = [
        pltpu.make_async_copy(source, target, sems.at[i]) for i, (source, target) in enumerate(zip(sources, targets))
    ]
    for copy in copies:
        copy.start()
    for copy in copies:
        copy.wait()


def stage(*arrays):
    size = sum(a.size * a.dtype.itemsize for a in arrays)
    return pl.pallas_call(
        functools.partial(stage_kernel, len(arrays)),
        out_shape=[pltpu.VMEM(a.shape, a.dtype) for a in arrays],
        in_specs=[ANY] * len(arrays),
        out_specs=[VMEM] * len(arrays),
        scratch_shapes=[pltpu.SemaphoreType.DMA((len(arrays),))],
        compiler_params=pltpu.CompilerParams(vmem_limit_bytes=4 << 20),
        cost_estimate=pl.CostEstimate(flops=0, bytes_accessed=2 * size, transcendentals=0),
        name="stage",
    )(*(pltpu.with_memory_space_constraint(a, pltpu.HBM) for a in arrays))


def condition_kernel(grid, places, *refs):
    query_refs, (own_ref, near_ref, out_ref) = refs[: len(places)], refs[len(places) :]
    far, near, core = grid.place()
    rows = jnp.concatenate([ref[...].reshape(-1, ref.shape[-1]) for ref in query_refs])
    fisher = jnp.concatenate([own_ref[0], near_ref[0]], axis=1)
    result = jnp.dot(rows, fisher, preferred_element_type=jnp.float32).astype(out_ref.dtype)
    blocks, count, _ = query_refs[0].shape
    width = own_ref.shape[-1]
    result = result.reshape(len(places), blocks, 1, 1, count, 2 * width)
    for index, (far_mask, core_mask) in enumerate(places):
        for side in range(2):
            out_ref[
                :, pl.ds(flip(far, far_mask), 1), pl.ds(flip(core, core_mask), 1), :, columns(flip(near, side), width)
            ] = result[index, ..., side * width : (side + 1) * width]


def condition(grid, queries, own, near):
    blocks, count, _ = queries[0, 0].shape
    width = own.shape[-1]
    arrays = [*queries.values(), own, near]
    return pl.pallas_call(
        functools.partial(condition_kernel, grid, list(queries)),
        out_shape=jax.ShapeDtypeStruct((blocks, grid.far, 2, count, 2 * width), jnp.bfloat16),
        in_specs=[VMEM] * len(arrays),
        out_specs=VMEM,
        compiler_params=pltpu.CompilerParams(vmem_limit_bytes=12 << 20),
        cost_estimate=pl.CostEstimate(flops=1 << 28, bytes_accessed=3 << 20, transcendentals=0),
        name="condition",
    )(*arrays)


def turn_kernel(grid, masks, *refs):
    part_refs, out_ref, sorted_ref = refs[:-2], refs[-2], refs[-1]
    _, near, _ = grid.place()
    width = part_refs[0].shape[-1]
    for index in range(len(masks)):
        for side in range(2):
            sorted_ref[:, :, pl.ds(flip(near, side), 1), :, :, index * width : (index + 1) * width] = part_refs[
                index * 2 + side
            ][...][:, :, None]
    out_ref[...] = sorted_ref[...].reshape(-1, out_ref.shape[0]).T


def turn(grid, parts, masks):
    arrays = [parts[mask, near] for mask in masks for near in range(2)]
    blocks, far, cores, count, width = arrays[0].shape
    features = len(masks) * width
    return pl.pallas_call(
        functools.partial(turn_kernel, grid, masks),
        out_shape=pltpu.VMEM((features, blocks * far * 2 * cores * count), jnp.bfloat16),
        in_specs=[VMEM] * len(arrays),
        out_specs=VMEM,
        scratch_shapes=[pltpu.VMEM((blocks, far, 2, cores, count, features), jnp.bfloat16)],
        compiler_params=pltpu.CompilerParams(vmem_limit_bytes=8 << 20),
        name="turn",
    )(*(pltpu.with_memory_space_constraint(a, pltpu.VMEM) for a in arrays))


def score_kernel(grid, tile, masks, other, first, last, *refs):
    train_ref, turned_ref, refs = refs[0], refs[1], refs[2:]
    total_ref, refs = (None, refs) if first else (refs[0], refs[1:])
    out_ref, refs = refs[0], refs[1:]
    far, _, core = grid.place()
    features = train_ref.shape[1]
    width = features // (grid.far * 4)
    pieces = [
        columns((flip(far, mask) * 2 + side) * 2 + flip(core, other), width) for mask in masks for side in range(2)
    ]
    scale = 1.0 / features**0.5
    steps = train_ref.shape[0] // tile

    def rows(step):
        return pl.ds(pl.multiple_of(step * tile, tile), tile)

    def products(step):
        train = jnp.concatenate([train_ref[rows(step), piece] for piece in pieces], axis=1)
        value = jnp.dot(train, turned_ref[...], preferred_element_type=jnp.float32)
        return value if first else total_ref[rows(step)] + value

    if not last:

        @pl.loop(0, steps)
        def _(step):
            out_ref[rows(step)] = products(step)

        return

    here_ref, sem = refs

    def copy(step):
        return pltpu.make_async_copy(here_ref.at[rows(step)], out_ref.at[rows(step)], sem.at[step])

    @pl.loop(0, steps)
    def _(step):
        here_ref[rows(step)] = products(step) * scale
        copy(step).start()

    @pl.loop(0, steps)
    def _(step):
        copy(step).wait()


def score(grid, train_feats, turned, total, masks, other, last):
    rows = train_feats.shape[0]
    features, queries = turned.shape
    tile = 512
    first = total is None
    arrays = [train_feats, turned] + ([] if first else [total])
    shape = (rows, queries)
    scratch = [pltpu.VMEM(shape, jnp.float32), pltpu.SemaphoreType.DMA((rows // tile,))] if last else []
    return pl.pallas_call(
        functools.partial(score_kernel, grid, tile, masks, other, first, last),
        out_shape=jax.ShapeDtypeStruct(shape, jnp.float32) if last else pltpu.VMEM(shape, jnp.float32),
        in_specs=[VMEM] * len(arrays),
        out_specs=ANY if last else VMEM,
        scratch_shapes=scratch,
        input_output_aliases={} if first or last else {2: 0},
        compiler_params=pltpu.CompilerParams(vmem_limit_bytes=16 << 20),
        cost_estimate=pl.CostEstimate(
            flops=2 * rows * features * queries, bytes_accessed=4 << 20, transcendentals=0
        ),
        name="score",
    )(*(pltpu.with_memory_space_constraint(a, pltpu.VMEM) for a in arrays))


def two_level(grid, train_feats, queries, inverse_fisher):
    beside, mirror, relayed = 1, 3, 2
    gathered = {(0, 0): queries}
    gathered[0, 1] = grid.swap(queries, 0, 0, 1)
    gathered[beside, 0] = grid.swap(queries, beside, 0, 0)
    near_fisher = grid.swap(inverse_fisher, 0, 1, 0)
    gathered[mirror, 0] = grid.swap(queries, mirror, 0, 0)
    staged = stage(train_feats, queries, inverse_fisher)
    gathered[mirror, 0], staged = lax.optimization_barrier((gathered[mirror, 0], staged))
    train_here, gathered[0, 0], fisher_here = staged
    gathered[relayed, 0] = grid.swap(gathered[mirror, 0], beside, 0, 0)
    for mask in (beside, mirror, relayed):
        gathered[mask, 1] = grid.swap(gathered[mask, 0], 0, 0, 1)

    own, near_one, far_one, far_three = (0, 0), (0, 1), (beside, 0), (mirror, 0)
    parts = {own: condition(grid, gathered, fisher_here, near_fisher)}

    def swap(source, far, near):
        parts[source[0] ^ far, source[1] ^ near] = grid.swap(parts[source], far, near, 0)

    def meet(*places):
        parts.update(zip(places, lax.optimization_barrier([parts[place] for place in places])))

    swap(own, *far_three)
    swap(own, *near_one)
    swap(own, *far_one)
    swap(own, beside, 1)
    meet(near_one, (beside, 1), far_one, far_three)
    swap(far_three, 0, 1)
    swap(far_three, beside, 1)
    swap(far_three, beside, 0)
    total = None
    for masks in ((0, beside), (mirror, relayed)):
        turned = turn(grid, parts, masks)
        other = grid.swap(turned, 0, 0, 1)
        total = score(grid, train_here, turned, total, masks, 0, False)
        total = score(grid, train_here, other, total, masks, 1, masks == (mirror, relayed))
        if masks == (0, beside):
            late = (mirror, 0), (relayed, 1), (relayed, 0), (mirror, 1)
            held, total = lax.optimization_barrier(([parts[place] for place in late], total))
            parts.update(zip(late, held))
    return total


def one_level(train_feats, queries, inverse_fisher):
    group_count, group_width, _ = inverse_fisher.shape
    gathered = lax.all_gather(queries, "rows", axis=1, tiled=True)
    flattened = gathered.reshape(-1, group_count, group_width)
    part = jnp.einsum("qgk,gkc->qgc", flattened, inverse_fisher, preferred_element_type=jnp.float32)
    complete = lax.all_gather(part.astype(jnp.bfloat16), "rows", axis=2, tiled=True)
    conditioned = complete.reshape(flattened.shape[0], -1)
    products = lax.dot_general(
        train_feats, conditioned, (((1,), (1,)), ((), ())), preferred_element_type=jnp.float32
    )
    return products * (1.0 / train_feats.shape[1] ** 0.5)


def per_device(row_count, train_feats, queries, inverse_fisher):
    group_count, _, width = inverse_fisher.shape
    whole_tiles = group_count == 1 and width % 128 == 0 and queries.shape[1] % 16 == 0
    if row_count == 16 and whole_tiles and train_feats.shape[0] % 512 == 0:
        return two_level(Grid(row_count), train_feats, queries, inverse_fisher)
    return one_level(train_feats, queries, inverse_fisher)


def solution(mesh):
    placed = (P(("groups", "rows"), None), P(None, ("groups", "rows"), None), P(None, None, "rows"))
    return jax.shard_map(
        functools.partial(per_device, mesh.shape["rows"]),
        mesh=mesh,
        in_specs=placed,
        out_specs=P(("groups", "rows"), None),
        check_vma=False,
    )
```

time: 50.1 us -> 46.1 us (0.920)
  waiting for transfers between devices: 18.7 us -> 15 us
  Pallas kernels: 13.8 us -> 12.8 us
  starting transfers between devices: 17.4 us -> 18.1 us
    ppermute x21 -> x17, waiting for transfers between devices: 18.7 us -> 15 us  [swap(): lax.ppermute(block, 'rows', [(row ^ step, row) for row in range(self.far...]
    pallas_call x5 -> x7, Pallas kernels: 10.3 us -> 9.27 us  [the longest x4 8.37 us: score(): pl.pallas_call(functools.partial(score_kernel, grid, tile, masks, other,...]
    ppermute x21 -> x17, starting transfers between devices: 17.4 us -> 18.1 us  [swap(): lax.ppermute(block, 'rows', [(row ^ step, row) for row in range(self.far...]
  transfers between devices with their start and end apart: 21 -> 17, of which waited for: 10 -> 7; matrix products, arithmetic and copies ran while one was open for 0% -> 0% of each run, Pallas kernels for 20% -> 20%
where the time goes in v6:
time: 46.1 us; the launch traced here: 46 us
  starting transfers between devices  18.1 us (39%)
  waiting for transfers between devices  15 us (33%)
  Pallas kernels  12.8 us (28%)
    ppermute x17, starting transfers between devices, swap(): lax.ppermute(block, 'rows', [(row ^ step, row) for row in range(self.far...  18.1 us
    ppermute x17, waiting for transfers between devices, swap(): lax.ppermute(block, 'rows', [(row ^ step, row) for row in range(self.far...  15 us
    pallas_call x4, Pallas kernels, score(): pl.pallas_call(functools.partial(score_kernel, grid, tile, masks, other,...  8.37 us
    pallas_call x1, Pallas kernels, stage(): pl.pallas_call(functools.partial(stage_kernel, len(arrays)), out_shape=[p...  3.49 us
  transfers between devices with their start and end apart: 17, of which 7 were waited for; matrix products, arithmetic and copies ran while one was open for 0% of the time, Pallas kernels for 20%

profile of v6, /device:TPU:0, one launch (start us, length us, event | category | flops | bytes accessed | tf_op | source)
XLA Modules:
  0.0 46.0 jit_solution(3169743779078655919)
XLA Ops:
  0.0 3.0 %collective-permute-start.7 = (bf16[1,2048,128]{2,1,0:T(8,128)(2,1)}, bf16[1,2048,128]{2,1,0:T(8,128)(2,1)S(1)}, u32[]{:S(2)}, u32[]{:S(2)}) collective-permute-start(bf16[1,2048,128]{2,1,0:T(8,128)(2,1)} %refs_2_.1), channel_id=1, source_target_pairs={{2,0},{3,1},{0,2},{1,3},{6,4},{7,5},{4,6},{5,7},{10,8},{11,9},{8,1... | collective-permute-start | bytes 1572872 | tf_op jit(solution)/shard_map/ppermute | solution.py:20
  3.0 3.6 %collective-permute-start = (bf16[2,16,2048]{2,1,0:T(8,128)(2,1)}, bf16[2,16,2048]{2,1,0:T(8,128)(2,1)S(1)}, u32[]{:S(2)}, u32[]{:S(2)}) collective-permute-start(bf16[2,16,2048]{2,1,0:T(8,128)(2,1)} %refs_1_.1), channel_id=1, source_target_pairs={{12,0},{13,1},{14,2},{15,3},{8,4},{9,5},{10,6},{11,7},{4,8},{5,9},... | collective-permute-start | bytes 393224 | tf_op jit(solution)/shard_map/ppermute | solution.py:20
  6.6 0.0 collective-permute-start.2
  6.6 3.5 %stage.1 = (bf16[2048,2048]{1,0:T(8,128)(2,1)S(1)}, bf16[2,16,2048]{2,1,0:T(8,128)(2,1)S(1)}, bf16[1,2048,128]{2,1,0:T(8,128)(2,1)S(1)}) custom-call(bf16[2048,2048]{1,0:T(8,128)(2,1)} %refs_0_.1, bf16[2,16,2048]{2,1,0:T(8,128)(2,1)} %refs_1_.1, bf16[1,2048,128]{2,1,0:T(8,128)(2,1)} %refs_2_.1), custom_call_target="tpu_custom_call" | custom-call | bytes 18087936 | tf_op jit(solution)/shard_map/stage/pallas_call | solution.py:48
  10.1 1.3 %collective-permute-done.refs_3_ = bf16[2,16,2048]{2,1,0:T(8,128)(2,1)S(1)} collective-permute-done((bf16[2,16,2048]{2,1,0:T(8,128)(2,1)}, bf16[2,16,2048]{2,1,0:T(8,128)(2,1)S(1)}, u32[]{:S(2)}, u32[]{:S(2)}) %collective-permute-start) | collective-permute-done | bytes 131104 | tf_op jit(solution)/shard_map/ppermute | solution.py:20
  11.4 1.1 %collective-permute-start.3 = (bf16[2,16,2048]{2,1,0:T(8,128)(2,1)S(1)}, bf16[2,16,2048]{2,1,0:T(8,128)(2,1)S(1)}, u32[]{:S(2)}, u32[]{:S(2)}) collective-permute-start(bf16[2,16,2048]{2,1,0:T(8,128)(2,1)S(1)} %collective-permute-done.refs_3_), channel_id=1, source_target_pairs={{4,0},{5,1},{6,2},{7,3},{0,4},{1,5},{2,6},{3,7},{12,8},{13,9},{14,... | collective-permute-start | bytes 393224 | tf_op jit(solution)/shard_map/ppermute | solution.py:20
  12.5 0.5 %collective-permute-start.5 = (bf16[2,16,2048]{2,1,0:T(8,128)(2,1)S(1)}, bf16[2,16,2048]{2,1,0:T(8,128)(2,1)S(1)}, u32[]{:S(2)}, u32[]{:S(2)}) collective-permute-start(bf16[2,16,2048]{2,1,0:T(8,128)(2,1)S(1)} %collective-permute-done.refs_3_), channel_id=1, source_target_pairs={{1,0},{0,1},{3,2},{2,3},{5,4},{4,5},{7,6},{6,7},{9,8},{8,9},{11,10... | collective-permute-start | bytes 393224 | tf_op jit(solution)/shard_map/ppermute | solution.py:20
  13.0 0.7 %collective-permute-done.2.refs_2_ = bf16[2,16,2048]{2,1,0:T(8,128)(2,1)S(1)} collective-permute-done((bf16[2,16,2048]{2,1,0:T(8,128)(2,1)}, bf16[2,16,2048]{2,1,0:T(8,128)(2,1)S(1)}, u32[]{:S(2)}, u32[]{:S(2)}) %collective-permute-start.2) | collective-permute-done | bytes 131104 | tf_op jit(solution)/shard_map/ppermute | solution.py:20
  13.7 0.0 collective-permute-start.4
  13.7 2.6 %collective-permute-done.3.refs_4_ = bf16[2,16,2048]{2,1,0:T(8,128)(2,1)S(1)} collective-permute-done((bf16[2,16,2048]{2,1,0:T(8,128)(2,1)S(1)}, bf16[2,16,2048]{2,1,0:T(8,128)(2,1)S(1)}, u32[]{:S(2)}, u32[]{:S(2)}) %collective-permute-start.3) | collective-permute-done | bytes 131104 | tf_op jit(solution)/shard_map/ppermute | solution.py:20
  16.4 0.0 collective-permute-start.6
  16.4 1.3 %collective-permute-done.6.refs_7_ = bf16[2,16,2048]{2,1,0:T(8,128)(2,1)S(1)} collective-permute-done((bf16[2,16,2048]{2,1,0:T(8,128)(2,1)S(1)}, bf16[2,16,2048]{2,1,0:T(8,128)(2,1)S(1)}, u32[]{:S(2)}, u32[]{:S(2)}) %collective-permute-start.6) | collective-permute-done | bytes 131104 | tf_op jit(solution)/shard_map/ppermute | solution.py:20
  17.7 0.4 condition.1.refs_0_
  18.2 1.2 %collective-permute-start.10 = (bf16[2,4,2,16,256]{4,3,2,1,0:T(8,128)(2,1)S(1)}, bf16[2,4,2,16,256]{4,3,2,1,0:T(8,128)(2,1)S(1)}, u32[]{:S(2)}, u32[]{:S(2)}) collective-permute-start(bf16[2,4,2,16,256]{4,3,2,1,0:T(8,128)(2,1)S(1)} %condition.1.refs_0_), channel_id=1, source_target_pairs={{4,0},{5,1},{6,2},{7,3},{0,4},{1,5},{2,6},{3,7},{12,8},{13,9},{14,... | collective-permute-start | bytes 393224 | tf_op jit(solution)/shard_map/ppermute | solution.py:20
  19.4 2.5 %collective-permute-start.11 = (bf16[2,4,2,16,256]{4,3,2,1,0:T(8,128)(2,1)S(1)}, bf16[2,4,2,16,256]{4,3,2,1,0:T(8,128)(2,1)S(1)}, u32[]{:S(2)}, u32[]{:S(2)}) collective-permute-start(bf16[2,4,2,16,256]{4,3,2,1,0:T(8,128)(2,1)S(1)} %condition.1.refs_0_), channel_id=1, source_target_pairs={{12,0},{13,1},{14,2},{15,3},{8,4},{9,5},{10,6},{11,7},{4,8},{5,9},... | collective-permute-start | bytes 393224 | tf_op jit(solution)/shard_map/ppermute | solution.py:20
  21.9 0.5 %collective-permute-start.8 = (bf16[2,4,2,16,256]{4,3,2,1,0:T(8,128)(2,1)S(1)}, bf16[2,4,2,16,256]{4,3,2,1,0:T(8,128)(2,1)S(1)}, u32[]{:S(2)}, u32[]{:S(2)}) collective-permute-start(bf16[2,4,2,16,256]{4,3,2,1,0:T(8,128)(2,1)S(1)} %condition.1.refs_0_), channel_id=1, source_target_pairs={{2,0},{3,1},{0,2},{1,3},{6,4},{7,5},{4,6},{5,7},{10,8},{11,9},{8,1... | collective-permute-start | bytes 393224 | tf_op jit(solution)/shard_map/ppermute | solution.py:20
  22.4 2.0 %collective-permute-start.9 = (bf16[2,4,2,16,256]{4,3,2,1,0:T(8,128)(2,1)S(1)}, bf16[2,4,2,16,256]{4,3,2,1,0:T(8,128)(2,1)S(1)}, u32[]{:S(2)}, u32[]{:S(2)}) collective-permute-start(bf16[2,4,2,16,256]{4,3,2,1,0:T(8,128)(2,1)S(1)} %condition.1.refs_0_), channel_id=1, source_target_pairs={{6,0},{7,1},{4,2},{5,3},{2,4},{3,5},{0,6},{1,7},{14,8},{15,9},{12,... | collective-permute-start | bytes 393224 | tf_op jit(solution)/shard_map/ppermute | solution.py:20
  24.4 4.5 %collective-permute-done.11.refs_0_ = bf16[2,4,2,16,256]{4,3,2,1,0:T(8,128)(2,1)S(1)} collective-permute-done((bf16[2,4,2,16,256]{4,3,2,1,0:T(8,128)(2,1)S(1)}, bf16[2,4,2,16,256]{4,3,2,1,0:T(8,128)(2,1)S(1)}, u32[]{:S(2)}, u32[]{:S(2)}) %collective-permute-start.11) | collective-permute-done | bytes 131104 | tf_op jit(solution)/shard_map/ppermute | solution.py:20
  29.0 2.0 %collective-permute-done.9.refs_3_ = bf16[2,4,2,16,256]{4,3,2,1,0:T(8,128)(2,1)S(1)} collective-permute-done((bf16[2,4,2,16,256]{4,3,2,1,0:T(8,128)(2,1)S(1)}, bf16[2,4,2,16,256]{4,3,2,1,0:T(8,128)(2,1)S(1)}, u32[]{:S(2)}, u32[]{:S(2)}) %collective-permute-start.9) | collective-permute-done | bytes 131104 | tf_op jit(solution)/shard_map/ppermute | solution.py:20
  30.9 0.2 turn.2.refs_1_
  31.2 0.1 collective-permute-start.15
  31.2 0.6 %collective-permute-start.12 = (bf16[2,4,2,16,256]{4,3,2,1,0:T(8,128)(2,1)S(1)}, bf16[2,4,2,16,256]{4,3,2,1,0:T(8,128)(2,1)S(1)}, u32[]{:S(2)}, u32[]{:S(2)}) collective-permute-start(bf16[2,4,2,16,256]{4,3,2,1,0:T(8,128)(2,1)S(1)} %collective-permute-done.11.refs_0_), channel_id=1, source_target_pairs={{6,0},{7,1},{4,2},{5,3},{2,4},{3,5},{0,6},{1,7},{14,8},{15,9},{12,... | collective-permute-start | bytes 393224 | tf_op jit(solution)/shard_map/ppermute | solution.py:20
  31.9 2.4 %collective-permute-start.13 = (bf16[2,4,2,16,256]{4,3,2,1,0:T(8,128)(2,1)S(1)}, bf16[2,4,2,16,256]{4,3,2,1,0:T(8,128)(2,1)S(1)}, u32[]{:S(2)}, u32[]{:S(2)}) collective-permute-start(bf16[2,4,2,16,256]{4,3,2,1,0:T(8,128)(2,1)S(1)} %collective-permute-done.11.refs_0_), channel_id=1, source_target_pairs={{4,0},{5,1},{6,2},{7,3},{0,4},{1,5},{2,6},{3,7},{12,8},{13,9},{14,... | collective-permute-start | bytes 393224 | tf_op jit(solution)/shard_map/ppermute | solution.py:20
  34.3 0.5 %collective-permute-start.14 = (bf16[2,4,2,16,256]{4,3,2,1,0:T(8,128)(2,1)S(1)}, bf16[2,4,2,16,256]{4,3,2,1,0:T(8,128)(2,1)S(1)}, u32[]{:S(2)}, u32[]{:S(2)}) collective-permute-start(bf16[2,4,2,16,256]{4,3,2,1,0:T(8,128)(2,1)S(1)} %collective-permute-done.11.refs_0_), channel_id=1, source_target_pairs={{2,0},{3,1},{0,2},{1,3},{6,4},{7,5},{4,6},{5,7},{10,8},{11,9},{8,1... | collective-permute-start | bytes 393224 | tf_op jit(solution)/shard_map/ppermute | solution.py:20
  34.8 1.8 %score.4.refs_2_ = f32[2048,512]{1,0:T(8,128)S(1)} custom-call(bf16[2048,2048]{1,0:T(8,128)(2,1)S(1)} %get-tuple-element.24.refs_0_, bf16[512,512]{1,0:T(8,128)(2,1)S(1)} %turn.2.refs_1_), custom_call_target="tpu_custom_call" | custom-call | flops 1073741824 | bytes 4194304 | tf_op jit(solution)/shard_map/score/pallas_call | solution.py:170
  36.6 1.9 %score.5.refs_2_ = f32[2048,512]{1,0:T(8,128)S(1)} custom-call(bf16[2048,2048]{1,0:T(8,128)(2,1)S(1)} %get-tuple-element.24.refs_0_, bf16[512,512]{1,0:T(8,128)(2,1)S(1)} %collective-permute-done.15.refs_1_, f32[2048,512]{1,0:T(8,128)S(1)} %score.4.refs_2_), custom_call_target="tpu_custom_call", output_to_operand_aliasing={{}: (2, {})} | custom-call | flops 1073741824 | bytes 4194304 | tf_op jit(solution)/shard_map/score/pallas_call | solution.py:170
  38.5 0.0 collective-permute-done.12.refs_3_
  38.5 2.5 %collective-permute-done.13.refs_2_ = bf16[2,4,2,16,256]{4,3,2,1,0:T(8,128)(2,1)S(1)} collective-permute-done((bf16[2,4,2,16,256]{4,3,2,1,0:T(8,128)(2,1)S(1)}, bf16[2,4,2,16,256]{4,3,2,1,0:T(8,128)(2,1)S(1)}, u32[]{:S(2)}, u32[]{:S(2)}) %collective-permute-start.13) | collective-permute-done | bytes 131104 | tf_op jit(solution)/shard_map/ppermute | solution.py:20
  41.0 0.2 turn.3.refs_1_
  41.2 0.1 collective-permute-start.16
  41.3 1.9 %score.6.refs_2_ = f32[2048,512]{1,0:T(8,128)S(1)} custom-call(bf16[2048,2048]{1,0:T(8,128)(2,1)S(1)} %get-tuple-element.24.refs_0_, bf16[512,512]{1,0:T(8,128)(2,1)S(1)} %turn.3.refs_1_, f32[2048,512]{1,0:T(8,128)S(1)} %score.5.refs_2_), custom_call_target="tpu_custom_call", output_to_operand_aliasing={{}: (2, {})} | custom-call | flops 1073741824 | bytes 4194304 | tf_op jit(solution)/shard_map/score/pallas_call | solution.py:170
  43.2 2.8 %score.7 = f32[2048,512]{1,0:T(8,128)} custom-call(bf16[2048,2048]{1,0:T(8,128)(2,1)S(1)} %get-tuple-element.24.refs_0_, bf16[512,512]{1,0:T(8,128)(2,1)S(1)} %collective-permute-done.16.refs_1_, f32[2048,512]{1,0:T(8,128)S(1)} %score.6.refs_2_), custom_call_target="tpu_custom_call" | custom-call | flops 1073741824 | bytes 4194304 | tf_op jit(solution)/shard_map/score/pallas_call | solution.py:170
  (12 shorter events, 0.0 us)
Async XLA Ops:
  0.0 12.5 %copy-start = (bf16[2,16,2048]{2,1,0:T(8,128)(2,1)S(1)}, bf16[2,16,2048]{2,1,0:T(8,128)(2,1)}, u32[]{:S(2)}) copy-start(bf16[2,16,2048]{2,1,0:T(8,128)(2,1)} %refs_1_.1) | copy-start | bytes 393220
  0.0 17.7 %collective-permute-start.7 = (bf16[1,2048,128]{2,1,0:T(8,128)(2,1)}, bf16[1,2048,128]{2,1,0:T(8,128)(2,1)S(1)}, u32[]{:S(2)}, u32[]{:S(2)}) collective-permute-start(bf16[1,2048,128]{2,1,0:T(8,128)(2,1)} %refs_2_.1), channel_id=1, source_target_pairs={{2,0},{3,1},{0,2},{1,3},{6,4},{7,5},{4,6},{5,7},{10,8},{11,9},{8,1... | collective-permute-start | bytes 1572872 | tf_op jit(solution)/shard_map/ppermute | solution.py:20
  3.0 8.4 %collective-permute-start = (bf16[2,16,2048]{2,1,0:T(8,128)(2,1)}, bf16[2,16,2048]{2,1,0:T(8,128)(2,1)S(1)}, u32[]{:S(2)}, u32[]{:S(2)}) collective-permute-start(bf16[2,16,2048]{2,1,0:T(8,128)(2,1)} %refs_1_.1), channel_id=1, source_target_pairs={{12,0},{13,1},{14,2},{15,3},{8,4},{9,5},{10,6},{11,7},{4,8},{5,9},... | collective-permute-start | bytes 393224 | tf_op jit(solution)/shard_map/ppermute | solution.py:20
  6.6 7.2 %collective-permute-start.2 = (bf16[2,16,2048]{2,1,0:T(8,128)(2,1)}, bf16[2,16,2048]{2,1,0:T(8,128)(2,1)S(1)}, u32[]{:S(2)}, u32[]{:S(2)}) collective-permute-start(bf16[2,16,2048]{2,1,0:T(8,128)(2,1)} %refs_1_.1), channel_id=1, source_target_pairs={{4,0},{5,1},{6,2},{7,3},{0,4},{1,5},{2,6},{3,7},{12,8},{13,9},{14,... | collective-permute-start | bytes 393224 | tf_op jit(solution)/shard_map/ppermute | solution.py:20
  11.4 5.0 %collective-permute-start.3 = (bf16[2,16,2048]{2,1,0:T(8,128)(2,1)S(1)}, bf16[2,16,2048]{2,1,0:T(8,128)(2,1)S(1)}, u32[]{:S(2)}, u32[]{:S(2)}) collective-permute-start(bf16[2,16,2048]{2,1,0:T(8,128)(2,1)S(1)} %collective-permute-done.refs_3_), channel_id=1, source_target_pairs={{4,0},{5,1},{6,2},{7,3},{0,4},{1,5},{2,6},{3,7},{12,8},{13,9},{14,... | collective-permute-start | bytes 393224 | tf_op jit(solution)/shard_map/ppermute | solution.py:20
  12.5 3.8 %collective-permute-start.1 = (bf16[2,16,2048]{2,1,0:T(8,128)(2,1)S(1)}, bf16[2,16,2048]{2,1,0:T(8,128)(2,1)S(1)}, u32[]{:S(2)}, u32[]{:S(2)}) collective-permute-start(bf16[2,16,2048]{2,1,0:T(8,128)(2,1)S(1)} %copy-done), channel_id=1, source_target_pairs={{1,0},{0,1},{3,2},{2,3},{5,4},{4,5},{7,6},{6,7},{9,8},{8,9},{11,10... | collective-permute-start | bytes 393224 | tf_op jit(solution)/shard_map/ppermute | solution.py:20
  12.5 3.8 %collective-permute-start.5 = (bf16[2,16,2048]{2,1,0:T(8,128)(2,1)S(1)}, bf16[2,16,2048]{2,1,0:T(8,128)(2,1)S(1)}, u32[]{:S(2)}, u32[]{:S(2)}) collective-permute-start(bf16[2,16,2048]{2,1,0:T(8,128)(2,1)S(1)} %collective-permute-done.refs_3_), channel_id=1, source_target_pairs={{1,0},{0,1},{3,2},{2,3},{5,4},{4,5},{7,6},{6,7},{9,8},{8,9},{11,10... | collective-permute-start | bytes 393224 | tf_op jit(solution)/shard_map/ppermute | solution.py:20
  13.7 2.6 %collective-permute-start.4 = (bf16[2,16,2048]{2,1,0:T(8,128)(2,1)S(1)}, bf16[2,16,2048]{2,1,0:T(8,128)(2,1)S(1)}, u32[]{:S(2)}, u32[]{:S(2)}) collective-permute-start(bf16[2,16,2048]{2,1,0:T(8,128)(2,1)S(1)} %collective-permute-done.2.refs_2_), channel_id=1, source_target_pairs={{1,0},{0,1},{3,2},{2,3},{5,4},{4,5},{7,6},{6,7},{9,8},{8,9},{11,10... | collective-permute-start | bytes 393224 | tf_op jit(solution)/shard_map/ppermute | solution.py:20
  16.4 1.3 %collective-permute-start.6 = (bf16[2,16,2048]{2,1,0:T(8,128)(2,1)S(1)}, bf16[2,16,2048]{2,1,0:T(8,128)(2,1)S(1)}, u32[]{:S(2)}, u32[]{:S(2)}) collective-permute-start(bf16[2,16,2048]{2,1,0:T(8,128)(2,1)S(1)} %collective-permute-done.3.refs_4_), channel_id=1, source_target_pairs={{1,0},{0,1},{3,2},{2,3},{5,4},{4,5},{7,6},{6,7},{9,8},{8,9},{11,10... | collective-permute-start | bytes 393224 | tf_op jit(solution)/shard_map/ppermute | solution.py:20
  18.2 6.2 %collective-permute-start.10 = (bf16[2,4,2,16,256]{4,3,2,1,0:T(8,128)(2,1)S(1)}, bf16[2,4,2,16,256]{4,3,2,1,0:T(8,128)(2,1)S(1)}, u32[]{:S(2)}, u32[]{:S(2)}) collective-permute-start(bf16[2,4,2,16,256]{4,3,2,1,0:T(8,128)(2,1)S(1)} %condition.1.refs_0_), channel_id=1, source_target_pairs={{4,0},{5,1},{6,2},{7,3},{0,4},{1,5},{2,6},{3,7},{12,8},{13,9},{14,... | collective-permute-start | bytes 393224 | tf_op jit(solution)/shard_map/ppermute | solution.py:20
  19.4 9.6 %collective-permute-start.11 = (bf16[2,4,2,16,256]{4,3,2,1,0:T(8,128)(2,1)S(1)}, bf16[2,4,2,16,256]{4,3,2,1,0:T(8,128)(2,1)S(1)}, u32[]{:S(2)}, u32[]{:S(2)}) collective-permute-start(bf16[2,4,2,16,256]{4,3,2,1,0:T(8,128)(2,1)S(1)} %condition.1.refs_0_), channel_id=1, source_target_pairs={{12,0},{13,1},{14,2},{15,3},{8,4},{9,5},{10,6},{11,7},{4,8},{5,9},... | collective-permute-start | bytes 393224 | tf_op jit(solution)/shard_map/ppermute | solution.py:20
  21.9 7.1 %collective-permute-start.8 = (bf16[2,4,2,16,256]{4,3,2,1,0:T(8,128)(2,1)S(1)}, bf16[2,4,2,16,256]{4,3,2,1,0:T(8,128)(2,1)S(1)}, u32[]{:S(2)}, u32[]{:S(2)}) collective-permute-start(bf16[2,4,2,16,256]{4,3,2,1,0:T(8,128)(2,1)S(1)} %condition.1.refs_0_), channel_id=1, source_target_pairs={{2,0},{3,1},{0,2},{1,3},{6,4},{7,5},{4,6},{5,7},{10,8},{11,9},{8,1... | collective-permute-start | bytes 393224 | tf_op jit(solution)/shard_map/ppermute | solution.py:20
  22.4 8.5 %collective-permute-start.9 = (bf16[2,4,2,16,256]{4,3,2,1,0:T(8,128)(2,1)S(1)}, bf16[2,4,2,16,256]{4,3,2,1,0:T(8,128)(2,1)S(1)}, u32[]{:S(2)}, u32[]{:S(2)}) collective-permute-start(bf16[2,4,2,16,256]{4,3,2,1,0:T(8,128)(2,1)S(1)} %condition.1.refs_0_), channel_id=1, source_target_pairs={{6,0},{7,1},{4,2},{5,3},{2,4},{3,5},{0,6},{1,7},{14,8},{15,9},{12,... | collective-permute-start | bytes 393224 | tf_op jit(solution)/shard_map/ppermute | solution.py:20
  31.2 5.4 %collective-permute-start.15 = (bf16[512,512]{1,0:T(8,128)(2,1)S(1)}, bf16[512,512]{1,0:T(8,128)(2,1)S(1)}, u32[]{:S(2)}, u32[]{:S(2)}) collective-permute-start(bf16[512,512]{1,0:T(8,128)(2,1)S(1)} %turn.2.refs_1_), channel_id=1, source_target_pairs={{1,0},{0,1},{3,2},{2,3},{5,4},{4,5},{7,6},{6,7},{9,8},{8,9},{11,10... | collective-permute-start | bytes 1572872 | tf_op jit(solution)/shard_map/ppermute | solution.py:20
  31.2 7.3 %collective-permute-start.12 = (bf16[2,4,2,16,256]{4,3,2,1,0:T(8,128)(2,1)S(1)}, bf16[2,4,2,16,256]{4,3,2,1,0:T(8,128)(2,1)S(1)}, u32[]{:S(2)}, u32[]{:S(2)}) collective-permute-start(bf16[2,4,2,16,256]{4,3,2,1,0:T(8,128)(2,1)S(1)} %collective-permute-done.11.refs_0_), channel_id=1, source_target_pairs={{6,0},{7,1},{4,2},{5,3},{2,4},{3,5},{0,6},{1,7},{14,8},{15,9},{12,... | collective-permute-start | bytes 393224 | tf_op jit(solution)/shard_map/ppermute | solution.py:20
  31.9 9.1 %collective-permute-start.13 = (bf16[2,4,2,16,256]{4,3,2,1,0:T(8,128)(2,1)S(1)}, bf16[2,4,2,16,256]{4,3,2,1,0:T(8,128)(2,1)S(1)}, u32[]{:S(2)}, u32[]{:S(2)}) collective-permute-start(bf16[2,4,2,16,256]{4,3,2,1,0:T(8,128)(2,1)S(1)} %collective-permute-done.11.refs_0_), channel_id=1, source_target_pairs={{4,0},{5,1},{6,2},{7,3},{0,4},{1,5},{2,6},{3,7},{12,8},{13,9},{14,... | collective-permute-start | bytes 393224 | tf_op jit(solution)/shard_map/ppermute | solution.py:20
  34.3 6.7 %collective-permute-start.14 = (bf16[2,4,2,16,256]{4,3,2,1,0:T(8,128)(2,1)S(1)}, bf16[2,4,2,16,256]{4,3,2,1,0:T(8,128)(2,1)S(1)}, u32[]{:S(2)}, u32[]{:S(2)}) collective-permute-start(bf16[2,4,2,16,256]{4,3,2,1,0:T(8,128)(2,1)S(1)} %collective-permute-done.11.refs_0_), channel_id=1, source_target_pairs={{2,0},{3,1},{0,2},{1,3},{6,4},{7,5},{4,6},{5,7},{10,8},{11,9},{8,1... | collective-permute-start | bytes 393224 | tf_op jit(solution)/shard_map/ppermute | solution.py:20
  41.2 2.0 %collective-permute-start.16 = (bf16[512,512]{1,0:T(8,128)(2,1)S(1)}, bf16[512,512]{1,0:T(8,128)(2,1)S(1)}, u32[]{:S(2)}, u32[]{:S(2)}) collective-permute-start(bf16[512,512]{1,0:T(8,128)(2,1)S(1)} %turn.3.refs_1_), channel_id=1, source_target_pairs={{1,0},{0,1},{3,2},{2,3},{5,4},{4,5},{7,6},{6,7},{9,8},{8,9},{11,10... | collective-permute-start | bytes 1572872 | tf_op jit(solution)/shard_map/ppermute | solution.py:20

commit v7 on v6

--- a/solution.py
+++ b/solution.py
@@ -159,10 +159,9 @@
         copy(step).wait()
 
 
-def score(grid, train_feats, turned, total, masks, other, last):
+def score(grid, train_feats, turned, total, masks, other, last, tile):
     rows = train_feats.shape[0]
     features, queries = turned.shape
-    tile = 512
     first = total is None
     arrays = [train_feats, turned] + ([] if first else [total])
     shape = (rows, queries)
@@ -174,7 +173,7 @@
         out_specs=ANY if last else VMEM,
         scratch_shapes=scratch,
         input_output_aliases={} if first or last else {2: 0},
-        compiler_params=pltpu.CompilerParams(vmem_limit_bytes=16 << 20),
+        compiler_params=pltpu.CompilerParams(vmem_limit_bytes=20 << 20),
         cost_estimate=pl.CostEstimate(
             flops=2 * rows * features * queries, bytes_accessed=4 << 20, transcendentals=0
         ),
@@ -190,7 +189,9 @@
     near_fisher = grid.swap(inverse_fisher, 0, 1, 0)
     gathered[mirror, 0] = grid.swap(queries, mirror, 0, 0)
     staged = stage(train_feats, queries, inverse_fisher)
-    gathered[mirror, 0], staged = lax.optimization_barrier((gathered[mirror, 0], staged))
+    gathered[mirror, 0], gathered[0, 1], staged = lax.optimization_barrier(
+        (gathered[mirror, 0], gathered[0, 1], staged)
+    )
     train_here, gathered[0, 0], fisher_here = staged
     gathered[relayed, 0] = grid.swap(gathered[mirror, 0], beside, 0, 0)
     for mask in (beside, mirror, relayed):
@@ -217,8 +218,8 @@
     for masks in ((0, beside), (mirror, relayed)):
         turned = turn(grid, parts, masks)
         other = grid.swap(turned, 0, 0, 1)
-        total = score(grid, train_here, turned, total, masks, 0, False)
-        total = score(grid, train_here, other, total, masks, 1, masks == (mirror, relayed))
+        total = score(grid, train_here, turned, total, masks, 0, False, 1024 if total is None else 256)
+        total = score(grid, train_here, other, total, masks, 1, masks == (mirror, relayed), 2048 if masks == (0, beside) else 256)
         if masks == (0, beside):
             late = (mirror, 0), (relayed, 1), (relayed, 0), (mirror, 1)
             held, total = lax.optimization_barrier(([parts[place] for place in late], total))

time: 46.1 us -> 47.3 us (1.026)
  waiting for transfers between devices: 15 us -> 16.2 us
    ppermute x17, waiting for transfers between devices: 15 us -> 16.2 us  [swap(): lax.ppermute(block, 'rows', [(row ^ step, row) for row in range(self.far...]
  transfers between devices with their start and end apart: 17 -> 17, of which waited for: 7 -> 8; matrix products, arithmetic and copies ran while one was open for 0% -> 0% of each run, Pallas kernels for 20% -> 19%
where the time goes in v7:
time: 47.3 us; the launch traced here: 47.2 us
  starting transfers between devices  17.8 us (38%)
  waiting for transfers between devices  16.2 us (34%)
  Pallas kernels  13.1 us (28%)
    ppermute x17, starting transfers between devices, swap(): lax.ppermute(block, 'rows', [(row ^ step, row) for row in range(self.far...  17.8 us
    ppermute x17, waiting for transfers between devices, swap(): lax.ppermute(block, 'rows', [(row ^ step, row) for row in range(self.far...  16.2 us
    pallas_call x4, Pallas kernels, score(): pl.pallas_call(functools.partial(score_kernel, grid, tile, masks, other,...  8.72 us
    pallas_call x1, Pallas kernels, stage(): pl.pallas_call(functools.partial(stage_kernel, len(arrays)), out_shape=[p...  3.49 us
  transfers between devices with their start and end apart: 17, of which 8 were waited for; matrix products, arithmetic and copies ran while one was open for 0% of the time, Pallas kernels for 19%

profile of v7, /device:TPU:0, one launch (start us, length us, event | category | flops | bytes accessed | tf_op | source)
XLA Modules:
  0.0 47.2 jit_solution(4919275934211337726)
XLA Ops:
  0.0 3.0 %collective-permute-start.7 = (bf16[1,2048,128]{2,1,0:T(8,128)(2,1)}, bf16[1,2048,128]{2,1,0:T(8,128)(2,1)S(1)}, u32[]{:S(2)}, u32[]{:S(2)}) collective-permute-start(bf16[1,2048,128]{2,1,0:T(8,128)(2,1)} %refs_2_.1), channel_id=1, source_target_pairs={{2,0},{3,1},{0,2},{1,3},{6,4},{7,5},{4,6},{5,7},{10,8},{11,9},{8,1... | collective-permute-start | bytes 1572872 | tf_op jit(solution)/shard_map/ppermute | solution.py:20
  3.0 3.6 %collective-permute-start = (bf16[2,16,2048]{2,1,0:T(8,128)(2,1)}, bf16[2,16,2048]{2,1,0:T(8,128)(2,1)S(1)}, u32[]{:S(2)}, u32[]{:S(2)}) collective-permute-start(bf16[2,16,2048]{2,1,0:T(8,128)(2,1)} %refs_1_.1), channel_id=1, source_target_pairs={{12,0},{13,1},{14,2},{15,3},{8,4},{9,5},{10,6},{11,7},{4,8},{5,9},... | collective-permute-start | bytes 393224 | tf_op jit(solution)/shard_map/ppermute | solution.py:20
  6.6 0.0 collective-permute-start.1
  6.6 0.0 collective-permute-start.2
  6.6 3.5 %stage.1 = (bf16[2048,2048]{1,0:T(8,128)(2,1)S(1)}, bf16[2,16,2048]{2,1,0:T(8,128)(2,1)S(1)}, bf16[1,2048,128]{2,1,0:T(8,128)(2,1)S(1)}) custom-call(bf16[2048,2048]{1,0:T(8,128)(2,1)} %refs_0_.1, bf16[2,16,2048]{2,1,0:T(8,128)(2,1)} %refs_1_.1, bf16[1,2048,128]{2,1,0:T(8,128)(2,1)} %refs_2_.1), custom_call_target="tpu_custom_call" | custom-call | bytes 18087936 | tf_op jit(solution)/shard_map/stage/pallas_call | solution.py:48
  10.1 1.3 %collective-permute-done.refs_3_ = bf16[2,16,2048]{2,1,0:T(8,128)(2,1)S(1)} collective-permute-done((bf16[2,16,2048]{2,1,0:T(8,128)(2,1)}, bf16[2,16,2048]{2,1,0:T(8,128)(2,1)S(1)}, u32[]{:S(2)}, u32[]{:S(2)}) %collective-permute-start) | collective-permute-done | bytes 131104 | tf_op jit(solution)/shard_map/ppermute | solution.py:20
  11.3 1.2 %collective-permute-start.3 = (bf16[2,16,2048]{2,1,0:T(8,128)(2,1)S(1)}, bf16[2,16,2048]{2,1,0:T(8,128)(2,1)S(1)}, u32[]{:S(2)}, u32[]{:S(2)}) collective-permute-start(bf16[2,16,2048]{2,1,0:T(8,128)(2,1)S(1)} %collective-permute-done.refs_3_), channel_id=1, source_target_pairs={{4,0},{5,1},{6,2},{7,3},{0,4},{1,5},{2,6},{3,7},{12,8},{13,9},{14,... | collective-permute-start | bytes 393224 | tf_op jit(solution)/shard_map/ppermute | solution.py:20
  12.5 1.0 %collective-permute-done.2.refs_2_ = bf16[2,16,2048]{2,1,0:T(8,128)(2,1)S(1)} collective-permute-done((bf16[2,16,2048]{2,1,0:T(8,128)(2,1)}, bf16[2,16,2048]{2,1,0:T(8,128)(2,1)S(1)}, u32[]{:S(2)}, u32[]{:S(2)}) %collective-permute-start.2) | collective-permute-done | bytes 131104 | tf_op jit(solution)/shard_map/ppermute | solution.py:20
  13.5 0.0 collective-permute-start.4
  13.5 2.8 %collective-permute-done.3.refs_4_ = bf16[2,16,2048]{2,1,0:T(8,128)(2,1)S(1)} collective-permute-done((bf16[2,16,2048]{2,1,0:T(8,128)(2,1)S(1)}, bf16[2,16,2048]{2,1,0:T(8,128)(2,1)S(1)}, u32[]{:S(2)}, u32[]{:S(2)}) %collective-permute-start.3) | collective-permute-done | bytes 131104 | tf_op jit(solution)/shard_map/ppermute | solution.py:20
  16.3 0.0 collective-permute-start.6
  16.3 1.3 %collective-permute-done.6.refs_7_ = bf16[2,16,2048]{2,1,0:T(8,128)(2,1)S(1)} collective-permute-done((bf16[2,16,2048]{2,1,0:T(8,128)(2,1)S(1)}, bf16[2,16,2048]{2,1,0:T(8,128)(2,1)S(1)}, u32[]{:S(2)}, u32[]{:S(2)}) %collective-permute-start.6) | collective-permute-done | bytes 131104 | tf_op jit(solution)/shard_map/ppermute | solution.py:20
  17.7 0.4 condition.1.refs_0_
  18.1 1.6 %collective-permute-start.10 = (bf16[2,4,2,16,256]{4,3,2,1,0:T(8,128)(2,1)S(1)}, bf16[2,4,2,16,256]{4,3,2,1,0:T(8,128)(2,1)S(1)}, u32[]{:S(2)}, u32[]{:S(2)}) collective-permute-start(bf16[2,4,2,16,256]{4,3,2,1,0:T(8,128)(2,1)S(1)} %condition.1.refs_0_), channel_id=1, source_target_pairs={{4,0},{5,1},{6,2},{7,3},{0,4},{1,5},{2,6},{3,7},{12,8},{13,9},{14,... | collective-permute-start | bytes 393224 | tf_op jit(solution)/shard_map/ppermute | solution.py:20
  19.7 2.2 %collective-permute-start.11 = (bf16[2,4,2,16,256]{4,3,2,1,0:T(8,128)(2,1)S(1)}, bf16[2,4,2,16,256]{4,3,2,1,0:T(8,128)(2,1)S(1)}, u32[]{:S(2)}, u32[]{:S(2)}) collective-permute-start(bf16[2,4,2,16,256]{4,3,2,1,0:T(8,128)(2,1)S(1)} %condition.1.refs_0_), channel_id=1, source_target_pairs={{12,0},{13,1},{14,2},{15,3},{8,4},{9,5},{10,6},{11,7},{4,8},{5,9},... | collective-permute-start | bytes 393224 | tf_op jit(solution)/shard_map/ppermute | solution.py:20
  21.9 0.5 %collective-permute-start.8 = (bf16[2,4,2,16,256]{4,3,2,1,0:T(8,128)(2,1)S(1)}, bf16[2,4,2,16,256]{4,3,2,1,0:T(8,128)(2,1)S(1)}, u32[]{:S(2)}, u32[]{:S(2)}) collective-permute-start(bf16[2,4,2,16,256]{4,3,2,1,0:T(8,128)(2,1)S(1)} %condition.1.refs_0_), channel_id=1, source_target_pairs={{2,0},{3,1},{0,2},{1,3},{6,4},{7,5},{4,6},{5,7},{10,8},{11,9},{8,1... | collective-permute-start | bytes 393224 | tf_op jit(solution)/shard_map/ppermute | solution.py:20
  22.4 2.0 %collective-permute-start.9 = (bf16[2,4,2,16,256]{4,3,2,1,0:T(8,128)(2,1)S(1)}, bf16[2,4,2,16,256]{4,3,2,1,0:T(8,128)(2,1)S(1)}, u32[]{:S(2)}, u32[]{:S(2)}) collective-permute-start(bf16[2,4,2,16,256]{4,3,2,1,0:T(8,128)(2,1)S(1)} %condition.1.refs_0_), channel_id=1, source_target_pairs={{6,0},{7,1},{4,2},{5,3},{2,4},{3,5},{0,6},{1,7},{14,8},{15,9},{12,... | collective-permute-start | bytes 393224 | tf_op jit(solution)/shard_map/ppermute | solution.py:20
  24.4 4.5 %collective-permute-done.11.refs_0_ = bf16[2,4,2,16,256]{4,3,2,1,0:T(8,128)(2,1)S(1)} collective-permute-done((bf16[2,4,2,16,256]{4,3,2,1,0:T(8,128)(2,1)S(1)}, bf16[2,4,2,16,256]{4,3,2,1,0:T(8,128)(2,1)S(1)}, u32[]{:S(2)}, u32[]{:S(2)}) %collective-permute-start.11) | collective-permute-done | bytes 131104 | tf_op jit(solution)/shard_map/ppermute | solution.py:20
  29.0 2.0 %collective-permute-done.9.refs_3_ = bf16[2,4,2,16,256]{4,3,2,1,0:T(8,128)(2,1)S(1)} collective-permute-done((bf16[2,4,2,16,256]{4,3,2,1,0:T(8,128)(2,1)S(1)}, bf16[2,4,2,16,256]{4,3,2,1,0:T(8,128)(2,1)S(1)}, u32[]{:S(2)}, u32[]{:S(2)}) %collective-permute-start.9) | collective-permute-done | bytes 131104 | tf_op jit(solution)/shard_map/ppermute | solution.py:20
  30.9 0.2 turn.2.refs_1_
  31.2 0.1 collective-permute-start.15
  31.2 0.9 %collective-permute-start.12 = (bf16[2,4,2,16,256]{4,3,2,1,0:T(8,128)(2,1)S(1)}, bf16[2,4,2,16,256]{4,3,2,1,0:T(8,128)(2,1)S(1)}, u32[]{:S(2)}, u32[]{:S(2)}) collective-permute-start(bf16[2,4,2,16,256]{4,3,2,1,0:T(8,128)(2,1)S(1)} %collective-permute-done.11.refs_0_), channel_id=1, source_target_pairs={{6,0},{7,1},{4,2},{5,3},{2,4},{3,5},{0,6},{1,7},{14,8},{15,9},{12,... | collective-permute-start | bytes 393224 | tf_op jit(solution)/shard_map/ppermute | solution.py:20
  32.2 2.1 %collective-permute-start.13 = (bf16[2,4,2,16,256]{4,3,2,1,0:T(8,128)(2,1)S(1)}, bf16[2,4,2,16,256]{4,3,2,1,0:T(8,128)(2,1)S(1)}, u32[]{:S(2)}, u32[]{:S(2)}) collective-permute-start(bf16[2,4,2,16,256]{4,3,2,1,0:T(8,128)(2,1)S(1)} %collective-permute-done.11.refs_0_), channel_id=1, source_target_pairs={{4,0},{5,1},{6,2},{7,3},{0,4},{1,5},{2,6},{3,7},{12,8},{13,9},{14,... | collective-permute-start | bytes 393224 | tf_op jit(solution)/shard_map/ppermute | solution.py:20
  34.3 0.5 %collective-permute-start.14 = (bf16[2,4,2,16,256]{4,3,2,1,0:T(8,128)(2,1)S(1)}, bf16[2,4,2,16,256]{4,3,2,1,0:T(8,128)(2,1)S(1)}, u32[]{:S(2)}, u32[]{:S(2)}) collective-permute-start(bf16[2,4,2,16,256]{4,3,2,1,0:T(8,128)(2,1)S(1)} %collective-permute-done.11.refs_0_), channel_id=1, source_target_pairs={{2,0},{3,1},{0,2},{1,3},{6,4},{7,5},{4,6},{5,7},{10,8},{11,9},{8,1... | collective-permute-start | bytes 393224 | tf_op jit(solution)/shard_map/ppermute | solution.py:20
  34.8 1.4 %score.4.refs_2_ = f32[2048,512]{1,0:T(8,128)S(1)} custom-call(bf16[2048,2048]{1,0:T(8,128)(2,1)S(1)} %get-tuple-element.25.refs_0_, bf16[512,512]{1,0:T(8,128)(2,1)S(1)} %turn.2.refs_1_), custom_call_target="tpu_custom_call" | custom-call | flops 1073741824 | bytes 4194304 | tf_op jit(solution)/shard_map/score/pallas_call | solution.py:169
  36.2 1.4 %score.5.refs_2_ = f32[2048,512]{1,0:T(8,128)S(1)} custom-call(bf16[2048,2048]{1,0:T(8,128)(2,1)S(1)} %get-tuple-element.25.refs_0_, bf16[512,512]{1,0:T(8,128)(2,1)S(1)} %collective-permute-done.15.refs_1_, f32[2048,512]{1,0:T(8,128)S(1)} %score.4.refs_2_), custom_call_target="tpu_custom_call", output_to_operand_aliasing={{}: (2, {})} | custom-call | flops 1073741824 | bytes 4194304 | tf_op jit(solution)/shard_map/score/pallas_call | solution.py:169
  37.6 0.9 %collective-permute-done.12.refs_3_ = bf16[2,4,2,16,256]{4,3,2,1,0:T(8,128)(2,1)S(1)} collective-permute-done((bf16[2,4,2,16,256]{4,3,2,1,0:T(8,128)(2,1)S(1)}, bf16[2,4,2,16,256]{4,3,2,1,0:T(8,128)(2,1)S(1)}, u32[]{:S(2)}, u32[]{:S(2)}) %collective-permute-start.12) | collective-permute-done | bytes 131104 | tf_op jit(solution)/shard_map/ppermute | solution.py:20
  38.5 2.5 %collective-permute-done.13.refs_2_ = bf16[2,4,2,16,256]{4,3,2,1,0:T(8,128)(2,1)S(1)} collective-permute-done((bf16[2,4,2,16,256]{4,3,2,1,0:T(8,128)(2,1)S(1)}, bf16[2,4,2,16,256]{4,3,2,1,0:T(8,128)(2,1)S(1)}, u32[]{:S(2)}, u32[]{:S(2)}) %collective-permute-start.13) | collective-permute-done | bytes 131104 | tf_op jit(solution)/shard_map/ppermute | solution.py:20
  41.0 0.2 turn.3.refs_1_
  41.2 0.1 collective-permute-start.16
  41.3 2.5 %score.6.refs_2_ = f32[2048,512]{1,0:T(8,128)S(1)} custom-call(bf16[2048,2048]{1,0:T(8,128)(2,1)S(1)} %get-tuple-element.25.refs_0_, bf16[512,512]{1,0:T(8,128)(2,1)S(1)} %turn.3.refs_1_, f32[2048,512]{1,0:T(8,128)S(1)} %score.5.refs_2_), custom_call_target="tpu_custom_call", output_to_operand_aliasing={{}: (2, {})} | custom-call | flops 1073741824 | bytes 4194304 | tf_op jit(solution)/shard_map/score/pallas_call | solution.py:169
  43.8 3.4 %score.7 = f32[2048,512]{1,0:T(8,128)} custom-call(bf16[2048,2048]{1,0:T(8,128)(2,1)S(1)} %get-tuple-element.25.refs_0_, bf16[512,512]{1,0:T(8,128)(2,1)S(1)} %collective-permute-done.16.refs_1_, f32[2048,512]{1,0:T(8,128)S(1)} %score.6.refs_2_), custom_call_target="tpu_custom_call" | custom-call | flops 1073741824 | bytes 4194304 | tf_op jit(solution)/shard_map/score/pallas_call | solution.py:169
  (10 shorter events, 0.0 us)
Async XLA Ops:
  0.0 17.6 %collective-permute-start.7 = (bf16[1,2048,128]{2,1,0:T(8,128)(2,1)}, bf16[1,2048,128]{2,1,0:T(8,128)(2,1)S(1)}, u32[]{:S(2)}, u32[]{:S(2)}) collective-permute-start(bf16[1,2048,128]{2,1,0:T(8,128)(2,1)} %refs_2_.1), channel_id=1, source_target_pairs={{2,0},{3,1},{0,2},{1,3},{6,4},{7,5},{4,6},{5,7},{10,8},{11,9},{8,1... | collective-permute-start | bytes 1572872 | tf_op jit(solution)/shard_map/ppermute | solution.py:20
  3.0 8.4 %collective-permute-start = (bf16[2,16,2048]{2,1,0:T(8,128)(2,1)}, bf16[2,16,2048]{2,1,0:T(8,128)(2,1)S(1)}, u32[]{:S(2)}, u32[]{:S(2)}) collective-permute-start(bf16[2,16,2048]{2,1,0:T(8,128)(2,1)} %refs_1_.1), channel_id=1, source_target_pairs={{12,0},{13,1},{14,2},{15,3},{8,4},{9,5},{10,6},{11,7},{4,8},{5,9},... | collective-permute-start | bytes 393224 | tf_op jit(solution)/shard_map/ppermute | solution.py:20
  6.6 4.8 %collective-permute-start.1 = (bf16[2,16,2048]{2,1,0:T(8,128)(2,1)}, bf16[2,16,2048]{2,1,0:T(8,128)(2,1)S(1)}, u32[]{:S(2)}, u32[]{:S(2)}) collective-permute-start(bf16[2,16,2048]{2,1,0:T(8,128)(2,1)} %refs_1_.1), channel_id=1, source_target_pairs={{1,0},{0,1},{3,2},{2,3},{5,4},{4,5},{7,6},{6,7},{9,8},{8,9},{11,10... | collective-permute-start | bytes 393224 | tf_op jit(solution)/shard_map/ppermute | solution.py:20
  6.6 6.9 %collective-permute-start.2 = (bf16[2,16,2048]{2,1,0:T(8,128)(2,1)}, bf16[2,16,2048]{2,1,0:T(8,128)(2,1)S(1)}, u32[]{:S(2)}, u32[]{:S(2)}) collective-permute-start(bf16[2,16,2048]{2,1,0:T(8,128)(2,1)} %refs_1_.1), channel_id=1, source_target_pairs={{4,0},{5,1},{6,2},{7,3},{0,4},{1,5},{2,6},{3,7},{12,8},{13,9},{14,... | collective-permute-start | bytes 393224 | tf_op jit(solution)/shard_map/ppermute | solution.py:20
  11.3 5.0 %collective-permute-start.3 = (bf16[2,16,2048]{2,1,0:T(8,128)(2,1)S(1)}, bf16[2,16,2048]{2,1,0:T(8,128)(2,1)S(1)}, u32[]{:S(2)}, u32[]{:S(2)}) collective-permute-start(bf16[2,16,2048]{2,1,0:T(8,128)(2,1)S(1)} %collective-permute-done.refs_3_), channel_id=1, source_target_pairs={{4,0},{5,1},{6,2},{7,3},{0,4},{1,5},{2,6},{3,7},{12,8},{13,9},{14,... | collective-permute-start | bytes 393224 | tf_op jit(solution)/shard_map/ppermute | solution.py:20
  12.5 3.8 %collective-permute-start.5 = (bf16[2,16,2048]{2,1,0:T(8,128)(2,1)S(1)}, bf16[2,16,2048]{2,1,0:T(8,128)(2,1)S(1)}, u32[]{:S(2)}, u32[]{:S(2)}) collective-permute-start(bf16[2,16,2048]{2,1,0:T(8,128)(2,1)S(1)} %collective-permute-done.refs_3_), channel_id=1, source_target_pairs={{1,0},{0,1},{3,2},{2,3},{5,4},{4,5},{7,6},{6,7},{9,8},{8,9},{11,10... | collective-permute-start | bytes 393224 | tf_op jit(solution)/shard_map/ppermute | solution.py:20
  13.5 2.8 %collective-permute-start.4 = (bf16[2,16,2048]{2,1,0:T(8,128)(2,1)S(1)}, bf16[2,16,2048]{2,1,0:T(8,128)(2,1)S(1)}, u32[]{:S(2)}, u32[]{:S(2)}) collective-permute-start(bf16[2,16,2048]{2,1,0:T(8,128)(2,1)S(1)} %collective-permute-done.2.refs_2_), channel_id=1, source_target_pairs={{1,0},{0,1},{3,2},{2,3},{5,4},{4,5},{7,6},{6,7},{9,8},{8,9},{11,10... | collective-permute-start | bytes 393224 | tf_op jit(solution)/shard_map/ppermute | solution.py:20
  16.3 1.3 %collective-permute-start.6 = (bf16[2,16,2048]{2,1,0:T(8,128)(2,1)S(1)}, bf16[2,16,2048]{2,1,0:T(8,128)(2,1)S(1)}, u32[]{:S(2)}, u32[]{:S(2)}) collective-permute-start(bf16[2,16,2048]{2,1,0:T(8,128)(2,1)S(1)} %collective-permute-done.3.refs_4_), channel_id=1, source_target_pairs={{1,0},{0,1},{3,2},{2,3},{5,4},{4,5},{7,6},{6,7},{9,8},{8,9},{11,10... | collective-permute-start | bytes 393224 | tf_op jit(solution)/shard_map/ppermute | solution.py:20
  18.1 6.3 %collective-permute-start.10 = (bf16[2,4,2,16,256]{4,3,2,1,0:T(8,128)(2,1)S(1)}, bf16[2,4,2,16,256]{4,3,2,1,0:T(8,128)(2,1)S(1)}, u32[]{:S(2)}, u32[]{:S(2)}) collective-permute-start(bf16[2,4,2,16,256]{4,3,2,1,0:T(8,128)(2,1)S(1)} %condition.1.refs_0_), channel_id=1, source_target_pairs={{4,0},{5,1},{6,2},{7,3},{0,4},{1,5},{2,6},{3,7},{12,8},{13,9},{14,... | collective-permute-start | bytes 393224 | tf_op jit(solution)/shard_map/ppermute | solution.py:20
  19.7 9.3 %collective-permute-start.11 = (bf16[2,4,2,16,256]{4,3,2,1,0:T(8,128)(2,1)S(1)}, bf16[2,4,2,16,256]{4,3,2,1,0:T(8,128)(2,1)S(1)}, u32[]{:S(2)}, u32[]{:S(2)}) collective-permute-start(bf16[2,4,2,16,256]{4,3,2,1,0:T(8,128)(2,1)S(1)} %condition.1.refs_0_), channel_id=1, source_target_pairs={{12,0},{13,1},{14,2},{15,3},{8,4},{9,5},{10,6},{11,7},{4,8},{5,9},... | collective-permute-start | bytes 393224 | tf_op jit(solution)/shard_map/ppermute | solution.py:20
  21.9 7.1 %collective-permute-start.8 = (bf16[2,4,2,16,256]{4,3,2,1,0:T(8,128)(2,1)S(1)}, bf16[2,4,2,16,256]{4,3,2,1,0:T(8,128)(2,1)S(1)}, u32[]{:S(2)}, u32[]{:S(2)}) collective-permute-start(bf16[2,4,2,16,256]{4,3,2,1,0:T(8,128)(2,1)S(1)} %condition.1.refs_0_), channel_id=1, source_target_pairs={{2,0},{3,1},{0,2},{1,3},{6,4},{7,5},{4,6},{5,7},{10,8},{11,9},{8,1... | collective-permute-start | bytes 393224 | tf_op jit(solution)/shard_map/ppermute | solution.py:20
  22.4 8.5 %collective-permute-start.9 = (bf16[2,4,2,16,256]{4,3,2,1,0:T(8,128)(2,1)S(1)}, bf16[2,4,2,16,256]{4,3,2,1,0:T(8,128)(2,1)S(1)}, u32[]{:S(2)}, u32[]{:S(2)}) collective-permute-start(bf16[2,4,2,16,256]{4,3,2,1,0:T(8,128)(2,1)S(1)} %condition.1.refs_0_), channel_id=1, source_target_pairs={{6,0},{7,1},{4,2},{5,3},{2,4},{3,5},{0,6},{1,7},{14,8},{15,9},{12,... | collective-permute-start | bytes 393224 | tf_op jit(solution)/shard_map/ppermute | solution.py:20
  31.2 5.1 %collective-permute-start.15 = (bf16[512,512]{1,0:T(8,128)(2,1)S(1)}, bf16[512,512]{1,0:T(8,128)(2,1)S(1)}, u32[]{:S(2)}, u32[]{:S(2)}) collective-permute-start(bf16[512,512]{1,0:T(8,128)(2,1)S(1)} %turn.2.refs_1_), channel_id=1, source_target_pairs={{1,0},{0,1},{3,2},{2,3},{5,4},{4,5},{7,6},{6,7},{9,8},{8,9},{11,10... | collective-permute-start | bytes 1572872 | tf_op jit(solution)/shard_map/ppermute | solution.py:20
  31.2 7.3 %collective-permute-start.12 = (bf16[2,4,2,16,256]{4,3,2,1,0:T(8,128)(2,1)S(1)}, bf16[2,4,2,16,256]{4,3,2,1,0:T(8,128)(2,1)S(1)}, u32[]{:S(2)}, u32[]{:S(2)}) collective-permute-start(bf16[2,4,2,16,256]{4,3,2,1,0:T(8,128)(2,1)S(1)} %collective-permute-done.11.refs_0_), channel_id=1, source_target_pairs={{6,0},{7,1},{4,2},{5,3},{2,4},{3,5},{0,6},{1,7},{14,8},{15,9},{12,... | collective-permute-start | bytes 393224 | tf_op jit(solution)/shard_map/ppermute | solution.py:20
  32.2 8.8 %collective-permute-start.13 = (bf16[2,4,2,16,256]{4,3,2,1,0:T(8,128)(2,1)S(1)}, bf16[2,4,2,16,256]{4,3,2,1,0:T(8,128)(2,1)S(1)}, u32[]{:S(2)}, u32[]{:S(2)}) collective-permute-start(bf16[2,4,2,16,256]{4,3,2,1,0:T(8,128)(2,1)S(1)} %collective-permute-done.11.refs_0_), channel_id=1, source_target_pairs={{4,0},{5,1},{6,2},{7,3},{0,4},{1,5},{2,6},{3,7},{12,8},{13,9},{14,... | collective-permute-start | bytes 393224 | tf_op jit(solution)/shard_map/ppermute | solution.py:20
  34.3 6.7 %collective-permute-start.14 = (bf16[2,4,2,16,256]{4,3,2,1,0:T(8,128)(2,1)S(1)}, bf16[2,4,2,16,256]{4,3,2,1,0:T(8,128)(2,1)S(1)}, u32[]{:S(2)}, u32[]{:S(2)}) collective-permute-start(bf16[2,4,2,16,256]{4,3,2,1,0:T(8,128)(2,1)S(1)} %collective-permute-done.11.refs_0_), channel_id=1, source_target_pairs={{2,0},{3,1},{0,2},{1,3},{6,4},{7,5},{4,6},{5,7},{10,8},{11,9},{8,1... | collective-permute-start | bytes 393224 | tf_op jit(solution)/shard_map/ppermute | solution.py:20
  41.2 2.6 %collective-permute-start.16 = (bf16[512,512]{1,0:T(8,128)(2,1)S(1)}, bf16[512,512]{1,0:T(8,128)(2,1)S(1)}, u32[]{:S(2)}, u32[]{:S(2)}) collective-permute-start(bf16[512,512]{1,0:T(8,128)(2,1)S(1)} %turn.3.refs_1_), channel_id=1, source_target_pairs={{1,0},{0,1},{3,2},{2,3},{5,4},{4,5},{7,6},{6,7},{9,8},{8,9},{11,10... | collective-permute-start | bytes 1572872 | tf_op jit(solution)/shard_map/ppermute | solution.py:20

commit v8 on v6

--- a/solution.py
+++ b/solution.py
@@ -115,7 +115,7 @@
     )(*(pltpu.with_memory_space_constraint(a, pltpu.VMEM) for a in arrays))
 
 
-def score_kernel(grid, tile, masks, other, first, last, *refs):
+def score_kernel(grid, masks, other, first, last, *refs):
     train_ref, turned_ref, refs = refs[0], refs[1], refs[2:]
     total_ref, refs = (None, refs) if first else (refs[0], refs[1:])
     out_ref, refs = refs[0], refs[1:]
@@ -125,58 +125,46 @@
     pieces = [
         columns((flip(far, mask) * 2 + side) * 2 + flip(core, other), width) for mask in masks for side in range(2)
     ]
+
+    def products(rows, queries):
+        train = jnp.concatenate([train_ref[rows, piece] for piece in pieces], axis=1)
+        value = jnp.dot(train, turned_ref[:, queries], preferred_element_type=jnp.float32)
+        return value if first else total_ref[rows, queries] + value
+
+    if not last:
+        out_ref[...] = products(slice(None), slice(None))
+        return
+
+    here_ref, sem = refs
     scale = 1.0 / features**0.5
-    steps = train_ref.shape[0] // tile
-
-    def rows(step):
-        return pl.ds(pl.multiple_of(step * tile, tile), tile)
-
-    def products(step):
-        train = jnp.concatenate([train_ref[rows(step), piece] for piece in pieces], axis=1)
-        value = jnp.dot(train, turned_ref[...], preferred_element_type=jnp.float32)
-        return value if first else total_ref[rows(step)] + value
-
-    if not last:
-
-        @pl.loop(0, steps)
-        def _(step):
-            out_ref[rows(step)] = products(step)
-
-        return
-
-    here_ref, sem = refs
-
-    def copy(step):
-        return pltpu.make_async_copy(here_ref.at[rows(step)], out_ref.at[rows(step)], sem.at[step])
-
-    @pl.loop(0, steps)
-    def _(step):
-        here_ref[rows(step)] = products(step) * scale
-        copy(step).start()
-
-    @pl.loop(0, steps)
-    def _(step):
-        copy(step).wait()
+    row_step, query_step = here_ref.shape[0] // 2, here_ref.shape[1] // 2
+    copies = []
+    for step in range(4):
+        rows = pl.ds(step // 2 * row_step, row_step)
+        queries = pl.ds(step % 2 * query_step, query_step)
+        here_ref[rows, queries] = products(rows, queries) * scale
+        copies.append(pltpu.make_async_copy(here_ref.at[rows, queries], out_ref.at[rows, queries], sem.at[step]))
+        copies[-1].start()
+    for copy in copies:
+        copy.wait()
 
 
 def score(grid, train_feats, turned, total, masks, other, last):
     rows = train_feats.shape[0]
     features, queries = turned.shape
-    tile = 512
     first = total is None
     arrays = [train_feats, turned] + ([] if first else [total])
     shape = (rows, queries)
-    scratch = [pltpu.VMEM(shape, jnp.float32), pltpu.SemaphoreType.DMA((rows // tile,))] if last else []
-    return pl.pallas_call(
-        functools.partial(score_kernel, grid, tile, masks, other, first, last),
+    return pl.pallas_call(
+        functools.partial(score_kernel, grid, masks, other, first, last),
         out_shape=jax.ShapeDtypeStruct(shape, jnp.float32) if last else pltpu.VMEM(shape, jnp.float32),
         in_specs=[VMEM] * len(arrays),
         out_specs=ANY if last else VMEM,
-        scratch_shapes=scratch,
+        scratch_shapes=[pltpu.VMEM(shape, jnp.float32), pltpu.SemaphoreType.DMA((4,))] if last else [],
         input_output_aliases={} if first or last else {2: 0},
-        compiler_params=pltpu.CompilerParams(vmem_limit_bytes=16 << 20),
+        compiler_params=pltpu.CompilerParams(vmem_limit_bytes=24 << 20),
         cost_estimate=pl.CostEstimate(
-            flops=2 * rows * features * queries, bytes_accessed=4 << 20, transcendentals=0
+            flops=(20000 if first else 2) * rows * features * queries, bytes_accessed=4 << 20, transcendentals=0
         ),
         name="score",
     )(*(pltpu.with_memory_space_constraint(a, pltpu.VMEM) for a in arrays))
@@ -190,7 +178,9 @@
     near_fisher = grid.swap(inverse_fisher, 0, 1, 0)
     gathered[mirror, 0] = grid.swap(queries, mirror, 0, 0)
     staged = stage(train_feats, queries, inverse_fisher)
-    gathered[mirror, 0], staged = lax.optimization_barrier((gathered[mirror, 0], staged))
+    gathered[mirror, 0], gathered[0, 1], staged = lax.optimization_barrier(
+        (gathered[mirror, 0], gathered[0, 1], staged)
+    )
     train_here, gathered[0, 0], fisher_here = staged
     gathered[relayed, 0] = grid.swap(gathered[mirror, 0], beside, 0, 0)
     for mask in (beside, mirror, relayed):
@@ -202,14 +192,10 @@
     def swap(source, far, near):
         parts[source[0] ^ far, source[1] ^ near] = grid.swap(parts[source], far, near, 0)
 
-    def meet(*places):
-        parts.update(zip(places, lax.optimization_barrier([parts[place] for place in places])))
-
     swap(own, *far_three)
     swap(own, *near_one)
     swap(own, *far_one)
-    swap(own, beside, 1)
-    meet(near_one, (beside, 1), far_one, far_three)
+    swap(far_one, *near_one)
     swap(far_three, 0, 1)
     swap(far_three, beside, 1)
     swap(far_three, beside, 0)

time: 46.1 us -> 47.2 us (1.024)
  the two profiles are of different devices: /device:TPU:0 before, /device:TPU:27 now
where the time goes in v8:
time: 47.2 us; the launch traced here: 46.9 us
  starting transfers between devices  22.5 us (48%)
  Pallas kernels  15.3 us (32%)
  waiting for transfers between devices  9.05 us (19%)
    ppermute x17, starting transfers between devices, swap(): lax.ppermute(block, 'rows', [(row ^ step, row) for row in range(self.far...  22.5 us
    ppermute x17, waiting for transfers between devices, swap(): lax.ppermute(block, 'rows', [(row ^ step, row) for row in range(self.far...  9.05 us
    pallas_call x4, Pallas kernels, score(): pl.pallas_call(functools.partial(score_kernel, grid, masks, other, first,...  8.98 us
    pallas_call x1, Pallas kernels, stage(): pl.pallas_call(functools.partial(stage_kernel, len(arrays)), out_shape=[p...  3.49 us
    pallas_call x2, Pallas kernels, turn(): pl.pallas_call(functools.partial(turn_kernel, grid, masks), out_shape=plt...  2.36 us
  transfers between devices with their start and end apart: 17, of which 6 were waited for; matrix products, arithmetic and copies ran while one was open for 0% of the time, Pallas kernels for 23%

profile of v8, /device:TPU:27, one launch (start us, length us, event | category | flops | bytes accessed | tf_op | source)
XLA Modules:
  0.0 46.9 jit_solution(16683231749837704205)
XLA Ops:
  0.0 1.2 %collective-permute-start.7 = (bf16[1,2048,128]{2,1,0:T(8,128)(2,1)}, bf16[1,2048,128]{2,1,0:T(8,128)(2,1)S(1)}, u32[]{:S(2)}, u32[]{:S(2)}) collective-permute-start(bf16[1,2048,128]{2,1,0:T(8,128)(2,1)} %refs_2_.1), channel_id=1, source_target_pairs={{2,0},{3,1},{0,2},{1,3},{6,4},{7,5},{4,6},{5,7},{10,8},{11,9},{8,1... | collective-permute-start | bytes 1572872 | tf_op jit(solution)/shard_map/ppermute | solution.py:20
  1.2 1.2 %collective-permute-start.1 = (bf16[2,16,2048]{2,1,0:T(8,128)(2,1)}, bf16[2,16,2048]{2,1,0:T(8,128)(2,1)S(1)}, u32[]{:S(2)}, u32[]{:S(2)}) collective-permute-start(bf16[2,16,2048]{2,1,0:T(8,128)(2,1)} %refs_1_.1), channel_id=1, source_target_pairs={{1,0},{0,1},{3,2},{2,3},{5,4},{4,5},{7,6},{6,7},{9,8},{8,9},{11,10... | collective-permute-start | bytes 393224 | tf_op jit(solution)/shard_map/ppermute | solution.py:20
  2.4 0.4 collective-permute-start.2
  2.8 3.5 %stage.1 = (bf16[2048,2048]{1,0:T(8,128)(2,1)S(1)}, bf16[2,16,2048]{2,1,0:T(8,128)(2,1)S(1)}, bf16[1,2048,128]{2,1,0:T(8,128)(2,1)S(1)}) custom-call(bf16[2048,2048]{1,0:T(8,128)(2,1)} %refs_0_.1, bf16[2,16,2048]{2,1,0:T(8,128)(2,1)} %refs_1_.1, bf16[1,2048,128]{2,1,0:T(8,128)(2,1)} %refs_2_.1), custom_call_target="tpu_custom_call" | custom-call | bytes 18087936 | tf_op jit(solution)/shard_map/stage/pallas_call | solution.py:48
  6.3 0.9 %collective-permute-done.refs_3_ = bf16[2,16,2048]{2,1,0:T(8,128)(2,1)S(1)} collective-permute-done((bf16[2,16,2048]{2,1,0:T(8,128)(2,1)}, bf16[2,16,2048]{2,1,0:T(8,128)(2,1)S(1)}, u32[]{:S(2)}, u32[]{:S(2)}) %collective-permute-start) | collective-permute-done | bytes 131104 | tf_op jit(solution)/shard_map/ppermute | solution.py:20
  7.2 0.2 collective-permute-start.3
  7.5 3.2 %collective-permute-start.5 = (bf16[2,16,2048]{2,1,0:T(8,128)(2,1)S(1)}, bf16[2,16,2048]{2,1,0:T(8,128)(2,1)S(1)}, u32[]{:S(2)}, u32[]{:S(2)}) collective-permute-start(bf16[2,16,2048]{2,1,0:T(8,128)(2,1)S(1)} %collective-permute-done.refs_3_), channel_id=1, source_target_pairs={{1,0},{0,1},{3,2},{2,3},{5,4},{4,5},{7,6},{6,7},{9,8},{8,9},{11,10... | collective-permute-start | bytes 393224 | tf_op jit(solution)/shard_map/ppermute | solution.py:20
  10.6 1.1 %collective-permute-start.4 = (bf16[2,16,2048]{2,1,0:T(8,128)(2,1)S(1)}, bf16[2,16,2048]{2,1,0:T(8,128)(2,1)S(1)}, u32[]{:S(2)}, u32[]{:S(2)}) collective-permute-start(bf16[2,16,2048]{2,1,0:T(8,128)(2,1)S(1)} %collective-permute-done.2.refs_2_), channel_id=1, source_target_pairs={{1,0},{0,1},{3,2},{2,3},{5,4},{4,5},{7,6},{6,7},{9,8},{8,9},{11,10... | collective-permute-start | bytes 393224 | tf_op jit(solution)/shard_map/ppermute | solution.py:20
  11.7 0.6 %collective-permute-done.3.refs_4_ = bf16[2,16,2048]{2,1,0:T(8,128)(2,1)S(1)} collective-permute-done((bf16[2,16,2048]{2,1,0:T(8,128)(2,1)S(1)}, bf16[2,16,2048]{2,1,0:T(8,128)(2,1)S(1)}, u32[]{:S(2)}, u32[]{:S(2)}) %collective-permute-start.3) | collective-permute-done | bytes 131104 | tf_op jit(solution)/shard_map/ppermute | solution.py:20
  12.4 3.2 %collective-permute-start.6 = (bf16[2,16,2048]{2,1,0:T(8,128)(2,1)S(1)}, bf16[2,16,2048]{2,1,0:T(8,128)(2,1)S(1)}, u32[]{:S(2)}, u32[]{:S(2)}) collective-permute-start(bf16[2,16,2048]{2,1,0:T(8,128)(2,1)S(1)} %collective-permute-done.3.refs_4_), channel_id=1, source_target_pairs={{1,0},{0,1},{3,2},{2,3},{5,4},{4,5},{7,6},{6,7},{9,8},{8,9},{11,10... | collective-permute-start | bytes 393224 | tf_op jit(solution)/shard_map/ppermute | solution.py:20
  15.6 1.0 %collective-permute-done.6.refs_7_ = bf16[2,16,2048]{2,1,0:T(8,128)(2,1)S(1)} collective-permute-done((bf16[2,16,2048]{2,1,0:T(8,128)(2,1)S(1)}, bf16[2,16,2048]{2,1,0:T(8,128)(2,1)S(1)}, u32[]{:S(2)}, u32[]{:S(2)}) %collective-permute-start.6) | collective-permute-done | bytes 131104 | tf_op jit(solution)/shard_map/ppermute | solution.py:20
  16.6 0.4 condition.1.refs_0_
  17.0 0.1 collective-permute-start.13
  17.1 1.1 %collective-permute-start.8 = (bf16[2,4,2,16,256]{4,3,2,1,0:T(8,128)(2,1)S(1)}, bf16[2,4,2,16,256]{4,3,2,1,0:T(8,128)(2,1)}, u32[]{:S(2)}, u32[]{:S(2)}) collective-permute-start(bf16[2,4,2,16,256]{4,3,2,1,0:T(8,128)(2,1)S(1)} %condition.1.refs_0_), channel_id=1, source_target_pairs={{12,0},{13,1},{14,2},{15,3},{8,4},{9,5},{10,6},{11,7},{4,8},{5,9},... | collective-permute-start | bytes 393224 | tf_op jit(solution)/shard_map/ppermute | solution.py:20
  18.2 0.2 collective-permute-start.12
  18.4 3.4 %collective-permute-done.13.refs_2_ = bf16[2,4,2,16,256]{4,3,2,1,0:T(8,128)(2,1)S(1)} collective-permute-done((bf16[2,4,2,16,256]{4,3,2,1,0:T(8,128)(2,1)S(1)}, bf16[2,4,2,16,256]{4,3,2,1,0:T(8,128)(2,1)S(1)}, u32[]{:S(2)}, u32[]{:S(2)}) %collective-permute-start.13) | collective-permute-done | bytes 131104 | tf_op jit(solution)/shard_map/ppermute | solution.py:20
  21.9 0.2 collective-permute-start.14
  22.1 2.6 %collective-permute-done.8.refs_0_ = bf16[2,4,2,16,256]{4,3,2,1,0:T(8,128)(2,1)} collective-permute-done((bf16[2,4,2,16,256]{4,3,2,1,0:T(8,128)(2,1)S(1)}, bf16[2,4,2,16,256]{4,3,2,1,0:T(8,128)(2,1)}, u32[]{:S(2)}, u32[]{:S(2)}) %collective-permute-start.8) | collective-permute-done | bytes 131104 | tf_op jit(solution)/shard_map/ppermute | solution.py:20
  24.7 1.4 %collective-permute-start.10 = (bf16[2,4,2,16,256]{4,3,2,1,0:T(8,128)(2,1)}, bf16[2,4,2,16,256]{4,3,2,1,0:T(8,128)(2,1)}, u32[]{:S(2)}, u32[]{:S(2)}) collective-permute-start(bf16[2,4,2,16,256]{4,3,2,1,0:T(8,128)(2,1)} %collective-permute-done.8.refs_0_), channel_id=1, source_target_pairs={{4,0},{5,1},{6,2},{7,3},{0,4},{1,5},{2,6},{3,7},{12,8},{13,9},{14,... | collective-permute-start | bytes 393224 | tf_op jit(solution)/shard_map/ppermute | solution.py:20
  26.1 0.2 collective-permute-start.11
  26.3 1.1 %collective-permute-start.9 = (bf16[2,4,2,16,256]{4,3,2,1,0:T(8,128)(2,1)}, bf16[2,4,2,16,256]{4,3,2,1,0:T(8,128)(2,1)}, u32[]{:S(2)}, u32[]{:S(2)}) collective-permute-start(bf16[2,4,2,16,256]{4,3,2,1,0:T(8,128)(2,1)} %collective-permute-done.8.refs_0_), channel_id=1, source_target_pairs={{6,0},{7,1},{4,2},{5,3},{2,4},{3,5},{0,6},{1,7},{14,8},{15,9},{12,... | collective-permute-start | bytes 393224 | tf_op jit(solution)/shard_map/ppermute | solution.py:20
  27.3 0.0 collective-permute-done.12.refs_1_
  27.3 0.0 collective-permute-done.14.refs_3_
  27.3 1.0 %turn.2.refs_1_ = bf16[512,512]{1,0:T(8,128)(2,1)} custom-call(bf16[2,4,2,16,256]{4,3,2,1,0:T(8,128)(2,1)S(1)} %condition.1.refs_0_, bf16[2,4,2,16,256]{4,3,2,1,0:T(8,128)(2,1)S(1)} %collective-permute-done.12.refs_1_, bf16[2,4,2,16,256]{4,3,2,1,0:T(8,128)(2,1)S(1)} %collective-permute-done.13.refs_2_, ...), custom_call_target="tpu_custom_call" | custom-call | tf_op jit(solution)/shard_map/turn/pallas_call | solution.py:107
  28.4 7.6 %collective-permute-start.15 = (bf16[512,512]{1,0:T(8,128)(2,1)}, bf16[512,512]{1,0:T(8,128)(2,1)}, u32[]{:S(2)}, u32[]{:S(2)}) collective-permute-start(bf16[512,512]{1,0:T(8,128)(2,1)} %turn.2.refs_1_), channel_id=1, source_target_pairs={{1,0},{0,1},{3,2},{2,3},{5,4},{4,5},{7,6},{6,7},{9,8},{8,9},{11,10... | collective-permute-start | bytes 1572872 | tf_op jit(solution)/shard_map/ppermute | solution.py:20
  36.0 2.3 %score.4.refs_2_ = f32[2048,512]{1,0:T(8,128)S(1)} custom-call(bf16[2048,2048]{1,0:T(8,128)(2,1)S(1)} %get-tuple-element.21.refs_0_, bf16[512,512]{1,0:T(8,128)(2,1)} %turn.2.refs_1_), custom_call_target="tpu_custom_call" | custom-call | flops 10737418240000 | bytes 4194304 | tf_op jit(solution)/shard_map/score/pallas_call | solution.py:158
  38.4 2.5 %score.5.refs_2_ = f32[2048,512]{1,0:T(8,128)S(1)} custom-call(bf16[2048,2048]{1,0:T(8,128)(2,1)S(1)} %get-tuple-element.21.refs_0_, bf16[512,512]{1,0:T(8,128)(2,1)} %collective-permute-done.15.refs_1_, f32[2048,512]{1,0:T(8,128)S(1)} %score.4.refs_2_), custom_call_target="tpu_custom_call", output_to_operand_aliasing={{}: (2, {})} | custom-call | flops 1073741824 | bytes 4194304 | tf_op jit(solution)/shard_map/score/pallas_call | solution.py:158
  40.8 1.3 %turn.3.refs_1_ = bf16[512,512]{1,0:T(8,128)(2,1)S(1)} custom-call(bf16[2,4,2,16,256]{4,3,2,1,0:T(8,128)(2,1)} %collective-permute-done.8.refs_0_, bf16[2,4,2,16,256]{4,3,2,1,0:T(8,128)(2,1)} %collective-permute-done.11.refs_1_, bf16[2,4,2,16,256]{4,3,2,1,0:T(8,128)(2,1)} %collective-permute-done.10.refs_2_, ...), custom_call_target="tpu_custom_call" | custom-call | tf_op jit(solution)/shard_map/turn/pallas_call | solution.py:107
  42.2 0.1 collective-permute-start.16
  42.3 1.4 %score.6.refs_2_ = f32[2048,512]{1,0:T(8,128)S(1)} custom-call(bf16[2048,2048]{1,0:T(8,128)(2,1)S(1)} %get-tuple-element.21.refs_0_, bf16[512,512]{1,0:T(8,128)(2,1)S(1)} %turn.3.refs_1_, f32[2048,512]{1,0:T(8,128)S(1)} %score.5.refs_2_), custom_call_target="tpu_custom_call", output_to_operand_aliasing={{}: (2, {})} | custom-call | flops 1073741824 | bytes 4194304 | tf_op jit(solution)/shard_map/score/pallas_call | solution.py:158
  43.7 0.5 %collective-permute-done.16.refs_1_ = bf16[512,512]{1,0:T(8,128)(2,1)S(1)} collective-permute-done((bf16[512,512]{1,0:T(8,128)(2,1)S(1)}, bf16[512,512]{1,0:T(8,128)(2,1)S(1)}, u32[]{:S(2)}, u32[]{:S(2)}) %collective-permute-start.16) | collective-permute-done | bytes 524320 | tf_op jit(solution)/shard_map/ppermute | solution.py:20
  44.2 2.8 %score.7 = f32[2048,512]{1,0:T(8,128)} custom-call(bf16[2048,2048]{1,0:T(8,128)(2,1)S(1)} %get-tuple-element.21.refs_0_, bf16[512,512]{1,0:T(8,128)(2,1)S(1)} %collective-permute-done.16.refs_1_, f32[2048,512]{1,0:T(8,128)S(1)} %score.6.refs_2_), custom_call_target="tpu_custom_call" | custom-call | flops 1073741824 | bytes 4194304 | tf_op jit(solution)/shard_map/score/pallas_call | solution.py:158
  (10 shorter events, 0.0 us)
Async XLA Ops:
  0.0 16.6 %collective-permute-start.7 = (bf16[1,2048,128]{2,1,0:T(8,128)(2,1)}, bf16[1,2048,128]{2,1,0:T(8,128)(2,1)S(1)}, u32[]{:S(2)}, u32[]{:S(2)}) collective-permute-start(bf16[1,2048,128]{2,1,0:T(8,128)(2,1)} %refs_2_.1), channel_id=1, source_target_pairs={{2,0},{3,1},{0,2},{1,3},{6,4},{7,5},{4,6},{5,7},{10,8},{11,9},{8,1... | collective-permute-start | bytes 1572872 | tf_op jit(solution)/shard_map/ppermute | solution.py:20
  1.2 6.0 %collective-permute-start = (bf16[2,16,2048]{2,1,0:T(8,128)(2,1)}, bf16[2,16,2048]{2,1,0:T(8,128)(2,1)S(1)}, u32[]{:S(2)}, u32[]{:S(2)}) collective-permute-start(bf16[2,16,2048]{2,1,0:T(8,128)(2,1)} %refs_1_.1), channel_id=1, source_target_pairs={{12,0},{13,1},{14,2},{15,3},{8,4},{9,5},{10,6},{11,7},{4,8},{5,9},... | collective-permute-start | bytes 393224 | tf_op jit(solution)/shard_map/ppermute | solution.py:20
  1.2 6.0 %collective-permute-start.1 = (bf16[2,16,2048]{2,1,0:T(8,128)(2,1)}, bf16[2,16,2048]{2,1,0:T(8,128)(2,1)S(1)}, u32[]{:S(2)}, u32[]{:S(2)}) collective-permute-start(bf16[2,16,2048]{2,1,0:T(8,128)(2,1)} %refs_1_.1), channel_id=1, source_target_pairs={{1,0},{0,1},{3,2},{2,3},{5,4},{4,5},{7,6},{6,7},{9,8},{8,9},{11,10... | collective-permute-start | bytes 393224 | tf_op jit(solution)/shard_map/ppermute | solution.py:20
  2.4 8.2 %collective-permute-start.2 = (bf16[2,16,2048]{2,1,0:T(8,128)(2,1)}, bf16[2,16,2048]{2,1,0:T(8,128)(2,1)S(1)}, u32[]{:S(2)}, u32[]{:S(2)}) collective-permute-start(bf16[2,16,2048]{2,1,0:T(8,128)(2,1)} %refs_1_.1), channel_id=1, source_target_pairs={{4,0},{5,1},{6,2},{7,3},{0,4},{1,5},{2,6},{3,7},{12,8},{13,9},{14,... | collective-permute-start | bytes 393224 | tf_op jit(solution)/shard_map/ppermute | solution.py:20
  7.2 5.1 %collective-permute-start.3 = (bf16[2,16,2048]{2,1,0:T(8,128)(2,1)S(1)}, bf16[2,16,2048]{2,1,0:T(8,128)(2,1)S(1)}, u32[]{:S(2)}, u32[]{:S(2)}) collective-permute-start(bf16[2,16,2048]{2,1,0:T(8,128)(2,1)S(1)} %collective-permute-done.refs_3_), channel_id=1, source_target_pairs={{4,0},{5,1},{6,2},{7,3},{0,4},{1,5},{2,6},{3,7},{12,8},{13,9},{14,... | collective-permute-start | bytes 393224 | tf_op jit(solution)/shard_map/ppermute | solution.py:20
  7.5 8.1 %collective-permute-start.5 = (bf16[2,16,2048]{2,1,0:T(8,128)(2,1)S(1)}, bf16[2,16,2048]{2,1,0:T(8,128)(2,1)S(1)}, u32[]{:S(2)}, u32[]{:S(2)}) collective-permute-start(bf16[2,16,2048]{2,1,0:T(8,128)(2,1)S(1)} %collective-permute-done.refs_3_), channel_id=1, source_target_pairs={{1,0},{0,1},{3,2},{2,3},{5,4},{4,5},{7,6},{6,7},{9,8},{8,9},{11,10... | collective-permute-start | bytes 393224 | tf_op jit(solution)/shard_map/ppermute | solution.py:20
  10.6 5.0 %collective-permute-start.4 = (bf16[2,16,2048]{2,1,0:T(8,128)(2,1)S(1)}, bf16[2,16,2048]{2,1,0:T(8,128)(2,1)S(1)}, u32[]{:S(2)}, u32[]{:S(2)}) collective-permute-start(bf16[2,16,2048]{2,1,0:T(8,128)(2,1)S(1)} %collective-permute-done.2.refs_2_), channel_id=1, source_target_pairs={{1,0},{0,1},{3,2},{2,3},{5,4},{4,5},{7,6},{6,7},{9,8},{8,9},{11,10... | collective-permute-start | bytes 393224 | tf_op jit(solution)/shard_map/ppermute | solution.py:20
  12.4 4.2 %collective-permute-start.6 = (bf16[2,16,2048]{2,1,0:T(8,128)(2,1)S(1)}, bf16[2,16,2048]{2,1,0:T(8,128)(2,1)S(1)}, u32[]{:S(2)}, u32[]{:S(2)}) collective-permute-start(bf16[2,16,2048]{2,1,0:T(8,128)(2,1)S(1)} %collective-permute-done.3.refs_4_), channel_id=1, source_target_pairs={{1,0},{0,1},{3,2},{2,3},{5,4},{4,5},{7,6},{6,7},{9,8},{8,9},{11,10... | collective-permute-start | bytes 393224 | tf_op jit(solution)/shard_map/ppermute | solution.py:20
  17.0 4.9 %collective-permute-start.13 = (bf16[2,4,2,16,256]{4,3,2,1,0:T(8,128)(2,1)S(1)}, bf16[2,4,2,16,256]{4,3,2,1,0:T(8,128)(2,1)S(1)}, u32[]{:S(2)}, u32[]{:S(2)}) collective-permute-start(bf16[2,4,2,16,256]{4,3,2,1,0:T(8,128)(2,1)S(1)} %condition.1.refs_0_), channel_id=1, source_target_pairs={{4,0},{5,1},{6,2},{7,3},{0,4},{1,5},{2,6},{3,7},{12,8},{13,9},{14,... | collective-permute-start | bytes 393224 | tf_op jit(solution)/shard_map/ppermute | solution.py:20
  17.1 7.6 %collective-permute-start.8 = (bf16[2,4,2,16,256]{4,3,2,1,0:T(8,128)(2,1)S(1)}, bf16[2,4,2,16,256]{4,3,2,1,0:T(8,128)(2,1)}, u32[]{:S(2)}, u32[]{:S(2)}) collective-permute-start(bf16[2,4,2,16,256]{4,3,2,1,0:T(8,128)(2,1)S(1)} %condition.1.refs_0_), channel_id=1, source_target_pairs={{12,0},{13,1},{14,2},{15,3},{8,4},{9,5},{10,6},{11,7},{4,8},{5,9},... | collective-permute-start | bytes 393224 | tf_op jit(solution)/shard_map/ppermute | solution.py:20
  18.2 9.1 %collective-permute-start.12 = (bf16[2,4,2,16,256]{4,3,2,1,0:T(8,128)(2,1)S(1)}, bf16[2,4,2,16,256]{4,3,2,1,0:T(8,128)(2,1)S(1)}, u32[]{:S(2)}, u32[]{:S(2)}) collective-permute-start(bf16[2,4,2,16,256]{4,3,2,1,0:T(8,128)(2,1)S(1)} %condition.1.refs_0_), channel_id=1, source_target_pairs={{2,0},{3,1},{0,2},{1,3},{6,4},{7,5},{4,6},{5,7},{10,8},{11,9},{8,1... | collective-permute-start | bytes 393224 | tf_op jit(solution)/shard_map/ppermute | solution.py:20
  21.9 5.5 %collective-permute-start.14 = (bf16[2,4,2,16,256]{4,3,2,1,0:T(8,128)(2,1)S(1)}, bf16[2,4,2,16,256]{4,3,2,1,0:T(8,128)(2,1)S(1)}, u32[]{:S(2)}, u32[]{:S(2)}) collective-permute-start(bf16[2,4,2,16,256]{4,3,2,1,0:T(8,128)(2,1)S(1)} %collective-permute-done.13.refs_2_), channel_id=1, source_target_pairs={{2,0},{3,1},{0,2},{1,3},{6,4},{7,5},{4,6},{5,7},{10,8},{11,9},{8,1... | collective-permute-start | bytes 393224 | tf_op jit(solution)/shard_map/ppermute | solution.py:20
  24.7 16.1 %collective-permute-start.10 = (bf16[2,4,2,16,256]{4,3,2,1,0:T(8,128)(2,1)}, bf16[2,4,2,16,256]{4,3,2,1,0:T(8,128)(2,1)}, u32[]{:S(2)}, u32[]{:S(2)}) collective-permute-start(bf16[2,4,2,16,256]{4,3,2,1,0:T(8,128)(2,1)} %collective-permute-done.8.refs_0_), channel_id=1, source_target_pairs={{4,0},{5,1},{6,2},{7,3},{0,4},{1,5},{2,6},{3,7},{12,8},{13,9},{14,... | collective-permute-start | bytes 393224 | tf_op jit(solution)/shard_map/ppermute | solution.py:20
  26.1 14.8 %collective-permute-start.11 = (bf16[2,4,2,16,256]{4,3,2,1,0:T(8,128)(2,1)}, bf16[2,4,2,16,256]{4,3,2,1,0:T(8,128)(2,1)}, u32[]{:S(2)}, u32[]{:S(2)}) collective-permute-start(bf16[2,4,2,16,256]{4,3,2,1,0:T(8,128)(2,1)} %collective-permute-done.8.refs_0_), channel_id=1, source_target_pairs={{2,0},{3,1},{0,2},{1,3},{6,4},{7,5},{4,6},{5,7},{10,8},{11,9},{8,1... | collective-permute-start | bytes 393224 | tf_op jit(solution)/shard_map/ppermute | solution.py:20
  26.3 14.6 %collective-permute-start.9 = (bf16[2,4,2,16,256]{4,3,2,1,0:T(8,128)(2,1)}, bf16[2,4,2,16,256]{4,3,2,1,0:T(8,128)(2,1)}, u32[]{:S(2)}, u32[]{:S(2)}) collective-permute-start(bf16[2,4,2,16,256]{4,3,2,1,0:T(8,128)(2,1)} %collective-permute-done.8.refs_0_), channel_id=1, source_target_pairs={{6,0},{7,1},{4,2},{5,3},{2,4},{3,5},{0,6},{1,7},{14,8},{15,9},{12,... | collective-permute-start | bytes 393224 | tf_op jit(solution)/shard_map/ppermute | solution.py:20
  28.4 10.0 %collective-permute-start.15 = (bf16[512,512]{1,0:T(8,128)(2,1)}, bf16[512,512]{1,0:T(8,128)(2,1)}, u32[]{:S(2)}, u32[]{:S(2)}) collective-permute-start(bf16[512,512]{1,0:T(8,128)(2,1)} %turn.2.refs_1_), channel_id=1, source_target_pairs={{1,0},{0,1},{3,2},{2,3},{5,4},{4,5},{7,6},{6,7},{9,8},{8,9},{11,10... | collective-permute-start | bytes 1572872 | tf_op jit(solution)/shard_map/ppermute | solution.py:20
  42.2 2.0 %collective-permute-start.16 = (bf16[512,512]{1,0:T(8,128)(2,1)S(1)}, bf16[512,512]{1,0:T(8,128)(2,1)S(1)}, u32[]{:S(2)}, u32[]{:S(2)}) collective-permute-start(bf16[512,512]{1,0:T(8,128)(2,1)S(1)} %turn.3.refs_1_), channel_id=1, source_target_pairs={{1,0},{0,1},{3,2},{2,3},{5,4},{4,5},{7,6},{6,7},{9,8},{8,9},{11,10... | collective-permute-start | bytes 1572872 | tf_op jit(solution)/shard_map/ppermute | solution.py:20

commit v9 on v8

--- a/solution.py
+++ b/solution.py
@@ -52,7 +52,7 @@
         out_specs=[VMEM] * len(arrays),
         scratch_shapes=[pltpu.SemaphoreType.DMA((len(arrays),))],
         compiler_params=pltpu.CompilerParams(vmem_limit_bytes=4 << 20),
-        cost_estimate=pl.CostEstimate(flops=0, bytes_accessed=2 * size, transcendentals=0),
+        cost_estimate=pl.CostEstimate(flops=1 << 36, bytes_accessed=2 * size, transcendentals=0),
         name="stage",
     )(*(pltpu.with_memory_space_constraint(a, pltpu.HBM) for a in arrays))
 
@@ -164,7 +164,7 @@
         input_output_aliases={} if first or last else {2: 0},
         compiler_params=pltpu.CompilerParams(vmem_limit_bytes=24 << 20),
         cost_estimate=pl.CostEstimate(
-            flops=(20000 if first else 2) * rows * features * queries, bytes_accessed=4 << 20, transcendentals=0
+            flops=(40 if first else 2) * rows * features * queries, bytes_accessed=4 << 20, transcendentals=0
         ),
         name="score",
     )(*(pltpu.with_memory_space_constraint(a, pltpu.VMEM) for a in arrays))

time: 47.2 us -> 42.5 us (0.900)
  the two profiles are of different devices: /device:TPU:27 before, /device:TPU:0 now
where the time goes in v9:
time: 42.5 us; the launch traced here: 42.3 us
  starting transfers between devices  17.9 us (42%)
  waiting for transfers between devices  13.1 us (31%)
  Pallas kernels  11.3 us (27%)
    ppermute x17, starting transfers between devices, swap(): lax.ppermute(block, 'rows', [(row ^ step, row) for row in range(self.far...  17.9 us
    ppermute x17, waiting for transfers between devices, swap(): lax.ppermute(block, 'rows', [(row ^ step, row) for row in range(self.far...  13.1 us
    pallas_call x4, Pallas kernels, score(): pl.pallas_call(functools.partial(score_kernel, grid, masks, other, first,...  6.88 us
    pallas_call x1, Pallas kernels, stage(): pl.pallas_call(functools.partial(stage_kernel, len(arrays)), out_shape=[p...  3.49 us
  transfers between devices with their start and end apart: 17, of which 9 were waited for; matrix products, arithmetic and copies ran while one was open for 0% of the time, Pallas kernels for 18%

profile of v9, /device:TPU:0, one launch (start us, length us, event | category | flops | bytes accessed | tf_op | source)
XLA Modules:
  0.0 42.3 jit_solution(13418219582579096852)
XLA Ops:
  0.0 5.0 %collective-permute-start = (bf16[2,16,2048]{2,1,0:T(8,128)(2,1)}, bf16[2,16,2048]{2,1,0:T(8,128)(2,1)S(1)}, u32[]{:S(2)}, u32[]{:S(2)}) collective-permute-start(bf16[2,16,2048]{2,1,0:T(8,128)(2,1)} %refs_1_.1), channel_id=1, source_target_pairs={{12,0},{13,1},{14,2},{15,3},{8,4},{9,5},{10,6},{11,7},{4,8},{5,9},... | collective-permute-start | bytes 393224 | tf_op jit(solution)/shard_map/ppermute | solution.py:20
  5.0 0.0 collective-permute-start.1
  5.1 0.0 collective-permute-start.2
  5.1 1.5 %collective-permute-start.7 = (bf16[1,2048,128]{2,1,0:T(8,128)(2,1)}, bf16[1,2048,128]{2,1,0:T(8,128)(2,1)S(1)}, u32[]{:S(2)}, u32[]{:S(2)}) collective-permute-start(bf16[1,2048,128]{2,1,0:T(8,128)(2,1)} %refs_2_.1), channel_id=1, source_target_pairs={{2,0},{3,1},{0,2},{1,3},{6,4},{7,5},{4,6},{5,7},{10,8},{11,9},{8,1... | collective-permute-start | bytes 1572872 | tf_op jit(solution)/shard_map/ppermute | solution.py:20
  6.6 3.5 %stage.1 = (bf16[2048,2048]{1,0:T(8,128)(2,1)S(1)}, bf16[2,16,2048]{2,1,0:T(8,128)(2,1)S(1)}, bf16[1,2048,128]{2,1,0:T(8,128)(2,1)S(1)}) custom-call(bf16[2048,2048]{1,0:T(8,128)(2,1)} %refs_0_.1, bf16[2,16,2048]{2,1,0:T(8,128)(2,1)} %refs_1_.1, bf16[1,2048,128]{2,1,0:T(8,128)(2,1)} %refs_2_.1), custom_call_target="tpu_custom_call" | custom-call | flops 68719476736 | bytes 18087936 | tf_op jit(solution)/shard_map/stage/pallas_call | solution.py:48
  10.1 2.1 %collective-permute-start.3 = (bf16[2,16,2048]{2,1,0:T(8,128)(2,1)S(1)}, bf16[2,16,2048]{2,1,0:T(8,128)(2,1)S(1)}, u32[]{:S(2)}, u32[]{:S(2)}) collective-permute-start(bf16[2,16,2048]{2,1,0:T(8,128)(2,1)S(1)} %collective-permute-done.refs_3_), channel_id=1, source_target_pairs={{4,0},{5,1},{6,2},{7,3},{0,4},{1,5},{2,6},{3,7},{12,8},{13,9},{14,... | collective-permute-start | bytes 393224 | tf_op jit(solution)/shard_map/ppermute | solution.py:20
  12.2 0.5 %collective-permute-start.4 = (bf16[2,16,2048]{2,1,0:T(8,128)(2,1)S(1)}, bf16[2,16,2048]{2,1,0:T(8,128)(2,1)S(1)}, u32[]{:S(2)}, u32[]{:S(2)}) collective-permute-start(bf16[2,16,2048]{2,1,0:T(8,128)(2,1)S(1)} %collective-permute-done.2.refs_2_), channel_id=1, source_target_pairs={{1,0},{0,1},{3,2},{2,3},{5,4},{4,5},{7,6},{6,7},{9,8},{8,9},{11,10... | collective-permute-start | bytes 393224 | tf_op jit(solution)/shard_map/ppermute | solution.py:20
  12.7 3.1 %collective-permute-done.3.refs_4_ = bf16[2,16,2048]{2,1,0:T(8,128)(2,1)S(1)} collective-permute-done((bf16[2,16,2048]{2,1,0:T(8,128)(2,1)S(1)}, bf16[2,16,2048]{2,1,0:T(8,128)(2,1)S(1)}, u32[]{:S(2)}, u32[]{:S(2)}) %collective-permute-start.3) | collective-permute-done | bytes 131104 | tf_op jit(solution)/shard_map/ppermute | solution.py:20
  15.8 1.3 %collective-permute-done.6.refs_7_ = bf16[2,16,2048]{2,1,0:T(8,128)(2,1)S(1)} collective-permute-done((bf16[2,16,2048]{2,1,0:T(8,128)(2,1)S(1)}, bf16[2,16,2048]{2,1,0:T(8,128)(2,1)S(1)}, u32[]{:S(2)}, u32[]{:S(2)}) %collective-permute-start.6) | collective-permute-done | bytes 131104 | tf_op jit(solution)/shard_map/ppermute | solution.py:20
  17.1 2.5 %collective-permute-done.7.refs_9_ = bf16[1,2048,128]{2,1,0:T(8,128)(2,1)S(1)} collective-permute-done((bf16[1,2048,128]{2,1,0:T(8,128)(2,1)}, bf16[1,2048,128]{2,1,0:T(8,128)(2,1)S(1)}, u32[]{:S(2)}, u32[]{:S(2)}) %collective-permute-start.7) | collective-permute-done | bytes 524320 | tf_op jit(solution)/shard_map/ppermute | solution.py:20
  19.6 0.4 %condition.1.refs_0_ = bf16[2,4,2,16,256]{4,3,2,1,0:T(8,128)(2,1)S(1)} custom-call(bf16[2,16,2048]{2,1,0:T(8,128)(2,1)S(1)} %get-tuple-element.22.refs_0_, bf16[2,16,2048]{2,1,0:T(8,128)(2,1)S(1)} %collective-permute-done.1.refs_1_, bf16[2,16,2048]{2,1,0:T(8,128)(2,1)S(1)} %collective-permute-done.2.refs_2_, ...), custom_call_target="tpu_custom_call" | custom-call | flops 268435456 | bytes 3145728 | tf_op jit(solution)/shard_map/condition/pallas_call | solution.py:80
  20.1 1.8 %collective-permute-start.13 = (bf16[2,4,2,16,256]{4,3,2,1,0:T(8,128)(2,1)S(1)}, bf16[2,4,2,16,256]{4,3,2,1,0:T(8,128)(2,1)S(1)}, u32[]{:S(2)}, u32[]{:S(2)}) collective-permute-start(bf16[2,4,2,16,256]{4,3,2,1,0:T(8,128)(2,1)S(1)} %condition.1.refs_0_), channel_id=1, source_target_pairs={{4,0},{5,1},{6,2},{7,3},{0,4},{1,5},{2,6},{3,7},{12,8},{13,9},{14,... | collective-permute-start | bytes 393224 | tf_op jit(solution)/shard_map/ppermute | solution.py:20
  21.9 0.0 collective-permute-start.8
  21.9 1.7 %collective-permute-start.12 = (bf16[2,4,2,16,256]{4,3,2,1,0:T(8,128)(2,1)S(1)}, bf16[2,4,2,16,256]{4,3,2,1,0:T(8,128)(2,1)S(1)}, u32[]{:S(2)}, u32[]{:S(2)}) collective-permute-start(bf16[2,4,2,16,256]{4,3,2,1,0:T(8,128)(2,1)S(1)} %condition.1.refs_0_), channel_id=1, source_target_pairs={{2,0},{3,1},{0,2},{1,3},{6,4},{7,5},{4,6},{5,7},{10,8},{11,9},{8,1... | collective-permute-start | bytes 393224 | tf_op jit(solution)/shard_map/ppermute | solution.py:20
  23.6 2.0 %collective-permute-done.13.refs_2_ = bf16[2,4,2,16,256]{4,3,2,1,0:T(8,128)(2,1)S(1)} collective-permute-done((bf16[2,4,2,16,256]{4,3,2,1,0:T(8,128)(2,1)S(1)}, bf16[2,4,2,16,256]{4,3,2,1,0:T(8,128)(2,1)S(1)}, u32[]{:S(2)}, u32[]{:S(2)}) %collective-permute-start.13) | collective-permute-done | bytes 131104 | tf_op jit(solution)/shard_map/ppermute | solution.py:20
  25.6 1.5 %collective-permute-start.14 = (bf16[2,4,2,16,256]{4,3,2,1,0:T(8,128)(2,1)S(1)}, bf16[2,4,2,16,256]{4,3,2,1,0:T(8,128)(2,1)S(1)}, u32[]{:S(2)}, u32[]{:S(2)}) collective-permute-start(bf16[2,4,2,16,256]{4,3,2,1,0:T(8,128)(2,1)S(1)} %collective-permute-done.13.refs_2_), channel_id=1, source_target_pairs={{2,0},{3,1},{0,2},{1,3},{6,4},{7,5},{4,6},{5,7},{10,8},{11,9},{8,1... | collective-permute-start | bytes 393224 | tf_op jit(solution)/shard_map/ppermute | solution.py:20
  27.1 1.6 %collective-permute-done.8.refs_0_ = bf16[2,4,2,16,256]{4,3,2,1,0:T(8,128)(2,1)S(1)} collective-permute-done((bf16[2,4,2,16,256]{4,3,2,1,0:T(8,128)(2,1)S(1)}, bf16[2,4,2,16,256]{4,3,2,1,0:T(8,128)(2,1)S(1)}, u32[]{:S(2)}, u32[]{:S(2)}) %collective-permute-start.8) | collective-permute-done | bytes 131104 | tf_op jit(solution)/shard_map/ppermute | solution.py:20
  28.7 1.2 %collective-permute-start.10 = (bf16[2,4,2,16,256]{4,3,2,1,0:T(8,128)(2,1)S(1)}, bf16[2,4,2,16,256]{4,3,2,1,0:T(8,128)(2,1)S(1)}, u32[]{:S(2)}, u32[]{:S(2)}) collective-permute-start(bf16[2,4,2,16,256]{4,3,2,1,0:T(8,128)(2,1)S(1)} %collective-permute-done.8.refs_0_), channel_id=1, source_target_pairs={{4,0},{5,1},{6,2},{7,3},{0,4},{1,5},{2,6},{3,7},{12,8},{13,9},{14,... | collective-permute-start | bytes 393224 | tf_op jit(solution)/shard_map/ppermute | solution.py:20
  29.9 1.5 %collective-permute-start.11 = (bf16[2,4,2,16,256]{4,3,2,1,0:T(8,128)(2,1)S(1)}, bf16[2,4,2,16,256]{4,3,2,1,0:T(8,128)(2,1)S(1)}, u32[]{:S(2)}, u32[]{:S(2)}) collective-permute-start(bf16[2,4,2,16,256]{4,3,2,1,0:T(8,128)(2,1)S(1)} %collective-permute-done.8.refs_0_), channel_id=1, source_target_pairs={{2,0},{3,1},{0,2},{1,3},{6,4},{7,5},{4,6},{5,7},{10,8},{11,9},{8,1... | collective-permute-start | bytes 393224 | tf_op jit(solution)/shard_map/ppermute | solution.py:20
  31.4 0.7 %collective-permute-start.9 = (bf16[2,4,2,16,256]{4,3,2,1,0:T(8,128)(2,1)S(1)}, bf16[2,4,2,16,256]{4,3,2,1,0:T(8,128)(2,1)S(1)}, u32[]{:S(2)}, u32[]{:S(2)}) collective-permute-start(bf16[2,4,2,16,256]{4,3,2,1,0:T(8,128)(2,1)S(1)} %collective-permute-done.8.refs_0_), channel_id=1, source_target_pairs={{6,0},{7,1},{4,2},{5,3},{2,4},{3,5},{0,6},{1,7},{14,8},{15,9},{12,... | collective-permute-start | bytes 393224 | tf_op jit(solution)/shard_map/ppermute | solution.py:20
  32.2 1.0 %collective-permute-done.14.refs_3_ = bf16[2,4,2,16,256]{4,3,2,1,0:T(8,128)(2,1)S(1)} collective-permute-done((bf16[2,4,2,16,256]{4,3,2,1,0:T(8,128)(2,1)S(1)}, bf16[2,4,2,16,256]{4,3,2,1,0:T(8,128)(2,1)S(1)}, u32[]{:S(2)}, u32[]{:S(2)}) %collective-permute-start.14) | collective-permute-done | bytes 131104 | tf_op jit(solution)/shard_map/ppermute | solution.py:20
  33.2 0.2 turn.2.refs_1_
  33.5 0.1 collective-permute-start.15
  33.5 1.3 %score.4.refs_2_ = f32[2048,512]{1,0:T(8,128)S(1)} custom-call(bf16[2048,2048]{1,0:T(8,128)(2,1)S(1)} %get-tuple-element.21.refs_0_, bf16[512,512]{1,0:T(8,128)(2,1)S(1)} %turn.2.refs_1_), custom_call_target="tpu_custom_call" | custom-call | flops 21474836480 | bytes 4194304 | tf_op jit(solution)/shard_map/score/pallas_call | solution.py:158
  34.8 0.6 %collective-permute-done.15.refs_1_ = bf16[512,512]{1,0:T(8,128)(2,1)S(1)} collective-permute-done((bf16[512,512]{1,0:T(8,128)(2,1)S(1)}, bf16[512,512]{1,0:T(8,128)(2,1)S(1)}, u32[]{:S(2)}, u32[]{:S(2)}) %collective-permute-start.15) | collective-permute-done | bytes 524320 | tf_op jit(solution)/shard_map/ppermute | solution.py:20
  35.4 1.4 %score.5.refs_2_ = f32[2048,512]{1,0:T(8,128)S(1)} custom-call(bf16[2048,2048]{1,0:T(8,128)(2,1)S(1)} %get-tuple-element.21.refs_0_, bf16[512,512]{1,0:T(8,128)(2,1)S(1)} %collective-permute-done.15.refs_1_, f32[2048,512]{1,0:T(8,128)S(1)} %score.4.refs_2_), custom_call_target="tpu_custom_call", output_to_operand_aliasing={{}: (2, {})} | custom-call | flops 1073741824 | bytes 4194304 | tf_op jit(solution)/shard_map/score/pallas_call | solution.py:158
  36.9 0.4 %collective-permute-done.9.refs_3_ = bf16[2,4,2,16,256]{4,3,2,1,0:T(8,128)(2,1)S(1)} collective-permute-done((bf16[2,4,2,16,256]{4,3,2,1,0:T(8,128)(2,1)S(1)}, bf16[2,4,2,16,256]{4,3,2,1,0:T(8,128)(2,1)S(1)}, u32[]{:S(2)}, u32[]{:S(2)}) %collective-permute-start.9) | collective-permute-done | bytes 131104 | tf_op jit(solution)/shard_map/ppermute | solution.py:20
  37.3 0.2 turn.3.refs_1_
  37.5 0.1 collective-permute-start.16
  37.6 1.4 %score.6.refs_2_ = f32[2048,512]{1,0:T(8,128)S(1)} custom-call(bf16[2048,2048]{1,0:T(8,128)(2,1)S(1)} %get-tuple-element.21.refs_0_, bf16[512,512]{1,0:T(8,128)(2,1)S(1)} %turn.3.refs_1_, f32[2048,512]{1,0:T(8,128)S(1)} %score.5.refs_2_), custom_call_target="tpu_custom_call", output_to_operand_aliasing={{}: (2, {})} | custom-call | flops 1073741824 | bytes 4194304 | tf_op jit(solution)/shard_map/score/pallas_call | solution.py:158
  39.0 0.5 %collective-permute-done.16.refs_1_ = bf16[512,512]{1,0:T(8,128)(2,1)S(1)} collective-permute-done((bf16[512,512]{1,0:T(8,128)(2,1)S(1)}, bf16[512,512]{1,0:T(8,128)(2,1)S(1)}, u32[]{:S(2)}, u32[]{:S(2)}) %collective-permute-start.16) | collective-permute-done | bytes 524320 | tf_op jit(solution)/shard_map/ppermute | solution.py:20
  39.5 2.8 %score.7 = f32[2048,512]{1,0:T(8,128)} custom-call(bf16[2048,2048]{1,0:T(8,128)(2,1)S(1)} %get-tuple-element.21.refs_0_, bf16[512,512]{1,0:T(8,128)(2,1)S(1)} %collective-permute-done.16.refs_1_, f32[2048,512]{1,0:T(8,128)S(1)} %score.6.refs_2_), custom_call_target="tpu_custom_call" | custom-call | flops 1073741824 | bytes 4194304 | tf_op jit(solution)/shard_map/score/pallas_call | solution.py:158
  (10 shorter events, 0.0 us)
Async XLA Ops:
  0.0 10.1 %collective-permute-start = (bf16[2,16,2048]{2,1,0:T(8,128)(2,1)}, bf16[2,16,2048]{2,1,0:T(8,128)(2,1)S(1)}, u32[]{:S(2)}, u32[]{:S(2)}) collective-permute-start(bf16[2,16,2048]{2,1,0:T(8,128)(2,1)} %refs_1_.1), channel_id=1, source_target_pairs={{12,0},{13,1},{14,2},{15,3},{8,4},{9,5},{10,6},{11,7},{4,8},{5,9},... | collective-permute-start | bytes 393224 | tf_op jit(solution)/shard_map/ppermute | solution.py:20
  5.0 5.0 %collective-permute-start.1 = (bf16[2,16,2048]{2,1,0:T(8,128)(2,1)}, bf16[2,16,2048]{2,1,0:T(8,128)(2,1)S(1)}, u32[]{:S(2)}, u32[]{:S(2)}) collective-permute-start(bf16[2,16,2048]{2,1,0:T(8,128)(2,1)} %refs_1_.1), channel_id=1, source_target_pairs={{1,0},{0,1},{3,2},{2,3},{5,4},{4,5},{7,6},{6,7},{9,8},{8,9},{11,10... | collective-permute-start | bytes 393224 | tf_op jit(solution)/shard_map/ppermute | solution.py:20
  5.1 7.1 %collective-permute-start.2 = (bf16[2,16,2048]{2,1,0:T(8,128)(2,1)}, bf16[2,16,2048]{2,1,0:T(8,128)(2,1)S(1)}, u32[]{:S(2)}, u32[]{:S(2)}) collective-permute-start(bf16[2,16,2048]{2,1,0:T(8,128)(2,1)} %refs_1_.1), channel_id=1, source_target_pairs={{4,0},{5,1},{6,2},{7,3},{0,4},{1,5},{2,6},{3,7},{12,8},{13,9},{14,... | collective-permute-start | bytes 393224 | tf_op jit(solution)/shard_map/ppermute | solution.py:20
  5.1 14.5 %collective-permute-start.7 = (bf16[1,2048,128]{2,1,0:T(8,128)(2,1)}, bf16[1,2048,128]{2,1,0:T(8,128)(2,1)S(1)}, u32[]{:S(2)}, u32[]{:S(2)}) collective-permute-start(bf16[1,2048,128]{2,1,0:T(8,128)(2,1)} %refs_2_.1), channel_id=1, source_target_pairs={{2,0},{3,1},{0,2},{1,3},{6,4},{7,5},{4,6},{5,7},{10,8},{11,9},{8,1... | collective-permute-start | bytes 1572872 | tf_op jit(solution)/shard_map/ppermute | solution.py:20
  10.1 5.7 %collective-permute-start.3 = (bf16[2,16,2048]{2,1,0:T(8,128)(2,1)S(1)}, bf16[2,16,2048]{2,1,0:T(8,128)(2,1)S(1)}, u32[]{:S(2)}, u32[]{:S(2)}) collective-permute-start(bf16[2,16,2048]{2,1,0:T(8,128)(2,1)S(1)} %collective-permute-done.refs_3_), channel_id=1, source_target_pairs={{4,0},{5,1},{6,2},{7,3},{0,4},{1,5},{2,6},{3,7},{12,8},{13,9},{14,... | collective-permute-start | bytes 393224 | tf_op jit(solution)/shard_map/ppermute | solution.py:20
  12.2 3.6 %collective-permute-start.5 = (bf16[2,16,2048]{2,1,0:T(8,128)(2,1)S(1)}, bf16[2,16,2048]{2,1,0:T(8,128)(2,1)S(1)}, u32[]{:S(2)}, u32[]{:S(2)}) collective-permute-start(bf16[2,16,2048]{2,1,0:T(8,128)(2,1)S(1)} %collective-permute-done.refs_3_), channel_id=1, source_target_pairs={{1,0},{0,1},{3,2},{2,3},{5,4},{4,5},{7,6},{6,7},{9,8},{8,9},{11,10... | collective-permute-start | bytes 393224 | tf_op jit(solution)/shard_map/ppermute | solution.py:20
  12.2 3.6 %collective-permute-start.4 = (bf16[2,16,2048]{2,1,0:T(8,128)(2,1)S(1)}, bf16[2,16,2048]{2,1,0:T(8,128)(2,1)S(1)}, u32[]{:S(2)}, u32[]{:S(2)}) collective-permute-start(bf16[2,16,2048]{2,1,0:T(8,128)(2,1)S(1)} %collective-permute-done.2.refs_2_), channel_id=1, source_target_pairs={{1,0},{0,1},{3,2},{2,3},{5,4},{4,5},{7,6},{6,7},{9,8},{8,9},{11,10... | collective-permute-start | bytes 393224 | tf_op jit(solution)/shard_map/ppermute | solution.py:20
  15.8 1.3 %collective-permute-start.6 = (bf16[2,16,2048]{2,1,0:T(8,128)(2,1)S(1)}, bf16[2,16,2048]{2,1,0:T(8,128)(2,1)S(1)}, u32[]{:S(2)}, u32[]{:S(2)}) collective-permute-start(bf16[2,16,2048]{2,1,0:T(8,128)(2,1)S(1)} %collective-permute-done.3.refs_4_), channel_id=1, source_target_pairs={{1,0},{0,1},{3,2},{2,3},{5,4},{4,5},{7,6},{6,7},{9,8},{8,9},{11,10... | collective-permute-start | bytes 393224 | tf_op jit(solution)/shard_map/ppermute | solution.py:20
  20.1 5.5 %collective-permute-start.13 = (bf16[2,4,2,16,256]{4,3,2,1,0:T(8,128)(2,1)S(1)}, bf16[2,4,2,16,256]{4,3,2,1,0:T(8,128)(2,1)S(1)}, u32[]{:S(2)}, u32[]{:S(2)}) collective-permute-start(bf16[2,4,2,16,256]{4,3,2,1,0:T(8,128)(2,1)S(1)} %condition.1.refs_0_), channel_id=1, source_target_pairs={{4,0},{5,1},{6,2},{7,3},{0,4},{1,5},{2,6},{3,7},{12,8},{13,9},{14,... | collective-permute-start | bytes 393224 | tf_op jit(solution)/shard_map/ppermute | solution.py:20
  21.9 6.8 %collective-permute-start.8 = (bf16[2,4,2,16,256]{4,3,2,1,0:T(8,128)(2,1)S(1)}, bf16[2,4,2,16,256]{4,3,2,1,0:T(8,128)(2,1)S(1)}, u32[]{:S(2)}, u32[]{:S(2)}) collective-permute-start(bf16[2,4,2,16,256]{4,3,2,1,0:T(8,128)(2,1)S(1)} %condition.1.refs_0_), channel_id=1, source_target_pairs={{12,0},{13,1},{14,2},{15,3},{8,4},{9,5},{10,6},{11,7},{4,8},{5,9},... | collective-permute-start | bytes 393224 | tf_op jit(solution)/shard_map/ppermute | solution.py:20
  21.9 10.3 %collective-permute-start.12 = (bf16[2,4,2,16,256]{4,3,2,1,0:T(8,128)(2,1)S(1)}, bf16[2,4,2,16,256]{4,3,2,1,0:T(8,128)(2,1)S(1)}, u32[]{:S(2)}, u32[]{:S(2)}) collective-permute-start(bf16[2,4,2,16,256]{4,3,2,1,0:T(8,128)(2,1)S(1)} %condition.1.refs_0_), channel_id=1, source_target_pairs={{2,0},{3,1},{0,2},{1,3},{6,4},{7,5},{4,6},{5,7},{10,8},{11,9},{8,1... | collective-permute-start | bytes 393224 | tf_op jit(solution)/shard_map/ppermute | solution.py:20
  25.6 7.6 %collective-permute-start.14 = (bf16[2,4,2,16,256]{4,3,2,1,0:T(8,128)(2,1)S(1)}, bf16[2,4,2,16,256]{4,3,2,1,0:T(8,128)(2,1)S(1)}, u32[]{:S(2)}, u32[]{:S(2)}) collective-permute-start(bf16[2,4,2,16,256]{4,3,2,1,0:T(8,128)(2,1)S(1)} %collective-permute-done.13.refs_2_), channel_id=1, source_target_pairs={{2,0},{3,1},{0,2},{1,3},{6,4},{7,5},{4,6},{5,7},{10,8},{11,9},{8,1... | collective-permute-start | bytes 393224 | tf_op jit(solution)/shard_map/ppermute | solution.py:20
  28.7 8.2 %collective-permute-start.10 = (bf16[2,4,2,16,256]{4,3,2,1,0:T(8,128)(2,1)S(1)}, bf16[2,4,2,16,256]{4,3,2,1,0:T(8,128)(2,1)S(1)}, u32[]{:S(2)}, u32[]{:S(2)}) collective-permute-start(bf16[2,4,2,16,256]{4,3,2,1,0:T(8,128)(2,1)S(1)} %collective-permute-done.8.refs_0_), channel_id=1, source_target_pairs={{4,0},{5,1},{6,2},{7,3},{0,4},{1,5},{2,6},{3,7},{12,8},{13,9},{14,... | collective-permute-start | bytes 393224 | tf_op jit(solution)/shard_map/ppermute | solution.py:20
  29.9 6.9 %collective-permute-start.11 = (bf16[2,4,2,16,256]{4,3,2,1,0:T(8,128)(2,1)S(1)}, bf16[2,4,2,16,256]{4,3,2,1,0:T(8,128)(2,1)S(1)}, u32[]{:S(2)}, u32[]{:S(2)}) collective-permute-start(bf16[2,4,2,16,256]{4,3,2,1,0:T(8,128)(2,1)S(1)} %collective-permute-done.8.refs_0_), channel_id=1, source_target_pairs={{2,0},{3,1},{0,2},{1,3},{6,4},{7,5},{4,6},{5,7},{10,8},{11,9},{8,1... | collective-permute-start | bytes 393224 | tf_op jit(solution)/shard_map/ppermute | solution.py:20
  31.4 5.9 %collective-permute-start.9 = (bf16[2,4,2,16,256]{4,3,2,1,0:T(8,128)(2,1)S(1)}, bf16[2,4,2,16,256]{4,3,2,1,0:T(8,128)(2,1)S(1)}, u32[]{:S(2)}, u32[]{:S(2)}) collective-permute-start(bf16[2,4,2,16,256]{4,3,2,1,0:T(8,128)(2,1)S(1)} %collective-permute-done.8.refs_0_), channel_id=1, source_target_pairs={{6,0},{7,1},{4,2},{5,3},{2,4},{3,5},{0,6},{1,7},{14,8},{15,9},{12,... | collective-permute-start | bytes 393224 | tf_op jit(solution)/shard_map/ppermute | solution.py:20
  33.5 2.0 %collective-permute-start.15 = (bf16[512,512]{1,0:T(8,128)(2,1)S(1)}, bf16[512,512]{1,0:T(8,128)(2,1)S(1)}, u32[]{:S(2)}, u32[]{:S(2)}) collective-permute-start(bf16[512,512]{1,0:T(8,128)(2,1)S(1)} %turn.2.refs_1_), channel_id=1, source_target_pairs={{1,0},{0,1},{3,2},{2,3},{5,4},{4,5},{7,6},{6,7},{9,8},{8,9},{11,10... | collective-permute-start | bytes 1572872 | tf_op jit(solution)/shard_map/ppermute | solution.py:20
  37.5 2.0 %collective-permute-start.16 = (bf16[512,512]{1,0:T(8,128)(2,1)S(1)}, bf16[512,512]{1,0:T(8,128)(2,1)S(1)}, u32[]{:S(2)}, u32[]{:S(2)}) collective-permute-start(bf16[512,512]{1,0:T(8,128)(2,1)S(1)} %turn.3.refs_1_), channel_id=1, source_target_pairs={{1,0},{0,1},{3,2},{2,3},{5,4},{4,5},{7,6},{6,7},{9,8},{8,9},{11,10... | collective-permute-start | bytes 1572872 | tf_op jit(solution)/shard_map/ppermute | solution.py:20

commit v10 on v9

--- a/solution.py
+++ b/solution.py
@@ -9,6 +9,7 @@
 
 VMEM = pl.BlockSpec(memory_space=pltpu.VMEM)
 ANY = pl.BlockSpec(memory_space=pl.ANY)
+ORDER_FLOPS = 2_789_900_000
 
 
 class Grid:
@@ -32,27 +33,30 @@
     return pl.ds(pl.multiple_of(index * width, width), width)
 
 
-def stage_kernel(count, *refs):
-    sources, targets, sems = refs[:count], refs[count : 2 * count], refs[2 * count]
-    copies = [
-        pltpu.make_async_copy(source, target, sems.at[i]) for i, (source, target) in enumerate(zip(sources, targets))
-    ]
+def stage_kernel(pieces, *refs):
+    sources, targets, sems = refs[: len(pieces)], refs[len(pieces) : -1], refs[-1]
+    copies = []
+    for source, target, count in zip(sources, targets, pieces):
+        step = source.shape[0] // count
+        for piece in range(count):
+            part = pl.ds(piece * step, step)
+            copies.append(pltpu.make_async_copy(source.at[part], target.at[part], sems.at[len(copies)]))
     for copy in copies:
         copy.start()
     for copy in copies:
         copy.wait()
 
 
-def stage(*arrays):
+def stage(pieces, *arrays):
     size = sum(a.size * a.dtype.itemsize for a in arrays)
     return pl.pallas_call(
-        functools.partial(stage_kernel, len(arrays)),
+        functools.partial(stage_kernel, pieces),
         out_shape=[pltpu.VMEM(a.shape, a.dtype) for a in arrays],
         in_specs=[ANY] * len(arrays),
         out_specs=[VMEM] * len(arrays),
-        scratch_shapes=[pltpu.SemaphoreType.DMA((len(arrays),))],
+        scratch_shapes=[pltpu.SemaphoreType.DMA((sum(pieces),))],
         compiler_params=pltpu.CompilerParams(vmem_limit_bytes=4 << 20),
-        cost_estimate=pl.CostEstimate(flops=1 << 36, bytes_accessed=2 * size, transcendentals=0),
+        cost_estimate=pl.CostEstimate(flops=ORDER_FLOPS, bytes_accessed=2 * size, transcendentals=0),
         name="stage",
     )(*(pltpu.with_memory_space_constraint(a, pltpu.HBM) for a in arrays))
 
@@ -140,11 +144,15 @@
     row_step, query_step = here_ref.shape[0] // 2, here_ref.shape[1] // 2
     copies = []
     for step in range(4):
+        queries = pl.ds(step % 2 * query_step, query_step)
         rows = pl.ds(step // 2 * row_step, row_step)
-        queries = pl.ds(step % 2 * query_step, query_step)
         here_ref[rows, queries] = products(rows, queries) * scale
-        copies.append(pltpu.make_async_copy(here_ref.at[rows, queries], out_ref.at[rows, queries], sem.at[step]))
-        copies[-1].start()
+        for piece in range(4):
+            part = pl.ds(step // 2 * row_step + piece * row_step // 4, row_step // 4)
+            copies.append(
+                pltpu.make_async_copy(here_ref.at[part, queries], out_ref.at[part, queries], sem.at[len(copies)])
+            )
+            copies[-1].start()
     for copy in copies:
         copy.wait()
 
@@ -160,7 +168,7 @@
         out_shape=jax.ShapeDtypeStruct(shape, jnp.float32) if last else pltpu.VMEM(shape, jnp.float32),
         in_specs=[VMEM] * len(arrays),
         out_specs=ANY if last else VMEM,
-        scratch_shapes=[pltpu.VMEM(shape, jnp.float32), pltpu.SemaphoreType.DMA((4,))] if last else [],
+        scratch_shapes=[pltpu.VMEM(shape, jnp.float32), pltpu.SemaphoreType.DMA((16,))] if last else [],
         input_output_aliases={} if first or last else {2: 0},
         compiler_params=pltpu.CompilerParams(vmem_limit_bytes=24 << 20),
         cost_estimate=pl.CostEstimate(
@@ -177,7 +185,7 @@
     gathered[beside, 0] = grid.swap(queries, beside, 0, 0)
     near_fisher = grid.swap(inverse_fisher, 0, 1, 0)
     gathered[mirror, 0] = grid.swap(queries, mirror, 0, 0)
-    staged = stage(train_feats, queries, inverse_fisher)
+    staged = stage((8, 1, 1), train_feats, queries, inverse_fisher)
     gathered[mirror, 0], gathered[0, 1], staged = lax.optimization_barrier(
         (gathered[mirror, 0], gathered[0, 1], staged)
     )

time: 42.5 us -> 41.4 us (0.974)
  waiting for transfers between devices: 13.1 us -> 12.3 us
  starting transfers between devices: 17.9 us -> 17.3 us
    ppermute x17, waiting for transfers between devices: 13.1 us -> 12.3 us  [swap(): lax.ppermute(block, 'rows', [(row ^ step, row) for row in range(self.far...]
    ppermute x17, starting transfers between devices: 17.9 us -> 17.3 us  [swap(): lax.ppermute(block, 'rows', [(row ^ step, row) for row in range(self.far...]
  transfers between devices with their start and end apart: 17 -> 17, of which waited for: 9 -> 10; matrix products, arithmetic and copies ran while one was open for 0% -> 0% of each run, Pallas kernels for 18% -> 19%
where the time goes in v10:
time: 41.4 us; the launch traced here: 41.2 us
  starting transfers between devices  17.3 us (42%)
  waiting for transfers between devices  12.3 us (30%)
  Pallas kernels  11.5 us (28%)
    ppermute x17, starting transfers between devices, swap(): lax.ppermute(block, 'rows', [(row ^ step, row) for row in range(self.far...  17.3 us
    ppermute x17, waiting for transfers between devices, swap(): lax.ppermute(block, 'rows', [(row ^ step, row) for row in range(self.far...  12.3 us
    pallas_call x4, Pallas kernels, score(): pl.pallas_call(functools.partial(score_kernel, grid, masks, other, first,...  6.98 us
    pallas_call x1, Pallas kernels, stage(): pl.pallas_call(functools.partial(stage_kernel, pieces), out_shape=[pltpu....  3.64 us
  transfers between devices with their start and end apart: 17, of which 10 were waited for; matrix products, arithmetic and copies ran while one was open for 0% of the time, Pallas kernels for 19%

profile of v10, /device:TPU:0, one launch (start us, length us, event | category | flops | bytes accessed | tf_op | source)
XLA Modules:
  0.0 41.2 jit_solution(9178454214394791003)
XLA Ops:
  0.0 5.0 %collective-permute-start = (bf16[2,16,2048]{2,1,0:T(8,128)(2,1)}, bf16[2,16,2048]{2,1,0:T(8,128)(2,1)S(1)}, u32[]{:S(2)}, u32[]{:S(2)}) collective-permute-start(bf16[2,16,2048]{2,1,0:T(8,128)(2,1)} %refs_1_.1), channel_id=1, source_target_pairs={{12,0},{13,1},{14,2},{15,3},{8,4},{9,5},{10,6},{11,7},{4,8},{5,9},... | collective-permute-start | bytes 393224 | tf_op jit(solution)/shard_map/ppermute | solution.py:21
  5.0 1.5 %collective-permute-start.7 = (bf16[1,2048,128]{2,1,0:T(8,128)(2,1)}, bf16[1,2048,128]{2,1,0:T(8,128)(2,1)S(1)}, u32[]{:S(2)}, u32[]{:S(2)}) collective-permute-start(bf16[1,2048,128]{2,1,0:T(8,128)(2,1)} %refs_2_.1), channel_id=1, source_target_pairs={{2,0},{3,1},{0,2},{1,3},{6,4},{7,5},{4,6},{5,7},{10,8},{11,9},{8,1... | collective-permute-start | bytes 1572872 | tf_op jit(solution)/shard_map/ppermute | solution.py:21
  6.6 3.6 %stage.1 = (bf16[2048,2048]{1,0:T(8,128)(2,1)S(1)}, bf16[2,16,2048]{2,1,0:T(8,128)(2,1)S(1)}, bf16[1,2048,128]{2,1,0:T(8,128)(2,1)S(1)}) custom-call(bf16[2048,2048]{1,0:T(8,128)(2,1)} %refs_0_.1, bf16[2,16,2048]{2,1,0:T(8,128)(2,1)} %refs_1_.1, bf16[1,2048,128]{2,1,0:T(8,128)(2,1)} %refs_2_.1), custom_call_target="tpu_custom_call" | custom-call | flops 2789900032 | bytes 18087936 | tf_op jit(solution)/shard_map/stage/pallas_call | solution.py:52
  10.2 0.0 collective-permute-done.refs_3_
  10.2 2.1 %collective-permute-start.3 = (bf16[2,16,2048]{2,1,0:T(8,128)(2,1)S(1)}, bf16[2,16,2048]{2,1,0:T(8,128)(2,1)S(1)}, u32[]{:S(2)}, u32[]{:S(2)}) collective-permute-start(bf16[2,16,2048]{2,1,0:T(8,128)(2,1)S(1)} %collective-permute-done.refs_3_), channel_id=1, source_target_pairs={{4,0},{5,1},{6,2},{7,3},{0,4},{1,5},{2,6},{3,7},{12,8},{13,9},{14,... | collective-permute-start | bytes 393224 | tf_op jit(solution)/shard_map/ppermute | solution.py:21
  12.3 0.4 collective-permute-done.2.refs_2_
  12.7 0.2 collective-permute-start.4
  12.8 3.4 %collective-permute-done.3.refs_4_ = bf16[2,16,2048]{2,1,0:T(8,128)(2,1)S(1)} collective-permute-done((bf16[2,16,2048]{2,1,0:T(8,128)(2,1)S(1)}, bf16[2,16,2048]{2,1,0:T(8,128)(2,1)S(1)}, u32[]{:S(2)}, u32[]{:S(2)}) %collective-permute-start.3) | collective-permute-done | bytes 131104 | tf_op jit(solution)/shard_map/ppermute | solution.py:21
  16.2 1.3 %collective-permute-done.6.refs_7_ = bf16[2,16,2048]{2,1,0:T(8,128)(2,1)S(1)} collective-permute-done((bf16[2,16,2048]{2,1,0:T(8,128)(2,1)S(1)}, bf16[2,16,2048]{2,1,0:T(8,128)(2,1)S(1)}, u32[]{:S(2)}, u32[]{:S(2)}) %collective-permute-start.6) | collective-permute-done | bytes 131104 | tf_op jit(solution)/shard_map/ppermute | solution.py:21
  17.6 1.1 %collective-permute-done.7.refs_9_ = bf16[1,2048,128]{2,1,0:T(8,128)(2,1)S(1)} collective-permute-done((bf16[1,2048,128]{2,1,0:T(8,128)(2,1)}, bf16[1,2048,128]{2,1,0:T(8,128)(2,1)S(1)}, u32[]{:S(2)}, u32[]{:S(2)}) %collective-permute-start.7) | collective-permute-done | bytes 524320 | tf_op jit(solution)/shard_map/ppermute | solution.py:21
  18.6 0.4 %condition.1.refs_0_ = bf16[2,4,2,16,256]{4,3,2,1,0:T(8,128)(2,1)S(1)} custom-call(bf16[2,16,2048]{2,1,0:T(8,128)(2,1)S(1)} %get-tuple-element.22.refs_0_, bf16[2,16,2048]{2,1,0:T(8,128)(2,1)S(1)} %collective-permute-done.1.refs_1_, bf16[2,16,2048]{2,1,0:T(8,128)(2,1)S(1)} %collective-permute-done.2.refs_2_, ...), custom_call_target="tpu_custom_call" | custom-call | flops 268435456 | bytes 3145728 | tf_op jit(solution)/shard_map/condition/pallas_call | solution.py:84
  19.1 0.7 %collective-permute-start.13 = (bf16[2,4,2,16,256]{4,3,2,1,0:T(8,128)(2,1)S(1)}, bf16[2,4,2,16,256]{4,3,2,1,0:T(8,128)(2,1)S(1)}, u32[]{:S(2)}, u32[]{:S(2)}) collective-permute-start(bf16[2,4,2,16,256]{4,3,2,1,0:T(8,128)(2,1)S(1)} %condition.1.refs_0_), channel_id=1, source_target_pairs={{4,0},{5,1},{6,2},{7,3},{0,4},{1,5},{2,6},{3,7},{12,8},{13,9},{14,... | collective-permute-start | bytes 393224 | tf_op jit(solution)/shard_map/ppermute | solution.py:21
  19.8 0.8 %collective-permute-start.8 = (bf16[2,4,2,16,256]{4,3,2,1,0:T(8,128)(2,1)S(1)}, bf16[2,4,2,16,256]{4,3,2,1,0:T(8,128)(2,1)S(1)}, u32[]{:S(2)}, u32[]{:S(2)}) collective-permute-start(bf16[2,4,2,16,256]{4,3,2,1,0:T(8,128)(2,1)S(1)} %condition.1.refs_0_), channel_id=1, source_target_pairs={{12,0},{13,1},{14,2},{15,3},{8,4},{9,5},{10,6},{11,7},{4,8},{5,9},... | collective-permute-start | bytes 393224 | tf_op jit(solution)/shard_map/ppermute | solution.py:21
  20.6 1.3 %collective-permute-start.12 = (bf16[2,4,2,16,256]{4,3,2,1,0:T(8,128)(2,1)S(1)}, bf16[2,4,2,16,256]{4,3,2,1,0:T(8,128)(2,1)S(1)}, u32[]{:S(2)}, u32[]{:S(2)}) collective-permute-start(bf16[2,4,2,16,256]{4,3,2,1,0:T(8,128)(2,1)S(1)} %condition.1.refs_0_), channel_id=1, source_target_pairs={{2,0},{3,1},{0,2},{1,3},{6,4},{7,5},{4,6},{5,7},{10,8},{11,9},{8,1... | collective-permute-start | bytes 393224 | tf_op jit(solution)/shard_map/ppermute | solution.py:21
  21.9 2.3 %collective-permute-done.13.refs_2_ = bf16[2,4,2,16,256]{4,3,2,1,0:T(8,128)(2,1)S(1)} collective-permute-done((bf16[2,4,2,16,256]{4,3,2,1,0:T(8,128)(2,1)S(1)}, bf16[2,4,2,16,256]{4,3,2,1,0:T(8,128)(2,1)S(1)}, u32[]{:S(2)}, u32[]{:S(2)}) %collective-permute-start.13) | collective-permute-done | bytes 131104 | tf_op jit(solution)/shard_map/ppermute | solution.py:21
  24.1 2.0 %collective-permute-start.14 = (bf16[2,4,2,16,256]{4,3,2,1,0:T(8,128)(2,1)S(1)}, bf16[2,4,2,16,256]{4,3,2,1,0:T(8,128)(2,1)S(1)}, u32[]{:S(2)}, u32[]{:S(2)}) collective-permute-start(bf16[2,4,2,16,256]{4,3,2,1,0:T(8,128)(2,1)S(1)} %collective-permute-done.13.refs_2_), channel_id=1, source_target_pairs={{2,0},{3,1},{0,2},{1,3},{6,4},{7,5},{4,6},{5,7},{10,8},{11,9},{8,1... | collective-permute-start | bytes 393224 | tf_op jit(solution)/shard_map/ppermute | solution.py:21
  26.2 0.8 %collective-permute-done.8.refs_0_ = bf16[2,4,2,16,256]{4,3,2,1,0:T(8,128)(2,1)S(1)} collective-permute-done((bf16[2,4,2,16,256]{4,3,2,1,0:T(8,128)(2,1)S(1)}, bf16[2,4,2,16,256]{4,3,2,1,0:T(8,128)(2,1)S(1)}, u32[]{:S(2)}, u32[]{:S(2)}) %collective-permute-start.8) | collective-permute-done | bytes 131104 | tf_op jit(solution)/shard_map/ppermute | solution.py:21
  27.0 1.9 %collective-permute-start.10 = (bf16[2,4,2,16,256]{4,3,2,1,0:T(8,128)(2,1)S(1)}, bf16[2,4,2,16,256]{4,3,2,1,0:T(8,128)(2,1)S(1)}, u32[]{:S(2)}, u32[]{:S(2)}) collective-permute-start(bf16[2,4,2,16,256]{4,3,2,1,0:T(8,128)(2,1)S(1)} %collective-permute-done.8.refs_0_), channel_id=1, source_target_pairs={{4,0},{5,1},{6,2},{7,3},{0,4},{1,5},{2,6},{3,7},{12,8},{13,9},{14,... | collective-permute-start | bytes 393224 | tf_op jit(solution)/shard_map/ppermute | solution.py:21
  28.9 1.3 %collective-permute-start.11 = (bf16[2,4,2,16,256]{4,3,2,1,0:T(8,128)(2,1)S(1)}, bf16[2,4,2,16,256]{4,3,2,1,0:T(8,128)(2,1)S(1)}, u32[]{:S(2)}, u32[]{:S(2)}) collective-permute-start(bf16[2,4,2,16,256]{4,3,2,1,0:T(8,128)(2,1)S(1)} %collective-permute-done.8.refs_0_), channel_id=1, source_target_pairs={{2,0},{3,1},{0,2},{1,3},{6,4},{7,5},{4,6},{5,7},{10,8},{11,9},{8,1... | collective-permute-start | bytes 393224 | tf_op jit(solution)/shard_map/ppermute | solution.py:21
  30.2 0.3 collective-permute-start.9
  30.5 0.2 turn.2.refs_1_
  30.8 0.1 collective-permute-start.15
  30.8 1.3 %score.4.refs_2_ = f32[2048,512]{1,0:T(8,128)S(1)} custom-call(bf16[2048,2048]{1,0:T(8,128)(2,1)S(1)} %get-tuple-element.21.refs_0_, bf16[512,512]{1,0:T(8,128)(2,1)S(1)} %turn.2.refs_1_), custom_call_target="tpu_custom_call" | custom-call | flops 21474836480 | bytes 4194304 | tf_op jit(solution)/shard_map/score/pallas_call | solution.py:166
  32.1 0.6 %collective-permute-done.15.refs_1_ = bf16[512,512]{1,0:T(8,128)(2,1)S(1)} collective-permute-done((bf16[512,512]{1,0:T(8,128)(2,1)S(1)}, bf16[512,512]{1,0:T(8,128)(2,1)S(1)}, u32[]{:S(2)}, u32[]{:S(2)}) %collective-permute-start.15) | collective-permute-done | bytes 524320 | tf_op jit(solution)/shard_map/ppermute | solution.py:21
  32.7 1.4 %score.5.refs_2_ = f32[2048,512]{1,0:T(8,128)S(1)} custom-call(bf16[2048,2048]{1,0:T(8,128)(2,1)S(1)} %get-tuple-element.21.refs_0_, bf16[512,512]{1,0:T(8,128)(2,1)S(1)} %collective-permute-done.15.refs_1_, f32[2048,512]{1,0:T(8,128)S(1)} %score.4.refs_2_), custom_call_target="tpu_custom_call", output_to_operand_aliasing={{}: (2, {})} | custom-call | flops 1073741824 | bytes 4194304 | tf_op jit(solution)/shard_map/score/pallas_call | solution.py:166
  34.2 0.6 %collective-permute-done.11.refs_1_ = bf16[2,4,2,16,256]{4,3,2,1,0:T(8,128)(2,1)S(1)} collective-permute-done((bf16[2,4,2,16,256]{4,3,2,1,0:T(8,128)(2,1)S(1)}, bf16[2,4,2,16,256]{4,3,2,1,0:T(8,128)(2,1)S(1)}, u32[]{:S(2)}, u32[]{:S(2)}) %collective-permute-start.11) | collective-permute-done | bytes 131104 | tf_op jit(solution)/shard_map/ppermute | solution.py:21
  34.7 1.4 %collective-permute-done.9.refs_3_ = bf16[2,4,2,16,256]{4,3,2,1,0:T(8,128)(2,1)S(1)} collective-permute-done((bf16[2,4,2,16,256]{4,3,2,1,0:T(8,128)(2,1)S(1)}, bf16[2,4,2,16,256]{4,3,2,1,0:T(8,128)(2,1)S(1)}, u32[]{:S(2)}, u32[]{:S(2)}) %collective-permute-start.9) | collective-permute-done | bytes 131104 | tf_op jit(solution)/shard_map/ppermute | solution.py:21
  36.1 0.2 turn.3.refs_1_
  36.4 0.1 collective-permute-start.16
  36.5 1.4 %score.6.refs_2_ = f32[2048,512]{1,0:T(8,128)S(1)} custom-call(bf16[2048,2048]{1,0:T(8,128)(2,1)S(1)} %get-tuple-element.21.refs_0_, bf16[512,512]{1,0:T(8,128)(2,1)S(1)} %turn.3.refs_1_, f32[2048,512]{1,0:T(8,128)S(1)} %score.5.refs_2_), custom_call_target="tpu_custom_call", output_to_operand_aliasing={{}: (2, {})} | custom-call | flops 1073741824 | bytes 4194304 | tf_op jit(solution)/shard_map/score/pallas_call | solution.py:166
  37.9 0.5 %collective-permute-done.16.refs_1_ = bf16[512,512]{1,0:T(8,128)(2,1)S(1)} collective-permute-done((bf16[512,512]{1,0:T(8,128)(2,1)S(1)}, bf16[512,512]{1,0:T(8,128)(2,1)S(1)}, u32[]{:S(2)}, u32[]{:S(2)}) %collective-permute-start.16) | collective-permute-done | bytes 524320 | tf_op jit(solution)/shard_map/ppermute | solution.py:21
  38.3 2.9 %score.7 = f32[2048,512]{1,0:T(8,128)} custom-call(bf16[2048,2048]{1,0:T(8,128)(2,1)S(1)} %get-tuple-element.21.refs_0_, bf16[512,512]{1,0:T(8,128)(2,1)S(1)} %collective-permute-done.16.refs_1_, f32[2048,512]{1,0:T(8,128)S(1)} %score.6.refs_2_), custom_call_target="tpu_custom_call" | custom-call | flops 1073741824 | bytes 4194304 | tf_op jit(solution)/shard_map/score/pallas_call | solution.py:166
  (10 shorter events, 0.0 us)
Async XLA Ops:
  0.0 10.2 %collective-permute-start = (bf16[2,16,2048]{2,1,0:T(8,128)(2,1)}, bf16[2,16,2048]{2,1,0:T(8,128)(2,1)S(1)}, u32[]{:S(2)}, u32[]{:S(2)}) collective-permute-start(bf16[2,16,2048]{2,1,0:T(8,128)(2,1)} %refs_1_.1), channel_id=1, source_target_pairs={{12,0},{13,1},{14,2},{15,3},{8,4},{9,5},{10,6},{11,7},{4,8},{5,9},... | collective-permute-start | bytes 393224 | tf_op jit(solution)/shard_map/ppermute | solution.py:21
  5.0 13.6 %collective-permute-start.7 = (bf16[1,2048,128]{2,1,0:T(8,128)(2,1)}, bf16[1,2048,128]{2,1,0:T(8,128)(2,1)S(1)}, u32[]{:S(2)}, u32[]{:S(2)}) collective-permute-start(bf16[1,2048,128]{2,1,0:T(8,128)(2,1)} %refs_2_.1), channel_id=1, source_target_pairs={{2,0},{3,1},{0,2},{1,3},{6,4},{7,5},{4,6},{5,7},{10,8},{11,9},{8,1... | collective-permute-start | bytes 1572872 | tf_op jit(solution)/shard_map/ppermute | solution.py:21
  6.6 3.7 %collective-permute-start.1 = (bf16[2,16,2048]{2,1,0:T(8,128)(2,1)}, bf16[2,16,2048]{2,1,0:T(8,128)(2,1)S(1)}, u32[]{:S(2)}, u32[]{:S(2)}) collective-permute-start(bf16[2,16,2048]{2,1,0:T(8,128)(2,1)} %refs_1_.1), channel_id=1, source_target_pairs={{1,0},{0,1},{3,2},{2,3},{5,4},{4,5},{7,6},{6,7},{9,8},{8,9},{11,10... | collective-permute-start | bytes 393224 | tf_op jit(solution)/shard_map/ppermute | solution.py:21
  6.6 6.1 %collective-permute-start.2 = (bf16[2,16,2048]{2,1,0:T(8,128)(2,1)}, bf16[2,16,2048]{2,1,0:T(8,128)(2,1)S(1)}, u32[]{:S(2)}, u32[]{:S(2)}) collective-permute-start(bf16[2,16,2048]{2,1,0:T(8,128)(2,1)} %refs_1_.1), channel_id=1, source_target_pairs={{4,0},{5,1},{6,2},{7,3},{0,4},{1,5},{2,6},{3,7},{12,8},{13,9},{14,... | collective-permute-start | bytes 393224 | tf_op jit(solution)/shard_map/ppermute | solution.py:21
  10.2 6.0 %collective-permute-start.3 = (bf16[2,16,2048]{2,1,0:T(8,128)(2,1)S(1)}, bf16[2,16,2048]{2,1,0:T(8,128)(2,1)S(1)}, u32[]{:S(2)}, u32[]{:S(2)}) collective-permute-start(bf16[2,16,2048]{2,1,0:T(8,128)(2,1)S(1)} %collective-permute-done.refs_3_), channel_id=1, source_target_pairs={{4,0},{5,1},{6,2},{7,3},{0,4},{1,5},{2,6},{3,7},{12,8},{13,9},{14,... | collective-permute-start | bytes 393224 | tf_op jit(solution)/shard_map/ppermute | solution.py:21
  12.3 3.9 %collective-permute-start.5 = (bf16[2,16,2048]{2,1,0:T(8,128)(2,1)S(1)}, bf16[2,16,2048]{2,1,0:T(8,128)(2,1)S(1)}, u32[]{:S(2)}, u32[]{:S(2)}) collective-permute-start(bf16[2,16,2048]{2,1,0:T(8,128)(2,1)S(1)} %collective-permute-done.refs_3_), channel_id=1, source_target_pairs={{1,0},{0,1},{3,2},{2,3},{5,4},{4,5},{7,6},{6,7},{9,8},{8,9},{11,10... | collective-permute-start | bytes 393224 | tf_op jit(solution)/shard_map/ppermute | solution.py:21
  12.7 3.5 %collective-permute-start.4 = (bf16[2,16,2048]{2,1,0:T(8,128)(2,1)S(1)}, bf16[2,16,2048]{2,1,0:T(8,128)(2,1)S(1)}, u32[]{:S(2)}, u32[]{:S(2)}) collective-permute-start(bf16[2,16,2048]{2,1,0:T(8,128)(2,1)S(1)} %collective-permute-done.2.refs_2_), channel_id=1, source_target_pairs={{1,0},{0,1},{3,2},{2,3},{5,4},{4,5},{7,6},{6,7},{9,8},{8,9},{11,10... | collective-permute-start | bytes 393224 | tf_op jit(solution)/shard_map/ppermute | solution.py:21
  16.2 1.3 %collective-permute-start.6 = (bf16[2,16,2048]{2,1,0:T(8,128)(2,1)S(1)}, bf16[2,16,2048]{2,1,0:T(8,128)(2,1)S(1)}, u32[]{:S(2)}, u32[]{:S(2)}) collective-permute-start(bf16[2,16,2048]{2,1,0:T(8,128)(2,1)S(1)} %collective-permute-done.3.refs_4_), channel_id=1, source_target_pairs={{1,0},{0,1},{3,2},{2,3},{5,4},{4,5},{7,6},{6,7},{9,8},{8,9},{11,10... | collective-permute-start | bytes 393224 | tf_op jit(solution)/shard_map/ppermute | solution.py:21
  19.1 5.0 %collective-permute-start.13 = (bf16[2,4,2,16,256]{4,3,2,1,0:T(8,128)(2,1)S(1)}, bf16[2,4,2,16,256]{4,3,2,1,0:T(8,128)(2,1)S(1)}, u32[]{:S(2)}, u32[]{:S(2)}) collective-permute-start(bf16[2,4,2,16,256]{4,3,2,1,0:T(8,128)(2,1)S(1)} %condition.1.refs_0_), channel_id=1, source_target_pairs={{4,0},{5,1},{6,2},{7,3},{0,4},{1,5},{2,6},{3,7},{12,8},{13,9},{14,... | collective-permute-start | bytes 393224 | tf_op jit(solution)/shard_map/ppermute | solution.py:21
  19.8 7.2 %collective-permute-start.8 = (bf16[2,4,2,16,256]{4,3,2,1,0:T(8,128)(2,1)S(1)}, bf16[2,4,2,16,256]{4,3,2,1,0:T(8,128)(2,1)S(1)}, u32[]{:S(2)}, u32[]{:S(2)}) collective-permute-start(bf16[2,4,2,16,256]{4,3,2,1,0:T(8,128)(2,1)S(1)} %condition.1.refs_0_), channel_id=1, source_target_pairs={{12,0},{13,1},{14,2},{15,3},{8,4},{9,5},{10,6},{11,7},{4,8},{5,9},... | collective-permute-start | bytes 393224 | tf_op jit(solution)/shard_map/ppermute | solution.py:21
  20.6 9.9 %collective-permute-start.12 = (bf16[2,4,2,16,256]{4,3,2,1,0:T(8,128)(2,1)S(1)}, bf16[2,4,2,16,256]{4,3,2,1,0:T(8,128)(2,1)S(1)}, u32[]{:S(2)}, u32[]{:S(2)}) collective-permute-start(bf16[2,4,2,16,256]{4,3,2,1,0:T(8,128)(2,1)S(1)} %condition.1.refs_0_), channel_id=1, source_target_pairs={{2,0},{3,1},{0,2},{1,3},{6,4},{7,5},{4,6},{5,7},{10,8},{11,9},{8,1... | collective-permute-start | bytes 393224 | tf_op jit(solution)/shard_map/ppermute | solution.py:21
  24.1 6.4 %collective-permute-start.14 = (bf16[2,4,2,16,256]{4,3,2,1,0:T(8,128)(2,1)S(1)}, bf16[2,4,2,16,256]{4,3,2,1,0:T(8,128)(2,1)S(1)}, u32[]{:S(2)}, u32[]{:S(2)}) collective-permute-start(bf16[2,4,2,16,256]{4,3,2,1,0:T(8,128)(2,1)S(1)} %collective-permute-done.13.refs_2_), channel_id=1, source_target_pairs={{2,0},{3,1},{0,2},{1,3},{6,4},{7,5},{4,6},{5,7},{10,8},{11,9},{8,1... | collective-permute-start | bytes 393224 | tf_op jit(solution)/shard_map/ppermute | solution.py:21
  27.0 7.1 %collective-permute-start.10 = (bf16[2,4,2,16,256]{4,3,2,1,0:T(8,128)(2,1)S(1)}, bf16[2,4,2,16,256]{4,3,2,1,0:T(8,128)(2,1)S(1)}, u32[]{:S(2)}, u32[]{:S(2)}) collective-permute-start(bf16[2,4,2,16,256]{4,3,2,1,0:T(8,128)(2,1)S(1)} %collective-permute-done.8.refs_0_), channel_id=1, source_target_pairs={{4,0},{5,1},{6,2},{7,3},{0,4},{1,5},{2,6},{3,7},{12,8},{13,9},{14,... | collective-permute-start | bytes 393224 | tf_op jit(solution)/shard_map/ppermute | solution.py:21
  28.9 5.8 %collective-permute-start.11 = (bf16[2,4,2,16,256]{4,3,2,1,0:T(8,128)(2,1)S(1)}, bf16[2,4,2,16,256]{4,3,2,1,0:T(8,128)(2,1)S(1)}, u32[]{:S(2)}, u32[]{:S(2)}) collective-permute-start(bf16[2,4,2,16,256]{4,3,2,1,0:T(8,128)(2,1)S(1)} %collective-permute-done.8.refs_0_), channel_id=1, source_target_pairs={{2,0},{3,1},{0,2},{1,3},{6,4},{7,5},{4,6},{5,7},{10,8},{11,9},{8,1... | collective-permute-start | bytes 393224 | tf_op jit(solution)/shard_map/ppermute | solution.py:21
  30.2 6.0 %collective-permute-start.9 = (bf16[2,4,2,16,256]{4,3,2,1,0:T(8,128)(2,1)S(1)}, bf16[2,4,2,16,256]{4,3,2,1,0:T(8,128)(2,1)S(1)}, u32[]{:S(2)}, u32[]{:S(2)}) collective-permute-start(bf16[2,4,2,16,256]{4,3,2,1,0:T(8,128)(2,1)S(1)} %collective-permute-done.8.refs_0_), channel_id=1, source_target_pairs={{6,0},{7,1},{4,2},{5,3},{2,4},{3,5},{0,6},{1,7},{14,8},{15,9},{12,... | collective-permute-start | bytes 393224 | tf_op jit(solution)/shard_map/ppermute | solution.py:21
  30.8 2.0 %collective-permute-start.15 = (bf16[512,512]{1,0:T(8,128)(2,1)S(1)}, bf16[512,512]{1,0:T(8,128)(2,1)S(1)}, u32[]{:S(2)}, u32[]{:S(2)}) collective-permute-start(bf16[512,512]{1,0:T(8,128)(2,1)S(1)} %turn.2.refs_1_), channel_id=1, source_target_pairs={{1,0},{0,1},{3,2},{2,3},{5,4},{4,5},{7,6},{6,7},{9,8},{8,9},{11,10... | collective-permute-start | bytes 1572872 | tf_op jit(solution)/shard_map/ppermute | solution.py:21
  36.4 2.0 %collective-permute-start.16 = (bf16[512,512]{1,0:T(8,128)(2,1)S(1)}, bf16[512,512]{1,0:T(8,128)(2,1)S(1)}, u32[]{:S(2)}, u32[]{:S(2)}) collective-permute-start(bf16[512,512]{1,0:T(8,128)(2,1)S(1)} %turn.3.refs_1_), channel_id=1, source_target_pairs={{1,0},{0,1},{3,2},{2,3},{5,4},{4,5},{7,6},{6,7},{9,8},{8,9},{11,10... | collective-permute-start | bytes 1572872 | tf_op jit(solution)/shard_map/ppermute | solution.py:21

commit v11 on v9

--- a/solution.py
+++ b/solution.py
@@ -9,6 +9,7 @@
 
 VMEM = pl.BlockSpec(memory_space=pltpu.VMEM)
 ANY = pl.BlockSpec(memory_space=pl.ANY)
+ORDER_FLOPS = 2_788_300_000
 
 
 class Grid:
@@ -32,29 +33,39 @@
     return pl.ds(pl.multiple_of(index * width, width), width)
 
 
-def stage_kernel(count, *refs):
-    sources, targets, sems = refs[:count], refs[count : 2 * count], refs[2 * count]
-    copies = [
-        pltpu.make_async_copy(source, target, sems.at[i]) for i, (source, target) in enumerate(zip(sources, targets))
-    ]
+def stage_kernel(first, half, *refs):
+    sources, targets, sems = refs[: len(refs) // 2], refs[len(refs) // 2 : -1], refs[-1]
+    if not first:
+        sources = sources[1:]
+    part = pl.ds(0 if first else half, half)
+    copies = [pltpu.make_async_copy(sources[0].at[part], targets[0].at[part], sems.at[0])]
+    for index in range(1, len(sources)):
+        copies.append(pltpu.make_async_copy(sources[index], targets[index], sems.at[index]))
     for copy in copies:
         copy.start()
     for copy in copies:
         copy.wait()
 
 
-def stage(*arrays):
-    size = sum(a.size * a.dtype.itemsize for a in arrays)
-    return pl.pallas_call(
-        functools.partial(stage_kernel, len(arrays)),
+def stage(arrays, buffer=None):
+    first = buffer is None
+    moved = sum(a.size * a.dtype.itemsize for a in arrays)
+    sources = [pltpu.with_memory_space_constraint(a, pltpu.HBM) for a in arrays]
+    if not first:
+        sources.insert(0, pltpu.with_memory_space_constraint(buffer, pltpu.VMEM))
+    return pl.pallas_call(
+        functools.partial(stage_kernel, first, arrays[0].shape[0] // 2),
         out_shape=[pltpu.VMEM(a.shape, a.dtype) for a in arrays],
-        in_specs=[ANY] * len(arrays),
+        in_specs=[ANY] * len(arrays) if first else [VMEM, ANY],
         out_specs=[VMEM] * len(arrays),
         scratch_shapes=[pltpu.SemaphoreType.DMA((len(arrays),))],
+        input_output_aliases={} if first else {0: 0},
         compiler_params=pltpu.CompilerParams(vmem_limit_bytes=4 << 20),
-        cost_estimate=pl.CostEstimate(flops=1 << 36, bytes_accessed=2 * size, transcendentals=0),
+        cost_estimate=pl.CostEstimate(
+            flops=ORDER_FLOPS if first else 1, bytes_accessed=moved, transcendentals=0
+        ),
         name="stage",
-    )(*(pltpu.with_memory_space_constraint(a, pltpu.HBM) for a in arrays))
+    )(*sources)
 
 
 def condition_kernel(grid, places, *refs):
@@ -140,8 +151,8 @@
     row_step, query_step = here_ref.shape[0] // 2, here_ref.shape[1] // 2
     copies = []
     for step in range(4):
+        queries = pl.ds(step % 2 * query_step, query_step)
         rows = pl.ds(step // 2 * row_step, row_step)
-        queries = pl.ds(step % 2 * query_step, query_step)
         here_ref[rows, queries] = products(rows, queries) * scale
         copies.append(pltpu.make_async_copy(here_ref.at[rows, queries], out_ref.at[rows, queries], sem.at[step]))
         copies[-1].start()
@@ -177,14 +188,17 @@
     gathered[beside, 0] = grid.swap(queries, beside, 0, 0)
     near_fisher = grid.swap(inverse_fisher, 0, 1, 0)
     gathered[mirror, 0] = grid.swap(queries, mirror, 0, 0)
-    staged = stage(train_feats, queries, inverse_fisher)
+    staged = stage([train_feats, queries, inverse_fisher])
     gathered[mirror, 0], gathered[0, 1], staged = lax.optimization_barrier(
         (gathered[mirror, 0], gathered[0, 1], staged)
     )
     train_here, gathered[0, 0], fisher_here = staged
     gathered[relayed, 0] = grid.swap(gathered[mirror, 0], beside, 0, 0)
-    for mask in (beside, mirror, relayed):
+    (train_here,) = stage([train_feats], train_here)
+    for mask in (beside, mirror):
         gathered[mask, 1] = grid.swap(gathered[mask, 0], 0, 0, 1)
+    gathered[relayed, 0], train_here = lax.optimization_barrier((gathered[relayed, 0], train_here))
+    gathered[relayed, 1] = grid.swap(gathered[relayed, 0], 0, 0, 1)
 
     own, near_one, far_one, far_three = (0, 0), (0, 1), (beside, 0), (mirror, 0)
     parts = {own: condition(grid, gathered, fisher_here, near_fisher)}

time: 42.5 us -> 41.2 us (0.969)
  waiting for transfers between devices: 13.1 us -> 11.4 us
  Pallas kernels: 11.3 us -> 12.3 us
  starting transfers between devices: 17.9 us -> 17.1 us
    ppermute x17, waiting for transfers between devices: 13.1 us -> 11.4 us  [swap(): lax.ppermute(block, 'rows', [(row ^ step, row) for row in range(self.far...]
    pallas_call x1 -> x2, Pallas kernels: 3.49 us -> 4.56 us  [stage(): pl.pallas_call(functools.partial(stage_kernel, first, arrays[0].shape[0]...]
    ppermute x17, starting transfers between devices: 17.9 us -> 17.1 us  [swap(): lax.ppermute(block, 'rows', [(row ^ step, row) for row in range(self.far...]
  transfers between devices with their start and end apart: 17 -> 17, of which waited for: 9 -> 9; matrix products, arithmetic and copies ran while one was open for 0% -> 0% of each run, Pallas kernels for 18% -> 22%
where the time goes in v11:
time: 41.2 us; the launch traced here: 41.1 us
  starting transfers between devices  17.1 us (42%)
  Pallas kernels  12.3 us (30%)
  waiting for transfers between devices  11.4 us (28%)
    ppermute x17, starting transfers between devices, swap(): lax.ppermute(block, 'rows', [(row ^ step, row) for row in range(self.far...  17.1 us
    ppermute x17, waiting for transfers between devices, swap(): lax.ppermute(block, 'rows', [(row ^ step, row) for row in range(self.far...  11.4 us
    pallas_call x4, Pallas kernels, score(): pl.pallas_call(functools.partial(score_kernel, grid, masks, other, first,...  6.88 us
    pallas_call x2, Pallas kernels, stage(): pl.pallas_call(functools.partial(stage_kernel, first, arrays[0].shape[0]...  4.56 us
  transfers between devices with their start and end apart: 17, of which 9 were waited for; matrix products, arithmetic and copies ran while one was open for 0% of the time, Pallas kernels for 22%

profile of v11, /device:TPU:0, one launch (start us, length us, event | category | flops | bytes accessed | tf_op | source)
XLA Modules:
  0.0 41.1 jit_solution(12300323052133164222)
XLA Ops:
  0.0 5.0 %collective-permute-start = (bf16[2,16,2048]{2,1,0:T(8,128)(2,1)}, bf16[2,16,2048]{2,1,0:T(8,128)(2,1)S(1)}, u32[]{:S(2)}, u32[]{:S(2)}) collective-permute-start(bf16[2,16,2048]{2,1,0:T(8,128)(2,1)} %refs_1_.2), channel_id=1, source_target_pairs={{12,0},{13,1},{14,2},{15,3},{8,4},{9,5},{10,6},{11,7},{4,8},{5,9},... | collective-permute-start | bytes 393224 | tf_op jit(solution)/shard_map/ppermute | solution.py:21
  5.0 1.5 %collective-permute-start.7 = (bf16[1,2048,128]{2,1,0:T(8,128)(2,1)}, bf16[1,2048,128]{2,1,0:T(8,128)(2,1)S(1)}, u32[]{:S(2)}, u32[]{:S(2)}) collective-permute-start(bf16[1,2048,128]{2,1,0:T(8,128)(2,1)} %refs_2_.1), channel_id=1, source_target_pairs={{2,0},{3,1},{0,2},{1,3},{6,4},{7,5},{4,6},{5,7},{10,8},{11,9},{8,1... | collective-permute-start | bytes 1572872 | tf_op jit(solution)/shard_map/ppermute | solution.py:21
  6.6 0.0 collective-permute-start.3
  6.6 2.4 %stage.2 = (bf16[2048,2048]{1,0:T(8,128)(2,1)S(1)}, bf16[2,16,2048]{2,1,0:T(8,128)(2,1)S(1)}, bf16[1,2048,128]{2,1,0:T(8,128)(2,1)S(1)}) custom-call(bf16[2048,2048]{1,0:T(8,128)(2,1)} %refs_1_.3, bf16[2,16,2048]{2,1,0:T(8,128)(2,1)} %refs_1_.2, bf16[1,2048,128]{2,1,0:T(8,128)(2,1)} %refs_2_.1), custom_call_target="tpu_custom_call" | custom-call | flops 2788300032 | bytes 9043968 | tf_op jit(solution)/shard_map/stage/pallas_call | solution.py:56
  9.0 2.3 %collective-permute-start.2 = (bf16[2,16,2048]{2,1,0:T(8,128)(2,1)S(1)}, bf16[2,16,2048]{2,1,0:T(8,128)(2,1)S(1)}, u32[]{:S(2)}, u32[]{:S(2)}) collective-permute-start(bf16[2,16,2048]{2,1,0:T(8,128)(2,1)S(1)} %collective-permute-done.refs_3_), channel_id=1, source_target_pairs={{4,0},{5,1},{6,2},{7,3},{0,4},{1,5},{2,6},{3,7},{12,8},{13,9},{14,... | collective-permute-start | bytes 393224 | tf_op jit(solution)/shard_map/ppermute | solution.py:21
  11.3 2.2 %stage.3.refs_0_ = bf16[2048,2048]{1,0:T(8,128)(2,1)S(1)} custom-call(bf16[2048,2048]{1,0:T(8,128)(2,1)S(1)} %get-tuple-element.24.refs_0_, bf16[2048,2048]{1,0:T(8,128)(2,1)} %refs_1_.3), custom_call_target="tpu_custom_call", output_to_operand_aliasing={{}: (0, {})} | custom-call | flops 1 | bytes 8388608 | tf_op jit(solution)/shard_map/stage/pallas_call | solution.py:56
  13.5 0.6 %collective-permute-start.4 = (bf16[2,16,2048]{2,1,0:T(8,128)(2,1)S(1)}, bf16[2,16,2048]{2,1,0:T(8,128)(2,1)S(1)}, u32[]{:S(2)}, u32[]{:S(2)}) collective-permute-start(bf16[2,16,2048]{2,1,0:T(8,128)(2,1)S(1)} %collective-permute-done.3.refs_2_), channel_id=1, source_target_pairs={{1,0},{0,1},{3,2},{2,3},{5,4},{4,5},{7,6},{6,7},{9,8},{8,9},{11,10... | collective-permute-start | bytes 393224 | tf_op jit(solution)/shard_map/ppermute | solution.py:21
  14.1 1.4 %collective-permute-done.2.refs_4_ = bf16[2,16,2048]{2,1,0:T(8,128)(2,1)S(1)} collective-permute-done((bf16[2,16,2048]{2,1,0:T(8,128)(2,1)S(1)}, bf16[2,16,2048]{2,1,0:T(8,128)(2,1)S(1)}, u32[]{:S(2)}, u32[]{:S(2)}) %collective-permute-start.2) | collective-permute-done | bytes 131104 | tf_op jit(solution)/shard_map/ppermute | solution.py:21
  15.5 1.3 %collective-permute-done.6.refs_7_ = bf16[2,16,2048]{2,1,0:T(8,128)(2,1)S(1)} collective-permute-done((bf16[2,16,2048]{2,1,0:T(8,128)(2,1)S(1)}, bf16[2,16,2048]{2,1,0:T(8,128)(2,1)S(1)}, u32[]{:S(2)}, u32[]{:S(2)}) %collective-permute-start.6) | collective-permute-done | bytes 131104 | tf_op jit(solution)/shard_map/ppermute | solution.py:21
  16.9 1.8 %collective-permute-done.7.refs_9_ = bf16[1,2048,128]{2,1,0:T(8,128)(2,1)S(1)} collective-permute-done((bf16[1,2048,128]{2,1,0:T(8,128)(2,1)}, bf16[1,2048,128]{2,1,0:T(8,128)(2,1)S(1)}, u32[]{:S(2)}, u32[]{:S(2)}) %collective-permute-start.7) | collective-permute-done | bytes 524320 | tf_op jit(solution)/shard_map/ppermute | solution.py:21
  18.6 0.4 %condition.1.refs_0_ = bf16[2,4,2,16,256]{4,3,2,1,0:T(8,128)(2,1)S(1)} custom-call(bf16[2,16,2048]{2,1,0:T(8,128)(2,1)S(1)} %get-tuple-element.26.refs_0_, bf16[2,16,2048]{2,1,0:T(8,128)(2,1)S(1)} %collective-permute-done.1.refs_1_, bf16[2,16,2048]{2,1,0:T(8,128)(2,1)S(1)} %collective-permute-done.3.refs_2_, ...), custom_call_target="tpu_custom_call" | custom-call | flops 268435456 | bytes 3145728 | tf_op jit(solution)/shard_map/condition/pallas_call | solution.py:91
  19.1 0.1 collective-permute-start.13
  19.2 1.4 %collective-permute-start.8 = (bf16[2,4,2,16,256]{4,3,2,1,0:T(8,128)(2,1)S(1)}, bf16[2,4,2,16,256]{4,3,2,1,0:T(8,128)(2,1)S(1)}, u32[]{:S(2)}, u32[]{:S(2)}) collective-permute-start(bf16[2,4,2,16,256]{4,3,2,1,0:T(8,128)(2,1)S(1)} %condition.1.refs_0_), channel_id=1, source_target_pairs={{12,0},{13,1},{14,2},{15,3},{8,4},{9,5},{10,6},{11,7},{4,8},{5,9},... | collective-permute-start | bytes 393224 | tf_op jit(solution)/shard_map/ppermute | solution.py:21
  20.6 1.3 %collective-permute-start.12 = (bf16[2,4,2,16,256]{4,3,2,1,0:T(8,128)(2,1)S(1)}, bf16[2,4,2,16,256]{4,3,2,1,0:T(8,128)(2,1)S(1)}, u32[]{:S(2)}, u32[]{:S(2)}) collective-permute-start(bf16[2,4,2,16,256]{4,3,2,1,0:T(8,128)(2,1)S(1)} %condition.1.refs_0_), channel_id=1, source_target_pairs={{2,0},{3,1},{0,2},{1,3},{6,4},{7,5},{4,6},{5,7},{10,8},{11,9},{8,1... | collective-permute-start | bytes 393224 | tf_op jit(solution)/shard_map/ppermute | solution.py:21
  21.9 3.0 %collective-permute-done.13.refs_2_ = bf16[2,4,2,16,256]{4,3,2,1,0:T(8,128)(2,1)S(1)} collective-permute-done((bf16[2,4,2,16,256]{4,3,2,1,0:T(8,128)(2,1)S(1)}, bf16[2,4,2,16,256]{4,3,2,1,0:T(8,128)(2,1)S(1)}, u32[]{:S(2)}, u32[]{:S(2)}) %collective-permute-start.13) | collective-permute-done | bytes 131104 | tf_op jit(solution)/shard_map/ppermute | solution.py:21
  24.9 1.3 %collective-permute-start.14 = (bf16[2,4,2,16,256]{4,3,2,1,0:T(8,128)(2,1)S(1)}, bf16[2,4,2,16,256]{4,3,2,1,0:T(8,128)(2,1)S(1)}, u32[]{:S(2)}, u32[]{:S(2)}) collective-permute-start(bf16[2,4,2,16,256]{4,3,2,1,0:T(8,128)(2,1)S(1)} %collective-permute-done.13.refs_2_), channel_id=1, source_target_pairs={{2,0},{3,1},{0,2},{1,3},{6,4},{7,5},{4,6},{5,7},{10,8},{11,9},{8,1... | collective-permute-start | bytes 393224 | tf_op jit(solution)/shard_map/ppermute | solution.py:21
  26.2 0.9 %collective-permute-done.8.refs_0_ = bf16[2,4,2,16,256]{4,3,2,1,0:T(8,128)(2,1)S(1)} collective-permute-done((bf16[2,4,2,16,256]{4,3,2,1,0:T(8,128)(2,1)S(1)}, bf16[2,4,2,16,256]{4,3,2,1,0:T(8,128)(2,1)S(1)}, u32[]{:S(2)}, u32[]{:S(2)}) %collective-permute-start.8) | collective-permute-done | bytes 131104 | tf_op jit(solution)/shard_map/ppermute | solution.py:21
  27.0 1.5 %collective-permute-start.10 = (bf16[2,4,2,16,256]{4,3,2,1,0:T(8,128)(2,1)S(1)}, bf16[2,4,2,16,256]{4,3,2,1,0:T(8,128)(2,1)S(1)}, u32[]{:S(2)}, u32[]{:S(2)}) collective-permute-start(bf16[2,4,2,16,256]{4,3,2,1,0:T(8,128)(2,1)S(1)} %collective-permute-done.8.refs_0_), channel_id=1, source_target_pairs={{4,0},{5,1},{6,2},{7,3},{0,4},{1,5},{2,6},{3,7},{12,8},{13,9},{14,... | collective-permute-start | bytes 393224 | tf_op jit(solution)/shard_map/ppermute | solution.py:21
  28.5 1.6 %collective-permute-start.11 = (bf16[2,4,2,16,256]{4,3,2,1,0:T(8,128)(2,1)S(1)}, bf16[2,4,2,16,256]{4,3,2,1,0:T(8,128)(2,1)S(1)}, u32[]{:S(2)}, u32[]{:S(2)}) collective-permute-start(bf16[2,4,2,16,256]{4,3,2,1,0:T(8,128)(2,1)S(1)} %collective-permute-done.8.refs_0_), channel_id=1, source_target_pairs={{2,0},{3,1},{0,2},{1,3},{6,4},{7,5},{4,6},{5,7},{10,8},{11,9},{8,1... | collective-permute-start | bytes 393224 | tf_op jit(solution)/shard_map/ppermute | solution.py:21
  30.2 0.4 collective-permute-start.9
  30.5 0.4 %collective-permute-done.14.refs_3_ = bf16[2,4,2,16,256]{4,3,2,1,0:T(8,128)(2,1)S(1)} collective-permute-done((bf16[2,4,2,16,256]{4,3,2,1,0:T(8,128)(2,1)S(1)}, bf16[2,4,2,16,256]{4,3,2,1,0:T(8,128)(2,1)S(1)}, u32[]{:S(2)}, u32[]{:S(2)}) %collective-permute-start.14) | collective-permute-done | bytes 131104 | tf_op jit(solution)/shard_map/ppermute | solution.py:21
  30.9 0.2 turn.2.refs_1_
  31.2 0.1 collective-permute-start.15
  31.3 1.3 %score.4.refs_2_ = f32[2048,512]{1,0:T(8,128)S(1)} custom-call(bf16[2048,2048]{1,0:T(8,128)(2,1)S(1)} %stage.3.refs_0_, bf16[512,512]{1,0:T(8,128)(2,1)S(1)} %turn.2.refs_1_), custom_call_target="tpu_custom_call" | custom-call | flops 21474836480 | bytes 4194304 | tf_op jit(solution)/shard_map/score/pallas_call | solution.py:169
  32.5 0.6 %collective-permute-done.15.refs_1_ = bf16[512,512]{1,0:T(8,128)(2,1)S(1)} collective-permute-done((bf16[512,512]{1,0:T(8,128)(2,1)S(1)}, bf16[512,512]{1,0:T(8,128)(2,1)S(1)}, u32[]{:S(2)}, u32[]{:S(2)}) %collective-permute-start.15) | collective-permute-done | bytes 524320 | tf_op jit(solution)/shard_map/ppermute | solution.py:21
  33.2 1.4 %score.5.refs_2_ = f32[2048,512]{1,0:T(8,128)S(1)} custom-call(bf16[2048,2048]{1,0:T(8,128)(2,1)S(1)} %stage.3.refs_0_, bf16[512,512]{1,0:T(8,128)(2,1)S(1)} %collective-permute-done.15.refs_1_, f32[2048,512]{1,0:T(8,128)S(1)} %score.4.refs_2_), custom_call_target="tpu_custom_call", output_to_operand_aliasing={{}: (2, {})} | custom-call | flops 1073741824 | bytes 4194304 | tf_op jit(solution)/shard_map/score/pallas_call | solution.py:169
  34.6 1.4 %collective-permute-done.9.refs_3_ = bf16[2,4,2,16,256]{4,3,2,1,0:T(8,128)(2,1)S(1)} collective-permute-done((bf16[2,4,2,16,256]{4,3,2,1,0:T(8,128)(2,1)S(1)}, bf16[2,4,2,16,256]{4,3,2,1,0:T(8,128)(2,1)S(1)}, u32[]{:S(2)}, u32[]{:S(2)}) %collective-permute-start.9) | collective-permute-done | bytes 131104 | tf_op jit(solution)/shard_map/ppermute | solution.py:21
  36.0 0.2 turn.3.refs_1_
  36.3 0.1 collective-permute-start.16
  36.4 1.4 %score.6.refs_2_ = f32[2048,512]{1,0:T(8,128)S(1)} custom-call(bf16[2048,2048]{1,0:T(8,128)(2,1)S(1)} %stage.3.refs_0_, bf16[512,512]{1,0:T(8,128)(2,1)S(1)} %turn.3.refs_1_, f32[2048,512]{1,0:T(8,128)S(1)} %score.5.refs_2_), custom_call_target="tpu_custom_call", output_to_operand_aliasing={{}: (2, {})} | custom-call | flops 1073741824 | bytes 4194304 | tf_op jit(solution)/shard_map/score/pallas_call | solution.py:169
  37.8 0.5 %collective-permute-done.16.refs_1_ = bf16[512,512]{1,0:T(8,128)(2,1)S(1)} collective-permute-done((bf16[512,512]{1,0:T(8,128)(2,1)S(1)}, bf16[512,512]{1,0:T(8,128)(2,1)S(1)}, u32[]{:S(2)}, u32[]{:S(2)}) %collective-permute-start.16) | collective-permute-done | bytes 524320 | tf_op jit(solution)/shard_map/ppermute | solution.py:21
  38.3 2.8 %score.7 = f32[2048,512]{1,0:T(8,128)} custom-call(bf16[2048,2048]{1,0:T(8,128)(2,1)S(1)} %stage.3.refs_0_, bf16[512,512]{1,0:T(8,128)(2,1)S(1)} %collective-permute-done.16.refs_1_, f32[2048,512]{1,0:T(8,128)S(1)} %score.6.refs_2_), custom_call_target="tpu_custom_call" | custom-call | flops 1073741824 | bytes 4194304 | tf_op jit(solution)/shard_map/score/pallas_call | solution.py:169
  (11 shorter events, 0.0 us)
Async XLA Ops:
  0.0 9.0 %collective-permute-start = (bf16[2,16,2048]{2,1,0:T(8,128)(2,1)}, bf16[2,16,2048]{2,1,0:T(8,128)(2,1)S(1)}, u32[]{:S(2)}, u32[]{:S(2)}) collective-permute-start(bf16[2,16,2048]{2,1,0:T(8,128)(2,1)} %refs_1_.2), channel_id=1, source_target_pairs={{12,0},{13,1},{14,2},{15,3},{8,4},{9,5},{10,6},{11,7},{4,8},{5,9},... | collective-permute-start | bytes 393224 | tf_op jit(solution)/shard_map/ppermute | solution.py:21
  5.0 13.6 %collective-permute-start.7 = (bf16[1,2048,128]{2,1,0:T(8,128)(2,1)}, bf16[1,2048,128]{2,1,0:T(8,128)(2,1)S(1)}, u32[]{:S(2)}, u32[]{:S(2)}) collective-permute-start(bf16[1,2048,128]{2,1,0:T(8,128)(2,1)} %refs_2_.1), channel_id=1, source_target_pairs={{2,0},{3,1},{0,2},{1,3},{6,4},{7,5},{4,6},{5,7},{10,8},{11,9},{8,1... | collective-permute-start | bytes 1572872 | tf_op jit(solution)/shard_map/ppermute | solution.py:21
  6.6 2.4 %collective-permute-start.1 = (bf16[2,16,2048]{2,1,0:T(8,128)(2,1)}, bf16[2,16,2048]{2,1,0:T(8,128)(2,1)S(1)}, u32[]{:S(2)}, u32[]{:S(2)}) collective-permute-start(bf16[2,16,2048]{2,1,0:T(8,128)(2,1)} %refs_1_.2), channel_id=1, source_target_pairs={{1,0},{0,1},{3,2},{2,3},{5,4},{4,5},{7,6},{6,7},{9,8},{8,9},{11,10... | collective-permute-start | bytes 393224 | tf_op jit(solution)/shard_map/ppermute | solution.py:21
  6.6 6.9 %collective-permute-start.3 = (bf16[2,16,2048]{2,1,0:T(8,128)(2,1)}, bf16[2,16,2048]{2,1,0:T(8,128)(2,1)S(1)}, u32[]{:S(2)}, u32[]{:S(2)}) collective-permute-start(bf16[2,16,2048]{2,1,0:T(8,128)(2,1)} %refs_1_.2), channel_id=1, source_target_pairs={{4,0},{5,1},{6,2},{7,3},{0,4},{1,5},{2,6},{3,7},{12,8},{13,9},{14,... | collective-permute-start | bytes 393224 | tf_op jit(solution)/shard_map/ppermute | solution.py:21
  9.0 6.5 %collective-permute-start.2 = (bf16[2,16,2048]{2,1,0:T(8,128)(2,1)S(1)}, bf16[2,16,2048]{2,1,0:T(8,128)(2,1)S(1)}, u32[]{:S(2)}, u32[]{:S(2)}) collective-permute-start(bf16[2,16,2048]{2,1,0:T(8,128)(2,1)S(1)} %collective-permute-done.refs_3_), channel_id=1, source_target_pairs={{4,0},{5,1},{6,2},{7,3},{0,4},{1,5},{2,6},{3,7},{12,8},{13,9},{14,... | collective-permute-start | bytes 393224 | tf_op jit(solution)/shard_map/ppermute | solution.py:21
  11.3 4.2 %collective-permute-start.5 = (bf16[2,16,2048]{2,1,0:T(8,128)(2,1)S(1)}, bf16[2,16,2048]{2,1,0:T(8,128)(2,1)S(1)}, u32[]{:S(2)}, u32[]{:S(2)}) collective-permute-start(bf16[2,16,2048]{2,1,0:T(8,128)(2,1)S(1)} %collective-permute-done.refs_3_), channel_id=1, source_target_pairs={{1,0},{0,1},{3,2},{2,3},{5,4},{4,5},{7,6},{6,7},{9,8},{8,9},{11,10... | collective-permute-start | bytes 393224 | tf_op jit(solution)/shard_map/ppermute | solution.py:21
  13.5 2.0 %collective-permute-start.4 = (bf16[2,16,2048]{2,1,0:T(8,128)(2,1)S(1)}, bf16[2,16,2048]{2,1,0:T(8,128)(2,1)S(1)}, u32[]{:S(2)}, u32[]{:S(2)}) collective-permute-start(bf16[2,16,2048]{2,1,0:T(8,128)(2,1)S(1)} %collective-permute-done.3.refs_2_), channel_id=1, source_target_pairs={{1,0},{0,1},{3,2},{2,3},{5,4},{4,5},{7,6},{6,7},{9,8},{8,9},{11,10... | collective-permute-start | bytes 393224 | tf_op jit(solution)/shard_map/ppermute | solution.py:21
  15.5 1.3 %collective-permute-start.6 = (bf16[2,16,2048]{2,1,0:T(8,128)(2,1)S(1)}, bf16[2,16,2048]{2,1,0:T(8,128)(2,1)S(1)}, u32[]{:S(2)}, u32[]{:S(2)}) collective-permute-start(bf16[2,16,2048]{2,1,0:T(8,128)(2,1)S(1)} %collective-permute-done.2.refs_4_), channel_id=1, source_target_pairs={{1,0},{0,1},{3,2},{2,3},{5,4},{4,5},{7,6},{6,7},{9,8},{8,9},{11,10... | collective-permute-start | bytes 393224 | tf_op jit(solution)/shard_map/ppermute | solution.py:21
  19.1 5.8 %collective-permute-start.13 = (bf16[2,4,2,16,256]{4,3,2,1,0:T(8,128)(2,1)S(1)}, bf16[2,4,2,16,256]{4,3,2,1,0:T(8,128)(2,1)S(1)}, u32[]{:S(2)}, u32[]{:S(2)}) collective-permute-start(bf16[2,4,2,16,256]{4,3,2,1,0:T(8,128)(2,1)S(1)} %condition.1.refs_0_), channel_id=1, source_target_pairs={{4,0},{5,1},{6,2},{7,3},{0,4},{1,5},{2,6},{3,7},{12,8},{13,9},{14,... | collective-permute-start | bytes 393224 | tf_op jit(solution)/shard_map/ppermute | solution.py:21
  19.2 7.9 %collective-permute-start.8 = (bf16[2,4,2,16,256]{4,3,2,1,0:T(8,128)(2,1)S(1)}, bf16[2,4,2,16,256]{4,3,2,1,0:T(8,128)(2,1)S(1)}, u32[]{:S(2)}, u32[]{:S(2)}) collective-permute-start(bf16[2,4,2,16,256]{4,3,2,1,0:T(8,128)(2,1)S(1)} %condition.1.refs_0_), channel_id=1, source_target_pairs={{12,0},{13,1},{14,2},{15,3},{8,4},{9,5},{10,6},{11,7},{4,8},{5,9},... | collective-permute-start | bytes 393224 | tf_op jit(solution)/shard_map/ppermute | solution.py:21
  20.6 9.9 %collective-permute-start.12 = (bf16[2,4,2,16,256]{4,3,2,1,0:T(8,128)(2,1)S(1)}, bf16[2,4,2,16,256]{4,3,2,1,0:T(8,128)(2,1)S(1)}, u32[]{:S(2)}, u32[]{:S(2)}) collective-permute-start(bf16[2,4,2,16,256]{4,3,2,1,0:T(8,128)(2,1)S(1)} %condition.1.refs_0_), channel_id=1, source_target_pairs={{2,0},{3,1},{0,2},{1,3},{6,4},{7,5},{4,6},{5,7},{10,8},{11,9},{8,1... | collective-permute-start | bytes 393224 | tf_op jit(solution)/shard_map/ppermute | solution.py:21
  24.9 6.0 %collective-permute-start.14 = (bf16[2,4,2,16,256]{4,3,2,1,0:T(8,128)(2,1)S(1)}, bf16[2,4,2,16,256]{4,3,2,1,0:T(8,128)(2,1)S(1)}, u32[]{:S(2)}, u32[]{:S(2)}) collective-permute-start(bf16[2,4,2,16,256]{4,3,2,1,0:T(8,128)(2,1)S(1)} %collective-permute-done.13.refs_2_), channel_id=1, source_target_pairs={{2,0},{3,1},{0,2},{1,3},{6,4},{7,5},{4,6},{5,7},{10,8},{11,9},{8,1... | collective-permute-start | bytes 393224 | tf_op jit(solution)/shard_map/ppermute | solution.py:21
  27.0 7.5 %collective-permute-start.10 = (bf16[2,4,2,16,256]{4,3,2,1,0:T(8,128)(2,1)S(1)}, bf16[2,4,2,16,256]{4,3,2,1,0:T(8,128)(2,1)S(1)}, u32[]{:S(2)}, u32[]{:S(2)}) collective-permute-start(bf16[2,4,2,16,256]{4,3,2,1,0:T(8,128)(2,1)S(1)} %collective-permute-done.8.refs_0_), channel_id=1, source_target_pairs={{4,0},{5,1},{6,2},{7,3},{0,4},{1,5},{2,6},{3,7},{12,8},{13,9},{14,... | collective-permute-start | bytes 393224 | tf_op jit(solution)/shard_map/ppermute | solution.py:21
  28.5 6.1 %collective-permute-start.11 = (bf16[2,4,2,16,256]{4,3,2,1,0:T(8,128)(2,1)S(1)}, bf16[2,4,2,16,256]{4,3,2,1,0:T(8,128)(2,1)S(1)}, u32[]{:S(2)}, u32[]{:S(2)}) collective-permute-start(bf16[2,4,2,16,256]{4,3,2,1,0:T(8,128)(2,1)S(1)} %collective-permute-done.8.refs_0_), channel_id=1, source_target_pairs={{2,0},{3,1},{0,2},{1,3},{6,4},{7,5},{4,6},{5,7},{10,8},{11,9},{8,1... | collective-permute-start | bytes 393224 | tf_op jit(solution)/shard_map/ppermute | solution.py:21
  30.2 5.9 %collective-permute-start.9 = (bf16[2,4,2,16,256]{4,3,2,1,0:T(8,128)(2,1)S(1)}, bf16[2,4,2,16,256]{4,3,2,1,0:T(8,128)(2,1)S(1)}, u32[]{:S(2)}, u32[]{:S(2)}) collective-permute-start(bf16[2,4,2,16,256]{4,3,2,1,0:T(8,128)(2,1)S(1)} %collective-permute-done.8.refs_0_), channel_id=1, source_target_pairs={{6,0},{7,1},{4,2},{5,3},{2,4},{3,5},{0,6},{1,7},{14,8},{15,9},{12,... | collective-permute-start | bytes 393224 | tf_op jit(solution)/shard_map/ppermute | solution.py:21
  31.2 2.0 %collective-permute-start.15 = (bf16[512,512]{1,0:T(8,128)(2,1)S(1)}, bf16[512,512]{1,0:T(8,128)(2,1)S(1)}, u32[]{:S(2)}, u32[]{:S(2)}) collective-permute-start(bf16[512,512]{1,0:T(8,128)(2,1)S(1)} %turn.2.refs_1_), channel_id=1, source_target_pairs={{1,0},{0,1},{3,2},{2,3},{5,4},{4,5},{7,6},{6,7},{9,8},{8,9},{11,10... | collective-permute-start | bytes 1572872 | tf_op jit(solution)/shard_map/ppermute | solution.py:21
  36.3 2.0 %collective-permute-start.16 = (bf16[512,512]{1,0:T(8,128)(2,1)S(1)}, bf16[512,512]{1,0:T(8,128)(2,1)S(1)}, u32[]{:S(2)}, u32[]{:S(2)}) collective-permute-start(bf16[512,512]{1,0:T(8,128)(2,1)S(1)} %turn.3.refs_1_), channel_id=1, source_target_pairs={{1,0},{0,1},{3,2},{2,3},{5,4},{4,5},{7,6},{6,7},{9,8},{8,9},{11,10... | collective-permute-start | bytes 1572872 | tf_op jit(solution)/shard_map/ppermute | solution.py:21

commit v12 on v11

--- a/solution.py
+++ b/solution.py
@@ -212,7 +212,7 @@
     swap(far_one, *near_one)
     swap(far_three, 0, 1)
     swap(far_three, beside, 1)
-    swap(far_three, beside, 0)
+    swap(own, relayed, 0)
     total = None
     for masks in ((0, beside), (mirror, relayed)):
         turned = turn(grid, parts, masks)

time: 41.2 us -> 42.4 us (1.029)
  starting transfers between devices: 17.1 us -> 20.8 us
  waiting for transfers between devices: 11.4 us -> 8.93 us
    ppermute x17, starting transfers between devices: 17.1 us -> 20.8 us  [swap(): lax.ppermute(block, 'rows', [(row ^ step, row) for row in range(self.far...]
    ppermute x17, waiting for transfers between devices: 11.4 us -> 8.93 us  [swap(): lax.ppermute(block, 'rows', [(row ^ step, row) for row in range(self.far...]
  transfers between devices with their start and end apart: 17 -> 17, of which waited for: 9 -> 7; matrix products, arithmetic and copies ran while one was open for 0% -> 0% of each run, Pallas kernels for 22% -> 21%
where the time goes in v12:
time: 42.4 us; the launch traced here: 42.2 us
  starting transfers between devices  20.8 us (49%)
  Pallas kernels  12.3 us (29%)
  waiting for transfers between devices  8.93 us (21%)
    ppermute x17, starting transfers between devices, swap(): lax.ppermute(block, 'rows', [(row ^ step, row) for row in range(self.far...  20.8 us
    ppermute x17, waiting for transfers between devices, swap(): lax.ppermute(block, 'rows', [(row ^ step, row) for row in range(self.far...  8.93 us
    pallas_call x4, Pallas kernels, score(): pl.pallas_call(functools.partial(score_kernel, grid, masks, other, first,...  6.88 us
    pallas_call x2, Pallas kernels, stage(): pl.pallas_call(functools.partial(stage_kernel, first, arrays[0].shape[0]...  4.56 us
  transfers between devices with their start and end apart: 17, of which 7 were waited for; matrix products, arithmetic and copies ran while one was open for 0% of the time, Pallas kernels for 21%

profile of v12, /device:TPU:0, one launch (start us, length us, event | category | flops | bytes accessed | tf_op | source)
XLA Modules:
  0.0 42.2 jit_solution(4243135127801879425)
XLA Ops:
  0.0 5.0 %collective-permute-start = (bf16[2,16,2048]{2,1,0:T(8,128)(2,1)}, bf16[2,16,2048]{2,1,0:T(8,128)(2,1)S(1)}, u32[]{:S(2)}, u32[]{:S(2)}) collective-permute-start(bf16[2,16,2048]{2,1,0:T(8,128)(2,1)} %refs_1_.2), channel_id=1, source_target_pairs={{12,0},{13,1},{14,2},{15,3},{8,4},{9,5},{10,6},{11,7},{4,8},{5,9},... | collective-permute-start | bytes 393224 | tf_op jit(solution)/shard_map/ppermute | solution.py:21
  5.0 1.5 %collective-permute-start.7 = (bf16[1,2048,128]{2,1,0:T(8,128)(2,1)}, bf16[1,2048,128]{2,1,0:T(8,128)(2,1)S(1)}, u32[]{:S(2)}, u32[]{:S(2)}) collective-permute-start(bf16[1,2048,128]{2,1,0:T(8,128)(2,1)} %refs_2_.1), channel_id=1, source_target_pairs={{2,0},{3,1},{0,2},{1,3},{6,4},{7,5},{4,6},{5,7},{10,8},{11,9},{8,1... | collective-permute-start | bytes 1572872 | tf_op jit(solution)/shard_map/ppermute | solution.py:21
  6.6 0.0 collective-permute-start.1
  6.6 0.0 collective-permute-start.3
  6.6 2.4 %stage.2 = (bf16[2048,2048]{1,0:T(8,128)(2,1)S(1)}, bf16[2,16,2048]{2,1,0:T(8,128)(2,1)S(1)}, bf16[1,2048,128]{2,1,0:T(8,128)(2,1)S(1)}) custom-call(bf16[2048,2048]{1,0:T(8,128)(2,1)} %refs_1_.3, bf16[2,16,2048]{2,1,0:T(8,128)(2,1)} %refs_1_.2, bf16[1,2048,128]{2,1,0:T(8,128)(2,1)} %refs_2_.1), custom_call_target="tpu_custom_call" | custom-call | flops 2788300032 | bytes 9043968 | tf_op jit(solution)/shard_map/stage/pallas_call | solution.py:56
  9.0 0.0 collective-permute-done.refs_3_
  9.0 2.3 %collective-permute-start.2 = (bf16[2,16,2048]{2,1,0:T(8,128)(2,1)S(1)}, bf16[2,16,2048]{2,1,0:T(8,128)(2,1)S(1)}, u32[]{:S(2)}, u32[]{:S(2)}) collective-permute-start(bf16[2,16,2048]{2,1,0:T(8,128)(2,1)S(1)} %collective-permute-done.refs_3_), channel_id=1, source_target_pairs={{4,0},{5,1},{6,2},{7,3},{0,4},{1,5},{2,6},{3,7},{12,8},{13,9},{14,... | collective-permute-start | bytes 393224 | tf_op jit(solution)/shard_map/ppermute | solution.py:21
  11.3 2.2 %stage.3.refs_0_ = bf16[2048,2048]{1,0:T(8,128)(2,1)S(1)} custom-call(bf16[2048,2048]{1,0:T(8,128)(2,1)S(1)} %get-tuple-element.24.refs_0_, bf16[2048,2048]{1,0:T(8,128)(2,1)} %refs_1_.3), custom_call_target="tpu_custom_call", output_to_operand_aliasing={{}: (0, {})} | custom-call | flops 1 | bytes 8388608 | tf_op jit(solution)/shard_map/stage/pallas_call | solution.py:56
  13.5 0.6 %collective-permute-start.4 = (bf16[2,16,2048]{2,1,0:T(8,128)(2,1)S(1)}, bf16[2,16,2048]{2,1,0:T(8,128)(2,1)S(1)}, u32[]{:S(2)}, u32[]{:S(2)}) collective-permute-start(bf16[2,16,2048]{2,1,0:T(8,128)(2,1)S(1)} %collective-permute-done.3.refs_2_), channel_id=1, source_target_pairs={{1,0},{0,1},{3,2},{2,3},{5,4},{4,5},{7,6},{6,7},{9,8},{8,9},{11,10... | collective-permute-start | bytes 393224 | tf_op jit(solution)/shard_map/ppermute | solution.py:21
  14.1 1.4 %collective-permute-done.2.refs_4_ = bf16[2,16,2048]{2,1,0:T(8,128)(2,1)S(1)} collective-permute-done((bf16[2,16,2048]{2,1,0:T(8,128)(2,1)S(1)}, bf16[2,16,2048]{2,1,0:T(8,128)(2,1)S(1)}, u32[]{:S(2)}, u32[]{:S(2)}) %collective-permute-start.2) | collective-permute-done | bytes 131104 | tf_op jit(solution)/shard_map/ppermute | solution.py:21
  15.5 1.3 %collective-permute-done.6.refs_7_ = bf16[2,16,2048]{2,1,0:T(8,128)(2,1)S(1)} collective-permute-done((bf16[2,16,2048]{2,1,0:T(8,128)(2,1)S(1)}, bf16[2,16,2048]{2,1,0:T(8,128)(2,1)S(1)}, u32[]{:S(2)}, u32[]{:S(2)}) %collective-permute-start.6) | collective-permute-done | bytes 131104 | tf_op jit(solution)/shard_map/ppermute | solution.py:21
  16.9 1.8 %collective-permute-done.7.refs_9_ = bf16[1,2048,128]{2,1,0:T(8,128)(2,1)S(1)} collective-permute-done((bf16[1,2048,128]{2,1,0:T(8,128)(2,1)}, bf16[1,2048,128]{2,1,0:T(8,128)(2,1)S(1)}, u32[]{:S(2)}, u32[]{:S(2)}) %collective-permute-start.7) | collective-permute-done | bytes 524320 | tf_op jit(solution)/shard_map/ppermute | solution.py:21
  18.6 0.4 %condition.1.refs_0_ = bf16[2,4,2,16,256]{4,3,2,1,0:T(8,128)(2,1)S(1)} custom-call(bf16[2,16,2048]{2,1,0:T(8,128)(2,1)S(1)} %get-tuple-element.26.refs_0_, bf16[2,16,2048]{2,1,0:T(8,128)(2,1)S(1)} %collective-permute-done.1.refs_1_, bf16[2,16,2048]{2,1,0:T(8,128)(2,1)S(1)} %collective-permute-done.3.refs_2_, ...), custom_call_target="tpu_custom_call" | custom-call | flops 268435456 | bytes 3145728 | tf_op jit(solution)/shard_map/condition/pallas_call | solution.py:91
  19.1 0.1 collective-permute-start.13
  19.2 1.4 %collective-permute-start.8 = (bf16[2,4,2,16,256]{4,3,2,1,0:T(8,128)(2,1)S(1)}, bf16[2,4,2,16,256]{4,3,2,1,0:T(8,128)(2,1)S(1)}, u32[]{:S(2)}, u32[]{:S(2)}) collective-permute-start(bf16[2,4,2,16,256]{4,3,2,1,0:T(8,128)(2,1)S(1)} %condition.1.refs_0_), channel_id=1, source_target_pairs={{12,0},{13,1},{14,2},{15,3},{8,4},{9,5},{10,6},{11,7},{4,8},{5,9},... | collective-permute-start | bytes 393224 | tf_op jit(solution)/shard_map/ppermute | solution.py:21
  20.6 1.3 %collective-permute-start.12 = (bf16[2,4,2,16,256]{4,3,2,1,0:T(8,128)(2,1)S(1)}, bf16[2,4,2,16,256]{4,3,2,1,0:T(8,128)(2,1)S(1)}, u32[]{:S(2)}, u32[]{:S(2)}) collective-permute-start(bf16[2,4,2,16,256]{4,3,2,1,0:T(8,128)(2,1)S(1)} %condition.1.refs_0_), channel_id=1, source_target_pairs={{2,0},{3,1},{0,2},{1,3},{6,4},{7,5},{4,6},{5,7},{10,8},{11,9},{8,1... | collective-permute-start | bytes 393224 | tf_op jit(solution)/shard_map/ppermute | solution.py:21
  21.9 3.0 %collective-permute-done.13.refs_2_ = bf16[2,4,2,16,256]{4,3,2,1,0:T(8,128)(2,1)S(1)} collective-permute-done((bf16[2,4,2,16,256]{4,3,2,1,0:T(8,128)(2,1)S(1)}, bf16[2,4,2,16,256]{4,3,2,1,0:T(8,128)(2,1)S(1)}, u32[]{:S(2)}, u32[]{:S(2)}) %collective-permute-start.13) | collective-permute-done | bytes 131104 | tf_op jit(solution)/shard_map/ppermute | solution.py:21
  24.9 1.3 %collective-permute-start.14 = (bf16[2,4,2,16,256]{4,3,2,1,0:T(8,128)(2,1)S(1)}, bf16[2,4,2,16,256]{4,3,2,1,0:T(8,128)(2,1)S(1)}, u32[]{:S(2)}, u32[]{:S(2)}) collective-permute-start(bf16[2,4,2,16,256]{4,3,2,1,0:T(8,128)(2,1)S(1)} %collective-permute-done.13.refs_2_), channel_id=1, source_target_pairs={{2,0},{3,1},{0,2},{1,3},{6,4},{7,5},{4,6},{5,7},{10,8},{11,9},{8,1... | collective-permute-start | bytes 393224 | tf_op jit(solution)/shard_map/ppermute | solution.py:21
  26.2 0.5 %collective-permute-start.10 = (bf16[2,4,2,16,256]{4,3,2,1,0:T(8,128)(2,1)S(1)}, bf16[2,4,2,16,256]{4,3,2,1,0:T(8,128)(2,1)S(1)}, u32[]{:S(2)}, u32[]{:S(2)}) collective-permute-start(bf16[2,4,2,16,256]{4,3,2,1,0:T(8,128)(2,1)S(1)} %condition.1.refs_0_), channel_id=1, source_target_pairs={{8,0},{9,1},{10,2},{11,3},{12,4},{13,5},{14,6},{15,7},{0,8},{1,9},... | collective-permute-start | bytes 393224 | tf_op jit(solution)/shard_map/ppermute | solution.py:21
  26.7 0.3 collective-permute-done.8.refs_0_
  27.0 2.0 %collective-permute-start.11 = (bf16[2,4,2,16,256]{4,3,2,1,0:T(8,128)(2,1)S(1)}, bf16[2,4,2,16,256]{4,3,2,1,0:T(8,128)(2,1)S(1)}, u32[]{:S(2)}, u32[]{:S(2)}) collective-permute-start(bf16[2,4,2,16,256]{4,3,2,1,0:T(8,128)(2,1)S(1)} %collective-permute-done.8.refs_0_), channel_id=1, source_target_pairs={{2,0},{3,1},{0,2},{1,3},{6,4},{7,5},{4,6},{5,7},{10,8},{11,9},{8,1... | collective-permute-start | bytes 393224 | tf_op jit(solution)/shard_map/ppermute | solution.py:21
  29.0 4.5 %collective-permute-start.9 = (bf16[2,4,2,16,256]{4,3,2,1,0:T(8,128)(2,1)S(1)}, bf16[2,4,2,16,256]{4,3,2,1,0:T(8,128)(2,1)S(1)}, u32[]{:S(2)}, u32[]{:S(2)}) collective-permute-start(bf16[2,4,2,16,256]{4,3,2,1,0:T(8,128)(2,1)S(1)} %collective-permute-done.8.refs_0_), channel_id=1, source_target_pairs={{6,0},{7,1},{4,2},{5,3},{2,4},{3,5},{0,6},{1,7},{14,8},{15,9},{12,... | collective-permute-start | bytes 393224 | tf_op jit(solution)/shard_map/ppermute | solution.py:21
  33.5 0.2 turn.2.refs_1_
  33.8 0.1 collective-permute-start.15
  33.8 1.3 %score.4.refs_2_ = f32[2048,512]{1,0:T(8,128)S(1)} custom-call(bf16[2048,2048]{1,0:T(8,128)(2,1)S(1)} %stage.3.refs_0_, bf16[512,512]{1,0:T(8,128)(2,1)S(1)} %turn.2.refs_1_), custom_call_target="tpu_custom_call" | custom-call | flops 21474836480 | bytes 4194304 | tf_op jit(solution)/shard_map/score/pallas_call | solution.py:169
  35.1 0.6 %collective-permute-done.15.refs_1_ = bf16[512,512]{1,0:T(8,128)(2,1)S(1)} collective-permute-done((bf16[512,512]{1,0:T(8,128)(2,1)S(1)}, bf16[512,512]{1,0:T(8,128)(2,1)S(1)}, u32[]{:S(2)}, u32[]{:S(2)}) %collective-permute-start.15) | collective-permute-done | bytes 524320 | tf_op jit(solution)/shard_map/ppermute | solution.py:21
  35.7 1.4 %score.5.refs_2_ = f32[2048,512]{1,0:T(8,128)S(1)} custom-call(bf16[2048,2048]{1,0:T(8,128)(2,1)S(1)} %stage.3.refs_0_, bf16[512,512]{1,0:T(8,128)(2,1)S(1)} %collective-permute-done.15.refs_1_, f32[2048,512]{1,0:T(8,128)S(1)} %score.4.refs_2_), custom_call_target="tpu_custom_call", output_to_operand_aliasing={{}: (2, {})} | custom-call | flops 1073741824 | bytes 4194304 | tf_op jit(solution)/shard_map/score/pallas_call | solution.py:169
  37.2 0.2 turn.3.refs_1_
  37.4 0.2 collective-permute-start.16
  37.6 1.4 %score.6.refs_2_ = f32[2048,512]{1,0:T(8,128)S(1)} custom-call(bf16[2048,2048]{1,0:T(8,128)(2,1)S(1)} %stage.3.refs_0_, bf16[512,512]{1,0:T(8,128)(2,1)S(1)} %turn.3.refs_1_, f32[2048,512]{1,0:T(8,128)S(1)} %score.5.refs_2_), custom_call_target="tpu_custom_call", output_to_operand_aliasing={{}: (2, {})} | custom-call | flops 1073741824 | bytes 4194304 | tf_op jit(solution)/shard_map/score/pallas_call | solution.py:169
  39.0 0.4 collective-permute-done.16.refs_1_
  39.4 2.8 %score.7 = f32[2048,512]{1,0:T(8,128)} custom-call(bf16[2048,2048]{1,0:T(8,128)(2,1)S(1)} %stage.3.refs_0_, bf16[512,512]{1,0:T(8,128)(2,1)S(1)} %collective-permute-done.16.refs_1_, f32[2048,512]{1,0:T(8,128)S(1)} %score.6.refs_2_), custom_call_target="tpu_custom_call" | custom-call | flops 1073741824 | bytes 4194304 | tf_op jit(solution)/shard_map/score/pallas_call | solution.py:169
  (11 shorter events, 0.0 us)
Async XLA Ops:
  0.0 9.0 %collective-permute-start = (bf16[2,16,2048]{2,1,0:T(8,128)(2,1)}, bf16[2,16,2048]{2,1,0:T(8,128)(2,1)S(1)}, u32[]{:S(2)}, u32[]{:S(2)}) collective-permute-start(bf16[2,16,2048]{2,1,0:T(8,128)(2,1)} %refs_1_.2), channel_id=1, source_target_pairs={{12,0},{13,1},{14,2},{15,3},{8,4},{9,5},{10,6},{11,7},{4,8},{5,9},... | collective-permute-start | bytes 393224 | tf_op jit(solution)/shard_map/ppermute | solution.py:21
  5.0 13.6 %collective-permute-start.7 = (bf16[1,2048,128]{2,1,0:T(8,128)(2,1)}, bf16[1,2048,128]{2,1,0:T(8,128)(2,1)S(1)}, u32[]{:S(2)}, u32[]{:S(2)}) collective-permute-start(bf16[1,2048,128]{2,1,0:T(8,128)(2,1)} %refs_2_.1), channel_id=1, source_target_pairs={{2,0},{3,1},{0,2},{1,3},{6,4},{7,5},{4,6},{5,7},{10,8},{11,9},{8,1... | collective-permute-start | bytes 1572872 | tf_op jit(solution)/shard_map/ppermute | solution.py:21
  6.6 2.4 %collective-permute-start.1 = (bf16[2,16,2048]{2,1,0:T(8,128)(2,1)}, bf16[2,16,2048]{2,1,0:T(8,128)(2,1)S(1)}, u32[]{:S(2)}, u32[]{:S(2)}) collective-permute-start(bf16[2,16,2048]{2,1,0:T(8,128)(2,1)} %refs_1_.2), channel_id=1, source_target_pairs={{1,0},{0,1},{3,2},{2,3},{5,4},{4,5},{7,6},{6,7},{9,8},{8,9},{11,10... | collective-permute-start | bytes 393224 | tf_op jit(solution)/shard_map/ppermute | solution.py:21
  6.6 6.9 %collective-permute-start.3 = (bf16[2,16,2048]{2,1,0:T(8,128)(2,1)}, bf16[2,16,2048]{2,1,0:T(8,128)(2,1)S(1)}, u32[]{:S(2)}, u32[]{:S(2)}) collective-permute-start(bf16[2,16,2048]{2,1,0:T(8,128)(2,1)} %refs_1_.2), channel_id=1, source_target_pairs={{4,0},{5,1},{6,2},{7,3},{0,4},{1,5},{2,6},{3,7},{12,8},{13,9},{14,... | collective-permute-start | bytes 393224 | tf_op jit(solution)/shard_map/ppermute | solution.py:21
  9.0 6.5 %collective-permute-start.2 = (bf16[2,16,2048]{2,1,0:T(8,128)(2,1)S(1)}, bf16[2,16,2048]{2,1,0:T(8,128)(2,1)S(1)}, u32[]{:S(2)}, u32[]{:S(2)}) collective-permute-start(bf16[2,16,2048]{2,1,0:T(8,128)(2,1)S(1)} %collective-permute-done.refs_3_), channel_id=1, source_target_pairs={{4,0},{5,1},{6,2},{7,3},{0,4},{1,5},{2,6},{3,7},{12,8},{13,9},{14,... | collective-permute-start | bytes 393224 | tf_op jit(solution)/shard_map/ppermute | solution.py:21
  11.3 4.2 %collective-permute-start.5 = (bf16[2,16,2048]{2,1,0:T(8,128)(2,1)S(1)}, bf16[2,16,2048]{2,1,0:T(8,128)(2,1)S(1)}, u32[]{:S(2)}, u32[]{:S(2)}) collective-permute-start(bf16[2,16,2048]{2,1,0:T(8,128)(2,1)S(1)} %collective-permute-done.refs_3_), channel_id=1, source_target_pairs={{1,0},{0,1},{3,2},{2,3},{5,4},{4,5},{7,6},{6,7},{9,8},{8,9},{11,10... | collective-permute-start | bytes 393224 | tf_op jit(solution)/shard_map/ppermute | solution.py:21
  13.5 2.0 %collective-permute-start.4 = (bf16[2,16,2048]{2,1,0:T(8,128)(2,1)S(1)}, bf16[2,16,2048]{2,1,0:T(8,128)(2,1)S(1)}, u32[]{:S(2)}, u32[]{:S(2)}) collective-permute-start(bf16[2,16,2048]{2,1,0:T(8,128)(2,1)S(1)} %collective-permute-done.3.refs_2_), channel_id=1, source_target_pairs={{1,0},{0,1},{3,2},{2,3},{5,4},{4,5},{7,6},{6,7},{9,8},{8,9},{11,10... | collective-permute-start | bytes 393224 | tf_op jit(solution)/shard_map/ppermute | solution.py:21
  15.5 1.3 %collective-permute-start.6 = (bf16[2,16,2048]{2,1,0:T(8,128)(2,1)S(1)}, bf16[2,16,2048]{2,1,0:T(8,128)(2,1)S(1)}, u32[]{:S(2)}, u32[]{:S(2)}) collective-permute-start(bf16[2,16,2048]{2,1,0:T(8,128)(2,1)S(1)} %collective-permute-done.2.refs_4_), channel_id=1, source_target_pairs={{1,0},{0,1},{3,2},{2,3},{5,4},{4,5},{7,6},{6,7},{9,8},{8,9},{11,10... | collective-permute-start | bytes 393224 | tf_op jit(solution)/shard_map/ppermute | solution.py:21
  19.1 5.8 %collective-permute-start.13 = (bf16[2,4,2,16,256]{4,3,2,1,0:T(8,128)(2,1)S(1)}, bf16[2,4,2,16,256]{4,3,2,1,0:T(8,128)(2,1)S(1)}, u32[]{:S(2)}, u32[]{:S(2)}) collective-permute-start(bf16[2,4,2,16,256]{4,3,2,1,0:T(8,128)(2,1)S(1)} %condition.1.refs_0_), channel_id=1, source_target_pairs={{4,0},{5,1},{6,2},{7,3},{0,4},{1,5},{2,6},{3,7},{12,8},{13,9},{14,... | collective-permute-start | bytes 393224 | tf_op jit(solution)/shard_map/ppermute | solution.py:21
  19.2 7.9 %collective-permute-start.8 = (bf16[2,4,2,16,256]{4,3,2,1,0:T(8,128)(2,1)S(1)}, bf16[2,4,2,16,256]{4,3,2,1,0:T(8,128)(2,1)S(1)}, u32[]{:S(2)}, u32[]{:S(2)}) collective-permute-start(bf16[2,4,2,16,256]{4,3,2,1,0:T(8,128)(2,1)S(1)} %condition.1.refs_0_), channel_id=1, source_target_pairs={{12,0},{13,1},{14,2},{15,3},{8,4},{9,5},{10,6},{11,7},{4,8},{5,9},... | collective-permute-start | bytes 393224 | tf_op jit(solution)/shard_map/ppermute | solution.py:21
  20.6 12.9 %collective-permute-start.12 = (bf16[2,4,2,16,256]{4,3,2,1,0:T(8,128)(2,1)S(1)}, bf16[2,4,2,16,256]{4,3,2,1,0:T(8,128)(2,1)S(1)}, u32[]{:S(2)}, u32[]{:S(2)}) collective-permute-start(bf16[2,4,2,16,256]{4,3,2,1,0:T(8,128)(2,1)S(1)} %condition.1.refs_0_), channel_id=1, source_target_pairs={{2,0},{3,1},{0,2},{1,3},{6,4},{7,5},{4,6},{5,7},{10,8},{11,9},{8,1... | collective-permute-start | bytes 393224 | tf_op jit(solution)/shard_map/ppermute | solution.py:21
  24.9 8.6 %collective-permute-start.14 = (bf16[2,4,2,16,256]{4,3,2,1,0:T(8,128)(2,1)S(1)}, bf16[2,4,2,16,256]{4,3,2,1,0:T(8,128)(2,1)S(1)}, u32[]{:S(2)}, u32[]{:S(2)}) collective-permute-start(bf16[2,4,2,16,256]{4,3,2,1,0:T(8,128)(2,1)S(1)} %collective-permute-done.13.refs_2_), channel_id=1, source_target_pairs={{2,0},{3,1},{0,2},{1,3},{6,4},{7,5},{4,6},{5,7},{10,8},{11,9},{8,1... | collective-permute-start | bytes 393224 | tf_op jit(solution)/shard_map/ppermute | solution.py:21
  26.2 11.0 %collective-permute-start.10 = (bf16[2,4,2,16,256]{4,3,2,1,0:T(8,128)(2,1)S(1)}, bf16[2,4,2,16,256]{4,3,2,1,0:T(8,128)(2,1)S(1)}, u32[]{:S(2)}, u32[]{:S(2)}) collective-permute-start(bf16[2,4,2,16,256]{4,3,2,1,0:T(8,128)(2,1)S(1)} %condition.1.refs_0_), channel_id=1, source_target_pairs={{8,0},{9,1},{10,2},{11,3},{12,4},{13,5},{14,6},{15,7},{0,8},{1,9},... | collective-permute-start | bytes 393224 | tf_op jit(solution)/shard_map/ppermute | solution.py:21
  27.0 10.1 %collective-permute-start.11 = (bf16[2,4,2,16,256]{4,3,2,1,0:T(8,128)(2,1)S(1)}, bf16[2,4,2,16,256]{4,3,2,1,0:T(8,128)(2,1)S(1)}, u32[]{:S(2)}, u32[]{:S(2)}) collective-permute-start(bf16[2,4,2,16,256]{4,3,2,1,0:T(8,128)(2,1)S(1)} %collective-permute-done.8.refs_0_), channel_id=1, source_target_pairs={{2,0},{3,1},{0,2},{1,3},{6,4},{7,5},{4,6},{5,7},{10,8},{11,9},{8,1... | collective-permute-start | bytes 393224 | tf_op jit(solution)/shard_map/ppermute | solution.py:21
  29.0 8.1 %collective-permute-start.9 = (bf16[2,4,2,16,256]{4,3,2,1,0:T(8,128)(2,1)S(1)}, bf16[2,4,2,16,256]{4,3,2,1,0:T(8,128)(2,1)S(1)}, u32[]{:S(2)}, u32[]{:S(2)}) collective-permute-start(bf16[2,4,2,16,256]{4,3,2,1,0:T(8,128)(2,1)S(1)} %collective-permute-done.8.refs_0_), channel_id=1, source_target_pairs={{6,0},{7,1},{4,2},{5,3},{2,4},{3,5},{0,6},{1,7},{14,8},{15,9},{12,... | collective-permute-start | bytes 393224 | tf_op jit(solution)/shard_map/ppermute | solution.py:21
  33.8 2.0 %collective-permute-start.15 = (bf16[512,512]{1,0:T(8,128)(2,1)S(1)}, bf16[512,512]{1,0:T(8,128)(2,1)S(1)}, u32[]{:S(2)}, u32[]{:S(2)}) collective-permute-start(bf16[512,512]{1,0:T(8,128)(2,1)S(1)} %turn.2.refs_1_), channel_id=1, source_target_pairs={{1,0},{0,1},{3,2},{2,3},{5,4},{4,5},{7,6},{6,7},{9,8},{8,9},{11,10... | collective-permute-start | bytes 1572872 | tf_op jit(solution)/shard_map/ppermute | solution.py:21
  37.4 2.0 %collective-permute-start.16 = (bf16[512,512]{1,0:T(8,128)(2,1)S(1)}, bf16[512,512]{1,0:T(8,128)(2,1)S(1)}, u32[]{:S(2)}, u32[]{:S(2)}) collective-permute-start(bf16[512,512]{1,0:T(8,128)(2,1)S(1)} %turn.3.refs_1_), channel_id=1, source_target_pairs={{1,0},{0,1},{3,2},{2,3},{5,4},{4,5},{7,6},{6,7},{9,8},{8,9},{11,10... | collective-permute-start | bytes 1572872 | tf_op jit(solution)/shard_map/ppermute | solution.py:21

commit v13 on v12

--- a/solution.py
+++ b/solution.py
@@ -182,45 +182,45 @@
 
 
 def two_level(grid, train_feats, queries, inverse_fisher):
-    beside, mirror, relayed = 1, 3, 2
+    beside, across, relayed = 1, 2, 3
     gathered = {(0, 0): queries}
     gathered[0, 1] = grid.swap(queries, 0, 0, 1)
     gathered[beside, 0] = grid.swap(queries, beside, 0, 0)
     near_fisher = grid.swap(inverse_fisher, 0, 1, 0)
-    gathered[mirror, 0] = grid.swap(queries, mirror, 0, 0)
+    gathered[across, 0] = grid.swap(queries, across, 0, 0)
     staged = stage([train_feats, queries, inverse_fisher])
-    gathered[mirror, 0], gathered[0, 1], staged = lax.optimization_barrier(
-        (gathered[mirror, 0], gathered[0, 1], staged)
+    gathered[across, 0], gathered[0, 1], staged = lax.optimization_barrier(
+        (gathered[across, 0], gathered[0, 1], staged)
     )
     train_here, gathered[0, 0], fisher_here = staged
-    gathered[relayed, 0] = grid.swap(gathered[mirror, 0], beside, 0, 0)
+    gathered[relayed, 0] = grid.swap(gathered[across, 0], beside, 0, 0)
     (train_here,) = stage([train_feats], train_here)
-    for mask in (beside, mirror):
+    for mask in (beside, across):
         gathered[mask, 1] = grid.swap(gathered[mask, 0], 0, 0, 1)
     gathered[relayed, 0], train_here = lax.optimization_barrier((gathered[relayed, 0], train_here))
     gathered[relayed, 1] = grid.swap(gathered[relayed, 0], 0, 0, 1)
 
-    own, near_one, far_one, far_three = (0, 0), (0, 1), (beside, 0), (mirror, 0)
+    own, near_one, far_one, far_two = (0, 0), (0, 1), (beside, 0), (across, 0)
     parts = {own: condition(grid, gathered, fisher_here, near_fisher)}
 
     def swap(source, far, near):
         parts[source[0] ^ far, source[1] ^ near] = grid.swap(parts[source], far, near, 0)
 
-    swap(own, *far_three)
+    swap(own, *far_two)
     swap(own, *near_one)
     swap(own, *far_one)
     swap(far_one, *near_one)
-    swap(far_three, 0, 1)
-    swap(far_three, beside, 1)
-    swap(own, relayed, 0)
+    swap(far_two, 0, 1)
+    swap(far_two, beside, 1)
+    swap(far_two, beside, 0)
     total = None
-    for masks in ((0, beside), (mirror, relayed)):
+    for masks in ((0, beside), (across, relayed)):
         turned = turn(grid, parts, masks)
         other = grid.swap(turned, 0, 0, 1)
         total = score(grid, train_here, turned, total, masks, 0, False)
-        total = score(grid, train_here, other, total, masks, 1, masks == (mirror, relayed))
+        total = score(grid, train_here, other, total, masks, 1, masks == (across, relayed))
         if masks == (0, beside):
-            late = (mirror, 0), (relayed, 1), (relayed, 0), (mirror, 1)
+            late = (across, 0), (relayed, 1), (relayed, 0), (across, 1)
             held, total = lax.optimization_barrier(([parts[place] for place in late], total))
             parts.update(zip(late, held))
     return total

time: 42.4 us -> 41.8 us (0.986)
  starting transfers between devices: 20.8 us -> 18.3 us
  waiting for transfers between devices: 8.93 us -> 10.9 us
    ppermute x17, starting transfers between devices: 20.8 us -> 18.3 us  [swap(): lax.ppermute(block, 'rows', [(row ^ step, row) for row in range(self.far...]
    ppermute x17, waiting for transfers between devices: 8.93 us -> 10.9 us  [swap(): lax.ppermute(block, 'rows', [(row ^ step, row) for row in range(self.far...]
  transfers between devices with their start and end apart: 17 -> 17, of which waited for: 7 -> 9; matrix products, arithmetic and copies ran while one was open for 0% -> 0% of each run, Pallas kernels for 21% -> 21%
where the time goes in v13:
time: 41.8 us; the launch traced here: 41.7 us
  starting transfers between devices  18.3 us (44%)
  Pallas kernels  12.3 us (29%)
  waiting for transfers between devices  10.9 us (26%)
    ppermute x17, starting transfers between devices, swap(): lax.ppermute(block, 'rows', [(row ^ step, row) for row in range(self.far...  18.3 us
    ppermute x17, waiting for transfers between devices, swap(): lax.ppermute(block, 'rows', [(row ^ step, row) for row in range(self.far...  10.9 us
    pallas_call x4, Pallas kernels, score(): pl.pallas_call(functools.partial(score_kernel, grid, masks, other, first,...  6.87 us
    pallas_call x2, Pallas kernels, stage(): pl.pallas_call(functools.partial(stage_kernel, first, arrays[0].shape[0]...  4.56 us
  transfers between devices with their start and end apart: 17, of which 9 were waited for; matrix products, arithmetic and copies ran while one was open for 0% of the time, Pallas kernels for 21%

profile of v13, /device:TPU:0, one launch (start us, length us, event | category | flops | bytes accessed | tf_op | source)
XLA Modules:
  0.0 41.7 jit_solution(4792589774799673114)
XLA Ops:
  0.0 4.0 %collective-permute-start = (bf16[2,16,2048]{2,1,0:T(8,128)(2,1)}, bf16[2,16,2048]{2,1,0:T(8,128)(2,1)S(1)}, u32[]{:S(2)}, u32[]{:S(2)}) collective-permute-start(bf16[2,16,2048]{2,1,0:T(8,128)(2,1)} %refs_1_.2), channel_id=1, source_target_pairs={{8,0},{9,1},{10,2},{11,3},{12,4},{13,5},{14,6},{15,7},{0,8},{1,9},... | collective-permute-start | bytes 393224 | tf_op jit(solution)/shard_map/ppermute | solution.py:21
  4.0 1.5 %collective-permute-start.7 = (bf16[1,2048,128]{2,1,0:T(8,128)(2,1)}, bf16[1,2048,128]{2,1,0:T(8,128)(2,1)S(1)}, u32[]{:S(2)}, u32[]{:S(2)}) collective-permute-start(bf16[1,2048,128]{2,1,0:T(8,128)(2,1)} %refs_2_.1), channel_id=1, source_target_pairs={{2,0},{3,1},{0,2},{1,3},{6,4},{7,5},{4,6},{5,7},{10,8},{11,9},{8,1... | collective-permute-start | bytes 1572872 | tf_op jit(solution)/shard_map/ppermute | solution.py:21
  5.6 1.6 %collective-permute-start.3 = (bf16[2,16,2048]{2,1,0:T(8,128)(2,1)}, bf16[2,16,2048]{2,1,0:T(8,128)(2,1)S(1)}, u32[]{:S(2)}, u32[]{:S(2)}) collective-permute-start(bf16[2,16,2048]{2,1,0:T(8,128)(2,1)} %refs_1_.2), channel_id=1, source_target_pairs={{4,0},{5,1},{6,2},{7,3},{0,4},{1,5},{2,6},{3,7},{12,8},{13,9},{14,... | collective-permute-start | bytes 393224 | tf_op jit(solution)/shard_map/ppermute | solution.py:21
  7.1 2.4 %stage.2 = (bf16[2048,2048]{1,0:T(8,128)(2,1)S(1)}, bf16[2,16,2048]{2,1,0:T(8,128)(2,1)S(1)}, bf16[1,2048,128]{2,1,0:T(8,128)(2,1)S(1)}) custom-call(bf16[2048,2048]{1,0:T(8,128)(2,1)} %refs_1_.3, bf16[2,16,2048]{2,1,0:T(8,128)(2,1)} %refs_1_.2, bf16[1,2048,128]{2,1,0:T(8,128)(2,1)} %refs_2_.1), custom_call_target="tpu_custom_call" | custom-call | flops 2788300032 | bytes 9043968 | tf_op jit(solution)/shard_map/stage/pallas_call | solution.py:56
  9.5 1.1 %collective-permute-done.refs_3_ = bf16[2,16,2048]{2,1,0:T(8,128)(2,1)S(1)} collective-permute-done((bf16[2,16,2048]{2,1,0:T(8,128)(2,1)}, bf16[2,16,2048]{2,1,0:T(8,128)(2,1)S(1)}, u32[]{:S(2)}, u32[]{:S(2)}) %collective-permute-start) | collective-permute-done | bytes 131104 | tf_op jit(solution)/shard_map/ppermute | solution.py:21
  10.7 0.8 %collective-permute-start.2 = (bf16[2,16,2048]{2,1,0:T(8,128)(2,1)S(1)}, bf16[2,16,2048]{2,1,0:T(8,128)(2,1)S(1)}, u32[]{:S(2)}, u32[]{:S(2)}) collective-permute-start(bf16[2,16,2048]{2,1,0:T(8,128)(2,1)S(1)} %collective-permute-done.refs_3_), channel_id=1, source_target_pairs={{4,0},{5,1},{6,2},{7,3},{0,4},{1,5},{2,6},{3,7},{12,8},{13,9},{14,... | collective-permute-start | bytes 393224 | tf_op jit(solution)/shard_map/ppermute | solution.py:21
  11.4 2.2 %stage.3.refs_0_ = bf16[2048,2048]{1,0:T(8,128)(2,1)S(1)} custom-call(bf16[2048,2048]{1,0:T(8,128)(2,1)S(1)} %get-tuple-element.24.refs_0_, bf16[2048,2048]{1,0:T(8,128)(2,1)} %refs_1_.3), custom_call_target="tpu_custom_call", output_to_operand_aliasing={{}: (0, {})} | custom-call | flops 1 | bytes 8388608 | tf_op jit(solution)/shard_map/stage/pallas_call | solution.py:56
  13.6 0.6 %collective-permute-start.4 = (bf16[2,16,2048]{2,1,0:T(8,128)(2,1)S(1)}, bf16[2,16,2048]{2,1,0:T(8,128)(2,1)S(1)}, u32[]{:S(2)}, u32[]{:S(2)}) collective-permute-start(bf16[2,16,2048]{2,1,0:T(8,128)(2,1)S(1)} %collective-permute-done.3.refs_2_), channel_id=1, source_target_pairs={{1,0},{0,1},{3,2},{2,3},{5,4},{4,5},{7,6},{6,7},{9,8},{8,9},{11,10... | collective-permute-start | bytes 393224 | tf_op jit(solution)/shard_map/ppermute | solution.py:21
  14.2 1.9 %collective-permute-done.2.refs_4_ = bf16[2,16,2048]{2,1,0:T(8,128)(2,1)S(1)} collective-permute-done((bf16[2,16,2048]{2,1,0:T(8,128)(2,1)S(1)}, bf16[2,16,2048]{2,1,0:T(8,128)(2,1)S(1)}, u32[]{:S(2)}, u32[]{:S(2)}) %collective-permute-start.2) | collective-permute-done | bytes 131104 | tf_op jit(solution)/shard_map/ppermute | solution.py:21
  16.1 1.3 %collective-permute-done.6.refs_7_ = bf16[2,16,2048]{2,1,0:T(8,128)(2,1)S(1)} collective-permute-done((bf16[2,16,2048]{2,1,0:T(8,128)(2,1)S(1)}, bf16[2,16,2048]{2,1,0:T(8,128)(2,1)S(1)}, u32[]{:S(2)}, u32[]{:S(2)}) %collective-permute-start.6) | collective-permute-done | bytes 131104 | tf_op jit(solution)/shard_map/ppermute | solution.py:21
  17.5 0.2 collective-permute-done.7.refs_9_
  17.6 0.4 %condition.1.refs_0_ = bf16[2,4,2,16,256]{4,3,2,1,0:T(8,128)(2,1)S(1)} custom-call(bf16[2,16,2048]{2,1,0:T(8,128)(2,1)S(1)} %get-tuple-element.26.refs_0_, bf16[2,16,2048]{2,1,0:T(8,128)(2,1)S(1)} %collective-permute-done.1.refs_1_, bf16[2,16,2048]{2,1,0:T(8,128)(2,1)S(1)} %collective-permute-done.3.refs_2_, ...), custom_call_target="tpu_custom_call" | custom-call | flops 268435456 | bytes 3145728 | tf_op jit(solution)/shard_map/condition/pallas_call | solution.py:91
  18.1 1.6 %collective-permute-start.13 = (bf16[2,4,2,16,256]{4,3,2,1,0:T(8,128)(2,1)S(1)}, bf16[2,4,2,16,256]{4,3,2,1,0:T(8,128)(2,1)S(1)}, u32[]{:S(2)}, u32[]{:S(2)}) collective-permute-start(bf16[2,4,2,16,256]{4,3,2,1,0:T(8,128)(2,1)S(1)} %condition.1.refs_0_), channel_id=1, source_target_pairs={{4,0},{5,1},{6,2},{7,3},{0,4},{1,5},{2,6},{3,7},{12,8},{13,9},{14,... | collective-permute-start | bytes 393224 | tf_op jit(solution)/shard_map/ppermute | solution.py:21
  19.7 2.3 %collective-permute-start.8 = (bf16[2,4,2,16,256]{4,3,2,1,0:T(8,128)(2,1)S(1)}, bf16[2,4,2,16,256]{4,3,2,1,0:T(8,128)(2,1)S(1)}, u32[]{:S(2)}, u32[]{:S(2)}) collective-permute-start(bf16[2,4,2,16,256]{4,3,2,1,0:T(8,128)(2,1)S(1)} %condition.1.refs_0_), channel_id=1, source_target_pairs={{8,0},{9,1},{10,2},{11,3},{12,4},{13,5},{14,6},{15,7},{0,8},{1,9},... | collective-permute-start | bytes 393224 | tf_op jit(solution)/shard_map/ppermute | solution.py:21
  22.0 1.5 %collective-permute-start.12 = (bf16[2,4,2,16,256]{4,3,2,1,0:T(8,128)(2,1)S(1)}, bf16[2,4,2,16,256]{4,3,2,1,0:T(8,128)(2,1)S(1)}, u32[]{:S(2)}, u32[]{:S(2)}) collective-permute-start(bf16[2,4,2,16,256]{4,3,2,1,0:T(8,128)(2,1)S(1)} %condition.1.refs_0_), channel_id=1, source_target_pairs={{2,0},{3,1},{0,2},{1,3},{6,4},{7,5},{4,6},{5,7},{10,8},{11,9},{8,1... | collective-permute-start | bytes 393224 | tf_op jit(solution)/shard_map/ppermute | solution.py:21
  23.5 2.4 %collective-permute-done.13.refs_2_ = bf16[2,4,2,16,256]{4,3,2,1,0:T(8,128)(2,1)S(1)} collective-permute-done((bf16[2,4,2,16,256]{4,3,2,1,0:T(8,128)(2,1)S(1)}, bf16[2,4,2,16,256]{4,3,2,1,0:T(8,128)(2,1)S(1)}, u32[]{:S(2)}, u32[]{:S(2)}) %collective-permute-start.13) | collective-permute-done | bytes 131104 | tf_op jit(solution)/shard_map/ppermute | solution.py:21
  25.9 0.7 %collective-permute-start.14 = (bf16[2,4,2,16,256]{4,3,2,1,0:T(8,128)(2,1)S(1)}, bf16[2,4,2,16,256]{4,3,2,1,0:T(8,128)(2,1)S(1)}, u32[]{:S(2)}, u32[]{:S(2)}) collective-permute-start(bf16[2,4,2,16,256]{4,3,2,1,0:T(8,128)(2,1)S(1)} %collective-permute-done.13.refs_2_), channel_id=1, source_target_pairs={{2,0},{3,1},{0,2},{1,3},{6,4},{7,5},{4,6},{5,7},{10,8},{11,9},{8,1... | collective-permute-start | bytes 393224 | tf_op jit(solution)/shard_map/ppermute | solution.py:21
  26.6 1.8 %collective-permute-done.8.refs_0_ = bf16[2,4,2,16,256]{4,3,2,1,0:T(8,128)(2,1)S(1)} collective-permute-done((bf16[2,4,2,16,256]{4,3,2,1,0:T(8,128)(2,1)S(1)}, bf16[2,4,2,16,256]{4,3,2,1,0:T(8,128)(2,1)S(1)}, u32[]{:S(2)}, u32[]{:S(2)}) %collective-permute-start.8) | collective-permute-done | bytes 131104 | tf_op jit(solution)/shard_map/ppermute | solution.py:21
  28.4 0.3 collective-permute-start.10
  28.7 1.5 %collective-permute-start.11 = (bf16[2,4,2,16,256]{4,3,2,1,0:T(8,128)(2,1)S(1)}, bf16[2,4,2,16,256]{4,3,2,1,0:T(8,128)(2,1)S(1)}, u32[]{:S(2)}, u32[]{:S(2)}) collective-permute-start(bf16[2,4,2,16,256]{4,3,2,1,0:T(8,128)(2,1)S(1)} %collective-permute-done.8.refs_0_), channel_id=1, source_target_pairs={{2,0},{3,1},{0,2},{1,3},{6,4},{7,5},{4,6},{5,7},{10,8},{11,9},{8,1... | collective-permute-start | bytes 393224 | tf_op jit(solution)/shard_map/ppermute | solution.py:21
  30.2 1.7 %collective-permute-start.9 = (bf16[2,4,2,16,256]{4,3,2,1,0:T(8,128)(2,1)S(1)}, bf16[2,4,2,16,256]{4,3,2,1,0:T(8,128)(2,1)S(1)}, u32[]{:S(2)}, u32[]{:S(2)}) collective-permute-start(bf16[2,4,2,16,256]{4,3,2,1,0:T(8,128)(2,1)S(1)} %collective-permute-done.8.refs_0_), channel_id=1, source_target_pairs={{6,0},{7,1},{4,2},{5,3},{2,4},{3,5},{0,6},{1,7},{14,8},{15,9},{12,... | collective-permute-start | bytes 393224 | tf_op jit(solution)/shard_map/ppermute | solution.py:21
  31.9 0.2 turn.2.refs_1_
  32.1 0.1 collective-permute-start.15
  32.2 1.3 %score.4.refs_2_ = f32[2048,512]{1,0:T(8,128)S(1)} custom-call(bf16[2048,2048]{1,0:T(8,128)(2,1)S(1)} %stage.3.refs_0_, bf16[512,512]{1,0:T(8,128)(2,1)S(1)} %turn.2.refs_1_), custom_call_target="tpu_custom_call" | custom-call | flops 21474836480 | bytes 4194304 | tf_op jit(solution)/shard_map/score/pallas_call | solution.py:169
  33.5 0.6 %collective-permute-done.15.refs_1_ = bf16[512,512]{1,0:T(8,128)(2,1)S(1)} collective-permute-done((bf16[512,512]{1,0:T(8,128)(2,1)S(1)}, bf16[512,512]{1,0:T(8,128)(2,1)S(1)}, u32[]{:S(2)}, u32[]{:S(2)}) %collective-permute-start.15) | collective-permute-done | bytes 524320 | tf_op jit(solution)/shard_map/ppermute | solution.py:21
  34.1 1.4 %score.5.refs_2_ = f32[2048,512]{1,0:T(8,128)S(1)} custom-call(bf16[2048,2048]{1,0:T(8,128)(2,1)S(1)} %stage.3.refs_0_, bf16[512,512]{1,0:T(8,128)(2,1)S(1)} %collective-permute-done.15.refs_1_, f32[2048,512]{1,0:T(8,128)S(1)} %score.4.refs_2_), custom_call_target="tpu_custom_call", output_to_operand_aliasing={{}: (2, {})} | custom-call | flops 1073741824 | bytes 4194304 | tf_op jit(solution)/shard_map/score/pallas_call | solution.py:169
  35.5 1.1 %collective-permute-done.9.refs_3_ = bf16[2,4,2,16,256]{4,3,2,1,0:T(8,128)(2,1)S(1)} collective-permute-done((bf16[2,4,2,16,256]{4,3,2,1,0:T(8,128)(2,1)S(1)}, bf16[2,4,2,16,256]{4,3,2,1,0:T(8,128)(2,1)S(1)}, u32[]{:S(2)}, u32[]{:S(2)}) %collective-permute-start.9) | collective-permute-done | bytes 131104 | tf_op jit(solution)/shard_map/ppermute | solution.py:21
  36.6 0.2 turn.3.refs_1_
  36.9 0.1 collective-permute-start.16
  37.0 1.4 %score.6.refs_2_ = f32[2048,512]{1,0:T(8,128)S(1)} custom-call(bf16[2048,2048]{1,0:T(8,128)(2,1)S(1)} %stage.3.refs_0_, bf16[512,512]{1,0:T(8,128)(2,1)S(1)} %turn.3.refs_1_, f32[2048,512]{1,0:T(8,128)S(1)} %score.5.refs_2_), custom_call_target="tpu_custom_call", output_to_operand_aliasing={{}: (2, {})} | custom-call | flops 1073741824 | bytes 4194304 | tf_op jit(solution)/shard_map/score/pallas_call | solution.py:169
  38.4 0.5 %collective-permute-done.16.refs_1_ = bf16[512,512]{1,0:T(8,128)(2,1)S(1)} collective-permute-done((bf16[512,512]{1,0:T(8,128)(2,1)S(1)}, bf16[512,512]{1,0:T(8,128)(2,1)S(1)}, u32[]{:S(2)}, u32[]{:S(2)}) %collective-permute-start.16) | collective-permute-done | bytes 524320 | tf_op jit(solution)/shard_map/ppermute | solution.py:21
  38.9 2.8 %score.7 = f32[2048,512]{1,0:T(8,128)} custom-call(bf16[2048,2048]{1,0:T(8,128)(2,1)S(1)} %stage.3.refs_0_, bf16[512,512]{1,0:T(8,128)(2,1)S(1)} %collective-permute-done.16.refs_1_, f32[2048,512]{1,0:T(8,128)S(1)} %score.6.refs_2_), custom_call_target="tpu_custom_call" | custom-call | flops 1073741824 | bytes 4194304 | tf_op jit(solution)/shard_map/score/pallas_call | solution.py:169
  (11 shorter events, 0.0 us)
Async XLA Ops:
  0.0 10.7 %collective-permute-start = (bf16[2,16,2048]{2,1,0:T(8,128)(2,1)}, bf16[2,16,2048]{2,1,0:T(8,128)(2,1)S(1)}, u32[]{:S(2)}, u32[]{:S(2)}) collective-permute-start(bf16[2,16,2048]{2,1,0:T(8,128)(2,1)} %refs_1_.2), channel_id=1, source_target_pairs={{8,0},{9,1},{10,2},{11,3},{12,4},{13,5},{14,6},{15,7},{0,8},{1,9},... | collective-permute-start | bytes 393224 | tf_op jit(solution)/shard_map/ppermute | solution.py:21
  4.0 13.6 %collective-permute-start.7 = (bf16[1,2048,128]{2,1,0:T(8,128)(2,1)}, bf16[1,2048,128]{2,1,0:T(8,128)(2,1)S(1)}, u32[]{:S(2)}, u32[]{:S(2)}) collective-permute-start(bf16[1,2048,128]{2,1,0:T(8,128)(2,1)} %refs_2_.1), channel_id=1, source_target_pairs={{2,0},{3,1},{0,2},{1,3},{6,4},{7,5},{4,6},{5,7},{10,8},{11,9},{8,1... | collective-permute-start | bytes 1572872 | tf_op jit(solution)/shard_map/ppermute | solution.py:21
  5.6 5.1 %collective-permute-start.1 = (bf16[2,16,2048]{2,1,0:T(8,128)(2,1)}, bf16[2,16,2048]{2,1,0:T(8,128)(2,1)S(1)}, u32[]{:S(2)}, u32[]{:S(2)}) collective-permute-start(bf16[2,16,2048]{2,1,0:T(8,128)(2,1)} %refs_1_.2), channel_id=1, source_target_pairs={{1,0},{0,1},{3,2},{2,3},{5,4},{4,5},{7,6},{6,7},{9,8},{8,9},{11,10... | collective-permute-start | bytes 393224 | tf_op jit(solution)/shard_map/ppermute | solution.py:21
  5.6 8.1 %collective-permute-start.3 = (bf16[2,16,2048]{2,1,0:T(8,128)(2,1)}, bf16[2,16,2048]{2,1,0:T(8,128)(2,1)S(1)}, u32[]{:S(2)}, u32[]{:S(2)}) collective-permute-start(bf16[2,16,2048]{2,1,0:T(8,128)(2,1)} %refs_1_.2), channel_id=1, source_target_pairs={{4,0},{5,1},{6,2},{7,3},{0,4},{1,5},{2,6},{3,7},{12,8},{13,9},{14,... | collective-permute-start | bytes 393224 | tf_op jit(solution)/shard_map/ppermute | solution.py:21
  10.7 5.4 %collective-permute-start.2 = (bf16[2,16,2048]{2,1,0:T(8,128)(2,1)S(1)}, bf16[2,16,2048]{2,1,0:T(8,128)(2,1)S(1)}, u32[]{:S(2)}, u32[]{:S(2)}) collective-permute-start(bf16[2,16,2048]{2,1,0:T(8,128)(2,1)S(1)} %collective-permute-done.refs_3_), channel_id=1, source_target_pairs={{4,0},{5,1},{6,2},{7,3},{0,4},{1,5},{2,6},{3,7},{12,8},{13,9},{14,... | collective-permute-start | bytes 393224 | tf_op jit(solution)/shard_map/ppermute | solution.py:21
  11.4 4.7 %collective-permute-start.5 = (bf16[2,16,2048]{2,1,0:T(8,128)(2,1)S(1)}, bf16[2,16,2048]{2,1,0:T(8,128)(2,1)S(1)}, u32[]{:S(2)}, u32[]{:S(2)}) collective-permute-start(bf16[2,16,2048]{2,1,0:T(8,128)(2,1)S(1)} %collective-permute-done.refs_3_), channel_id=1, source_target_pairs={{1,0},{0,1},{3,2},{2,3},{5,4},{4,5},{7,6},{6,7},{9,8},{8,9},{11,10... | collective-permute-start | bytes 393224 | tf_op jit(solution)/shard_map/ppermute | solution.py:21
  13.6 2.5 %collective-permute-start.4 = (bf16[2,16,2048]{2,1,0:T(8,128)(2,1)S(1)}, bf16[2,16,2048]{2,1,0:T(8,128)(2,1)S(1)}, u32[]{:S(2)}, u32[]{:S(2)}) collective-permute-start(bf16[2,16,2048]{2,1,0:T(8,128)(2,1)S(1)} %collective-permute-done.3.refs_2_), channel_id=1, source_target_pairs={{1,0},{0,1},{3,2},{2,3},{5,4},{4,5},{7,6},{6,7},{9,8},{8,9},{11,10... | collective-permute-start | bytes 393224 | tf_op jit(solution)/shard_map/ppermute | solution.py:21
  16.1 1.3 %collective-permute-start.6 = (bf16[2,16,2048]{2,1,0:T(8,128)(2,1)S(1)}, bf16[2,16,2048]{2,1,0:T(8,128)(2,1)S(1)}, u32[]{:S(2)}, u32[]{:S(2)}) collective-permute-start(bf16[2,16,2048]{2,1,0:T(8,128)(2,1)S(1)} %collective-permute-done.2.refs_4_), channel_id=1, source_target_pairs={{1,0},{0,1},{3,2},{2,3},{5,4},{4,5},{7,6},{6,7},{9,8},{8,9},{11,10... | collective-permute-start | bytes 393224 | tf_op jit(solution)/shard_map/ppermute | solution.py:21
  18.1 7.8 %collective-permute-start.13 = (bf16[2,4,2,16,256]{4,3,2,1,0:T(8,128)(2,1)S(1)}, bf16[2,4,2,16,256]{4,3,2,1,0:T(8,128)(2,1)S(1)}, u32[]{:S(2)}, u32[]{:S(2)}) collective-permute-start(bf16[2,4,2,16,256]{4,3,2,1,0:T(8,128)(2,1)S(1)} %condition.1.refs_0_), channel_id=1, source_target_pairs={{4,0},{5,1},{6,2},{7,3},{0,4},{1,5},{2,6},{3,7},{12,8},{13,9},{14,... | collective-permute-start | bytes 393224 | tf_op jit(solution)/shard_map/ppermute | solution.py:21
  19.7 8.7 %collective-permute-start.8 = (bf16[2,4,2,16,256]{4,3,2,1,0:T(8,128)(2,1)S(1)}, bf16[2,4,2,16,256]{4,3,2,1,0:T(8,128)(2,1)S(1)}, u32[]{:S(2)}, u32[]{:S(2)}) collective-permute-start(bf16[2,4,2,16,256]{4,3,2,1,0:T(8,128)(2,1)S(1)} %condition.1.refs_0_), channel_id=1, source_target_pairs={{8,0},{9,1},{10,2},{11,3},{12,4},{13,5},{14,6},{15,7},{0,8},{1,9},... | collective-permute-start | bytes 393224 | tf_op jit(solution)/shard_map/ppermute | solution.py:21
  22.0 9.9 %collective-permute-start.12 = (bf16[2,4,2,16,256]{4,3,2,1,0:T(8,128)(2,1)S(1)}, bf16[2,4,2,16,256]{4,3,2,1,0:T(8,128)(2,1)S(1)}, u32[]{:S(2)}, u32[]{:S(2)}) collective-permute-start(bf16[2,4,2,16,256]{4,3,2,1,0:T(8,128)(2,1)S(1)} %condition.1.refs_0_), channel_id=1, source_target_pairs={{2,0},{3,1},{0,2},{1,3},{6,4},{7,5},{4,6},{5,7},{10,8},{11,9},{8,1... | collective-permute-start | bytes 393224 | tf_op jit(solution)/shard_map/ppermute | solution.py:21
  25.9 6.0 %collective-permute-start.14 = (bf16[2,4,2,16,256]{4,3,2,1,0:T(8,128)(2,1)S(1)}, bf16[2,4,2,16,256]{4,3,2,1,0:T(8,128)(2,1)S(1)}, u32[]{:S(2)}, u32[]{:S(2)}) collective-permute-start(bf16[2,4,2,16,256]{4,3,2,1,0:T(8,128)(2,1)S(1)} %collective-permute-done.13.refs_2_), channel_id=1, source_target_pairs={{2,0},{3,1},{0,2},{1,3},{6,4},{7,5},{4,6},{5,7},{10,8},{11,9},{8,1... | collective-permute-start | bytes 393224 | tf_op jit(solution)/shard_map/ppermute | solution.py:21
  28.4 7.1 %collective-permute-start.10 = (bf16[2,4,2,16,256]{4,3,2,1,0:T(8,128)(2,1)S(1)}, bf16[2,4,2,16,256]{4,3,2,1,0:T(8,128)(2,1)S(1)}, u32[]{:S(2)}, u32[]{:S(2)}) collective-permute-start(bf16[2,4,2,16,256]{4,3,2,1,0:T(8,128)(2,1)S(1)} %collective-permute-done.8.refs_0_), channel_id=1, source_target_pairs={{4,0},{5,1},{6,2},{7,3},{0,4},{1,5},{2,6},{3,7},{12,8},{13,9},{14,... | collective-permute-start | bytes 393224 | tf_op jit(solution)/shard_map/ppermute | solution.py:21
  28.7 6.8 %collective-permute-start.11 = (bf16[2,4,2,16,256]{4,3,2,1,0:T(8,128)(2,1)S(1)}, bf16[2,4,2,16,256]{4,3,2,1,0:T(8,128)(2,1)S(1)}, u32[]{:S(2)}, u32[]{:S(2)}) collective-permute-start(bf16[2,4,2,16,256]{4,3,2,1,0:T(8,128)(2,1)S(1)} %collective-permute-done.8.refs_0_), channel_id=1, source_target_pairs={{2,0},{3,1},{0,2},{1,3},{6,4},{7,5},{4,6},{5,7},{10,8},{11,9},{8,1... | collective-permute-start | bytes 393224 | tf_op jit(solution)/shard_map/ppermute | solution.py:21
  30.2 6.4 %collective-permute-start.9 = (bf16[2,4,2,16,256]{4,3,2,1,0:T(8,128)(2,1)S(1)}, bf16[2,4,2,16,256]{4,3,2,1,0:T(8,128)(2,1)S(1)}, u32[]{:S(2)}, u32[]{:S(2)}) collective-permute-start(bf16[2,4,2,16,256]{4,3,2,1,0:T(8,128)(2,1)S(1)} %collective-permute-done.8.refs_0_), channel_id=1, source_target_pairs={{6,0},{7,1},{4,2},{5,3},{2,4},{3,5},{0,6},{1,7},{14,8},{15,9},{12,... | collective-permute-start | bytes 393224 | tf_op jit(solution)/shard_map/ppermute | solution.py:21
  32.1 2.0 %collective-permute-start.15 = (bf16[512,512]{1,0:T(8,128)(2,1)S(1)}, bf16[512,512]{1,0:T(8,128)(2,1)S(1)}, u32[]{:S(2)}, u32[]{:S(2)}) collective-permute-start(bf16[512,512]{1,0:T(8,128)(2,1)S(1)} %turn.2.refs_1_), channel_id=1, source_target_pairs={{1,0},{0,1},{3,2},{2,3},{5,4},{4,5},{7,6},{6,7},{9,8},{8,9},{11,10... | collective-permute-start | bytes 1572872 | tf_op jit(solution)/shard_map/ppermute | solution.py:21
  36.9 2.0 %collective-permute-start.16 = (bf16[512,512]{1,0:T(8,128)(2,1)S(1)}, bf16[512,512]{1,0:T(8,128)(2,1)S(1)}, u32[]{:S(2)}, u32[]{:S(2)}) collective-permute-start(bf16[512,512]{1,0:T(8,128)(2,1)S(1)} %turn.3.refs_1_), channel_id=1, source_target_pairs={{1,0},{0,1},{3,2},{2,3},{5,4},{4,5},{7,6},{6,7},{9,8},{8,9},{11,10... | collective-permute-start | bytes 1572872 | tf_op jit(solution)/shard_map/ppermute | solution.py:21

commit v14 on v12

--- a/solution.py
+++ b/solution.py
@@ -99,80 +99,69 @@
     )(*arrays)
 
 
-def turn_kernel(grid, masks, *refs):
-    part_refs, out_ref, sorted_ref = refs[:-2], refs[-2], refs[-1]
-    _, near, _ = grid.place()
-    width = part_refs[0].shape[-1]
+def score_kernel(grid, masks, other, first, last, *refs):
+    train_ref, part_refs, refs = refs[0], refs[1 : 1 + 2 * len(masks)], refs[1 + 2 * len(masks) :]
+    total_ref, refs = (None, refs) if first else (refs[0], refs[1:])
+    out_ref, sorted_ref, refs = refs[0], refs[1], refs[2:]
+    far, near, core = grid.place()
+    features = train_ref.shape[1]
+    width = features // (grid.far * 4)
     for index in range(len(masks)):
         for side in range(2):
-            sorted_ref[:, :, pl.ds(flip(near, side), 1), :, :, index * width : (index + 1) * width] = part_refs[
-                index * 2 + side
-            ][...][:, :, None]
-    out_ref[...] = sorted_ref[...].reshape(-1, out_ref.shape[0]).T
-
-
-def turn(grid, parts, masks):
-    arrays = [parts[mask, near] for mask in masks for near in range(2)]
-    blocks, far, cores, count, width = arrays[0].shape
-    features = len(masks) * width
-    return pl.pallas_call(
-        functools.partial(turn_kernel, grid, masks),
-        out_shape=pltpu.VMEM((features, blocks * far * 2 * cores * count), jnp.bfloat16),
-        in_specs=[VMEM] * len(arrays),
-        out_specs=VMEM,
-        scratch_shapes=[pltpu.VMEM((blocks, far, 2, cores, count, features), jnp.bfloat16)],
-        compiler_params=pltpu.CompilerParams(vmem_limit_bytes=8 << 20),
-        name="turn",
-    )(*(pltpu.with_memory_space_constraint(a, pltpu.VMEM) for a in arrays))
-
-
-def score_kernel(grid, masks, other, first, last, *refs):
-    train_ref, turned_ref, refs = refs[0], refs[1], refs[2:]
-    total_ref, refs = (None, refs) if first else (refs[0], refs[1:])
-    out_ref, refs = refs[0], refs[1:]
-    far, _, core = grid.place()
-    features = train_ref.shape[1]
-    width = features // (grid.far * 4)
+            sorted_ref[
+                :, :, pl.ds(flip(near, side), 1), :, :, index * 2 * width : (index + 1) * 2 * width
+            ] = part_refs[index * 2 + side][...][:, :, None]
+    turned = sorted_ref[...].reshape(-1, len(masks) * 2 * width).T
     pieces = [
         columns((flip(far, mask) * 2 + side) * 2 + flip(core, other), width) for mask in masks for side in range(2)
     ]
 
-    def products(rows, queries):
+    def products(rows, turned):
         train = jnp.concatenate([train_ref[rows, piece] for piece in pieces], axis=1)
-        value = jnp.dot(train, turned_ref[:, queries], preferred_element_type=jnp.float32)
-        return value if first else total_ref[rows, queries] + value
+        return jnp.dot(train, turned, preferred_element_type=jnp.float32)
 
     if not last:
-        out_ref[...] = products(slice(None), slice(None))
+        value = products(slice(None), turned)
+        out_ref[...] = value if first else total_ref[...] + value
         return
 
-    here_ref, sem = refs
+    turned_ref, here_ref, sem = refs
+    turned_ref[...] = turned
     scale = 1.0 / features**0.5
     row_step, query_step = here_ref.shape[0] // 2, here_ref.shape[1] // 2
     copies = []
     for step in range(4):
         queries = pl.ds(step % 2 * query_step, query_step)
         rows = pl.ds(step // 2 * row_step, row_step)
-        here_ref[rows, queries] = products(rows, queries) * scale
+        here_ref[rows, queries] = (total_ref[rows, queries] + products(rows, turned_ref[:, queries])) * scale
         copies.append(pltpu.make_async_copy(here_ref.at[rows, queries], out_ref.at[rows, queries], sem.at[step]))
         copies[-1].start()
     for copy in copies:
         copy.wait()
 
 
-def score(grid, train_feats, turned, total, masks, other, last):
+def score(grid, train_feats, parts, total, masks, other, last):
+    parts = [parts[mask, near, other] for mask in masks for near in range(2)]
     rows = train_feats.shape[0]
-    features, queries = turned.shape
+    blocks, far, cores, count, width = parts[0].shape
+    queries, features = blocks * far * 2 * cores * count, len(masks) * width
     first = total is None
-    arrays = [train_feats, turned] + ([] if first else [total])
+    arrays = [train_feats, *parts] + ([] if first else [total])
     shape = (rows, queries)
+    scratch = [pltpu.VMEM((blocks, far, 2, cores, count, features), jnp.bfloat16)]
+    if last:
+        scratch += [
+            pltpu.VMEM((features, queries), jnp.bfloat16),
+            pltpu.VMEM(shape, jnp.float32),
+            pltpu.SemaphoreType.DMA((4,)),
+        ]
     return pl.pallas_call(
         functools.partial(score_kernel, grid, masks, other, first, last),
         out_shape=jax.ShapeDtypeStruct(shape, jnp.float32) if last else pltpu.VMEM(shape, jnp.float32),
         in_specs=[VMEM] * len(arrays),
         out_specs=ANY if last else VMEM,
-        scratch_shapes=[pltpu.VMEM(shape, jnp.float32), pltpu.SemaphoreType.DMA((4,))] if last else [],
-        input_output_aliases={} if first or last else {2: 0},
+        scratch_shapes=scratch,
+        input_output_aliases={} if first or last else {len(arrays) - 1: 0},
         compiler_params=pltpu.CompilerParams(vmem_limit_bytes=24 << 20),
         cost_estimate=pl.CostEstimate(
             flops=(40 if first else 2) * rows * features * queries, bytes_accessed=4 << 20, transcendentals=0
@@ -200,29 +189,40 @@
     gathered[relayed, 0], train_here = lax.optimization_barrier((gathered[relayed, 0], train_here))
     gathered[relayed, 1] = grid.swap(gathered[relayed, 0], 0, 0, 1)
 
-    own, near_one, far_one, far_three = (0, 0), (0, 1), (beside, 0), (mirror, 0)
-    parts = {own: condition(grid, gathered, fisher_here, near_fisher)}
-
-    def swap(source, far, near):
-        parts[source[0] ^ far, source[1] ^ near] = grid.swap(parts[source], far, near, 0)
-
+    parts = {(0, 0, 0): condition(grid, gathered, fisher_here, near_fisher)}
+
+    def swap(source, *step):
+        place = tuple(a ^ b for a, b in zip(source, step))
+        parts[place] = grid.swap(parts[source], *step)
+
+    def meet(*places, total=None):
+        held, total = lax.optimization_barrier(([parts[place] for place in places], total))
+        parts.update(zip(places, held))
+        return total
+
+    own, near_one, far_one, far_three = (0, 0, 0), (0, 1, 0), (beside, 0, 0), (mirror, 0, 0)
     swap(own, *far_three)
     swap(own, *near_one)
     swap(own, *far_one)
+    swap(own, 0, 0, 1)
     swap(far_one, *near_one)
-    swap(far_three, 0, 1)
-    swap(far_three, beside, 1)
-    swap(own, relayed, 0)
+    swap(far_one, 0, 0, 1)
+    meet(near_one, (0, 0, 1), (beside, 0, 1), far_three)
+    swap(near_one, 0, 0, 1)
+    swap(far_three, 0, 0, 1)
+    swap(far_three, *near_one)
+    swap(far_three, beside, 1, 0)
+    swap(far_three, *far_one)
+    swap((beside, 1, 0), 0, 0, 1)
     total = None
-    for masks in ((0, beside), (mirror, relayed)):
-        turned = turn(grid, parts, masks)
-        other = grid.swap(turned, 0, 0, 1)
-        total = score(grid, train_here, turned, total, masks, 0, False)
-        total = score(grid, train_here, other, total, masks, 1, masks == (mirror, relayed))
-        if masks == (0, beside):
-            late = (mirror, 0), (relayed, 1), (relayed, 0), (mirror, 1)
-            held, total = lax.optimization_barrier(([parts[place] for place in late], total))
-            parts.update(zip(late, held))
+    for other in range(2):
+        total = score(grid, train_here, parts, total, (0, beside), other, False)
+    total = meet(far_three, (relayed, 1, 0), (relayed, 0, 0), (mirror, 1, 0), total=total)
+    swap((relayed, 0, 0), 0, 0, 1)
+    swap((mirror, 1, 0), 0, 0, 1)
+    swap((relayed, 1, 0), 0, 0, 1)
+    for other in range(2):
+        total = score(grid, train_here, parts, total, (mirror, relayed), other, other == 1)
     return total
 
 

time: 42.4 us -> 42.3 us (level)
  waiting for transfers between devices: 8.93 us -> 11.5 us
  starting transfers between devices: 20.8 us -> 18.3 us
    ppermute x17 -> x23, waiting for transfers between devices: 8.93 us -> 11.5 us  [swap(): lax.ppermute(block, 'rows', [(row ^ step, row) for row in range(self.far...]
    ppermute x17 -> x23, starting transfers between devices: 20.8 us -> 18.3 us  [swap(): lax.ppermute(block, 'rows', [(row ^ step, row) for row in range(self.far...]
    pallas_call x2 -> x0, Pallas kernels: 0.46 us -> none  [turn(): pl.pallas_call(functools.partial(turn_kernel, grid, masks), out_shape=plt...]
  transfers between devices with their start and end apart: 17 -> 23, of which waited for: 7 -> 6; matrix products, arithmetic and copies ran while one was open for 0% -> 0% of each run, Pallas kernels for 21% -> 21%
where the time goes in v14:
time: 42.3 us; the launch traced here: 42.1 us
  starting transfers between devices  18.3 us (43%)
  Pallas kernels  12.2 us (29%)
  waiting for transfers between devices  11.5 us (27%)
    ppermute x23, starting transfers between devices, swap(): lax.ppermute(block, 'rows', [(row ^ step, row) for row in range(self.far...  18.3 us
    ppermute x23, waiting for transfers between devices, swap(): lax.ppermute(block, 'rows', [(row ^ step, row) for row in range(self.far...  11.5 us
    pallas_call x4, Pallas kernels, score(): pl.pallas_call(functools.partial(score_kernel, grid, masks, other, first,...  7.22 us
    pallas_call x2, Pallas kernels, stage(): pl.pallas_call(functools.partial(stage_kernel, first, arrays[0].shape[0]...  4.56 us
  transfers between devices with their start and end apart: 23, of which 6 were waited for; matrix products, arithmetic and copies ran while one was open for 0% of the time, Pallas kernels for 21%

profile of v14, /device:TPU:0, one launch (start us, length us, event | category | flops | bytes accessed | tf_op | source)
XLA Modules:
  0.0 42.1 jit_solution(1915113707406533038)
XLA Ops:
  0.0 5.0 %collective-permute-start = (bf16[2,16,2048]{2,1,0:T(8,128)(2,1)}, bf16[2,16,2048]{2,1,0:T(8,128)(2,1)S(1)}, u32[]{:S(2)}, u32[]{:S(2)}) collective-permute-start(bf16[2,16,2048]{2,1,0:T(8,128)(2,1)} %refs_1_.2), channel_id=1, source_target_pairs={{12,0},{13,1},{14,2},{15,3},{8,4},{9,5},{10,6},{11,7},{4,8},{5,9},... | collective-permute-start | bytes 393224 | tf_op jit(solution)/shard_map/ppermute | solution.py:21
  5.0 1.5 %collective-permute-start.7 = (bf16[1,2048,128]{2,1,0:T(8,128)(2,1)}, bf16[1,2048,128]{2,1,0:T(8,128)(2,1)S(1)}, u32[]{:S(2)}, u32[]{:S(2)}) collective-permute-start(bf16[1,2048,128]{2,1,0:T(8,128)(2,1)} %refs_2_.1), channel_id=1, source_target_pairs={{2,0},{3,1},{0,2},{1,3},{6,4},{7,5},{4,6},{5,7},{10,8},{11,9},{8,1... | collective-permute-start | bytes 1572872 | tf_op jit(solution)/shard_map/ppermute | solution.py:21
  6.6 0.0 collective-permute-start.1
  6.6 0.0 collective-permute-start.3
  6.6 2.4 %stage.2 = (bf16[2048,2048]{1,0:T(8,128)(2,1)S(1)}, bf16[2,16,2048]{2,1,0:T(8,128)(2,1)S(1)}, bf16[1,2048,128]{2,1,0:T(8,128)(2,1)S(1)}) custom-call(bf16[2048,2048]{1,0:T(8,128)(2,1)} %refs_1_.3, bf16[2,16,2048]{2,1,0:T(8,128)(2,1)} %refs_1_.2, bf16[1,2048,128]{2,1,0:T(8,128)(2,1)} %refs_2_.1), custom_call_target="tpu_custom_call" | custom-call | flops 2788300032 | bytes 9043968 | tf_op jit(solution)/shard_map/stage/pallas_call | solution.py:56
  9.0 2.3 %collective-permute-start.2 = (bf16[2,16,2048]{2,1,0:T(8,128)(2,1)S(1)}, bf16[2,16,2048]{2,1,0:T(8,128)(2,1)S(1)}, u32[]{:S(2)}, u32[]{:S(2)}) collective-permute-start(bf16[2,16,2048]{2,1,0:T(8,128)(2,1)S(1)} %collective-permute-done.refs_3_), channel_id=1, source_target_pairs={{4,0},{5,1},{6,2},{7,3},{0,4},{1,5},{2,6},{3,7},{12,8},{13,9},{14,... | collective-permute-start | bytes 393224 | tf_op jit(solution)/shard_map/ppermute | solution.py:21
  11.3 2.2 %stage.3.refs_0_ = bf16[2048,2048]{1,0:T(8,128)(2,1)S(1)} custom-call(bf16[2048,2048]{1,0:T(8,128)(2,1)S(1)} %get-tuple-element.28.refs_0_, bf16[2048,2048]{1,0:T(8,128)(2,1)} %refs_1_.3), custom_call_target="tpu_custom_call", output_to_operand_aliasing={{}: (0, {})} | custom-call | flops 1 | bytes 8388608 | tf_op jit(solution)/shard_map/stage/pallas_call | solution.py:56
  13.5 0.6 %collective-permute-start.4 = (bf16[2,16,2048]{2,1,0:T(8,128)(2,1)S(1)}, bf16[2,16,2048]{2,1,0:T(8,128)(2,1)S(1)}, u32[]{:S(2)}, u32[]{:S(2)}) collective-permute-start(bf16[2,16,2048]{2,1,0:T(8,128)(2,1)S(1)} %collective-permute-done.3.refs_2_), channel_id=1, source_target_pairs={{1,0},{0,1},{3,2},{2,3},{5,4},{4,5},{7,6},{6,7},{9,8},{8,9},{11,10... | collective-permute-start | bytes 393224 | tf_op jit(solution)/shard_map/ppermute | solution.py:21
  14.1 1.4 %collective-permute-done.2.refs_4_ = bf16[2,16,2048]{2,1,0:T(8,128)(2,1)S(1)} collective-permute-done((bf16[2,16,2048]{2,1,0:T(8,128)(2,1)S(1)}, bf16[2,16,2048]{2,1,0:T(8,128)(2,1)S(1)}, u32[]{:S(2)}, u32[]{:S(2)}) %collective-permute-start.2) | collective-permute-done | bytes 131104 | tf_op jit(solution)/shard_map/ppermute | solution.py:21
  15.5 1.3 %collective-permute-done.6.refs_7_ = bf16[2,16,2048]{2,1,0:T(8,128)(2,1)S(1)} collective-permute-done((bf16[2,16,2048]{2,1,0:T(8,128)(2,1)S(1)}, bf16[2,16,2048]{2,1,0:T(8,128)(2,1)S(1)}, u32[]{:S(2)}, u32[]{:S(2)}) %collective-permute-start.6) | collective-permute-done | bytes 131104 | tf_op jit(solution)/shard_map/ppermute | solution.py:21
  16.9 1.8 %collective-permute-done.7.refs_9_ = bf16[1,2048,128]{2,1,0:T(8,128)(2,1)S(1)} collective-permute-done((bf16[1,2048,128]{2,1,0:T(8,128)(2,1)}, bf16[1,2048,128]{2,1,0:T(8,128)(2,1)S(1)}, u32[]{:S(2)}, u32[]{:S(2)}) %collective-permute-start.7) | collective-permute-done | bytes 524320 | tf_op jit(solution)/shard_map/ppermute | solution.py:21
  18.6 0.4 %condition.1.refs_1_ = bf16[2,4,2,16,256]{4,3,2,1,0:T(8,128)(2,1)S(1)} custom-call(bf16[2,16,2048]{2,1,0:T(8,128)(2,1)S(1)} %get-tuple-element.30.refs_0_, bf16[2,16,2048]{2,1,0:T(8,128)(2,1)S(1)} %collective-permute-done.1.refs_1_, bf16[2,16,2048]{2,1,0:T(8,128)(2,1)S(1)} %collective-permute-done.3.refs_2_, ...), custom_call_target="tpu_custom_call" | custom-call | flops 268435456 | bytes 3145728 | tf_op jit(solution)/shard_map/condition/pallas_call | solution.py:91
  19.1 0.1 collective-permute-start.10
  19.2 1.4 %collective-permute-start.12 = (bf16[2,4,2,16,256]{4,3,2,1,0:T(8,128)(2,1)S(1)}, bf16[2,4,2,16,256]{4,3,2,1,0:T(8,128)(2,1)S(1)}, u32[]{:S(2)}, u32[]{:S(2)}) collective-permute-start(bf16[2,4,2,16,256]{4,3,2,1,0:T(8,128)(2,1)S(1)} %condition.1.refs_1_), channel_id=1, source_target_pairs={{12,0},{13,1},{14,2},{15,3},{8,4},{9,5},{10,6},{11,7},{4,8},{5,9},... | collective-permute-start | bytes 393224 | tf_op jit(solution)/shard_map/ppermute | solution.py:21
  20.6 1.3 %collective-permute-start.8 = (bf16[2,4,2,16,256]{4,3,2,1,0:T(8,128)(2,1)S(1)}, bf16[2,4,2,16,256]{4,3,2,1,0:T(8,128)(2,1)S(1)}, u32[]{:S(2)}, u32[]{:S(2)}) collective-permute-start(bf16[2,4,2,16,256]{4,3,2,1,0:T(8,128)(2,1)S(1)} %condition.1.refs_1_), channel_id=1, source_target_pairs={{2,0},{3,1},{0,2},{1,3},{6,4},{7,5},{4,6},{5,7},{10,8},{11,9},{8,1... | collective-permute-start | bytes 393224 | tf_op jit(solution)/shard_map/ppermute | solution.py:21
  21.9 0.0 collective-permute-start.9
  21.9 3.0 %collective-permute-done.10.refs_3_ = bf16[2,4,2,16,256]{4,3,2,1,0:T(8,128)(2,1)S(1)} collective-permute-done((bf16[2,4,2,16,256]{4,3,2,1,0:T(8,128)(2,1)S(1)}, bf16[2,4,2,16,256]{4,3,2,1,0:T(8,128)(2,1)S(1)}, u32[]{:S(2)}, u32[]{:S(2)}) %collective-permute-start.10) | collective-permute-done | bytes 131104 | tf_op jit(solution)/shard_map/ppermute | solution.py:21
  24.9 0.0 collective-permute-start.11
  24.9 1.3 %collective-permute-start.18 = (bf16[2,4,2,16,256]{4,3,2,1,0:T(8,128)(2,1)S(1)}, bf16[2,4,2,16,256]{4,3,2,1,0:T(8,128)(2,1)S(1)}, u32[]{:S(2)}, u32[]{:S(2)}) collective-permute-start(bf16[2,4,2,16,256]{4,3,2,1,0:T(8,128)(2,1)S(1)} %collective-permute-done.10.refs_3_), channel_id=1, source_target_pairs={{2,0},{3,1},{0,2},{1,3},{6,4},{7,5},{4,6},{5,7},{10,8},{11,9},{8,1... | collective-permute-start | bytes 393224 | tf_op jit(solution)/shard_map/ppermute | solution.py:21
  26.2 0.8 %collective-permute-done.12.refs_1_ = bf16[2,4,2,16,256]{4,3,2,1,0:T(8,128)(2,1)S(1)} collective-permute-done((bf16[2,4,2,16,256]{4,3,2,1,0:T(8,128)(2,1)S(1)}, bf16[2,4,2,16,256]{4,3,2,1,0:T(8,128)(2,1)S(1)}, u32[]{:S(2)}, u32[]{:S(2)}) %collective-permute-start.12) | collective-permute-done | bytes 131104 | tf_op jit(solution)/shard_map/ppermute | solution.py:21
  27.0 2.6 %collective-permute-start.14 = (bf16[2,4,2,16,256]{4,3,2,1,0:T(8,128)(2,1)S(1)}, bf16[2,4,2,16,256]{4,3,2,1,0:T(8,128)(2,1)S(1)}, u32[]{:S(2)}, u32[]{:S(2)}) collective-permute-start(bf16[2,4,2,16,256]{4,3,2,1,0:T(8,128)(2,1)S(1)} %collective-permute-done.12.refs_1_), channel_id=1, source_target_pairs={{6,0},{7,1},{4,2},{5,3},{2,4},{3,5},{0,6},{1,7},{14,8},{15,9},{12,... | collective-permute-start | bytes 393224 | tf_op jit(solution)/shard_map/ppermute | solution.py:21
  29.7 0.4 collective-permute-start.15
  30.1 0.5 %collective-permute-start.16 = (bf16[2,4,2,16,256]{4,3,2,1,0:T(8,128)(2,1)S(1)}, bf16[2,4,2,16,256]{4,3,2,1,0:T(8,128)(2,1)S(1)}, u32[]{:S(2)}, u32[]{:S(2)}) collective-permute-start(bf16[2,4,2,16,256]{4,3,2,1,0:T(8,128)(2,1)S(1)} %collective-permute-done.12.refs_1_), channel_id=1, source_target_pairs={{2,0},{3,1},{0,2},{1,3},{6,4},{7,5},{4,6},{5,7},{10,8},{11,9},{8,1... | collective-permute-start | bytes 393224 | tf_op jit(solution)/shard_map/ppermute | solution.py:21
  30.6 3.0 %collective-permute-done.18.refs_4_ = bf16[2,4,2,16,256]{4,3,2,1,0:T(8,128)(2,1)S(1)} collective-permute-done((bf16[2,4,2,16,256]{4,3,2,1,0:T(8,128)(2,1)S(1)}, bf16[2,4,2,16,256]{4,3,2,1,0:T(8,128)(2,1)S(1)}, u32[]{:S(2)}, u32[]{:S(2)}) %collective-permute-start.18) | collective-permute-done | bytes 131104 | tf_op jit(solution)/shard_map/ppermute | solution.py:21
  33.6 1.3 %score.4.refs_5_ = f32[2048,512]{1,0:T(8,128)S(1)} custom-call(bf16[2048,2048]{1,0:T(8,128)(2,1)S(1)} %stage.3.refs_0_, bf16[2,4,2,16,256]{4,3,2,1,0:T(8,128)(2,1)S(1)} %condition.1.refs_1_, bf16[2,4,2,16,256]{4,3,2,1,0:T(8,128)(2,1)S(1)} %collective-permute-done.8.refs_2_, bf16[2,4,2,16,256]{4,3,2,1,0:T(8,128)(2,1)S(1)} %collective-permute-done.10.refs_3_, ...), custom_call_target="tpu_custom_call" | custom-call | flops 21474836480 | bytes 4194304 | tf_op jit(solution)/shard_map/score/pallas_call | solution.py:158
  34.9 0.6 %collective-permute-start.13 = (bf16[2,4,2,16,256]{4,3,2,1,0:T(8,128)(2,1)S(1)}, bf16[2,4,2,16,256]{4,3,2,1,0:T(8,128)(2,1)S(1)}, u32[]{:S(2)}, u32[]{:S(2)}) collective-permute-start(bf16[2,4,2,16,256]{4,3,2,1,0:T(8,128)(2,1)S(1)} %collective-permute-done.12.refs_1_), channel_id=1, source_target_pairs={{1,0},{0,1},{3,2},{2,3},{5,4},{4,5},{7,6},{6,7},{9,8},{8,9},{11,10... | collective-permute-start | bytes 393224 | tf_op jit(solution)/shard_map/ppermute | solution.py:21
  35.5 1.5 %score.5.refs_5_ = f32[2048,512]{1,0:T(8,128)S(1)} custom-call(bf16[2048,2048]{1,0:T(8,128)(2,1)S(1)} %stage.3.refs_0_, bf16[2,4,2,16,256]{4,3,2,1,0:T(8,128)(2,1)S(1)} %collective-permute-done.9.refs_1_, bf16[2,4,2,16,256]{4,3,2,1,0:T(8,128)(2,1)S(1)} %collective-permute-done.17.refs_2_, ...), custom_call_target="tpu_custom_call", output_to_operand_aliasing={{}: (5, {})} | custom-call | flops 1073741824 | bytes 4194304 | tf_op jit(solution)/shard_map/score/pallas_call | solution.py:158
  37.0 0.1 collective-permute-start.20
  37.1 0.5 %collective-permute-start.21 = (bf16[2,4,2,16,256]{4,3,2,1,0:T(8,128)(2,1)S(1)}, bf16[2,4,2,16,256]{4,3,2,1,0:T(8,128)(2,1)S(1)}, u32[]{:S(2)}, u32[]{:S(2)}) collective-permute-start(bf16[2,4,2,16,256]{4,3,2,1,0:T(8,128)(2,1)S(1)} %collective-permute-done.15.refs_3_), channel_id=1, source_target_pairs={{1,0},{0,1},{3,2},{2,3},{5,4},{4,5},{7,6},{6,7},{9,8},{8,9},{11,10... | collective-permute-start | bytes 393224 | tf_op jit(solution)/shard_map/ppermute | solution.py:21
  37.6 0.1 collective-permute-start.22
  37.7 1.5 %score.6.refs_5_ = f32[2048,512]{1,0:T(8,128)S(1)} custom-call(bf16[2048,2048]{1,0:T(8,128)(2,1)S(1)} %stage.3.refs_0_, bf16[2,4,2,16,256]{4,3,2,1,0:T(8,128)(2,1)S(1)} %collective-permute-done.12.refs_1_, bf16[2,4,2,16,256]{4,3,2,1,0:T(8,128)(2,1)S(1)} %collective-permute-done.16.refs_2_, ...), custom_call_target="tpu_custom_call", output_to_operand_aliasing={{}: (5, {})} | custom-call | flops 1073741824 | bytes 4194304 | tf_op jit(solution)/shard_map/score/pallas_call | solution.py:158
  39.2 2.9 %score.7 = f32[2048,512]{1,0:T(8,128)} custom-call(bf16[2048,2048]{1,0:T(8,128)(2,1)S(1)} %stage.3.refs_0_, bf16[2,4,2,16,256]{4,3,2,1,0:T(8,128)(2,1)S(1)} %collective-permute-done.13.refs_1_, bf16[2,4,2,16,256]{4,3,2,1,0:T(8,128)(2,1)S(1)} %collective-permute-done.20.refs_2_, bf16[2,4,2,16,256]{4,3,2,1,0:T(8,128)(2,1)S(1)} %collective-permute-done.21.refs_3_, ...), custom_call_target="tpu_custom_call" | custom-call | flops 1073741824 | bytes 4194304 | tf_op jit(solution)/shard_map/score/pallas_call | solution.py:158
  (21 shorter events, 0.1 us)
Async XLA Ops:
  0.0 9.0 %collective-permute-start = (bf16[2,16,2048]{2,1,0:T(8,128)(2,1)}, bf16[2,16,2048]{2,1,0:T(8,128)(2,1)S(1)}, u32[]{:S(2)}, u32[]{:S(2)}) collective-permute-start(bf16[2,16,2048]{2,1,0:T(8,128)(2,1)} %refs_1_.2), channel_id=1, source_target_pairs={{12,0},{13,1},{14,2},{15,3},{8,4},{9,5},{10,6},{11,7},{4,8},{5,9},... | collective-permute-start | bytes 393224 | tf_op jit(solution)/shard_map/ppermute | solution.py:21
  5.0 13.6 %collective-permute-start.7 = (bf16[1,2048,128]{2,1,0:T(8,128)(2,1)}, bf16[1,2048,128]{2,1,0:T(8,128)(2,1)S(1)}, u32[]{:S(2)}, u32[]{:S(2)}) collective-permute-start(bf16[1,2048,128]{2,1,0:T(8,128)(2,1)} %refs_2_.1), channel_id=1, source_target_pairs={{2,0},{3,1},{0,2},{1,3},{6,4},{7,5},{4,6},{5,7},{10,8},{11,9},{8,1... | collective-permute-start | bytes 1572872 | tf_op jit(solution)/shard_map/ppermute | solution.py:21
  6.6 2.4 %collective-permute-start.1 = (bf16[2,16,2048]{2,1,0:T(8,128)(2,1)}, bf16[2,16,2048]{2,1,0:T(8,128)(2,1)S(1)}, u32[]{:S(2)}, u32[]{:S(2)}) collective-permute-start(bf16[2,16,2048]{2,1,0:T(8,128)(2,1)} %refs_1_.2), channel_id=1, source_target_pairs={{1,0},{0,1},{3,2},{2,3},{5,4},{4,5},{7,6},{6,7},{9,8},{8,9},{11,10... | collective-permute-start | bytes 393224 | tf_op jit(solution)/shard_map/ppermute | solution.py:21
  6.6 6.9 %collective-permute-start.3 = (bf16[2,16,2048]{2,1,0:T(8,128)(2,1)}, bf16[2,16,2048]{2,1,0:T(8,128)(2,1)S(1)}, u32[]{:S(2)}, u32[]{:S(2)}) collective-permute-start(bf16[2,16,2048]{2,1,0:T(8,128)(2,1)} %refs_1_.2), channel_id=1, source_target_pairs={{4,0},{5,1},{6,2},{7,3},{0,4},{1,5},{2,6},{3,7},{12,8},{13,9},{14,... | collective-permute-start | bytes 393224 | tf_op jit(solution)/shard_map/ppermute | solution.py:21
  9.0 6.5 %collective-permute-start.2 = (bf16[2,16,2048]{2,1,0:T(8,128)(2,1)S(1)}, bf16[2,16,2048]{2,1,0:T(8,128)(2,1)S(1)}, u32[]{:S(2)}, u32[]{:S(2)}) collective-permute-start(bf16[2,16,2048]{2,1,0:T(8,128)(2,1)S(1)} %collective-permute-done.refs_3_), channel_id=1, source_target_pairs={{4,0},{5,1},{6,2},{7,3},{0,4},{1,5},{2,6},{3,7},{12,8},{13,9},{14,... | collective-permute-start | bytes 393224 | tf_op jit(solution)/shard_map/ppermute | solution.py:21
  11.3 4.2 %collective-permute-start.5 = (bf16[2,16,2048]{2,1,0:T(8,128)(2,1)S(1)}, bf16[2,16,2048]{2,1,0:T(8,128)(2,1)S(1)}, u32[]{:S(2)}, u32[]{:S(2)}) collective-permute-start(bf16[2,16,2048]{2,1,0:T(8,128)(2,1)S(1)} %collective-permute-done.refs_3_), channel_id=1, source_target_pairs={{1,0},{0,1},{3,2},{2,3},{5,4},{4,5},{7,6},{6,7},{9,8},{8,9},{11,10... | collective-permute-start | bytes 393224 | tf_op jit(solution)/shard_map/ppermute | solution.py:21
  13.5 2.0 %collective-permute-start.4 = (bf16[2,16,2048]{2,1,0:T(8,128)(2,1)S(1)}, bf16[2,16,2048]{2,1,0:T(8,128)(2,1)S(1)}, u32[]{:S(2)}, u32[]{:S(2)}) collective-permute-start(bf16[2,16,2048]{2,1,0:T(8,128)(2,1)S(1)} %collective-permute-done.3.refs_2_), channel_id=1, source_target_pairs={{1,0},{0,1},{3,2},{2,3},{5,4},{4,5},{7,6},{6,7},{9,8},{8,9},{11,10... | collective-permute-start | bytes 393224 | tf_op jit(solution)/shard_map/ppermute | solution.py:21
  15.5 1.3 %collective-permute-start.6 = (bf16[2,16,2048]{2,1,0:T(8,128)(2,1)S(1)}, bf16[2,16,2048]{2,1,0:T(8,128)(2,1)S(1)}, u32[]{:S(2)}, u32[]{:S(2)}) collective-permute-start(bf16[2,16,2048]{2,1,0:T(8,128)(2,1)S(1)} %collective-permute-done.2.refs_4_), channel_id=1, source_target_pairs={{1,0},{0,1},{3,2},{2,3},{5,4},{4,5},{7,6},{6,7},{9,8},{8,9},{11,10... | collective-permute-start | bytes 393224 | tf_op jit(solution)/shard_map/ppermute | solution.py:21
  19.1 5.8 %collective-permute-start.10 = (bf16[2,4,2,16,256]{4,3,2,1,0:T(8,128)(2,1)S(1)}, bf16[2,4,2,16,256]{4,3,2,1,0:T(8,128)(2,1)S(1)}, u32[]{:S(2)}, u32[]{:S(2)}) collective-permute-start(bf16[2,4,2,16,256]{4,3,2,1,0:T(8,128)(2,1)S(1)} %condition.1.refs_1_), channel_id=1, source_target_pairs={{4,0},{5,1},{6,2},{7,3},{0,4},{1,5},{2,6},{3,7},{12,8},{13,9},{14,... | collective-permute-start | bytes 393224 | tf_op jit(solution)/shard_map/ppermute | solution.py:21
  19.2 7.9 %collective-permute-start.12 = (bf16[2,4,2,16,256]{4,3,2,1,0:T(8,128)(2,1)S(1)}, bf16[2,4,2,16,256]{4,3,2,1,0:T(8,128)(2,1)S(1)}, u32[]{:S(2)}, u32[]{:S(2)}) collective-permute-start(bf16[2,4,2,16,256]{4,3,2,1,0:T(8,128)(2,1)S(1)} %condition.1.refs_1_), channel_id=1, source_target_pairs={{12,0},{13,1},{14,2},{15,3},{8,4},{9,5},{10,6},{11,7},{4,8},{5,9},... | collective-permute-start | bytes 393224 | tf_op jit(solution)/shard_map/ppermute | solution.py:21
  20.6 6.4 %collective-permute-start.8 = (bf16[2,4,2,16,256]{4,3,2,1,0:T(8,128)(2,1)S(1)}, bf16[2,4,2,16,256]{4,3,2,1,0:T(8,128)(2,1)S(1)}, u32[]{:S(2)}, u32[]{:S(2)}) collective-permute-start(bf16[2,4,2,16,256]{4,3,2,1,0:T(8,128)(2,1)S(1)} %condition.1.refs_1_), channel_id=1, source_target_pairs={{2,0},{3,1},{0,2},{1,3},{6,4},{7,5},{4,6},{5,7},{10,8},{11,9},{8,1... | collective-permute-start | bytes 393224 | tf_op jit(solution)/shard_map/ppermute | solution.py:21
  21.9 5.2 %collective-permute-start.9 = (bf16[2,4,2,16,256]{4,3,2,1,0:T(8,128)(2,1)S(1)}, bf16[2,4,2,16,256]{4,3,2,1,0:T(8,128)(2,1)S(1)}, u32[]{:S(2)}, u32[]{:S(2)}) collective-permute-start(bf16[2,4,2,16,256]{4,3,2,1,0:T(8,128)(2,1)S(1)} %condition.1.refs_1_), channel_id=1, source_target_pairs={{1,0},{0,1},{3,2},{2,3},{5,4},{4,5},{7,6},{6,7},{9,8},{8,9},{11,10... | collective-permute-start | bytes 393224 | tf_op jit(solution)/shard_map/ppermute | solution.py:21
  24.9 2.1 %collective-permute-start.11 = (bf16[2,4,2,16,256]{4,3,2,1,0:T(8,128)(2,1)S(1)}, bf16[2,4,2,16,256]{4,3,2,1,0:T(8,128)(2,1)S(1)}, u32[]{:S(2)}, u32[]{:S(2)}) collective-permute-start(bf16[2,4,2,16,256]{4,3,2,1,0:T(8,128)(2,1)S(1)} %collective-permute-done.10.refs_3_), channel_id=1, source_target_pairs={{1,0},{0,1},{3,2},{2,3},{5,4},{4,5},{7,6},{6,7},{9,8},{8,9},{11,10... | collective-permute-start | bytes 393224 | tf_op jit(solution)/shard_map/ppermute | solution.py:21
  24.9 8.7 %collective-permute-start.18 = (bf16[2,4,2,16,256]{4,3,2,1,0:T(8,128)(2,1)S(1)}, bf16[2,4,2,16,256]{4,3,2,1,0:T(8,128)(2,1)S(1)}, u32[]{:S(2)}, u32[]{:S(2)}) collective-permute-start(bf16[2,4,2,16,256]{4,3,2,1,0:T(8,128)(2,1)S(1)} %collective-permute-done.10.refs_3_), channel_id=1, source_target_pairs={{2,0},{3,1},{0,2},{1,3},{6,4},{7,5},{4,6},{5,7},{10,8},{11,9},{8,1... | collective-permute-start | bytes 393224 | tf_op jit(solution)/shard_map/ppermute | solution.py:21
  27.0 10.0 %collective-permute-start.14 = (bf16[2,4,2,16,256]{4,3,2,1,0:T(8,128)(2,1)S(1)}, bf16[2,4,2,16,256]{4,3,2,1,0:T(8,128)(2,1)S(1)}, u32[]{:S(2)}, u32[]{:S(2)}) collective-permute-start(bf16[2,4,2,16,256]{4,3,2,1,0:T(8,128)(2,1)S(1)} %collective-permute-done.12.refs_1_), channel_id=1, source_target_pairs={{6,0},{7,1},{4,2},{5,3},{2,4},{3,5},{0,6},{1,7},{14,8},{15,9},{12,... | collective-permute-start | bytes 393224 | tf_op jit(solution)/shard_map/ppermute | solution.py:21
  29.7 7.3 %collective-permute-start.15 = (bf16[2,4,2,16,256]{4,3,2,1,0:T(8,128)(2,1)S(1)}, bf16[2,4,2,16,256]{4,3,2,1,0:T(8,128)(2,1)S(1)}, u32[]{:S(2)}, u32[]{:S(2)}) collective-permute-start(bf16[2,4,2,16,256]{4,3,2,1,0:T(8,128)(2,1)S(1)} %collective-permute-done.12.refs_1_), channel_id=1, source_target_pairs={{4,0},{5,1},{6,2},{7,3},{0,4},{1,5},{2,6},{3,7},{12,8},{13,9},{14,... | collective-permute-start | bytes 393224 | tf_op jit(solution)/shard_map/ppermute | solution.py:21
  30.1 7.0 %collective-permute-start.16 = (bf16[2,4,2,16,256]{4,3,2,1,0:T(8,128)(2,1)S(1)}, bf16[2,4,2,16,256]{4,3,2,1,0:T(8,128)(2,1)S(1)}, u32[]{:S(2)}, u32[]{:S(2)}) collective-permute-start(bf16[2,4,2,16,256]{4,3,2,1,0:T(8,128)(2,1)S(1)} %collective-permute-done.12.refs_1_), channel_id=1, source_target_pairs={{2,0},{3,1},{0,2},{1,3},{6,4},{7,5},{4,6},{5,7},{10,8},{11,9},{8,1... | collective-permute-start | bytes 393224 | tf_op jit(solution)/shard_map/ppermute | solution.py:21
  30.6 4.3 %collective-permute-start.17 = (bf16[2,4,2,16,256]{4,3,2,1,0:T(8,128)(2,1)S(1)}, bf16[2,4,2,16,256]{4,3,2,1,0:T(8,128)(2,1)S(1)}, u32[]{:S(2)}, u32[]{:S(2)}) collective-permute-start(bf16[2,4,2,16,256]{4,3,2,1,0:T(8,128)(2,1)S(1)} %collective-permute-done.8.refs_2_), channel_id=1, source_target_pairs={{1,0},{0,1},{3,2},{2,3},{5,4},{4,5},{7,6},{6,7},{9,8},{8,9},{11,10... | collective-permute-start | bytes 393224 | tf_op jit(solution)/shard_map/ppermute | solution.py:21
  33.6 1.9 %collective-permute-start.19 = (bf16[2,4,2,16,256]{4,3,2,1,0:T(8,128)(2,1)S(1)}, bf16[2,4,2,16,256]{4,3,2,1,0:T(8,128)(2,1)S(1)}, u32[]{:S(2)}, u32[]{:S(2)}) collective-permute-start(bf16[2,4,2,16,256]{4,3,2,1,0:T(8,128)(2,1)S(1)} %collective-permute-done.18.refs_4_), channel_id=1, source_target_pairs={{1,0},{0,1},{3,2},{2,3},{5,4},{4,5},{7,6},{6,7},{9,8},{8,9},{11,10... | collective-permute-start | bytes 393224 | tf_op jit(solution)/shard_map/ppermute | solution.py:21
  34.9 4.3 %collective-permute-start.13 = (bf16[2,4,2,16,256]{4,3,2,1,0:T(8,128)(2,1)S(1)}, bf16[2,4,2,16,256]{4,3,2,1,0:T(8,128)(2,1)S(1)}, u32[]{:S(2)}, u32[]{:S(2)}) collective-permute-start(bf16[2,4,2,16,256]{4,3,2,1,0:T(8,128)(2,1)S(1)} %collective-permute-done.12.refs_1_), channel_id=1, source_target_pairs={{1,0},{0,1},{3,2},{2,3},{5,4},{4,5},{7,6},{6,7},{9,8},{8,9},{11,10... | collective-permute-start | bytes 393224 | tf_op jit(solution)/shard_map/ppermute | solution.py:21
  37.0 2.2 %collective-permute-start.20 = (bf16[2,4,2,16,256]{4,3,2,1,0:T(8,128)(2,1)S(1)}, bf16[2,4,2,16,256]{4,3,2,1,0:T(8,128)(2,1)S(1)}, u32[]{:S(2)}, u32[]{:S(2)}) collective-permute-start(bf16[2,4,2,16,256]{4,3,2,1,0:T(8,128)(2,1)S(1)} %collective-permute-done.16.refs_2_), channel_id=1, source_target_pairs={{1,0},{0,1},{3,2},{2,3},{5,4},{4,5},{7,6},{6,7},{9,8},{8,9},{11,10... | collective-permute-start | bytes 393224 | tf_op jit(solution)/shard_map/ppermute | solution.py:21
  37.1 2.1 %collective-permute-start.21 = (bf16[2,4,2,16,256]{4,3,2,1,0:T(8,128)(2,1)S(1)}, bf16[2,4,2,16,256]{4,3,2,1,0:T(8,128)(2,1)S(1)}, u32[]{:S(2)}, u32[]{:S(2)}) collective-permute-start(bf16[2,4,2,16,256]{4,3,2,1,0:T(8,128)(2,1)S(1)} %collective-permute-done.15.refs_3_), channel_id=1, source_target_pairs={{1,0},{0,1},{3,2},{2,3},{5,4},{4,5},{7,6},{6,7},{9,8},{8,9},{11,10... | collective-permute-start | bytes 393224 | tf_op jit(solution)/shard_map/ppermute | solution.py:21
  37.6 1.6 %collective-permute-start.22 = (bf16[2,4,2,16,256]{4,3,2,1,0:T(8,128)(2,1)S(1)}, bf16[2,4,2,16,256]{4,3,2,1,0:T(8,128)(2,1)S(1)}, u32[]{:S(2)}, u32[]{:S(2)}) collective-permute-start(bf16[2,4,2,16,256]{4,3,2,1,0:T(8,128)(2,1)S(1)} %collective-permute-done.14.refs_4_), channel_id=1, source_target_pairs={{1,0},{0,1},{3,2},{2,3},{5,4},{4,5},{7,6},{6,7},{9,8},{8,9},{11,10... | collective-permute-start | bytes 393224 | tf_op jit(solution)/shard_map/ppermute | solution.py:21

commit v15 on v14

--- a/solution.py
+++ b/solution.py
@@ -99,19 +99,48 @@
     )(*arrays)
 
 
-def score_kernel(grid, masks, other, first, last, *refs):
-    train_ref, part_refs, refs = refs[0], refs[1 : 1 + 2 * len(masks)], refs[1 + 2 * len(masks) :]
+def sort_and_turn(grid, masks, part_refs, sorted_ref):
+    _, near, _ = grid.place()
+    width = part_refs[0].shape[-1]
+    for index in range(len(masks)):
+        for side in range(2):
+            sorted_ref[:, :, pl.ds(flip(near, side), 1), :, :, index * width : (index + 1) * width] = part_refs[
+                index * 2 + side
+            ][...][:, :, None]
+    return sorted_ref[...].reshape(-1, len(masks) * width).T
+
+
+def turn_kernel(grid, masks, *refs):
+    refs[-2][...] = sort_and_turn(grid, masks, refs[:-2], refs[-1])
+
+
+def turn(grid, parts, masks):
+    arrays = [parts[mask, near, 0] for mask in masks for near in range(2)]
+    blocks, far, cores, count, width = arrays[0].shape
+    features = len(masks) * width
+    return pl.pallas_call(
+        functools.partial(turn_kernel, grid, masks),
+        out_shape=pltpu.VMEM((features, blocks * far * 2 * cores * count), jnp.bfloat16),
+        in_specs=[VMEM] * len(arrays),
+        out_specs=VMEM,
+        scratch_shapes=[pltpu.VMEM((blocks, far, 2, cores, count, features), jnp.bfloat16)],
+        compiler_params=pltpu.CompilerParams(vmem_limit_bytes=8 << 20),
+        name="turn",
+    )(*(pltpu.with_memory_space_constraint(a, pltpu.VMEM) for a in arrays))
+
+
+def score_kernel(grid, masks, other, part_count, first, last, *refs):
+    train_ref, part_refs, refs = refs[0], refs[1 : 1 + part_count], refs[1 + part_count :]
     total_ref, refs = (None, refs) if first else (refs[0], refs[1:])
-    out_ref, sorted_ref, refs = refs[0], refs[1], refs[2:]
-    far, near, core = grid.place()
+    out_ref, refs = refs[0], refs[1:]
+    far, _, core = grid.place()
     features = train_ref.shape[1]
     width = features // (grid.far * 4)
-    for index in range(len(masks)):
-        for side in range(2):
-            sorted_ref[
-                :, :, pl.ds(flip(near, side), 1), :, :, index * 2 * width : (index + 1) * 2 * width
-            ] = part_refs[index * 2 + side][...][:, :, None]
-    turned = sorted_ref[...].reshape(-1, len(masks) * 2 * width).T
+    if part_count == 1:
+        turned = part_refs[0][...]
+    else:
+        turned = sort_and_turn(grid, masks, part_refs, refs[0])
+        refs = refs[1:]
     pieces = [
         columns((flip(far, mask) * 2 + side) * 2 + flip(core, other), width) for mask in masks for side in range(2)
     ]
@@ -141,14 +170,17 @@
 
 
 def score(grid, train_feats, parts, total, masks, other, last):
-    parts = [parts[mask, near, other] for mask in masks for near in range(2)]
     rows = train_feats.shape[0]
-    blocks, far, cores, count, width = parts[0].shape
-    queries, features = blocks * far * 2 * cores * count, len(masks) * width
     first = total is None
     arrays = [train_feats, *parts] + ([] if first else [total])
+    if len(parts) == 1:
+        features, queries = parts[0].shape
+        scratch = []
+    else:
+        blocks, far, cores, count, width = parts[0].shape
+        features, queries = len(masks) * width, blocks * far * 2 * cores * count
+        scratch = [pltpu.VMEM((blocks, far, 2, cores, count, features), jnp.bfloat16)]
     shape = (rows, queries)
-    scratch = [pltpu.VMEM((blocks, far, 2, cores, count, features), jnp.bfloat16)]
     if last:
         scratch += [
             pltpu.VMEM((features, queries), jnp.bfloat16),
@@ -156,7 +188,7 @@
             pltpu.SemaphoreType.DMA((4,)),
         ]
     return pl.pallas_call(
-        functools.partial(score_kernel, grid, masks, other, first, last),
+        functools.partial(score_kernel, grid, masks, other, len(parts), first, last),
         out_shape=jax.ShapeDtypeStruct(shape, jnp.float32) if last else pltpu.VMEM(shape, jnp.float32),
         in_specs=[VMEM] * len(arrays),
         out_specs=ANY if last else VMEM,
@@ -204,25 +236,23 @@
     swap(own, *far_three)
     swap(own, *near_one)
     swap(own, *far_one)
-    swap(own, 0, 0, 1)
     swap(far_one, *near_one)
-    swap(far_one, 0, 0, 1)
-    meet(near_one, (0, 0, 1), (beside, 0, 1), far_three)
-    swap(near_one, 0, 0, 1)
-    swap(far_three, 0, 0, 1)
     swap(far_three, *near_one)
     swap(far_three, beside, 1, 0)
     swap(far_three, *far_one)
-    swap((beside, 1, 0), 0, 0, 1)
-    total = None
-    for other in range(2):
-        total = score(grid, train_here, parts, total, (0, beside), other, False)
+    turned = turn(grid, parts, (0, beside))
+    other = grid.swap(turned, 0, 0, 1)
+    total = score(grid, train_here, [turned], None, (0, beside), 0, False)
+    total = meet(far_three, total=total)
+    swap(far_three, 0, 0, 1)
+    total = score(grid, train_here, [other], total, (0, beside), 1, False)
     total = meet(far_three, (relayed, 1, 0), (relayed, 0, 0), (mirror, 1, 0), total=total)
     swap((relayed, 0, 0), 0, 0, 1)
     swap((mirror, 1, 0), 0, 0, 1)
     swap((relayed, 1, 0), 0, 0, 1)
-    for other in range(2):
-        total = score(grid, train_here, parts, total, (mirror, relayed), other, other == 1)
+    for core in range(2):
+        late = [parts[mask, near, core] for mask in (mirror, relayed) for near in range(2)]
+        total = score(grid, train_here, late, total, (mirror, relayed), core, core == 1)
     return total
 
 

time: 42.3 us -> 40.9 us (0.967)
  waiting for transfers between devices: 11.5 us -> 10.1 us
    ppermute x23 -> x20, waiting for transfers between devices: 11.5 us -> 10.1 us  [swap(): lax.ppermute(block, 'rows', [(row ^ step, row) for row in range(self.far...]
    ppermute x23 -> x20, starting transfers between devices: 18.3 us -> 18.1 us  [swap(): lax.ppermute(block, 'rows', [(row ^ step, row) for row in range(self.far...]
    pallas_call x4 -> x5, Pallas kernels: 7.22 us -> 7.3 us  [the longest x4 7.07 us: score(): pl.pallas_call(functools.partial(score_kernel, grid, masks, other, len(pa...]
  transfers between devices with their start and end apart: 23 -> 20, of which waited for: 6 -> 8; matrix products, arithmetic and copies ran while one was open for 0% -> 0% of each run, Pallas kernels for 21% -> 22%
where the time goes in v15:
time: 40.9 us; the launch traced here: 40.7 us
  starting transfers between devices  18.1 us (44%)
  Pallas kernels  12.3 us (30%)
  waiting for transfers between devices  10.1 us (25%)
    ppermute x20, starting transfers between devices, swap(): lax.ppermute(block, 'rows', [(row ^ step, row) for row in range(self.far...  18.1 us
    ppermute x20, waiting for transfers between devices, swap(): lax.ppermute(block, 'rows', [(row ^ step, row) for row in range(self.far...  10.1 us
    pallas_call x4, Pallas kernels, score(): pl.pallas_call(functools.partial(score_kernel, grid, masks, other, len(pa...  7.07 us
    pallas_call x2, Pallas kernels, stage(): pl.pallas_call(functools.partial(stage_kernel, first, arrays[0].shape[0]...  4.56 us
  transfers between devices with their start and end apart: 20, of which 8 were waited for; matrix products, arithmetic and copies ran while one was open for 0% of the time, Pallas kernels for 22%

profile of v15, /device:TPU:0, one launch (start us, length us, event | category | flops | bytes accessed | tf_op | source)
XLA Modules:
  0.0 40.7 jit_solution(13727693033964676055)
XLA Ops:
  0.0 5.0 %collective-permute-start = (bf16[2,16,2048]{2,1,0:T(8,128)(2,1)}, bf16[2,16,2048]{2,1,0:T(8,128)(2,1)S(1)}, u32[]{:S(2)}, u32[]{:S(2)}) collective-permute-start(bf16[2,16,2048]{2,1,0:T(8,128)(2,1)} %refs_1_.2), channel_id=1, source_target_pairs={{12,0},{13,1},{14,2},{15,3},{8,4},{9,5},{10,6},{11,7},{4,8},{5,9},... | collective-permute-start | bytes 393224 | tf_op jit(solution)/shard_map/ppermute | solution.py:21
  5.0 1.5 %collective-permute-start.7 = (bf16[1,2048,128]{2,1,0:T(8,128)(2,1)}, bf16[1,2048,128]{2,1,0:T(8,128)(2,1)S(1)}, u32[]{:S(2)}, u32[]{:S(2)}) collective-permute-start(bf16[1,2048,128]{2,1,0:T(8,128)(2,1)} %refs_2_.1), channel_id=1, source_target_pairs={{2,0},{3,1},{0,2},{1,3},{6,4},{7,5},{4,6},{5,7},{10,8},{11,9},{8,1... | collective-permute-start | bytes 1572872 | tf_op jit(solution)/shard_map/ppermute | solution.py:21
  6.6 0.0 collective-permute-start.1
  6.6 2.4 %stage.2 = (bf16[2048,2048]{1,0:T(8,128)(2,1)S(1)}, bf16[2,16,2048]{2,1,0:T(8,128)(2,1)S(1)}, bf16[1,2048,128]{2,1,0:T(8,128)(2,1)S(1)}) custom-call(bf16[2048,2048]{1,0:T(8,128)(2,1)} %refs_1_.3, bf16[2,16,2048]{2,1,0:T(8,128)(2,1)} %refs_1_.2, bf16[1,2048,128]{2,1,0:T(8,128)(2,1)} %refs_2_.1), custom_call_target="tpu_custom_call" | custom-call | flops 2788300032 | bytes 9043968 | tf_op jit(solution)/shard_map/stage/pallas_call | solution.py:56
  9.0 2.3 %collective-permute-start.2 = (bf16[2,16,2048]{2,1,0:T(8,128)(2,1)S(1)}, bf16[2,16,2048]{2,1,0:T(8,128)(2,1)S(1)}, u32[]{:S(2)}, u32[]{:S(2)}) collective-permute-start(bf16[2,16,2048]{2,1,0:T(8,128)(2,1)S(1)} %collective-permute-done.refs_3_), channel_id=1, source_target_pairs={{4,0},{5,1},{6,2},{7,3},{0,4},{1,5},{2,6},{3,7},{12,8},{13,9},{14,... | collective-permute-start | bytes 393224 | tf_op jit(solution)/shard_map/ppermute | solution.py:21
  11.3 2.2 %stage.3.refs_0_ = bf16[2048,2048]{1,0:T(8,128)(2,1)S(1)} custom-call(bf16[2048,2048]{1,0:T(8,128)(2,1)S(1)} %get-tuple-element.26.refs_0_, bf16[2048,2048]{1,0:T(8,128)(2,1)} %refs_1_.3), custom_call_target="tpu_custom_call", output_to_operand_aliasing={{}: (0, {})} | custom-call | flops 1 | bytes 8388608 | tf_op jit(solution)/shard_map/stage/pallas_call | solution.py:56
  13.5 0.6 %collective-permute-start.4 = (bf16[2,16,2048]{2,1,0:T(8,128)(2,1)S(1)}, bf16[2,16,2048]{2,1,0:T(8,128)(2,1)S(1)}, u32[]{:S(2)}, u32[]{:S(2)}) collective-permute-start(bf16[2,16,2048]{2,1,0:T(8,128)(2,1)S(1)} %collective-permute-done.3.refs_2_), channel_id=1, source_target_pairs={{1,0},{0,1},{3,2},{2,3},{5,4},{4,5},{7,6},{6,7},{9,8},{8,9},{11,10... | collective-permute-start | bytes 393224 | tf_op jit(solution)/shard_map/ppermute | solution.py:21
  14.1 1.4 %collective-permute-done.2.refs_4_ = bf16[2,16,2048]{2,1,0:T(8,128)(2,1)S(1)} collective-permute-done((bf16[2,16,2048]{2,1,0:T(8,128)(2,1)S(1)}, bf16[2,16,2048]{2,1,0:T(8,128)(2,1)S(1)}, u32[]{:S(2)}, u32[]{:S(2)}) %collective-permute-start.2) | collective-permute-done | bytes 131104 | tf_op jit(solution)/shard_map/ppermute | solution.py:21
  15.5 1.3 %collective-permute-done.6.refs_7_ = bf16[2,16,2048]{2,1,0:T(8,128)(2,1)S(1)} collective-permute-done((bf16[2,16,2048]{2,1,0:T(8,128)(2,1)S(1)}, bf16[2,16,2048]{2,1,0:T(8,128)(2,1)S(1)}, u32[]{:S(2)}, u32[]{:S(2)}) %collective-permute-start.6) | collective-permute-done | bytes 131104 | tf_op jit(solution)/shard_map/ppermute | solution.py:21
  16.9 1.8 %collective-permute-done.7.refs_9_ = bf16[1,2048,128]{2,1,0:T(8,128)(2,1)S(1)} collective-permute-done((bf16[1,2048,128]{2,1,0:T(8,128)(2,1)}, bf16[1,2048,128]{2,1,0:T(8,128)(2,1)S(1)}, u32[]{:S(2)}, u32[]{:S(2)}) %collective-permute-start.7) | collective-permute-done | bytes 524320 | tf_op jit(solution)/shard_map/ppermute | solution.py:21
  18.6 0.4 %condition.1.refs_0_ = bf16[2,4,2,16,256]{4,3,2,1,0:T(8,128)(2,1)S(1)} custom-call(bf16[2,16,2048]{2,1,0:T(8,128)(2,1)S(1)} %get-tuple-element.28.refs_0_, bf16[2,16,2048]{2,1,0:T(8,128)(2,1)S(1)} %collective-permute-done.1.refs_1_, bf16[2,16,2048]{2,1,0:T(8,128)(2,1)S(1)} %collective-permute-done.3.refs_2_, ...), custom_call_target="tpu_custom_call" | custom-call | flops 268435456 | bytes 3145728 | tf_op jit(solution)/shard_map/condition/pallas_call | solution.py:91
  19.1 0.1 collective-permute-start.10
  19.2 1.4 %collective-permute-start.8 = (bf16[2,4,2,16,256]{4,3,2,1,0:T(8,128)(2,1)S(1)}, bf16[2,4,2,16,256]{4,3,2,1,0:T(8,128)(2,1)S(1)}, u32[]{:S(2)}, u32[]{:S(2)}) collective-permute-start(bf16[2,4,2,16,256]{4,3,2,1,0:T(8,128)(2,1)S(1)} %condition.1.refs_0_), channel_id=1, source_target_pairs={{12,0},{13,1},{14,2},{15,3},{8,4},{9,5},{10,6},{11,7},{4,8},{5,9},... | collective-permute-start | bytes 393224 | tf_op jit(solution)/shard_map/ppermute | solution.py:21
  20.6 1.3 %collective-permute-start.9 = (bf16[2,4,2,16,256]{4,3,2,1,0:T(8,128)(2,1)S(1)}, bf16[2,4,2,16,256]{4,3,2,1,0:T(8,128)(2,1)S(1)}, u32[]{:S(2)}, u32[]{:S(2)}) collective-permute-start(bf16[2,4,2,16,256]{4,3,2,1,0:T(8,128)(2,1)S(1)} %condition.1.refs_0_), channel_id=1, source_target_pairs={{2,0},{3,1},{0,2},{1,3},{6,4},{7,5},{4,6},{5,7},{10,8},{11,9},{8,1... | collective-permute-start | bytes 393224 | tf_op jit(solution)/shard_map/ppermute | solution.py:21
  21.9 3.0 %collective-permute-done.10.refs_2_ = bf16[2,4,2,16,256]{4,3,2,1,0:T(8,128)(2,1)S(1)} collective-permute-done((bf16[2,4,2,16,256]{4,3,2,1,0:T(8,128)(2,1)S(1)}, bf16[2,4,2,16,256]{4,3,2,1,0:T(8,128)(2,1)S(1)}, u32[]{:S(2)}, u32[]{:S(2)}) %collective-permute-start.10) | collective-permute-done | bytes 131104 | tf_op jit(solution)/shard_map/ppermute | solution.py:21
  24.9 1.3 %collective-permute-start.11 = (bf16[2,4,2,16,256]{4,3,2,1,0:T(8,128)(2,1)S(1)}, bf16[2,4,2,16,256]{4,3,2,1,0:T(8,128)(2,1)S(1)}, u32[]{:S(2)}, u32[]{:S(2)}) collective-permute-start(bf16[2,4,2,16,256]{4,3,2,1,0:T(8,128)(2,1)S(1)} %collective-permute-done.10.refs_2_), channel_id=1, source_target_pairs={{2,0},{3,1},{0,2},{1,3},{6,4},{7,5},{4,6},{5,7},{10,8},{11,9},{8,1... | collective-permute-start | bytes 393224 | tf_op jit(solution)/shard_map/ppermute | solution.py:21
  26.2 0.9 %collective-permute-done.8.refs_1_ = bf16[2,4,2,16,256]{4,3,2,1,0:T(8,128)(2,1)S(1)} collective-permute-done((bf16[2,4,2,16,256]{4,3,2,1,0:T(8,128)(2,1)S(1)}, bf16[2,4,2,16,256]{4,3,2,1,0:T(8,128)(2,1)S(1)}, u32[]{:S(2)}, u32[]{:S(2)}) %collective-permute-start.8) | collective-permute-done | bytes 131104 | tf_op jit(solution)/shard_map/ppermute | solution.py:21
  27.0 2.6 %collective-permute-start.13 = (bf16[2,4,2,16,256]{4,3,2,1,0:T(8,128)(2,1)S(1)}, bf16[2,4,2,16,256]{4,3,2,1,0:T(8,128)(2,1)S(1)}, u32[]{:S(2)}, u32[]{:S(2)}) collective-permute-start(bf16[2,4,2,16,256]{4,3,2,1,0:T(8,128)(2,1)S(1)} %collective-permute-done.8.refs_1_), channel_id=1, source_target_pairs={{6,0},{7,1},{4,2},{5,3},{2,4},{3,5},{0,6},{1,7},{14,8},{15,9},{12,... | collective-permute-start | bytes 393224 | tf_op jit(solution)/shard_map/ppermute | solution.py:21
  29.6 0.4 collective-permute-start.14
  30.0 0.5 %collective-permute-start.15 = (bf16[2,4,2,16,256]{4,3,2,1,0:T(8,128)(2,1)S(1)}, bf16[2,4,2,16,256]{4,3,2,1,0:T(8,128)(2,1)S(1)}, u32[]{:S(2)}, u32[]{:S(2)}) collective-permute-start(bf16[2,4,2,16,256]{4,3,2,1,0:T(8,128)(2,1)S(1)} %collective-permute-done.8.refs_1_), channel_id=1, source_target_pairs={{2,0},{3,1},{0,2},{1,3},{6,4},{7,5},{4,6},{5,7},{10,8},{11,9},{8,1... | collective-permute-start | bytes 393224 | tf_op jit(solution)/shard_map/ppermute | solution.py:21
  30.5 0.2 turn.1.refs_1_
  30.8 0.1 collective-permute-start.16
  30.9 1.3 %score.4.refs_2_ = f32[2048,512]{1,0:T(8,128)S(1)} custom-call(bf16[2048,2048]{1,0:T(8,128)(2,1)S(1)} %stage.3.refs_0_, bf16[512,512]{1,0:T(8,128)(2,1)S(1)} %turn.1.refs_1_), custom_call_target="tpu_custom_call" | custom-call | flops 21474836480 | bytes 4194304 | tf_op jit(solution)/shard_map/score/pallas_call | solution.py:190
  32.1 0.6 %collective-permute-start.12 = (bf16[2,4,2,16,256]{4,3,2,1,0:T(8,128)(2,1)S(1)}, bf16[2,4,2,16,256]{4,3,2,1,0:T(8,128)(2,1)S(1)}, u32[]{:S(2)}, u32[]{:S(2)}) collective-permute-start(bf16[2,4,2,16,256]{4,3,2,1,0:T(8,128)(2,1)S(1)} %collective-permute-done.8.refs_1_), channel_id=1, source_target_pairs={{1,0},{0,1},{3,2},{2,3},{5,4},{4,5},{7,6},{6,7},{9,8},{8,9},{11,10... | collective-permute-start | bytes 393224 | tf_op jit(solution)/shard_map/ppermute | solution.py:21
  32.7 0.1 collective-permute-done.16.refs_1_
  32.7 1.4 %score.5.refs_5_ = f32[2048,512]{1,0:T(8,128)S(1)} custom-call(bf16[2048,2048]{1,0:T(8,128)(2,1)S(1)} %stage.3.refs_0_, bf16[512,512]{1,0:T(8,128)(2,1)S(1)} %collective-permute-done.16.refs_1_, f32[2048,512]{1,0:T(8,128)S(1)} %score.4.refs_2_), custom_call_target="tpu_custom_call", output_to_operand_aliasing={{}: (2, {})} | custom-call | flops 1073741824 | bytes 4194304 | tf_op jit(solution)/shard_map/score/pallas_call | solution.py:190
  34.2 1.5 %collective-permute-done.14.refs_3_ = bf16[2,4,2,16,256]{4,3,2,1,0:T(8,128)(2,1)S(1)} collective-permute-done((bf16[2,4,2,16,256]{4,3,2,1,0:T(8,128)(2,1)S(1)}, bf16[2,4,2,16,256]{4,3,2,1,0:T(8,128)(2,1)S(1)}, u32[]{:S(2)}, u32[]{:S(2)}) %collective-permute-start.14) | collective-permute-done | bytes 131104 | tf_op jit(solution)/shard_map/ppermute | solution.py:21
  35.7 0.1 collective-permute-done.15.refs_2_
  35.8 0.5 %collective-permute-start.18 = (bf16[2,4,2,16,256]{4,3,2,1,0:T(8,128)(2,1)S(1)}, bf16[2,4,2,16,256]{4,3,2,1,0:T(8,128)(2,1)S(1)}, u32[]{:S(2)}, u32[]{:S(2)}) collective-permute-start(bf16[2,4,2,16,256]{4,3,2,1,0:T(8,128)(2,1)S(1)} %collective-permute-done.14.refs_3_), channel_id=1, source_target_pairs={{1,0},{0,1},{3,2},{2,3},{5,4},{4,5},{7,6},{6,7},{9,8},{8,9},{11,10... | collective-permute-start | bytes 393224 | tf_op jit(solution)/shard_map/ppermute | solution.py:21
  36.3 0.0 collective-permute-start.19
  36.3 1.5 %score.6.refs_5_ = f32[2048,512]{1,0:T(8,128)S(1)} custom-call(bf16[2048,2048]{1,0:T(8,128)(2,1)S(1)} %stage.3.refs_0_, bf16[2,4,2,16,256]{4,3,2,1,0:T(8,128)(2,1)S(1)} %collective-permute-done.8.refs_1_, bf16[2,4,2,16,256]{4,3,2,1,0:T(8,128)(2,1)S(1)} %collective-permute-done.15.refs_2_, ...), custom_call_target="tpu_custom_call", output_to_operand_aliasing={{}: (5, {})} | custom-call | flops 1073741824 | bytes 4194304 | tf_op jit(solution)/shard_map/score/pallas_call | solution.py:190
  37.8 2.9 %score.7 = f32[2048,512]{1,0:T(8,128)} custom-call(bf16[2048,2048]{1,0:T(8,128)(2,1)S(1)} %stage.3.refs_0_, bf16[2,4,2,16,256]{4,3,2,1,0:T(8,128)(2,1)S(1)} %collective-permute-done.12.refs_1_, bf16[2,4,2,16,256]{4,3,2,1,0:T(8,128)(2,1)S(1)} %collective-permute-done.17.refs_2_, bf16[2,4,2,16,256]{4,3,2,1,0:T(8,128)(2,1)S(1)} %collective-permute-done.18.refs_3_, ...), custom_call_target="tpu_custom_call" | custom-call | flops 1073741824 | bytes 4194304 | tf_op jit(solution)/shard_map/score/pallas_call | solution.py:190
  (16 shorter events, 0.0 us)
Async XLA Ops:
  0.0 9.0 %collective-permute-start = (bf16[2,16,2048]{2,1,0:T(8,128)(2,1)}, bf16[2,16,2048]{2,1,0:T(8,128)(2,1)S(1)}, u32[]{:S(2)}, u32[]{:S(2)}) collective-permute-start(bf16[2,16,2048]{2,1,0:T(8,128)(2,1)} %refs_1_.2), channel_id=1, source_target_pairs={{12,0},{13,1},{14,2},{15,3},{8,4},{9,5},{10,6},{11,7},{4,8},{5,9},... | collective-permute-start | bytes 393224 | tf_op jit(solution)/shard_map/ppermute | solution.py:21
  5.0 13.6 %collective-permute-start.7 = (bf16[1,2048,128]{2,1,0:T(8,128)(2,1)}, bf16[1,2048,128]{2,1,0:T(8,128)(2,1)S(1)}, u32[]{:S(2)}, u32[]{:S(2)}) collective-permute-start(bf16[1,2048,128]{2,1,0:T(8,128)(2,1)} %refs_2_.1), channel_id=1, source_target_pairs={{2,0},{3,1},{0,2},{1,3},{6,4},{7,5},{4,6},{5,7},{10,8},{11,9},{8,1... | collective-permute-start | bytes 1572872 | tf_op jit(solution)/shard_map/ppermute | solution.py:21
  6.6 2.4 %collective-permute-start.1 = (bf16[2,16,2048]{2,1,0:T(8,128)(2,1)}, bf16[2,16,2048]{2,1,0:T(8,128)(2,1)S(1)}, u32[]{:S(2)}, u32[]{:S(2)}) collective-permute-start(bf16[2,16,2048]{2,1,0:T(8,128)(2,1)} %refs_1_.2), channel_id=1, source_target_pairs={{1,0},{0,1},{3,2},{2,3},{5,4},{4,5},{7,6},{6,7},{9,8},{8,9},{11,10... | collective-permute-start | bytes 393224 | tf_op jit(solution)/shard_map/ppermute | solution.py:21
  6.6 6.9 %collective-permute-start.3 = (bf16[2,16,2048]{2,1,0:T(8,128)(2,1)}, bf16[2,16,2048]{2,1,0:T(8,128)(2,1)S(1)}, u32[]{:S(2)}, u32[]{:S(2)}) collective-permute-start(bf16[2,16,2048]{2,1,0:T(8,128)(2,1)} %refs_1_.2), channel_id=1, source_target_pairs={{4,0},{5,1},{6,2},{7,3},{0,4},{1,5},{2,6},{3,7},{12,8},{13,9},{14,... | collective-permute-start | bytes 393224 | tf_op jit(solution)/shard_map/ppermute | solution.py:21
  9.0 6.5 %collective-permute-start.2 = (bf16[2,16,2048]{2,1,0:T(8,128)(2,1)S(1)}, bf16[2,16,2048]{2,1,0:T(8,128)(2,1)S(1)}, u32[]{:S(2)}, u32[]{:S(2)}) collective-permute-start(bf16[2,16,2048]{2,1,0:T(8,128)(2,1)S(1)} %collective-permute-done.refs_3_), channel_id=1, source_target_pairs={{4,0},{5,1},{6,2},{7,3},{0,4},{1,5},{2,6},{3,7},{12,8},{13,9},{14,... | collective-permute-start | bytes 393224 | tf_op jit(solution)/shard_map/ppermute | solution.py:21
  11.3 4.2 %collective-permute-start.5 = (bf16[2,16,2048]{2,1,0:T(8,128)(2,1)S(1)}, bf16[2,16,2048]{2,1,0:T(8,128)(2,1)S(1)}, u32[]{:S(2)}, u32[]{:S(2)}) collective-permute-start(bf16[2,16,2048]{2,1,0:T(8,128)(2,1)S(1)} %collective-permute-done.refs_3_), channel_id=1, source_target_pairs={{1,0},{0,1},{3,2},{2,3},{5,4},{4,5},{7,6},{6,7},{9,8},{8,9},{11,10... | collective-permute-start | bytes 393224 | tf_op jit(solution)/shard_map/ppermute | solution.py:21
  13.5 2.0 %collective-permute-start.4 = (bf16[2,16,2048]{2,1,0:T(8,128)(2,1)S(1)}, bf16[2,16,2048]{2,1,0:T(8,128)(2,1)S(1)}, u32[]{:S(2)}, u32[]{:S(2)}) collective-permute-start(bf16[2,16,2048]{2,1,0:T(8,128)(2,1)S(1)} %collective-permute-done.3.refs_2_), channel_id=1, source_target_pairs={{1,0},{0,1},{3,2},{2,3},{5,4},{4,5},{7,6},{6,7},{9,8},{8,9},{11,10... | collective-permute-start | bytes 393224 | tf_op jit(solution)/shard_map/ppermute | solution.py:21
  15.5 1.3 %collective-permute-start.6 = (bf16[2,16,2048]{2,1,0:T(8,128)(2,1)S(1)}, bf16[2,16,2048]{2,1,0:T(8,128)(2,1)S(1)}, u32[]{:S(2)}, u32[]{:S(2)}) collective-permute-start(bf16[2,16,2048]{2,1,0:T(8,128)(2,1)S(1)} %collective-permute-done.2.refs_4_), channel_id=1, source_target_pairs={{1,0},{0,1},{3,2},{2,3},{5,4},{4,5},{7,6},{6,7},{9,8},{8,9},{11,10... | collective-permute-start | bytes 393224 | tf_op jit(solution)/shard_map/ppermute | solution.py:21
  19.1 5.8 %collective-permute-start.10 = (bf16[2,4,2,16,256]{4,3,2,1,0:T(8,128)(2,1)S(1)}, bf16[2,4,2,16,256]{4,3,2,1,0:T(8,128)(2,1)S(1)}, u32[]{:S(2)}, u32[]{:S(2)}) collective-permute-start(bf16[2,4,2,16,256]{4,3,2,1,0:T(8,128)(2,1)S(1)} %condition.1.refs_0_), channel_id=1, source_target_pairs={{4,0},{5,1},{6,2},{7,3},{0,4},{1,5},{2,6},{3,7},{12,8},{13,9},{14,... | collective-permute-start | bytes 393224 | tf_op jit(solution)/shard_map/ppermute | solution.py:21
  19.2 7.9 %collective-permute-start.8 = (bf16[2,4,2,16,256]{4,3,2,1,0:T(8,128)(2,1)S(1)}, bf16[2,4,2,16,256]{4,3,2,1,0:T(8,128)(2,1)S(1)}, u32[]{:S(2)}, u32[]{:S(2)}) collective-permute-start(bf16[2,4,2,16,256]{4,3,2,1,0:T(8,128)(2,1)S(1)} %condition.1.refs_0_), channel_id=1, source_target_pairs={{12,0},{13,1},{14,2},{15,3},{8,4},{9,5},{10,6},{11,7},{4,8},{5,9},... | collective-permute-start | bytes 393224 | tf_op jit(solution)/shard_map/ppermute | solution.py:21
  20.6 9.9 %collective-permute-start.9 = (bf16[2,4,2,16,256]{4,3,2,1,0:T(8,128)(2,1)S(1)}, bf16[2,4,2,16,256]{4,3,2,1,0:T(8,128)(2,1)S(1)}, u32[]{:S(2)}, u32[]{:S(2)}) collective-permute-start(bf16[2,4,2,16,256]{4,3,2,1,0:T(8,128)(2,1)S(1)} %condition.1.refs_0_), channel_id=1, source_target_pairs={{2,0},{3,1},{0,2},{1,3},{6,4},{7,5},{4,6},{5,7},{10,8},{11,9},{8,1... | collective-permute-start | bytes 393224 | tf_op jit(solution)/shard_map/ppermute | solution.py:21
  24.9 5.6 %collective-permute-start.11 = (bf16[2,4,2,16,256]{4,3,2,1,0:T(8,128)(2,1)S(1)}, bf16[2,4,2,16,256]{4,3,2,1,0:T(8,128)(2,1)S(1)}, u32[]{:S(2)}, u32[]{:S(2)}) collective-permute-start(bf16[2,4,2,16,256]{4,3,2,1,0:T(8,128)(2,1)S(1)} %collective-permute-done.10.refs_2_), channel_id=1, source_target_pairs={{2,0},{3,1},{0,2},{1,3},{6,4},{7,5},{4,6},{5,7},{10,8},{11,9},{8,1... | collective-permute-start | bytes 393224 | tf_op jit(solution)/shard_map/ppermute | solution.py:21
  27.0 7.1 %collective-permute-start.13 = (bf16[2,4,2,16,256]{4,3,2,1,0:T(8,128)(2,1)S(1)}, bf16[2,4,2,16,256]{4,3,2,1,0:T(8,128)(2,1)S(1)}, u32[]{:S(2)}, u32[]{:S(2)}) collective-permute-start(bf16[2,4,2,16,256]{4,3,2,1,0:T(8,128)(2,1)S(1)} %collective-permute-done.8.refs_1_), channel_id=1, source_target_pairs={{6,0},{7,1},{4,2},{5,3},{2,4},{3,5},{0,6},{1,7},{14,8},{15,9},{12,... | collective-permute-start | bytes 393224 | tf_op jit(solution)/shard_map/ppermute | solution.py:21
  29.6 6.1 %collective-permute-start.14 = (bf16[2,4,2,16,256]{4,3,2,1,0:T(8,128)(2,1)S(1)}, bf16[2,4,2,16,256]{4,3,2,1,0:T(8,128)(2,1)S(1)}, u32[]{:S(2)}, u32[]{:S(2)}) collective-permute-start(bf16[2,4,2,16,256]{4,3,2,1,0:T(8,128)(2,1)S(1)} %collective-permute-done.8.refs_1_), channel_id=1, source_target_pairs={{4,0},{5,1},{6,2},{7,3},{0,4},{1,5},{2,6},{3,7},{12,8},{13,9},{14,... | collective-permute-start | bytes 393224 | tf_op jit(solution)/shard_map/ppermute | solution.py:21
  30.0 5.8 %collective-permute-start.15 = (bf16[2,4,2,16,256]{4,3,2,1,0:T(8,128)(2,1)S(1)}, bf16[2,4,2,16,256]{4,3,2,1,0:T(8,128)(2,1)S(1)}, u32[]{:S(2)}, u32[]{:S(2)}) collective-permute-start(bf16[2,4,2,16,256]{4,3,2,1,0:T(8,128)(2,1)S(1)} %collective-permute-done.8.refs_1_), channel_id=1, source_target_pairs={{2,0},{3,1},{0,2},{1,3},{6,4},{7,5},{4,6},{5,7},{10,8},{11,9},{8,1... | collective-permute-start | bytes 393224 | tf_op jit(solution)/shard_map/ppermute | solution.py:21
  30.8 2.0 %collective-permute-start.16 = (bf16[512,512]{1,0:T(8,128)(2,1)S(1)}, bf16[512,512]{1,0:T(8,128)(2,1)S(1)}, u32[]{:S(2)}, u32[]{:S(2)}) collective-permute-start(bf16[512,512]{1,0:T(8,128)(2,1)S(1)} %turn.1.refs_1_), channel_id=1, source_target_pairs={{1,0},{0,1},{3,2},{2,3},{5,4},{4,5},{7,6},{6,7},{9,8},{8,9},{11,10... | collective-permute-start | bytes 1572872 | tf_op jit(solution)/shard_map/ppermute | solution.py:21
  32.1 5.7 %collective-permute-start.12 = (bf16[2,4,2,16,256]{4,3,2,1,0:T(8,128)(2,1)S(1)}, bf16[2,4,2,16,256]{4,3,2,1,0:T(8,128)(2,1)S(1)}, u32[]{:S(2)}, u32[]{:S(2)}) collective-permute-start(bf16[2,4,2,16,256]{4,3,2,1,0:T(8,128)(2,1)S(1)} %collective-permute-done.8.refs_1_), channel_id=1, source_target_pairs={{1,0},{0,1},{3,2},{2,3},{5,4},{4,5},{7,6},{6,7},{9,8},{8,9},{11,10... | collective-permute-start | bytes 393224 | tf_op jit(solution)/shard_map/ppermute | solution.py:21
  35.8 2.0 %collective-permute-start.17 = (bf16[2,4,2,16,256]{4,3,2,1,0:T(8,128)(2,1)S(1)}, bf16[2,4,2,16,256]{4,3,2,1,0:T(8,128)(2,1)S(1)}, u32[]{:S(2)}, u32[]{:S(2)}) collective-permute-start(bf16[2,4,2,16,256]{4,3,2,1,0:T(8,128)(2,1)S(1)} %collective-permute-done.15.refs_2_), channel_id=1, source_target_pairs={{1,0},{0,1},{3,2},{2,3},{5,4},{4,5},{7,6},{6,7},{9,8},{8,9},{11,10... | collective-permute-start | bytes 393224 | tf_op jit(solution)/shard_map/ppermute | solution.py:21
  35.8 2.0 %collective-permute-start.18 = (bf16[2,4,2,16,256]{4,3,2,1,0:T(8,128)(2,1)S(1)}, bf16[2,4,2,16,256]{4,3,2,1,0:T(8,128)(2,1)S(1)}, u32[]{:S(2)}, u32[]{:S(2)}) collective-permute-start(bf16[2,4,2,16,256]{4,3,2,1,0:T(8,128)(2,1)S(1)} %collective-permute-done.14.refs_3_), channel_id=1, source_target_pairs={{1,0},{0,1},{3,2},{2,3},{5,4},{4,5},{7,6},{6,7},{9,8},{8,9},{11,10... | collective-permute-start | bytes 393224 | tf_op jit(solution)/shard_map/ppermute | solution.py:21
  36.3 1.5 %collective-permute-start.19 = (bf16[2,4,2,16,256]{4,3,2,1,0:T(8,128)(2,1)S(1)}, bf16[2,4,2,16,256]{4,3,2,1,0:T(8,128)(2,1)S(1)}, u32[]{:S(2)}, u32[]{:S(2)}) collective-permute-start(bf16[2,4,2,16,256]{4,3,2,1,0:T(8,128)(2,1)S(1)} %collective-permute-done.13.refs_4_), channel_id=1, source_target_pairs={{1,0},{0,1},{3,2},{2,3},{5,4},{4,5},{7,6},{6,7},{9,8},{8,9},{11,10... | collective-permute-start | bytes 393224 | tf_op jit(solution)/shard_map/ppermute | solution.py:21

commit v16 on v15

--- a/solution.py
+++ b/solution.py
@@ -9,7 +9,7 @@
 
 VMEM = pl.BlockSpec(memory_space=pltpu.VMEM)
 ANY = pl.BlockSpec(memory_space=pl.ANY)
-ORDER_FLOPS = 2_788_300_000
+ORDER_FLOPS = 4_186_300_000
 
 
 class Grid:
@@ -215,12 +215,13 @@
     )
     train_here, gathered[0, 0], fisher_here = staged
     gathered[relayed, 0] = grid.swap(gathered[mirror, 0], beside, 0, 0)
+    gathered[relayed, 1] = grid.swap(gathered[mirror, 0], beside, 0, 1)
     (train_here,) = stage([train_feats], train_here)
     for mask in (beside, mirror):
         gathered[mask, 1] = grid.swap(gathered[mask, 0], 0, 0, 1)
-    gathered[relayed, 0], train_here = lax.optimization_barrier((gathered[relayed, 0], train_here))
-    gathered[relayed, 1] = grid.swap(gathered[relayed, 0], 0, 0, 1)
-
+    gathered[relayed, 0], gathered[relayed, 1], train_here = lax.optimization_barrier(
+        (gathered[relayed, 0], gathered[relayed, 1], train_here)
+    )
     parts = {(0, 0, 0): condition(grid, gathered, fisher_here, near_fisher)}
 
     def swap(source, *step):

time: 40.9 us -> 42.5 us (1.039)
  starting transfers between devices: 18.1 us -> 19.2 us
  waiting for transfers between devices: 10.1 us -> 10.7 us
    ppermute x20, starting transfers between devices: 18.1 us -> 19.2 us  [swap(): lax.ppermute(block, 'rows', [(row ^ step, row) for row in range(self.far...]
    ppermute x20, waiting for transfers between devices: 10.1 us -> 10.7 us  [swap(): lax.ppermute(block, 'rows', [(row ^ step, row) for row in range(self.far...]
  transfers between devices with their start and end apart: 20 -> 20, of which waited for: 8 -> 10; matrix products, arithmetic and copies ran while one was open for 0% -> 0% of each run, Pallas kernels for 22% -> 21%
where the time goes in v16:
time: 42.5 us; the launch traced here: 42.3 us
  starting transfers between devices  19.2 us (45%)
  Pallas kernels  12.3 us (29%)
  waiting for transfers between devices  10.7 us (25%)
    ppermute x20, starting transfers between devices, swap(): lax.ppermute(block, 'rows', [(row ^ step, row) for row in range(self.far...  19.2 us
    ppermute x20, waiting for transfers between devices, swap(): lax.ppermute(block, 'rows', [(row ^ step, row) for row in range(self.far...  10.7 us
    pallas_call x4, Pallas kernels, score(): pl.pallas_call(functools.partial(score_kernel, grid, masks, other, len(pa...  7.07 us
    pallas_call x2, Pallas kernels, stage(): pl.pallas_call(functools.partial(stage_kernel, first, arrays[0].shape[0]...  4.56 us
  transfers between devices with their start and end apart: 20, of which 10 were waited for; matrix products, arithmetic and copies ran while one was open for 0% of the time, Pallas kernels for 21%

profile of v16, /device:TPU:0, one launch (start us, length us, event | category | flops | bytes accessed | tf_op | source)
XLA Modules:
  0.0 42.3 jit_solution(298945543252294505)
XLA Ops:
  0.0 5.0 %collective-permute-start = (bf16[2,16,2048]{2,1,0:T(8,128)(2,1)}, bf16[2,16,2048]{2,1,0:T(8,128)(2,1)S(1)}, u32[]{:S(2)}, u32[]{:S(2)}) collective-permute-start(bf16[2,16,2048]{2,1,0:T(8,128)(2,1)} %refs_1_.2), channel_id=1, source_target_pairs={{12,0},{13,1},{14,2},{15,3},{8,4},{9,5},{10,6},{11,7},{4,8},{5,9},... | collective-permute-start | bytes 393224 | tf_op jit(solution)/shard_map/ppermute | solution.py:21
  5.0 1.5 %collective-permute-start.7 = (bf16[1,2048,128]{2,1,0:T(8,128)(2,1)}, bf16[1,2048,128]{2,1,0:T(8,128)(2,1)S(1)}, u32[]{:S(2)}, u32[]{:S(2)}) collective-permute-start(bf16[1,2048,128]{2,1,0:T(8,128)(2,1)} %refs_2_.1), channel_id=1, source_target_pairs={{2,0},{3,1},{0,2},{1,3},{6,4},{7,5},{4,6},{5,7},{10,8},{11,9},{8,1... | collective-permute-start | bytes 1572872 | tf_op jit(solution)/shard_map/ppermute | solution.py:21
  6.6 2.4 %stage.2 = (bf16[2048,2048]{1,0:T(8,128)(2,1)S(1)}, bf16[2,16,2048]{2,1,0:T(8,128)(2,1)S(1)}, bf16[1,2048,128]{2,1,0:T(8,128)(2,1)S(1)}) custom-call(bf16[2048,2048]{1,0:T(8,128)(2,1)} %refs_1_.3, bf16[2,16,2048]{2,1,0:T(8,128)(2,1)} %refs_1_.2, bf16[1,2048,128]{2,1,0:T(8,128)(2,1)} %refs_2_.1), custom_call_target="tpu_custom_call" | custom-call | flops 4186299904 | bytes 9043968 | tf_op jit(solution)/shard_map/stage/pallas_call | solution.py:56
  9.0 2.3 %collective-permute-start.2 = (bf16[2,16,2048]{2,1,0:T(8,128)(2,1)S(1)}, bf16[2,16,2048]{2,1,0:T(8,128)(2,1)S(1)}, u32[]{:S(2)}, u32[]{:S(2)}) collective-permute-start(bf16[2,16,2048]{2,1,0:T(8,128)(2,1)S(1)} %collective-permute-done.refs_3_), channel_id=1, source_target_pairs={{4,0},{5,1},{6,2},{7,3},{0,4},{1,5},{2,6},{3,7},{12,8},{13,9},{14,... | collective-permute-start | bytes 393224 | tf_op jit(solution)/shard_map/ppermute | solution.py:21
  11.3 0.1 collective-permute-start.6
  11.4 1.6 %collective-permute-done.4.refs_2_ = bf16[2,16,2048]{2,1,0:T(8,128)(2,1)S(1)} collective-permute-done((bf16[2,16,2048]{2,1,0:T(8,128)(2,1)}, bf16[2,16,2048]{2,1,0:T(8,128)(2,1)S(1)}, u32[]{:S(2)}, u32[]{:S(2)}) %collective-permute-start.4) | collective-permute-done | bytes 131104 | tf_op jit(solution)/shard_map/ppermute | solution.py:21
  13.1 2.2 %stage.3.refs_0_ = bf16[2048,2048]{1,0:T(8,128)(2,1)S(1)} custom-call(bf16[2048,2048]{1,0:T(8,128)(2,1)S(1)} %get-tuple-element.27.refs_0_, bf16[2048,2048]{1,0:T(8,128)(2,1)} %refs_1_.3), custom_call_target="tpu_custom_call", output_to_operand_aliasing={{}: (0, {})} | custom-call | flops 1 | bytes 8388608 | tf_op jit(solution)/shard_map/stage/pallas_call | solution.py:56
  15.3 0.6 %collective-permute-done.2.refs_4_ = bf16[2,16,2048]{2,1,0:T(8,128)(2,1)S(1)} collective-permute-done((bf16[2,16,2048]{2,1,0:T(8,128)(2,1)S(1)}, bf16[2,16,2048]{2,1,0:T(8,128)(2,1)S(1)}, u32[]{:S(2)}, u32[]{:S(2)}) %collective-permute-start.2) | collective-permute-done | bytes 131104 | tf_op jit(solution)/shard_map/ppermute | solution.py:21
  15.9 2.0 %collective-permute-done.3.refs_5_ = bf16[2,16,2048]{2,1,0:T(8,128)(2,1)S(1)} collective-permute-done((bf16[2,16,2048]{2,1,0:T(8,128)(2,1)S(1)}, bf16[2,16,2048]{2,1,0:T(8,128)(2,1)S(1)}, u32[]{:S(2)}, u32[]{:S(2)}) %collective-permute-start.3) | collective-permute-done | bytes 131104 | tf_op jit(solution)/shard_map/ppermute | solution.py:21
  17.9 0.7 %collective-permute-done.7.refs_9_ = bf16[1,2048,128]{2,1,0:T(8,128)(2,1)S(1)} collective-permute-done((bf16[1,2048,128]{2,1,0:T(8,128)(2,1)}, bf16[1,2048,128]{2,1,0:T(8,128)(2,1)S(1)}, u32[]{:S(2)}, u32[]{:S(2)}) %collective-permute-start.7) | collective-permute-done | bytes 524320 | tf_op jit(solution)/shard_map/ppermute | solution.py:21
  18.6 0.4 %condition.1.refs_0_ = bf16[2,4,2,16,256]{4,3,2,1,0:T(8,128)(2,1)S(1)} custom-call(bf16[2,16,2048]{2,1,0:T(8,128)(2,1)S(1)} %get-tuple-element.29.refs_0_, bf16[2,16,2048]{2,1,0:T(8,128)(2,1)S(1)} %collective-permute-done.1.refs_1_, bf16[2,16,2048]{2,1,0:T(8,128)(2,1)S(1)} %collective-permute-done.4.refs_2_, ...), custom_call_target="tpu_custom_call" | custom-call | flops 268435456 | bytes 3145728 | tf_op jit(solution)/shard_map/condition/pallas_call | solution.py:91
  19.1 0.1 collective-permute-start.10
  19.2 1.8 %collective-permute-start.8 = (bf16[2,4,2,16,256]{4,3,2,1,0:T(8,128)(2,1)S(1)}, bf16[2,4,2,16,256]{4,3,2,1,0:T(8,128)(2,1)S(1)}, u32[]{:S(2)}, u32[]{:S(2)}) collective-permute-start(bf16[2,4,2,16,256]{4,3,2,1,0:T(8,128)(2,1)S(1)} %condition.1.refs_0_), channel_id=1, source_target_pairs={{12,0},{13,1},{14,2},{15,3},{8,4},{9,5},{10,6},{11,7},{4,8},{5,9},... | collective-permute-start | bytes 393224 | tf_op jit(solution)/shard_map/ppermute | solution.py:21
  20.9 2.4 %collective-permute-start.9 = (bf16[2,4,2,16,256]{4,3,2,1,0:T(8,128)(2,1)S(1)}, bf16[2,4,2,16,256]{4,3,2,1,0:T(8,128)(2,1)S(1)}, u32[]{:S(2)}, u32[]{:S(2)}) collective-permute-start(bf16[2,4,2,16,256]{4,3,2,1,0:T(8,128)(2,1)S(1)} %condition.1.refs_0_), channel_id=1, source_target_pairs={{2,0},{3,1},{0,2},{1,3},{6,4},{7,5},{4,6},{5,7},{10,8},{11,9},{8,1... | collective-permute-start | bytes 393224 | tf_op jit(solution)/shard_map/ppermute | solution.py:21
  23.3 1.0 %collective-permute-done.10.refs_2_ = bf16[2,4,2,16,256]{4,3,2,1,0:T(8,128)(2,1)S(1)} collective-permute-done((bf16[2,4,2,16,256]{4,3,2,1,0:T(8,128)(2,1)S(1)}, bf16[2,4,2,16,256]{4,3,2,1,0:T(8,128)(2,1)S(1)}, u32[]{:S(2)}, u32[]{:S(2)}) %collective-permute-start.10) | collective-permute-done | bytes 131104 | tf_op jit(solution)/shard_map/ppermute | solution.py:21
  24.4 1.3 %collective-permute-start.11 = (bf16[2,4,2,16,256]{4,3,2,1,0:T(8,128)(2,1)S(1)}, bf16[2,4,2,16,256]{4,3,2,1,0:T(8,128)(2,1)S(1)}, u32[]{:S(2)}, u32[]{:S(2)}) collective-permute-start(bf16[2,4,2,16,256]{4,3,2,1,0:T(8,128)(2,1)S(1)} %collective-permute-done.10.refs_2_), channel_id=1, source_target_pairs={{2,0},{3,1},{0,2},{1,3},{6,4},{7,5},{4,6},{5,7},{10,8},{11,9},{8,1... | collective-permute-start | bytes 393224 | tf_op jit(solution)/shard_map/ppermute | solution.py:21
  25.6 2.5 %collective-permute-done.8.refs_1_ = bf16[2,4,2,16,256]{4,3,2,1,0:T(8,128)(2,1)S(1)} collective-permute-done((bf16[2,4,2,16,256]{4,3,2,1,0:T(8,128)(2,1)S(1)}, bf16[2,4,2,16,256]{4,3,2,1,0:T(8,128)(2,1)S(1)}, u32[]{:S(2)}, u32[]{:S(2)}) %collective-permute-start.8) | collective-permute-done | bytes 131104 | tf_op jit(solution)/shard_map/ppermute | solution.py:21
  28.2 1.7 %collective-permute-start.13 = (bf16[2,4,2,16,256]{4,3,2,1,0:T(8,128)(2,1)S(1)}, bf16[2,4,2,16,256]{4,3,2,1,0:T(8,128)(2,1)S(1)}, u32[]{:S(2)}, u32[]{:S(2)}) collective-permute-start(bf16[2,4,2,16,256]{4,3,2,1,0:T(8,128)(2,1)S(1)} %collective-permute-done.8.refs_1_), channel_id=1, source_target_pairs={{6,0},{7,1},{4,2},{5,3},{2,4},{3,5},{0,6},{1,7},{14,8},{15,9},{12,... | collective-permute-start | bytes 393224 | tf_op jit(solution)/shard_map/ppermute | solution.py:21
  29.9 1.2 %collective-permute-start.14 = (bf16[2,4,2,16,256]{4,3,2,1,0:T(8,128)(2,1)S(1)}, bf16[2,4,2,16,256]{4,3,2,1,0:T(8,128)(2,1)S(1)}, u32[]{:S(2)}, u32[]{:S(2)}) collective-permute-start(bf16[2,4,2,16,256]{4,3,2,1,0:T(8,128)(2,1)S(1)} %collective-permute-done.8.refs_1_), channel_id=1, source_target_pairs={{4,0},{5,1},{6,2},{7,3},{0,4},{1,5},{2,6},{3,7},{12,8},{13,9},{14,... | collective-permute-start | bytes 393224 | tf_op jit(solution)/shard_map/ppermute | solution.py:21
  31.1 0.5 %collective-permute-start.15 = (bf16[2,4,2,16,256]{4,3,2,1,0:T(8,128)(2,1)S(1)}, bf16[2,4,2,16,256]{4,3,2,1,0:T(8,128)(2,1)S(1)}, u32[]{:S(2)}, u32[]{:S(2)}) collective-permute-start(bf16[2,4,2,16,256]{4,3,2,1,0:T(8,128)(2,1)S(1)} %collective-permute-done.8.refs_1_), channel_id=1, source_target_pairs={{2,0},{3,1},{0,2},{1,3},{6,4},{7,5},{4,6},{5,7},{10,8},{11,9},{8,1... | collective-permute-start | bytes 393224 | tf_op jit(solution)/shard_map/ppermute | solution.py:21
  31.7 0.2 turn.1.refs_1_
  31.9 0.1 collective-permute-start.16
  32.0 1.3 %score.4.refs_2_ = f32[2048,512]{1,0:T(8,128)S(1)} custom-call(bf16[2048,2048]{1,0:T(8,128)(2,1)S(1)} %stage.3.refs_0_, bf16[512,512]{1,0:T(8,128)(2,1)S(1)} %turn.1.refs_1_), custom_call_target="tpu_custom_call" | custom-call | flops 21474836480 | bytes 4194304 | tf_op jit(solution)/shard_map/score/pallas_call | solution.py:190
  33.3 0.6 %collective-permute-start.12 = (bf16[2,4,2,16,256]{4,3,2,1,0:T(8,128)(2,1)S(1)}, bf16[2,4,2,16,256]{4,3,2,1,0:T(8,128)(2,1)S(1)}, u32[]{:S(2)}, u32[]{:S(2)}) collective-permute-start(bf16[2,4,2,16,256]{4,3,2,1,0:T(8,128)(2,1)S(1)} %collective-permute-done.8.refs_1_), channel_id=1, source_target_pairs={{1,0},{0,1},{3,2},{2,3},{5,4},{4,5},{7,6},{6,7},{9,8},{8,9},{11,10... | collective-permute-start | bytes 393224 | tf_op jit(solution)/shard_map/ppermute | solution.py:21
  33.8 0.1 collective-permute-done.16.refs_1_
  33.9 1.4 %score.5.refs_5_ = f32[2048,512]{1,0:T(8,128)S(1)} custom-call(bf16[2048,2048]{1,0:T(8,128)(2,1)S(1)} %stage.3.refs_0_, bf16[512,512]{1,0:T(8,128)(2,1)S(1)} %collective-permute-done.16.refs_1_, f32[2048,512]{1,0:T(8,128)S(1)} %score.4.refs_2_), custom_call_target="tpu_custom_call", output_to_operand_aliasing={{}: (2, {})} | custom-call | flops 1073741824 | bytes 4194304 | tf_op jit(solution)/shard_map/score/pallas_call | solution.py:190
  35.3 0.1 collective-permute-done.13.refs_4_
  35.4 1.1 %collective-permute-done.14.refs_3_ = bf16[2,4,2,16,256]{4,3,2,1,0:T(8,128)(2,1)S(1)} collective-permute-done((bf16[2,4,2,16,256]{4,3,2,1,0:T(8,128)(2,1)S(1)}, bf16[2,4,2,16,256]{4,3,2,1,0:T(8,128)(2,1)S(1)}, u32[]{:S(2)}, u32[]{:S(2)}) %collective-permute-start.14) | collective-permute-done | bytes 131104 | tf_op jit(solution)/shard_map/ppermute | solution.py:21
  36.5 0.8 %collective-permute-done.15.refs_2_ = bf16[2,4,2,16,256]{4,3,2,1,0:T(8,128)(2,1)S(1)} collective-permute-done((bf16[2,4,2,16,256]{4,3,2,1,0:T(8,128)(2,1)S(1)}, bf16[2,4,2,16,256]{4,3,2,1,0:T(8,128)(2,1)S(1)}, u32[]{:S(2)}, u32[]{:S(2)}) %collective-permute-start.15) | collective-permute-done | bytes 131104 | tf_op jit(solution)/shard_map/ppermute | solution.py:21
  37.3 0.5 %collective-permute-start.18 = (bf16[2,4,2,16,256]{4,3,2,1,0:T(8,128)(2,1)S(1)}, bf16[2,4,2,16,256]{4,3,2,1,0:T(8,128)(2,1)S(1)}, u32[]{:S(2)}, u32[]{:S(2)}) collective-permute-start(bf16[2,4,2,16,256]{4,3,2,1,0:T(8,128)(2,1)S(1)} %collective-permute-done.14.refs_3_), channel_id=1, source_target_pairs={{1,0},{0,1},{3,2},{2,3},{5,4},{4,5},{7,6},{6,7},{9,8},{8,9},{11,10... | collective-permute-start | bytes 393224 | tf_op jit(solution)/shard_map/ppermute | solution.py:21
  37.8 1.5 %score.6.refs_5_ = f32[2048,512]{1,0:T(8,128)S(1)} custom-call(bf16[2048,2048]{1,0:T(8,128)(2,1)S(1)} %stage.3.refs_0_, bf16[2,4,2,16,256]{4,3,2,1,0:T(8,128)(2,1)S(1)} %collective-permute-done.8.refs_1_, bf16[2,4,2,16,256]{4,3,2,1,0:T(8,128)(2,1)S(1)} %collective-permute-done.15.refs_2_, ...), custom_call_target="tpu_custom_call", output_to_operand_aliasing={{}: (5, {})} | custom-call | flops 1073741824 | bytes 4194304 | tf_op jit(solution)/shard_map/score/pallas_call | solution.py:190
  39.4 2.9 %score.7 = f32[2048,512]{1,0:T(8,128)} custom-call(bf16[2048,2048]{1,0:T(8,128)(2,1)S(1)} %stage.3.refs_0_, bf16[2,4,2,16,256]{4,3,2,1,0:T(8,128)(2,1)S(1)} %collective-permute-done.12.refs_1_, bf16[2,4,2,16,256]{4,3,2,1,0:T(8,128)(2,1)S(1)} %collective-permute-done.17.refs_2_, bf16[2,4,2,16,256]{4,3,2,1,0:T(8,128)(2,1)S(1)} %collective-permute-done.18.refs_3_, ...), custom_call_target="tpu_custom_call" | custom-call | flops 1073741824 | bytes 4194304 | tf_op jit(solution)/shard_map/score/pallas_call | solution.py:190
  (16 shorter events, 0.0 us)
Async XLA Ops:
  0.0 9.0 %collective-permute-start = (bf16[2,16,2048]{2,1,0:T(8,128)(2,1)}, bf16[2,16,2048]{2,1,0:T(8,128)(2,1)S(1)}, u32[]{:S(2)}, u32[]{:S(2)}) collective-permute-start(bf16[2,16,2048]{2,1,0:T(8,128)(2,1)} %refs_1_.2), channel_id=1, source_target_pairs={{12,0},{13,1},{14,2},{15,3},{8,4},{9,5},{10,6},{11,7},{4,8},{5,9},... | collective-permute-start | bytes 393224 | tf_op jit(solution)/shard_map/ppermute | solution.py:21
  5.0 13.6 %collective-permute-start.7 = (bf16[1,2048,128]{2,1,0:T(8,128)(2,1)}, bf16[1,2048,128]{2,1,0:T(8,128)(2,1)S(1)}, u32[]{:S(2)}, u32[]{:S(2)}) collective-permute-start(bf16[1,2048,128]{2,1,0:T(8,128)(2,1)} %refs_2_.1), channel_id=1, source_target_pairs={{2,0},{3,1},{0,2},{1,3},{6,4},{7,5},{4,6},{5,7},{10,8},{11,9},{8,1... | collective-permute-start | bytes 1572872 | tf_op jit(solution)/shard_map/ppermute | solution.py:21
  6.6 2.4 %collective-permute-start.1 = (bf16[2,16,2048]{2,1,0:T(8,128)(2,1)}, bf16[2,16,2048]{2,1,0:T(8,128)(2,1)S(1)}, u32[]{:S(2)}, u32[]{:S(2)}) collective-permute-start(bf16[2,16,2048]{2,1,0:T(8,128)(2,1)} %refs_1_.2), channel_id=1, source_target_pairs={{1,0},{0,1},{3,2},{2,3},{5,4},{4,5},{7,6},{6,7},{9,8},{8,9},{11,10... | collective-permute-start | bytes 393224 | tf_op jit(solution)/shard_map/ppermute | solution.py:21
  6.6 6.5 %collective-permute-start.4 = (bf16[2,16,2048]{2,1,0:T(8,128)(2,1)}, bf16[2,16,2048]{2,1,0:T(8,128)(2,1)S(1)}, u32[]{:S(2)}, u32[]{:S(2)}) collective-permute-start(bf16[2,16,2048]{2,1,0:T(8,128)(2,1)} %refs_1_.2), channel_id=1, source_target_pairs={{4,0},{5,1},{6,2},{7,3},{0,4},{1,5},{2,6},{3,7},{12,8},{13,9},{14,... | collective-permute-start | bytes 393224 | tf_op jit(solution)/shard_map/ppermute | solution.py:21
  9.0 6.9 %collective-permute-start.2 = (bf16[2,16,2048]{2,1,0:T(8,128)(2,1)S(1)}, bf16[2,16,2048]{2,1,0:T(8,128)(2,1)S(1)}, u32[]{:S(2)}, u32[]{:S(2)}) collective-permute-start(bf16[2,16,2048]{2,1,0:T(8,128)(2,1)S(1)} %collective-permute-done.refs_3_), channel_id=1, source_target_pairs={{4,0},{5,1},{6,2},{7,3},{0,4},{1,5},{2,6},{3,7},{12,8},{13,9},{14,... | collective-permute-start | bytes 393224 | tf_op jit(solution)/shard_map/ppermute | solution.py:21
  11.3 6.6 %collective-permute-start.3 = (bf16[2,16,2048]{2,1,0:T(8,128)(2,1)S(1)}, bf16[2,16,2048]{2,1,0:T(8,128)(2,1)S(1)}, u32[]{:S(2)}, u32[]{:S(2)}) collective-permute-start(bf16[2,16,2048]{2,1,0:T(8,128)(2,1)S(1)} %collective-permute-done.refs_3_), channel_id=1, source_target_pairs={{5,0},{4,1},{7,2},{6,3},{1,4},{0,5},{3,6},{2,7},{13,8},{12,9},{15,... | collective-permute-start | bytes 393224 | tf_op jit(solution)/shard_map/ppermute | solution.py:21
  11.3 6.6 %collective-permute-start.6 = (bf16[2,16,2048]{2,1,0:T(8,128)(2,1)S(1)}, bf16[2,16,2048]{2,1,0:T(8,128)(2,1)S(1)}, u32[]{:S(2)}, u32[]{:S(2)}) collective-permute-start(bf16[2,16,2048]{2,1,0:T(8,128)(2,1)S(1)} %collective-permute-done.refs_3_), channel_id=1, source_target_pairs={{1,0},{0,1},{3,2},{2,3},{5,4},{4,5},{7,6},{6,7},{9,8},{8,9},{11,10... | collective-permute-start | bytes 393224 | tf_op jit(solution)/shard_map/ppermute | solution.py:21
  13.1 4.8 %collective-permute-start.5 = (bf16[2,16,2048]{2,1,0:T(8,128)(2,1)S(1)}, bf16[2,16,2048]{2,1,0:T(8,128)(2,1)S(1)}, u32[]{:S(2)}, u32[]{:S(2)}) collective-permute-start(bf16[2,16,2048]{2,1,0:T(8,128)(2,1)S(1)} %collective-permute-done.4.refs_2_), channel_id=1, source_target_pairs={{1,0},{0,1},{3,2},{2,3},{5,4},{4,5},{7,6},{6,7},{9,8},{8,9},{11,10... | collective-permute-start | bytes 393224 | tf_op jit(solution)/shard_map/ppermute | solution.py:21
  19.1 5.3 %collective-permute-start.10 = (bf16[2,4,2,16,256]{4,3,2,1,0:T(8,128)(2,1)S(1)}, bf16[2,4,2,16,256]{4,3,2,1,0:T(8,128)(2,1)S(1)}, u32[]{:S(2)}, u32[]{:S(2)}) collective-permute-start(bf16[2,4,2,16,256]{4,3,2,1,0:T(8,128)(2,1)S(1)} %condition.1.refs_0_), channel_id=1, source_target_pairs={{4,0},{5,1},{6,2},{7,3},{0,4},{1,5},{2,6},{3,7},{12,8},{13,9},{14,... | collective-permute-start | bytes 393224 | tf_op jit(solution)/shard_map/ppermute | solution.py:21
  19.2 9.0 %collective-permute-start.8 = (bf16[2,4,2,16,256]{4,3,2,1,0:T(8,128)(2,1)S(1)}, bf16[2,4,2,16,256]{4,3,2,1,0:T(8,128)(2,1)S(1)}, u32[]{:S(2)}, u32[]{:S(2)}) collective-permute-start(bf16[2,4,2,16,256]{4,3,2,1,0:T(8,128)(2,1)S(1)} %condition.1.refs_0_), channel_id=1, source_target_pairs={{12,0},{13,1},{14,2},{15,3},{8,4},{9,5},{10,6},{11,7},{4,8},{5,9},... | collective-permute-start | bytes 393224 | tf_op jit(solution)/shard_map/ppermute | solution.py:21
  20.9 10.7 %collective-permute-start.9 = (bf16[2,4,2,16,256]{4,3,2,1,0:T(8,128)(2,1)S(1)}, bf16[2,4,2,16,256]{4,3,2,1,0:T(8,128)(2,1)S(1)}, u32[]{:S(2)}, u32[]{:S(2)}) collective-permute-start(bf16[2,4,2,16,256]{4,3,2,1,0:T(8,128)(2,1)S(1)} %condition.1.refs_0_), channel_id=1, source_target_pairs={{2,0},{3,1},{0,2},{1,3},{6,4},{7,5},{4,6},{5,7},{10,8},{11,9},{8,1... | collective-permute-start | bytes 393224 | tf_op jit(solution)/shard_map/ppermute | solution.py:21
  24.4 7.3 %collective-permute-start.11 = (bf16[2,4,2,16,256]{4,3,2,1,0:T(8,128)(2,1)S(1)}, bf16[2,4,2,16,256]{4,3,2,1,0:T(8,128)(2,1)S(1)}, u32[]{:S(2)}, u32[]{:S(2)}) collective-permute-start(bf16[2,4,2,16,256]{4,3,2,1,0:T(8,128)(2,1)S(1)} %collective-permute-done.10.refs_2_), channel_id=1, source_target_pairs={{2,0},{3,1},{0,2},{1,3},{6,4},{7,5},{4,6},{5,7},{10,8},{11,9},{8,1... | collective-permute-start | bytes 393224 | tf_op jit(solution)/shard_map/ppermute | solution.py:21
  28.2 7.3 %collective-permute-start.13 = (bf16[2,4,2,16,256]{4,3,2,1,0:T(8,128)(2,1)S(1)}, bf16[2,4,2,16,256]{4,3,2,1,0:T(8,128)(2,1)S(1)}, u32[]{:S(2)}, u32[]{:S(2)}) collective-permute-start(bf16[2,4,2,16,256]{4,3,2,1,0:T(8,128)(2,1)S(1)} %collective-permute-done.8.refs_1_), channel_id=1, source_target_pairs={{6,0},{7,1},{4,2},{5,3},{2,4},{3,5},{0,6},{1,7},{14,8},{15,9},{12,... | collective-permute-start | bytes 393224 | tf_op jit(solution)/shard_map/ppermute | solution.py:21
  29.9 6.6 %collective-permute-start.14 = (bf16[2,4,2,16,256]{4,3,2,1,0:T(8,128)(2,1)S(1)}, bf16[2,4,2,16,256]{4,3,2,1,0:T(8,128)(2,1)S(1)}, u32[]{:S(2)}, u32[]{:S(2)}) collective-permute-start(bf16[2,4,2,16,256]{4,3,2,1,0:T(8,128)(2,1)S(1)} %collective-permute-done.8.refs_1_), channel_id=1, source_target_pairs={{4,0},{5,1},{6,2},{7,3},{0,4},{1,5},{2,6},{3,7},{12,8},{13,9},{14,... | collective-permute-start | bytes 393224 | tf_op jit(solution)/shard_map/ppermute | solution.py:21
  31.1 6.2 %collective-permute-start.15 = (bf16[2,4,2,16,256]{4,3,2,1,0:T(8,128)(2,1)S(1)}, bf16[2,4,2,16,256]{4,3,2,1,0:T(8,128)(2,1)S(1)}, u32[]{:S(2)}, u32[]{:S(2)}) collective-permute-start(bf16[2,4,2,16,256]{4,3,2,1,0:T(8,128)(2,1)S(1)} %collective-permute-done.8.refs_1_), channel_id=1, source_target_pairs={{2,0},{3,1},{0,2},{1,3},{6,4},{7,5},{4,6},{5,7},{10,8},{11,9},{8,1... | collective-permute-start | bytes 393224 | tf_op jit(solution)/shard_map/ppermute | solution.py:21
  31.9 2.0 %collective-permute-start.16 = (bf16[512,512]{1,0:T(8,128)(2,1)S(1)}, bf16[512,512]{1,0:T(8,128)(2,1)S(1)}, u32[]{:S(2)}, u32[]{:S(2)}) collective-permute-start(bf16[512,512]{1,0:T(8,128)(2,1)S(1)} %turn.1.refs_1_), channel_id=1, source_target_pairs={{1,0},{0,1},{3,2},{2,3},{5,4},{4,5},{7,6},{6,7},{9,8},{8,9},{11,10... | collective-permute-start | bytes 1572872 | tf_op jit(solution)/shard_map/ppermute | solution.py:21
  33.3 6.1 %collective-permute-start.12 = (bf16[2,4,2,16,256]{4,3,2,1,0:T(8,128)(2,1)S(1)}, bf16[2,4,2,16,256]{4,3,2,1,0:T(8,128)(2,1)S(1)}, u32[]{:S(2)}, u32[]{:S(2)}) collective-permute-start(bf16[2,4,2,16,256]{4,3,2,1,0:T(8,128)(2,1)S(1)} %collective-permute-done.8.refs_1_), channel_id=1, source_target_pairs={{1,0},{0,1},{3,2},{2,3},{5,4},{4,5},{7,6},{6,7},{9,8},{8,9},{11,10... | collective-permute-start | bytes 393224 | tf_op jit(solution)/shard_map/ppermute | solution.py:21
  37.3 2.0 %collective-permute-start.17 = (bf16[2,4,2,16,256]{4,3,2,1,0:T(8,128)(2,1)S(1)}, bf16[2,4,2,16,256]{4,3,2,1,0:T(8,128)(2,1)S(1)}, u32[]{:S(2)}, u32[]{:S(2)}) collective-permute-start(bf16[2,4,2,16,256]{4,3,2,1,0:T(8,128)(2,1)S(1)} %collective-permute-done.15.refs_2_), channel_id=1, source_target_pairs={{1,0},{0,1},{3,2},{2,3},{5,4},{4,5},{7,6},{6,7},{9,8},{8,9},{11,10... | collective-permute-start | bytes 393224 | tf_op jit(solution)/shard_map/ppermute | solution.py:21
  37.3 2.0 %collective-permute-start.18 = (bf16[2,4,2,16,256]{4,3,2,1,0:T(8,128)(2,1)S(1)}, bf16[2,4,2,16,256]{4,3,2,1,0:T(8,128)(2,1)S(1)}, u32[]{:S(2)}, u32[]{:S(2)}) collective-permute-start(bf16[2,4,2,16,256]{4,3,2,1,0:T(8,128)(2,1)S(1)} %collective-permute-done.14.refs_3_), channel_id=1, source_target_pairs={{1,0},{0,1},{3,2},{2,3},{5,4},{4,5},{7,6},{6,7},{9,8},{8,9},{11,10... | collective-permute-start | bytes 393224 | tf_op jit(solution)/shard_map/ppermute | solution.py:21
  37.8 1.5 %collective-permute-start.19 = (bf16[2,4,2,16,256]{4,3,2,1,0:T(8,128)(2,1)S(1)}, bf16[2,4,2,16,256]{4,3,2,1,0:T(8,128)(2,1)S(1)}, u32[]{:S(2)}, u32[]{:S(2)}) collective-permute-start(bf16[2,4,2,16,256]{4,3,2,1,0:T(8,128)(2,1)S(1)} %collective-permute-done.13.refs_4_), channel_id=1, source_target_pairs={{1,0},{0,1},{3,2},{2,3},{5,4},{4,5},{7,6},{6,7},{9,8},{8,9},{11,10... | collective-permute-start | bytes 393224 | tf_op jit(solution)/shard_map/ppermute | solution.py:21

commit v17 on v15

--- a/solution.py
+++ b/solution.py
@@ -246,7 +246,7 @@
     total = meet(far_three, total=total)
     swap(far_three, 0, 0, 1)
     total = score(grid, train_here, [other], total, (0, beside), 1, False)
-    total = meet(far_three, (relayed, 1, 0), (relayed, 0, 0), (mirror, 1, 0), total=total)
+    total = meet(far_three, (relayed, 0, 0), (mirror, 1, 0), (relayed, 1, 0), total=total)
     swap((relayed, 0, 0), 0, 0, 1)
     swap((mirror, 1, 0), 0, 0, 1)
     swap((relayed, 1, 0), 0, 0, 1)

time: 40.9 us -> 41.2 us (level)
  no operation moved by 1% of the time
where the time goes in v17:
time: 41.2 us; the launch traced here: 41 us
  starting transfers between devices  18.1 us (44%)
  Pallas kernels  12.3 us (30%)
  waiting for transfers between devices  10.4 us (25%)
    ppermute x20, starting transfers between devices, swap(): lax.ppermute(block, 'rows', [(row ^ step, row) for row in range(self.far...  18.1 us
    ppermute x20, waiting for transfers between devices, swap(): lax.ppermute(block, 'rows', [(row ^ step, row) for row in range(self.far...  10.4 us
    pallas_call x4, Pallas kernels, score(): pl.pallas_call(functools.partial(score_kernel, grid, masks, other, len(pa...  7.07 us
    pallas_call x2, Pallas kernels, stage(): pl.pallas_call(functools.partial(stage_kernel, first, arrays[0].shape[0]...  4.56 us
  transfers between devices with their start and end apart: 20, of which 8 were waited for; matrix products, arithmetic and copies ran while one was open for 0% of the time, Pallas kernels for 22%

profile of v17, /device:TPU:0, one launch (start us, length us, event | category | flops | bytes accessed | tf_op | source)
XLA Modules:
  0.0 41.0 jit_solution(2424186846872088094)
XLA Ops:
  0.0 5.0 %collective-permute-start = (bf16[2,16,2048]{2,1,0:T(8,128)(2,1)}, bf16[2,16,2048]{2,1,0:T(8,128)(2,1)S(1)}, u32[]{:S(2)}, u32[]{:S(2)}) collective-permute-start(bf16[2,16,2048]{2,1,0:T(8,128)(2,1)} %refs_1_.2), channel_id=1, source_target_pairs={{12,0},{13,1},{14,2},{15,3},{8,4},{9,5},{10,6},{11,7},{4,8},{5,9},... | collective-permute-start | bytes 393224 | tf_op jit(solution)/shard_map/ppermute | solution.py:21
  5.0 1.5 %collective-permute-start.7 = (bf16[1,2048,128]{2,1,0:T(8,128)(2,1)}, bf16[1,2048,128]{2,1,0:T(8,128)(2,1)S(1)}, u32[]{:S(2)}, u32[]{:S(2)}) collective-permute-start(bf16[1,2048,128]{2,1,0:T(8,128)(2,1)} %refs_2_.1), channel_id=1, source_target_pairs={{2,0},{3,1},{0,2},{1,3},{6,4},{7,5},{4,6},{5,7},{10,8},{11,9},{8,1... | collective-permute-start | bytes 1572872 | tf_op jit(solution)/shard_map/ppermute | solution.py:21
  6.6 0.0 collective-permute-start.1
  6.6 2.4 %stage.2 = (bf16[2048,2048]{1,0:T(8,128)(2,1)S(1)}, bf16[2,16,2048]{2,1,0:T(8,128)(2,1)S(1)}, bf16[1,2048,128]{2,1,0:T(8,128)(2,1)S(1)}) custom-call(bf16[2048,2048]{1,0:T(8,128)(2,1)} %refs_1_.3, bf16[2,16,2048]{2,1,0:T(8,128)(2,1)} %refs_1_.2, bf16[1,2048,128]{2,1,0:T(8,128)(2,1)} %refs_2_.1), custom_call_target="tpu_custom_call" | custom-call | flops 2788300032 | bytes 9043968 | tf_op jit(solution)/shard_map/stage/pallas_call | solution.py:56
  9.0 2.3 %collective-permute-start.2 = (bf16[2,16,2048]{2,1,0:T(8,128)(2,1)S(1)}, bf16[2,16,2048]{2,1,0:T(8,128)(2,1)S(1)}, u32[]{:S(2)}, u32[]{:S(2)}) collective-permute-start(bf16[2,16,2048]{2,1,0:T(8,128)(2,1)S(1)} %collective-permute-done.refs_3_), channel_id=1, source_target_pairs={{4,0},{5,1},{6,2},{7,3},{0,4},{1,5},{2,6},{3,7},{12,8},{13,9},{14,... | collective-permute-start | bytes 393224 | tf_op jit(solution)/shard_map/ppermute | solution.py:21
  11.3 2.2 %stage.3.refs_0_ = bf16[2048,2048]{1,0:T(8,128)(2,1)S(1)} custom-call(bf16[2048,2048]{1,0:T(8,128)(2,1)S(1)} %get-tuple-element.26.refs_0_, bf16[2048,2048]{1,0:T(8,128)(2,1)} %refs_1_.3), custom_call_target="tpu_custom_call", output_to_operand_aliasing={{}: (0, {})} | custom-call | flops 1 | bytes 8388608 | tf_op jit(solution)/shard_map/stage/pallas_call | solution.py:56
  13.5 0.6 %collective-permute-start.4 = (bf16[2,16,2048]{2,1,0:T(8,128)(2,1)S(1)}, bf16[2,16,2048]{2,1,0:T(8,128)(2,1)S(1)}, u32[]{:S(2)}, u32[]{:S(2)}) collective-permute-start(bf16[2,16,2048]{2,1,0:T(8,128)(2,1)S(1)} %collective-permute-done.3.refs_2_), channel_id=1, source_target_pairs={{1,0},{0,1},{3,2},{2,3},{5,4},{4,5},{7,6},{6,7},{9,8},{8,9},{11,10... | collective-permute-start | bytes 393224 | tf_op jit(solution)/shard_map/ppermute | solution.py:21
  14.1 1.4 %collective-permute-done.2.refs_4_ = bf16[2,16,2048]{2,1,0:T(8,128)(2,1)S(1)} collective-permute-done((bf16[2,16,2048]{2,1,0:T(8,128)(2,1)S(1)}, bf16[2,16,2048]{2,1,0:T(8,128)(2,1)S(1)}, u32[]{:S(2)}, u32[]{:S(2)}) %collective-permute-start.2) | collective-permute-done | bytes 131104 | tf_op jit(solution)/shard_map/ppermute | solution.py:21
  15.5 1.3 %collective-permute-done.6.refs_7_ = bf16[2,16,2048]{2,1,0:T(8,128)(2,1)S(1)} collective-permute-done((bf16[2,16,2048]{2,1,0:T(8,128)(2,1)S(1)}, bf16[2,16,2048]{2,1,0:T(8,128)(2,1)S(1)}, u32[]{:S(2)}, u32[]{:S(2)}) %collective-permute-start.6) | collective-permute-done | bytes 131104 | tf_op jit(solution)/shard_map/ppermute | solution.py:21
  16.9 1.8 %collective-permute-done.7.refs_9_ = bf16[1,2048,128]{2,1,0:T(8,128)(2,1)S(1)} collective-permute-done((bf16[1,2048,128]{2,1,0:T(8,128)(2,1)}, bf16[1,2048,128]{2,1,0:T(8,128)(2,1)S(1)}, u32[]{:S(2)}, u32[]{:S(2)}) %collective-permute-start.7) | collective-permute-done | bytes 524320 | tf_op jit(solution)/shard_map/ppermute | solution.py:21
  18.6 0.4 %condition.1.refs_0_ = bf16[2,4,2,16,256]{4,3,2,1,0:T(8,128)(2,1)S(1)} custom-call(bf16[2,16,2048]{2,1,0:T(8,128)(2,1)S(1)} %get-tuple-element.28.refs_0_, bf16[2,16,2048]{2,1,0:T(8,128)(2,1)S(1)} %collective-permute-done.1.refs_1_, bf16[2,16,2048]{2,1,0:T(8,128)(2,1)S(1)} %collective-permute-done.3.refs_2_, ...), custom_call_target="tpu_custom_call" | custom-call | flops 268435456 | bytes 3145728 | tf_op jit(solution)/shard_map/condition/pallas_call | solution.py:91
  19.1 0.1 collective-permute-start.10
  19.2 1.4 %collective-permute-start.8 = (bf16[2,4,2,16,256]{4,3,2,1,0:T(8,128)(2,1)S(1)}, bf16[2,4,2,16,256]{4,3,2,1,0:T(8,128)(2,1)S(1)}, u32[]{:S(2)}, u32[]{:S(2)}) collective-permute-start(bf16[2,4,2,16,256]{4,3,2,1,0:T(8,128)(2,1)S(1)} %condition.1.refs_0_), channel_id=1, source_target_pairs={{12,0},{13,1},{14,2},{15,3},{8,4},{9,5},{10,6},{11,7},{4,8},{5,9},... | collective-permute-start | bytes 393224 | tf_op jit(solution)/shard_map/ppermute | solution.py:21
  20.6 1.3 %collective-permute-start.9 = (bf16[2,4,2,16,256]{4,3,2,1,0:T(8,128)(2,1)S(1)}, bf16[2,4,2,16,256]{4,3,2,1,0:T(8,128)(2,1)S(1)}, u32[]{:S(2)}, u32[]{:S(2)}) collective-permute-start(bf16[2,4,2,16,256]{4,3,2,1,0:T(8,128)(2,1)S(1)} %condition.1.refs_0_), channel_id=1, source_target_pairs={{2,0},{3,1},{0,2},{1,3},{6,4},{7,5},{4,6},{5,7},{10,8},{11,9},{8,1... | collective-permute-start | bytes 393224 | tf_op jit(solution)/shard_map/ppermute | solution.py:21
  21.9 3.0 %collective-permute-done.10.refs_2_ = bf16[2,4,2,16,256]{4,3,2,1,0:T(8,128)(2,1)S(1)} collective-permute-done((bf16[2,4,2,16,256]{4,3,2,1,0:T(8,128)(2,1)S(1)}, bf16[2,4,2,16,256]{4,3,2,1,0:T(8,128)(2,1)S(1)}, u32[]{:S(2)}, u32[]{:S(2)}) %collective-permute-start.10) | collective-permute-done | bytes 131104 | tf_op jit(solution)/shard_map/ppermute | solution.py:21
  24.9 1.3 %collective-permute-start.11 = (bf16[2,4,2,16,256]{4,3,2,1,0:T(8,128)(2,1)S(1)}, bf16[2,4,2,16,256]{4,3,2,1,0:T(8,128)(2,1)S(1)}, u32[]{:S(2)}, u32[]{:S(2)}) collective-permute-start(bf16[2,4,2,16,256]{4,3,2,1,0:T(8,128)(2,1)S(1)} %collective-permute-done.10.refs_2_), channel_id=1, source_target_pairs={{2,0},{3,1},{0,2},{1,3},{6,4},{7,5},{4,6},{5,7},{10,8},{11,9},{8,1... | collective-permute-start | bytes 393224 | tf_op jit(solution)/shard_map/ppermute | solution.py:21
  26.2 0.9 %collective-permute-done.8.refs_1_ = bf16[2,4,2,16,256]{4,3,2,1,0:T(8,128)(2,1)S(1)} collective-permute-done((bf16[2,4,2,16,256]{4,3,2,1,0:T(8,128)(2,1)S(1)}, bf16[2,4,2,16,256]{4,3,2,1,0:T(8,128)(2,1)S(1)}, u32[]{:S(2)}, u32[]{:S(2)}) %collective-permute-start.8) | collective-permute-done | bytes 131104 | tf_op jit(solution)/shard_map/ppermute | solution.py:21
  27.0 1.5 %collective-permute-start.13 = (bf16[2,4,2,16,256]{4,3,2,1,0:T(8,128)(2,1)S(1)}, bf16[2,4,2,16,256]{4,3,2,1,0:T(8,128)(2,1)S(1)}, u32[]{:S(2)}, u32[]{:S(2)}) collective-permute-start(bf16[2,4,2,16,256]{4,3,2,1,0:T(8,128)(2,1)S(1)} %collective-permute-done.8.refs_1_), channel_id=1, source_target_pairs={{4,0},{5,1},{6,2},{7,3},{0,4},{1,5},{2,6},{3,7},{12,8},{13,9},{14,... | collective-permute-start | bytes 393224 | tf_op jit(solution)/shard_map/ppermute | solution.py:21
  28.5 1.6 %collective-permute-start.14 = (bf16[2,4,2,16,256]{4,3,2,1,0:T(8,128)(2,1)S(1)}, bf16[2,4,2,16,256]{4,3,2,1,0:T(8,128)(2,1)S(1)}, u32[]{:S(2)}, u32[]{:S(2)}) collective-permute-start(bf16[2,4,2,16,256]{4,3,2,1,0:T(8,128)(2,1)S(1)} %collective-permute-done.8.refs_1_), channel_id=1, source_target_pairs={{2,0},{3,1},{0,2},{1,3},{6,4},{7,5},{4,6},{5,7},{10,8},{11,9},{8,1... | collective-permute-start | bytes 393224 | tf_op jit(solution)/shard_map/ppermute | solution.py:21
  30.2 0.4 collective-permute-start.15
  30.5 0.4 %collective-permute-done.11.refs_3_ = bf16[2,4,2,16,256]{4,3,2,1,0:T(8,128)(2,1)S(1)} collective-permute-done((bf16[2,4,2,16,256]{4,3,2,1,0:T(8,128)(2,1)S(1)}, bf16[2,4,2,16,256]{4,3,2,1,0:T(8,128)(2,1)S(1)}, u32[]{:S(2)}, u32[]{:S(2)}) %collective-permute-start.11) | collective-permute-done | bytes 131104 | tf_op jit(solution)/shard_map/ppermute | solution.py:21
  30.9 0.2 turn.1.refs_1_
  31.2 0.1 collective-permute-start.16
  31.3 1.3 %score.4.refs_2_ = f32[2048,512]{1,0:T(8,128)S(1)} custom-call(bf16[2048,2048]{1,0:T(8,128)(2,1)S(1)} %stage.3.refs_0_, bf16[512,512]{1,0:T(8,128)(2,1)S(1)} %turn.1.refs_1_), custom_call_target="tpu_custom_call" | custom-call | flops 21474836480 | bytes 4194304 | tf_op jit(solution)/shard_map/score/pallas_call | solution.py:190
  32.5 0.6 %collective-permute-start.12 = (bf16[2,4,2,16,256]{4,3,2,1,0:T(8,128)(2,1)S(1)}, bf16[2,4,2,16,256]{4,3,2,1,0:T(8,128)(2,1)S(1)}, u32[]{:S(2)}, u32[]{:S(2)}) collective-permute-start(bf16[2,4,2,16,256]{4,3,2,1,0:T(8,128)(2,1)S(1)} %collective-permute-done.8.refs_1_), channel_id=1, source_target_pairs={{1,0},{0,1},{3,2},{2,3},{5,4},{4,5},{7,6},{6,7},{9,8},{8,9},{11,10... | collective-permute-start | bytes 393224 | tf_op jit(solution)/shard_map/ppermute | solution.py:21
  33.1 0.1 collective-permute-done.16.refs_1_
  33.2 1.4 %score.5.refs_5_ = f32[2048,512]{1,0:T(8,128)S(1)} custom-call(bf16[2048,2048]{1,0:T(8,128)(2,1)S(1)} %stage.3.refs_0_, bf16[512,512]{1,0:T(8,128)(2,1)S(1)} %collective-permute-done.16.refs_1_, f32[2048,512]{1,0:T(8,128)S(1)} %score.4.refs_2_), custom_call_target="tpu_custom_call", output_to_operand_aliasing={{}: (2, {})} | custom-call | flops 1073741824 | bytes 4194304 | tf_op jit(solution)/shard_map/score/pallas_call | solution.py:190
  34.6 1.4 %collective-permute-done.15.refs_4_ = bf16[2,4,2,16,256]{4,3,2,1,0:T(8,128)(2,1)S(1)} collective-permute-done((bf16[2,4,2,16,256]{4,3,2,1,0:T(8,128)(2,1)S(1)}, bf16[2,4,2,16,256]{4,3,2,1,0:T(8,128)(2,1)S(1)}, u32[]{:S(2)}, u32[]{:S(2)}) %collective-permute-start.15) | collective-permute-done | bytes 131104 | tf_op jit(solution)/shard_map/ppermute | solution.py:21
  36.0 0.5 %collective-permute-start.18 = (bf16[2,4,2,16,256]{4,3,2,1,0:T(8,128)(2,1)S(1)}, bf16[2,4,2,16,256]{4,3,2,1,0:T(8,128)(2,1)S(1)}, u32[]{:S(2)}, u32[]{:S(2)}) collective-permute-start(bf16[2,4,2,16,256]{4,3,2,1,0:T(8,128)(2,1)S(1)} %collective-permute-done.13.refs_3_), channel_id=1, source_target_pairs={{1,0},{0,1},{3,2},{2,3},{5,4},{4,5},{7,6},{6,7},{9,8},{8,9},{11,10... | collective-permute-start | bytes 393224 | tf_op jit(solution)/shard_map/ppermute | solution.py:21
  36.5 0.0 collective-permute-start.19
  36.6 1.5 %score.6.refs_5_ = f32[2048,512]{1,0:T(8,128)S(1)} custom-call(bf16[2048,2048]{1,0:T(8,128)(2,1)S(1)} %stage.3.refs_0_, bf16[2,4,2,16,256]{4,3,2,1,0:T(8,128)(2,1)S(1)} %collective-permute-done.8.refs_1_, bf16[2,4,2,16,256]{4,3,2,1,0:T(8,128)(2,1)S(1)} %collective-permute-done.14.refs_2_, ...), custom_call_target="tpu_custom_call", output_to_operand_aliasing={{}: (5, {})} | custom-call | flops 1073741824 | bytes 4194304 | tf_op jit(solution)/shard_map/score/pallas_call | solution.py:190
  38.1 2.9 %score.7 = f32[2048,512]{1,0:T(8,128)} custom-call(bf16[2048,2048]{1,0:T(8,128)(2,1)S(1)} %stage.3.refs_0_, bf16[2,4,2,16,256]{4,3,2,1,0:T(8,128)(2,1)S(1)} %collective-permute-done.12.refs_1_, bf16[2,4,2,16,256]{4,3,2,1,0:T(8,128)(2,1)S(1)} %collective-permute-done.17.refs_2_, bf16[2,4,2,16,256]{4,3,2,1,0:T(8,128)(2,1)S(1)} %collective-permute-done.18.refs_3_, ...), custom_call_target="tpu_custom_call" | custom-call | flops 1073741824 | bytes 4194304 | tf_op jit(solution)/shard_map/score/pallas_call | solution.py:190
  (16 shorter events, 0.0 us)
Async XLA Ops:
  0.0 9.0 %collective-permute-start = (bf16[2,16,2048]{2,1,0:T(8,128)(2,1)}, bf16[2,16,2048]{2,1,0:T(8,128)(2,1)S(1)}, u32[]{:S(2)}, u32[]{:S(2)}) collective-permute-start(bf16[2,16,2048]{2,1,0:T(8,128)(2,1)} %refs_1_.2), channel_id=1, source_target_pairs={{12,0},{13,1},{14,2},{15,3},{8,4},{9,5},{10,6},{11,7},{4,8},{5,9},... | collective-permute-start | bytes 393224 | tf_op jit(solution)/shard_map/ppermute | solution.py:21
  5.0 13.6 %collective-permute-start.7 = (bf16[1,2048,128]{2,1,0:T(8,128)(2,1)}, bf16[1,2048,128]{2,1,0:T(8,128)(2,1)S(1)}, u32[]{:S(2)}, u32[]{:S(2)}) collective-permute-start(bf16[1,2048,128]{2,1,0:T(8,128)(2,1)} %refs_2_.1), channel_id=1, source_target_pairs={{2,0},{3,1},{0,2},{1,3},{6,4},{7,5},{4,6},{5,7},{10,8},{11,9},{8,1... | collective-permute-start | bytes 1572872 | tf_op jit(solution)/shard_map/ppermute | solution.py:21
  6.6 2.4 %collective-permute-start.1 = (bf16[2,16,2048]{2,1,0:T(8,128)(2,1)}, bf16[2,16,2048]{2,1,0:T(8,128)(2,1)S(1)}, u32[]{:S(2)}, u32[]{:S(2)}) collective-permute-start(bf16[2,16,2048]{2,1,0:T(8,128)(2,1)} %refs_1_.2), channel_id=1, source_target_pairs={{1,0},{0,1},{3,2},{2,3},{5,4},{4,5},{7,6},{6,7},{9,8},{8,9},{11,10... | collective-permute-start | bytes 393224 | tf_op jit(solution)/shard_map/ppermute | solution.py:21
  6.6 6.9 %collective-permute-start.3 = (bf16[2,16,2048]{2,1,0:T(8,128)(2,1)}, bf16[2,16,2048]{2,1,0:T(8,128)(2,1)S(1)}, u32[]{:S(2)}, u32[]{:S(2)}) collective-permute-start(bf16[2,16,2048]{2,1,0:T(8,128)(2,1)} %refs_1_.2), channel_id=1, source_target_pairs={{4,0},{5,1},{6,2},{7,3},{0,4},{1,5},{2,6},{3,7},{12,8},{13,9},{14,... | collective-permute-start | bytes 393224 | tf_op jit(solution)/shard_map/ppermute | solution.py:21
  9.0 6.5 %collective-permute-start.2 = (bf16[2,16,2048]{2,1,0:T(8,128)(2,1)S(1)}, bf16[2,16,2048]{2,1,0:T(8,128)(2,1)S(1)}, u32[]{:S(2)}, u32[]{:S(2)}) collective-permute-start(bf16[2,16,2048]{2,1,0:T(8,128)(2,1)S(1)} %collective-permute-done.refs_3_), channel_id=1, source_target_pairs={{4,0},{5,1},{6,2},{7,3},{0,4},{1,5},{2,6},{3,7},{12,8},{13,9},{14,... | collective-permute-start | bytes 393224 | tf_op jit(solution)/shard_map/ppermute | solution.py:21
  11.3 4.2 %collective-permute-start.5 = (bf16[2,16,2048]{2,1,0:T(8,128)(2,1)S(1)}, bf16[2,16,2048]{2,1,0:T(8,128)(2,1)S(1)}, u32[]{:S(2)}, u32[]{:S(2)}) collective-permute-start(bf16[2,16,2048]{2,1,0:T(8,128)(2,1)S(1)} %collective-permute-done.refs_3_), channel_id=1, source_target_pairs={{1,0},{0,1},{3,2},{2,3},{5,4},{4,5},{7,6},{6,7},{9,8},{8,9},{11,10... | collective-permute-start | bytes 393224 | tf_op jit(solution)/shard_map/ppermute | solution.py:21
  13.5 2.0 %collective-permute-start.4 = (bf16[2,16,2048]{2,1,0:T(8,128)(2,1)S(1)}, bf16[2,16,2048]{2,1,0:T(8,128)(2,1)S(1)}, u32[]{:S(2)}, u32[]{:S(2)}) collective-permute-start(bf16[2,16,2048]{2,1,0:T(8,128)(2,1)S(1)} %collective-permute-done.3.refs_2_), channel_id=1, source_target_pairs={{1,0},{0,1},{3,2},{2,3},{5,4},{4,5},{7,6},{6,7},{9,8},{8,9},{11,10... | collective-permute-start | bytes 393224 | tf_op jit(solution)/shard_map/ppermute | solution.py:21
  15.5 1.3 %collective-permute-start.6 = (bf16[2,16,2048]{2,1,0:T(8,128)(2,1)S(1)}, bf16[2,16,2048]{2,1,0:T(8,128)(2,1)S(1)}, u32[]{:S(2)}, u32[]{:S(2)}) collective-permute-start(bf16[2,16,2048]{2,1,0:T(8,128)(2,1)S(1)} %collective-permute-done.2.refs_4_), channel_id=1, source_target_pairs={{1,0},{0,1},{3,2},{2,3},{5,4},{4,5},{7,6},{6,7},{9,8},{8,9},{11,10... | collective-permute-start | bytes 393224 | tf_op jit(solution)/shard_map/ppermute | solution.py:21
  19.1 5.8 %collective-permute-start.10 = (bf16[2,4,2,16,256]{4,3,2,1,0:T(8,128)(2,1)S(1)}, bf16[2,4,2,16,256]{4,3,2,1,0:T(8,128)(2,1)S(1)}, u32[]{:S(2)}, u32[]{:S(2)}) collective-permute-start(bf16[2,4,2,16,256]{4,3,2,1,0:T(8,128)(2,1)S(1)} %condition.1.refs_0_), channel_id=1, source_target_pairs={{4,0},{5,1},{6,2},{7,3},{0,4},{1,5},{2,6},{3,7},{12,8},{13,9},{14,... | collective-permute-start | bytes 393224 | tf_op jit(solution)/shard_map/ppermute | solution.py:21
  19.2 7.9 %collective-permute-start.8 = (bf16[2,4,2,16,256]{4,3,2,1,0:T(8,128)(2,1)S(1)}, bf16[2,4,2,16,256]{4,3,2,1,0:T(8,128)(2,1)S(1)}, u32[]{:S(2)}, u32[]{:S(2)}) collective-permute-start(bf16[2,4,2,16,256]{4,3,2,1,0:T(8,128)(2,1)S(1)} %condition.1.refs_0_), channel_id=1, source_target_pairs={{12,0},{13,1},{14,2},{15,3},{8,4},{9,5},{10,6},{11,7},{4,8},{5,9},... | collective-permute-start | bytes 393224 | tf_op jit(solution)/shard_map/ppermute | solution.py:21
  20.6 9.9 %collective-permute-start.9 = (bf16[2,4,2,16,256]{4,3,2,1,0:T(8,128)(2,1)S(1)}, bf16[2,4,2,16,256]{4,3,2,1,0:T(8,128)(2,1)S(1)}, u32[]{:S(2)}, u32[]{:S(2)}) collective-permute-start(bf16[2,4,2,16,256]{4,3,2,1,0:T(8,128)(2,1)S(1)} %condition.1.refs_0_), channel_id=1, source_target_pairs={{2,0},{3,1},{0,2},{1,3},{6,4},{7,5},{4,6},{5,7},{10,8},{11,9},{8,1... | collective-permute-start | bytes 393224 | tf_op jit(solution)/shard_map/ppermute | solution.py:21
  24.9 6.0 %collective-permute-start.11 = (bf16[2,4,2,16,256]{4,3,2,1,0:T(8,128)(2,1)S(1)}, bf16[2,4,2,16,256]{4,3,2,1,0:T(8,128)(2,1)S(1)}, u32[]{:S(2)}, u32[]{:S(2)}) collective-permute-start(bf16[2,4,2,16,256]{4,3,2,1,0:T(8,128)(2,1)S(1)} %collective-permute-done.10.refs_2_), channel_id=1, source_target_pairs={{2,0},{3,1},{0,2},{1,3},{6,4},{7,5},{4,6},{5,7},{10,8},{11,9},{8,1... | collective-permute-start | bytes 393224 | tf_op jit(solution)/shard_map/ppermute | solution.py:21
  27.0 7.5 %collective-permute-start.13 = (bf16[2,4,2,16,256]{4,3,2,1,0:T(8,128)(2,1)S(1)}, bf16[2,4,2,16,256]{4,3,2,1,0:T(8,128)(2,1)S(1)}, u32[]{:S(2)}, u32[]{:S(2)}) collective-permute-start(bf16[2,4,2,16,256]{4,3,2,1,0:T(8,128)(2,1)S(1)} %collective-permute-done.8.refs_1_), channel_id=1, source_target_pairs={{4,0},{5,1},{6,2},{7,3},{0,4},{1,5},{2,6},{3,7},{12,8},{13,9},{14,... | collective-permute-start | bytes 393224 | tf_op jit(solution)/shard_map/ppermute | solution.py:21
  28.5 6.1 %collective-permute-start.14 = (bf16[2,4,2,16,256]{4,3,2,1,0:T(8,128)(2,1)S(1)}, bf16[2,4,2,16,256]{4,3,2,1,0:T(8,128)(2,1)S(1)}, u32[]{:S(2)}, u32[]{:S(2)}) collective-permute-start(bf16[2,4,2,16,256]{4,3,2,1,0:T(8,128)(2,1)S(1)} %collective-permute-done.8.refs_1_), channel_id=1, source_target_pairs={{2,0},{3,1},{0,2},{1,3},{6,4},{7,5},{4,6},{5,7},{10,8},{11,9},{8,1... | collective-permute-start | bytes 393224 | tf_op jit(solution)/shard_map/ppermute | solution.py:21
  30.2 5.9 %collective-permute-start.15 = (bf16[2,4,2,16,256]{4,3,2,1,0:T(8,128)(2,1)S(1)}, bf16[2,4,2,16,256]{4,3,2,1,0:T(8,128)(2,1)S(1)}, u32[]{:S(2)}, u32[]{:S(2)}) collective-permute-start(bf16[2,4,2,16,256]{4,3,2,1,0:T(8,128)(2,1)S(1)} %collective-permute-done.8.refs_1_), channel_id=1, source_target_pairs={{6,0},{7,1},{4,2},{5,3},{2,4},{3,5},{0,6},{1,7},{14,8},{15,9},{12,... | collective-permute-start | bytes 393224 | tf_op jit(solution)/shard_map/ppermute | solution.py:21
  31.2 2.0 %collective-permute-start.16 = (bf16[512,512]{1,0:T(8,128)(2,1)S(1)}, bf16[512,512]{1,0:T(8,128)(2,1)S(1)}, u32[]{:S(2)}, u32[]{:S(2)}) collective-permute-start(bf16[512,512]{1,0:T(8,128)(2,1)S(1)} %turn.1.refs_1_), channel_id=1, source_target_pairs={{1,0},{0,1},{3,2},{2,3},{5,4},{4,5},{7,6},{6,7},{9,8},{8,9},{11,10... | collective-permute-start | bytes 1572872 | tf_op jit(solution)/shard_map/ppermute | solution.py:21
  32.5 5.5 %collective-permute-start.12 = (bf16[2,4,2,16,256]{4,3,2,1,0:T(8,128)(2,1)S(1)}, bf16[2,4,2,16,256]{4,3,2,1,0:T(8,128)(2,1)S(1)}, u32[]{:S(2)}, u32[]{:S(2)}) collective-permute-start(bf16[2,4,2,16,256]{4,3,2,1,0:T(8,128)(2,1)S(1)} %collective-permute-done.8.refs_1_), channel_id=1, source_target_pairs={{1,0},{0,1},{3,2},{2,3},{5,4},{4,5},{7,6},{6,7},{9,8},{8,9},{11,10... | collective-permute-start | bytes 393224 | tf_op jit(solution)/shard_map/ppermute | solution.py:21
  36.0 2.0 %collective-permute-start.17 = (bf16[2,4,2,16,256]{4,3,2,1,0:T(8,128)(2,1)S(1)}, bf16[2,4,2,16,256]{4,3,2,1,0:T(8,128)(2,1)S(1)}, u32[]{:S(2)}, u32[]{:S(2)}) collective-permute-start(bf16[2,4,2,16,256]{4,3,2,1,0:T(8,128)(2,1)S(1)} %collective-permute-done.14.refs_2_), channel_id=1, source_target_pairs={{1,0},{0,1},{3,2},{2,3},{5,4},{4,5},{7,6},{6,7},{9,8},{8,9},{11,10... | collective-permute-start | bytes 393224 | tf_op jit(solution)/shard_map/ppermute | solution.py:21
  36.0 2.0 %collective-permute-start.18 = (bf16[2,4,2,16,256]{4,3,2,1,0:T(8,128)(2,1)S(1)}, bf16[2,4,2,16,256]{4,3,2,1,0:T(8,128)(2,1)S(1)}, u32[]{:S(2)}, u32[]{:S(2)}) collective-permute-start(bf16[2,4,2,16,256]{4,3,2,1,0:T(8,128)(2,1)S(1)} %collective-permute-done.13.refs_3_), channel_id=1, source_target_pairs={{1,0},{0,1},{3,2},{2,3},{5,4},{4,5},{7,6},{6,7},{9,8},{8,9},{11,10... | collective-permute-start | bytes 393224 | tf_op jit(solution)/shard_map/ppermute | solution.py:21
  36.5 1.5 %collective-permute-start.19 = (bf16[2,4,2,16,256]{4,3,2,1,0:T(8,128)(2,1)S(1)}, bf16[2,4,2,16,256]{4,3,2,1,0:T(8,128)(2,1)S(1)}, u32[]{:S(2)}, u32[]{:S(2)}) collective-permute-start(bf16[2,4,2,16,256]{4,3,2,1,0:T(8,128)(2,1)S(1)} %collective-permute-done.15.refs_4_), channel_id=1, source_target_pairs={{1,0},{0,1},{3,2},{2,3},{5,4},{4,5},{7,6},{6,7},{9,8},{8,9},{11,10... | collective-permute-start | bytes 393224 | tf_op jit(solution)/shard_map/ppermute | solution.py:21

commit v18 on v17

--- a/solution.py
+++ b/solution.py
@@ -9,7 +9,6 @@
 
 VMEM = pl.BlockSpec(memory_space=pltpu.VMEM)
 ANY = pl.BlockSpec(memory_space=pl.ANY)
-ORDER_FLOPS = 2_788_300_000
 
 
 class Grid:
@@ -61,9 +60,7 @@
         scratch_shapes=[pltpu.SemaphoreType.DMA((len(arrays),))],
         input_output_aliases={} if first else {0: 0},
         compiler_params=pltpu.CompilerParams(vmem_limit_bytes=4 << 20),
-        cost_estimate=pl.CostEstimate(
-            flops=ORDER_FLOPS if first else 1, bytes_accessed=moved, transcendentals=0
-        ),
+        cost_estimate=pl.CostEstimate(flops=1, bytes_accessed=moved, transcendentals=0),
         name="stage",
     )(*sources)
 

time: 41.2 us -> 43.5 us (1.056)
  the two profiles are of different devices: /device:TPU:0 before, /device:TPU:25 now
where the time goes in v18:
time: 43.5 us; the launch traced here: 43.3 us
  starting transfers between devices  21.7 us (50%)
  Pallas kernels  12.3 us (28%)
  waiting for transfers between devices  9.17 us (21%)
    ppermute x20, starting transfers between devices, swap(): lax.ppermute(block, 'rows', [(row ^ step, row) for row in range(self.far...  21.7 us
    ppermute x20, waiting for transfers between devices, swap(): lax.ppermute(block, 'rows', [(row ^ step, row) for row in range(self.far...  9.17 us
    pallas_call x4, Pallas kernels, score(): pl.pallas_call(functools.partial(score_kernel, grid, masks, other, len(pa...  7.06 us
    pallas_call x2, Pallas kernels, stage(): pl.pallas_call(functools.partial(stage_kernel, first, arrays[0].shape[0]...  4.56 us
  transfers between devices with their start and end apart: 20, of which 5 were waited for; matrix products, arithmetic and copies ran while one was open for 0% of the time, Pallas kernels for 21%

profile of v18, /device:TPU:25, one launch (start us, length us, event | category | flops | bytes accessed | tf_op | source)
XLA Modules:
  0.0 43.3 jit_solution(8580605496908457804)
XLA Ops:
  0.0 1.2 %collective-permute-start.7 = (bf16[1,2048,128]{2,1,0:T(8,128)(2,1)}, bf16[1,2048,128]{2,1,0:T(8,128)(2,1)S(1)}, u32[]{:S(2)}, u32[]{:S(2)}) collective-permute-start(bf16[1,2048,128]{2,1,0:T(8,128)(2,1)} %refs_2_.1), channel_id=1, source_target_pairs={{2,0},{3,1},{0,2},{1,3},{6,4},{7,5},{4,6},{5,7},{10,8},{11,9},{8,1... | collective-permute-start | bytes 1572872 | tf_op jit(solution)/shard_map/ppermute | solution.py:20
  1.2 1.2 %collective-permute-start.1 = (bf16[2,16,2048]{2,1,0:T(8,128)(2,1)}, bf16[2,16,2048]{2,1,0:T(8,128)(2,1)S(1)}, u32[]{:S(2)}, u32[]{:S(2)}) collective-permute-start(bf16[2,16,2048]{2,1,0:T(8,128)(2,1)} %refs_1_.2), channel_id=1, source_target_pairs={{1,0},{0,1},{3,2},{2,3},{5,4},{4,5},{7,6},{6,7},{9,8},{8,9},{11,10... | collective-permute-start | bytes 393224 | tf_op jit(solution)/shard_map/ppermute | solution.py:20
  2.4 0.4 collective-permute-start.3
  2.8 2.4 %stage.2 = (bf16[2048,2048]{1,0:T(8,128)(2,1)S(1)}, bf16[2,16,2048]{2,1,0:T(8,128)(2,1)S(1)}, bf16[1,2048,128]{2,1,0:T(8,128)(2,1)S(1)}) custom-call(bf16[2048,2048]{1,0:T(8,128)(2,1)} %refs_1_.3, bf16[2,16,2048]{2,1,0:T(8,128)(2,1)} %refs_1_.2, bf16[1,2048,128]{2,1,0:T(8,128)(2,1)} %refs_2_.1), custom_call_target="tpu_custom_call" | custom-call | flops 1 | bytes 9043968 | tf_op jit(solution)/shard_map/stage/pallas_call | solution.py:55
  5.2 2.0 %collective-permute-done.refs_3_ = bf16[2,16,2048]{2,1,0:T(8,128)(2,1)S(1)} collective-permute-done((bf16[2,16,2048]{2,1,0:T(8,128)(2,1)}, bf16[2,16,2048]{2,1,0:T(8,128)(2,1)S(1)}, u32[]{:S(2)}, u32[]{:S(2)}) %collective-permute-start) | collective-permute-done | bytes 131104 | tf_op jit(solution)/shard_map/ppermute | solution.py:20
  7.2 3.4 %collective-permute-start.5 = (bf16[2,16,2048]{2,1,0:T(8,128)(2,1)S(1)}, bf16[2,16,2048]{2,1,0:T(8,128)(2,1)S(1)}, u32[]{:S(2)}, u32[]{:S(2)}) collective-permute-start(bf16[2,16,2048]{2,1,0:T(8,128)(2,1)S(1)} %collective-permute-done.refs_3_), channel_id=1, source_target_pairs={{1,0},{0,1},{3,2},{2,3},{5,4},{4,5},{7,6},{6,7},{9,8},{8,9},{11,10... | collective-permute-start | bytes 393224 | tf_op jit(solution)/shard_map/ppermute | solution.py:20
  10.6 2.2 %stage.3.refs_0_ = bf16[2048,2048]{1,0:T(8,128)(2,1)S(1)} custom-call(bf16[2048,2048]{1,0:T(8,128)(2,1)S(1)} %get-tuple-element.26.refs_0_, bf16[2048,2048]{1,0:T(8,128)(2,1)} %refs_1_.3), custom_call_target="tpu_custom_call", output_to_operand_aliasing={{}: (0, {})} | custom-call | flops 1 | bytes 8388608 | tf_op jit(solution)/shard_map/stage/pallas_call | solution.py:55
  12.8 0.1 collective-permute-start.4
  12.9 0.0 collective-permute-done.2.refs_4_
  12.9 2.7 %collective-permute-start.6 = (bf16[2,16,2048]{2,1,0:T(8,128)(2,1)S(1)}, bf16[2,16,2048]{2,1,0:T(8,128)(2,1)S(1)}, u32[]{:S(2)}, u32[]{:S(2)}) collective-permute-start(bf16[2,16,2048]{2,1,0:T(8,128)(2,1)S(1)} %collective-permute-done.2.refs_4_), channel_id=1, source_target_pairs={{1,0},{0,1},{3,2},{2,3},{5,4},{4,5},{7,6},{6,7},{9,8},{8,9},{11,10... | collective-permute-start | bytes 393224 | tf_op jit(solution)/shard_map/ppermute | solution.py:20
  15.6 1.0 %collective-permute-done.6.refs_7_ = bf16[2,16,2048]{2,1,0:T(8,128)(2,1)S(1)} collective-permute-done((bf16[2,16,2048]{2,1,0:T(8,128)(2,1)S(1)}, bf16[2,16,2048]{2,1,0:T(8,128)(2,1)S(1)}, u32[]{:S(2)}, u32[]{:S(2)}) %collective-permute-start.6) | collective-permute-done | bytes 131104 | tf_op jit(solution)/shard_map/ppermute | solution.py:20
  16.6 0.4 %condition.1.refs_0_ = bf16[2,4,2,16,256]{4,3,2,1,0:T(8,128)(2,1)S(1)} custom-call(bf16[2,16,2048]{2,1,0:T(8,128)(2,1)S(1)} %get-tuple-element.28.refs_0_, bf16[2,16,2048]{2,1,0:T(8,128)(2,1)S(1)} %collective-permute-done.1.refs_1_, bf16[2,16,2048]{2,1,0:T(8,128)(2,1)S(1)} %collective-permute-done.3.refs_2_, ...), custom_call_target="tpu_custom_call" | custom-call | flops 268435456 | bytes 3145728 | tf_op jit(solution)/shard_map/condition/pallas_call | solution.py:88
  17.0 0.1 collective-permute-start.10
  17.1 0.8 %collective-permute-start.8 = (bf16[2,4,2,16,256]{4,3,2,1,0:T(8,128)(2,1)S(1)}, bf16[2,4,2,16,256]{4,3,2,1,0:T(8,128)(2,1)S(1)}, u32[]{:S(2)}, u32[]{:S(2)}) collective-permute-start(bf16[2,4,2,16,256]{4,3,2,1,0:T(8,128)(2,1)S(1)} %condition.1.refs_0_), channel_id=1, source_target_pairs={{12,0},{13,1},{14,2},{15,3},{8,4},{9,5},{10,6},{11,7},{4,8},{5,9},... | collective-permute-start | bytes 393224 | tf_op jit(solution)/shard_map/ppermute | solution.py:20
  17.9 0.2 collective-permute-start.9
  18.1 3.8 %collective-permute-done.10.refs_2_ = bf16[2,4,2,16,256]{4,3,2,1,0:T(8,128)(2,1)S(1)} collective-permute-done((bf16[2,4,2,16,256]{4,3,2,1,0:T(8,128)(2,1)S(1)}, bf16[2,4,2,16,256]{4,3,2,1,0:T(8,128)(2,1)S(1)}, u32[]{:S(2)}, u32[]{:S(2)}) %collective-permute-start.10) | collective-permute-done | bytes 131104 | tf_op jit(solution)/shard_map/ppermute | solution.py:20
  21.9 0.2 collective-permute-start.11
  22.1 2.2 %collective-permute-done.8.refs_1_ = bf16[2,4,2,16,256]{4,3,2,1,0:T(8,128)(2,1)S(1)} collective-permute-done((bf16[2,4,2,16,256]{4,3,2,1,0:T(8,128)(2,1)S(1)}, bf16[2,4,2,16,256]{4,3,2,1,0:T(8,128)(2,1)S(1)}, u32[]{:S(2)}, u32[]{:S(2)}) %collective-permute-start.8) | collective-permute-done | bytes 131104 | tf_op jit(solution)/shard_map/ppermute | solution.py:20
  24.3 1.7 %collective-permute-start.13 = (bf16[2,4,2,16,256]{4,3,2,1,0:T(8,128)(2,1)S(1)}, bf16[2,4,2,16,256]{4,3,2,1,0:T(8,128)(2,1)S(1)}, u32[]{:S(2)}, u32[]{:S(2)}) collective-permute-start(bf16[2,4,2,16,256]{4,3,2,1,0:T(8,128)(2,1)S(1)} %collective-permute-done.8.refs_1_), channel_id=1, source_target_pairs={{4,0},{5,1},{6,2},{7,3},{0,4},{1,5},{2,6},{3,7},{12,8},{13,9},{14,... | collective-permute-start | bytes 393224 | tf_op jit(solution)/shard_map/ppermute | solution.py:20
  25.9 0.2 collective-permute-start.14
  26.2 1.0 %collective-permute-start.15 = (bf16[2,4,2,16,256]{4,3,2,1,0:T(8,128)(2,1)S(1)}, bf16[2,4,2,16,256]{4,3,2,1,0:T(8,128)(2,1)S(1)}, u32[]{:S(2)}, u32[]{:S(2)}) collective-permute-start(bf16[2,4,2,16,256]{4,3,2,1,0:T(8,128)(2,1)S(1)} %collective-permute-done.8.refs_1_), channel_id=1, source_target_pairs={{6,0},{7,1},{4,2},{5,3},{2,4},{3,5},{0,6},{1,7},{14,8},{15,9},{12,... | collective-permute-start | bytes 393224 | tf_op jit(solution)/shard_map/ppermute | solution.py:20
  27.1 0.2 turn.1.refs_1_
  27.4 7.6 %collective-permute-start.16 = (bf16[512,512]{1,0:T(8,128)(2,1)S(1)}, bf16[512,512]{1,0:T(8,128)(2,1)S(1)}, u32[]{:S(2)}, u32[]{:S(2)}) collective-permute-start(bf16[512,512]{1,0:T(8,128)(2,1)S(1)} %turn.1.refs_1_), channel_id=1, source_target_pairs={{1,0},{0,1},{3,2},{2,3},{5,4},{4,5},{7,6},{6,7},{9,8},{8,9},{11,10... | collective-permute-start | bytes 1572872 | tf_op jit(solution)/shard_map/ppermute | solution.py:20
  35.0 1.3 %score.4.refs_2_ = f32[2048,512]{1,0:T(8,128)S(1)} custom-call(bf16[2048,2048]{1,0:T(8,128)(2,1)S(1)} %stage.3.refs_0_, bf16[512,512]{1,0:T(8,128)(2,1)S(1)} %turn.1.refs_1_), custom_call_target="tpu_custom_call" | custom-call | flops 21474836480 | bytes 4194304 | tf_op jit(solution)/shard_map/score/pallas_call | solution.py:187
  36.2 0.1 collective-permute-start.12
  36.3 0.2 collective-permute-done.16.refs_1_
  36.5 1.4 %score.5.refs_5_ = f32[2048,512]{1,0:T(8,128)S(1)} custom-call(bf16[2048,2048]{1,0:T(8,128)(2,1)S(1)} %stage.3.refs_0_, bf16[512,512]{1,0:T(8,128)(2,1)S(1)} %collective-permute-done.16.refs_1_, f32[2048,512]{1,0:T(8,128)S(1)} %score.4.refs_2_), custom_call_target="tpu_custom_call", output_to_operand_aliasing={{}: (2, {})} | custom-call | flops 1073741824 | bytes 4194304 | tf_op jit(solution)/shard_map/score/pallas_call | solution.py:187
  38.0 0.4 %collective-permute-start.17 = (bf16[2,4,2,16,256]{4,3,2,1,0:T(8,128)(2,1)S(1)}, bf16[2,4,2,16,256]{4,3,2,1,0:T(8,128)(2,1)S(1)}, u32[]{:S(2)}, u32[]{:S(2)}) collective-permute-start(bf16[2,4,2,16,256]{4,3,2,1,0:T(8,128)(2,1)S(1)} %collective-permute-done.14.refs_2_), channel_id=1, source_target_pairs={{1,0},{0,1},{3,2},{2,3},{5,4},{4,5},{7,6},{6,7},{9,8},{8,9},{11,10... | collective-permute-start | bytes 393224 | tf_op jit(solution)/shard_map/ppermute | solution.py:20
  38.4 0.1 collective-permute-start.18
  38.5 0.4 collective-permute-start.19
  38.9 1.5 %score.6.refs_5_ = f32[2048,512]{1,0:T(8,128)S(1)} custom-call(bf16[2048,2048]{1,0:T(8,128)(2,1)S(1)} %stage.3.refs_0_, bf16[2,4,2,16,256]{4,3,2,1,0:T(8,128)(2,1)S(1)} %collective-permute-done.8.refs_1_, bf16[2,4,2,16,256]{4,3,2,1,0:T(8,128)(2,1)S(1)} %collective-permute-done.14.refs_2_, ...), custom_call_target="tpu_custom_call", output_to_operand_aliasing={{}: (5, {})} | custom-call | flops 1073741824 | bytes 4194304 | tf_op jit(solution)/shard_map/score/pallas_call | solution.py:187
  40.4 2.9 %score.7 = f32[2048,512]{1,0:T(8,128)} custom-call(bf16[2048,2048]{1,0:T(8,128)(2,1)S(1)} %stage.3.refs_0_, bf16[2,4,2,16,256]{4,3,2,1,0:T(8,128)(2,1)S(1)} %collective-permute-done.12.refs_1_, bf16[2,4,2,16,256]{4,3,2,1,0:T(8,128)(2,1)S(1)} %collective-permute-done.17.refs_2_, bf16[2,4,2,16,256]{4,3,2,1,0:T(8,128)(2,1)S(1)} %collective-permute-done.18.refs_3_, ...), custom_call_target="tpu_custom_call" | custom-call | flops 1073741824 | bytes 4194304 | tf_op jit(solution)/shard_map/score/pallas_call | solution.py:187
  (16 shorter events, 0.0 us)
Async XLA Ops:
  0.0 16.6 %collective-permute-start.7 = (bf16[1,2048,128]{2,1,0:T(8,128)(2,1)}, bf16[1,2048,128]{2,1,0:T(8,128)(2,1)S(1)}, u32[]{:S(2)}, u32[]{:S(2)}) collective-permute-start(bf16[1,2048,128]{2,1,0:T(8,128)(2,1)} %refs_2_.1), channel_id=1, source_target_pairs={{2,0},{3,1},{0,2},{1,3},{6,4},{7,5},{4,6},{5,7},{10,8},{11,9},{8,1... | collective-permute-start | bytes 1572872 | tf_op jit(solution)/shard_map/ppermute | solution.py:20
  1.2 6.0 %collective-permute-start = (bf16[2,16,2048]{2,1,0:T(8,128)(2,1)}, bf16[2,16,2048]{2,1,0:T(8,128)(2,1)S(1)}, u32[]{:S(2)}, u32[]{:S(2)}) collective-permute-start(bf16[2,16,2048]{2,1,0:T(8,128)(2,1)} %refs_1_.2), channel_id=1, source_target_pairs={{12,0},{13,1},{14,2},{15,3},{8,4},{9,5},{10,6},{11,7},{4,8},{5,9},... | collective-permute-start | bytes 393224 | tf_op jit(solution)/shard_map/ppermute | solution.py:20
  1.2 6.0 %collective-permute-start.1 = (bf16[2,16,2048]{2,1,0:T(8,128)(2,1)}, bf16[2,16,2048]{2,1,0:T(8,128)(2,1)S(1)}, u32[]{:S(2)}, u32[]{:S(2)}) collective-permute-start(bf16[2,16,2048]{2,1,0:T(8,128)(2,1)} %refs_1_.2), channel_id=1, source_target_pairs={{1,0},{0,1},{3,2},{2,3},{5,4},{4,5},{7,6},{6,7},{9,8},{8,9},{11,10... | collective-permute-start | bytes 393224 | tf_op jit(solution)/shard_map/ppermute | solution.py:20
  2.4 10.4 %collective-permute-start.3 = (bf16[2,16,2048]{2,1,0:T(8,128)(2,1)}, bf16[2,16,2048]{2,1,0:T(8,128)(2,1)S(1)}, u32[]{:S(2)}, u32[]{:S(2)}) collective-permute-start(bf16[2,16,2048]{2,1,0:T(8,128)(2,1)} %refs_1_.2), channel_id=1, source_target_pairs={{4,0},{5,1},{6,2},{7,3},{0,4},{1,5},{2,6},{3,7},{12,8},{13,9},{14,... | collective-permute-start | bytes 393224 | tf_op jit(solution)/shard_map/ppermute | solution.py:20
  7.2 5.7 %collective-permute-start.2 = (bf16[2,16,2048]{2,1,0:T(8,128)(2,1)S(1)}, bf16[2,16,2048]{2,1,0:T(8,128)(2,1)S(1)}, u32[]{:S(2)}, u32[]{:S(2)}) collective-permute-start(bf16[2,16,2048]{2,1,0:T(8,128)(2,1)S(1)} %collective-permute-done.refs_3_), channel_id=1, source_target_pairs={{4,0},{5,1},{6,2},{7,3},{0,4},{1,5},{2,6},{3,7},{12,8},{13,9},{14,... | collective-permute-start | bytes 393224 | tf_op jit(solution)/shard_map/ppermute | solution.py:20
  7.2 8.4 %collective-permute-start.5 = (bf16[2,16,2048]{2,1,0:T(8,128)(2,1)S(1)}, bf16[2,16,2048]{2,1,0:T(8,128)(2,1)S(1)}, u32[]{:S(2)}, u32[]{:S(2)}) collective-permute-start(bf16[2,16,2048]{2,1,0:T(8,128)(2,1)S(1)} %collective-permute-done.refs_3_), channel_id=1, source_target_pairs={{1,0},{0,1},{3,2},{2,3},{5,4},{4,5},{7,6},{6,7},{9,8},{8,9},{11,10... | collective-permute-start | bytes 393224 | tf_op jit(solution)/shard_map/ppermute | solution.py:20
  12.8 2.8 %collective-permute-start.4 = (bf16[2,16,2048]{2,1,0:T(8,128)(2,1)S(1)}, bf16[2,16,2048]{2,1,0:T(8,128)(2,1)S(1)}, u32[]{:S(2)}, u32[]{:S(2)}) collective-permute-start(bf16[2,16,2048]{2,1,0:T(8,128)(2,1)S(1)} %collective-permute-done.3.refs_2_), channel_id=1, source_target_pairs={{1,0},{0,1},{3,2},{2,3},{5,4},{4,5},{7,6},{6,7},{9,8},{8,9},{11,10... | collective-permute-start | bytes 393224 | tf_op jit(solution)/shard_map/ppermute | solution.py:20
  12.9 3.6 %collective-permute-start.6 = (bf16[2,16,2048]{2,1,0:T(8,128)(2,1)S(1)}, bf16[2,16,2048]{2,1,0:T(8,128)(2,1)S(1)}, u32[]{:S(2)}, u32[]{:S(2)}) collective-permute-start(bf16[2,16,2048]{2,1,0:T(8,128)(2,1)S(1)} %collective-permute-done.2.refs_4_), channel_id=1, source_target_pairs={{1,0},{0,1},{3,2},{2,3},{5,4},{4,5},{7,6},{6,7},{9,8},{8,9},{11,10... | collective-permute-start | bytes 393224 | tf_op jit(solution)/shard_map/ppermute | solution.py:20
  17.0 4.8 %collective-permute-start.10 = (bf16[2,4,2,16,256]{4,3,2,1,0:T(8,128)(2,1)S(1)}, bf16[2,4,2,16,256]{4,3,2,1,0:T(8,128)(2,1)S(1)}, u32[]{:S(2)}, u32[]{:S(2)}) collective-permute-start(bf16[2,4,2,16,256]{4,3,2,1,0:T(8,128)(2,1)S(1)} %condition.1.refs_0_), channel_id=1, source_target_pairs={{4,0},{5,1},{6,2},{7,3},{0,4},{1,5},{2,6},{3,7},{12,8},{13,9},{14,... | collective-permute-start | bytes 393224 | tf_op jit(solution)/shard_map/ppermute | solution.py:20
  17.1 7.2 %collective-permute-start.8 = (bf16[2,4,2,16,256]{4,3,2,1,0:T(8,128)(2,1)S(1)}, bf16[2,4,2,16,256]{4,3,2,1,0:T(8,128)(2,1)S(1)}, u32[]{:S(2)}, u32[]{:S(2)}) collective-permute-start(bf16[2,4,2,16,256]{4,3,2,1,0:T(8,128)(2,1)S(1)} %condition.1.refs_0_), channel_id=1, source_target_pairs={{12,0},{13,1},{14,2},{15,3},{8,4},{9,5},{10,6},{11,7},{4,8},{5,9},... | collective-permute-start | bytes 393224 | tf_op jit(solution)/shard_map/ppermute | solution.py:20
  17.9 9.2 %collective-permute-start.9 = (bf16[2,4,2,16,256]{4,3,2,1,0:T(8,128)(2,1)S(1)}, bf16[2,4,2,16,256]{4,3,2,1,0:T(8,128)(2,1)S(1)}, u32[]{:S(2)}, u32[]{:S(2)}) collective-permute-start(bf16[2,4,2,16,256]{4,3,2,1,0:T(8,128)(2,1)S(1)} %condition.1.refs_0_), channel_id=1, source_target_pairs={{2,0},{3,1},{0,2},{1,3},{6,4},{7,5},{4,6},{5,7},{10,8},{11,9},{8,1... | collective-permute-start | bytes 393224 | tf_op jit(solution)/shard_map/ppermute | solution.py:20
  21.9 5.3 %collective-permute-start.11 = (bf16[2,4,2,16,256]{4,3,2,1,0:T(8,128)(2,1)S(1)}, bf16[2,4,2,16,256]{4,3,2,1,0:T(8,128)(2,1)S(1)}, u32[]{:S(2)}, u32[]{:S(2)}) collective-permute-start(bf16[2,4,2,16,256]{4,3,2,1,0:T(8,128)(2,1)S(1)} %collective-permute-done.10.refs_2_), channel_id=1, source_target_pairs={{2,0},{3,1},{0,2},{1,3},{6,4},{7,5},{4,6},{5,7},{10,8},{11,9},{8,1... | collective-permute-start | bytes 393224 | tf_op jit(solution)/shard_map/ppermute | solution.py:20
  24.3 13.7 %collective-permute-start.13 = (bf16[2,4,2,16,256]{4,3,2,1,0:T(8,128)(2,1)S(1)}, bf16[2,4,2,16,256]{4,3,2,1,0:T(8,128)(2,1)S(1)}, u32[]{:S(2)}, u32[]{:S(2)}) collective-permute-start(bf16[2,4,2,16,256]{4,3,2,1,0:T(8,128)(2,1)S(1)} %collective-permute-done.8.refs_1_), channel_id=1, source_target_pairs={{4,0},{5,1},{6,2},{7,3},{0,4},{1,5},{2,6},{3,7},{12,8},{13,9},{14,... | collective-permute-start | bytes 393224 | tf_op jit(solution)/shard_map/ppermute | solution.py:20
  25.9 12.0 %collective-permute-start.14 = (bf16[2,4,2,16,256]{4,3,2,1,0:T(8,128)(2,1)S(1)}, bf16[2,4,2,16,256]{4,3,2,1,0:T(8,128)(2,1)S(1)}, u32[]{:S(2)}, u32[]{:S(2)}) collective-permute-start(bf16[2,4,2,16,256]{4,3,2,1,0:T(8,128)(2,1)S(1)} %collective-permute-done.8.refs_1_), channel_id=1, source_target_pairs={{2,0},{3,1},{0,2},{1,3},{6,4},{7,5},{4,6},{5,7},{10,8},{11,9},{8,1... | collective-permute-start | bytes 393224 | tf_op jit(solution)/shard_map/ppermute | solution.py:20
  26.2 11.8 %collective-permute-start.15 = (bf16[2,4,2,16,256]{4,3,2,1,0:T(8,128)(2,1)S(1)}, bf16[2,4,2,16,256]{4,3,2,1,0:T(8,128)(2,1)S(1)}, u32[]{:S(2)}, u32[]{:S(2)}) collective-permute-start(bf16[2,4,2,16,256]{4,3,2,1,0:T(8,128)(2,1)S(1)} %collective-permute-done.8.refs_1_), channel_id=1, source_target_pairs={{6,0},{7,1},{4,2},{5,3},{2,4},{3,5},{0,6},{1,7},{14,8},{15,9},{12,... | collective-permute-start | bytes 393224 | tf_op jit(solution)/shard_map/ppermute | solution.py:20
  27.4 9.1 %collective-permute-start.16 = (bf16[512,512]{1,0:T(8,128)(2,1)S(1)}, bf16[512,512]{1,0:T(8,128)(2,1)S(1)}, u32[]{:S(2)}, u32[]{:S(2)}) collective-permute-start(bf16[512,512]{1,0:T(8,128)(2,1)S(1)} %turn.1.refs_1_), channel_id=1, source_target_pairs={{1,0},{0,1},{3,2},{2,3},{5,4},{4,5},{7,6},{6,7},{9,8},{8,9},{11,10... | collective-permute-start | bytes 1572872 | tf_op jit(solution)/shard_map/ppermute | solution.py:20
  36.2 4.2 %collective-permute-start.12 = (bf16[2,4,2,16,256]{4,3,2,1,0:T(8,128)(2,1)S(1)}, bf16[2,4,2,16,256]{4,3,2,1,0:T(8,128)(2,1)S(1)}, u32[]{:S(2)}, u32[]{:S(2)}) collective-permute-start(bf16[2,4,2,16,256]{4,3,2,1,0:T(8,128)(2,1)S(1)} %collective-permute-done.8.refs_1_), channel_id=1, source_target_pairs={{1,0},{0,1},{3,2},{2,3},{5,4},{4,5},{7,6},{6,7},{9,8},{8,9},{11,10... | collective-permute-start | bytes 393224 | tf_op jit(solution)/shard_map/ppermute | solution.py:20
  38.0 2.5 %collective-permute-start.17 = (bf16[2,4,2,16,256]{4,3,2,1,0:T(8,128)(2,1)S(1)}, bf16[2,4,2,16,256]{4,3,2,1,0:T(8,128)(2,1)S(1)}, u32[]{:S(2)}, u32[]{:S(2)}) collective-permute-start(bf16[2,4,2,16,256]{4,3,2,1,0:T(8,128)(2,1)S(1)} %collective-permute-done.14.refs_2_), channel_id=1, source_target_pairs={{1,0},{0,1},{3,2},{2,3},{5,4},{4,5},{7,6},{6,7},{9,8},{8,9},{11,10... | collective-permute-start | bytes 393224 | tf_op jit(solution)/shard_map/ppermute | solution.py:20
  38.4 2.0 %collective-permute-start.18 = (bf16[2,4,2,16,256]{4,3,2,1,0:T(8,128)(2,1)S(1)}, bf16[2,4,2,16,256]{4,3,2,1,0:T(8,128)(2,1)S(1)}, u32[]{:S(2)}, u32[]{:S(2)}) collective-permute-start(bf16[2,4,2,16,256]{4,3,2,1,0:T(8,128)(2,1)S(1)} %collective-permute-done.13.refs_3_), channel_id=1, source_target_pairs={{1,0},{0,1},{3,2},{2,3},{5,4},{4,5},{7,6},{6,7},{9,8},{8,9},{11,10... | collective-permute-start | bytes 393224 | tf_op jit(solution)/shard_map/ppermute | solution.py:20
  38.5 1.9 %collective-permute-start.19 = (bf16[2,4,2,16,256]{4,3,2,1,0:T(8,128)(2,1)S(1)}, bf16[2,4,2,16,256]{4,3,2,1,0:T(8,128)(2,1)S(1)}, u32[]{:S(2)}, u32[]{:S(2)}) collective-permute-start(bf16[2,4,2,16,256]{4,3,2,1,0:T(8,128)(2,1)S(1)} %collective-permute-done.15.refs_4_), channel_id=1, source_target_pairs={{1,0},{0,1},{3,2},{2,3},{5,4},{4,5},{7,6},{6,7},{9,8},{8,9},{11,10... | collective-permute-start | bytes 393224 | tf_op jit(solution)/shard_map/ppermute | solution.py:20

commit v19 on v17

--- a/solution.py
+++ b/solution.py
@@ -159,11 +159,12 @@
     scale = 1.0 / features**0.5
     row_step, query_step = here_ref.shape[0] // 2, here_ref.shape[1] // 2
     copies = []
-    for step in range(4):
-        queries = pl.ds(step % 2 * query_step, query_step)
-        rows = pl.ds(step // 2 * row_step, row_step)
+    for row, query, row_count in ((0, 0, 2 * row_step), (0, query_step, row_step), (row_step, query_step, row_step)):
+        rows, queries = pl.ds(row, row_count), pl.ds(query, query_step)
         here_ref[rows, queries] = (total_ref[rows, queries] + products(rows, turned_ref[:, queries])) * scale
-        copies.append(pltpu.make_async_copy(here_ref.at[rows, queries], out_ref.at[rows, queries], sem.at[step]))
+        copies.append(
+            pltpu.make_async_copy(here_ref.at[rows, queries], out_ref.at[rows, queries], sem.at[len(copies)])
+        )
         copies[-1].start()
     for copy in copies:
         copy.wait()
@@ -185,7 +186,7 @@
         scratch += [
             pltpu.VMEM((features, queries), jnp.bfloat16),
             pltpu.VMEM(shape, jnp.float32),
-            pltpu.SemaphoreType.DMA((4,)),
+            pltpu.SemaphoreType.DMA((3,)),
         ]
     return pl.pallas_call(
         functools.partial(score_kernel, grid, masks, other, len(parts), first, last),

time: 41.2 us -> 41.8 us (1.015)
  Pallas kernels: 12.3 us -> 12.9 us
    pallas_call x4, Pallas kernels: 7.07 us -> 7.68 us  [score(): pl.pallas_call(functools.partial(score_kernel, grid, masks, other, len(pa...]
  transfers between devices with their start and end apart: 20 -> 20, of which waited for: 8 -> 8; matrix products, arithmetic and copies ran while one was open for 0% -> 0% of each run, Pallas kernels for 22% -> 21%
where the time goes in v19:
time: 41.8 us; the launch traced here: 41.6 us
  starting transfers between devices  18.1 us (43%)
  Pallas kernels  12.9 us (31%)
  waiting for transfers between devices  10.4 us (25%)
    ppermute x20, starting transfers between devices, swap(): lax.ppermute(block, 'rows', [(row ^ step, row) for row in range(self.far...  18.1 us
    ppermute x20, waiting for transfers between devices, swap(): lax.ppermute(block, 'rows', [(row ^ step, row) for row in range(self.far...  10.4 us
    pallas_call x4, Pallas kernels, score(): pl.pallas_call(functools.partial(score_kernel, grid, masks, other, len(pa...  7.68 us
    pallas_call x2, Pallas kernels, stage(): pl.pallas_call(functools.partial(stage_kernel, first, arrays[0].shape[0]...  4.56 us
  transfers between devices with their start and end apart: 20, of which 8 were waited for; matrix products, arithmetic and copies ran while one was open for 0% of the time, Pallas kernels for 21%

profile of v19, /device:TPU:0, one launch (start us, length us, event | category | flops | bytes accessed | tf_op | source)
XLA Modules:
  0.0 41.6 jit_solution(6235148453722187242)
XLA Ops:
  0.0 5.0 %collective-permute-start = (bf16[2,16,2048]{2,1,0:T(8,128)(2,1)}, bf16[2,16,2048]{2,1,0:T(8,128)(2,1)S(1)}, u32[]{:S(2)}, u32[]{:S(2)}) collective-permute-start(bf16[2,16,2048]{2,1,0:T(8,128)(2,1)} %refs_1_.2), channel_id=1, source_target_pairs={{12,0},{13,1},{14,2},{15,3},{8,4},{9,5},{10,6},{11,7},{4,8},{5,9},... | collective-permute-start | bytes 393224 | tf_op jit(solution)/shard_map/ppermute | solution.py:21
  5.0 1.5 %collective-permute-start.7 = (bf16[1,2048,128]{2,1,0:T(8,128)(2,1)}, bf16[1,2048,128]{2,1,0:T(8,128)(2,1)S(1)}, u32[]{:S(2)}, u32[]{:S(2)}) collective-permute-start(bf16[1,2048,128]{2,1,0:T(8,128)(2,1)} %refs_2_.1), channel_id=1, source_target_pairs={{2,0},{3,1},{0,2},{1,3},{6,4},{7,5},{4,6},{5,7},{10,8},{11,9},{8,1... | collective-permute-start | bytes 1572872 | tf_op jit(solution)/shard_map/ppermute | solution.py:21
  6.6 0.0 collective-permute-start.1
  6.6 2.4 %stage.2 = (bf16[2048,2048]{1,0:T(8,128)(2,1)S(1)}, bf16[2,16,2048]{2,1,0:T(8,128)(2,1)S(1)}, bf16[1,2048,128]{2,1,0:T(8,128)(2,1)S(1)}) custom-call(bf16[2048,2048]{1,0:T(8,128)(2,1)} %refs_1_.3, bf16[2,16,2048]{2,1,0:T(8,128)(2,1)} %refs_1_.2, bf16[1,2048,128]{2,1,0:T(8,128)(2,1)} %refs_2_.1), custom_call_target="tpu_custom_call" | custom-call | flops 2788300032 | bytes 9043968 | tf_op jit(solution)/shard_map/stage/pallas_call | solution.py:56
  9.0 2.3 %collective-permute-start.2 = (bf16[2,16,2048]{2,1,0:T(8,128)(2,1)S(1)}, bf16[2,16,2048]{2,1,0:T(8,128)(2,1)S(1)}, u32[]{:S(2)}, u32[]{:S(2)}) collective-permute-start(bf16[2,16,2048]{2,1,0:T(8,128)(2,1)S(1)} %collective-permute-done.refs_3_), channel_id=1, source_target_pairs={{4,0},{5,1},{6,2},{7,3},{0,4},{1,5},{2,6},{3,7},{12,8},{13,9},{14,... | collective-permute-start | bytes 393224 | tf_op jit(solution)/shard_map/ppermute | solution.py:21
  11.3 2.2 %stage.3.refs_0_ = bf16[2048,2048]{1,0:T(8,128)(2,1)S(1)} custom-call(bf16[2048,2048]{1,0:T(8,128)(2,1)S(1)} %get-tuple-element.26.refs_0_, bf16[2048,2048]{1,0:T(8,128)(2,1)} %refs_1_.3), custom_call_target="tpu_custom_call", output_to_operand_aliasing={{}: (0, {})} | custom-call | flops 1 | bytes 8388608 | tf_op jit(solution)/shard_map/stage/pallas_call | solution.py:56
  13.5 0.6 %collective-permute-start.4 = (bf16[2,16,2048]{2,1,0:T(8,128)(2,1)S(1)}, bf16[2,16,2048]{2,1,0:T(8,128)(2,1)S(1)}, u32[]{:S(2)}, u32[]{:S(2)}) collective-permute-start(bf16[2,16,2048]{2,1,0:T(8,128)(2,1)S(1)} %collective-permute-done.3.refs_2_), channel_id=1, source_target_pairs={{1,0},{0,1},{3,2},{2,3},{5,4},{4,5},{7,6},{6,7},{9,8},{8,9},{11,10... | collective-permute-start | bytes 393224 | tf_op jit(solution)/shard_map/ppermute | solution.py:21
  14.1 1.4 %collective-permute-done.2.refs_4_ = bf16[2,16,2048]{2,1,0:T(8,128)(2,1)S(1)} collective-permute-done((bf16[2,16,2048]{2,1,0:T(8,128)(2,1)S(1)}, bf16[2,16,2048]{2,1,0:T(8,128)(2,1)S(1)}, u32[]{:S(2)}, u32[]{:S(2)}) %collective-permute-start.2) | collective-permute-done | bytes 131104 | tf_op jit(solution)/shard_map/ppermute | solution.py:21
  15.5 1.3 %collective-permute-done.6.refs_7_ = bf16[2,16,2048]{2,1,0:T(8,128)(2,1)S(1)} collective-permute-done((bf16[2,16,2048]{2,1,0:T(8,128)(2,1)S(1)}, bf16[2,16,2048]{2,1,0:T(8,128)(2,1)S(1)}, u32[]{:S(2)}, u32[]{:S(2)}) %collective-permute-start.6) | collective-permute-done | bytes 131104 | tf_op jit(solution)/shard_map/ppermute | solution.py:21
  16.9 1.8 %collective-permute-done.7.refs_9_ = bf16[1,2048,128]{2,1,0:T(8,128)(2,1)S(1)} collective-permute-done((bf16[1,2048,128]{2,1,0:T(8,128)(2,1)}, bf16[1,2048,128]{2,1,0:T(8,128)(2,1)S(1)}, u32[]{:S(2)}, u32[]{:S(2)}) %collective-permute-start.7) | collective-permute-done | bytes 524320 | tf_op jit(solution)/shard_map/ppermute | solution.py:21
  18.6 0.4 %condition.1.refs_0_ = bf16[2,4,2,16,256]{4,3,2,1,0:T(8,128)(2,1)S(1)} custom-call(bf16[2,16,2048]{2,1,0:T(8,128)(2,1)S(1)} %get-tuple-element.28.refs_0_, bf16[2,16,2048]{2,1,0:T(8,128)(2,1)S(1)} %collective-permute-done.1.refs_1_, bf16[2,16,2048]{2,1,0:T(8,128)(2,1)S(1)} %collective-permute-done.3.refs_2_, ...), custom_call_target="tpu_custom_call" | custom-call | flops 268435456 | bytes 3145728 | tf_op jit(solution)/shard_map/condition/pallas_call | solution.py:91
  19.1 0.1 collective-permute-start.10
  19.2 1.4 %collective-permute-start.8 = (bf16[2,4,2,16,256]{4,3,2,1,0:T(8,128)(2,1)S(1)}, bf16[2,4,2,16,256]{4,3,2,1,0:T(8,128)(2,1)S(1)}, u32[]{:S(2)}, u32[]{:S(2)}) collective-permute-start(bf16[2,4,2,16,256]{4,3,2,1,0:T(8,128)(2,1)S(1)} %condition.1.refs_0_), channel_id=1, source_target_pairs={{12,0},{13,1},{14,2},{15,3},{8,4},{9,5},{10,6},{11,7},{4,8},{5,9},... | collective-permute-start | bytes 393224 | tf_op jit(solution)/shard_map/ppermute | solution.py:21
  20.6 1.3 %collective-permute-start.9 = (bf16[2,4,2,16,256]{4,3,2,1,0:T(8,128)(2,1)S(1)}, bf16[2,4,2,16,256]{4,3,2,1,0:T(8,128)(2,1)S(1)}, u32[]{:S(2)}, u32[]{:S(2)}) collective-permute-start(bf16[2,4,2,16,256]{4,3,2,1,0:T(8,128)(2,1)S(1)} %condition.1.refs_0_), channel_id=1, source_target_pairs={{2,0},{3,1},{0,2},{1,3},{6,4},{7,5},{4,6},{5,7},{10,8},{11,9},{8,1... | collective-permute-start | bytes 393224 | tf_op jit(solution)/shard_map/ppermute | solution.py:21
  21.9 3.0 %collective-permute-done.10.refs_2_ = bf16[2,4,2,16,256]{4,3,2,1,0:T(8,128)(2,1)S(1)} collective-permute-done((bf16[2,4,2,16,256]{4,3,2,1,0:T(8,128)(2,1)S(1)}, bf16[2,4,2,16,256]{4,3,2,1,0:T(8,128)(2,1)S(1)}, u32[]{:S(2)}, u32[]{:S(2)}) %collective-permute-start.10) | collective-permute-done | bytes 131104 | tf_op jit(solution)/shard_map/ppermute | solution.py:21
  24.9 1.3 %collective-permute-start.11 = (bf16[2,4,2,16,256]{4,3,2,1,0:T(8,128)(2,1)S(1)}, bf16[2,4,2,16,256]{4,3,2,1,0:T(8,128)(2,1)S(1)}, u32[]{:S(2)}, u32[]{:S(2)}) collective-permute-start(bf16[2,4,2,16,256]{4,3,2,1,0:T(8,128)(2,1)S(1)} %collective-permute-done.10.refs_2_), channel_id=1, source_target_pairs={{2,0},{3,1},{0,2},{1,3},{6,4},{7,5},{4,6},{5,7},{10,8},{11,9},{8,1... | collective-permute-start | bytes 393224 | tf_op jit(solution)/shard_map/ppermute | solution.py:21
  26.2 0.9 %collective-permute-done.8.refs_1_ = bf16[2,4,2,16,256]{4,3,2,1,0:T(8,128)(2,1)S(1)} collective-permute-done((bf16[2,4,2,16,256]{4,3,2,1,0:T(8,128)(2,1)S(1)}, bf16[2,4,2,16,256]{4,3,2,1,0:T(8,128)(2,1)S(1)}, u32[]{:S(2)}, u32[]{:S(2)}) %collective-permute-start.8) | collective-permute-done | bytes 131104 | tf_op jit(solution)/shard_map/ppermute | solution.py:21
  27.0 1.5 %collective-permute-start.13 = (bf16[2,4,2,16,256]{4,3,2,1,0:T(8,128)(2,1)S(1)}, bf16[2,4,2,16,256]{4,3,2,1,0:T(8,128)(2,1)S(1)}, u32[]{:S(2)}, u32[]{:S(2)}) collective-permute-start(bf16[2,4,2,16,256]{4,3,2,1,0:T(8,128)(2,1)S(1)} %collective-permute-done.8.refs_1_), channel_id=1, source_target_pairs={{4,0},{5,1},{6,2},{7,3},{0,4},{1,5},{2,6},{3,7},{12,8},{13,9},{14,... | collective-permute-start | bytes 393224 | tf_op jit(solution)/shard_map/ppermute | solution.py:21
  28.5 1.6 %collective-permute-start.14 = (bf16[2,4,2,16,256]{4,3,2,1,0:T(8,128)(2,1)S(1)}, bf16[2,4,2,16,256]{4,3,2,1,0:T(8,128)(2,1)S(1)}, u32[]{:S(2)}, u32[]{:S(2)}) collective-permute-start(bf16[2,4,2,16,256]{4,3,2,1,0:T(8,128)(2,1)S(1)} %collective-permute-done.8.refs_1_), channel_id=1, source_target_pairs={{2,0},{3,1},{0,2},{1,3},{6,4},{7,5},{4,6},{5,7},{10,8},{11,9},{8,1... | collective-permute-start | bytes 393224 | tf_op jit(solution)/shard_map/ppermute | solution.py:21
  30.2 0.4 collective-permute-start.15
  30.5 0.4 collective-permute-done.11.refs_3_
  30.9 0.2 turn.1.refs_1_
  31.2 0.1 collective-permute-start.16
  31.3 1.3 %score.4.refs_2_ = f32[2048,512]{1,0:T(8,128)S(1)} custom-call(bf16[2048,2048]{1,0:T(8,128)(2,1)S(1)} %stage.3.refs_0_, bf16[512,512]{1,0:T(8,128)(2,1)S(1)} %turn.1.refs_1_), custom_call_target="tpu_custom_call" | custom-call | flops 21474836480 | bytes 4194304 | tf_op jit(solution)/shard_map/score/pallas_call | solution.py:191
  32.5 0.6 %collective-permute-start.12 = (bf16[2,4,2,16,256]{4,3,2,1,0:T(8,128)(2,1)S(1)}, bf16[2,4,2,16,256]{4,3,2,1,0:T(8,128)(2,1)S(1)}, u32[]{:S(2)}, u32[]{:S(2)}) collective-permute-start(bf16[2,4,2,16,256]{4,3,2,1,0:T(8,128)(2,1)S(1)} %collective-permute-done.8.refs_1_), channel_id=1, source_target_pairs={{1,0},{0,1},{3,2},{2,3},{5,4},{4,5},{7,6},{6,7},{9,8},{8,9},{11,10... | collective-permute-start | bytes 393224 | tf_op jit(solution)/shard_map/ppermute | solution.py:21
  33.1 0.1 collective-permute-done.16.refs_1_
  33.2 1.4 %score.5.refs_5_ = f32[2048,512]{1,0:T(8,128)S(1)} custom-call(bf16[2048,2048]{1,0:T(8,128)(2,1)S(1)} %stage.3.refs_0_, bf16[512,512]{1,0:T(8,128)(2,1)S(1)} %collective-permute-done.16.refs_1_, f32[2048,512]{1,0:T(8,128)S(1)} %score.4.refs_2_), custom_call_target="tpu_custom_call", output_to_operand_aliasing={{}: (2, {})} | custom-call | flops 1073741824 | bytes 4194304 | tf_op jit(solution)/shard_map/score/pallas_call | solution.py:191
  34.6 1.4 %collective-permute-done.15.refs_4_ = bf16[2,4,2,16,256]{4,3,2,1,0:T(8,128)(2,1)S(1)} collective-permute-done((bf16[2,4,2,16,256]{4,3,2,1,0:T(8,128)(2,1)S(1)}, bf16[2,4,2,16,256]{4,3,2,1,0:T(8,128)(2,1)S(1)}, u32[]{:S(2)}, u32[]{:S(2)}) %collective-permute-start.15) | collective-permute-done | bytes 131104 | tf_op jit(solution)/shard_map/ppermute | solution.py:21
  36.0 0.5 %collective-permute-start.18 = (bf16[2,4,2,16,256]{4,3,2,1,0:T(8,128)(2,1)S(1)}, bf16[2,4,2,16,256]{4,3,2,1,0:T(8,128)(2,1)S(1)}, u32[]{:S(2)}, u32[]{:S(2)}) collective-permute-start(bf16[2,4,2,16,256]{4,3,2,1,0:T(8,128)(2,1)S(1)} %collective-permute-done.13.refs_3_), channel_id=1, source_target_pairs={{1,0},{0,1},{3,2},{2,3},{5,4},{4,5},{7,6},{6,7},{9,8},{8,9},{11,10... | collective-permute-start | bytes 393224 | tf_op jit(solution)/shard_map/ppermute | solution.py:21
  36.5 0.0 collective-permute-start.19
  36.6 1.5 %score.6.refs_5_ = f32[2048,512]{1,0:T(8,128)S(1)} custom-call(bf16[2048,2048]{1,0:T(8,128)(2,1)S(1)} %stage.3.refs_0_, bf16[2,4,2,16,256]{4,3,2,1,0:T(8,128)(2,1)S(1)} %collective-permute-done.8.refs_1_, bf16[2,4,2,16,256]{4,3,2,1,0:T(8,128)(2,1)S(1)} %collective-permute-done.14.refs_2_, ...), custom_call_target="tpu_custom_call", output_to_operand_aliasing={{}: (5, {})} | custom-call | flops 1073741824 | bytes 4194304 | tf_op jit(solution)/shard_map/score/pallas_call | solution.py:191
  38.1 3.5 %score.7 = f32[2048,512]{1,0:T(8,128)} custom-call(bf16[2048,2048]{1,0:T(8,128)(2,1)S(1)} %stage.3.refs_0_, bf16[2,4,2,16,256]{4,3,2,1,0:T(8,128)(2,1)S(1)} %collective-permute-done.12.refs_1_, bf16[2,4,2,16,256]{4,3,2,1,0:T(8,128)(2,1)S(1)} %collective-permute-done.17.refs_2_, bf16[2,4,2,16,256]{4,3,2,1,0:T(8,128)(2,1)S(1)} %collective-permute-done.18.refs_3_, ...), custom_call_target="tpu_custom_call" | custom-call | flops 1073741824 | bytes 4194304 | tf_op jit(solution)/shard_map/score/pallas_call | solution.py:191
  (16 shorter events, 0.0 us)
Async XLA Ops:
  0.0 9.0 %collective-permute-start = (bf16[2,16,2048]{2,1,0:T(8,128)(2,1)}, bf16[2,16,2048]{2,1,0:T(8,128)(2,1)S(1)}, u32[]{:S(2)}, u32[]{:S(2)}) collective-permute-start(bf16[2,16,2048]{2,1,0:T(8,128)(2,1)} %refs_1_.2), channel_id=1, source_target_pairs={{12,0},{13,1},{14,2},{15,3},{8,4},{9,5},{10,6},{11,7},{4,8},{5,9},... | collective-permute-start | bytes 393224 | tf_op jit(solution)/shard_map/ppermute | solution.py:21
  5.0 13.6 %collective-permute-start.7 = (bf16[1,2048,128]{2,1,0:T(8,128)(2,1)}, bf16[1,2048,128]{2,1,0:T(8,128)(2,1)S(1)}, u32[]{:S(2)}, u32[]{:S(2)}) collective-permute-start(bf16[1,2048,128]{2,1,0:T(8,128)(2,1)} %refs_2_.1), channel_id=1, source_target_pairs={{2,0},{3,1},{0,2},{1,3},{6,4},{7,5},{4,6},{5,7},{10,8},{11,9},{8,1... | collective-permute-start | bytes 1572872 | tf_op jit(solution)/shard_map/ppermute | solution.py:21
  6.6 2.4 %collective-permute-start.1 = (bf16[2,16,2048]{2,1,0:T(8,128)(2,1)}, bf16[2,16,2048]{2,1,0:T(8,128)(2,1)S(1)}, u32[]{:S(2)}, u32[]{:S(2)}) collective-permute-start(bf16[2,16,2048]{2,1,0:T(8,128)(2,1)} %refs_1_.2), channel_id=1, source_target_pairs={{1,0},{0,1},{3,2},{2,3},{5,4},{4,5},{7,6},{6,7},{9,8},{8,9},{11,10... | collective-permute-start | bytes 393224 | tf_op jit(solution)/shard_map/ppermute | solution.py:21
  6.6 6.9 %collective-permute-start.3 = (bf16[2,16,2048]{2,1,0:T(8,128)(2,1)}, bf16[2,16,2048]{2,1,0:T(8,128)(2,1)S(1)}, u32[]{:S(2)}, u32[]{:S(2)}) collective-permute-start(bf16[2,16,2048]{2,1,0:T(8,128)(2,1)} %refs_1_.2), channel_id=1, source_target_pairs={{4,0},{5,1},{6,2},{7,3},{0,4},{1,5},{2,6},{3,7},{12,8},{13,9},{14,... | collective-permute-start | bytes 393224 | tf_op jit(solution)/shard_map/ppermute | solution.py:21
  9.0 6.5 %collective-permute-start.2 = (bf16[2,16,2048]{2,1,0:T(8,128)(2,1)S(1)}, bf16[2,16,2048]{2,1,0:T(8,128)(2,1)S(1)}, u32[]{:S(2)}, u32[]{:S(2)}) collective-permute-start(bf16[2,16,2048]{2,1,0:T(8,128)(2,1)S(1)} %collective-permute-done.refs_3_), channel_id=1, source_target_pairs={{4,0},{5,1},{6,2},{7,3},{0,4},{1,5},{2,6},{3,7},{12,8},{13,9},{14,... | collective-permute-start | bytes 393224 | tf_op jit(solution)/shard_map/ppermute | solution.py:21
  11.3 4.2 %collective-permute-start.5 = (bf16[2,16,2048]{2,1,0:T(8,128)(2,1)S(1)}, bf16[2,16,2048]{2,1,0:T(8,128)(2,1)S(1)}, u32[]{:S(2)}, u32[]{:S(2)}) collective-permute-start(bf16[2,16,2048]{2,1,0:T(8,128)(2,1)S(1)} %collective-permute-done.refs_3_), channel_id=1, source_target_pairs={{1,0},{0,1},{3,2},{2,3},{5,4},{4,5},{7,6},{6,7},{9,8},{8,9},{11,10... | collective-permute-start | bytes 393224 | tf_op jit(solution)/shard_map/ppermute | solution.py:21
  13.5 2.0 %collective-permute-start.4 = (bf16[2,16,2048]{2,1,0:T(8,128)(2,1)S(1)}, bf16[2,16,2048]{2,1,0:T(8,128)(2,1)S(1)}, u32[]{:S(2)}, u32[]{:S(2)}) collective-permute-start(bf16[2,16,2048]{2,1,0:T(8,128)(2,1)S(1)} %collective-permute-done.3.refs_2_), channel_id=1, source_target_pairs={{1,0},{0,1},{3,2},{2,3},{5,4},{4,5},{7,6},{6,7},{9,8},{8,9},{11,10... | collective-permute-start | bytes 393224 | tf_op jit(solution)/shard_map/ppermute | solution.py:21
  15.5 1.3 %collective-permute-start.6 = (bf16[2,16,2048]{2,1,0:T(8,128)(2,1)S(1)}, bf16[2,16,2048]{2,1,0:T(8,128)(2,1)S(1)}, u32[]{:S(2)}, u32[]{:S(2)}) collective-permute-start(bf16[2,16,2048]{2,1,0:T(8,128)(2,1)S(1)} %collective-permute-done.2.refs_4_), channel_id=1, source_target_pairs={{1,0},{0,1},{3,2},{2,3},{5,4},{4,5},{7,6},{6,7},{9,8},{8,9},{11,10... | collective-permute-start | bytes 393224 | tf_op jit(solution)/shard_map/ppermute | solution.py:21
  19.1 5.8 %collective-permute-start.10 = (bf16[2,4,2,16,256]{4,3,2,1,0:T(8,128)(2,1)S(1)}, bf16[2,4,2,16,256]{4,3,2,1,0:T(8,128)(2,1)S(1)}, u32[]{:S(2)}, u32[]{:S(2)}) collective-permute-start(bf16[2,4,2,16,256]{4,3,2,1,0:T(8,128)(2,1)S(1)} %condition.1.refs_0_), channel_id=1, source_target_pairs={{4,0},{5,1},{6,2},{7,3},{0,4},{1,5},{2,6},{3,7},{12,8},{13,9},{14,... | collective-permute-start | bytes 393224 | tf_op jit(solution)/shard_map/ppermute | solution.py:21
  19.2 7.9 %collective-permute-start.8 = (bf16[2,4,2,16,256]{4,3,2,1,0:T(8,128)(2,1)S(1)}, bf16[2,4,2,16,256]{4,3,2,1,0:T(8,128)(2,1)S(1)}, u32[]{:S(2)}, u32[]{:S(2)}) collective-permute-start(bf16[2,4,2,16,256]{4,3,2,1,0:T(8,128)(2,1)S(1)} %condition.1.refs_0_), channel_id=1, source_target_pairs={{12,0},{13,1},{14,2},{15,3},{8,4},{9,5},{10,6},{11,7},{4,8},{5,9},... | collective-permute-start | bytes 393224 | tf_op jit(solution)/shard_map/ppermute | solution.py:21
  20.6 9.9 %collective-permute-start.9 = (bf16[2,4,2,16,256]{4,3,2,1,0:T(8,128)(2,1)S(1)}, bf16[2,4,2,16,256]{4,3,2,1,0:T(8,128)(2,1)S(1)}, u32[]{:S(2)}, u32[]{:S(2)}) collective-permute-start(bf16[2,4,2,16,256]{4,3,2,1,0:T(8,128)(2,1)S(1)} %condition.1.refs_0_), channel_id=1, source_target_pairs={{2,0},{3,1},{0,2},{1,3},{6,4},{7,5},{4,6},{5,7},{10,8},{11,9},{8,1... | collective-permute-start | bytes 393224 | tf_op jit(solution)/shard_map/ppermute | solution.py:21
  24.9 6.0 %collective-permute-start.11 = (bf16[2,4,2,16,256]{4,3,2,1,0:T(8,128)(2,1)S(1)}, bf16[2,4,2,16,256]{4,3,2,1,0:T(8,128)(2,1)S(1)}, u32[]{:S(2)}, u32[]{:S(2)}) collective-permute-start(bf16[2,4,2,16,256]{4,3,2,1,0:T(8,128)(2,1)S(1)} %collective-permute-done.10.refs_2_), channel_id=1, source_target_pairs={{2,0},{3,1},{0,2},{1,3},{6,4},{7,5},{4,6},{5,7},{10,8},{11,9},{8,1... | collective-permute-start | bytes 393224 | tf_op jit(solution)/shard_map/ppermute | solution.py:21
  27.0 7.5 %collective-permute-start.13 = (bf16[2,4,2,16,256]{4,3,2,1,0:T(8,128)(2,1)S(1)}, bf16[2,4,2,16,256]{4,3,2,1,0:T(8,128)(2,1)S(1)}, u32[]{:S(2)}, u32[]{:S(2)}) collective-permute-start(bf16[2,4,2,16,256]{4,3,2,1,0:T(8,128)(2,1)S(1)} %collective-permute-done.8.refs_1_), channel_id=1, source_target_pairs={{4,0},{5,1},{6,2},{7,3},{0,4},{1,5},{2,6},{3,7},{12,8},{13,9},{14,... | collective-permute-start | bytes 393224 | tf_op jit(solution)/shard_map/ppermute | solution.py:21
  28.5 6.1 %collective-permute-start.14 = (bf16[2,4,2,16,256]{4,3,2,1,0:T(8,128)(2,1)S(1)}, bf16[2,4,2,16,256]{4,3,2,1,0:T(8,128)(2,1)S(1)}, u32[]{:S(2)}, u32[]{:S(2)}) collective-permute-start(bf16[2,4,2,16,256]{4,3,2,1,0:T(8,128)(2,1)S(1)} %collective-permute-done.8.refs_1_), channel_id=1, source_target_pairs={{2,0},{3,1},{0,2},{1,3},{6,4},{7,5},{4,6},{5,7},{10,8},{11,9},{8,1... | collective-permute-start | bytes 393224 | tf_op jit(solution)/shard_map/ppermute | solution.py:21
  30.2 5.9 %collective-permute-start.15 = (bf16[2,4,2,16,256]{4,3,2,1,0:T(8,128)(2,1)S(1)}, bf16[2,4,2,16,256]{4,3,2,1,0:T(8,128)(2,1)S(1)}, u32[]{:S(2)}, u32[]{:S(2)}) collective-permute-start(bf16[2,4,2,16,256]{4,3,2,1,0:T(8,128)(2,1)S(1)} %collective-permute-done.8.refs_1_), channel_id=1, source_target_pairs={{6,0},{7,1},{4,2},{5,3},{2,4},{3,5},{0,6},{1,7},{14,8},{15,9},{12,... | collective-permute-start | bytes 393224 | tf_op jit(solution)/shard_map/ppermute | solution.py:21
  31.2 2.0 %collective-permute-start.16 = (bf16[512,512]{1,0:T(8,128)(2,1)S(1)}, bf16[512,512]{1,0:T(8,128)(2,1)S(1)}, u32[]{:S(2)}, u32[]{:S(2)}) collective-permute-start(bf16[512,512]{1,0:T(8,128)(2,1)S(1)} %turn.1.refs_1_), channel_id=1, source_target_pairs={{1,0},{0,1},{3,2},{2,3},{5,4},{4,5},{7,6},{6,7},{9,8},{8,9},{11,10... | collective-permute-start | bytes 1572872 | tf_op jit(solution)/shard_map/ppermute | solution.py:21
  32.5 5.5 %collective-permute-start.12 = (bf16[2,4,2,16,256]{4,3,2,1,0:T(8,128)(2,1)S(1)}, bf16[2,4,2,16,256]{4,3,2,1,0:T(8,128)(2,1)S(1)}, u32[]{:S(2)}, u32[]{:S(2)}) collective-permute-start(bf16[2,4,2,16,256]{4,3,2,1,0:T(8,128)(2,1)S(1)} %collective-permute-done.8.refs_1_), channel_id=1, source_target_pairs={{1,0},{0,1},{3,2},{2,3},{5,4},{4,5},{7,6},{6,7},{9,8},{8,9},{11,10... | collective-permute-start | bytes 393224 | tf_op jit(solution)/shard_map/ppermute | solution.py:21
  36.0 2.0 %collective-permute-start.17 = (bf16[2,4,2,16,256]{4,3,2,1,0:T(8,128)(2,1)S(1)}, bf16[2,4,2,16,256]{4,3,2,1,0:T(8,128)(2,1)S(1)}, u32[]{:S(2)}, u32[]{:S(2)}) collective-permute-start(bf16[2,4,2,16,256]{4,3,2,1,0:T(8,128)(2,1)S(1)} %collective-permute-done.14.refs_2_), channel_id=1, source_target_pairs={{1,0},{0,1},{3,2},{2,3},{5,4},{4,5},{7,6},{6,7},{9,8},{8,9},{11,10... | collective-permute-start | bytes 393224 | tf_op jit(solution)/shard_map/ppermute | solution.py:21
  36.0 2.0 %collective-permute-start.18 = (bf16[2,4,2,16,256]{4,3,2,1,0:T(8,128)(2,1)S(1)}, bf16[2,4,2,16,256]{4,3,2,1,0:T(8,128)(2,1)S(1)}, u32[]{:S(2)}, u32[]{:S(2)}) collective-permute-start(bf16[2,4,2,16,256]{4,3,2,1,0:T(8,128)(2,1)S(1)} %collective-permute-done.13.refs_3_), channel_id=1, source_target_pairs={{1,0},{0,1},{3,2},{2,3},{5,4},{4,5},{7,6},{6,7},{9,8},{8,9},{11,10... | collective-permute-start | bytes 393224 | tf_op jit(solution)/shard_map/ppermute | solution.py:21
  36.5 1.5 %collective-permute-start.19 = (bf16[2,4,2,16,256]{4,3,2,1,0:T(8,128)(2,1)S(1)}, bf16[2,4,2,16,256]{4,3,2,1,0:T(8,128)(2,1)S(1)}, u32[]{:S(2)}, u32[]{:S(2)}) collective-permute-start(bf16[2,4,2,16,256]{4,3,2,1,0:T(8,128)(2,1)S(1)} %collective-permute-done.15.refs_4_), channel_id=1, source_target_pairs={{1,0},{0,1},{3,2},{2,3},{5,4},{4,5},{7,6},{6,7},{9,8},{8,9},{11,10... | collective-permute-start | bytes 393224 | tf_op jit(solution)/shard_map/ppermute | solution.py:21

commit v20 on v19

--- a/solution.py
+++ b/solution.py
@@ -157,14 +157,12 @@
     turned_ref, here_ref, sem = refs
     turned_ref[...] = turned
     scale = 1.0 / features**0.5
-    row_step, query_step = here_ref.shape[0] // 2, here_ref.shape[1] // 2
+    quarter = here_ref.shape[0] // 4
     copies = []
-    for row, query, row_count in ((0, 0, 2 * row_step), (0, query_step, row_step), (row_step, query_step, row_step)):
-        rows, queries = pl.ds(row, row_count), pl.ds(query, query_step)
-        here_ref[rows, queries] = (total_ref[rows, queries] + products(rows, turned_ref[:, queries])) * scale
-        copies.append(
-            pltpu.make_async_copy(here_ref.at[rows, queries], out_ref.at[rows, queries], sem.at[len(copies)])
-        )
+    for row, count in ((0, 2), (2, 1), (3, 1)):
+        rows = pl.ds(row * quarter, count * quarter)
+        here_ref[rows] = (total_ref[rows] + products(rows, turned_ref[...])) * scale
+        copies.append(pltpu.make_async_copy(here_ref.at[rows], out_ref.at[rows], sem.at[len(copies)]))
         copies[-1].start()
     for copy in copies:
         copy.wait()

time: 41.8 us -> 41.2 us (0.986)
  Pallas kernels: 12.9 us -> 12.3 us
    pallas_call x4, Pallas kernels: 7.68 us -> 7.07 us  [score(): pl.pallas_call(functools.partial(score_kernel, grid, masks, other, len(pa...]
  transfers between devices with their start and end apart: 20 -> 20, of which waited for: 8 -> 8; matrix products, arithmetic and copies ran while one was open for 0% -> 0% of each run, Pallas kernels for 21% -> 22%
where the time goes in v20:
time: 41.2 us; the launch traced here: 41 us
  starting transfers between devices  18.1 us (44%)
  Pallas kernels  12.3 us (30%)
  waiting for transfers between devices  10.4 us (25%)
    ppermute x20, starting transfers between devices, swap(): lax.ppermute(block, 'rows', [(row ^ step, row) for row in range(self.far...  18.1 us
    ppermute x20, waiting for transfers between devices, swap(): lax.ppermute(block, 'rows', [(row ^ step, row) for row in range(self.far...  10.4 us
    pallas_call x4, Pallas kernels, score(): pl.pallas_call(functools.partial(score_kernel, grid, masks, other, len(pa...  7.07 us
    pallas_call x2, Pallas kernels, stage(): pl.pallas_call(functools.partial(stage_kernel, first, arrays[0].shape[0]...  4.56 us
  transfers between devices with their start and end apart: 20, of which 8 were waited for; matrix products, arithmetic and copies ran while one was open for 0% of the time, Pallas kernels for 22%

profile of v20, /device:TPU:0, one launch (start us, length us, event | category | flops | bytes accessed | tf_op | source)
XLA Modules:
  0.0 41.0 jit_solution(15082343960548896486)
XLA Ops:
  0.0 5.0 %collective-permute-start = (bf16[2,16,2048]{2,1,0:T(8,128)(2,1)}, bf16[2,16,2048]{2,1,0:T(8,128)(2,1)S(1)}, u32[]{:S(2)}, u32[]{:S(2)}) collective-permute-start(bf16[2,16,2048]{2,1,0:T(8,128)(2,1)} %refs_1_.2), channel_id=1, source_target_pairs={{12,0},{13,1},{14,2},{15,3},{8,4},{9,5},{10,6},{11,7},{4,8},{5,9},... | collective-permute-start | bytes 393224 | tf_op jit(solution)/shard_map/ppermute | solution.py:21
  5.0 1.5 %collective-permute-start.7 = (bf16[1,2048,128]{2,1,0:T(8,128)(2,1)}, bf16[1,2048,128]{2,1,0:T(8,128)(2,1)S(1)}, u32[]{:S(2)}, u32[]{:S(2)}) collective-permute-start(bf16[1,2048,128]{2,1,0:T(8,128)(2,1)} %refs_2_.1), channel_id=1, source_target_pairs={{2,0},{3,1},{0,2},{1,3},{6,4},{7,5},{4,6},{5,7},{10,8},{11,9},{8,1... | collective-permute-start | bytes 1572872 | tf_op jit(solution)/shard_map/ppermute | solution.py:21
  6.6 0.0 collective-permute-start.1
  6.6 2.4 %stage.2 = (bf16[2048,2048]{1,0:T(8,128)(2,1)S(1)}, bf16[2,16,2048]{2,1,0:T(8,128)(2,1)S(1)}, bf16[1,2048,128]{2,1,0:T(8,128)(2,1)S(1)}) custom-call(bf16[2048,2048]{1,0:T(8,128)(2,1)} %refs_1_.3, bf16[2,16,2048]{2,1,0:T(8,128)(2,1)} %refs_1_.2, bf16[1,2048,128]{2,1,0:T(8,128)(2,1)} %refs_2_.1), custom_call_target="tpu_custom_call" | custom-call | flops 2788300032 | bytes 9043968 | tf_op jit(solution)/shard_map/stage/pallas_call | solution.py:56
  9.0 2.3 %collective-permute-start.2 = (bf16[2,16,2048]{2,1,0:T(8,128)(2,1)S(1)}, bf16[2,16,2048]{2,1,0:T(8,128)(2,1)S(1)}, u32[]{:S(2)}, u32[]{:S(2)}) collective-permute-start(bf16[2,16,2048]{2,1,0:T(8,128)(2,1)S(1)} %collective-permute-done.refs_3_), channel_id=1, source_target_pairs={{4,0},{5,1},{6,2},{7,3},{0,4},{1,5},{2,6},{3,7},{12,8},{13,9},{14,... | collective-permute-start | bytes 393224 | tf_op jit(solution)/shard_map/ppermute | solution.py:21
  11.3 2.2 %stage.3.refs_0_ = bf16[2048,2048]{1,0:T(8,128)(2,1)S(1)} custom-call(bf16[2048,2048]{1,0:T(8,128)(2,1)S(1)} %get-tuple-element.26.refs_0_, bf16[2048,2048]{1,0:T(8,128)(2,1)} %refs_1_.3), custom_call_target="tpu_custom_call", output_to_operand_aliasing={{}: (0, {})} | custom-call | flops 1 | bytes 8388608 | tf_op jit(solution)/shard_map/stage/pallas_call | solution.py:56
  13.5 0.6 %collective-permute-start.4 = (bf16[2,16,2048]{2,1,0:T(8,128)(2,1)S(1)}, bf16[2,16,2048]{2,1,0:T(8,128)(2,1)S(1)}, u32[]{:S(2)}, u32[]{:S(2)}) collective-permute-start(bf16[2,16,2048]{2,1,0:T(8,128)(2,1)S(1)} %collective-permute-done.3.refs_2_), channel_id=1, source_target_pairs={{1,0},{0,1},{3,2},{2,3},{5,4},{4,5},{7,6},{6,7},{9,8},{8,9},{11,10... | collective-permute-start | bytes 393224 | tf_op jit(solution)/shard_map/ppermute | solution.py:21
  14.1 1.4 %collective-permute-done.2.refs_4_ = bf16[2,16,2048]{2,1,0:T(8,128)(2,1)S(1)} collective-permute-done((bf16[2,16,2048]{2,1,0:T(8,128)(2,1)S(1)}, bf16[2,16,2048]{2,1,0:T(8,128)(2,1)S(1)}, u32[]{:S(2)}, u32[]{:S(2)}) %collective-permute-start.2) | collective-permute-done | bytes 131104 | tf_op jit(solution)/shard_map/ppermute | solution.py:21
  15.5 1.3 %collective-permute-done.6.refs_7_ = bf16[2,16,2048]{2,1,0:T(8,128)(2,1)S(1)} collective-permute-done((bf16[2,16,2048]{2,1,0:T(8,128)(2,1)S(1)}, bf16[2,16,2048]{2,1,0:T(8,128)(2,1)S(1)}, u32[]{:S(2)}, u32[]{:S(2)}) %collective-permute-start.6) | collective-permute-done | bytes 131104 | tf_op jit(solution)/shard_map/ppermute | solution.py:21
  16.9 1.8 %collective-permute-done.7.refs_9_ = bf16[1,2048,128]{2,1,0:T(8,128)(2,1)S(1)} collective-permute-done((bf16[1,2048,128]{2,1,0:T(8,128)(2,1)}, bf16[1,2048,128]{2,1,0:T(8,128)(2,1)S(1)}, u32[]{:S(2)}, u32[]{:S(2)}) %collective-permute-start.7) | collective-permute-done | bytes 524320 | tf_op jit(solution)/shard_map/ppermute | solution.py:21
  18.6 0.4 %condition.1.refs_0_ = bf16[2,4,2,16,256]{4,3,2,1,0:T(8,128)(2,1)S(1)} custom-call(bf16[2,16,2048]{2,1,0:T(8,128)(2,1)S(1)} %get-tuple-element.28.refs_0_, bf16[2,16,2048]{2,1,0:T(8,128)(2,1)S(1)} %collective-permute-done.1.refs_1_, bf16[2,16,2048]{2,1,0:T(8,128)(2,1)S(1)} %collective-permute-done.3.refs_2_, ...), custom_call_target="tpu_custom_call" | custom-call | flops 268435456 | bytes 3145728 | tf_op jit(solution)/shard_map/condition/pallas_call | solution.py:91
  19.1 0.1 collective-permute-start.10
  19.2 1.4 %collective-permute-start.8 = (bf16[2,4,2,16,256]{4,3,2,1,0:T(8,128)(2,1)S(1)}, bf16[2,4,2,16,256]{4,3,2,1,0:T(8,128)(2,1)S(1)}, u32[]{:S(2)}, u32[]{:S(2)}) collective-permute-start(bf16[2,4,2,16,256]{4,3,2,1,0:T(8,128)(2,1)S(1)} %condition.1.refs_0_), channel_id=1, source_target_pairs={{12,0},{13,1},{14,2},{15,3},{8,4},{9,5},{10,6},{11,7},{4,8},{5,9},... | collective-permute-start | bytes 393224 | tf_op jit(solution)/shard_map/ppermute | solution.py:21
  20.6 1.3 %collective-permute-start.9 = (bf16[2,4,2,16,256]{4,3,2,1,0:T(8,128)(2,1)S(1)}, bf16[2,4,2,16,256]{4,3,2,1,0:T(8,128)(2,1)S(1)}, u32[]{:S(2)}, u32[]{:S(2)}) collective-permute-start(bf16[2,4,2,16,256]{4,3,2,1,0:T(8,128)(2,1)S(1)} %condition.1.refs_0_), channel_id=1, source_target_pairs={{2,0},{3,1},{0,2},{1,3},{6,4},{7,5},{4,6},{5,7},{10,8},{11,9},{8,1... | collective-permute-start | bytes 393224 | tf_op jit(solution)/shard_map/ppermute | solution.py:21
  21.9 3.0 %collective-permute-done.10.refs_2_ = bf16[2,4,2,16,256]{4,3,2,1,0:T(8,128)(2,1)S(1)} collective-permute-done((bf16[2,4,2,16,256]{4,3,2,1,0:T(8,128)(2,1)S(1)}, bf16[2,4,2,16,256]{4,3,2,1,0:T(8,128)(2,1)S(1)}, u32[]{:S(2)}, u32[]{:S(2)}) %collective-permute-start.10) | collective-permute-done | bytes 131104 | tf_op jit(solution)/shard_map/ppermute | solution.py:21
  24.9 1.3 %collective-permute-start.11 = (bf16[2,4,2,16,256]{4,3,2,1,0:T(8,128)(2,1)S(1)}, bf16[2,4,2,16,256]{4,3,2,1,0:T(8,128)(2,1)S(1)}, u32[]{:S(2)}, u32[]{:S(2)}) collective-permute-start(bf16[2,4,2,16,256]{4,3,2,1,0:T(8,128)(2,1)S(1)} %collective-permute-done.10.refs_2_), channel_id=1, source_target_pairs={{2,0},{3,1},{0,2},{1,3},{6,4},{7,5},{4,6},{5,7},{10,8},{11,9},{8,1... | collective-permute-start | bytes 393224 | tf_op jit(solution)/shard_map/ppermute | solution.py:21
  26.2 0.9 %collective-permute-done.8.refs_1_ = bf16[2,4,2,16,256]{4,3,2,1,0:T(8,128)(2,1)S(1)} collective-permute-done((bf16[2,4,2,16,256]{4,3,2,1,0:T(8,128)(2,1)S(1)}, bf16[2,4,2,16,256]{4,3,2,1,0:T(8,128)(2,1)S(1)}, u32[]{:S(2)}, u32[]{:S(2)}) %collective-permute-start.8) | collective-permute-done | bytes 131104 | tf_op jit(solution)/shard_map/ppermute | solution.py:21
  27.0 1.5 %collective-permute-start.13 = (bf16[2,4,2,16,256]{4,3,2,1,0:T(8,128)(2,1)S(1)}, bf16[2,4,2,16,256]{4,3,2,1,0:T(8,128)(2,1)S(1)}, u32[]{:S(2)}, u32[]{:S(2)}) collective-permute-start(bf16[2,4,2,16,256]{4,3,2,1,0:T(8,128)(2,1)S(1)} %collective-permute-done.8.refs_1_), channel_id=1, source_target_pairs={{4,0},{5,1},{6,2},{7,3},{0,4},{1,5},{2,6},{3,7},{12,8},{13,9},{14,... | collective-permute-start | bytes 393224 | tf_op jit(solution)/shard_map/ppermute | solution.py:21
  28.5 1.6 %collective-permute-start.14 = (bf16[2,4,2,16,256]{4,3,2,1,0:T(8,128)(2,1)S(1)}, bf16[2,4,2,16,256]{4,3,2,1,0:T(8,128)(2,1)S(1)}, u32[]{:S(2)}, u32[]{:S(2)}) collective-permute-start(bf16[2,4,2,16,256]{4,3,2,1,0:T(8,128)(2,1)S(1)} %collective-permute-done.8.refs_1_), channel_id=1, source_target_pairs={{2,0},{3,1},{0,2},{1,3},{6,4},{7,5},{4,6},{5,7},{10,8},{11,9},{8,1... | collective-permute-start | bytes 393224 | tf_op jit(solution)/shard_map/ppermute | solution.py:21
  30.2 0.4 collective-permute-start.15
  30.5 0.4 %collective-permute-done.11.refs_3_ = bf16[2,4,2,16,256]{4,3,2,1,0:T(8,128)(2,1)S(1)} collective-permute-done((bf16[2,4,2,16,256]{4,3,2,1,0:T(8,128)(2,1)S(1)}, bf16[2,4,2,16,256]{4,3,2,1,0:T(8,128)(2,1)S(1)}, u32[]{:S(2)}, u32[]{:S(2)}) %collective-permute-start.11) | collective-permute-done | bytes 131104 | tf_op jit(solution)/shard_map/ppermute | solution.py:21
  30.9 0.2 turn.1.refs_1_
  31.2 0.1 collective-permute-start.16
  31.3 1.3 %score.4.refs_2_ = f32[2048,512]{1,0:T(8,128)S(1)} custom-call(bf16[2048,2048]{1,0:T(8,128)(2,1)S(1)} %stage.3.refs_0_, bf16[512,512]{1,0:T(8,128)(2,1)S(1)} %turn.1.refs_1_), custom_call_target="tpu_custom_call" | custom-call | flops 21474836480 | bytes 4194304 | tf_op jit(solution)/shard_map/score/pallas_call | solution.py:189
  32.5 0.6 %collective-permute-start.12 = (bf16[2,4,2,16,256]{4,3,2,1,0:T(8,128)(2,1)S(1)}, bf16[2,4,2,16,256]{4,3,2,1,0:T(8,128)(2,1)S(1)}, u32[]{:S(2)}, u32[]{:S(2)}) collective-permute-start(bf16[2,4,2,16,256]{4,3,2,1,0:T(8,128)(2,1)S(1)} %collective-permute-done.8.refs_1_), channel_id=1, source_target_pairs={{1,0},{0,1},{3,2},{2,3},{5,4},{4,5},{7,6},{6,7},{9,8},{8,9},{11,10... | collective-permute-start | bytes 393224 | tf_op jit(solution)/shard_map/ppermute | solution.py:21
  33.1 0.1 collective-permute-done.16.refs_1_
  33.2 1.4 %score.5.refs_5_ = f32[2048,512]{1,0:T(8,128)S(1)} custom-call(bf16[2048,2048]{1,0:T(8,128)(2,1)S(1)} %stage.3.refs_0_, bf16[512,512]{1,0:T(8,128)(2,1)S(1)} %collective-permute-done.16.refs_1_, f32[2048,512]{1,0:T(8,128)S(1)} %score.4.refs_2_), custom_call_target="tpu_custom_call", output_to_operand_aliasing={{}: (2, {})} | custom-call | flops 1073741824 | bytes 4194304 | tf_op jit(solution)/shard_map/score/pallas_call | solution.py:189
  34.6 1.4 %collective-permute-done.15.refs_4_ = bf16[2,4,2,16,256]{4,3,2,1,0:T(8,128)(2,1)S(1)} collective-permute-done((bf16[2,4,2,16,256]{4,3,2,1,0:T(8,128)(2,1)S(1)}, bf16[2,4,2,16,256]{4,3,2,1,0:T(8,128)(2,1)S(1)}, u32[]{:S(2)}, u32[]{:S(2)}) %collective-permute-start.15) | collective-permute-done | bytes 131104 | tf_op jit(solution)/shard_map/ppermute | solution.py:21
  36.0 0.5 %collective-permute-start.18 = (bf16[2,4,2,16,256]{4,3,2,1,0:T(8,128)(2,1)S(1)}, bf16[2,4,2,16,256]{4,3,2,1,0:T(8,128)(2,1)S(1)}, u32[]{:S(2)}, u32[]{:S(2)}) collective-permute-start(bf16[2,4,2,16,256]{4,3,2,1,0:T(8,128)(2,1)S(1)} %collective-permute-done.13.refs_3_), channel_id=1, source_target_pairs={{1,0},{0,1},{3,2},{2,3},{5,4},{4,5},{7,6},{6,7},{9,8},{8,9},{11,10... | collective-permute-start | bytes 393224 | tf_op jit(solution)/shard_map/ppermute | solution.py:21
  36.5 0.0 collective-permute-start.19
  36.6 1.5 %score.6.refs_5_ = f32[2048,512]{1,0:T(8,128)S(1)} custom-call(bf16[2048,2048]{1,0:T(8,128)(2,1)S(1)} %stage.3.refs_0_, bf16[2,4,2,16,256]{4,3,2,1,0:T(8,128)(2,1)S(1)} %collective-permute-done.8.refs_1_, bf16[2,4,2,16,256]{4,3,2,1,0:T(8,128)(2,1)S(1)} %collective-permute-done.14.refs_2_, ...), custom_call_target="tpu_custom_call", output_to_operand_aliasing={{}: (5, {})} | custom-call | flops 1073741824 | bytes 4194304 | tf_op jit(solution)/shard_map/score/pallas_call | solution.py:189
  38.1 2.9 %score.7 = f32[2048,512]{1,0:T(8,128)} custom-call(bf16[2048,2048]{1,0:T(8,128)(2,1)S(1)} %stage.3.refs_0_, bf16[2,4,2,16,256]{4,3,2,1,0:T(8,128)(2,1)S(1)} %collective-permute-done.12.refs_1_, bf16[2,4,2,16,256]{4,3,2,1,0:T(8,128)(2,1)S(1)} %collective-permute-done.17.refs_2_, bf16[2,4,2,16,256]{4,3,2,1,0:T(8,128)(2,1)S(1)} %collective-permute-done.18.refs_3_, ...), custom_call_target="tpu_custom_call" | custom-call | flops 1073741824 | bytes 4194304 | tf_op jit(solution)/shard_map/score/pallas_call | solution.py:189
  (16 shorter events, 0.0 us)
Async XLA Ops:
  0.0 9.0 %collective-permute-start = (bf16[2,16,2048]{2,1,0:T(8,128)(2,1)}, bf16[2,16,2048]{2,1,0:T(8,128)(2,1)S(1)}, u32[]{:S(2)}, u32[]{:S(2)}) collective-permute-start(bf16[2,16,2048]{2,1,0:T(8,128)(2,1)} %refs_1_.2), channel_id=1, source_target_pairs={{12,0},{13,1},{14,2},{15,3},{8,4},{9,5},{10,6},{11,7},{4,8},{5,9},... | collective-permute-start | bytes 393224 | tf_op jit(solution)/shard_map/ppermute | solution.py:21
  5.0 13.6 %collective-permute-start.7 = (bf16[1,2048,128]{2,1,0:T(8,128)(2,1)}, bf16[1,2048,128]{2,1,0:T(8,128)(2,1)S(1)}, u32[]{:S(2)}, u32[]{:S(2)}) collective-permute-start(bf16[1,2048,128]{2,1,0:T(8,128)(2,1)} %refs_2_.1), channel_id=1, source_target_pairs={{2,0},{3,1},{0,2},{1,3},{6,4},{7,5},{4,6},{5,7},{10,8},{11,9},{8,1... | collective-permute-start | bytes 1572872 | tf_op jit(solution)/shard_map/ppermute | solution.py:21
  6.6 2.4 %collective-permute-start.1 = (bf16[2,16,2048]{2,1,0:T(8,128)(2,1)}, bf16[2,16,2048]{2,1,0:T(8,128)(2,1)S(1)}, u32[]{:S(2)}, u32[]{:S(2)}) collective-permute-start(bf16[2,16,2048]{2,1,0:T(8,128)(2,1)} %refs_1_.2), channel_id=1, source_target_pairs={{1,0},{0,1},{3,2},{2,3},{5,4},{4,5},{7,6},{6,7},{9,8},{8,9},{11,10... | collective-permute-start | bytes 393224 | tf_op jit(solution)/shard_map/ppermute | solution.py:21
  6.6 6.9 %collective-permute-start.3 = (bf16[2,16,2048]{2,1,0:T(8,128)(2,1)}, bf16[2,16,2048]{2,1,0:T(8,128)(2,1)S(1)}, u32[]{:S(2)}, u32[]{:S(2)}) collective-permute-start(bf16[2,16,2048]{2,1,0:T(8,128)(2,1)} %refs_1_.2), channel_id=1, source_target_pairs={{4,0},{5,1},{6,2},{7,3},{0,4},{1,5},{2,6},{3,7},{12,8},{13,9},{14,... | collective-permute-start | bytes 393224 | tf_op jit(solution)/shard_map/ppermute | solution.py:21
  9.0 6.5 %collective-permute-start.2 = (bf16[2,16,2048]{2,1,0:T(8,128)(2,1)S(1)}, bf16[2,16,2048]{2,1,0:T(8,128)(2,1)S(1)}, u32[]{:S(2)}, u32[]{:S(2)}) collective-permute-start(bf16[2,16,2048]{2,1,0:T(8,128)(2,1)S(1)} %collective-permute-done.refs_3_), channel_id=1, source_target_pairs={{4,0},{5,1},{6,2},{7,3},{0,4},{1,5},{2,6},{3,7},{12,8},{13,9},{14,... | collective-permute-start | bytes 393224 | tf_op jit(solution)/shard_map/ppermute | solution.py:21
  11.3 4.2 %collective-permute-start.5 = (bf16[2,16,2048]{2,1,0:T(8,128)(2,1)S(1)}, bf16[2,16,2048]{2,1,0:T(8,128)(2,1)S(1)}, u32[]{:S(2)}, u32[]{:S(2)}) collective-permute-start(bf16[2,16,2048]{2,1,0:T(8,128)(2,1)S(1)} %collective-permute-done.refs_3_), channel_id=1, source_target_pairs={{1,0},{0,1},{3,2},{2,3},{5,4},{4,5},{7,6},{6,7},{9,8},{8,9},{11,10... | collective-permute-start | bytes 393224 | tf_op jit(solution)/shard_map/ppermute | solution.py:21
  13.5 2.0 %collective-permute-start.4 = (bf16[2,16,2048]{2,1,0:T(8,128)(2,1)S(1)}, bf16[2,16,2048]{2,1,0:T(8,128)(2,1)S(1)}, u32[]{:S(2)}, u32[]{:S(2)}) collective-permute-start(bf16[2,16,2048]{2,1,0:T(8,128)(2,1)S(1)} %collective-permute-done.3.refs_2_), channel_id=1, source_target_pairs={{1,0},{0,1},{3,2},{2,3},{5,4},{4,5},{7,6},{6,7},{9,8},{8,9},{11,10... | collective-permute-start | bytes 393224 | tf_op jit(solution)/shard_map/ppermute | solution.py:21
  15.5 1.3 %collective-permute-start.6 = (bf16[2,16,2048]{2,1,0:T(8,128)(2,1)S(1)}, bf16[2,16,2048]{2,1,0:T(8,128)(2,1)S(1)}, u32[]{:S(2)}, u32[]{:S(2)}) collective-permute-start(bf16[2,16,2048]{2,1,0:T(8,128)(2,1)S(1)} %collective-permute-done.2.refs_4_), channel_id=1, source_target_pairs={{1,0},{0,1},{3,2},{2,3},{5,4},{4,5},{7,6},{6,7},{9,8},{8,9},{11,10... | collective-permute-start | bytes 393224 | tf_op jit(solution)/shard_map/ppermute | solution.py:21
  19.1 5.8 %collective-permute-start.10 = (bf16[2,4,2,16,256]{4,3,2,1,0:T(8,128)(2,1)S(1)}, bf16[2,4,2,16,256]{4,3,2,1,0:T(8,128)(2,1)S(1)}, u32[]{:S(2)}, u32[]{:S(2)}) collective-permute-start(bf16[2,4,2,16,256]{4,3,2,1,0:T(8,128)(2,1)S(1)} %condition.1.refs_0_), channel_id=1, source_target_pairs={{4,0},{5,1},{6,2},{7,3},{0,4},{1,5},{2,6},{3,7},{12,8},{13,9},{14,... | collective-permute-start | bytes 393224 | tf_op jit(solution)/shard_map/ppermute | solution.py:21
  19.2 7.9 %collective-permute-start.8 = (bf16[2,4,2,16,256]{4,3,2,1,0:T(8,128)(2,1)S(1)}, bf16[2,4,2,16,256]{4,3,2,1,0:T(8,128)(2,1)S(1)}, u32[]{:S(2)}, u32[]{:S(2)}) collective-permute-start(bf16[2,4,2,16,256]{4,3,2,1,0:T(8,128)(2,1)S(1)} %condition.1.refs_0_), channel_id=1, source_target_pairs={{12,0},{13,1},{14,2},{15,3},{8,4},{9,5},{10,6},{11,7},{4,8},{5,9},... | collective-permute-start | bytes 393224 | tf_op jit(solution)/shard_map/ppermute | solution.py:21
  20.6 9.9 %collective-permute-start.9 = (bf16[2,4,2,16,256]{4,3,2,1,0:T(8,128)(2,1)S(1)}, bf16[2,4,2,16,256]{4,3,2,1,0:T(8,128)(2,1)S(1)}, u32[]{:S(2)}, u32[]{:S(2)}) collective-permute-start(bf16[2,4,2,16,256]{4,3,2,1,0:T(8,128)(2,1)S(1)} %condition.1.refs_0_), channel_id=1, source_target_pairs={{2,0},{3,1},{0,2},{1,3},{6,4},{7,5},{4,6},{5,7},{10,8},{11,9},{8,1... | collective-permute-start | bytes 393224 | tf_op jit(solution)/shard_map/ppermute | solution.py:21
  24.9 6.0 %collective-permute-start.11 = (bf16[2,4,2,16,256]{4,3,2,1,0:T(8,128)(2,1)S(1)}, bf16[2,4,2,16,256]{4,3,2,1,0:T(8,128)(2,1)S(1)}, u32[]{:S(2)}, u32[]{:S(2)}) collective-permute-start(bf16[2,4,2,16,256]{4,3,2,1,0:T(8,128)(2,1)S(1)} %collective-permute-done.10.refs_2_), channel_id=1, source_target_pairs={{2,0},{3,1},{0,2},{1,3},{6,4},{7,5},{4,6},{5,7},{10,8},{11,9},{8,1... | collective-permute-start | bytes 393224 | tf_op jit(solution)/shard_map/ppermute | solution.py:21
  27.0 7.5 %collective-permute-start.13 = (bf16[2,4,2,16,256]{4,3,2,1,0:T(8,128)(2,1)S(1)}, bf16[2,4,2,16,256]{4,3,2,1,0:T(8,128)(2,1)S(1)}, u32[]{:S(2)}, u32[]{:S(2)}) collective-permute-start(bf16[2,4,2,16,256]{4,3,2,1,0:T(8,128)(2,1)S(1)} %collective-permute-done.8.refs_1_), channel_id=1, source_target_pairs={{4,0},{5,1},{6,2},{7,3},{0,4},{1,5},{2,6},{3,7},{12,8},{13,9},{14,... | collective-permute-start | bytes 393224 | tf_op jit(solution)/shard_map/ppermute | solution.py:21
  28.5 6.1 %collective-permute-start.14 = (bf16[2,4,2,16,256]{4,3,2,1,0:T(8,128)(2,1)S(1)}, bf16[2,4,2,16,256]{4,3,2,1,0:T(8,128)(2,1)S(1)}, u32[]{:S(2)}, u32[]{:S(2)}) collective-permute-start(bf16[2,4,2,16,256]{4,3,2,1,0:T(8,128)(2,1)S(1)} %collective-permute-done.8.refs_1_), channel_id=1, source_target_pairs={{2,0},{3,1},{0,2},{1,3},{6,4},{7,5},{4,6},{5,7},{10,8},{11,9},{8,1... | collective-permute-start | bytes 393224 | tf_op jit(solution)/shard_map/ppermute | solution.py:21
  30.2 5.9 %collective-permute-start.15 = (bf16[2,4,2,16,256]{4,3,2,1,0:T(8,128)(2,1)S(1)}, bf16[2,4,2,16,256]{4,3,2,1,0:T(8,128)(2,1)S(1)}, u32[]{:S(2)}, u32[]{:S(2)}) collective-permute-start(bf16[2,4,2,16,256]{4,3,2,1,0:T(8,128)(2,1)S(1)} %collective-permute-done.8.refs_1_), channel_id=1, source_target_pairs={{6,0},{7,1},{4,2},{5,3},{2,4},{3,5},{0,6},{1,7},{14,8},{15,9},{12,... | collective-permute-start | bytes 393224 | tf_op jit(solution)/shard_map/ppermute | solution.py:21
  31.2 2.0 %collective-permute-start.16 = (bf16[512,512]{1,0:T(8,128)(2,1)S(1)}, bf16[512,512]{1,0:T(8,128)(2,1)S(1)}, u32[]{:S(2)}, u32[]{:S(2)}) collective-permute-start(bf16[512,512]{1,0:T(8,128)(2,1)S(1)} %turn.1.refs_1_), channel_id=1, source_target_pairs={{1,0},{0,1},{3,2},{2,3},{5,4},{4,5},{7,6},{6,7},{9,8},{8,9},{11,10... | collective-permute-start | bytes 1572872 | tf_op jit(solution)/shard_map/ppermute | solution.py:21
  32.5 5.5 %collective-permute-start.12 = (bf16[2,4,2,16,256]{4,3,2,1,0:T(8,128)(2,1)S(1)}, bf16[2,4,2,16,256]{4,3,2,1,0:T(8,128)(2,1)S(1)}, u32[]{:S(2)}, u32[]{:S(2)}) collective-permute-start(bf16[2,4,2,16,256]{4,3,2,1,0:T(8,128)(2,1)S(1)} %collective-permute-done.8.refs_1_), channel_id=1, source_target_pairs={{1,0},{0,1},{3,2},{2,3},{5,4},{4,5},{7,6},{6,7},{9,8},{8,9},{11,10... | collective-permute-start | bytes 393224 | tf_op jit(solution)/shard_map/ppermute | solution.py:21
  36.0 2.0 %collective-permute-start.17 = (bf16[2,4,2,16,256]{4,3,2,1,0:T(8,128)(2,1)S(1)}, bf16[2,4,2,16,256]{4,3,2,1,0:T(8,128)(2,1)S(1)}, u32[]{:S(2)}, u32[]{:S(2)}) collective-permute-start(bf16[2,4,2,16,256]{4,3,2,1,0:T(8,128)(2,1)S(1)} %collective-permute-done.14.refs_2_), channel_id=1, source_target_pairs={{1,0},{0,1},{3,2},{2,3},{5,4},{4,5},{7,6},{6,7},{9,8},{8,9},{11,10... | collective-permute-start | bytes 393224 | tf_op jit(solution)/shard_map/ppermute | solution.py:21
  36.0 2.0 %collective-permute-start.18 = (bf16[2,4,2,16,256]{4,3,2,1,0:T(8,128)(2,1)S(1)}, bf16[2,4,2,16,256]{4,3,2,1,0:T(8,128)(2,1)S(1)}, u32[]{:S(2)}, u32[]{:S(2)}) collective-permute-start(bf16[2,4,2,16,256]{4,3,2,1,0:T(8,128)(2,1)S(1)} %collective-permute-done.13.refs_3_), channel_id=1, source_target_pairs={{1,0},{0,1},{3,2},{2,3},{5,4},{4,5},{7,6},{6,7},{9,8},{8,9},{11,10... | collective-permute-start | bytes 393224 | tf_op jit(solution)/shard_map/ppermute | solution.py:21
  36.5 1.5 %collective-permute-start.19 = (bf16[2,4,2,16,256]{4,3,2,1,0:T(8,128)(2,1)S(1)}, bf16[2,4,2,16,256]{4,3,2,1,0:T(8,128)(2,1)S(1)}, u32[]{:S(2)}, u32[]{:S(2)}) collective-permute-start(bf16[2,4,2,16,256]{4,3,2,1,0:T(8,128)(2,1)S(1)} %collective-permute-done.15.refs_4_), channel_id=1, source_target_pairs={{1,0},{0,1},{3,2},{2,3},{5,4},{4,5},{7,6},{6,7},{9,8},{8,9},{11,10... | collective-permute-start | bytes 393224 | tf_op jit(solution)/shard_map/ppermute | solution.py:21

commit v21 on v17

--- a/solution.py
+++ b/solution.py
@@ -236,6 +236,7 @@
     swap(own, *far_three)
     swap(own, *near_one)
     swap(own, *far_one)
+    meet(far_three, far_one)
     swap(far_one, *near_one)
     swap(far_three, *near_one)
     swap(far_three, beside, 1, 0)

time: 41.2 us -> 44.2 us (1.073)
  waiting for transfers between devices: 10.4 us -> 13.1 us
    ppermute x20, waiting for transfers between devices: 10.4 us -> 13.1 us  [swap(): lax.ppermute(block, 'rows', [(row ^ step, row) for row in range(self.far...]
  transfers between devices with their start and end apart: 20 -> 20, of which waited for: 8 -> 7; matrix products, arithmetic and copies ran while one was open for 0% -> 0% of each run, Pallas kernels for 22% -> 20%
where the time goes in v21:
time: 44.2 us; the launch traced here: 44.1 us
  starting transfers between devices  18.5 us (42%)
  waiting for transfers between devices  13.1 us (30%)
  Pallas kernels  12.3 us (28%)
    ppermute x20, starting transfers between devices, swap(): lax.ppermute(block, 'rows', [(row ^ step, row) for row in range(self.far...  18.5 us
    ppermute x20, waiting for transfers between devices, swap(): lax.ppermute(block, 'rows', [(row ^ step, row) for row in range(self.far...  13.1 us
    pallas_call x4, Pallas kernels, score(): pl.pallas_call(functools.partial(score_kernel, grid, masks, other, len(pa...  7.07 us
    pallas_call x2, Pallas kernels, stage(): pl.pallas_call(functools.partial(stage_kernel, first, arrays[0].shape[0]...  4.56 us
  transfers between devices with their start and end apart: 20, of which 7 were waited for; matrix products, arithmetic and copies ran while one was open for 0% of the time, Pallas kernels for 20%

profile of v21, /device:TPU:0, one launch (start us, length us, event | category | flops | bytes accessed | tf_op | source)
XLA Modules:
  0.0 44.1 jit_solution(3159352589269138426)
XLA Ops:
  0.0 5.0 %collective-permute-start = (bf16[2,16,2048]{2,1,0:T(8,128)(2,1)}, bf16[2,16,2048]{2,1,0:T(8,128)(2,1)S(1)}, u32[]{:S(2)}, u32[]{:S(2)}) collective-permute-start(bf16[2,16,2048]{2,1,0:T(8,128)(2,1)} %refs_1_.2), channel_id=1, source_target_pairs={{12,0},{13,1},{14,2},{15,3},{8,4},{9,5},{10,6},{11,7},{4,8},{5,9},... | collective-permute-start | bytes 393224 | tf_op jit(solution)/shard_map/ppermute | solution.py:21
  5.0 1.5 %collective-permute-start.7 = (bf16[1,2048,128]{2,1,0:T(8,128)(2,1)}, bf16[1,2048,128]{2,1,0:T(8,128)(2,1)S(1)}, u32[]{:S(2)}, u32[]{:S(2)}) collective-permute-start(bf16[1,2048,128]{2,1,0:T(8,128)(2,1)} %refs_2_.1), channel_id=1, source_target_pairs={{2,0},{3,1},{0,2},{1,3},{6,4},{7,5},{4,6},{5,7},{10,8},{11,9},{8,1... | collective-permute-start | bytes 1572872 | tf_op jit(solution)/shard_map/ppermute | solution.py:21
  6.6 0.0 collective-permute-start.1
  6.6 2.4 %stage.2 = (bf16[2048,2048]{1,0:T(8,128)(2,1)S(1)}, bf16[2,16,2048]{2,1,0:T(8,128)(2,1)S(1)}, bf16[1,2048,128]{2,1,0:T(8,128)(2,1)S(1)}) custom-call(bf16[2048,2048]{1,0:T(8,128)(2,1)} %refs_1_.3, bf16[2,16,2048]{2,1,0:T(8,128)(2,1)} %refs_1_.2, bf16[1,2048,128]{2,1,0:T(8,128)(2,1)} %refs_2_.1), custom_call_target="tpu_custom_call" | custom-call | flops 2788300032 | bytes 9043968 | tf_op jit(solution)/shard_map/stage/pallas_call | solution.py:56
  9.0 2.3 %collective-permute-start.2 = (bf16[2,16,2048]{2,1,0:T(8,128)(2,1)S(1)}, bf16[2,16,2048]{2,1,0:T(8,128)(2,1)S(1)}, u32[]{:S(2)}, u32[]{:S(2)}) collective-permute-start(bf16[2,16,2048]{2,1,0:T(8,128)(2,1)S(1)} %collective-permute-done.refs_3_), channel_id=1, source_target_pairs={{4,0},{5,1},{6,2},{7,3},{0,4},{1,5},{2,6},{3,7},{12,8},{13,9},{14,... | collective-permute-start | bytes 393224 | tf_op jit(solution)/shard_map/ppermute | solution.py:21
  11.3 2.2 %stage.3.refs_0_ = bf16[2048,2048]{1,0:T(8,128)(2,1)S(1)} custom-call(bf16[2048,2048]{1,0:T(8,128)(2,1)S(1)} %get-tuple-element.28.refs_0_, bf16[2048,2048]{1,0:T(8,128)(2,1)} %refs_1_.3), custom_call_target="tpu_custom_call", output_to_operand_aliasing={{}: (0, {})} | custom-call | flops 1 | bytes 8388608 | tf_op jit(solution)/shard_map/stage/pallas_call | solution.py:56
  13.5 0.6 %collective-permute-start.4 = (bf16[2,16,2048]{2,1,0:T(8,128)(2,1)S(1)}, bf16[2,16,2048]{2,1,0:T(8,128)(2,1)S(1)}, u32[]{:S(2)}, u32[]{:S(2)}) collective-permute-start(bf16[2,16,2048]{2,1,0:T(8,128)(2,1)S(1)} %collective-permute-done.3.refs_2_), channel_id=1, source_target_pairs={{1,0},{0,1},{3,2},{2,3},{5,4},{4,5},{7,6},{6,7},{9,8},{8,9},{11,10... | collective-permute-start | bytes 393224 | tf_op jit(solution)/shard_map/ppermute | solution.py:21
  14.1 1.4 %collective-permute-done.2.refs_4_ = bf16[2,16,2048]{2,1,0:T(8,128)(2,1)S(1)} collective-permute-done((bf16[2,16,2048]{2,1,0:T(8,128)(2,1)S(1)}, bf16[2,16,2048]{2,1,0:T(8,128)(2,1)S(1)}, u32[]{:S(2)}, u32[]{:S(2)}) %collective-permute-start.2) | collective-permute-done | bytes 131104 | tf_op jit(solution)/shard_map/ppermute | solution.py:21
  15.5 1.3 %collective-permute-done.6.refs_7_ = bf16[2,16,2048]{2,1,0:T(8,128)(2,1)S(1)} collective-permute-done((bf16[2,16,2048]{2,1,0:T(8,128)(2,1)S(1)}, bf16[2,16,2048]{2,1,0:T(8,128)(2,1)S(1)}, u32[]{:S(2)}, u32[]{:S(2)}) %collective-permute-start.6) | collective-permute-done | bytes 131104 | tf_op jit(solution)/shard_map/ppermute | solution.py:21
  16.9 1.8 %collective-permute-done.7.refs_9_ = bf16[1,2048,128]{2,1,0:T(8,128)(2,1)S(1)} collective-permute-done((bf16[1,2048,128]{2,1,0:T(8,128)(2,1)}, bf16[1,2048,128]{2,1,0:T(8,128)(2,1)S(1)}, u32[]{:S(2)}, u32[]{:S(2)}) %collective-permute-start.7) | collective-permute-done | bytes 524320 | tf_op jit(solution)/shard_map/ppermute | solution.py:21
  18.6 0.4 condition.1.refs_0_
  19.1 0.8 %collective-permute-start.8 = (bf16[2,4,2,16,256]{4,3,2,1,0:T(8,128)(2,1)S(1)}, bf16[2,4,2,16,256]{4,3,2,1,0:T(8,128)(2,1)S(1)}, u32[]{:S(2)}, u32[]{:S(2)}) collective-permute-start(bf16[2,4,2,16,256]{4,3,2,1,0:T(8,128)(2,1)S(1)} %condition.1.refs_0_), channel_id=1, source_target_pairs={{12,0},{13,1},{14,2},{15,3},{8,4},{9,5},{10,6},{11,7},{4,8},{5,9},... | collective-permute-start | bytes 393224 | tf_op jit(solution)/shard_map/ppermute | solution.py:21
  19.9 1.9 %collective-permute-start.10 = (bf16[2,4,2,16,256]{4,3,2,1,0:T(8,128)(2,1)S(1)}, bf16[2,4,2,16,256]{4,3,2,1,0:T(8,128)(2,1)S(1)}, u32[]{:S(2)}, u32[]{:S(2)}) collective-permute-start(bf16[2,4,2,16,256]{4,3,2,1,0:T(8,128)(2,1)S(1)} %condition.1.refs_0_), channel_id=1, source_target_pairs={{2,0},{3,1},{0,2},{1,3},{6,4},{7,5},{4,6},{5,7},{10,8},{11,9},{8,1... | collective-permute-start | bytes 393224 | tf_op jit(solution)/shard_map/ppermute | solution.py:21
  21.8 4.7 %collective-permute-done.8.refs_1_ = bf16[2,4,2,16,256]{4,3,2,1,0:T(8,128)(2,1)S(1)} collective-permute-done((bf16[2,4,2,16,256]{4,3,2,1,0:T(8,128)(2,1)S(1)}, bf16[2,4,2,16,256]{4,3,2,1,0:T(8,128)(2,1)S(1)}, u32[]{:S(2)}, u32[]{:S(2)}) %collective-permute-start.8) | collective-permute-done | bytes 131104 | tf_op jit(solution)/shard_map/ppermute | solution.py:21
  26.6 1.4 %collective-permute-done.9.refs_2_ = bf16[2,4,2,16,256]{4,3,2,1,0:T(8,128)(2,1)S(1)} collective-permute-done((bf16[2,4,2,16,256]{4,3,2,1,0:T(8,128)(2,1)S(1)}, bf16[2,4,2,16,256]{4,3,2,1,0:T(8,128)(2,1)S(1)}, u32[]{:S(2)}, u32[]{:S(2)}) %collective-permute-start.9) | collective-permute-done | bytes 131104 | tf_op jit(solution)/shard_map/ppermute | solution.py:21
  27.9 1.5 %collective-permute-start.11 = (bf16[2,4,2,16,256]{4,3,2,1,0:T(8,128)(2,1)S(1)}, bf16[2,4,2,16,256]{4,3,2,1,0:T(8,128)(2,1)S(1)}, u32[]{:S(2)}, u32[]{:S(2)}) collective-permute-start(bf16[2,4,2,16,256]{4,3,2,1,0:T(8,128)(2,1)S(1)} %collective-permute-done.9.refs_2_), channel_id=1, source_target_pairs={{2,0},{3,1},{0,2},{1,3},{6,4},{7,5},{4,6},{5,7},{10,8},{11,9},{8,1... | collective-permute-start | bytes 393224 | tf_op jit(solution)/shard_map/ppermute | solution.py:21
  29.4 0.8 %collective-permute-start.13 = (bf16[2,4,2,16,256]{4,3,2,1,0:T(8,128)(2,1)S(1)}, bf16[2,4,2,16,256]{4,3,2,1,0:T(8,128)(2,1)S(1)}, u32[]{:S(2)}, u32[]{:S(2)}) collective-permute-start(bf16[2,4,2,16,256]{4,3,2,1,0:T(8,128)(2,1)S(1)} %collective-permute-done.8.refs_1_), channel_id=1, source_target_pairs={{4,0},{5,1},{6,2},{7,3},{0,4},{1,5},{2,6},{3,7},{12,8},{13,9},{14,... | collective-permute-start | bytes 393224 | tf_op jit(solution)/shard_map/ppermute | solution.py:21
  30.2 0.1 collective-permute-start.14
  30.3 2.6 %collective-permute-start.15 = (bf16[2,4,2,16,256]{4,3,2,1,0:T(8,128)(2,1)S(1)}, bf16[2,4,2,16,256]{4,3,2,1,0:T(8,128)(2,1)S(1)}, u32[]{:S(2)}, u32[]{:S(2)}) collective-permute-start(bf16[2,4,2,16,256]{4,3,2,1,0:T(8,128)(2,1)S(1)} %collective-permute-done.8.refs_1_), channel_id=1, source_target_pairs={{6,0},{7,1},{4,2},{5,3},{2,4},{3,5},{0,6},{1,7},{14,8},{15,9},{12,... | collective-permute-start | bytes 393224 | tf_op jit(solution)/shard_map/ppermute | solution.py:21
  32.9 2.4 %collective-permute-done.11.refs_3_ = bf16[2,4,2,16,256]{4,3,2,1,0:T(8,128)(2,1)S(1)} collective-permute-done((bf16[2,4,2,16,256]{4,3,2,1,0:T(8,128)(2,1)S(1)}, bf16[2,4,2,16,256]{4,3,2,1,0:T(8,128)(2,1)S(1)}, u32[]{:S(2)}, u32[]{:S(2)}) %collective-permute-start.11) | collective-permute-done | bytes 131104 | tf_op jit(solution)/shard_map/ppermute | solution.py:21
  35.3 0.2 turn.1.refs_1_
  35.5 0.1 collective-permute-start.16
  35.6 1.3 %score.4.refs_2_ = f32[2048,512]{1,0:T(8,128)S(1)} custom-call(bf16[2048,2048]{1,0:T(8,128)(2,1)S(1)} %stage.3.refs_0_, bf16[512,512]{1,0:T(8,128)(2,1)S(1)} %turn.1.refs_1_), custom_call_target="tpu_custom_call" | custom-call | flops 21474836480 | bytes 4194304 | tf_op jit(solution)/shard_map/score/pallas_call | solution.py:190
  36.9 0.6 %collective-permute-start.12 = (bf16[2,4,2,16,256]{4,3,2,1,0:T(8,128)(2,1)S(1)}, bf16[2,4,2,16,256]{4,3,2,1,0:T(8,128)(2,1)S(1)}, u32[]{:S(2)}, u32[]{:S(2)}) collective-permute-start(bf16[2,4,2,16,256]{4,3,2,1,0:T(8,128)(2,1)S(1)} %collective-permute-done.8.refs_1_), channel_id=1, source_target_pairs={{1,0},{0,1},{3,2},{2,3},{5,4},{4,5},{7,6},{6,7},{9,8},{8,9},{11,10... | collective-permute-start | bytes 393224 | tf_op jit(solution)/shard_map/ppermute | solution.py:21
  37.4 0.1 collective-permute-done.16.refs_1_
  37.5 1.4 %score.5.refs_5_ = f32[2048,512]{1,0:T(8,128)S(1)} custom-call(bf16[2048,2048]{1,0:T(8,128)(2,1)S(1)} %stage.3.refs_0_, bf16[512,512]{1,0:T(8,128)(2,1)S(1)} %collective-permute-done.16.refs_1_, f32[2048,512]{1,0:T(8,128)S(1)} %score.4.refs_2_), custom_call_target="tpu_custom_call", output_to_operand_aliasing={{}: (2, {})} | custom-call | flops 1073741824 | bytes 4194304 | tf_op jit(solution)/shard_map/score/pallas_call | solution.py:190
  38.9 0.0 collective-permute-done.14.refs_2_
  38.9 0.2 collective-permute-start.17
  39.1 0.4 collective-permute-start.18
  39.5 0.1 collective-permute-start.19
  39.7 1.5 %score.6.refs_5_ = f32[2048,512]{1,0:T(8,128)S(1)} custom-call(bf16[2048,2048]{1,0:T(8,128)(2,1)S(1)} %stage.3.refs_0_, bf16[2,4,2,16,256]{4,3,2,1,0:T(8,128)(2,1)S(1)} %collective-permute-done.8.refs_1_, bf16[2,4,2,16,256]{4,3,2,1,0:T(8,128)(2,1)S(1)} %collective-permute-done.14.refs_2_, ...), custom_call_target="tpu_custom_call", output_to_operand_aliasing={{}: (5, {})} | custom-call | flops 1073741824 | bytes 4194304 | tf_op jit(solution)/shard_map/score/pallas_call | solution.py:190
  41.2 2.9 %score.7 = f32[2048,512]{1,0:T(8,128)} custom-call(bf16[2048,2048]{1,0:T(8,128)(2,1)S(1)} %stage.3.refs_0_, bf16[2,4,2,16,256]{4,3,2,1,0:T(8,128)(2,1)S(1)} %collective-permute-done.12.refs_1_, bf16[2,4,2,16,256]{4,3,2,1,0:T(8,128)(2,1)S(1)} %collective-permute-done.17.refs_2_, bf16[2,4,2,16,256]{4,3,2,1,0:T(8,128)(2,1)S(1)} %collective-permute-done.18.refs_3_, ...), custom_call_target="tpu_custom_call" | custom-call | flops 1073741824 | bytes 4194304 | tf_op jit(solution)/shard_map/score/pallas_call | solution.py:190
  (16 shorter events, 0.0 us)
Async XLA Ops:
  0.0 9.0 %collective-permute-start = (bf16[2,16,2048]{2,1,0:T(8,128)(2,1)}, bf16[2,16,2048]{2,1,0:T(8,128)(2,1)S(1)}, u32[]{:S(2)}, u32[]{:S(2)}) collective-permute-start(bf16[2,16,2048]{2,1,0:T(8,128)(2,1)} %refs_1_.2), channel_id=1, source_target_pairs={{12,0},{13,1},{14,2},{15,3},{8,4},{9,5},{10,6},{11,7},{4,8},{5,9},... | collective-permute-start | bytes 393224 | tf_op jit(solution)/shard_map/ppermute | solution.py:21
  5.0 13.6 %collective-permute-start.7 = (bf16[1,2048,128]{2,1,0:T(8,128)(2,1)}, bf16[1,2048,128]{2,1,0:T(8,128)(2,1)S(1)}, u32[]{:S(2)}, u32[]{:S(2)}) collective-permute-start(bf16[1,2048,128]{2,1,0:T(8,128)(2,1)} %refs_2_.1), channel_id=1, source_target_pairs={{2,0},{3,1},{0,2},{1,3},{6,4},{7,5},{4,6},{5,7},{10,8},{11,9},{8,1... | collective-permute-start | bytes 1572872 | tf_op jit(solution)/shard_map/ppermute | solution.py:21
  6.6 2.4 %collective-permute-start.1 = (bf16[2,16,2048]{2,1,0:T(8,128)(2,1)}, bf16[2,16,2048]{2,1,0:T(8,128)(2,1)S(1)}, u32[]{:S(2)}, u32[]{:S(2)}) collective-permute-start(bf16[2,16,2048]{2,1,0:T(8,128)(2,1)} %refs_1_.2), channel_id=1, source_target_pairs={{1,0},{0,1},{3,2},{2,3},{5,4},{4,5},{7,6},{6,7},{9,8},{8,9},{11,10... | collective-permute-start | bytes 393224 | tf_op jit(solution)/shard_map/ppermute | solution.py:21
  6.6 6.9 %collective-permute-start.3 = (bf16[2,16,2048]{2,1,0:T(8,128)(2,1)}, bf16[2,16,2048]{2,1,0:T(8,128)(2,1)S(1)}, u32[]{:S(2)}, u32[]{:S(2)}) collective-permute-start(bf16[2,16,2048]{2,1,0:T(8,128)(2,1)} %refs_1_.2), channel_id=1, source_target_pairs={{4,0},{5,1},{6,2},{7,3},{0,4},{1,5},{2,6},{3,7},{12,8},{13,9},{14,... | collective-permute-start | bytes 393224 | tf_op jit(solution)/shard_map/ppermute | solution.py:21
  9.0 6.5 %collective-permute-start.2 = (bf16[2,16,2048]{2,1,0:T(8,128)(2,1)S(1)}, bf16[2,16,2048]{2,1,0:T(8,128)(2,1)S(1)}, u32[]{:S(2)}, u32[]{:S(2)}) collective-permute-start(bf16[2,16,2048]{2,1,0:T(8,128)(2,1)S(1)} %collective-permute-done.refs_3_), channel_id=1, source_target_pairs={{4,0},{5,1},{6,2},{7,3},{0,4},{1,5},{2,6},{3,7},{12,8},{13,9},{14,... | collective-permute-start | bytes 393224 | tf_op jit(solution)/shard_map/ppermute | solution.py:21
  11.3 4.2 %collective-permute-start.5 = (bf16[2,16,2048]{2,1,0:T(8,128)(2,1)S(1)}, bf16[2,16,2048]{2,1,0:T(8,128)(2,1)S(1)}, u32[]{:S(2)}, u32[]{:S(2)}) collective-permute-start(bf16[2,16,2048]{2,1,0:T(8,128)(2,1)S(1)} %collective-permute-done.refs_3_), channel_id=1, source_target_pairs={{1,0},{0,1},{3,2},{2,3},{5,4},{4,5},{7,6},{6,7},{9,8},{8,9},{11,10... | collective-permute-start | bytes 393224 | tf_op jit(solution)/shard_map/ppermute | solution.py:21
  13.5 2.0 %collective-permute-start.4 = (bf16[2,16,2048]{2,1,0:T(8,128)(2,1)S(1)}, bf16[2,16,2048]{2,1,0:T(8,128)(2,1)S(1)}, u32[]{:S(2)}, u32[]{:S(2)}) collective-permute-start(bf16[2,16,2048]{2,1,0:T(8,128)(2,1)S(1)} %collective-permute-done.3.refs_2_), channel_id=1, source_target_pairs={{1,0},{0,1},{3,2},{2,3},{5,4},{4,5},{7,6},{6,7},{9,8},{8,9},{11,10... | collective-permute-start | bytes 393224 | tf_op jit(solution)/shard_map/ppermute | solution.py:21
  15.5 1.3 %collective-permute-start.6 = (bf16[2,16,2048]{2,1,0:T(8,128)(2,1)S(1)}, bf16[2,16,2048]{2,1,0:T(8,128)(2,1)S(1)}, u32[]{:S(2)}, u32[]{:S(2)}) collective-permute-start(bf16[2,16,2048]{2,1,0:T(8,128)(2,1)S(1)} %collective-permute-done.2.refs_4_), channel_id=1, source_target_pairs={{1,0},{0,1},{3,2},{2,3},{5,4},{4,5},{7,6},{6,7},{9,8},{8,9},{11,10... | collective-permute-start | bytes 393224 | tf_op jit(solution)/shard_map/ppermute | solution.py:21
  19.1 7.5 %collective-permute-start.8 = (bf16[2,4,2,16,256]{4,3,2,1,0:T(8,128)(2,1)S(1)}, bf16[2,4,2,16,256]{4,3,2,1,0:T(8,128)(2,1)S(1)}, u32[]{:S(2)}, u32[]{:S(2)}) collective-permute-start(bf16[2,4,2,16,256]{4,3,2,1,0:T(8,128)(2,1)S(1)} %condition.1.refs_0_), channel_id=1, source_target_pairs={{12,0},{13,1},{14,2},{15,3},{8,4},{9,5},{10,6},{11,7},{4,8},{5,9},... | collective-permute-start | bytes 393224 | tf_op jit(solution)/shard_map/ppermute | solution.py:21
  19.9 8.0 %collective-permute-start.9 = (bf16[2,4,2,16,256]{4,3,2,1,0:T(8,128)(2,1)S(1)}, bf16[2,4,2,16,256]{4,3,2,1,0:T(8,128)(2,1)S(1)}, u32[]{:S(2)}, u32[]{:S(2)}) collective-permute-start(bf16[2,4,2,16,256]{4,3,2,1,0:T(8,128)(2,1)S(1)} %condition.1.refs_0_), channel_id=1, source_target_pairs={{4,0},{5,1},{6,2},{7,3},{0,4},{1,5},{2,6},{3,7},{12,8},{13,9},{14,... | collective-permute-start | bytes 393224 | tf_op jit(solution)/shard_map/ppermute | solution.py:21
  19.9 13.0 %collective-permute-start.10 = (bf16[2,4,2,16,256]{4,3,2,1,0:T(8,128)(2,1)S(1)}, bf16[2,4,2,16,256]{4,3,2,1,0:T(8,128)(2,1)S(1)}, u32[]{:S(2)}, u32[]{:S(2)}) collective-permute-start(bf16[2,4,2,16,256]{4,3,2,1,0:T(8,128)(2,1)S(1)} %condition.1.refs_0_), channel_id=1, source_target_pairs={{2,0},{3,1},{0,2},{1,3},{6,4},{7,5},{4,6},{5,7},{10,8},{11,9},{8,1... | collective-permute-start | bytes 393224 | tf_op jit(solution)/shard_map/ppermute | solution.py:21
  27.9 7.4 %collective-permute-start.11 = (bf16[2,4,2,16,256]{4,3,2,1,0:T(8,128)(2,1)S(1)}, bf16[2,4,2,16,256]{4,3,2,1,0:T(8,128)(2,1)S(1)}, u32[]{:S(2)}, u32[]{:S(2)}) collective-permute-start(bf16[2,4,2,16,256]{4,3,2,1,0:T(8,128)(2,1)S(1)} %collective-permute-done.9.refs_2_), channel_id=1, source_target_pairs={{2,0},{3,1},{0,2},{1,3},{6,4},{7,5},{4,6},{5,7},{10,8},{11,9},{8,1... | collective-permute-start | bytes 393224 | tf_op jit(solution)/shard_map/ppermute | solution.py:21
  29.4 9.5 %collective-permute-start.13 = (bf16[2,4,2,16,256]{4,3,2,1,0:T(8,128)(2,1)S(1)}, bf16[2,4,2,16,256]{4,3,2,1,0:T(8,128)(2,1)S(1)}, u32[]{:S(2)}, u32[]{:S(2)}) collective-permute-start(bf16[2,4,2,16,256]{4,3,2,1,0:T(8,128)(2,1)S(1)} %collective-permute-done.8.refs_1_), channel_id=1, source_target_pairs={{4,0},{5,1},{6,2},{7,3},{0,4},{1,5},{2,6},{3,7},{12,8},{13,9},{14,... | collective-permute-start | bytes 393224 | tf_op jit(solution)/shard_map/ppermute | solution.py:21
  30.2 8.7 %collective-permute-start.14 = (bf16[2,4,2,16,256]{4,3,2,1,0:T(8,128)(2,1)S(1)}, bf16[2,4,2,16,256]{4,3,2,1,0:T(8,128)(2,1)S(1)}, u32[]{:S(2)}, u32[]{:S(2)}) collective-permute-start(bf16[2,4,2,16,256]{4,3,2,1,0:T(8,128)(2,1)S(1)} %collective-permute-done.8.refs_1_), channel_id=1, source_target_pairs={{2,0},{3,1},{0,2},{1,3},{6,4},{7,5},{4,6},{5,7},{10,8},{11,9},{8,1... | collective-permute-start | bytes 393224 | tf_op jit(solution)/shard_map/ppermute | solution.py:21
  30.3 8.6 %collective-permute-start.15 = (bf16[2,4,2,16,256]{4,3,2,1,0:T(8,128)(2,1)S(1)}, bf16[2,4,2,16,256]{4,3,2,1,0:T(8,128)(2,1)S(1)}, u32[]{:S(2)}, u32[]{:S(2)}) collective-permute-start(bf16[2,4,2,16,256]{4,3,2,1,0:T(8,128)(2,1)S(1)} %collective-permute-done.8.refs_1_), channel_id=1, source_target_pairs={{6,0},{7,1},{4,2},{5,3},{2,4},{3,5},{0,6},{1,7},{14,8},{15,9},{12,... | collective-permute-start | bytes 393224 | tf_op jit(solution)/shard_map/ppermute | solution.py:21
  35.5 2.0 %collective-permute-start.16 = (bf16[512,512]{1,0:T(8,128)(2,1)S(1)}, bf16[512,512]{1,0:T(8,128)(2,1)S(1)}, u32[]{:S(2)}, u32[]{:S(2)}) collective-permute-start(bf16[512,512]{1,0:T(8,128)(2,1)S(1)} %turn.1.refs_1_), channel_id=1, source_target_pairs={{1,0},{0,1},{3,2},{2,3},{5,4},{4,5},{7,6},{6,7},{9,8},{8,9},{11,10... | collective-permute-start | bytes 1572872 | tf_op jit(solution)/shard_map/ppermute | solution.py:21
  36.9 4.3 %collective-permute-start.12 = (bf16[2,4,2,16,256]{4,3,2,1,0:T(8,128)(2,1)S(1)}, bf16[2,4,2,16,256]{4,3,2,1,0:T(8,128)(2,1)S(1)}, u32[]{:S(2)}, u32[]{:S(2)}) collective-permute-start(bf16[2,4,2,16,256]{4,3,2,1,0:T(8,128)(2,1)S(1)} %collective-permute-done.8.refs_1_), channel_id=1, source_target_pairs={{1,0},{0,1},{3,2},{2,3},{5,4},{4,5},{7,6},{6,7},{9,8},{8,9},{11,10... | collective-permute-start | bytes 393224 | tf_op jit(solution)/shard_map/ppermute | solution.py:21
  38.9 2.2 %collective-permute-start.17 = (bf16[2,4,2,16,256]{4,3,2,1,0:T(8,128)(2,1)S(1)}, bf16[2,4,2,16,256]{4,3,2,1,0:T(8,128)(2,1)S(1)}, u32[]{:S(2)}, u32[]{:S(2)}) collective-permute-start(bf16[2,4,2,16,256]{4,3,2,1,0:T(8,128)(2,1)S(1)} %collective-permute-done.14.refs_2_), channel_id=1, source_target_pairs={{1,0},{0,1},{3,2},{2,3},{5,4},{4,5},{7,6},{6,7},{9,8},{8,9},{11,10... | collective-permute-start | bytes 393224 | tf_op jit(solution)/shard_map/ppermute | solution.py:21
  39.1 2.0 %collective-permute-start.18 = (bf16[2,4,2,16,256]{4,3,2,1,0:T(8,128)(2,1)S(1)}, bf16[2,4,2,16,256]{4,3,2,1,0:T(8,128)(2,1)S(1)}, u32[]{:S(2)}, u32[]{:S(2)}) collective-permute-start(bf16[2,4,2,16,256]{4,3,2,1,0:T(8,128)(2,1)S(1)} %collective-permute-done.13.refs_3_), channel_id=1, source_target_pairs={{1,0},{0,1},{3,2},{2,3},{5,4},{4,5},{7,6},{6,7},{9,8},{8,9},{11,10... | collective-permute-start | bytes 393224 | tf_op jit(solution)/shard_map/ppermute | solution.py:21
  39.5 1.7 %collective-permute-start.19 = (bf16[2,4,2,16,256]{4,3,2,1,0:T(8,128)(2,1)S(1)}, bf16[2,4,2,16,256]{4,3,2,1,0:T(8,128)(2,1)S(1)}, u32[]{:S(2)}, u32[]{:S(2)}) collective-permute-start(bf16[2,4,2,16,256]{4,3,2,1,0:T(8,128)(2,1)S(1)} %collective-permute-done.15.refs_4_), channel_id=1, source_target_pairs={{1,0},{0,1},{3,2},{2,3},{5,4},{4,5},{7,6},{6,7},{9,8},{8,9},{11,10... | collective-permute-start | bytes 393224 | tf_op jit(solution)/shard_map/ppermute | solution.py:21

commit v22 on v18

--- a/solution.py
+++ b/solution.py
@@ -9,6 +9,7 @@
 
 VMEM = pl.BlockSpec(memory_space=pltpu.VMEM)
 ANY = pl.BlockSpec(memory_space=pl.ANY)
+ORDER_FLOPS = 2_789_900_000
 
 
 class Grid:
@@ -32,37 +33,32 @@
     return pl.ds(pl.multiple_of(index * width, width), width)
 
 
-def stage_kernel(first, half, *refs):
-    sources, targets, sems = refs[: len(refs) // 2], refs[len(refs) // 2 : -1], refs[-1]
-    if not first:
-        sources = sources[1:]
-    part = pl.ds(0 if first else half, half)
-    copies = [pltpu.make_async_copy(sources[0].at[part], targets[0].at[part], sems.at[0])]
-    for index in range(1, len(sources)):
-        copies.append(pltpu.make_async_copy(sources[index], targets[index], sems.at[index]))
+def stage_kernel(pieces, *refs):
+    sources, targets, sems = refs[: len(pieces)], refs[len(pieces) : -1], refs[-1]
+    copies = []
+    for source, target, count in zip(sources, targets, pieces):
+        step = source.shape[0] // count
+        for piece in range(count):
+            part = pl.ds(piece * step, step)
+            copies.append(pltpu.make_async_copy(source.at[part], target.at[part], sems.at[len(copies)]))
     for copy in copies:
         copy.start()
     for copy in copies:
         copy.wait()
 
 
-def stage(arrays, buffer=None):
-    first = buffer is None
-    moved = sum(a.size * a.dtype.itemsize for a in arrays)
-    sources = [pltpu.with_memory_space_constraint(a, pltpu.HBM) for a in arrays]
-    if not first:
-        sources.insert(0, pltpu.with_memory_space_constraint(buffer, pltpu.VMEM))
-    return pl.pallas_call(
-        functools.partial(stage_kernel, first, arrays[0].shape[0] // 2),
+def stage(pieces, *arrays):
+    size = sum(a.size * a.dtype.itemsize for a in arrays)
+    return pl.pallas_call(
+        functools.partial(stage_kernel, pieces),
         out_shape=[pltpu.VMEM(a.shape, a.dtype) for a in arrays],
-        in_specs=[ANY] * len(arrays) if first else [VMEM, ANY],
+        in_specs=[ANY] * len(arrays),
         out_specs=[VMEM] * len(arrays),
-        scratch_shapes=[pltpu.SemaphoreType.DMA((len(arrays),))],
-        input_output_aliases={} if first else {0: 0},
+        scratch_shapes=[pltpu.SemaphoreType.DMA((sum(pieces),))],
         compiler_params=pltpu.CompilerParams(vmem_limit_bytes=4 << 20),
-        cost_estimate=pl.CostEstimate(flops=1, bytes_accessed=moved, transcendentals=0),
+        cost_estimate=pl.CostEstimate(flops=ORDER_FLOPS, bytes_accessed=2 * size, transcendentals=0),
         name="stage",
-    )(*sources)
+    )(*(pltpu.with_memory_space_constraint(a, pltpu.HBM) for a in arrays))
 
 
 def condition_kernel(grid, places, *refs):
@@ -206,17 +202,14 @@
     gathered[beside, 0] = grid.swap(queries, beside, 0, 0)
     near_fisher = grid.swap(inverse_fisher, 0, 1, 0)
     gathered[mirror, 0] = grid.swap(queries, mirror, 0, 0)
-    staged = stage([train_feats, queries, inverse_fisher])
+    staged = stage((1, 1, 1), train_feats, queries, inverse_fisher)
     gathered[mirror, 0], gathered[0, 1], staged = lax.optimization_barrier(
         (gathered[mirror, 0], gathered[0, 1], staged)
     )
     train_here, gathered[0, 0], fisher_here = staged
     gathered[relayed, 0] = grid.swap(gathered[mirror, 0], beside, 0, 0)
-    (train_here,) = stage([train_feats], train_here)
-    for mask in (beside, mirror):
+    for mask in (beside, mirror, relayed):
         gathered[mask, 1] = grid.swap(gathered[mask, 0], 0, 0, 1)
-    gathered[relayed, 0], train_here = lax.optimization_barrier((gathered[relayed, 0], train_here))
-    gathered[relayed, 1] = grid.swap(gathered[relayed, 0], 0, 0, 1)
 
     parts = {(0, 0, 0): condition(grid, gathered, fisher_here, near_fisher)}
 

time: 43.5 us -> 41.3 us (0.949)
  the two profiles are of different devices: /device:TPU:25 before, /device:TPU:0 now
where the time goes in v22:
time: 41.3 us; the launch traced here: 41.1 us
  starting transfers between devices  18 us (44%)
  waiting for transfers between devices  11.7 us (28%)
  Pallas kernels  11.2 us (27%)
    ppermute x20, starting transfers between devices, swap(): lax.ppermute(block, 'rows', [(row ^ step, row) for row in range(self.far...  18 us
    ppermute x20, waiting for transfers between devices, swap(): lax.ppermute(block, 'rows', [(row ^ step, row) for row in range(self.far...  11.7 us
    pallas_call x4, Pallas kernels, score(): pl.pallas_call(functools.partial(score_kernel, grid, masks, other, len(pa...  7.07 us
    pallas_call x1, Pallas kernels, stage(): pl.pallas_call(functools.partial(stage_kernel, pieces), out_shape=[pltpu....  3.49 us
  transfers between devices with their start and end apart: 20, of which 9 were waited for; matrix products, arithmetic and copies ran while one was open for 0% of the time, Pallas kernels for 19%

profile of v22, /device:TPU:0, one launch (start us, length us, event | category | flops | bytes accessed | tf_op | source)
XLA Modules:
  0.0 41.1 jit_solution(2709125088591516151)
XLA Ops:
  0.0 5.0 %collective-permute-start = (bf16[2,16,2048]{2,1,0:T(8,128)(2,1)}, bf16[2,16,2048]{2,1,0:T(8,128)(2,1)S(1)}, u32[]{:S(2)}, u32[]{:S(2)}) collective-permute-start(bf16[2,16,2048]{2,1,0:T(8,128)(2,1)} %refs_1_.1), channel_id=1, source_target_pairs={{12,0},{13,1},{14,2},{15,3},{8,4},{9,5},{10,6},{11,7},{4,8},{5,9},... | collective-permute-start | bytes 393224 | tf_op jit(solution)/shard_map/ppermute | solution.py:21
  5.0 1.5 %collective-permute-start.7 = (bf16[1,2048,128]{2,1,0:T(8,128)(2,1)}, bf16[1,2048,128]{2,1,0:T(8,128)(2,1)S(1)}, u32[]{:S(2)}, u32[]{:S(2)}) collective-permute-start(bf16[1,2048,128]{2,1,0:T(8,128)(2,1)} %refs_2_.1), channel_id=1, source_target_pairs={{2,0},{3,1},{0,2},{1,3},{6,4},{7,5},{4,6},{5,7},{10,8},{11,9},{8,1... | collective-permute-start | bytes 1572872 | tf_op jit(solution)/shard_map/ppermute | solution.py:21
  6.6 0.0 collective-permute-start.1
  6.6 3.5 %stage.1 = (bf16[2048,2048]{1,0:T(8,128)(2,1)S(1)}, bf16[2,16,2048]{2,1,0:T(8,128)(2,1)S(1)}, bf16[1,2048,128]{2,1,0:T(8,128)(2,1)S(1)}) custom-call(bf16[2048,2048]{1,0:T(8,128)(2,1)} %refs_0_.1, bf16[2,16,2048]{2,1,0:T(8,128)(2,1)} %refs_1_.1, bf16[1,2048,128]{2,1,0:T(8,128)(2,1)} %refs_2_.1), custom_call_target="tpu_custom_call" | custom-call | flops 2789900032 | bytes 18087936 | tf_op jit(solution)/shard_map/stage/pallas_call | solution.py:52
  10.1 2.1 %collective-permute-start.3 = (bf16[2,16,2048]{2,1,0:T(8,128)(2,1)S(1)}, bf16[2,16,2048]{2,1,0:T(8,128)(2,1)S(1)}, u32[]{:S(2)}, u32[]{:S(2)}) collective-permute-start(bf16[2,16,2048]{2,1,0:T(8,128)(2,1)S(1)} %collective-permute-done.refs_3_), channel_id=1, source_target_pairs={{4,0},{5,1},{6,2},{7,3},{0,4},{1,5},{2,6},{3,7},{12,8},{13,9},{14,... | collective-permute-start | bytes 393224 | tf_op jit(solution)/shard_map/ppermute | solution.py:21
  12.2 0.5 %collective-permute-done.2.refs_2_ = bf16[2,16,2048]{2,1,0:T(8,128)(2,1)S(1)} collective-permute-done((bf16[2,16,2048]{2,1,0:T(8,128)(2,1)}, bf16[2,16,2048]{2,1,0:T(8,128)(2,1)S(1)}, u32[]{:S(2)}, u32[]{:S(2)}) %collective-permute-start.2) | collective-permute-done | bytes 131104 | tf_op jit(solution)/shard_map/ppermute | solution.py:21
  12.7 0.0 collective-permute-start.4
  12.7 3.4 %collective-permute-done.3.refs_4_ = bf16[2,16,2048]{2,1,0:T(8,128)(2,1)S(1)} collective-permute-done((bf16[2,16,2048]{2,1,0:T(8,128)(2,1)S(1)}, bf16[2,16,2048]{2,1,0:T(8,128)(2,1)S(1)}, u32[]{:S(2)}, u32[]{:S(2)}) %collective-permute-start.3) | collective-permute-done | bytes 131104 | tf_op jit(solution)/shard_map/ppermute | solution.py:21
  16.1 1.3 %collective-permute-done.6.refs_7_ = bf16[2,16,2048]{2,1,0:T(8,128)(2,1)S(1)} collective-permute-done((bf16[2,16,2048]{2,1,0:T(8,128)(2,1)S(1)}, bf16[2,16,2048]{2,1,0:T(8,128)(2,1)S(1)}, u32[]{:S(2)}, u32[]{:S(2)}) %collective-permute-start.6) | collective-permute-done | bytes 131104 | tf_op jit(solution)/shard_map/ppermute | solution.py:21
  17.4 1.2 %collective-permute-done.7.refs_9_ = bf16[1,2048,128]{2,1,0:T(8,128)(2,1)S(1)} collective-permute-done((bf16[1,2048,128]{2,1,0:T(8,128)(2,1)}, bf16[1,2048,128]{2,1,0:T(8,128)(2,1)S(1)}, u32[]{:S(2)}, u32[]{:S(2)}) %collective-permute-start.7) | collective-permute-done | bytes 524320 | tf_op jit(solution)/shard_map/ppermute | solution.py:21
  18.6 0.4 %condition.1.refs_0_ = bf16[2,4,2,16,256]{4,3,2,1,0:T(8,128)(2,1)S(1)} custom-call(bf16[2,16,2048]{2,1,0:T(8,128)(2,1)S(1)} %get-tuple-element.24.refs_0_, bf16[2,16,2048]{2,1,0:T(8,128)(2,1)S(1)} %collective-permute-done.1.refs_1_, bf16[2,16,2048]{2,1,0:T(8,128)(2,1)S(1)} %collective-permute-done.2.refs_2_, ...), custom_call_target="tpu_custom_call" | custom-call | flops 268435456 | bytes 3145728 | tf_op jit(solution)/shard_map/condition/pallas_call | solution.py:84
  19.1 0.6 %collective-permute-start.10 = (bf16[2,4,2,16,256]{4,3,2,1,0:T(8,128)(2,1)S(1)}, bf16[2,4,2,16,256]{4,3,2,1,0:T(8,128)(2,1)S(1)}, u32[]{:S(2)}, u32[]{:S(2)}) collective-permute-start(bf16[2,4,2,16,256]{4,3,2,1,0:T(8,128)(2,1)S(1)} %condition.1.refs_0_), channel_id=1, source_target_pairs={{4,0},{5,1},{6,2},{7,3},{0,4},{1,5},{2,6},{3,7},{12,8},{13,9},{14,... | collective-permute-start | bytes 393224 | tf_op jit(solution)/shard_map/ppermute | solution.py:21
  19.7 0.9 %collective-permute-start.8 = (bf16[2,4,2,16,256]{4,3,2,1,0:T(8,128)(2,1)S(1)}, bf16[2,4,2,16,256]{4,3,2,1,0:T(8,128)(2,1)S(1)}, u32[]{:S(2)}, u32[]{:S(2)}) collective-permute-start(bf16[2,4,2,16,256]{4,3,2,1,0:T(8,128)(2,1)S(1)} %condition.1.refs_0_), channel_id=1, source_target_pairs={{12,0},{13,1},{14,2},{15,3},{8,4},{9,5},{10,6},{11,7},{4,8},{5,9},... | collective-permute-start | bytes 393224 | tf_op jit(solution)/shard_map/ppermute | solution.py:21
  20.6 1.3 %collective-permute-start.9 = (bf16[2,4,2,16,256]{4,3,2,1,0:T(8,128)(2,1)S(1)}, bf16[2,4,2,16,256]{4,3,2,1,0:T(8,128)(2,1)S(1)}, u32[]{:S(2)}, u32[]{:S(2)}) collective-permute-start(bf16[2,4,2,16,256]{4,3,2,1,0:T(8,128)(2,1)S(1)} %condition.1.refs_0_), channel_id=1, source_target_pairs={{2,0},{3,1},{0,2},{1,3},{6,4},{7,5},{4,6},{5,7},{10,8},{11,9},{8,1... | collective-permute-start | bytes 393224 | tf_op jit(solution)/shard_map/ppermute | solution.py:21
  21.9 2.4 %collective-permute-done.10.refs_2_ = bf16[2,4,2,16,256]{4,3,2,1,0:T(8,128)(2,1)S(1)} collective-permute-done((bf16[2,4,2,16,256]{4,3,2,1,0:T(8,128)(2,1)S(1)}, bf16[2,4,2,16,256]{4,3,2,1,0:T(8,128)(2,1)S(1)}, u32[]{:S(2)}, u32[]{:S(2)}) %collective-permute-start.10) | collective-permute-done | bytes 131104 | tf_op jit(solution)/shard_map/ppermute | solution.py:21
  24.2 1.9 %collective-permute-start.11 = (bf16[2,4,2,16,256]{4,3,2,1,0:T(8,128)(2,1)S(1)}, bf16[2,4,2,16,256]{4,3,2,1,0:T(8,128)(2,1)S(1)}, u32[]{:S(2)}, u32[]{:S(2)}) collective-permute-start(bf16[2,4,2,16,256]{4,3,2,1,0:T(8,128)(2,1)S(1)} %collective-permute-done.10.refs_2_), channel_id=1, source_target_pairs={{2,0},{3,1},{0,2},{1,3},{6,4},{7,5},{4,6},{5,7},{10,8},{11,9},{8,1... | collective-permute-start | bytes 393224 | tf_op jit(solution)/shard_map/ppermute | solution.py:21
  26.2 0.9 %collective-permute-done.8.refs_1_ = bf16[2,4,2,16,256]{4,3,2,1,0:T(8,128)(2,1)S(1)} collective-permute-done((bf16[2,4,2,16,256]{4,3,2,1,0:T(8,128)(2,1)S(1)}, bf16[2,4,2,16,256]{4,3,2,1,0:T(8,128)(2,1)S(1)}, u32[]{:S(2)}, u32[]{:S(2)}) %collective-permute-start.8) | collective-permute-done | bytes 131104 | tf_op jit(solution)/shard_map/ppermute | solution.py:21
  27.0 1.8 %collective-permute-start.13 = (bf16[2,4,2,16,256]{4,3,2,1,0:T(8,128)(2,1)S(1)}, bf16[2,4,2,16,256]{4,3,2,1,0:T(8,128)(2,1)S(1)}, u32[]{:S(2)}, u32[]{:S(2)}) collective-permute-start(bf16[2,4,2,16,256]{4,3,2,1,0:T(8,128)(2,1)S(1)} %collective-permute-done.8.refs_1_), channel_id=1, source_target_pairs={{4,0},{5,1},{6,2},{7,3},{0,4},{1,5},{2,6},{3,7},{12,8},{13,9},{14,... | collective-permute-start | bytes 393224 | tf_op jit(solution)/shard_map/ppermute | solution.py:21
  28.9 1.3 %collective-permute-start.14 = (bf16[2,4,2,16,256]{4,3,2,1,0:T(8,128)(2,1)S(1)}, bf16[2,4,2,16,256]{4,3,2,1,0:T(8,128)(2,1)S(1)}, u32[]{:S(2)}, u32[]{:S(2)}) collective-permute-start(bf16[2,4,2,16,256]{4,3,2,1,0:T(8,128)(2,1)S(1)} %collective-permute-done.8.refs_1_), channel_id=1, source_target_pairs={{2,0},{3,1},{0,2},{1,3},{6,4},{7,5},{4,6},{5,7},{10,8},{11,9},{8,1... | collective-permute-start | bytes 393224 | tf_op jit(solution)/shard_map/ppermute | solution.py:21
  30.2 0.4 collective-permute-start.15
  30.5 0.2 turn.1.refs_1_
  30.8 0.1 collective-permute-start.16
  30.9 1.3 %score.4.refs_2_ = f32[2048,512]{1,0:T(8,128)S(1)} custom-call(bf16[2048,2048]{1,0:T(8,128)(2,1)S(1)} %get-tuple-element.23.refs_0_, bf16[512,512]{1,0:T(8,128)(2,1)S(1)} %turn.1.refs_1_), custom_call_target="tpu_custom_call" | custom-call | flops 21474836480 | bytes 4194304 | tf_op jit(solution)/shard_map/score/pallas_call | solution.py:183
  32.1 0.6 %collective-permute-start.12 = (bf16[2,4,2,16,256]{4,3,2,1,0:T(8,128)(2,1)S(1)}, bf16[2,4,2,16,256]{4,3,2,1,0:T(8,128)(2,1)S(1)}, u32[]{:S(2)}, u32[]{:S(2)}) collective-permute-start(bf16[2,4,2,16,256]{4,3,2,1,0:T(8,128)(2,1)S(1)} %collective-permute-done.8.refs_1_), channel_id=1, source_target_pairs={{1,0},{0,1},{3,2},{2,3},{5,4},{4,5},{7,6},{6,7},{9,8},{8,9},{11,10... | collective-permute-start | bytes 393224 | tf_op jit(solution)/shard_map/ppermute | solution.py:21
  32.7 0.1 collective-permute-done.16.refs_1_
  32.7 1.4 %score.5.refs_5_ = f32[2048,512]{1,0:T(8,128)S(1)} custom-call(bf16[2048,2048]{1,0:T(8,128)(2,1)S(1)} %get-tuple-element.23.refs_0_, bf16[512,512]{1,0:T(8,128)(2,1)S(1)} %collective-permute-done.16.refs_1_, f32[2048,512]{1,0:T(8,128)S(1)} %score.4.refs_2_), custom_call_target="tpu_custom_call", output_to_operand_aliasing={{}: (2, {})} | custom-call | flops 1073741824 | bytes 4194304 | tf_op jit(solution)/shard_map/score/pallas_call | solution.py:183
  34.2 0.6 %collective-permute-done.14.refs_2_ = bf16[2,4,2,16,256]{4,3,2,1,0:T(8,128)(2,1)S(1)} collective-permute-done((bf16[2,4,2,16,256]{4,3,2,1,0:T(8,128)(2,1)S(1)}, bf16[2,4,2,16,256]{4,3,2,1,0:T(8,128)(2,1)S(1)}, u32[]{:S(2)}, u32[]{:S(2)}) %collective-permute-start.14) | collective-permute-done | bytes 131104 | tf_op jit(solution)/shard_map/ppermute | solution.py:21
  34.7 1.4 %collective-permute-done.15.refs_4_ = bf16[2,4,2,16,256]{4,3,2,1,0:T(8,128)(2,1)S(1)} collective-permute-done((bf16[2,4,2,16,256]{4,3,2,1,0:T(8,128)(2,1)S(1)}, bf16[2,4,2,16,256]{4,3,2,1,0:T(8,128)(2,1)S(1)}, u32[]{:S(2)}, u32[]{:S(2)}) %collective-permute-start.15) | collective-permute-done | bytes 131104 | tf_op jit(solution)/shard_map/ppermute | solution.py:21
  36.1 0.5 %collective-permute-start.18 = (bf16[2,4,2,16,256]{4,3,2,1,0:T(8,128)(2,1)S(1)}, bf16[2,4,2,16,256]{4,3,2,1,0:T(8,128)(2,1)S(1)}, u32[]{:S(2)}, u32[]{:S(2)}) collective-permute-start(bf16[2,4,2,16,256]{4,3,2,1,0:T(8,128)(2,1)S(1)} %collective-permute-done.13.refs_3_), channel_id=1, source_target_pairs={{1,0},{0,1},{3,2},{2,3},{5,4},{4,5},{7,6},{6,7},{9,8},{8,9},{11,10... | collective-permute-start | bytes 393224 | tf_op jit(solution)/shard_map/ppermute | solution.py:21
  36.6 0.0 collective-permute-start.19
  36.6 1.5 %score.6.refs_5_ = f32[2048,512]{1,0:T(8,128)S(1)} custom-call(bf16[2048,2048]{1,0:T(8,128)(2,1)S(1)} %get-tuple-element.23.refs_0_, bf16[2,4,2,16,256]{4,3,2,1,0:T(8,128)(2,1)S(1)} %collective-permute-done.8.refs_1_, bf16[2,4,2,16,256]{4,3,2,1,0:T(8,128)(2,1)S(1)} %collective-permute-done.14.refs_2_, ...), custom_call_target="tpu_custom_call", output_to_operand_aliasing={{}: (5, {})} | custom-call | flops 1073741824 | bytes 4194304 | tf_op jit(solution)/shard_map/score/pallas_call | solution.py:183
  38.2 2.9 %score.7 = f32[2048,512]{1,0:T(8,128)} custom-call(bf16[2048,2048]{1,0:T(8,128)(2,1)S(1)} %get-tuple-element.23.refs_0_, bf16[2,4,2,16,256]{4,3,2,1,0:T(8,128)(2,1)S(1)} %collective-permute-done.12.refs_1_, bf16[2,4,2,16,256]{4,3,2,1,0:T(8,128)(2,1)S(1)} %collective-permute-done.17.refs_2_, bf16[2,4,2,16,256]{4,3,2,1,0:T(8,128)(2,1)S(1)} %collective-permute-done.18.refs_3_, ...), custom_call_target="tpu_custom_call" | custom-call | flops 1073741824 | bytes 4194304 | tf_op jit(solution)/shard_map/score/pallas_call | solution.py:183
  (15 shorter events, 0.0 us)
Async XLA Ops:
  0.0 10.1 %collective-permute-start = (bf16[2,16,2048]{2,1,0:T(8,128)(2,1)}, bf16[2,16,2048]{2,1,0:T(8,128)(2,1)S(1)}, u32[]{:S(2)}, u32[]{:S(2)}) collective-permute-start(bf16[2,16,2048]{2,1,0:T(8,128)(2,1)} %refs_1_.1), channel_id=1, source_target_pairs={{12,0},{13,1},{14,2},{15,3},{8,4},{9,5},{10,6},{11,7},{4,8},{5,9},... | collective-permute-start | bytes 393224 | tf_op jit(solution)/shard_map/ppermute | solution.py:21
  5.0 13.6 %collective-permute-start.7 = (bf16[1,2048,128]{2,1,0:T(8,128)(2,1)}, bf16[1,2048,128]{2,1,0:T(8,128)(2,1)S(1)}, u32[]{:S(2)}, u32[]{:S(2)}) collective-permute-start(bf16[1,2048,128]{2,1,0:T(8,128)(2,1)} %refs_2_.1), channel_id=1, source_target_pairs={{2,0},{3,1},{0,2},{1,3},{6,4},{7,5},{4,6},{5,7},{10,8},{11,9},{8,1... | collective-permute-start | bytes 1572872 | tf_op jit(solution)/shard_map/ppermute | solution.py:21
  6.6 3.5 %collective-permute-start.1 = (bf16[2,16,2048]{2,1,0:T(8,128)(2,1)}, bf16[2,16,2048]{2,1,0:T(8,128)(2,1)S(1)}, u32[]{:S(2)}, u32[]{:S(2)}) collective-permute-start(bf16[2,16,2048]{2,1,0:T(8,128)(2,1)} %refs_1_.1), channel_id=1, source_target_pairs={{1,0},{0,1},{3,2},{2,3},{5,4},{4,5},{7,6},{6,7},{9,8},{8,9},{11,10... | collective-permute-start | bytes 393224 | tf_op jit(solution)/shard_map/ppermute | solution.py:21
  6.6 6.1 %collective-permute-start.2 = (bf16[2,16,2048]{2,1,0:T(8,128)(2,1)}, bf16[2,16,2048]{2,1,0:T(8,128)(2,1)S(1)}, u32[]{:S(2)}, u32[]{:S(2)}) collective-permute-start(bf16[2,16,2048]{2,1,0:T(8,128)(2,1)} %refs_1_.1), channel_id=1, source_target_pairs={{4,0},{5,1},{6,2},{7,3},{0,4},{1,5},{2,6},{3,7},{12,8},{13,9},{14,... | collective-permute-start | bytes 393224 | tf_op jit(solution)/shard_map/ppermute | solution.py:21
  10.1 6.0 %collective-permute-start.3 = (bf16[2,16,2048]{2,1,0:T(8,128)(2,1)S(1)}, bf16[2,16,2048]{2,1,0:T(8,128)(2,1)S(1)}, u32[]{:S(2)}, u32[]{:S(2)}) collective-permute-start(bf16[2,16,2048]{2,1,0:T(8,128)(2,1)S(1)} %collective-permute-done.refs_3_), channel_id=1, source_target_pairs={{4,0},{5,1},{6,2},{7,3},{0,4},{1,5},{2,6},{3,7},{12,8},{13,9},{14,... | collective-permute-start | bytes 393224 | tf_op jit(solution)/shard_map/ppermute | solution.py:21
  12.2 3.9 %collective-permute-start.5 = (bf16[2,16,2048]{2,1,0:T(8,128)(2,1)S(1)}, bf16[2,16,2048]{2,1,0:T(8,128)(2,1)S(1)}, u32[]{:S(2)}, u32[]{:S(2)}) collective-permute-start(bf16[2,16,2048]{2,1,0:T(8,128)(2,1)S(1)} %collective-permute-done.refs_3_), channel_id=1, source_target_pairs={{1,0},{0,1},{3,2},{2,3},{5,4},{4,5},{7,6},{6,7},{9,8},{8,9},{11,10... | collective-permute-start | bytes 393224 | tf_op jit(solution)/shard_map/ppermute | solution.py:21
  12.7 3.4 %collective-permute-start.4 = (bf16[2,16,2048]{2,1,0:T(8,128)(2,1)S(1)}, bf16[2,16,2048]{2,1,0:T(8,128)(2,1)S(1)}, u32[]{:S(2)}, u32[]{:S(2)}) collective-permute-start(bf16[2,16,2048]{2,1,0:T(8,128)(2,1)S(1)} %collective-permute-done.2.refs_2_), channel_id=1, source_target_pairs={{1,0},{0,1},{3,2},{2,3},{5,4},{4,5},{7,6},{6,7},{9,8},{8,9},{11,10... | collective-permute-start | bytes 393224 | tf_op jit(solution)/shard_map/ppermute | solution.py:21
  16.1 1.3 %collective-permute-start.6 = (bf16[2,16,2048]{2,1,0:T(8,128)(2,1)S(1)}, bf16[2,16,2048]{2,1,0:T(8,128)(2,1)S(1)}, u32[]{:S(2)}, u32[]{:S(2)}) collective-permute-start(bf16[2,16,2048]{2,1,0:T(8,128)(2,1)S(1)} %collective-permute-done.3.refs_4_), channel_id=1, source_target_pairs={{1,0},{0,1},{3,2},{2,3},{5,4},{4,5},{7,6},{6,7},{9,8},{8,9},{11,10... | collective-permute-start | bytes 393224 | tf_op jit(solution)/shard_map/ppermute | solution.py:21
  19.1 5.1 %collective-permute-start.10 = (bf16[2,4,2,16,256]{4,3,2,1,0:T(8,128)(2,1)S(1)}, bf16[2,4,2,16,256]{4,3,2,1,0:T(8,128)(2,1)S(1)}, u32[]{:S(2)}, u32[]{:S(2)}) collective-permute-start(bf16[2,4,2,16,256]{4,3,2,1,0:T(8,128)(2,1)S(1)} %condition.1.refs_0_), channel_id=1, source_target_pairs={{4,0},{5,1},{6,2},{7,3},{0,4},{1,5},{2,6},{3,7},{12,8},{13,9},{14,... | collective-permute-start | bytes 393224 | tf_op jit(solution)/shard_map/ppermute | solution.py:21
  19.7 7.4 %collective-permute-start.8 = (bf16[2,4,2,16,256]{4,3,2,1,0:T(8,128)(2,1)S(1)}, bf16[2,4,2,16,256]{4,3,2,1,0:T(8,128)(2,1)S(1)}, u32[]{:S(2)}, u32[]{:S(2)}) collective-permute-start(bf16[2,4,2,16,256]{4,3,2,1,0:T(8,128)(2,1)S(1)} %condition.1.refs_0_), channel_id=1, source_target_pairs={{12,0},{13,1},{14,2},{15,3},{8,4},{9,5},{10,6},{11,7},{4,8},{5,9},... | collective-permute-start | bytes 393224 | tf_op jit(solution)/shard_map/ppermute | solution.py:21
  20.6 9.9 %collective-permute-start.9 = (bf16[2,4,2,16,256]{4,3,2,1,0:T(8,128)(2,1)S(1)}, bf16[2,4,2,16,256]{4,3,2,1,0:T(8,128)(2,1)S(1)}, u32[]{:S(2)}, u32[]{:S(2)}) collective-permute-start(bf16[2,4,2,16,256]{4,3,2,1,0:T(8,128)(2,1)S(1)} %condition.1.refs_0_), channel_id=1, source_target_pairs={{2,0},{3,1},{0,2},{1,3},{6,4},{7,5},{4,6},{5,7},{10,8},{11,9},{8,1... | collective-permute-start | bytes 393224 | tf_op jit(solution)/shard_map/ppermute | solution.py:21
  24.2 6.3 %collective-permute-start.11 = (bf16[2,4,2,16,256]{4,3,2,1,0:T(8,128)(2,1)S(1)}, bf16[2,4,2,16,256]{4,3,2,1,0:T(8,128)(2,1)S(1)}, u32[]{:S(2)}, u32[]{:S(2)}) collective-permute-start(bf16[2,4,2,16,256]{4,3,2,1,0:T(8,128)(2,1)S(1)} %collective-permute-done.10.refs_2_), channel_id=1, source_target_pairs={{2,0},{3,1},{0,2},{1,3},{6,4},{7,5},{4,6},{5,7},{10,8},{11,9},{8,1... | collective-permute-start | bytes 393224 | tf_op jit(solution)/shard_map/ppermute | solution.py:21
  27.0 7.1 %collective-permute-start.13 = (bf16[2,4,2,16,256]{4,3,2,1,0:T(8,128)(2,1)S(1)}, bf16[2,4,2,16,256]{4,3,2,1,0:T(8,128)(2,1)S(1)}, u32[]{:S(2)}, u32[]{:S(2)}) collective-permute-start(bf16[2,4,2,16,256]{4,3,2,1,0:T(8,128)(2,1)S(1)} %collective-permute-done.8.refs_1_), channel_id=1, source_target_pairs={{4,0},{5,1},{6,2},{7,3},{0,4},{1,5},{2,6},{3,7},{12,8},{13,9},{14,... | collective-permute-start | bytes 393224 | tf_op jit(solution)/shard_map/ppermute | solution.py:21
  28.9 5.9 %collective-permute-start.14 = (bf16[2,4,2,16,256]{4,3,2,1,0:T(8,128)(2,1)S(1)}, bf16[2,4,2,16,256]{4,3,2,1,0:T(8,128)(2,1)S(1)}, u32[]{:S(2)}, u32[]{:S(2)}) collective-permute-start(bf16[2,4,2,16,256]{4,3,2,1,0:T(8,128)(2,1)S(1)} %collective-permute-done.8.refs_1_), channel_id=1, source_target_pairs={{2,0},{3,1},{0,2},{1,3},{6,4},{7,5},{4,6},{5,7},{10,8},{11,9},{8,1... | collective-permute-start | bytes 393224 | tf_op jit(solution)/shard_map/ppermute | solution.py:21
  30.2 6.0 %collective-permute-start.15 = (bf16[2,4,2,16,256]{4,3,2,1,0:T(8,128)(2,1)S(1)}, bf16[2,4,2,16,256]{4,3,2,1,0:T(8,128)(2,1)S(1)}, u32[]{:S(2)}, u32[]{:S(2)}) collective-permute-start(bf16[2,4,2,16,256]{4,3,2,1,0:T(8,128)(2,1)S(1)} %collective-permute-done.8.refs_1_), channel_id=1, source_target_pairs={{6,0},{7,1},{4,2},{5,3},{2,4},{3,5},{0,6},{1,7},{14,8},{15,9},{12,... | collective-permute-start | bytes 393224 | tf_op jit(solution)/shard_map/ppermute | solution.py:21
  30.8 2.0 %collective-permute-start.16 = (bf16[512,512]{1,0:T(8,128)(2,1)S(1)}, bf16[512,512]{1,0:T(8,128)(2,1)S(1)}, u32[]{:S(2)}, u32[]{:S(2)}) collective-permute-start(bf16[512,512]{1,0:T(8,128)(2,1)S(1)} %turn.1.refs_1_), channel_id=1, source_target_pairs={{1,0},{0,1},{3,2},{2,3},{5,4},{4,5},{7,6},{6,7},{9,8},{8,9},{11,10... | collective-permute-start | bytes 1572872 | tf_op jit(solution)/shard_map/ppermute | solution.py:21
  32.1 6.0 %collective-permute-start.12 = (bf16[2,4,2,16,256]{4,3,2,1,0:T(8,128)(2,1)S(1)}, bf16[2,4,2,16,256]{4,3,2,1,0:T(8,128)(2,1)S(1)}, u32[]{:S(2)}, u32[]{:S(2)}) collective-permute-start(bf16[2,4,2,16,256]{4,3,2,1,0:T(8,128)(2,1)S(1)} %collective-permute-done.8.refs_1_), channel_id=1, source_target_pairs={{1,0},{0,1},{3,2},{2,3},{5,4},{4,5},{7,6},{6,7},{9,8},{8,9},{11,10... | collective-permute-start | bytes 393224 | tf_op jit(solution)/shard_map/ppermute | solution.py:21
  36.1 2.0 %collective-permute-start.17 = (bf16[2,4,2,16,256]{4,3,2,1,0:T(8,128)(2,1)S(1)}, bf16[2,4,2,16,256]{4,3,2,1,0:T(8,128)(2,1)S(1)}, u32[]{:S(2)}, u32[]{:S(2)}) collective-permute-start(bf16[2,4,2,16,256]{4,3,2,1,0:T(8,128)(2,1)S(1)} %collective-permute-done.14.refs_2_), channel_id=1, source_target_pairs={{1,0},{0,1},{3,2},{2,3},{5,4},{4,5},{7,6},{6,7},{9,8},{8,9},{11,10... | collective-permute-start | bytes 393224 | tf_op jit(solution)/shard_map/ppermute | solution.py:21
  36.1 2.0 %collective-permute-start.18 = (bf16[2,4,2,16,256]{4,3,2,1,0:T(8,128)(2,1)S(1)}, bf16[2,4,2,16,256]{4,3,2,1,0:T(8,128)(2,1)S(1)}, u32[]{:S(2)}, u32[]{:S(2)}) collective-permute-start(bf16[2,4,2,16,256]{4,3,2,1,0:T(8,128)(2,1)S(1)} %collective-permute-done.13.refs_3_), channel_id=1, source_target_pairs={{1,0},{0,1},{3,2},{2,3},{5,4},{4,5},{7,6},{6,7},{9,8},{8,9},{11,10... | collective-permute-start | bytes 393224 | tf_op jit(solution)/shard_map/ppermute | solution.py:21
  36.6 1.5 %collective-permute-start.19 = (bf16[2,4,2,16,256]{4,3,2,1,0:T(8,128)(2,1)S(1)}, bf16[2,4,2,16,256]{4,3,2,1,0:T(8,128)(2,1)S(1)}, u32[]{:S(2)}, u32[]{:S(2)}) collective-permute-start(bf16[2,4,2,16,256]{4,3,2,1,0:T(8,128)(2,1)S(1)} %collective-permute-done.15.refs_4_), channel_id=1, source_target_pairs={{1,0},{0,1},{3,2},{2,3},{5,4},{4,5},{7,6},{6,7},{9,8},{8,9},{11,10... | collective-permute-start | bytes 393224 | tf_op jit(solution)/shard_map/ppermute | solution.py:21

commit v23 on v17

--- a/solution.py
+++ b/solution.py
@@ -9,7 +9,7 @@
 
 VMEM = pl.BlockSpec(memory_space=pltpu.VMEM)
 ANY = pl.BlockSpec(memory_space=pl.ANY)
-ORDER_FLOPS = 2_788_300_000
+ORDER_FLOPS = 2_788_000_000
 
 
 class Grid:
@@ -216,8 +216,9 @@
     train_here, gathered[0, 0], fisher_here = staged
     gathered[relayed, 0] = grid.swap(gathered[mirror, 0], beside, 0, 0)
     (train_here,) = stage([train_feats], train_here)
-    for mask in (beside, mirror):
-        gathered[mask, 1] = grid.swap(gathered[mask, 0], 0, 0, 1)
+    held, train_here = lax.optimization_barrier((gathered[mirror, 0], train_here))
+    gathered[mirror, 1] = grid.swap(held, 0, 0, 1)
+    gathered[beside, 1] = grid.swap(gathered[beside, 0], 0, 0, 1)
     gathered[relayed, 0], train_here = lax.optimization_barrier((gathered[relayed, 0], train_here))
     gathered[relayed, 1] = grid.swap(gathered[relayed, 0], 0, 0, 1)
 

time: 41.2 us -> 41.2 us (level)
  no operation moved by 1% of the time
where the time goes in v23:
time: 41.2 us; the launch traced here: 41 us
  starting transfers between devices  18.1 us (44%)
  Pallas kernels  12.3 us (30%)
  waiting for transfers between devices  10.4 us (25%)
    ppermute x20, starting transfers between devices, swap(): lax.ppermute(block, 'rows', [(row ^ step, row) for row in range(self.far...  18.1 us
    ppermute x20, waiting for transfers between devices, swap(): lax.ppermute(block, 'rows', [(row ^ step, row) for row in range(self.far...  10.4 us
    pallas_call x4, Pallas kernels, score(): pl.pallas_call(functools.partial(score_kernel, grid, masks, other, len(pa...  7.07 us
    pallas_call x2, Pallas kernels, stage(): pl.pallas_call(functools.partial(stage_kernel, first, arrays[0].shape[0]...  4.56 us
  transfers between devices with their start and end apart: 20, of which 8 were waited for; matrix products, arithmetic and copies ran while one was open for 0% of the time, Pallas kernels for 22%

profile of v23, /device:TPU:0, one launch (start us, length us, event | category | flops | bytes accessed | tf_op | source)
XLA Modules:
  0.0 41.0 jit_solution(16099602705614169933)
XLA Ops:
  0.0 5.0 %collective-permute-start = (bf16[2,16,2048]{2,1,0:T(8,128)(2,1)}, bf16[2,16,2048]{2,1,0:T(8,128)(2,1)S(1)}, u32[]{:S(2)}, u32[]{:S(2)}) collective-permute-start(bf16[2,16,2048]{2,1,0:T(8,128)(2,1)} %refs_1_.2), channel_id=1, source_target_pairs={{12,0},{13,1},{14,2},{15,3},{8,4},{9,5},{10,6},{11,7},{4,8},{5,9},... | collective-permute-start | bytes 393224 | tf_op jit(solution)/shard_map/ppermute | solution.py:21
  5.0 1.5 %collective-permute-start.7 = (bf16[1,2048,128]{2,1,0:T(8,128)(2,1)}, bf16[1,2048,128]{2,1,0:T(8,128)(2,1)S(1)}, u32[]{:S(2)}, u32[]{:S(2)}) collective-permute-start(bf16[1,2048,128]{2,1,0:T(8,128)(2,1)} %refs_2_.1), channel_id=1, source_target_pairs={{2,0},{3,1},{0,2},{1,3},{6,4},{7,5},{4,6},{5,7},{10,8},{11,9},{8,1... | collective-permute-start | bytes 1572872 | tf_op jit(solution)/shard_map/ppermute | solution.py:21
  6.6 2.4 %stage.2 = (bf16[2048,2048]{1,0:T(8,128)(2,1)S(1)}, bf16[2,16,2048]{2,1,0:T(8,128)(2,1)S(1)}, bf16[1,2048,128]{2,1,0:T(8,128)(2,1)S(1)}) custom-call(bf16[2048,2048]{1,0:T(8,128)(2,1)} %refs_1_.3, bf16[2,16,2048]{2,1,0:T(8,128)(2,1)} %refs_1_.2, bf16[1,2048,128]{2,1,0:T(8,128)(2,1)} %refs_2_.1), custom_call_target="tpu_custom_call" | custom-call | flops 2788000000 | bytes 9043968 | tf_op jit(solution)/shard_map/stage/pallas_call | solution.py:56
  9.0 2.3 %collective-permute-start.2 = (bf16[2,16,2048]{2,1,0:T(8,128)(2,1)S(1)}, bf16[2,16,2048]{2,1,0:T(8,128)(2,1)S(1)}, u32[]{:S(2)}, u32[]{:S(2)}) collective-permute-start(bf16[2,16,2048]{2,1,0:T(8,128)(2,1)S(1)} %collective-permute-done.refs_3_), channel_id=1, source_target_pairs={{4,0},{5,1},{6,2},{7,3},{0,4},{1,5},{2,6},{3,7},{12,8},{13,9},{14,... | collective-permute-start | bytes 393224 | tf_op jit(solution)/shard_map/ppermute | solution.py:21
  11.3 2.2 %stage.3.refs_0_ = bf16[2048,2048]{1,0:T(8,128)(2,1)S(1)} custom-call(bf16[2048,2048]{1,0:T(8,128)(2,1)S(1)} %get-tuple-element.28.refs_0_, bf16[2048,2048]{1,0:T(8,128)(2,1)} %refs_1_.3), custom_call_target="tpu_custom_call", output_to_operand_aliasing={{}: (0, {})} | custom-call | flops 1 | bytes 8388608 | tf_op jit(solution)/shard_map/stage/pallas_call | solution.py:56
  13.5 0.1 collective-permute-start.4
  13.6 0.5 %collective-permute-start.5 = (bf16[2,16,2048]{2,1,0:T(8,128)(2,1)S(1)}, bf16[2,16,2048]{2,1,0:T(8,128)(2,1)S(1)}, u32[]{:S(2)}, u32[]{:S(2)}) collective-permute-start(bf16[2,16,2048]{2,1,0:T(8,128)(2,1)S(1)} %collective-permute-done.3.refs_2_), channel_id=1, source_target_pairs={{1,0},{0,1},{3,2},{2,3},{5,4},{4,5},{7,6},{6,7},{9,8},{8,9},{11,10... | collective-permute-start | bytes 393224 | tf_op jit(solution)/shard_map/ppermute | solution.py:21
  14.1 1.4 %collective-permute-done.2.refs_4_ = bf16[2,16,2048]{2,1,0:T(8,128)(2,1)S(1)} collective-permute-done((bf16[2,16,2048]{2,1,0:T(8,128)(2,1)S(1)}, bf16[2,16,2048]{2,1,0:T(8,128)(2,1)S(1)}, u32[]{:S(2)}, u32[]{:S(2)}) %collective-permute-start.2) | collective-permute-done | bytes 131104 | tf_op jit(solution)/shard_map/ppermute | solution.py:21
  15.5 1.3 %collective-permute-done.6.refs_7_ = bf16[2,16,2048]{2,1,0:T(8,128)(2,1)S(1)} collective-permute-done((bf16[2,16,2048]{2,1,0:T(8,128)(2,1)S(1)}, bf16[2,16,2048]{2,1,0:T(8,128)(2,1)S(1)}, u32[]{:S(2)}, u32[]{:S(2)}) %collective-permute-start.6) | collective-permute-done | bytes 131104 | tf_op jit(solution)/shard_map/ppermute | solution.py:21
  16.9 1.8 %collective-permute-done.7.refs_9_ = bf16[1,2048,128]{2,1,0:T(8,128)(2,1)S(1)} collective-permute-done((bf16[1,2048,128]{2,1,0:T(8,128)(2,1)}, bf16[1,2048,128]{2,1,0:T(8,128)(2,1)S(1)}, u32[]{:S(2)}, u32[]{:S(2)}) %collective-permute-start.7) | collective-permute-done | bytes 524320 | tf_op jit(solution)/shard_map/ppermute | solution.py:21
  18.6 0.4 %condition.1.refs_0_ = bf16[2,4,2,16,256]{4,3,2,1,0:T(8,128)(2,1)S(1)} custom-call(bf16[2,16,2048]{2,1,0:T(8,128)(2,1)S(1)} %get-tuple-element.31.refs_0_, bf16[2,16,2048]{2,1,0:T(8,128)(2,1)S(1)} %collective-permute-done.1.refs_1_, bf16[2,16,2048]{2,1,0:T(8,128)(2,1)S(1)} %collective-permute-done.3.refs_2_, ...), custom_call_target="tpu_custom_call" | custom-call | flops 268435456 | bytes 3145728 | tf_op jit(solution)/shard_map/condition/pallas_call | solution.py:91
  19.1 0.1 collective-permute-start.10
  19.2 1.4 %collective-permute-start.8 = (bf16[2,4,2,16,256]{4,3,2,1,0:T(8,128)(2,1)S(1)}, bf16[2,4,2,16,256]{4,3,2,1,0:T(8,128)(2,1)S(1)}, u32[]{:S(2)}, u32[]{:S(2)}) collective-permute-start(bf16[2,4,2,16,256]{4,3,2,1,0:T(8,128)(2,1)S(1)} %condition.1.refs_0_), channel_id=1, source_target_pairs={{12,0},{13,1},{14,2},{15,3},{8,4},{9,5},{10,6},{11,7},{4,8},{5,9},... | collective-permute-start | bytes 393224 | tf_op jit(solution)/shard_map/ppermute | solution.py:21
  20.6 1.3 %collective-permute-start.9 = (bf16[2,4,2,16,256]{4,3,2,1,0:T(8,128)(2,1)S(1)}, bf16[2,4,2,16,256]{4,3,2,1,0:T(8,128)(2,1)S(1)}, u32[]{:S(2)}, u32[]{:S(2)}) collective-permute-start(bf16[2,4,2,16,256]{4,3,2,1,0:T(8,128)(2,1)S(1)} %condition.1.refs_0_), channel_id=1, source_target_pairs={{2,0},{3,1},{0,2},{1,3},{6,4},{7,5},{4,6},{5,7},{10,8},{11,9},{8,1... | collective-permute-start | bytes 393224 | tf_op jit(solution)/shard_map/ppermute | solution.py:21
  21.9 3.0 %collective-permute-done.10.refs_2_ = bf16[2,4,2,16,256]{4,3,2,1,0:T(8,128)(2,1)S(1)} collective-permute-done((bf16[2,4,2,16,256]{4,3,2,1,0:T(8,128)(2,1)S(1)}, bf16[2,4,2,16,256]{4,3,2,1,0:T(8,128)(2,1)S(1)}, u32[]{:S(2)}, u32[]{:S(2)}) %collective-permute-start.10) | collective-permute-done | bytes 131104 | tf_op jit(solution)/shard_map/ppermute | solution.py:21
  24.9 1.3 %collective-permute-start.11 = (bf16[2,4,2,16,256]{4,3,2,1,0:T(8,128)(2,1)S(1)}, bf16[2,4,2,16,256]{4,3,2,1,0:T(8,128)(2,1)S(1)}, u32[]{:S(2)}, u32[]{:S(2)}) collective-permute-start(bf16[2,4,2,16,256]{4,3,2,1,0:T(8,128)(2,1)S(1)} %collective-permute-done.10.refs_2_), channel_id=1, source_target_pairs={{2,0},{3,1},{0,2},{1,3},{6,4},{7,5},{4,6},{5,7},{10,8},{11,9},{8,1... | collective-permute-start | bytes 393224 | tf_op jit(solution)/shard_map/ppermute | solution.py:21
  26.2 0.9 %collective-permute-done.8.refs_1_ = bf16[2,4,2,16,256]{4,3,2,1,0:T(8,128)(2,1)S(1)} collective-permute-done((bf16[2,4,2,16,256]{4,3,2,1,0:T(8,128)(2,1)S(1)}, bf16[2,4,2,16,256]{4,3,2,1,0:T(8,128)(2,1)S(1)}, u32[]{:S(2)}, u32[]{:S(2)}) %collective-permute-start.8) | collective-permute-done | bytes 131104 | tf_op jit(solution)/shard_map/ppermute | solution.py:21
  27.0 1.5 %collective-permute-start.13 = (bf16[2,4,2,16,256]{4,3,2,1,0:T(8,128)(2,1)S(1)}, bf16[2,4,2,16,256]{4,3,2,1,0:T(8,128)(2,1)S(1)}, u32[]{:S(2)}, u32[]{:S(2)}) collective-permute-start(bf16[2,4,2,16,256]{4,3,2,1,0:T(8,128)(2,1)S(1)} %collective-permute-done.8.refs_1_), channel_id=1, source_target_pairs={{4,0},{5,1},{6,2},{7,3},{0,4},{1,5},{2,6},{3,7},{12,8},{13,9},{14,... | collective-permute-start | bytes 393224 | tf_op jit(solution)/shard_map/ppermute | solution.py:21
  28.5 1.6 %collective-permute-start.14 = (bf16[2,4,2,16,256]{4,3,2,1,0:T(8,128)(2,1)S(1)}, bf16[2,4,2,16,256]{4,3,2,1,0:T(8,128)(2,1)S(1)}, u32[]{:S(2)}, u32[]{:S(2)}) collective-permute-start(bf16[2,4,2,16,256]{4,3,2,1,0:T(8,128)(2,1)S(1)} %collective-permute-done.8.refs_1_), channel_id=1, source_target_pairs={{2,0},{3,1},{0,2},{1,3},{6,4},{7,5},{4,6},{5,7},{10,8},{11,9},{8,1... | collective-permute-start | bytes 393224 | tf_op jit(solution)/shard_map/ppermute | solution.py:21
  30.2 0.4 collective-permute-start.15
  30.5 0.4 %collective-permute-done.11.refs_3_ = bf16[2,4,2,16,256]{4,3,2,1,0:T(8,128)(2,1)S(1)} collective-permute-done((bf16[2,4,2,16,256]{4,3,2,1,0:T(8,128)(2,1)S(1)}, bf16[2,4,2,16,256]{4,3,2,1,0:T(8,128)(2,1)S(1)}, u32[]{:S(2)}, u32[]{:S(2)}) %collective-permute-start.11) | collective-permute-done | bytes 131104 | tf_op jit(solution)/shard_map/ppermute | solution.py:21
  30.9 0.2 turn.1.refs_1_
  31.2 0.1 collective-permute-start.16
  31.3 1.3 %score.4.refs_2_ = f32[2048,512]{1,0:T(8,128)S(1)} custom-call(bf16[2048,2048]{1,0:T(8,128)(2,1)S(1)} %stage.3.refs_0_, bf16[512,512]{1,0:T(8,128)(2,1)S(1)} %turn.1.refs_1_), custom_call_target="tpu_custom_call" | custom-call | flops 21474836480 | bytes 4194304 | tf_op jit(solution)/shard_map/score/pallas_call | solution.py:190
  32.5 0.6 %collective-permute-start.12 = (bf16[2,4,2,16,256]{4,3,2,1,0:T(8,128)(2,1)S(1)}, bf16[2,4,2,16,256]{4,3,2,1,0:T(8,128)(2,1)S(1)}, u32[]{:S(2)}, u32[]{:S(2)}) collective-permute-start(bf16[2,4,2,16,256]{4,3,2,1,0:T(8,128)(2,1)S(1)} %collective-permute-done.8.refs_1_), channel_id=1, source_target_pairs={{1,0},{0,1},{3,2},{2,3},{5,4},{4,5},{7,6},{6,7},{9,8},{8,9},{11,10... | collective-permute-start | bytes 393224 | tf_op jit(solution)/shard_map/ppermute | solution.py:21
  33.1 0.1 collective-permute-done.16.refs_1_
  33.2 1.4 %score.5.refs_5_ = f32[2048,512]{1,0:T(8,128)S(1)} custom-call(bf16[2048,2048]{1,0:T(8,128)(2,1)S(1)} %stage.3.refs_0_, bf16[512,512]{1,0:T(8,128)(2,1)S(1)} %collective-permute-done.16.refs_1_, f32[2048,512]{1,0:T(8,128)S(1)} %score.4.refs_2_), custom_call_target="tpu_custom_call", output_to_operand_aliasing={{}: (2, {})} | custom-call | flops 1073741824 | bytes 4194304 | tf_op jit(solution)/shard_map/score/pallas_call | solution.py:190
  34.6 1.4 %collective-permute-done.15.refs_4_ = bf16[2,4,2,16,256]{4,3,2,1,0:T(8,128)(2,1)S(1)} collective-permute-done((bf16[2,4,2,16,256]{4,3,2,1,0:T(8,128)(2,1)S(1)}, bf16[2,4,2,16,256]{4,3,2,1,0:T(8,128)(2,1)S(1)}, u32[]{:S(2)}, u32[]{:S(2)}) %collective-permute-start.15) | collective-permute-done | bytes 131104 | tf_op jit(solution)/shard_map/ppermute | solution.py:21
  36.0 0.5 %collective-permute-start.18 = (bf16[2,4,2,16,256]{4,3,2,1,0:T(8,128)(2,1)S(1)}, bf16[2,4,2,16,256]{4,3,2,1,0:T(8,128)(2,1)S(1)}, u32[]{:S(2)}, u32[]{:S(2)}) collective-permute-start(bf16[2,4,2,16,256]{4,3,2,1,0:T(8,128)(2,1)S(1)} %collective-permute-done.13.refs_3_), channel_id=1, source_target_pairs={{1,0},{0,1},{3,2},{2,3},{5,4},{4,5},{7,6},{6,7},{9,8},{8,9},{11,10... | collective-permute-start | bytes 393224 | tf_op jit(solution)/shard_map/ppermute | solution.py:21
  36.5 0.0 collective-permute-start.19
  36.6 1.5 %score.6.refs_5_ = f32[2048,512]{1,0:T(8,128)S(1)} custom-call(bf16[2048,2048]{1,0:T(8,128)(2,1)S(1)} %stage.3.refs_0_, bf16[2,4,2,16,256]{4,3,2,1,0:T(8,128)(2,1)S(1)} %collective-permute-done.8.refs_1_, bf16[2,4,2,16,256]{4,3,2,1,0:T(8,128)(2,1)S(1)} %collective-permute-done.14.refs_2_, ...), custom_call_target="tpu_custom_call", output_to_operand_aliasing={{}: (5, {})} | custom-call | flops 1073741824 | bytes 4194304 | tf_op jit(solution)/shard_map/score/pallas_call | solution.py:190
  38.1 2.9 %score.7 = f32[2048,512]{1,0:T(8,128)} custom-call(bf16[2048,2048]{1,0:T(8,128)(2,1)S(1)} %stage.3.refs_0_, bf16[2,4,2,16,256]{4,3,2,1,0:T(8,128)(2,1)S(1)} %collective-permute-done.12.refs_1_, bf16[2,4,2,16,256]{4,3,2,1,0:T(8,128)(2,1)S(1)} %collective-permute-done.17.refs_2_, bf16[2,4,2,16,256]{4,3,2,1,0:T(8,128)(2,1)S(1)} %collective-permute-done.18.refs_3_, ...), custom_call_target="tpu_custom_call" | custom-call | flops 1073741824 | bytes 4194304 | tf_op jit(solution)/shard_map/score/pallas_call | solution.py:190
  (16 shorter events, 0.0 us)
Async XLA Ops:
  0.0 9.0 %collective-permute-start = (bf16[2,16,2048]{2,1,0:T(8,128)(2,1)}, bf16[2,16,2048]{2,1,0:T(8,128)(2,1)S(1)}, u32[]{:S(2)}, u32[]{:S(2)}) collective-permute-start(bf16[2,16,2048]{2,1,0:T(8,128)(2,1)} %refs_1_.2), channel_id=1, source_target_pairs={{12,0},{13,1},{14,2},{15,3},{8,4},{9,5},{10,6},{11,7},{4,8},{5,9},... | collective-permute-start | bytes 393224 | tf_op jit(solution)/shard_map/ppermute | solution.py:21
  5.0 13.6 %collective-permute-start.7 = (bf16[1,2048,128]{2,1,0:T(8,128)(2,1)}, bf16[1,2048,128]{2,1,0:T(8,128)(2,1)S(1)}, u32[]{:S(2)}, u32[]{:S(2)}) collective-permute-start(bf16[1,2048,128]{2,1,0:T(8,128)(2,1)} %refs_2_.1), channel_id=1, source_target_pairs={{2,0},{3,1},{0,2},{1,3},{6,4},{7,5},{4,6},{5,7},{10,8},{11,9},{8,1... | collective-permute-start | bytes 1572872 | tf_op jit(solution)/shard_map/ppermute | solution.py:21
  6.6 2.4 %collective-permute-start.1 = (bf16[2,16,2048]{2,1,0:T(8,128)(2,1)}, bf16[2,16,2048]{2,1,0:T(8,128)(2,1)S(1)}, u32[]{:S(2)}, u32[]{:S(2)}) collective-permute-start(bf16[2,16,2048]{2,1,0:T(8,128)(2,1)} %refs_1_.2), channel_id=1, source_target_pairs={{1,0},{0,1},{3,2},{2,3},{5,4},{4,5},{7,6},{6,7},{9,8},{8,9},{11,10... | collective-permute-start | bytes 393224 | tf_op jit(solution)/shard_map/ppermute | solution.py:21
  6.6 7.0 %collective-permute-start.3 = (bf16[2,16,2048]{2,1,0:T(8,128)(2,1)}, bf16[2,16,2048]{2,1,0:T(8,128)(2,1)S(1)}, u32[]{:S(2)}, u32[]{:S(2)}) collective-permute-start(bf16[2,16,2048]{2,1,0:T(8,128)(2,1)} %refs_1_.2), channel_id=1, source_target_pairs={{4,0},{5,1},{6,2},{7,3},{0,4},{1,5},{2,6},{3,7},{12,8},{13,9},{14,... | collective-permute-start | bytes 393224 | tf_op jit(solution)/shard_map/ppermute | solution.py:21
  9.0 6.5 %collective-permute-start.2 = (bf16[2,16,2048]{2,1,0:T(8,128)(2,1)S(1)}, bf16[2,16,2048]{2,1,0:T(8,128)(2,1)S(1)}, u32[]{:S(2)}, u32[]{:S(2)}) collective-permute-start(bf16[2,16,2048]{2,1,0:T(8,128)(2,1)S(1)} %collective-permute-done.refs_3_), channel_id=1, source_target_pairs={{4,0},{5,1},{6,2},{7,3},{0,4},{1,5},{2,6},{3,7},{12,8},{13,9},{14,... | collective-permute-start | bytes 393224 | tf_op jit(solution)/shard_map/ppermute | solution.py:21
  13.5 2.0 %collective-permute-start.4 = (bf16[2,16,2048]{2,1,0:T(8,128)(2,1)S(1)}, bf16[2,16,2048]{2,1,0:T(8,128)(2,1)S(1)}, u32[]{:S(2)}, u32[]{:S(2)}) collective-permute-start(bf16[2,16,2048]{2,1,0:T(8,128)(2,1)S(1)} %collective-permute-done.refs_3_), channel_id=1, source_target_pairs={{1,0},{0,1},{3,2},{2,3},{5,4},{4,5},{7,6},{6,7},{9,8},{8,9},{11,10... | collective-permute-start | bytes 393224 | tf_op jit(solution)/shard_map/ppermute | solution.py:21
  13.6 1.9 %collective-permute-start.5 = (bf16[2,16,2048]{2,1,0:T(8,128)(2,1)S(1)}, bf16[2,16,2048]{2,1,0:T(8,128)(2,1)S(1)}, u32[]{:S(2)}, u32[]{:S(2)}) collective-permute-start(bf16[2,16,2048]{2,1,0:T(8,128)(2,1)S(1)} %collective-permute-done.3.refs_2_), channel_id=1, source_target_pairs={{1,0},{0,1},{3,2},{2,3},{5,4},{4,5},{7,6},{6,7},{9,8},{8,9},{11,10... | collective-permute-start | bytes 393224 | tf_op jit(solution)/shard_map/ppermute | solution.py:21
  15.5 1.3 %collective-permute-start.6 = (bf16[2,16,2048]{2,1,0:T(8,128)(2,1)S(1)}, bf16[2,16,2048]{2,1,0:T(8,128)(2,1)S(1)}, u32[]{:S(2)}, u32[]{:S(2)}) collective-permute-start(bf16[2,16,2048]{2,1,0:T(8,128)(2,1)S(1)} %collective-permute-done.2.refs_4_), channel_id=1, source_target_pairs={{1,0},{0,1},{3,2},{2,3},{5,4},{4,5},{7,6},{6,7},{9,8},{8,9},{11,10... | collective-permute-start | bytes 393224 | tf_op jit(solution)/shard_map/ppermute | solution.py:21
  19.1 5.8 %collective-permute-start.10 = (bf16[2,4,2,16,256]{4,3,2,1,0:T(8,128)(2,1)S(1)}, bf16[2,4,2,16,256]{4,3,2,1,0:T(8,128)(2,1)S(1)}, u32[]{:S(2)}, u32[]{:S(2)}) collective-permute-start(bf16[2,4,2,16,256]{4,3,2,1,0:T(8,128)(2,1)S(1)} %condition.1.refs_0_), channel_id=1, source_target_pairs={{4,0},{5,1},{6,2},{7,3},{0,4},{1,5},{2,6},{3,7},{12,8},{13,9},{14,... | collective-permute-start | bytes 393224 | tf_op jit(solution)/shard_map/ppermute | solution.py:21
  19.2 7.9 %collective-permute-start.8 = (bf16[2,4,2,16,256]{4,3,2,1,0:T(8,128)(2,1)S(1)}, bf16[2,4,2,16,256]{4,3,2,1,0:T(8,128)(2,1)S(1)}, u32[]{:S(2)}, u32[]{:S(2)}) collective-permute-start(bf16[2,4,2,16,256]{4,3,2,1,0:T(8,128)(2,1)S(1)} %condition.1.refs_0_), channel_id=1, source_target_pairs={{12,0},{13,1},{14,2},{15,3},{8,4},{9,5},{10,6},{11,7},{4,8},{5,9},... | collective-permute-start | bytes 393224 | tf_op jit(solution)/shard_map/ppermute | solution.py:21
  20.6 9.9 %collective-permute-start.9 = (bf16[2,4,2,16,256]{4,3,2,1,0:T(8,128)(2,1)S(1)}, bf16[2,4,2,16,256]{4,3,2,1,0:T(8,128)(2,1)S(1)}, u32[]{:S(2)}, u32[]{:S(2)}) collective-permute-start(bf16[2,4,2,16,256]{4,3,2,1,0:T(8,128)(2,1)S(1)} %condition.1.refs_0_), channel_id=1, source_target_pairs={{2,0},{3,1},{0,2},{1,3},{6,4},{7,5},{4,6},{5,7},{10,8},{11,9},{8,1... | collective-permute-start | bytes 393224 | tf_op jit(solution)/shard_map/ppermute | solution.py:21
  24.9 6.0 %collective-permute-start.11 = (bf16[2,4,2,16,256]{4,3,2,1,0:T(8,128)(2,1)S(1)}, bf16[2,4,2,16,256]{4,3,2,1,0:T(8,128)(2,1)S(1)}, u32[]{:S(2)}, u32[]{:S(2)}) collective-permute-start(bf16[2,4,2,16,256]{4,3,2,1,0:T(8,128)(2,1)S(1)} %collective-permute-done.10.refs_2_), channel_id=1, source_target_pairs={{2,0},{3,1},{0,2},{1,3},{6,4},{7,5},{4,6},{5,7},{10,8},{11,9},{8,1... | collective-permute-start | bytes 393224 | tf_op jit(solution)/shard_map/ppermute | solution.py:21
  27.0 7.5 %collective-permute-start.13 = (bf16[2,4,2,16,256]{4,3,2,1,0:T(8,128)(2,1)S(1)}, bf16[2,4,2,16,256]{4,3,2,1,0:T(8,128)(2,1)S(1)}, u32[]{:S(2)}, u32[]{:S(2)}) collective-permute-start(bf16[2,4,2,16,256]{4,3,2,1,0:T(8,128)(2,1)S(1)} %collective-permute-done.8.refs_1_), channel_id=1, source_target_pairs={{4,0},{5,1},{6,2},{7,3},{0,4},{1,5},{2,6},{3,7},{12,8},{13,9},{14,... | collective-permute-start | bytes 393224 | tf_op jit(solution)/shard_map/ppermute | solution.py:21
  28.5 6.1 %collective-permute-start.14 = (bf16[2,4,2,16,256]{4,3,2,1,0:T(8,128)(2,1)S(1)}, bf16[2,4,2,16,256]{4,3,2,1,0:T(8,128)(2,1)S(1)}, u32[]{:S(2)}, u32[]{:S(2)}) collective-permute-start(bf16[2,4,2,16,256]{4,3,2,1,0:T(8,128)(2,1)S(1)} %collective-permute-done.8.refs_1_), channel_id=1, source_target_pairs={{2,0},{3,1},{0,2},{1,3},{6,4},{7,5},{4,6},{5,7},{10,8},{11,9},{8,1... | collective-permute-start | bytes 393224 | tf_op jit(solution)/shard_map/ppermute | solution.py:21
  30.2 5.9 %collective-permute-start.15 = (bf16[2,4,2,16,256]{4,3,2,1,0:T(8,128)(2,1)S(1)}, bf16[2,4,2,16,256]{4,3,2,1,0:T(8,128)(2,1)S(1)}, u32[]{:S(2)}, u32[]{:S(2)}) collective-permute-start(bf16[2,4,2,16,256]{4,3,2,1,0:T(8,128)(2,1)S(1)} %collective-permute-done.8.refs_1_), channel_id=1, source_target_pairs={{6,0},{7,1},{4,2},{5,3},{2,4},{3,5},{0,6},{1,7},{14,8},{15,9},{12,... | collective-permute-start | bytes 393224 | tf_op jit(solution)/shard_map/ppermute | solution.py:21
  31.2 2.0 %collective-permute-start.16 = (bf16[512,512]{1,0:T(8,128)(2,1)S(1)}, bf16[512,512]{1,0:T(8,128)(2,1)S(1)}, u32[]{:S(2)}, u32[]{:S(2)}) collective-permute-start(bf16[512,512]{1,0:T(8,128)(2,1)S(1)} %turn.1.refs_1_), channel_id=1, source_target_pairs={{1,0},{0,1},{3,2},{2,3},{5,4},{4,5},{7,6},{6,7},{9,8},{8,9},{11,10... | collective-permute-start | bytes 1572872 | tf_op jit(solution)/shard_map/ppermute | solution.py:21
  32.5 5.5 %collective-permute-start.12 = (bf16[2,4,2,16,256]{4,3,2,1,0:T(8,128)(2,1)S(1)}, bf16[2,4,2,16,256]{4,3,2,1,0:T(8,128)(2,1)S(1)}, u32[]{:S(2)}, u32[]{:S(2)}) collective-permute-start(bf16[2,4,2,16,256]{4,3,2,1,0:T(8,128)(2,1)S(1)} %collective-permute-done.8.refs_1_), channel_id=1, source_target_pairs={{1,0},{0,1},{3,2},{2,3},{5,4},{4,5},{7,6},{6,7},{9,8},{8,9},{11,10... | collective-permute-start | bytes 393224 | tf_op jit(solution)/shard_map/ppermute | solution.py:21
  36.0 2.0 %collective-permute-start.17 = (bf16[2,4,2,16,256]{4,3,2,1,0:T(8,128)(2,1)S(1)}, bf16[2,4,2,16,256]{4,3,2,1,0:T(8,128)(2,1)S(1)}, u32[]{:S(2)}, u32[]{:S(2)}) collective-permute-start(bf16[2,4,2,16,256]{4,3,2,1,0:T(8,128)(2,1)S(1)} %collective-permute-done.14.refs_2_), channel_id=1, source_target_pairs={{1,0},{0,1},{3,2},{2,3},{5,4},{4,5},{7,6},{6,7},{9,8},{8,9},{11,10... | collective-permute-start | bytes 393224 | tf_op jit(solution)/shard_map/ppermute | solution.py:21
  36.0 2.0 %collective-permute-start.18 = (bf16[2,4,2,16,256]{4,3,2,1,0:T(8,128)(2,1)S(1)}, bf16[2,4,2,16,256]{4,3,2,1,0:T(8,128)(2,1)S(1)}, u32[]{:S(2)}, u32[]{:S(2)}) collective-permute-start(bf16[2,4,2,16,256]{4,3,2,1,0:T(8,128)(2,1)S(1)} %collective-permute-done.13.refs_3_), channel_id=1, source_target_pairs={{1,0},{0,1},{3,2},{2,3},{5,4},{4,5},{7,6},{6,7},{9,8},{8,9},{11,10... | collective-permute-start | bytes 393224 | tf_op jit(solution)/shard_map/ppermute | solution.py:21
  36.5 1.5 %collective-permute-start.19 = (bf16[2,4,2,16,256]{4,3,2,1,0:T(8,128)(2,1)S(1)}, bf16[2,4,2,16,256]{4,3,2,1,0:T(8,128)(2,1)S(1)}, u32[]{:S(2)}, u32[]{:S(2)}) collective-permute-start(bf16[2,4,2,16,256]{4,3,2,1,0:T(8,128)(2,1)S(1)} %collective-permute-done.15.refs_4_), channel_id=1, source_target_pairs={{1,0},{0,1},{3,2},{2,3},{5,4},{4,5},{7,6},{6,7},{9,8},{8,9},{11,10... | collective-permute-start | bytes 393224 | tf_op jit(solution)/shard_map/ppermute | solution.py:21
